TPU v7x, 32 devices: a whole 2x2x4 slice. The times are simulated.
32 devices in a mesh: rows: 8 (over z, y), cols: 4 (over x, core).
Axes of the slice: x: 2, y: 2, z: 4, core: 2. Of those that a mesh axis runs over, the one named last changes fastest.
Arguments:
- h_start: float32 [4096, 128], P(('rows', 'cols')), may hold values from -6 to 6
- cotangent: float32 [4096, 128], P(('rows', 'cols')), may hold values from -6 to 6
- node_type: int32 [4096], P(('rows', 'cols')), may hold values from 0 to 7
- teleport: float32 [8], replicated, may hold values from 0.05 to 0.5
- tile_values: bfloat16 [8, 4, 24, 128, 128], P('rows', 'cols'), may hold values from -0.109375 to 0.109375
- tile_row: int32 [8, 4, 24], P('rows', 'cols'), may hold values from 0 to 3, as said below
- tile_col: int32 [8, 4, 24], P('rows', 'cols'), may hold values from 0 to 7
- tile_count: int32 [8, 4], P('rows', 'cols'), may hold values from 3 to 24, as said below
Outputs:
- propagated: float32 [4096, 128], P(('rows', 'cols'))
- input_grad: float32 [4096, 128], P(('rows', 'cols'))
Inputs may be any that keep to these rules, and one draw needn't show every extreme that they name: Within one row block and column range, the pairs (tile_row, tile_col) of the 24 slots are all different. `tile_count`: slots at or beyond the count are not part of A. In every draw 1 row blocks use all 24 slots in every column range.
All inputs are finite; a program needn't handle non-finite values.
Results may differ from a plain program's by a relative error of at most 0.0029.
Values may be sent and summed in bfloat16 or wider, within the bound.
No kernel may reach another device: no remote copies, remote signals or barrier semaphores. Data moves between devices by JAX's collectives and lax.ppermute only.
A program may use at most 64 MiB of HBM per device.

v0:
```python
import jax
import jax.numpy as jnp
from jax import lax
from jax.sharding import PartitionSpec as P

SLOT_BLOCK = 24


def tile_pass(
    tile_data,
    slot_rows,
    slot_cols,
    slot_count,
    panel_tiles,
    block_tiles,
    row_tiles,
    col_start,
    col_window,
):
    tile_size = tile_data.shape[-1]
    features = (panel_tiles if panel_tiles is not None else block_tiles).shape[-1]
    slot_total = tile_data.shape[0]
    running = []
    if panel_tiles is not None:
        running.append(jnp.zeros((row_tiles + 1, tile_size, features), jnp.float32))
    if block_tiles is not None:
        running.append(jnp.zeros((col_window + 1, tile_size, features), jnp.float32))
    block_count = (slot_count + SLOT_BLOCK - 1) // SLOT_BLOCK

    def advance(block_index, totals):
        slot_ids = block_index * SLOT_BLOCK + jnp.arange(SLOT_BLOCK, dtype=jnp.int32)
        active = slot_ids < slot_count
        where_at = jnp.clip(slot_ids, 0, slot_total - 1)
        values = jnp.take(tile_data, where_at, axis=0)
        row_ids = jnp.take(slot_rows, where_at)
        col_ids = jnp.take(slot_cols, where_at)
        updated = list(totals)
        if panel_tiles is not None:
            fetched = jnp.take(panel_tiles, col_ids, axis=0)
            product = jnp.einsum(
                "sij,sjf->sif", values, fetched, preferred_element_type=jnp.float32
            )
            segment = jnp.where(active, row_ids, row_tiles)
            updated[0] = totals[0].at[segment].add(product)
        if block_tiles is not None:
            fetched = jnp.take(block_tiles, row_ids, axis=0)
            product = jnp.einsum(
                "sji,sjf->sif", values, fetched, preferred_element_type=jnp.float32
            )
            local_col = col_ids - col_start
            inside = active & (local_col >= 0) & (local_col < col_window)
            segment = jnp.where(inside, local_col, col_window)
            updated[-1] = totals[-1].at[segment].add(product)
        return tuple(updated)

    totals = lax.fori_loop(0, block_count, advance, tuple(running))
    return [entry[:-1] for entry in totals]


def shards(h_start, cotangent, node_type, teleport, tile_values, tile_row, tile_col, tile_count):
    tile_data = tile_values[0, 0]
    slot_rows = tile_row[0, 0]
    slot_cols = tile_col[0, 0]
    slot_count = tile_count[0, 0]
    tile_size = tile_data.shape[-1]
    features = h_start.shape[-1]
    local_tiles = h_start.shape[0] // tile_size
    row_tiles = lax.axis_size("cols") * local_tiles
    col_tiles = lax.axis_size("rows") * local_tiles
    type_ids = jnp.arange(teleport.shape[0], dtype=jnp.int32)
    teleport_rate = jnp.sum(
        jnp.where(node_type[:, None] == type_ids[None, :], teleport[None, :], 0.0), axis=1
    )[:, None]
    keep_rate = 1.0 - teleport_rate

    def run_tiles(panel_tiles, block_tiles, col_start, col_window):
        return tile_pass(
            tile_data,
            slot_rows,
            slot_cols,
            slot_count,
            panel_tiles,
            block_tiles,
            row_tiles,
            col_start,
            col_window,
        )

    def gather_panel(local_part):
        gathered = lax.all_gather(local_part, "rows", axis=0, tiled=True)
        return gathered.reshape(col_tiles, tile_size, features)

    def gather_block(local_part):
        gathered = lax.all_gather(local_part, "cols", axis=0, tiled=True)
        return gathered.reshape(row_tiles, tile_size, features)

    def finish_forward(partial_value):
        return lax.psum_scatter(
            partial_value.reshape(row_tiles * tile_size, features),
            "cols",
            scatter_dimension=0,
            tiled=True,
        )

    def finish_adjoint(partial_value):
        return lax.psum_scatter(
            partial_value.reshape(col_tiles * tile_size, features),
            "rows",
            scatter_dimension=0,
            tiled=True,
        )

    def forward_hop(local_part):
        return finish_forward(run_tiles(gather_panel(local_part), None, 0, col_tiles)[0])

    first_panel = h_start.astype(jnp.bfloat16)
    first_adjoint = (keep_rate * cotangent).astype(jnp.bfloat16)
    hop_one = keep_rate * forward_hop(first_panel) + teleport_rate * h_start
    propagated = keep_rate * forward_hop(hop_one.astype(jnp.bfloat16)) + teleport_rate * h_start
    back_one = finish_adjoint(run_tiles(None, gather_block(first_adjoint), 0, col_tiles)[0])
    back_two = finish_adjoint(
        run_tiles(None, gather_block((keep_rate * back_one).astype(jnp.bfloat16)), 0, col_tiles)[0]
    )
    input_grad = teleport_rate * cotangent + teleport_rate * back_one + back_two
    return (propagated, input_grad)


def solution(mesh):
    placed = (
        P(("rows", "cols"), None),
        P(("rows", "cols"), None),
        P(("rows", "cols")),
        P(),
        P("rows", "cols", None, None, None),
        P("rows", "cols", None),
        P("rows", "cols", None),
        P("rows", "cols"),
    )
    return jax.shard_map(
        shards,
        mesh=mesh,
        in_specs=placed,
        out_specs=(P(("rows", "cols"), None), P(("rows", "cols"), None)),
        check_vma=False,
    )
```

profile of v0, /device:TPU:0, one launch (start us, length us, event | category | flops | bytes accessed | tf_op | source)
XLA Modules:
  0.0 281.8 jit_solution(12034508150601700552)
XLA Ops:
  7.9 0.8 convert_element_type.12
  8.7 34.5 %all_gather.12 = bf16[1024,128]{1,0:T(8,128)(2,1)} all-gather(bf16[128,128]{1,0:T(8,128)(2,1)S(1)} %convert_element_type.12), channel_id=1, replica_groups=mesh['rows'=8,'cols'=4] {'rows'}, dimensions={0}, use_global_device_ids=true | all-gather | bytes 294912 | tf_op jit(solution)/shard_map/all_gather | solution.py:90
  43.3 10.4 %while.40 = (s32[]{:T(128)}, f32[5,128,128]{2,1,0:T(8,128)S(1)}, s32[]{:T(128)}, s32[]{:T(128)}, s32[24]{0:T(128)}, /*index=5*/bf16[24,128,128]{2,1,0:T(8,128)(2...) while((s32[]{:T(128)}, f32[5,128,128]{2,1,0:T(8,128)S(1)}, s32[]{:T(128)}, s32[]{:T(128)}, ...), condition=%wide.region_3.7_spmd, body=%wide.region_1.6_spmd.sunk | while | flops 101845808 | bytes 14166169 | solution.py:56
  43.3 1.4 gather_fusion.1
  44.8 1.6 gather_fusion.2
  46.5 1.6 gather_fusion.3
  48.0 1.6 fusion.42
  49.6 0.7 gather_fusion
  50.3 0.7 compare_select_fusion.27
  51.0 2.6 scatter_fusion
  53.7 0.7 slice.12
  54.5 0.8 select_reduce_fusion
  55.3 5.4 %all_gather.14 = bf16[512,128]{1,0:T(8,128)(2,1)S(1)} all-gather(bf16[128,128]{1,0:T(8,128)(2,1)S(1)} %multiply_convert_fusion.1), channel_id=1, replica_groups=mesh['rows'=8,'cols'=4] {'cols'}, dimensions={0}, use_global_device_ids=true | all-gather | bytes 163840 | tf_op jit(solution)/shard_map/all_gather | solution.py:94
  60.8 9.8 %while.42 = (s32[]{:T(128)}, f32[9,128,128]{2,1,0:T(8,128)S(1)}, s32[]{:T(128)}, s32[]{:T(128)}, s32[24]{0:T(128)S(1)}, /*index=5*/bf16[24,128,128]{2,1,0:T(8,12...) while((s32[]{:T(128)}, f32[9,128,128]{2,1,0:T(8,128)S(1)}, s32[]{:T(128)}, ...), condition=%wide.region_11.16_spmd, body=%wide.region_9.15_spmd.sunk | while | flops 101845904 | bytes 11020001 | solution.py:56
  60.9 0.7 gather_fusion.9
  61.6 1.6 gather_fusion.10
  63.2 1.6 gather_fusion.11
  64.7 1.9 fusion.48
  66.6 0.7 gather_fusion.8
  67.3 0.7 compare_select_fusion.31
  68.0 2.6 scatter_fusion.2
  70.6 0.8 slice.14
  71.5 4.0 %reduce-scatter.5.cloned.1.call-done = f32[128,128]{1,0:T(8,128)} async-done(((f32[512,128]{1,0:T(8,128)}), f32[128,128]{1,0:T(8,128)}) %reduce-scatter.5.cloned.1.call-update) | async-done | bytes 65552 | tf_op jit(solution)/shard_map/reduce_scatter | solution.py:98
  75.5 65.7 %reduce-scatter.9.cloned.1.call-done = f32[128,128]{1,0:T(8,128)} async-done(((f32[1024,128]{1,0:T(8,128)}), f32[128,128]{1,0:T(8,128)}) %reduce-scatter.9.cloned.1.call-update) | async-done | bytes 65552 | tf_op jit(solution)/shard_map/reduce_scatter | solution.py:106
  141.2 1.0 multiply_convert_fusion
  142.2 5.4 %all_gather.15 = bf16[512,128]{1,0:T(8,128)(2,1)S(1)} all-gather(bf16[128,128]{1,0:T(8,128)(2,1)S(1)} %get-tuple-element.260), channel_id=1, replica_groups=mesh['rows'=8,'cols'=4] {'cols'}, dimensions={0}, use_global_device_ids=true | all-gather | bytes 163840 | tf_op jit(solution)/shard_map/all_gather | solution.py:94
  147.6 30.7 %all_gather.13 = bf16[1024,128]{1,0:T(8,128)(2,1)S(1)} all-gather(bf16[128,128]{1,0:T(8,128)(2,1)S(1)} %get-tuple-element.261), channel_id=1, replica_groups=mesh['rows'=8,'cols'=4] {'rows'}, dimensions={0}, use_global_device_ids=true | all-gather | bytes 294912 | tf_op jit(solution)/shard_map/all_gather | solution.py:90
  178.4 9.7 %while.41 = (s32[]{:T(128)}, f32[5,128,128]{2,1,0:T(8,128)S(1)}, s32[]{:T(128)}, s32[]{:T(128)}, s32[24]{0:T(128)S(1)}, /*index=5*/bf16[24,128,128]{2,1,0:T(8,12...) while((s32[]{:T(128)}, f32[5,128,128]{2,1,0:T(8,128)S(1)}, s32[]{:T(128)}, ...), condition=%wide.region_7.11_spmd, body=%wide.region_5.10_spmd.sunk | while | flops 101845808 | bytes 11020001 | solution.py:56
  178.4 0.7 gather_fusion.5
  179.1 1.6 gather_fusion.6
  180.7 1.6 gather_fusion.7
  182.3 1.8 fusion.45
  184.1 0.7 gather_fusion.4
  184.8 0.7 compare_select_fusion.29
  185.5 2.6 scatter_fusion.1
  188.1 0.7 slice.13
  188.9 9.8 %while.43 = (s32[]{:T(128)}, f32[9,128,128]{2,1,0:T(8,128)S(1)}, s32[]{:T(128)}, s32[]{:T(128)}, s32[24]{0:T(128)S(1)}, /*index=5*/bf16[24,128,128]{2,1,0:T(8,12...) while((s32[]{:T(128)}, f32[9,128,128]{2,1,0:T(8,128)S(1)}, ...), condition=%wide.region_15.20_spmd, body=%wide.region_13.19_spmd.sunk | while | flops 101845904 | bytes 11020001 | solution.py:56
  189.0 0.7 gather_fusion.13
  189.7 1.6 gather_fusion.14
  191.3 1.6 gather_fusion.15
  192.9 1.9 fusion.51
  194.7 0.7 gather_fusion.12
  195.4 0.7 compare_select_fusion.33
  196.1 2.6 scatter_fusion.3
  198.8 0.8 slice.15
  199.6 8.4 %reduce-scatter.7.cloned.1.call-done = f32[128,128]{1,0:T(8,128)} async-done(((f32[512,128]{1,0:T(8,128)}), f32[128,128]{1,0:T(8,128)}) %reduce-scatter.7.cloned.1.call-update) | async-done | bytes 65552 | tf_op jit(solution)/shard_map/reduce_scatter | solution.py:98
  208.1 65.6 %reduce-scatter.11.cloned.1.call-done = f32[128,128]{1,0:T(8,128)} async-done(((f32[1024,128]{1,0:T(8,128)}), f32[128,128]{1,0:T(8,128)}) %reduce-scatter.11.cloned.1.call-update) | async-done | bytes 65552 | tf_op jit(solution)/shard_map/reduce_scatter | solution.py:106
  273.6 1.6 multiply_add_fusion
  (46 shorter events, 0.6 us)
Async XLA Ops:
  7.2 68.4 %reduce-scatter.5.cloned.1.call-start = ((), (), s32[]{:S(2)}) async-start(), calls=%async_computation.4 | async-start | bytes 327680 | tf_op jit(solution)/shard_map/reduce_scatter | solution.py:98
  43.3 12.0 %copy-start.6 = (f32[128,128]{1,0:T(8,128)S(1)}, f32[128,128]{1,0:T(8,128)}, u32[]{:S(2)}) copy-start(f32[128,128]{1,0:T(8,128)} %param.25) | copy-start | bytes 196612
  43.3 3.2 %copy-start.3 = (bf16[24,128,128]{2,1,0:T(8,128)(2,1)S(1)}, bf16[24,128,128]{2,1,0:T(8,128)(2,1)}, u32[]{:S(2)}) copy-start(bf16[24,128,128]{2,1,0:T(8,128)(2,1)} %get-tuple-element.541) | copy-start | bytes 2359300 | tf_op jit(solution)/shard_map/while
  48.0 1.6 copy-start
  53.6 7.2 %copy-start.1 = (s32[24]{0:T(128)S(1)}, s32[24]{0:T(128)}, u32[]{:S(2)}) copy-start(s32[24]{0:T(128)} %get-tuple-element.610) | copy-start | bytes 292
  53.7 7.2 %copy-start.2 = (s32[24]{0:T(128)S(1)}, s32[24]{0:T(128)}, u32[]{:S(2)}) copy-start(s32[24]{0:T(128)} %get-tuple-element.613) | copy-start | bytes 292
  53.7 7.2 %copy-start.4 = (bf16[24,128,128]{2,1,0:T(8,128)(2,1)S(1)}, bf16[24,128,128]{2,1,0:T(8,128)(2,1)}, u32[]{:S(2)}) copy-start(bf16[24,128,128]{2,1,0:T(8,128)(2,1)} %get-tuple-element.616) | copy-start | bytes 2359300
  54.4 86.8 %reduce-scatter.9.cloned.1.call-start = ((), (), s32[]{:S(2)}) async-start(), calls=%async_computation.6 | async-start | bytes 589824 | tf_op jit(solution)/shard_map/reduce_scatter | solution.py:106
  70.6 70.6 %copy-start.5 = (f32[128,128]{1,0:T(8,128)S(1)}, f32[128,128]{1,0:T(8,128)}, u32[]{:S(2)}) copy-start(f32[128,128]{1,0:T(8,128)} %param.24) | copy-start | bytes 196612
  71.5 136.6 %reduce-scatter.7.cloned.1.call-start = ((), (), s32[]{:S(2)}) async-start(), calls=%async_computation.5 | async-start | bytes 327680 | tf_op jit(solution)/shard_map/reduce_scatter | solution.py:98
  188.9 84.8 %reduce-scatter.11.cloned.1.call-start = ((), (), s32[]{:S(2)}) async-start(), calls=%async_computation.7 | async-start | bytes 589824 | tf_op jit(solution)/shard_map/reduce_scatter | solution.py:106
  198.8 74.9 %copy-start.7 = (f32[128,128]{1,0:T(8,128)S(1)}, f32[128,128]{1,0:T(8,128)}, u32[]{:S(2)}) copy-start(f32[128,128]{1,0:T(8,128)} %reduce-scatter.9.cloned.1.call-done) | copy-start | bytes 196612
Sparse Core Ops, SparseCore 0:
  54.5 20.9 reduce-scatter.4
  79.2 61.9 reduce-scatter.8
  189.0 19.0 reduce-scatter.6
  211.6 61.9 reduce-scatter.10
where the time goes:
time: 282 us
  waiting for transfers between devices  144 us (51%)
  blocking collectives  76.1 us (27%)
  local copies, waits for them, and re-layouts  22.2 us (8%)
  other arithmetic  17.6 us (6%)
  between operations  14.6 us (5%)
  matrix products  7.17 us (3%)
    reduce_scatter x2, waiting for transfers between devices, finish_adjoint(): lax.psum_scatter(partial_value.reshape(col_tiles * tile_size, features),...  131 us
    all_gather x2, blocking collectives, gather_panel(): gathered = lax.all_gather(local_part, 'rows', axis=0, tiled=True)  65.2 us
    reduce_scatter x2, waiting for transfers between devices, finish_forward(): lax.psum_scatter(partial_value.reshape(row_tiles * tile_size, features),...  12.4 us
    all_gather x2, blocking collectives, gather_block(): gathered = lax.all_gather(local_part, 'cols', axis=0, tiled=True)  10.9 us
    gather x4, local copies, waits for them, and re-layouts, advance(): values = jnp.take(tile_data, where_at, axis=0)  6.24 us
  transfers between devices with their start and end apart: 4, of which 4 were waited for; matrix products, arithmetic and copies ran while one was open for 8% of the time, Pallas kernels for 0%

commit v1 on v0

v1 whole, which is shorter than its diff:
```python
import jax
import jax.numpy as jnp
from jax import lax
from jax.experimental import pallas as pl
from jax.experimental.pallas import tpu as pltpu
from jax.sharding import PartitionSpec as P

VMEM_LIMIT = 48 * 1024 * 1024
BF16 = jnp.bfloat16
F32 = jnp.float32


def vmem():
    return pl.BlockSpec(memory_space=pltpu.VMEM)


def smem():
    return pl.BlockSpec(memory_space=pltpu.SMEM)


def call(body, outs, in_specs, args, flops, name, scratch=()):
    nbytes = sum(a.size * a.dtype.itemsize for a in (*args, *outs))
    return pl.pallas_call(
        body,
        out_shape=outs,
        in_specs=in_specs,
        out_specs=[vmem()] * len(outs),
        scratch_shapes=list(scratch),
        compiler_params=pltpu.CompilerParams(vmem_limit_bytes=VMEM_LIMIT),
        cost_estimate=pl.CostEstimate(flops=flops, bytes_accessed=nbytes, transcendentals=0),
        name=name,
    )(*args)


def rate_row(types_ref, teleport_ref):
    types = types_ref[...]
    rate = jnp.zeros(types.shape, F32)
    for t in range(teleport_ref.shape[0]):
        rate = jnp.where(types == t, teleport_ref[t], rate)
    return rate


def rate_column(row, width):
    size = row.shape[1]
    return jnp.broadcast_to(row, (width, size)).T


def start_body(h_ref, cot_ref, types_ref, teleport_ref, p_ref, q_ref):
    rate = rate_row(types_ref, teleport_ref)
    p_ref[...] = h_ref[...].astype(BF16)
    q_ref[...] = ((1.0 - rate) * cot_ref[...].T).astype(BF16)


def dense_body(rows, cols, local_tiles, tiles_ref, row_ref, col_ref, count_ref, dense_ref):
    size = tiles_ref.shape[-1]
    me_row = lax.axis_index("rows")
    me_col = lax.axis_index("cols")
    dense_ref[...] = jnp.zeros_like(dense_ref)

    def place(slot, carry):
        row = row_ref[0, 0, slot] ^ me_col
        col = col_ref[0, 0, slot] ^ me_row
        dense_ref[
            pl.ds(pl.multiple_of(row * size, size), size),
            pl.ds(pl.multiple_of(col * size, size), size),
        ] = tiles_ref[0, 0, slot]
        return carry

    lax.fori_loop(0, count_ref[0, 0], place, 0)


def forward_body(n_rows, n_cols, dense_ref, *refs):
    panels, outs = refs[:n_rows], refs[n_rows:]
    size = panels[0].shape[0]
    total = None
    step = 2 if n_rows % 2 == 0 else 1
    for s in range(0, n_rows, step):
        panel = jnp.concatenate([panels[s + e][...] for e in range(step)], axis=0)
        part = jnp.dot(
            dense_ref[:, s * size : (s + step) * size], panel, preferred_element_type=F32
        )
        total = part if total is None else total + part
    for j in range(n_cols):
        outs[j][...] = total[j * size : (j + 1) * size].astype(outs[j].dtype)


def adjoint_body(n_rows, n_cols, dense_ref, *refs):
    blocks, outs = refs[:n_cols], refs[n_cols:]
    size = blocks[0].shape[1]
    left = jnp.concatenate([b[...] for b in blocks], axis=1)
    step = 2 if n_rows % 2 == 0 else 1
    for s in range(0, n_rows, step):
        part = jnp.dot(
            left, dense_ref[:, s * size : (s + step) * size], preferred_element_type=F32
        )
        for e in range(step):
            outs[s + e][...] = part[:, e * size : (e + 1) * size].astype(outs[s + e].dtype)


def sum_refs(refs):
    terms = [ref[...].astype(F32) for ref in refs]
    while len(terms) > 1:
        terms = [sum(terms[i : i + 2][1:], terms[i]) for i in range(0, len(terms), 2)]
    return terms[0]


def forward_end_body(h_ref, types_ref, teleport_ref, *refs):
    *parts, out_ref = refs
    rate = rate_column(rate_row(types_ref, teleport_ref), h_ref.shape[1])
    value = (1.0 - rate) * sum_refs(parts) + rate * h_ref[...]
    out_ref[...] = value.astype(out_ref.dtype)


def adjoint_mid_body(types_ref, teleport_ref, *refs):
    *parts, d_ref, q_ref = refs
    rate = rate_row(types_ref, teleport_ref)
    total = sum_refs(parts)
    d_ref[...] = total
    q_ref[...] = ((1.0 - rate) * total).astype(BF16)


def adjoint_end_body(cot_ref, d_ref, types_ref, teleport_ref, *refs):
    *parts, out_ref = refs
    rate = rate_row(types_ref, teleport_ref)
    column = rate_column(rate, cot_ref.shape[1])
    out_ref[...] = column * cot_ref[...] + (rate * d_ref[...] + sum_refs(parts)).T


def swap(values, axis, count):
    return [values[0]] + [
        lax.ppermute(values[s], axis, [(i, i ^ s) for i in range(count)]) for s in range(1, count)
    ]


def shards(h_start, cotangent, node_type, teleport, tile_values, tile_row, tile_col, tile_count):
    n_rows = lax.axis_size("rows")
    n_cols = lax.axis_size("cols")
    size = tile_values.shape[-1]
    features = h_start.shape[-1]
    types = node_type.reshape(1, size)
    hop_flops = 2 * n_rows * n_cols * size * size * features

    def shape(kind, rows=size, columns=features):
        return jax.ShapeDtypeStruct((rows, columns), kind)

    p0, q0 = call(
        start_body,
        [shape(BF16), shape(BF16, features, size)],
        [vmem(), vmem(), vmem(), smem()],
        (h_start, cotangent, types, teleport),
        0,
        "start",
    )
    (dense,) = call(
        lambda *refs: dense_body(n_rows, n_cols, 1, *refs),
        [shape(BF16, n_cols * size, n_rows * size)],
        [vmem(), smem(), smem(), smem()],
        (tile_values, tile_row, tile_col, tile_count),
        0,
        "dense",
    )

    def forward_hop(part, kind):
        panels = swap([part] * n_rows, "rows", n_rows)
        sums = call(
            lambda *refs: forward_body(n_rows, n_cols, *refs),
            [shape(kind)] * n_cols,
            [vmem()] * (1 + n_rows),
            (dense, *panels),
            hop_flops,
            "forward",
        )
        return swap(sums, "cols", n_cols)

    def adjoint_hop(part, kind):
        blocks = swap([part] * n_cols, "cols", n_cols)
        sums = call(
            lambda *refs: adjoint_body(n_rows, n_cols, *refs),
            [shape(kind, features, size)] * n_rows,
            [vmem()] * (1 + n_cols),
            (dense, *blocks),
            hop_flops,
            "adjoint",
        )
        return swap(sums, "rows", n_rows)

    def forward_end(parts, kind):
        return call(
            forward_end_body,
            [shape(kind)],
            [vmem(), vmem(), smem()] + [vmem()] * n_cols,
            (h_start, types, teleport, *parts),
            0,
            "forward_end",
        )[0]

    first = forward_hop(p0, F32)
    back = adjoint_hop(q0, F32)
    p1 = forward_end(first, BF16)
    d1, q1 = call(
        adjoint_mid_body,
        [shape(F32, features, size), shape(BF16, features, size)],
        [vmem(), smem()] + [vmem()] * n_rows,
        (types, teleport, *back),
        0,
        "adjoint_mid",
    )
    second = forward_hop(p1, F32)
    back_two = adjoint_hop(q1, F32)
    propagated = forward_end(second, F32)
    (input_grad,) = call(
        adjoint_end_body,
        [shape(F32)],
        [vmem(), vmem(), vmem(), smem()] + [vmem()] * n_rows,
        (cotangent, d1, types, teleport, *back_two),
        0,
        "adjoint_end",
    )
    return propagated, input_grad


def solution(mesh):
    placed = (
        P(("rows", "cols"), None),
        P(("rows", "cols"), None),
        P(("rows", "cols")),
        P(),
        P("rows", "cols", None, None, None),
        P("rows", "cols", None),
        P("rows", "cols", None),
        P("rows", "cols"),
    )
    return jax.shard_map(
        shards,
        mesh=mesh,
        in_specs=placed,
        out_specs=(P(("rows", "cols"), None), P(("rows", "cols"), None)),
        check_vma=False,
    )
```

time: 282 us -> 75.1 us (0.27)
  waiting for transfers between devices: 144 us -> 11.1 us
  blocking collectives: 76.1 us -> 0 us
  starting transfers between devices: 0.16 us -> 52.1 us
  local copies, waits for them, and re-layouts: 22.2 us -> 3.48 us
  other arithmetic: 17.6 us -> 0 us
  between operations: 14.6 us -> 1.47 us
  matrix products: 7.17 us -> 0 us
  Pallas kernels: 0 us -> 6.67 us
    reduce_scatter x4 -> x0, waiting for transfers between devices: 144 us -> none  [the longest x2 131 us: finish_adjoint(): lax.psum_scatter(partial_value.reshape(col_tiles * tile_size, features),...]
    all_gather x4 -> x0, blocking collectives: 76.1 us -> none  [the longest x2 65.2 us: gather_panel(): gathered = lax.all_gather(local_part, 'rows', axis=0, tiled=True)]
    ppermute x0 -> x40, starting transfers between devices: none -> 52.1 us  [swap(): lax.ppermute(values[s], axis, [(i, i ^ s) for i in range(count)])]
    gather x16 -> x0, local copies, waits for them, and re-layouts: 18.9 us -> none  [the longest x4 6.24 us: advance(): values = jnp.take(tile_data, where_at, axis=0)]
    ppermute x0 -> x40, waiting for transfers between devices: none -> 11.1 us  [swap(): lax.ppermute(values[s], axis, [(i, i ^ s) for i in range(count)])]
    scatter-add x4 -> x0, other arithmetic: 10.5 us -> none  [the longest x2 5.25 us: advance(): updated[-1] = totals[-1].at[segment].add(product)]
    dot_general x4 -> x0, matrix products: 7.17 us -> none  [the longest x2 3.76 us: advance(): jnp.einsum('sji,sjf->sif', values, fetched, preferred_element_type=jnp.fl...]
    pallas_call x0 -> x10, Pallas kernels: none -> 6.67 us  [call(): pl.pallas_call(body, out_shape=outs, in_specs=in_specs, out_specs=[vmem()...]
  transfers between devices with their start and end apart: 4 -> 40, of which waited for: 4 -> 6; matrix products, arithmetic and copies ran while one was open for 8% -> 0% of each run, Pallas kernels for 0% -> 6%
where the time goes in v1:
time: 75.1 us; the launch traced here: 74.9 us
  starting transfers between devices  52.1 us (69%)
  waiting for transfers between devices  11.1 us (15%)
  Pallas kernels  6.67 us (9%)
  local copies, waits for them, and re-layouts  3.48 us (5%)
  between operations  1.47 us (2%)
    ppermute x40, starting transfers between devices, swap(): lax.ppermute(values[s], axis, [(i, i ^ s) for i in range(count)])  52.1 us
    ppermute x40, waiting for transfers between devices, swap(): lax.ppermute(values[s], axis, [(i, i ^ s) for i in range(count)])  11.1 us
    pallas_call x10, Pallas kernels, call(): pl.pallas_call(body, out_shape=outs, in_specs=in_specs, out_specs=[vmem()...  6.67 us
    unnamed x18, local copies, waits for them, and re-layouts  3.48 us
  transfers between devices with their start and end apart: 40, of which 6 were waited for; matrix products, arithmetic and copies ran while one was open for 0% of the time, Pallas kernels for 6%

profile of v1, /device:TPU:0, one launch (start us, length us, event | category | flops | bytes accessed | tf_op | source)
XLA Modules:
  0.0 74.9 jit_solution(7563649077810635800)
XLA Ops:
  0.6 0.6 copy-done.5
  1.3 0.8 %copy-done.1 = f32[128,128]{1,0:T(8,128)S(1)} copy-done((f32[128,128]{1,0:T(8,128)S(1)}, f32[128,128]{1,0:T(8,128)}, u32[]{:S(2)}) %copy-start.1) | copy-done | bytes 65560
  2.1 0.8 %copy-done.3 = f32[128,128]{1,0:T(8,128)S(1)} copy-done((f32[128,128]{1,0:T(8,128)S(1)}, f32[128,128]{1,0:T(8,128)}, u32[]{:S(2)}) %copy-start.3) | copy-done | bytes 65560
  3.0 0.6 start.1
  3.6 0.5 collective-permute-start.20
  4.1 2.6 %collective-permute-start.21 = (bf16[128,128]{1,0:T(8,128)(2,1)S(1)}, bf16[128,128]{1,0:T(8,128)(2,1)S(1)}, u32[]{:S(2)}, u32[]{:S(2)}) collective-permute-start(bf16[128,128]{1,0:T(8,128)(2,1)S(1)} %get-tuple-element.39.refs_1_), channel_id=1, source_target_pairs={{0,2},{1,3},{2,0},{3,1},{4,6},{5,7},{6,4},{7,5},{8,10},{9,11},{10,... | collective-permute-start | bytes 98312 | tf_op jit(solution)/shard_map/ppermute | solution.py:131
  6.8 1.8 %collective-permute-start = (bf16[128,128]{1,0:T(8,128)(2,1)S(1)}, bf16[128,128]{1,0:T(8,128)(2,1)S(1)}, u32[]{:S(2)}, u32[]{:S(2)}) collective-permute-start(bf16[128,128]{1,0:T(8,128)(2,1)S(1)} %get-tuple-element.30.refs_1_), channel_id=1, source_target_pairs={{0,4},{4,0},{8,12},{12,8},{16,20},{20,16},{24,28},{28,24},{1,5},{5... | collective-permute-start | bytes 98312 | tf_op jit(solution)/shard_map/ppermute | solution.py:131
  8.5 1.6 %collective-permute-start.1 = (bf16[128,128]{1,0:T(8,128)(2,1)S(1)}, bf16[128,128]{1,0:T(8,128)(2,1)S(1)}, u32[]{:S(2)}, u32[]{:S(2)}) collective-permute-start(bf16[128,128]{1,0:T(8,128)(2,1)S(1)} %get-tuple-element.30.refs_1_), channel_id=1, source_target_pairs={{0,8},{4,12},{8,0},{12,4},{16,24},{20,28},{24,16},{28,20},{1,9},{5... | collective-permute-start | bytes 98312 | tf_op jit(solution)/shard_map/ppermute | solution.py:131
  10.3 2.8 %collective-permute-start.3 = (bf16[128,128]{1,0:T(8,128)(2,1)S(1)}, bf16[128,128]{1,0:T(8,128)(2,1)S(1)}, u32[]{:S(2)}, u32[]{:S(2)}) collective-permute-start(bf16[128,128]{1,0:T(8,128)(2,1)S(1)} %get-tuple-element.30.refs_1_), channel_id=1, source_target_pairs={{0,16},{4,20},{8,24},{12,28},{16,0},{20,4},{24,8},{28,12},{1,17},{... | collective-permute-start | bytes 98312 | tf_op jit(solution)/shard_map/ppermute | solution.py:131
  13.1 1.3 %collective-permute-start.4 = (bf16[128,128]{1,0:T(8,128)(2,1)S(1)}, bf16[128,128]{1,0:T(8,128)(2,1)S(1)}, u32[]{:S(2)}, u32[]{:S(2)}) collective-permute-start(bf16[128,128]{1,0:T(8,128)(2,1)S(1)} %get-tuple-element.30.refs_1_), channel_id=1, source_target_pairs={{0,20},{4,16},{8,28},{12,24},{16,4},{20,0},{24,12},{28,8},{1,21},{... | collective-permute-start | bytes 98312 | tf_op jit(solution)/shard_map/ppermute | solution.py:131
  14.4 3.6 %collective-permute-start.5 = (bf16[128,128]{1,0:T(8,128)(2,1)S(1)}, bf16[128,128]{1,0:T(8,128)(2,1)S(1)}, u32[]{:S(2)}, u32[]{:S(2)}) collective-permute-start(bf16[128,128]{1,0:T(8,128)(2,1)S(1)} %get-tuple-element.30.refs_1_), channel_id=1, source_target_pairs={{0,24},{4,28},{8,16},{12,20},{16,8},{20,12},{24,0},{28,4},{1,25},{... | collective-permute-start | bytes 98312 | tf_op jit(solution)/shard_map/ppermute | solution.py:131
  18.7 1.1 %copy-done = bf16[1,1,24,128,128]{4,3,2,1,0:T(8,128)(2,1)S(1)} copy-done((bf16[1,1,24,128,128]{4,3,2,1,0:T(8,128)(2,1)S(1)}, bf16[1,1,24,128,128]{4,3,2,1,0:T(8,128)(2,1)}, u32[]{:S(2)}) %copy-start) | copy-done | bytes 786456
  19.8 0.7 dense.1.refs_0_
  20.6 0.3 adjoint.2
  20.9 1.8 %collective-permute-start.23 = (f32[128,128]{1,0:T(8,128)S(1)}, f32[128,128]{1,0:T(8,128)S(1)}, u32[]{:S(2)}, u32[]{:S(2)}) collective-permute-start(f32[128,128]{1,0:T(8,128)S(1)} %get-tuple-element.41), channel_id=1, source_target_pairs={{0,4},{4,0},{8,12},{12,8},{16,20},{20,16},{24,28},{28,24},{1,5},{5... | collective-permute-start | bytes 196616 | tf_op jit(solution)/shard_map/ppermute | solution.py:131
  22.7 1.8 %collective-permute-start.25 = (f32[128,128]{1,0:T(8,128)S(1)}, f32[128,128]{1,0:T(8,128)S(1)}, u32[]{:S(2)}, u32[]{:S(2)}) collective-permute-start(f32[128,128]{1,0:T(8,128)S(1)} %get-tuple-element.43), channel_id=1, source_target_pairs={{0,12},{4,8},{8,4},{12,0},{16,28},{20,24},{24,20},{28,16},{1,13},{... | collective-permute-start | bytes 196616 | tf_op jit(solution)/shard_map/ppermute | solution.py:131
  24.5 2.5 %collective-permute-start.26 = (f32[128,128]{1,0:T(8,128)S(1)}, f32[128,128]{1,0:T(8,128)S(1)}, u32[]{:S(2)}, u32[]{:S(2)}) collective-permute-start(f32[128,128]{1,0:T(8,128)S(1)} %get-tuple-element.44), channel_id=1, source_target_pairs={{0,16},{4,20},{8,24},{12,28},{16,0},{20,4},{24,8},{28,12},{1,17},{... | collective-permute-start | bytes 196616 | tf_op jit(solution)/shard_map/ppermute | solution.py:131
  27.0 1.5 %collective-permute-start.27 = (f32[128,128]{1,0:T(8,128)S(1)}, f32[128,128]{1,0:T(8,128)S(1)}, u32[]{:S(2)}, u32[]{:S(2)}) collective-permute-start(f32[128,128]{1,0:T(8,128)S(1)} %get-tuple-element.45), channel_id=1, source_target_pairs={{0,20},{4,16},{8,28},{12,24},{16,4},{20,0},{24,12},{28,8},{1,21},{... | collective-permute-start | bytes 196616 | tf_op jit(solution)/shard_map/ppermute | solution.py:131
  28.5 0.4 forward.2
  29.0 3.7 %collective-permute-start.28 = (f32[128,128]{1,0:T(8,128)S(1)}, f32[128,128]{1,0:T(8,128)S(1)}, u32[]{:S(2)}, u32[]{:S(2)}) collective-permute-start(f32[128,128]{1,0:T(8,128)S(1)} %get-tuple-element.46), channel_id=1, source_target_pairs={{0,24},{4,28},{8,16},{12,20},{16,8},{20,12},{24,0},{28,4},{1,25},{... | collective-permute-start | bytes 196616 | tf_op jit(solution)/shard_map/ppermute | solution.py:131
  32.8 1.6 %collective-permute-start.8 = (f32[128,128]{1,0:T(8,128)S(1)}, f32[128,128]{1,0:T(8,128)S(1)}, u32[]{:S(2)}, u32[]{:S(2)}) collective-permute-start(f32[128,128]{1,0:T(8,128)S(1)} %get-tuple-element.33), channel_id=1, source_target_pairs={{0,2},{1,3},{2,0},{3,1},{4,6},{5,7},{6,4},{7,5},{8,10},{9,11},{10,... | collective-permute-start | bytes 196616 | tf_op jit(solution)/shard_map/ppermute | solution.py:131
  34.4 2.7 %collective-permute-done.27.refs_5_ = f32[128,128]{1,0:T(8,128)S(1)} collective-permute-done((f32[128,128]{1,0:T(8,128)S(1)}, f32[128,128]{1,0:T(8,128)S(1)}, u32[]{:S(2)}, u32[]{:S(2)}) %collective-permute-start.27) | collective-permute-done | bytes 65568 | tf_op jit(solution)/shard_map/ppermute | solution.py:131
  37.1 2.5 %collective-permute-done.29.refs_7_ = f32[128,128]{1,0:T(8,128)S(1)} collective-permute-done((f32[128,128]{1,0:T(8,128)S(1)}, f32[128,128]{1,0:T(8,128)S(1)}, u32[]{:S(2)}, u32[]{:S(2)}) %collective-permute-start.29) | collective-permute-done | bytes 65568 | tf_op jit(solution)/shard_map/ppermute | solution.py:131
  39.6 0.6 adjoint_mid.1
  40.3 1.5 %collective-permute-start.31 = (bf16[128,128]{1,0:T(8,128)(2,1)S(1)}, bf16[128,128]{1,0:T(8,128)(2,1)S(1)}, u32[]{:S(2)}, u32[]{:S(2)}) collective-permute-start(bf16[128,128]{1,0:T(8,128)(2,1)S(1)} %get-tuple-element.49.refs_1_), channel_id=1, source_target_pairs={{0,2},{1,3},{2,0},{3,1},{4,6},{5,7},{6,4},{7,5},{8,10},{9,11},{10,... | collective-permute-start | bytes 98312 | tf_op jit(solution)/shard_map/ppermute | solution.py:131
  41.8 0.4 collective-permute-start.32
  42.1 0.7 forward_end.2.refs_1_
  42.8 0.7 collective-permute-start.10
  43.5 2.8 %collective-permute-start.12 = (bf16[128,128]{1,0:T(8,128)(2,1)S(1)}, bf16[128,128]{1,0:T(8,128)(2,1)S(1)}, u32[]{:S(2)}, u32[]{:S(2)}) collective-permute-start(bf16[128,128]{1,0:T(8,128)(2,1)S(1)} %forward_end.2.refs_1_), channel_id=1, source_target_pairs={{0,12},{4,8},{8,4},{12,0},{16,28},{20,24},{24,20},{28,16},{1,13},{... | collective-permute-start | bytes 98312 | tf_op jit(solution)/shard_map/ppermute | solution.py:131
  46.4 0.7 collective-permute-start.13
  47.1 2.3 %collective-permute-start.14 = (bf16[128,128]{1,0:T(8,128)(2,1)S(1)}, bf16[128,128]{1,0:T(8,128)(2,1)S(1)}, u32[]{:S(2)}, u32[]{:S(2)}) collective-permute-start(bf16[128,128]{1,0:T(8,128)(2,1)S(1)} %forward_end.2.refs_1_), channel_id=1, source_target_pairs={{0,20},{4,16},{8,28},{12,24},{16,4},{20,0},{24,12},{28,8},{1,21},{... | collective-permute-start | bytes 98312 | tf_op jit(solution)/shard_map/ppermute | solution.py:131
  49.4 0.9 %collective-permute-start.15 = (bf16[128,128]{1,0:T(8,128)(2,1)S(1)}, bf16[128,128]{1,0:T(8,128)(2,1)S(1)}, u32[]{:S(2)}, u32[]{:S(2)}) collective-permute-start(bf16[128,128]{1,0:T(8,128)(2,1)S(1)} %forward_end.2.refs_1_), channel_id=1, source_target_pairs={{0,24},{4,28},{8,16},{12,20},{16,8},{20,12},{24,0},{28,4},{1,25},{... | collective-permute-start | bytes 98312 | tf_op jit(solution)/shard_map/ppermute | solution.py:131
  50.3 3.7 %collective-permute-start.16 = (bf16[128,128]{1,0:T(8,128)(2,1)S(1)}, bf16[128,128]{1,0:T(8,128)(2,1)S(1)}, u32[]{:S(2)}, u32[]{:S(2)}) collective-permute-start(bf16[128,128]{1,0:T(8,128)(2,1)S(1)} %forward_end.2.refs_1_), channel_id=1, source_target_pairs={{0,28},{4,24},{8,20},{12,16},{16,12},{20,8},{24,4},{28,0},{1,29},{... | collective-permute-start | bytes 98312 | tf_op jit(solution)/shard_map/ppermute | solution.py:131
  54.0 0.3 adjoint.3
  54.3 0.7 collective-permute-start.33
  55.1 0.2 collective-permute-done.15.refs_7_
  55.3 1.7 %collective-permute-done.16.refs_8_ = bf16[128,128]{1,0:T(8,128)(2,1)S(1)} collective-permute-done((bf16[128,128]{1,0:T(8,128)(2,1)S(1)}, bf16[128,128]{1,0:T(8,128)(2,1)S(1)}, u32[]{:S(2)}, u32[]{:S(2)}) %collective-permute-start.16) | collective-permute-done | bytes 32800 | tf_op jit(solution)/shard_map/ppermute | solution.py:131
  57.0 0.4 forward.3
  57.6 1.2 %collective-permute-start.18 = (f32[128,128]{1,0:T(8,128)S(1)}, f32[128,128]{1,0:T(8,128)S(1)}, u32[]{:S(2)}, u32[]{:S(2)}) collective-permute-start(f32[128,128]{1,0:T(8,128)S(1)} %get-tuple-element.37), channel_id=1, source_target_pairs={{0,2},{1,3},{2,0},{3,1},{4,6},{5,7},{6,4},{7,5},{8,10},{9,11},{10,... | collective-permute-start | bytes 196616 | tf_op jit(solution)/shard_map/ppermute | solution.py:131
  58.8 0.7 collective-permute-start.19
  59.4 0.9 %collective-permute-start.35 = (f32[128,128]{1,0:T(8,128)S(1)}, f32[128,128]{1,0:T(8,128)S(1)}, u32[]{:S(2)}, u32[]{:S(2)}) collective-permute-start(f32[128,128]{1,0:T(8,128)S(1)} %get-tuple-element.53), channel_id=1, source_target_pairs={{0,12},{4,8},{8,4},{12,0},{16,28},{20,24},{24,20},{28,16},{1,13},{... | collective-permute-start | bytes 196616 | tf_op jit(solution)/shard_map/ppermute | solution.py:131
  60.3 3.3 %collective-permute-start.36 = (f32[128,128]{1,0:T(8,128)S(1)}, f32[128,128]{1,0:T(8,128)S(1)}, u32[]{:S(2)}, u32[]{:S(2)}) collective-permute-start(f32[128,128]{1,0:T(8,128)S(1)} %get-tuple-element.54), channel_id=1, source_target_pairs={{0,16},{4,20},{8,24},{12,28},{16,0},{20,4},{24,8},{28,12},{1,17},{... | collective-permute-start | bytes 196616 | tf_op jit(solution)/shard_map/ppermute | solution.py:131
  63.9 2.2 %collective-permute-start.38 = (f32[128,128]{1,0:T(8,128)S(1)}, f32[128,128]{1,0:T(8,128)S(1)}, u32[]{:S(2)}, u32[]{:S(2)}) collective-permute-start(f32[128,128]{1,0:T(8,128)S(1)} %get-tuple-element.56), channel_id=1, source_target_pairs={{0,24},{4,28},{8,16},{12,20},{16,8},{20,12},{24,0},{28,4},{1,25},{... | collective-permute-start | bytes 196616 | tf_op jit(solution)/shard_map/ppermute | solution.py:131
  66.1 2.4 %collective-permute-start.39 = (f32[128,128]{1,0:T(8,128)S(1)}, f32[128,128]{1,0:T(8,128)S(1)}, u32[]{:S(2)}, u32[]{:S(2)}) collective-permute-start(f32[128,128]{1,0:T(8,128)S(1)} %get-tuple-element.57), channel_id=1, source_target_pairs={{0,28},{4,24},{8,20},{12,16},{16,12},{20,8},{24,4},{28,0},{1,29},{... | collective-permute-start | bytes 196616 | tf_op jit(solution)/shard_map/ppermute | solution.py:131
  68.4 1.3 %forward_end.3 = f32[128,128]{1,0:T(8,128)} custom-call(f32[128,128]{1,0:T(8,128)S(1)} %copy-done.2, s32[1,128]{1,0:T(1,128)S(1)} %bitcast.4, f32[8]{0:T(128)S(1)} %copy-done.6, f32[128,128]{1,0:T(8,128)S(1)} %get-tuple-element.35.refs_0_, f32[128,128]{1,0:T(8,128)S(1)} %collective-permute-done.17.refs_1_, f32[128,128]{1,0:T(8,128)S(1)} %collective-permute-done.18.refs_2_, ...), custom_call_target="tpu_custom_call" | custom-call | bytes 393760 | tf_op jit(solution)/shard_map/forward_end/pallas_call | solution.py:23
  69.7 1.3 %collective-permute-done.36.refs_4_ = f32[128,128]{1,0:T(8,128)S(1)} collective-permute-done((f32[128,128]{1,0:T(8,128)S(1)}, f32[128,128]{1,0:T(8,128)S(1)}, u32[]{:S(2)}, u32[]{:S(2)}) %collective-permute-start.36) | collective-permute-done | bytes 65568 | tf_op jit(solution)/shard_map/ppermute | solution.py:131
  71.0 2.6 %collective-permute-done.37.refs_5_ = f32[128,128]{1,0:T(8,128)S(1)} collective-permute-done((f32[128,128]{1,0:T(8,128)S(1)}, f32[128,128]{1,0:T(8,128)S(1)}, u32[]{:S(2)}, u32[]{:S(2)}) %collective-permute-start.37) | collective-permute-done | bytes 65568 | tf_op jit(solution)/shard_map/ppermute | solution.py:131
  73.6 1.3 %adjoint_end.1 = f32[128,128]{1,0:T(8,128)} custom-call(f32[128,128]{1,0:T(8,128)S(1)} %copy-done.4, f32[128,128]{1,0:T(8,128)S(1)} %get-tuple-element.48.d_ref, s32[1,128]{1,0:T(1,128)S(1)} %bitcast.5, f32[8]{0:T(128)S(1)} %copy-done.6, f32[128,128]{1,0:T(8,128)S(1)} %get-tuple-element.50.refs_0_, f32[128,128]{1,0:T(8,128)S(1)} %collective-permute-done.33.refs_1_, ...), custom_call_target="tpu_custom_call" | custom-call | bytes 721440 | tf_op jit(solution)/shard_map/adjoint_end/pallas_call | solution.py:23
  (60 shorter events, 0.9 us)
Async XLA Ops:
  0.6 0.7 copy-start.6
  1.3 0.8 %copy-start.1 = (f32[128,128]{1,0:T(8,128)S(1)}, f32[128,128]{1,0:T(8,128)}, u32[]{:S(2)}) copy-start(f32[128,128]{1,0:T(8,128)} %h_ref.5) | copy-start | bytes 196612
  2.1 0.8 %copy-start.3 = (f32[128,128]{1,0:T(8,128)S(1)}, f32[128,128]{1,0:T(8,128)}, u32[]{:S(2)}) copy-start(f32[128,128]{1,0:T(8,128)} %cot_ref.3) | copy-start | bytes 196612
  3.6 6.5 %collective-permute-start.20 = (bf16[128,128]{1,0:T(8,128)(2,1)S(1)}, bf16[128,128]{1,0:T(8,128)(2,1)S(1)}, u32[]{:S(2)}, u32[]{:S(2)}) collective-permute-start(bf16[128,128]{1,0:T(8,128)(2,1)S(1)} %get-tuple-element.39.refs_1_), channel_id=1, source_target_pairs={{0,1},{1,0},{2,3},{3,2},{4,5},{5,4},{6,7},{7,6},{8,9},{9,8},{10,11... | collective-permute-start | bytes 98312 | tf_op jit(solution)/shard_map/ppermute | solution.py:131
  4.1 6.1 %collective-permute-start.21 = (bf16[128,128]{1,0:T(8,128)(2,1)S(1)}, bf16[128,128]{1,0:T(8,128)(2,1)S(1)}, u32[]{:S(2)}, u32[]{:S(2)}) collective-permute-start(bf16[128,128]{1,0:T(8,128)(2,1)S(1)} %get-tuple-element.39.refs_1_), channel_id=1, source_target_pairs={{0,2},{1,3},{2,0},{3,1},{4,6},{5,7},{6,4},{7,5},{8,10},{9,11},{10,... | collective-permute-start | bytes 98312 | tf_op jit(solution)/shard_map/ppermute | solution.py:131
  6.7 6.4 %collective-permute-start.22 = (bf16[128,128]{1,0:T(8,128)(2,1)S(1)}, bf16[128,128]{1,0:T(8,128)(2,1)S(1)}, u32[]{:S(2)}, u32[]{:S(2)}) collective-permute-start(bf16[128,128]{1,0:T(8,128)(2,1)S(1)} %get-tuple-element.39.refs_1_), channel_id=1, source_target_pairs={{0,3},{1,2},{2,1},{3,0},{4,7},{5,6},{6,5},{7,4},{8,11},{9,10},{10,... | collective-permute-start | bytes 98312 | tf_op jit(solution)/shard_map/ppermute | solution.py:131
  6.8 11.9 %copy-start.7 = (s32[1,1,24]{2,1,0:T(1,128)S(1)}, s32[1,1,24]{2,1,0:T(1,128)}, u32[]{:S(2)}) copy-start(s32[1,1,24]{2,1,0:T(1,128)} %refs_1_.1) | copy-start | bytes 292
  6.8 11.9 %copy-start.8 = (s32[1,1,24]{2,1,0:T(1,128)S(1)}, s32[1,1,24]{2,1,0:T(1,128)}, u32[]{:S(2)}) copy-start(s32[1,1,24]{2,1,0:T(1,128)} %refs_2_.1) | copy-start | bytes 292
  6.8 7.6 %collective-permute-start = (bf16[128,128]{1,0:T(8,128)(2,1)S(1)}, bf16[128,128]{1,0:T(8,128)(2,1)S(1)}, u32[]{:S(2)}, u32[]{:S(2)}) collective-permute-start(bf16[128,128]{1,0:T(8,128)(2,1)S(1)} %get-tuple-element.30.refs_1_), channel_id=1, source_target_pairs={{0,4},{4,0},{8,12},{12,8},{16,20},{20,16},{24,28},{28,24},{1,5},{5... | collective-permute-start | bytes 98312 | tf_op jit(solution)/shard_map/ppermute | solution.py:131
  8.5 9.5 %collective-permute-start.1 = (bf16[128,128]{1,0:T(8,128)(2,1)S(1)}, bf16[128,128]{1,0:T(8,128)(2,1)S(1)}, u32[]{:S(2)}, u32[]{:S(2)}) collective-permute-start(bf16[128,128]{1,0:T(8,128)(2,1)S(1)} %get-tuple-element.30.refs_1_), channel_id=1, source_target_pairs={{0,8},{4,12},{8,0},{12,4},{16,24},{20,28},{24,16},{28,20},{1,9},{5... | collective-permute-start | bytes 98312 | tf_op jit(solution)/shard_map/ppermute | solution.py:131
  10.1 10.8 %collective-permute-start.2 = (bf16[128,128]{1,0:T(8,128)(2,1)S(1)}, bf16[128,128]{1,0:T(8,128)(2,1)S(1)}, u32[]{:S(2)}, u32[]{:S(2)}) collective-permute-start(bf16[128,128]{1,0:T(8,128)(2,1)S(1)} %get-tuple-element.30.refs_1_), channel_id=1, source_target_pairs={{0,12},{4,8},{8,4},{12,0},{16,28},{20,24},{24,20},{28,16},{1,13},{... | collective-permute-start | bytes 98312 | tf_op jit(solution)/shard_map/ppermute | solution.py:131
  10.3 12.4 %collective-permute-start.3 = (bf16[128,128]{1,0:T(8,128)(2,1)S(1)}, bf16[128,128]{1,0:T(8,128)(2,1)S(1)}, u32[]{:S(2)}, u32[]{:S(2)}) collective-permute-start(bf16[128,128]{1,0:T(8,128)(2,1)S(1)} %get-tuple-element.30.refs_1_), channel_id=1, source_target_pairs={{0,16},{4,20},{8,24},{12,28},{16,0},{20,4},{24,8},{28,12},{1,17},{... | collective-permute-start | bytes 98312 | tf_op jit(solution)/shard_map/ppermute | solution.py:131
  13.1 9.6 %collective-permute-start.4 = (bf16[128,128]{1,0:T(8,128)(2,1)S(1)}, bf16[128,128]{1,0:T(8,128)(2,1)S(1)}, u32[]{:S(2)}, u32[]{:S(2)}) collective-permute-start(bf16[128,128]{1,0:T(8,128)(2,1)S(1)} %get-tuple-element.30.refs_1_), channel_id=1, source_target_pairs={{0,20},{4,16},{8,28},{12,24},{16,4},{20,0},{24,12},{28,8},{1,21},{... | collective-permute-start | bytes 98312 | tf_op jit(solution)/shard_map/ppermute | solution.py:131
  14.4 10.1 %collective-permute-start.5 = (bf16[128,128]{1,0:T(8,128)(2,1)S(1)}, bf16[128,128]{1,0:T(8,128)(2,1)S(1)}, u32[]{:S(2)}, u32[]{:S(2)}) collective-permute-start(bf16[128,128]{1,0:T(8,128)(2,1)S(1)} %get-tuple-element.30.refs_1_), channel_id=1, source_target_pairs={{0,24},{4,28},{8,16},{12,20},{16,8},{20,12},{24,0},{28,4},{1,25},{... | collective-permute-start | bytes 98312 | tf_op jit(solution)/shard_map/ppermute | solution.py:131
  18.0 9.0 %collective-permute-start.6 = (bf16[128,128]{1,0:T(8,128)(2,1)S(1)}, bf16[128,128]{1,0:T(8,128)(2,1)S(1)}, u32[]{:S(2)}, u32[]{:S(2)}) collective-permute-start(bf16[128,128]{1,0:T(8,128)(2,1)S(1)} %get-tuple-element.30.refs_1_), channel_id=1, source_target_pairs={{0,28},{4,24},{8,20},{12,16},{16,12},{20,8},{24,4},{28,0},{1,29},{... | collective-permute-start | bytes 98312 | tf_op jit(solution)/shard_map/ppermute | solution.py:131
  18.7 1.1 %copy-start = (bf16[1,1,24,128,128]{4,3,2,1,0:T(8,128)(2,1)S(1)}, bf16[1,1,24,128,128]{4,3,2,1,0:T(8,128)(2,1)}, u32[]{:S(2)}) copy-start(bf16[1,1,24,128,128]{4,3,2,1,0:T(8,128)(2,1)} %refs_0_.1) | copy-start | bytes 2359300
  20.9 8.1 %collective-permute-start.23 = (f32[128,128]{1,0:T(8,128)S(1)}, f32[128,128]{1,0:T(8,128)S(1)}, u32[]{:S(2)}, u32[]{:S(2)}) collective-permute-start(f32[128,128]{1,0:T(8,128)S(1)} %get-tuple-element.41), channel_id=1, source_target_pairs={{0,4},{4,0},{8,12},{12,8},{16,20},{20,16},{24,28},{28,24},{1,5},{5... | collective-permute-start | bytes 196616 | tf_op jit(solution)/shard_map/ppermute | solution.py:131
  22.7 10.0 %collective-permute-start.24 = (f32[128,128]{1,0:T(8,128)S(1)}, f32[128,128]{1,0:T(8,128)S(1)}, u32[]{:S(2)}, u32[]{:S(2)}) collective-permute-start(f32[128,128]{1,0:T(8,128)S(1)} %get-tuple-element.42), channel_id=1, source_target_pairs={{0,8},{4,12},{8,0},{12,4},{16,24},{20,28},{24,16},{28,20},{1,9},{5... | collective-permute-start | bytes 196616 | tf_op jit(solution)/shard_map/ppermute | solution.py:131
  22.7 10.1 %collective-permute-start.25 = (f32[128,128]{1,0:T(8,128)S(1)}, f32[128,128]{1,0:T(8,128)S(1)}, u32[]{:S(2)}, u32[]{:S(2)}) collective-permute-start(f32[128,128]{1,0:T(8,128)S(1)} %get-tuple-element.43), channel_id=1, source_target_pairs={{0,12},{4,8},{8,4},{12,0},{16,28},{20,24},{24,20},{28,16},{1,13},{... | collective-permute-start | bytes 196616 | tf_op jit(solution)/shard_map/ppermute | solution.py:131
  24.5 8.4 %collective-permute-start.26 = (f32[128,128]{1,0:T(8,128)S(1)}, f32[128,128]{1,0:T(8,128)S(1)}, u32[]{:S(2)}, u32[]{:S(2)}) collective-permute-start(f32[128,128]{1,0:T(8,128)S(1)} %get-tuple-element.44), channel_id=1, source_target_pairs={{0,16},{4,20},{8,24},{12,28},{16,0},{20,4},{24,8},{28,12},{1,17},{... | collective-permute-start | bytes 196616 | tf_op jit(solution)/shard_map/ppermute | solution.py:131
  27.0 10.1 %collective-permute-start.27 = (f32[128,128]{1,0:T(8,128)S(1)}, f32[128,128]{1,0:T(8,128)S(1)}, u32[]{:S(2)}, u32[]{:S(2)}) collective-permute-start(f32[128,128]{1,0:T(8,128)S(1)} %get-tuple-element.45), channel_id=1, source_target_pairs={{0,20},{4,16},{8,28},{12,24},{16,4},{20,0},{24,12},{28,8},{1,21},{... | collective-permute-start | bytes 196616 | tf_op jit(solution)/shard_map/ppermute | solution.py:131
  29.0 8.1 %collective-permute-start.28 = (f32[128,128]{1,0:T(8,128)S(1)}, f32[128,128]{1,0:T(8,128)S(1)}, u32[]{:S(2)}, u32[]{:S(2)}) collective-permute-start(f32[128,128]{1,0:T(8,128)S(1)} %get-tuple-element.46), channel_id=1, source_target_pairs={{0,24},{4,28},{8,16},{12,20},{16,8},{20,12},{24,0},{28,4},{1,25},{... | collective-permute-start | bytes 196616 | tf_op jit(solution)/shard_map/ppermute | solution.py:131
  32.6 7.0 %collective-permute-start.29 = (f32[128,128]{1,0:T(8,128)S(1)}, f32[128,128]{1,0:T(8,128)S(1)}, u32[]{:S(2)}, u32[]{:S(2)}) collective-permute-start(f32[128,128]{1,0:T(8,128)S(1)} %get-tuple-element.47), channel_id=1, source_target_pairs={{0,28},{4,24},{8,20},{12,16},{16,12},{20,8},{24,4},{28,0},{1,29},{... | collective-permute-start | bytes 196616 | tf_op jit(solution)/shard_map/ppermute | solution.py:131
  32.8 9.0 %collective-permute-start.7 = (f32[128,128]{1,0:T(8,128)S(1)}, f32[128,128]{1,0:T(8,128)S(1)}, u32[]{:S(2)}, u32[]{:S(2)}) collective-permute-start(f32[128,128]{1,0:T(8,128)S(1)} %get-tuple-element.32), channel_id=1, source_target_pairs={{0,1},{1,0},{2,3},{3,2},{4,5},{5,4},{6,7},{7,6},{8,9},{9,8},{10,11... | collective-permute-start | bytes 196616 | tf_op jit(solution)/shard_map/ppermute | solution.py:131
  32.8 9.3 %collective-permute-start.8 = (f32[128,128]{1,0:T(8,128)S(1)}, f32[128,128]{1,0:T(8,128)S(1)}, u32[]{:S(2)}, u32[]{:S(2)}) collective-permute-start(f32[128,128]{1,0:T(8,128)S(1)} %get-tuple-element.33), channel_id=1, source_target_pairs={{0,2},{1,3},{2,0},{3,1},{4,6},{5,7},{6,4},{7,5},{8,10},{9,11},{10,... | collective-permute-start | bytes 196616 | tf_op jit(solution)/shard_map/ppermute | solution.py:131
  37.1 5.1 %collective-permute-start.9 = (f32[128,128]{1,0:T(8,128)S(1)}, f32[128,128]{1,0:T(8,128)S(1)}, u32[]{:S(2)}, u32[]{:S(2)}) collective-permute-start(f32[128,128]{1,0:T(8,128)S(1)} %get-tuple-element.34), channel_id=1, source_target_pairs={{0,3},{1,2},{2,1},{3,0},{4,7},{5,6},{6,5},{7,4},{8,11},{9,10},{10,... | collective-permute-start | bytes 196616 | tf_op jit(solution)/shard_map/ppermute | solution.py:131
  39.6 2.5 %copy-start.2 = (f32[128,128]{1,0:T(8,128)S(1)}, f32[128,128]{1,0:T(8,128)}, u32[]{:S(2)}) copy-start(f32[128,128]{1,0:T(8,128)} %h_ref.5) | copy-start | bytes 196612
  40.2 3.3 %collective-permute-start.30 = (bf16[128,128]{1,0:T(8,128)(2,1)S(1)}, bf16[128,128]{1,0:T(8,128)(2,1)S(1)}, u32[]{:S(2)}, u32[]{:S(2)}) collective-permute-start(bf16[128,128]{1,0:T(8,128)(2,1)S(1)} %get-tuple-element.49.refs_1_), channel_id=1, source_target_pairs={{0,1},{1,0},{2,3},{3,2},{4,5},{5,4},{6,7},{7,6},{8,9},{9,8},{10,11... | collective-permute-start | bytes 98312 | tf_op jit(solution)/shard_map/ppermute | solution.py:131
  40.3 6.1 %collective-permute-start.31 = (bf16[128,128]{1,0:T(8,128)(2,1)S(1)}, bf16[128,128]{1,0:T(8,128)(2,1)S(1)}, u32[]{:S(2)}, u32[]{:S(2)}) collective-permute-start(bf16[128,128]{1,0:T(8,128)(2,1)S(1)} %get-tuple-element.49.refs_1_), channel_id=1, source_target_pairs={{0,2},{1,3},{2,0},{3,1},{4,6},{5,7},{6,4},{7,5},{8,10},{9,11},{10,... | collective-permute-start | bytes 98312 | tf_op jit(solution)/shard_map/ppermute | solution.py:131
  41.8 5.3 %collective-permute-start.32 = (bf16[128,128]{1,0:T(8,128)(2,1)S(1)}, bf16[128,128]{1,0:T(8,128)(2,1)S(1)}, u32[]{:S(2)}, u32[]{:S(2)}) collective-permute-start(bf16[128,128]{1,0:T(8,128)(2,1)S(1)} %get-tuple-element.49.refs_1_), channel_id=1, source_target_pairs={{0,3},{1,2},{2,1},{3,0},{4,7},{5,6},{6,5},{7,4},{8,11},{9,10},{10,... | collective-permute-start | bytes 98312 | tf_op jit(solution)/shard_map/ppermute | solution.py:131
  42.8 6.6 %collective-permute-start.10 = (bf16[128,128]{1,0:T(8,128)(2,1)S(1)}, bf16[128,128]{1,0:T(8,128)(2,1)S(1)}, u32[]{:S(2)}, u32[]{:S(2)}) collective-permute-start(bf16[128,128]{1,0:T(8,128)(2,1)S(1)} %forward_end.2.refs_1_), channel_id=1, source_target_pairs={{0,4},{4,0},{8,12},{12,8},{16,20},{20,16},{24,28},{28,24},{1,5},{5... | collective-permute-start | bytes 98312 | tf_op jit(solution)/shard_map/ppermute | solution.py:131
  43.5 6.8 %collective-permute-start.11 = (bf16[128,128]{1,0:T(8,128)(2,1)S(1)}, bf16[128,128]{1,0:T(8,128)(2,1)S(1)}, u32[]{:S(2)}, u32[]{:S(2)}) collective-permute-start(bf16[128,128]{1,0:T(8,128)(2,1)S(1)} %forward_end.2.refs_1_), channel_id=1, source_target_pairs={{0,8},{4,12},{8,0},{12,4},{16,24},{20,28},{24,16},{28,20},{1,9},{5... | collective-permute-start | bytes 98312 | tf_op jit(solution)/shard_map/ppermute | solution.py:131
  43.5 10.8 %collective-permute-start.12 = (bf16[128,128]{1,0:T(8,128)(2,1)S(1)}, bf16[128,128]{1,0:T(8,128)(2,1)S(1)}, u32[]{:S(2)}, u32[]{:S(2)}) collective-permute-start(bf16[128,128]{1,0:T(8,128)(2,1)S(1)} %forward_end.2.refs_1_), channel_id=1, source_target_pairs={{0,12},{4,8},{8,4},{12,0},{16,28},{20,24},{24,20},{28,16},{1,13},{... | collective-permute-start | bytes 98312 | tf_op jit(solution)/shard_map/ppermute | solution.py:131
  46.4 8.7 %collective-permute-start.13 = (bf16[128,128]{1,0:T(8,128)(2,1)S(1)}, bf16[128,128]{1,0:T(8,128)(2,1)S(1)}, u32[]{:S(2)}, u32[]{:S(2)}) collective-permute-start(bf16[128,128]{1,0:T(8,128)(2,1)S(1)} %forward_end.2.refs_1_), channel_id=1, source_target_pairs={{0,16},{4,20},{8,24},{12,28},{16,0},{20,4},{24,8},{28,12},{1,17},{... | collective-permute-start | bytes 98312 | tf_op jit(solution)/shard_map/ppermute | solution.py:131
  47.1 8.0 %collective-permute-start.14 = (bf16[128,128]{1,0:T(8,128)(2,1)S(1)}, bf16[128,128]{1,0:T(8,128)(2,1)S(1)}, u32[]{:S(2)}, u32[]{:S(2)}) collective-permute-start(bf16[128,128]{1,0:T(8,128)(2,1)S(1)} %forward_end.2.refs_1_), channel_id=1, source_target_pairs={{0,20},{4,16},{8,28},{12,24},{16,4},{20,0},{24,12},{28,8},{1,21},{... | collective-permute-start | bytes 98312 | tf_op jit(solution)/shard_map/ppermute | solution.py:131
  49.4 5.9 %collective-permute-start.15 = (bf16[128,128]{1,0:T(8,128)(2,1)S(1)}, bf16[128,128]{1,0:T(8,128)(2,1)S(1)}, u32[]{:S(2)}, u32[]{:S(2)}) collective-permute-start(bf16[128,128]{1,0:T(8,128)(2,1)S(1)} %forward_end.2.refs_1_), channel_id=1, source_target_pairs={{0,24},{4,28},{8,16},{12,20},{16,8},{20,12},{24,0},{28,4},{1,25},{... | collective-permute-start | bytes 98312 | tf_op jit(solution)/shard_map/ppermute | solution.py:131
  50.3 6.8 %collective-permute-start.16 = (bf16[128,128]{1,0:T(8,128)(2,1)S(1)}, bf16[128,128]{1,0:T(8,128)(2,1)S(1)}, u32[]{:S(2)}, u32[]{:S(2)}) collective-permute-start(bf16[128,128]{1,0:T(8,128)(2,1)S(1)} %forward_end.2.refs_1_), channel_id=1, source_target_pairs={{0,28},{4,24},{8,20},{12,16},{16,12},{20,8},{24,4},{28,0},{1,29},{... | collective-permute-start | bytes 98312 | tf_op jit(solution)/shard_map/ppermute | solution.py:131
  54.3 5.1 %collective-permute-start.33 = (f32[128,128]{1,0:T(8,128)S(1)}, f32[128,128]{1,0:T(8,128)S(1)}, u32[]{:S(2)}, u32[]{:S(2)}) collective-permute-start(f32[128,128]{1,0:T(8,128)S(1)} %get-tuple-element.51), channel_id=1, source_target_pairs={{0,4},{4,0},{8,12},{12,8},{16,20},{20,16},{24,28},{28,24},{1,5},{5... | collective-permute-start | bytes 196616 | tf_op jit(solution)/shard_map/ppermute | solution.py:131
  55.1 5.2 %collective-permute-start.34 = (f32[128,128]{1,0:T(8,128)S(1)}, f32[128,128]{1,0:T(8,128)S(1)}, u32[]{:S(2)}, u32[]{:S(2)}) collective-permute-start(f32[128,128]{1,0:T(8,128)S(1)} %get-tuple-element.52), channel_id=1, source_target_pairs={{0,8},{4,12},{8,0},{12,4},{16,24},{20,28},{24,16},{28,20},{1,9},{5... | collective-permute-start | bytes 196616 | tf_op jit(solution)/shard_map/ppermute | solution.py:131
  57.5 6.1 %collective-permute-start.17 = (f32[128,128]{1,0:T(8,128)S(1)}, f32[128,128]{1,0:T(8,128)S(1)}, u32[]{:S(2)}, u32[]{:S(2)}) collective-permute-start(f32[128,128]{1,0:T(8,128)S(1)} %get-tuple-element.36), channel_id=1, source_target_pairs={{0,1},{1,0},{2,3},{3,2},{4,5},{5,4},{6,7},{7,6},{8,9},{9,8},{10,11... | collective-permute-start | bytes 196616 | tf_op jit(solution)/shard_map/ppermute | solution.py:131
  57.6 6.3 %collective-permute-start.18 = (f32[128,128]{1,0:T(8,128)S(1)}, f32[128,128]{1,0:T(8,128)S(1)}, u32[]{:S(2)}, u32[]{:S(2)}) collective-permute-start(f32[128,128]{1,0:T(8,128)S(1)} %get-tuple-element.37), channel_id=1, source_target_pairs={{0,2},{1,3},{2,0},{3,1},{4,6},{5,7},{6,4},{7,5},{8,10},{9,11},{10,... | collective-permute-start | bytes 196616 | tf_op jit(solution)/shard_map/ppermute | solution.py:131
  58.8 7.3 %collective-permute-start.19 = (f32[128,128]{1,0:T(8,128)S(1)}, f32[128,128]{1,0:T(8,128)S(1)}, u32[]{:S(2)}, u32[]{:S(2)}) collective-permute-start(f32[128,128]{1,0:T(8,128)S(1)} %get-tuple-element.38), channel_id=1, source_target_pairs={{0,3},{1,2},{2,1},{3,0},{4,7},{5,6},{6,5},{7,4},{8,11},{9,10},{10,... | collective-permute-start | bytes 196616 | tf_op jit(solution)/shard_map/ppermute | solution.py:131
  59.4 10.3 %collective-permute-start.35 = (f32[128,128]{1,0:T(8,128)S(1)}, f32[128,128]{1,0:T(8,128)S(1)}, u32[]{:S(2)}, u32[]{:S(2)}) collective-permute-start(f32[128,128]{1,0:T(8,128)S(1)} %get-tuple-element.53), channel_id=1, source_target_pairs={{0,12},{4,8},{8,4},{12,0},{16,28},{20,24},{24,20},{28,16},{1,13},{... | collective-permute-start | bytes 196616 | tf_op jit(solution)/shard_map/ppermute | solution.py:131
  60.3 10.7 %collective-permute-start.36 = (f32[128,128]{1,0:T(8,128)S(1)}, f32[128,128]{1,0:T(8,128)S(1)}, u32[]{:S(2)}, u32[]{:S(2)}) collective-permute-start(f32[128,128]{1,0:T(8,128)S(1)} %get-tuple-element.54), channel_id=1, source_target_pairs={{0,16},{4,20},{8,24},{12,28},{16,0},{20,4},{24,8},{28,12},{1,17},{... | collective-permute-start | bytes 196616 | tf_op jit(solution)/shard_map/ppermute | solution.py:131
  63.6 10.0 %collective-permute-start.37 = (f32[128,128]{1,0:T(8,128)S(1)}, f32[128,128]{1,0:T(8,128)S(1)}, u32[]{:S(2)}, u32[]{:S(2)}) collective-permute-start(f32[128,128]{1,0:T(8,128)S(1)} %get-tuple-element.55), channel_id=1, source_target_pairs={{0,20},{4,16},{8,28},{12,24},{16,4},{20,0},{24,12},{28,8},{1,21},{... | collective-permute-start | bytes 196616 | tf_op jit(solution)/shard_map/ppermute | solution.py:131
  63.9 9.7 %collective-permute-start.38 = (f32[128,128]{1,0:T(8,128)S(1)}, f32[128,128]{1,0:T(8,128)S(1)}, u32[]{:S(2)}, u32[]{:S(2)}) collective-permute-start(f32[128,128]{1,0:T(8,128)S(1)} %get-tuple-element.56), channel_id=1, source_target_pairs={{0,24},{4,28},{8,16},{12,20},{16,8},{20,12},{24,0},{28,4},{1,25},{... | collective-permute-start | bytes 196616 | tf_op jit(solution)/shard_map/ppermute | solution.py:131
  66.1 7.5 %collective-permute-start.39 = (f32[128,128]{1,0:T(8,128)S(1)}, f32[128,128]{1,0:T(8,128)S(1)}, u32[]{:S(2)}, u32[]{:S(2)}) collective-permute-start(f32[128,128]{1,0:T(8,128)S(1)} %get-tuple-element.57), channel_id=1, source_target_pairs={{0,28},{4,24},{8,20},{12,16},{16,12},{20,8},{24,4},{28,0},{1,29},{... | collective-permute-start | bytes 196616 | tf_op jit(solution)/shard_map/ppermute | solution.py:131
  68.4 5.2 %copy-start.4 = (f32[128,128]{1,0:T(8,128)S(1)}, f32[128,128]{1,0:T(8,128)}, u32[]{:S(2)}) copy-start(f32[128,128]{1,0:T(8,128)} %cot_ref.3) | copy-start | bytes 196612
  (1 other events, 0.7 us)

commit v2 on v1

v2 whole, which is shorter than its diff:
```python
import jax
import jax.numpy as jnp
from jax import lax
from jax.experimental import pallas as pl
from jax.experimental.pallas import tpu as pltpu
from jax.sharding import PartitionSpec as P

VMEM_LIMIT = 32 * 1024 * 1024
BF16 = jnp.bfloat16
F32 = jnp.float32


def vmem():
    return pl.BlockSpec(memory_space=pltpu.VMEM)


def smem():
    return pl.BlockSpec(memory_space=pltpu.SMEM)


def call(body, outs, in_specs, args, flops, name):
    nbytes = sum(a.size * a.dtype.itemsize for a in (*args, *outs))
    return pl.pallas_call(
        body,
        out_shape=outs,
        in_specs=in_specs,
        out_specs=[vmem()] * len(outs),
        compiler_params=pltpu.CompilerParams(vmem_limit_bytes=VMEM_LIMIT),
        cost_estimate=pl.CostEstimate(flops=flops, bytes_accessed=nbytes, transcendentals=0),
        name=name,
    )(*args)


def rate_row(types_ref, teleport_ref):
    types = types_ref[...]
    rate = jnp.zeros(types.shape, F32)
    for t in range(teleport_ref.shape[0]):
        rate = jnp.where(types == t, teleport_ref[t], rate)
    return rate


def rate_column(row, width):
    size = row.shape[1]
    return jnp.broadcast_to(row, (width, size)).T


def split_store(out_ref, block, first, count, value):
    rest = value
    for part in range(count):
        high = rest.astype(BF16)
        out_ref[block, first + part] = high
        rest = rest - high.astype(F32)


def merged(in_ref, first, count):
    total = None
    for part in reversed(range(first, first + count)):
        for block in range(in_ref.shape[0]):
            term = in_ref[block, part].astype(F32)
            total = term if total is None else total + term
    return total


def start_body(cot_ref, types_ref, teleport_ref, q_ref):
    rate = rate_row(types_ref, teleport_ref)
    value = ((1.0 - rate) * cot_ref[...].T).astype(BF16)
    for block in range(q_ref.shape[0]):
        q_ref[block, 0] = value


def dense_body(tiles_ref, row_ref, col_ref, count_ref, dense_ref):
    size = tiles_ref.shape[-1]
    dense_ref[...] = jnp.zeros_like(dense_ref)

    def place(slot, carry):
        row = row_ref[0, 0, slot]
        col = col_ref[0, 0, slot]
        dense_ref[
            pl.ds(pl.multiple_of(row * size, size), size),
            pl.ds(pl.multiple_of(col * size, size), size),
        ] = tiles_ref[0, 0, slot]
        return carry

    lax.fori_loop(0, count_ref[0, 0], place, 0)


def adjoint_product(dense_ref, in_ref, part, out_ref, first, count):
    size = in_ref.shape[-1]
    n_rows, n_cols = out_ref.shape[0], in_ref.shape[0]
    left = jnp.concatenate([in_ref[j, part] for j in range(n_cols)], axis=1)
    step = 2 if n_rows % 2 == 0 else 1
    for s in range(0, n_rows, step):
        product = jnp.dot(
            left, dense_ref[:, s * size : (s + step) * size], preferred_element_type=F32
        )
        for e in range(step):
            split_store(out_ref, s + e, first, count, product[:, e * size : (e + 1) * size])


def forward_product(dense_ref, in_ref, part, out_ref, first, count):
    size = in_ref.shape[-1]
    n_rows, n_cols = in_ref.shape[0], out_ref.shape[0]
    total = None
    step = 2 if n_rows % 2 == 0 else 1
    for s in range(0, n_rows, step):
        panel = jnp.concatenate([in_ref[s + e, part] for e in range(step)], axis=0)
        term = jnp.dot(
            dense_ref[:, s * size : (s + step) * size], panel, preferred_element_type=F32
        )
        total = term if total is None else total + term
    for j in range(n_cols):
        split_store(out_ref, j, first, count, total[j * size : (j + 1) * size])


def first_body(dense_ref, q_ref, h_ref, out_ref):
    panel = h_ref[...].astype(BF16)
    for block in range(out_ref.shape[0]):
        out_ref[block, 0] = panel
    adjoint_product(dense_ref, q_ref, 0, out_ref, 1, 2)


def second_body(dense_ref, in_ref, types_ref, teleport_ref, out_ref, d_ref):
    rate = rate_row(types_ref, teleport_ref)
    total = merged(in_ref, 1, 2)
    d_ref[...] = total
    value = ((1.0 - rate) * total).astype(BF16)
    for block in range(out_ref.shape[0]):
        out_ref[block, 0] = value
    forward_product(dense_ref, in_ref, 0, out_ref, 1, 2)


def third_body(dense_ref, in_ref, h_ref, types_ref, teleport_ref, out_ref):
    rate = rate_column(rate_row(types_ref, teleport_ref), h_ref.shape[1])
    panel = ((1.0 - rate) * merged(in_ref, 1, 2) + rate * h_ref[...]).astype(BF16)
    for block in range(out_ref.shape[0]):
        out_ref[block, 0] = panel
    adjoint_product(dense_ref, in_ref, 0, out_ref, 1, 1)


def fourth_body(dense_ref, in_ref, cot_ref, d_ref, types_ref, teleport_ref, out_ref, grad_ref):
    forward_product(dense_ref, in_ref, 0, out_ref, 0, 1)
    rate = rate_row(types_ref, teleport_ref)
    column = rate_column(rate, cot_ref.shape[1])
    grad_ref[...] = column * cot_ref[...] + (rate * d_ref[...] + merged(in_ref, 1, 1)).T


def fifth_body(in_ref, h_ref, types_ref, teleport_ref, out_ref):
    rate = rate_column(rate_row(types_ref, teleport_ref), h_ref.shape[1])
    out_ref[...] = (1.0 - rate) * merged(in_ref, 0, 1) + rate * h_ref[...]


def exchange(blocks, axis):
    return lax.all_to_all(blocks, axis, split_axis=0, concat_axis=0, tiled=True)


def shards(h_start, cotangent, node_type, teleport, tile_values, tile_row, tile_col, tile_count):
    n_rows = lax.axis_size("rows")
    n_cols = lax.axis_size("cols")
    size = tile_values.shape[-1]
    features = h_start.shape[-1]
    types = node_type.reshape(1, size)
    hop_flops = 2 * n_rows * n_cols * size * size * features

    def blocks(count, parts):
        return jax.ShapeDtypeStruct((count, parts, size, features), BF16)

    def single():
        return jax.ShapeDtypeStruct((size, features), F32)

    (dense,) = call(
        dense_body,
        [jax.ShapeDtypeStruct((n_cols * size, n_rows * size), BF16)],
        [vmem(), smem(), smem(), smem()],
        (tile_values, tile_row, tile_col, tile_count),
        0,
        "dense",
    )
    (out,) = call(
        start_body,
        [blocks(n_cols, 1)],
        [vmem(), vmem(), smem()],
        (cotangent, types, teleport),
        0,
        "start",
    )
    got = exchange(out, "cols")
    (out,) = call(
        first_body, [blocks(n_rows, 3)], [vmem()] * 3, (dense, got, h_start), hop_flops, "first"
    )
    got = exchange(out, "rows")
    out, d1 = call(
        second_body,
        [blocks(n_cols, 3), single()],
        [vmem()] * 3 + [smem()],
        (dense, got, types, teleport),
        hop_flops,
        "second",
    )
    got = exchange(out, "cols")
    (out,) = call(
        third_body,
        [blocks(n_rows, 2)],
        [vmem()] * 4 + [smem()],
        (dense, got, h_start, types, teleport),
        hop_flops,
        "third",
    )
    got = exchange(out, "rows")
    out, input_grad = call(
        fourth_body,
        [blocks(n_cols, 1), single()],
        [vmem()] * 5 + [smem()],
        (dense, got, cotangent, d1, types, teleport),
        hop_flops,
        "fourth",
    )
    got = exchange(out, "cols")
    (propagated,) = call(
        fifth_body,
        [single()],
        [vmem()] * 3 + [smem()],
        (got, h_start, types, teleport),
        0,
        "fifth",
    )
    return propagated, input_grad


def solution(mesh):
    placed = (
        P(("rows", "cols"), None),
        P(("rows", "cols"), None),
        P(("rows", "cols")),
        P(),
        P("rows", "cols", None, None, None),
        P("rows", "cols", None),
        P("rows", "cols", None),
        P("rows", "cols"),
    )
    return jax.shard_map(
        shards,
        mesh=mesh,
        in_specs=placed,
        out_specs=(P(("rows", "cols"), None), P(("rows", "cols"), None)),
        check_vma=False,
    )
```

time: 75.1 us -> 78.3 us (1.043)
  blocking collectives: 0 us -> 60.4 us
  starting transfers between devices: 52.1 us -> 4.21 us
  waiting for transfers between devices: 11.1 us -> 2.14 us
  local copies, waits for them, and re-layouts: 3.48 us -> 2.64 us
    all_to_all x0 -> x4, blocking collectives: none -> 60.4 us  [exchange(): return lax.all_to_all(blocks, axis, split_axis=0, concat_axis=0, tiled=True)]
    ppermute x40 -> x0, starting transfers between devices: 52.1 us -> none  [swap(): lax.ppermute(values[s], axis, [(i, i ^ s) for i in range(count)])]
    ppermute x40 -> x0, waiting for transfers between devices: 11.1 us -> none  [swap(): lax.ppermute(values[s], axis, [(i, i ^ s) for i in range(count)])]
    all_to_all x0 -> x1, starting transfers between devices: none -> 4.21 us  [exchange(): return lax.all_to_all(blocks, axis, split_axis=0, concat_axis=0, tiled=True)]
    all_to_all x0 -> x1, waiting for transfers between devices: none -> 2.14 us  [exchange(): return lax.all_to_all(blocks, axis, split_axis=0, concat_axis=0, tiled=True)]
    unnamed x18 -> x16, local copies, waits for them, and re-layouts: 3.48 us -> 2.64 us
    pallas_call x10 -> x7, Pallas kernels: 6.67 us -> 6.96 us  [call(): pl.pallas_call(body, out_shape=outs, in_specs=in_specs, out_specs=[vmem()...]
  transfers between devices with their start and end apart: 40 -> 1, of which waited for: 6 -> 1; matrix products, arithmetic and copies ran while one was open for 0% -> 0% of each run, Pallas kernels for 6% -> 1%
where the time goes in v2:
time: 78.3 us; the launch traced here: 77.8 us
  blocking collectives  60.4 us (77%)
  Pallas kernels  6.96 us (9%)
  starting transfers between devices  4.21 us (5%)
  local copies, waits for them, and re-layouts  2.64 us (3%)
  waiting for transfers between devices  2.14 us (3%)
  between operations  1.39 us (2%)
    all_to_all x4, blocking collectives, exchange(): return lax.all_to_all(blocks, axis, split_axis=0, concat_axis=0, tiled=True)  60.4 us
    pallas_call x7, Pallas kernels, call(): pl.pallas_call(body, out_shape=outs, in_specs=in_specs, out_specs=[vmem()...  6.96 us
    all_to_all x1, starting transfers between devices, exchange(): return lax.all_to_all(blocks, axis, split_axis=0, concat_axis=0, tiled=True)  4.21 us
    unnamed x16, local copies, waits for them, and re-layouts  2.64 us
    all_to_all x1, waiting for transfers between devices, exchange(): return lax.all_to_all(blocks, axis, split_axis=0, concat_axis=0, tiled=True)  2.14 us
  transfers between devices with their start and end apart: 1, of which 1 were waited for; matrix products, arithmetic and copies ran while one was open for 0% of the time, Pallas kernels for 1%

profile of v2, /device:TPU:0, one launch (start us, length us, event | category | flops | bytes accessed | tf_op | source)
XLA Modules:
  0.0 77.8 jit_solution(1477029086672305905)
XLA Ops:
  0.6 0.0 copy-start.5
  0.6 0.0 copy-start.4
  0.6 0.6 copy-done.5
  1.3 0.0 copy-done.4
  1.3 0.0 copy-start.2
  1.3 0.8 %copy-done.2 = f32[128,128]{1,0:T(8,128)S(1)} copy-done((f32[128,128]{1,0:T(8,128)S(1)}, f32[128,128]{1,0:T(8,128)}, u32[]{:S(2)}) %copy-start.2) | copy-done | bytes 65560
  2.1 1.3 %start.1 = bf16[4,1,128,128]{3,2,1,0:T(8,128)(2,1)} custom-call(f32[128,128]{1,0:T(8,128)S(1)} %copy-done.2, s32[1,128]{1,0:T(1,128)S(1)} %bitcast.1, f32[8]{0:T(128)S(1)} %copy-done.5), custom_call_target="tpu_custom_call" | custom-call | bytes 197152 | tf_op jit(solution)/shard_map/start/pallas_call | solution.py:23
  3.4 4.2 %all-to-all-start = ((bf16[4,1,128,128]{3,2,1,0:T(8,128)(2,1)}), bf16[4,1,128,128]{3,2,1,0:T(8,128)(2,1)S(1)}, u32[]{:S(2)}, u32[]{:S(2)}) async-start(bf16[4,1,128,128]{3,2,1,0:T(8,128)(2,1)} %start.1), calls=%async_computation | async-start | bytes 262144 | tf_op jit(solution)/shard_map/all_to_all | solution.py:153
  7.6 0.0 copy-start.6
  7.6 0.0 copy-start.7
  8.3 0.0 copy-done.6
  8.3 0.0 copy-done.7
  8.3 0.0 copy-start
  8.3 1.1 %copy-done = bf16[1,1,24,128,128]{4,3,2,1,0:T(8,128)(2,1)S(1)} copy-done((bf16[1,1,24,128,128]{4,3,2,1,0:T(8,128)(2,1)S(1)}, bf16[1,1,24,128,128]{4,3,2,1,0:T(8,128)(2,1)}, u32[]{:S(2)}) %copy-start) | copy-done | bytes 786456
  9.5 0.0 copy-start.1
  9.5 0.6 dense.1.dense_ref
  10.1 2.1 %all-to-all-done.q_ref = bf16[4,1,128,128]{3,2,1,0:T(8,128)(2,1)S(1)} async-done(((bf16[4,1,128,128]{3,2,1,0:T(8,128)(2,1)}), bf16[4,1,128,128]{3,2,1,0:T(8,128)(2,1)S(1)}, u32[]{:S(2)}, u32[]{:S(2)}) %all-to-all-start) | async-done | bytes 131104 | tf_op jit(solution)/shard_map/all_to_all | solution.py:153
  12.3 0.0 copy-done.1
  12.3 0.3 first.1
  12.6 26.0 %all_to_all.25.in_ref = bf16[8,3,128,128]{3,2,1,0:T(8,128)(2,1)S(1)} all-to-all(bf16[8,3,128,128]{3,2,1,0:T(8,128)(2,1)S(1)} %first.1), channel_id=1, replica_groups=mesh['rows'=8,'cols'=4] {'rows'}, dimensions={0} | all-to-all | bytes 1572864 | tf_op jit(solution)/shard_map/all_to_all | solution.py:153
  38.5 1.0 %second.1 = (bf16[4,3,128,128]{3,2,1,0:T(8,128)(2,1)S(1)}, f32[128,128]{1,0:T(8,128)S(1)}) custom-call(bf16[512,1024]{1,0:T(8,128)(2,1)S(1)} %dense.1.dense_ref, bf16[8,3,128,128]{3,2,1,0:T(8,128)(2,1)S(1)} %all_to_all.25.in_ref, s32[1,128]{1,0:T(1,128)S(1)} %bitcast.2, f32[8]{0:T(128)S(1)} %copy-done.5), custom_call_target="tpu_custom_call" | custom-call | flops 134217728 | bytes 2294304 | tf_op jit(solution)/shard_map/second/pallas_call | solution.py:23
  39.6 9.8 %all_to_all.26.in_ref = bf16[4,3,128,128]{3,2,1,0:T(8,128)(2,1)S(1)} all-to-all(bf16[4,3,128,128]{3,2,1,0:T(8,128)(2,1)S(1)} %get-tuple-element.6), channel_id=1, replica_groups=mesh['rows'=8,'cols'=4] {'cols'}, dimensions={0} | all-to-all | bytes 786432 | tf_op jit(solution)/shard_map/all_to_all | solution.py:153
  49.4 0.9 %third.1 = bf16[8,2,128,128]{3,2,1,0:T(8,128)(2,1)S(1)} custom-call(bf16[512,1024]{1,0:T(8,128)(2,1)S(1)} %dense.1.dense_ref, bf16[4,3,128,128]{3,2,1,0:T(8,128)(2,1)S(1)} %all_to_all.26.in_ref, f32[128,128]{1,0:T(8,128)S(1)} %copy-done.1, s32[1,128]{1,0:T(1,128)S(1)} %bitcast.3, f32[8]{0:T(128)S(1)} %copy-done.5), custom_call_target="tpu_custom_call" | custom-call | flops 134217728 | bytes 2032160 | tf_op jit(solution)/shard_map/third/pallas_call | solution.py:23
  50.3 0.0 copy-start.3
  50.3 17.6 %all_to_all.27.in_ref = bf16[8,2,128,128]{3,2,1,0:T(8,128)(2,1)S(1)} all-to-all(bf16[8,2,128,128]{3,2,1,0:T(8,128)(2,1)S(1)} %third.1), channel_id=1, replica_groups=mesh['rows'=8,'cols'=4] {'rows'}, dimensions={0} | all-to-all | bytes 1048576 | tf_op jit(solution)/shard_map/all_to_all | solution.py:153
  67.9 0.0 copy-done.3
  67.9 1.6 %fourth.1 = (bf16[4,1,128,128]{3,2,1,0:T(8,128)(2,1)S(1)}, f32[128,128]{1,0:T(8,128)}) custom-call(bf16[512,1024]{1,0:T(8,128)(2,1)S(1)} %dense.1.dense_ref, bf16[8,2,128,128]{3,2,1,0:T(8,128)(2,1)S(1)} %all_to_all.27.in_ref, f32[128,128]{1,0:T(8,128)S(1)} %copy-done.3, f32[128,128]{1,0:T(8,128)S(1)} %get-tuple-element.7.d_ref, s32[1,128]{1,0:T(1,128)S(1)} %bitcast.4, ...), custom_call_target="tpu_custom_call" | custom-call | flops 134217728 | bytes 1901088 | tf_op jit(solution)/shard_map/fourth/pallas_call | solution.py:23
  69.5 7.0 %all_to_all.28.in_ref = bf16[4,1,128,128]{3,2,1,0:T(8,128)(2,1)S(1)} all-to-all(bf16[4,1,128,128]{3,2,1,0:T(8,128)(2,1)S(1)} %get-tuple-element.8), channel_id=1, replica_groups=mesh['rows'=8,'cols'=4] {'cols'}, dimensions={0} | all-to-all | bytes 262144 | tf_op jit(solution)/shard_map/all_to_all | solution.py:153
  76.5 1.3 %fifth.1 = f32[128,128]{1,0:T(8,128)} custom-call(bf16[4,1,128,128]{3,2,1,0:T(8,128)(2,1)S(1)} %all_to_all.28.in_ref, f32[128,128]{1,0:T(8,128)S(1)} %copy-done.1, s32[1,128]{1,0:T(1,128)S(1)} %bitcast.5, f32[8]{0:T(128)S(1)} %copy-done.5), custom_call_target="tpu_custom_call" | custom-call | bytes 262688 | tf_op jit(solution)/shard_map/fifth/pallas_call | solution.py:23
Async XLA Ops:
  0.6 0.7 copy-start.5
  0.6 0.7 copy-start.4
  1.3 0.8 %copy-start.2 = (f32[128,128]{1,0:T(8,128)S(1)}, f32[128,128]{1,0:T(8,128)}, u32[]{:S(2)}) copy-start(f32[128,128]{1,0:T(8,128)} %cot_ref.3) | copy-start | bytes 196612
  3.4 8.8 %all-to-all-start = ((bf16[4,1,128,128]{3,2,1,0:T(8,128)(2,1)}), bf16[4,1,128,128]{3,2,1,0:T(8,128)(2,1)S(1)}, u32[]{:S(2)}, u32[]{:S(2)}) async-start(bf16[4,1,128,128]{3,2,1,0:T(8,128)(2,1)} %start.1), calls=%async_computation | async-start | bytes 262144 | tf_op jit(solution)/shard_map/all_to_all | solution.py:153
  7.6 0.7 copy-start.6
  7.6 0.7 copy-start.7
  8.3 1.1 %copy-start = (bf16[1,1,24,128,128]{4,3,2,1,0:T(8,128)(2,1)S(1)}, bf16[1,1,24,128,128]{4,3,2,1,0:T(8,128)(2,1)}, u32[]{:S(2)}) copy-start(bf16[1,1,24,128,128]{4,3,2,1,0:T(8,128)(2,1)} %tiles_ref.1) | copy-start | bytes 2359300
  9.5 2.8 %copy-start.1 = (f32[128,128]{1,0:T(8,128)S(1)}, f32[128,128]{1,0:T(8,128)}, u32[]{:S(2)}) copy-start(f32[128,128]{1,0:T(8,128)} %h_ref.5) | copy-start | bytes 196612
  50.3 17.7 %copy-start.3 = (f32[128,128]{1,0:T(8,128)S(1)}, f32[128,128]{1,0:T(8,128)}, u32[]{:S(2)}) copy-start(f32[128,128]{1,0:T(8,128)} %cot_ref.3) | copy-start | bytes 196612

commit v3 on v1

v3 whole, which is shorter than its diff:
```python
import jax
import jax.numpy as jnp
from jax import lax
from jax.experimental import pallas as pl
from jax.experimental.pallas import tpu as pltpu
from jax.sharding import PartitionSpec as P

VMEM_LIMIT = 32 * 1024 * 1024
BF16 = jnp.bfloat16
F32 = jnp.float32


def vmem():
    return pl.BlockSpec(memory_space=pltpu.VMEM)


def smem():
    return pl.BlockSpec(memory_space=pltpu.SMEM)


def hbm():
    return pl.BlockSpec(memory_space=pltpu.HBM)


def call(body, outs, in_specs, args, flops, name, scratch=()):
    nbytes = sum(a.size * a.dtype.itemsize for a in (*args, *outs))
    return pl.pallas_call(
        body,
        out_shape=outs,
        in_specs=in_specs,
        out_specs=[vmem()] * len(outs),
        scratch_shapes=list(scratch),
        compiler_params=pltpu.CompilerParams(vmem_limit_bytes=VMEM_LIMIT),
        cost_estimate=pl.CostEstimate(flops=flops, bytes_accessed=nbytes, transcendentals=0),
        name=name,
    )(*args)


def fetch(pairs, sems):
    copies = [pltpu.make_async_copy(a, b, sems.at[i]) for i, (a, b) in enumerate(pairs)]
    for copy in copies:
        copy.start()
    for copy in copies:
        copy.wait()


def rate_row(types_ref, teleport_ref):
    types = types_ref[...]
    rate = jnp.zeros(types.shape, F32)
    for t in range(teleport_ref.shape[0]):
        rate = jnp.where(types == t, teleport_ref[t], rate)
    return rate


def rate_column(row, width):
    size = row.shape[1]
    return jnp.broadcast_to(row, (width, size)).T


def start_body(cot_hbm, types_hbm, teleport_hbm, q_ref, cot_ref, types_ref, teleport_ref, sems):
    fetch(
        [(cot_hbm, cot_ref), (types_hbm, types_ref), (teleport_hbm, teleport_ref)],
        sems,
    )
    rate = rate_row(types_ref, teleport_ref)
    q_ref[...] = ((1.0 - rate) * cot_ref[...].T).astype(BF16)


def dense_body(
    tiles_hbm, row_hbm, col_hbm, count_hbm, dense_ref, row_ref, col_ref, count_ref, sems, slot_sems
):
    size = tiles_hbm.shape[-1]
    me_row = lax.axis_index("rows")
    me_col = lax.axis_index("cols")
    dense_ref[...] = jnp.zeros_like(dense_ref)
    fetch([(row_hbm, row_ref), (col_hbm, col_ref), (count_hbm, count_ref)], sems)
    count = count_ref[0, 0]

    def copy(slot):
        row = row_ref[0, 0, slot] ^ me_col
        col = col_ref[0, 0, slot] ^ me_row
        return pltpu.make_async_copy(
            tiles_hbm.at[0, 0, slot],
            dense_ref.at[
                pl.ds(pl.multiple_of(row * size, size), size),
                pl.ds(pl.multiple_of(col * size, size), size),
            ],
            slot_sems.at[slot],
        )

    def begin(slot, carry):
        copy(slot).start()
        return carry

    def end(slot, carry):
        copy(slot).wait()
        return carry

    lax.fori_loop(0, count, begin, 0)
    lax.fori_loop(0, count, end, 0)


def adjoint_body(n_rows, n_cols, dense_ref, *refs):
    blocks, outs = refs[:n_cols], refs[n_cols:]
    send_far, send_near, keep_far, keep_near = outs
    half = n_rows // 2
    near = send_near.shape[0]
    size = blocks[0].shape[1]
    left = jnp.concatenate([b[...] for b in blocks], axis=1)
    for zz in reversed(range(half)):
        part = jnp.dot(
            left, dense_ref[:, 2 * zz * size : (2 * zz + 2) * size], preferred_element_type=F32
        )
        keep, send, at = (
            (keep_near, send_near, zz) if zz < near else (keep_far, send_far, zz - near)
        )
        keep[at] = part[:, :size]
        send[at] = part[:, size:].astype(send.dtype)


def add_body(keep_ref, got_ref, *outs):
    for at, out in enumerate(outs):
        out[...] = (keep_ref[at] + got_ref[at].astype(F32)).astype(out.dtype)


def pack_body(*refs):
    *parts, out_ref = refs
    for at, part in enumerate(parts):
        out_ref[at] = part[...]


def forward_body(half, n_cols, dense_ref, other_ref, *refs):
    panels, outs = refs[:half], refs[half:]
    size = panels[0].shape[0]
    total = None
    for zz in range(half):
        panel = jnp.concatenate([panels[zz][...], other_ref[zz]], axis=0)
        part = jnp.dot(
            dense_ref[:, 2 * zz * size : (2 * zz + 2) * size], panel, preferred_element_type=F32
        )
        total = part if total is None else total + part
    for j in range(n_cols):
        outs[j][...] = total[j * size : (j + 1) * size].astype(outs[j].dtype)


def sum_refs(refs):
    terms = [ref[...].astype(F32) for ref in refs]
    while len(terms) > 1:
        terms = [sum(terms[i : i + 2][1:], terms[i]) for i in range(0, len(terms), 2)]
    return terms[0]


def forward_end_body(h_ref, types_ref, teleport_ref, *refs):
    *parts, out_ref = refs
    rate = rate_column(rate_row(types_ref, teleport_ref), h_ref.shape[1])
    value = (1.0 - rate) * sum_refs(parts) + rate * h_ref[...]
    out_ref[...] = value.astype(out_ref.dtype)


def adjoint_mid_body(types_ref, teleport_ref, *refs):
    *parts, d_ref, q_ref = refs
    rate = rate_row(types_ref, teleport_ref)
    total = sum_refs(parts)
    d_ref[...] = total
    q_ref[...] = ((1.0 - rate) * total).astype(BF16)


def adjoint_end_body(cot_ref, d_ref, types_ref, teleport_ref, *refs):
    *parts, out_ref = refs
    rate = rate_row(types_ref, teleport_ref)
    column = rate_column(rate, cot_ref.shape[1])
    out_ref[...] = column * cot_ref[...] + (rate * d_ref[...] + sum_refs(parts)).T


def send(value, axis, count, step):
    return lax.ppermute(value, axis, [(i, i ^ step) for i in range(count)])


def shards(h_start, cotangent, node_type, teleport, tile_values, tile_row, tile_col, tile_count):
    n_rows = lax.axis_size("rows")
    n_cols = lax.axis_size("cols")
    half = n_rows // 2
    near = half // 2
    size = tile_values.shape[-1]
    slots = tile_values.shape[2]
    features = h_start.shape[-1]
    types = node_type.reshape(1, size)
    hop_flops = 2 * n_rows * n_cols * size * size * features

    def shape(kind, *lead):
        return jax.ShapeDtypeStruct((*lead, size, features), kind)

    (q0,) = call(
        start_body,
        [shape(BF16)],
        [hbm()] * 3,
        (cotangent, types, teleport),
        0,
        "start",
        [
            pltpu.VMEM(cotangent.shape, F32),
            pltpu.VMEM(types.shape, jnp.int32),
            pltpu.SMEM(teleport.shape, F32),
            pltpu.SemaphoreType.DMA((3,)),
        ],
    )
    (dense,) = call(
        dense_body,
        [jax.ShapeDtypeStruct((n_cols * size, n_rows * size), BF16)],
        [hbm()] * 4,
        (tile_values, tile_row, tile_col, tile_count),
        0,
        "dense",
        [
            pltpu.SMEM(tile_row.shape, jnp.int32),
            pltpu.SMEM(tile_col.shape, jnp.int32),
            pltpu.SMEM(tile_count.shape, jnp.int32),
            pltpu.SemaphoreType.DMA((3,)),
            pltpu.SemaphoreType.DMA((slots,)),
        ],
    )
    p0 = h_start.astype(BF16)

    def add(keep, got, kinds, name):
        return call(add_body, [shape(kind) for kind in kinds], [vmem()] * 2, (keep, got), 0, name)

    def adjoint_hop(part, kind):
        blocks = [part] + [send(part, "cols", n_cols, s) for s in range(1, n_cols)]
        send_far, send_near, keep_far, keep_near = call(
            lambda *refs: adjoint_body(n_rows, n_cols, *refs),
            [shape(kind, half - near), shape(kind, near), shape(F32, half - near), shape(F32, near)],
            [vmem()] * (1 + n_cols),
            [dense, *blocks],
            hop_flops,
            "adjoint",
        )
        far = add(keep_far, send(send_far, "rows", n_rows, 1), [kind] * (half - near), "add_far")
        far = [send(far[s - near], "rows", n_rows, 2 * s) for s in range(near, half)]
        kinds = [F32] + [kind] * (near - 1)
        close = add(keep_near, send(send_near, "rows", n_rows, 1), kinds, "add_near")
        close = [close[0]] + [send(close[s], "rows", n_rows, 2 * s) for s in range(1, near)]
        return close + far

    def forward_hop(part, kind):
        panels = [part] + [send(part, "rows", n_rows, 2 * s) for s in range(1, half)]
        (packed,) = call(
            pack_body, [shape(BF16, half)], [vmem()] * half, panels, 0, "pack"
        )
        other = send(packed, "rows", n_rows, 1)
        sums = call(
            lambda *refs: forward_body(half, n_cols, *refs),
            [shape(kind)] * n_cols,
            [vmem()] * (2 + half),
            (dense, other, *panels),
            hop_flops,
            "forward",
        )
        return [sums[0]] + [send(sums[s], "cols", n_cols, s) for s in range(1, n_cols)]

    def forward_end(parts, kind):
        return call(
            forward_end_body,
            [shape(kind)],
            [vmem(), vmem(), smem()] + [vmem()] * n_cols,
            (h_start, types, teleport, *parts),
            0,
            "forward_end",
        )[0]

    back = adjoint_hop(q0, F32)
    first = forward_hop(p0, F32)
    d1, q1 = call(
        adjoint_mid_body,
        [shape(F32), shape(BF16)],
        [vmem(), smem()] + [vmem()] * half,
        (types, teleport, *back),
        0,
        "adjoint_mid",
    )
    p1 = forward_end(first, BF16)
    back_two = adjoint_hop(q1, BF16)
    second = forward_hop(p1, BF16)
    propagated = forward_end(second, F32)
    (input_grad,) = call(
        adjoint_end_body,
        [shape(F32)],
        [vmem(), vmem(), vmem(), smem()] + [vmem()] * half,
        (cotangent, d1, types, teleport, *back_two),
        0,
        "adjoint_end",
    )
    return propagated, input_grad


def solution(mesh):
    placed = (
        P(("rows", "cols"), None),
        P(("rows", "cols"), None),
        P(("rows", "cols")),
        P(),
        P("rows", "cols", None, None, None),
        P("rows", "cols", None),
        P("rows", "cols", None),
        P("rows", "cols"),
    )
    return jax.shard_map(
        shards,
        mesh=mesh,
        in_specs=placed,
        out_specs=(P(("rows", "cols"), None), P(("rows", "cols"), None)),
        check_vma=False,
    )
```

time: 75.1 us -> 57.9 us (0.77)
  starting transfers between devices: 52.1 us -> 29.6 us
  waiting for transfers between devices: 11.1 us -> 17.4 us
  local copies, waits for them, and re-layouts: 3.48 us -> 1.16 us
  other arithmetic: 0 us -> 0.85 us
    ppermute x40 -> x30, starting transfers between devices: 52.1 us -> 29.6 us  [send(): return lax.ppermute(value, axis, [(i, i ^ step) for i in range(count)])]
    ppermute x40 -> x30, waiting for transfers between devices: 11.1 us -> 17.4 us  [send(): return lax.ppermute(value, axis, [(i, i ^ step) for i in range(count)])]
    unnamed x18 -> x14, local copies, waits for them, and re-layouts: 3.48 us -> 1.16 us
    convert_element_type x0 -> x1, other arithmetic: none -> 0.85 us  [shards(): p0 = h_start.astype(BF16)]
    pallas_call x10 -> x16, Pallas kernels: 6.67 us -> 7.19 us  [call(): pl.pallas_call(body, out_shape=outs, in_specs=in_specs, out_specs=[vmem()...]
  transfers between devices with their start and end apart: 40 -> 30, of which waited for: 6 -> 10; matrix products, arithmetic and copies ran while one was open for 0% -> 0% of each run, Pallas kernels for 6% -> 10%
where the time goes in v3:
time: 57.9 us; the launch traced here: 57.7 us
  starting transfers between devices  29.6 us (51%)
  waiting for transfers between devices  17.4 us (30%)
  Pallas kernels  7.19 us (12%)
  between operations  1.5 us (3%)
  local copies, waits for them, and re-layouts  1.16 us (2%)
  other arithmetic  0.85 us (1%)
    ppermute x30, starting transfers between devices, send(): return lax.ppermute(value, axis, [(i, i ^ step) for i in range(count)])  29.6 us
    ppermute x30, waiting for transfers between devices, send(): return lax.ppermute(value, axis, [(i, i ^ step) for i in range(count)])  17.4 us
    pallas_call x16, Pallas kernels, call(): pl.pallas_call(body, out_shape=outs, in_specs=in_specs, out_specs=[vmem()...  7.19 us
    unnamed x14, local copies, waits for them, and re-layouts  1.16 us
  transfers between devices with their start and end apart: 30, of which 10 were waited for; matrix products, arithmetic and copies ran while one was open for 0% of the time, Pallas kernels for 10%

profile of v3, /device:TPU:0, one launch (start us, length us, event | category | flops | bytes accessed | tf_op | source)
XLA Modules:
  0.0 57.7 jit_solution(12602254983337270289)
XLA Ops:
  0.6 0.8 %convert_element_type.3.refs_0_.refs_2_ = bf16[128,128]{1,0:T(8,128)(2,1)S(1)} convert(f32[128,128]{1,0:T(8,128)} %h_ref.3) | non-fusion elementwise | flops 16384 | bytes 98304 | tf_op jit(solution)/shard_map/convert_element_type | solution.py:222
  1.5 3.0 %collective-permute-start = (bf16[128,128]{1,0:T(8,128)(2,1)S(1)}, bf16[128,128]{1,0:T(8,128)(2,1)S(1)}, u32[]{:S(2)}, u32[]{:S(2)}) collective-permute-start(bf16[128,128]{1,0:T(8,128)(2,1)S(1)} %convert_element_type.3.refs_0_.refs_2_), channel_id=1, source_target_pairs={{0,8},{4,12},{8,0},{12,4},{16,24},{20,28},{24,16},{28,20},{1,9},{5... | collective-permute-start | bytes 98312 | tf_op jit(solution)/shard_map/ppermute | solution.py:176
  4.5 2.6 %collective-permute-start.1 = (bf16[128,128]{1,0:T(8,128)(2,1)S(1)}, bf16[128,128]{1,0:T(8,128)(2,1)S(1)}, u32[]{:S(2)}, u32[]{:S(2)}) collective-permute-start(bf16[128,128]{1,0:T(8,128)(2,1)S(1)} %convert_element_type.3.refs_0_.refs_2_), channel_id=1, source_target_pairs={{0,16},{4,20},{8,24},{12,28},{16,0},{20,4},{24,8},{28,12},{1,17},{... | collective-permute-start | bytes 98312 | tf_op jit(solution)/shard_map/ppermute | solution.py:176
  7.1 2.8 %collective-permute-done.1.refs_2_.refs_4_ = bf16[128,128]{1,0:T(8,128)(2,1)S(1)} collective-permute-done((bf16[128,128]{1,0:T(8,128)(2,1)S(1)}, bf16[128,128]{1,0:T(8,128)(2,1)S(1)}, u32[]{:S(2)}, u32[]{:S(2)}) %collective-permute-start.1) | collective-permute-done | bytes 32800 | tf_op jit(solution)/shard_map/ppermute | solution.py:176
  9.9 2.9 %collective-permute-done.2.refs_3_.refs_5_ = bf16[128,128]{1,0:T(8,128)(2,1)S(1)} collective-permute-done((bf16[128,128]{1,0:T(8,128)(2,1)S(1)}, bf16[128,128]{1,0:T(8,128)(2,1)S(1)}, u32[]{:S(2)}, u32[]{:S(2)}) %collective-permute-start.2) | collective-permute-done | bytes 32800 | tf_op jit(solution)/shard_map/ppermute | solution.py:176
  12.8 1.6 %collective-permute-start.3 = (bf16[4,128,128]{2,1,0:T(8,128)(2,1)S(1)}, bf16[4,128,128]{2,1,0:T(8,128)(2,1)S(1)}, u32[]{:S(2)}, u32[]{:S(2)}) collective-permute-start(bf16[4,128,128]{2,1,0:T(8,128)(2,1)S(1)} %pack.2), channel_id=1, source_target_pairs={{0,4},{4,0},{8,12},{12,8},{16,20},{20,16},{24,28},{28,24},{1,5},{5... | collective-permute-start | bytes 393224 | tf_op jit(solution)/shard_map/ppermute | solution.py:176
  14.4 0.7 %start.1.refs_1_ = bf16[128,128]{1,0:T(8,128)(2,1)S(1)} custom-call(f32[128,128]{1,0:T(8,128)S(1)} %copy-done.2, s32[1,128]{1,0:T(1,128)S(1)} %bitcast.1, f32[8]{0:T(128)S(1)} %copy-done.4), custom_call_target="tpu_custom_call" | custom-call | bytes 98848 | tf_op jit(solution)/shard_map/start/pallas_call | solution.py:27
  15.2 0.1 collective-permute-start.14
  15.3 1.6 %collective-permute-start.15 = (bf16[128,128]{1,0:T(8,128)(2,1)S(1)}, bf16[128,128]{1,0:T(8,128)(2,1)S(1)}, u32[]{:S(2)}, u32[]{:S(2)}) collective-permute-start(bf16[128,128]{1,0:T(8,128)(2,1)S(1)} %start.1.refs_1_), channel_id=1, source_target_pairs={{0,2},{1,3},{2,0},{3,1},{4,6},{5,7},{6,4},{7,5},{8,10},{9,11},{10,... | collective-permute-start | bytes 98312 | tf_op jit(solution)/shard_map/ppermute | solution.py:176
  16.9 0.3 collective-permute-start.16
  17.8 1.1 %copy-done = bf16[1,1,24,128,128]{4,3,2,1,0:T(8,128)(2,1)S(1)} copy-done((bf16[1,1,24,128,128]{4,3,2,1,0:T(8,128)(2,1)S(1)}, bf16[1,1,24,128,128]{4,3,2,1,0:T(8,128)(2,1)}, u32[]{:S(2)}) %copy-start) | copy-done | bytes 786456
  19.0 1.1 %dense.1.refs_0_ = bf16[512,1024]{1,0:T(8,128)(2,1)S(1)} custom-call(bf16[1,1,24,128,128]{4,3,2,1,0:T(8,128)(2,1)S(1)} %copy-done, s32[1,1,24]{2,1,0:T(1,128)S(1)} %copy-done.5, s32[1,1,24]{2,1,0:T(1,128)S(1)} %copy-done.6, s32[1,1]{1,0:T(1,128)S(6)} %copy.10.count_hbm), custom_call_target="tpu_custom_call" | custom-call | bytes 1835204 | tf_op jit(solution)/shard_map/dense/pallas_call | solution.py:27
  20.0 0.1 collective-permute-done.16.refs_4_
  20.2 0.3 adjoint.2
  20.5 0.6 %collective-permute-start.19 = (f32[2,128,128]{2,1,0:T(8,128)S(1)}, f32[2,128,128]{2,1,0:T(8,128)S(1)}, u32[]{:S(2)}, u32[]{:S(2)}) collective-permute-start(f32[2,128,128]{2,1,0:T(8,128)S(1)} %get-tuple-element.41), channel_id=1, source_target_pairs={{0,4},{4,0},{8,12},{12,8},{16,20},{20,16},{24,28},{28,24},{1,5},{5... | collective-permute-start | bytes 393224 | tf_op jit(solution)/shard_map/ppermute | solution.py:176
  21.1 1.5 %collective-permute-start.17 = (f32[2,128,128]{2,1,0:T(8,128)S(1)}, f32[2,128,128]{2,1,0:T(8,128)S(1)}, u32[]{:S(2)}, u32[]{:S(2)}) collective-permute-start(f32[2,128,128]{2,1,0:T(8,128)S(1)} %get-tuple-element.37), channel_id=1, source_target_pairs={{0,4},{4,0},{8,12},{12,8},{16,20},{20,16},{24,28},{28,24},{1,5},{5... | collective-permute-start | bytes 393224 | tf_op jit(solution)/shard_map/ppermute | solution.py:176
  22.6 0.4 forward.2
  23.1 1.4 %collective-permute-start.5 = (f32[128,128]{1,0:T(8,128)S(1)}, f32[128,128]{1,0:T(8,128)S(1)}, u32[]{:S(2)}, u32[]{:S(2)}) collective-permute-start(f32[128,128]{1,0:T(8,128)S(1)} %get-tuple-element.30), channel_id=1, source_target_pairs={{0,2},{1,3},{2,0},{3,1},{4,6},{5,7},{6,4},{7,5},{8,10},{9,11},{10,... | collective-permute-start | bytes 196616 | tf_op jit(solution)/shard_map/ppermute | solution.py:176
  24.5 0.5 collective-permute-start.6
  25.0 1.9 %collective-permute-done.19.got_ref = f32[2,128,128]{2,1,0:T(8,128)S(1)} collective-permute-done((f32[2,128,128]{2,1,0:T(8,128)S(1)}, f32[2,128,128]{2,1,0:T(8,128)S(1)}, u32[]{:S(2)}, u32[]{:S(2)}) %collective-permute-start.19) | collective-permute-done | bytes 131104 | tf_op jit(solution)/shard_map/ppermute | solution.py:176
  26.9 0.1 collective-permute-start.20
  27.0 1.9 %collective-permute-done.17.got_ref = f32[2,128,128]{2,1,0:T(8,128)S(1)} collective-permute-done((f32[2,128,128]{2,1,0:T(8,128)S(1)}, f32[2,128,128]{2,1,0:T(8,128)S(1)}, u32[]{:S(2)}, u32[]{:S(2)}) %collective-permute-start.17) | collective-permute-done | bytes 131104 | tf_op jit(solution)/shard_map/ppermute | solution.py:176
  29.0 0.4 collective-permute-start.21
  29.3 1.3 %collective-permute-start.18 = (f32[128,128]{1,0:T(8,128)S(1)}, f32[128,128]{1,0:T(8,128)S(1)}, u32[]{:S(2)}, u32[]{:S(2)}) collective-permute-start(f32[128,128]{1,0:T(8,128)S(1)} %get-tuple-element.39), channel_id=1, source_target_pairs={{0,8},{4,12},{8,0},{12,4},{16,24},{20,28},{24,16},{28,20},{1,9},{5... | collective-permute-start | bytes 196616 | tf_op jit(solution)/shard_map/ppermute | solution.py:176
  30.6 0.7 %forward_end.2.refs_0_.refs_2_ = bf16[128,128]{1,0:T(8,128)(2,1)S(1)} custom-call(f32[128,128]{1,0:T(8,128)S(1)} %copy-done.1, s32[1,128]{1,0:T(1,128)S(1)} %bitcast.2, f32[8]{0:T(128)S(1)} %copy-done.4, f32[128,128]{1,0:T(8,128)S(1)} %get-tuple-element.28.refs_0_, f32[128,128]{1,0:T(8,128)S(1)} %collective-permute-done.4.refs_1_, ...), custom_call_target="tpu_custom_call" | custom-call | bytes 360992 | tf_op jit(solution)/shard_map/forward_end/pallas_call | solution.py:27
  31.3 0.9 %collective-permute-start.7 = (bf16[128,128]{1,0:T(8,128)(2,1)S(1)}, bf16[128,128]{1,0:T(8,128)(2,1)S(1)}, u32[]{:S(2)}, u32[]{:S(2)}) collective-permute-start(bf16[128,128]{1,0:T(8,128)(2,1)S(1)} %forward_end.2.refs_0_.refs_2_), channel_id=1, source_target_pairs={{0,8},{4,12},{8,0},{12,4},{16,24},{20,28},{24,16},{28,20},{1,9},{5... | collective-permute-start | bytes 98312 | tf_op jit(solution)/shard_map/ppermute | solution.py:176
  32.2 2.7 %collective-permute-start.8 = (bf16[128,128]{1,0:T(8,128)(2,1)S(1)}, bf16[128,128]{1,0:T(8,128)(2,1)S(1)}, u32[]{:S(2)}, u32[]{:S(2)}) collective-permute-start(bf16[128,128]{1,0:T(8,128)(2,1)S(1)} %forward_end.2.refs_0_.refs_2_), channel_id=1, source_target_pairs={{0,16},{4,20},{8,24},{12,28},{16,0},{20,4},{24,8},{28,12},{1,17},{... | collective-permute-start | bytes 98312 | tf_op jit(solution)/shard_map/ppermute | solution.py:176
  34.9 0.8 %collective-permute-start.9 = (bf16[128,128]{1,0:T(8,128)(2,1)S(1)}, bf16[128,128]{1,0:T(8,128)(2,1)S(1)}, u32[]{:S(2)}, u32[]{:S(2)}) collective-permute-start(bf16[128,128]{1,0:T(8,128)(2,1)S(1)} %forward_end.2.refs_0_.refs_2_), channel_id=1, source_target_pairs={{0,24},{4,28},{8,16},{12,20},{16,8},{20,12},{24,0},{28,4},{1,25},{... | collective-permute-start | bytes 98312 | tf_op jit(solution)/shard_map/ppermute | solution.py:176
  35.7 0.6 adjoint_mid.1
  36.4 1.5 %collective-permute-start.23 = (bf16[128,128]{1,0:T(8,128)(2,1)S(1)}, bf16[128,128]{1,0:T(8,128)(2,1)S(1)}, u32[]{:S(2)}, u32[]{:S(2)}) collective-permute-start(bf16[128,128]{1,0:T(8,128)(2,1)S(1)} %get-tuple-element.45.refs_1_), channel_id=1, source_target_pairs={{0,2},{1,3},{2,0},{3,1},{4,6},{5,7},{6,4},{7,5},{8,10},{9,11},{10,... | collective-permute-start | bytes 98312 | tf_op jit(solution)/shard_map/ppermute | solution.py:176
  37.8 0.4 collective-permute-start.24
  38.3 2.4 %collective-permute-done.9.refs_3_.refs_5_ = bf16[128,128]{1,0:T(8,128)(2,1)S(1)} collective-permute-done((bf16[128,128]{1,0:T(8,128)(2,1)S(1)}, bf16[128,128]{1,0:T(8,128)(2,1)S(1)}, u32[]{:S(2)}, u32[]{:S(2)}) %collective-permute-start.9) | collective-permute-done | bytes 32800 | tf_op jit(solution)/shard_map/ppermute | solution.py:176
  40.6 0.7 %collective-permute-start.10 = (bf16[4,128,128]{2,1,0:T(8,128)(2,1)S(1)}, bf16[4,128,128]{2,1,0:T(8,128)(2,1)S(1)}, u32[]{:S(2)}, u32[]{:S(2)}) collective-permute-start(bf16[4,128,128]{2,1,0:T(8,128)(2,1)S(1)} %pack.3), channel_id=1, source_target_pairs={{0,4},{4,0},{8,12},{12,8},{16,20},{20,16},{24,28},{28,24},{1,5},{5... | collective-permute-start | bytes 393224 | tf_op jit(solution)/shard_map/ppermute | solution.py:176
  41.4 0.3 adjoint.3
  41.7 1.4 %collective-permute-start.27 = (bf16[2,128,128]{2,1,0:T(8,128)(2,1)S(1)}, bf16[2,128,128]{2,1,0:T(8,128)(2,1)S(1)}, u32[]{:S(2)}, u32[]{:S(2)}) collective-permute-start(bf16[2,128,128]{2,1,0:T(8,128)(2,1)S(1)} %get-tuple-element.51), channel_id=1, source_target_pairs={{0,4},{4,0},{8,12},{12,8},{16,20},{20,16},{24,28},{28,24},{1,5},{5... | collective-permute-start | bytes 196616 | tf_op jit(solution)/shard_map/ppermute | solution.py:176
  43.1 0.7 %collective-permute-start.25 = (bf16[2,128,128]{2,1,0:T(8,128)(2,1)S(1)}, bf16[2,128,128]{2,1,0:T(8,128)(2,1)S(1)}, u32[]{:S(2)}, u32[]{:S(2)}) collective-permute-start(bf16[2,128,128]{2,1,0:T(8,128)(2,1)S(1)} %get-tuple-element.47), channel_id=1, source_target_pairs={{0,4},{4,0},{8,12},{12,8},{16,20},{20,16},{24,28},{28,24},{1,5},{5... | collective-permute-start | bytes 196616 | tf_op jit(solution)/shard_map/ppermute | solution.py:176
  43.8 4.0 %collective-permute-done.27.got_ref = bf16[2,128,128]{2,1,0:T(8,128)(2,1)S(1)} collective-permute-done((bf16[2,128,128]{2,1,0:T(8,128)(2,1)S(1)}, bf16[2,128,128]{2,1,0:T(8,128)(2,1)S(1)}, u32[]{:S(2)}, u32[]{:S(2)}) %collective-permute-start.27) | collective-permute-done | bytes 65568 | tf_op jit(solution)/shard_map/ppermute | solution.py:176
  47.8 0.8 %collective-permute-start.28 = (bf16[128,128]{1,0:T(8,128)(2,1)S(1)}, bf16[128,128]{1,0:T(8,128)(2,1)S(1)}, u32[]{:S(2)}, u32[]{:S(2)}) collective-permute-start(bf16[128,128]{1,0:T(8,128)(2,1)S(1)} %get-tuple-element.52), channel_id=1, source_target_pairs={{0,16},{4,20},{8,24},{12,28},{16,0},{20,4},{24,8},{28,12},{1,17},{... | collective-permute-start | bytes 98312 | tf_op jit(solution)/shard_map/ppermute | solution.py:176
  48.6 1.1 %collective-permute-start.29 = (bf16[128,128]{1,0:T(8,128)(2,1)S(1)}, bf16[128,128]{1,0:T(8,128)(2,1)S(1)}, u32[]{:S(2)}, u32[]{:S(2)}) collective-permute-start(bf16[128,128]{1,0:T(8,128)(2,1)S(1)} %get-tuple-element.53), channel_id=1, source_target_pairs={{0,24},{4,28},{8,16},{12,20},{16,8},{20,12},{24,0},{28,4},{1,25},{... | collective-permute-start | bytes 98312 | tf_op jit(solution)/shard_map/ppermute | solution.py:176
  49.7 1.7 %collective-permute-start.26 = (bf16[128,128]{1,0:T(8,128)(2,1)S(1)}, bf16[128,128]{1,0:T(8,128)(2,1)S(1)}, u32[]{:S(2)}, u32[]{:S(2)}) collective-permute-start(bf16[128,128]{1,0:T(8,128)(2,1)S(1)} %get-tuple-element.49), channel_id=1, source_target_pairs={{0,8},{4,12},{8,0},{12,4},{16,24},{20,28},{24,16},{28,20},{1,9},{5... | collective-permute-start | bytes 98312 | tf_op jit(solution)/shard_map/ppermute | solution.py:176
  51.5 0.4 forward.3
  52.0 1.1 %collective-permute-start.12 = (bf16[128,128]{1,0:T(8,128)(2,1)S(1)}, bf16[128,128]{1,0:T(8,128)(2,1)S(1)}, u32[]{:S(2)}, u32[]{:S(2)}) collective-permute-start(bf16[128,128]{1,0:T(8,128)(2,1)S(1)} %get-tuple-element.34), channel_id=1, source_target_pairs={{0,2},{1,3},{2,0},{3,1},{4,6},{5,7},{6,4},{7,5},{8,10},{9,11},{10,... | collective-permute-start | bytes 98312 | tf_op jit(solution)/shard_map/ppermute | solution.py:176
  53.0 0.8 %collective-permute-start.13 = (bf16[128,128]{1,0:T(8,128)(2,1)S(1)}, bf16[128,128]{1,0:T(8,128)(2,1)S(1)}, u32[]{:S(2)}, u32[]{:S(2)}) collective-permute-start(bf16[128,128]{1,0:T(8,128)(2,1)S(1)} %get-tuple-element.35), channel_id=1, source_target_pairs={{0,3},{1,2},{2,1},{3,0},{4,7},{5,6},{6,5},{7,4},{8,11},{9,10},{10,... | collective-permute-start | bytes 98312 | tf_op jit(solution)/shard_map/ppermute | solution.py:176
  53.8 0.4 collective-permute-done.29.refs_3_
  54.3 1.3 %adjoint_end.1 = f32[128,128]{1,0:T(8,128)} custom-call(f32[128,128]{1,0:T(8,128)S(1)} %copy-done.2, f32[128,128]{1,0:T(8,128)S(1)} %get-tuple-element.44.d_ref, s32[1,128]{1,0:T(1,128)S(1)} %bitcast.4, f32[8]{0:T(128)S(1)} %copy-done.4, f32[128,128]{1,0:T(8,128)S(1)} %get-tuple-element.48.refs_0_, bf16[128,128]{1,0:T(8,128)(2,1)S(1)} %collective-permute-done.26.refs_1_, ...), custom_call_target="tpu_custom_call" | custom-call | bytes 360992 | tf_op jit(solution)/shard_map/adjoint_end/pallas_call | solution.py:27
  55.6 0.4 collective-permute-done.12.refs_2_
  56.0 0.4 collective-permute-done.13.refs_3_
  56.4 1.3 %forward_end.3 = f32[128,128]{1,0:T(8,128)} custom-call(f32[128,128]{1,0:T(8,128)S(1)} %copy-done.1, s32[1,128]{1,0:T(1,128)S(1)} %bitcast.5, f32[8]{0:T(128)S(1)} %copy-done.4, bf16[128,128]{1,0:T(8,128)(2,1)S(1)} %get-tuple-element.32.refs_0_, bf16[128,128]{1,0:T(8,128)(2,1)S(1)} %collective-permute-done.11.refs_1_, ...), custom_call_target="tpu_custom_call" | custom-call | bytes 262688 | tf_op jit(solution)/shard_map/forward_end/pallas_call | solution.py:27
  (43 shorter events, 0.4 us)
Async XLA Ops:
  1.5 13.0 %copy-start.2 = (f32[128,128]{1,0:T(8,128)S(1)}, f32[128,128]{1,0:T(8,128)}, u32[]{:S(2)}) copy-start(f32[128,128]{1,0:T(8,128)} %cot_ref.1) | copy-start | bytes 196612
  1.5 5.6 %collective-permute-start = (bf16[128,128]{1,0:T(8,128)(2,1)S(1)}, bf16[128,128]{1,0:T(8,128)(2,1)S(1)}, u32[]{:S(2)}, u32[]{:S(2)}) collective-permute-start(bf16[128,128]{1,0:T(8,128)(2,1)S(1)} %convert_element_type.3.refs_0_.refs_2_), channel_id=1, source_target_pairs={{0,8},{4,12},{8,0},{12,4},{16,24},{20,28},{24,16},{28,20},{1,9},{5... | collective-permute-start | bytes 98312 | tf_op jit(solution)/shard_map/ppermute | solution.py:176
  4.5 5.4 %collective-permute-start.1 = (bf16[128,128]{1,0:T(8,128)(2,1)S(1)}, bf16[128,128]{1,0:T(8,128)(2,1)S(1)}, u32[]{:S(2)}, u32[]{:S(2)}) collective-permute-start(bf16[128,128]{1,0:T(8,128)(2,1)S(1)} %convert_element_type.3.refs_0_.refs_2_), channel_id=1, source_target_pairs={{0,16},{4,20},{8,24},{12,28},{16,0},{20,4},{24,8},{28,12},{1,17},{... | collective-permute-start | bytes 98312 | tf_op jit(solution)/shard_map/ppermute | solution.py:176
  7.1 5.7 %collective-permute-start.2 = (bf16[128,128]{1,0:T(8,128)(2,1)S(1)}, bf16[128,128]{1,0:T(8,128)(2,1)S(1)}, u32[]{:S(2)}, u32[]{:S(2)}) collective-permute-start(bf16[128,128]{1,0:T(8,128)(2,1)S(1)} %convert_element_type.3.refs_0_.refs_2_), channel_id=1, source_target_pairs={{0,24},{4,28},{8,16},{12,20},{16,8},{20,12},{24,0},{28,4},{1,25},{... | collective-permute-start | bytes 98312 | tf_op jit(solution)/shard_map/ppermute | solution.py:176
  12.8 1.6 %copy-start.3 = (s32[128]{0:T(128)S(1)}, s32[128]{0:T(128)}, u32[]{:S(2)}) copy-start(s32[128]{0:T(128)} %param.10) | copy-start | bytes 1540
  12.8 1.6 %copy-start.4 = (f32[8]{0:T(128)S(1)}, f32[8]{0:T(128)}, u32[]{:S(2)}) copy-start(f32[8]{0:T(128)} %teleport_ref.7) | copy-start | bytes 100
  12.8 9.8 %collective-permute-start.3 = (bf16[4,128,128]{2,1,0:T(8,128)(2,1)S(1)}, bf16[4,128,128]{2,1,0:T(8,128)(2,1)S(1)}, u32[]{:S(2)}, u32[]{:S(2)}) collective-permute-start(bf16[4,128,128]{2,1,0:T(8,128)(2,1)S(1)} %pack.2), channel_id=1, source_target_pairs={{0,4},{4,0},{8,12},{12,8},{16,20},{20,16},{24,28},{28,24},{1,5},{5... | collective-permute-start | bytes 393224 | tf_op jit(solution)/shard_map/ppermute | solution.py:176
  15.2 2.6 %copy-start.5 = (s32[1,1,24]{2,1,0:T(1,128)S(1)}, s32[1,1,24]{2,1,0:T(1,128)}, u32[]{:S(2)}) copy-start(s32[1,1,24]{2,1,0:T(1,128)} %row_hbm.1) | copy-start | bytes 292
  15.2 2.6 %copy-start.6 = (s32[1,1,24]{2,1,0:T(1,128)S(1)}, s32[1,1,24]{2,1,0:T(1,128)}, u32[]{:S(2)}) copy-start(s32[1,1,24]{2,1,0:T(1,128)} %col_hbm.1) | copy-start | bytes 292
  15.2 4.8 %collective-permute-start.14 = (bf16[128,128]{1,0:T(8,128)(2,1)S(1)}, bf16[128,128]{1,0:T(8,128)(2,1)S(1)}, u32[]{:S(2)}, u32[]{:S(2)}) collective-permute-start(bf16[128,128]{1,0:T(8,128)(2,1)S(1)} %start.1.refs_1_), channel_id=1, source_target_pairs={{0,1},{1,0},{2,3},{3,2},{4,5},{5,4},{6,7},{7,6},{8,9},{9,8},{10,11... | collective-permute-start | bytes 98312 | tf_op jit(solution)/shard_map/ppermute | solution.py:176
  15.3 4.7 %collective-permute-start.15 = (bf16[128,128]{1,0:T(8,128)(2,1)S(1)}, bf16[128,128]{1,0:T(8,128)(2,1)S(1)}, u32[]{:S(2)}, u32[]{:S(2)}) collective-permute-start(bf16[128,128]{1,0:T(8,128)(2,1)S(1)} %start.1.refs_1_), channel_id=1, source_target_pairs={{0,2},{1,3},{2,0},{3,1},{4,6},{5,7},{6,4},{7,5},{8,10},{9,11},{10,... | collective-permute-start | bytes 98312 | tf_op jit(solution)/shard_map/ppermute | solution.py:176
  16.9 3.3 %collective-permute-start.16 = (bf16[128,128]{1,0:T(8,128)(2,1)S(1)}, bf16[128,128]{1,0:T(8,128)(2,1)S(1)}, u32[]{:S(2)}, u32[]{:S(2)}) collective-permute-start(bf16[128,128]{1,0:T(8,128)(2,1)S(1)} %start.1.refs_1_), channel_id=1, source_target_pairs={{0,3},{1,2},{2,1},{3,0},{4,7},{5,6},{6,5},{7,4},{8,11},{9,10},{10,... | collective-permute-start | bytes 98312 | tf_op jit(solution)/shard_map/ppermute | solution.py:176
  17.8 1.1 %copy-start = (bf16[1,1,24,128,128]{4,3,2,1,0:T(8,128)(2,1)S(1)}, bf16[1,1,24,128,128]{4,3,2,1,0:T(8,128)(2,1)}, u32[]{:S(2)}) copy-start(bf16[1,1,24,128,128]{4,3,2,1,0:T(8,128)(2,1)} %tiles_hbm.1) | copy-start | bytes 2359300
  20.5 6.4 %collective-permute-start.19 = (f32[2,128,128]{2,1,0:T(8,128)S(1)}, f32[2,128,128]{2,1,0:T(8,128)S(1)}, u32[]{:S(2)}, u32[]{:S(2)}) collective-permute-start(f32[2,128,128]{2,1,0:T(8,128)S(1)} %get-tuple-element.41), channel_id=1, source_target_pairs={{0,4},{4,0},{8,12},{12,8},{16,20},{20,16},{24,28},{28,24},{1,5},{5... | collective-permute-start | bytes 393224 | tf_op jit(solution)/shard_map/ppermute | solution.py:176
  21.1 7.8 %collective-permute-start.17 = (f32[2,128,128]{2,1,0:T(8,128)S(1)}, f32[2,128,128]{2,1,0:T(8,128)S(1)}, u32[]{:S(2)}, u32[]{:S(2)}) collective-permute-start(f32[2,128,128]{2,1,0:T(8,128)S(1)} %get-tuple-element.37), channel_id=1, source_target_pairs={{0,4},{4,0},{8,12},{12,8},{16,20},{20,16},{24,28},{28,24},{1,5},{5... | collective-permute-start | bytes 393224 | tf_op jit(solution)/shard_map/ppermute | solution.py:176
  23.1 6.3 %collective-permute-start.4 = (f32[128,128]{1,0:T(8,128)S(1)}, f32[128,128]{1,0:T(8,128)S(1)}, u32[]{:S(2)}, u32[]{:S(2)}) collective-permute-start(f32[128,128]{1,0:T(8,128)S(1)} %get-tuple-element.29), channel_id=1, source_target_pairs={{0,1},{1,0},{2,3},{3,2},{4,5},{5,4},{6,7},{7,6},{8,9},{9,8},{10,11... | collective-permute-start | bytes 196616 | tf_op jit(solution)/shard_map/ppermute | solution.py:176
  23.1 7.5 %collective-permute-start.5 = (f32[128,128]{1,0:T(8,128)S(1)}, f32[128,128]{1,0:T(8,128)S(1)}, u32[]{:S(2)}, u32[]{:S(2)}) collective-permute-start(f32[128,128]{1,0:T(8,128)S(1)} %get-tuple-element.30), channel_id=1, source_target_pairs={{0,2},{1,3},{2,0},{3,1},{4,6},{5,7},{6,4},{7,5},{8,10},{9,11},{10,... | collective-permute-start | bytes 196616 | tf_op jit(solution)/shard_map/ppermute | solution.py:176
  24.5 6.1 %collective-permute-start.6 = (f32[128,128]{1,0:T(8,128)S(1)}, f32[128,128]{1,0:T(8,128)S(1)}, u32[]{:S(2)}, u32[]{:S(2)}) collective-permute-start(f32[128,128]{1,0:T(8,128)S(1)} %get-tuple-element.31), channel_id=1, source_target_pairs={{0,3},{1,2},{2,1},{3,0},{4,7},{5,6},{6,5},{7,4},{8,11},{9,10},{10,... | collective-permute-start | bytes 196616 | tf_op jit(solution)/shard_map/ppermute | solution.py:176
  26.9 8.0 %collective-permute-start.20 = (f32[128,128]{1,0:T(8,128)S(1)}, f32[128,128]{1,0:T(8,128)S(1)}, u32[]{:S(2)}, u32[]{:S(2)}) collective-permute-start(f32[128,128]{1,0:T(8,128)S(1)} %get-tuple-element.42), channel_id=1, source_target_pairs={{0,16},{4,20},{8,24},{12,28},{16,0},{20,4},{24,8},{28,12},{1,17},{... | collective-permute-start | bytes 196616 | tf_op jit(solution)/shard_map/ppermute | solution.py:176
  29.0 6.8 %collective-permute-start.21 = (f32[128,128]{1,0:T(8,128)S(1)}, f32[128,128]{1,0:T(8,128)S(1)}, u32[]{:S(2)}, u32[]{:S(2)}) collective-permute-start(f32[128,128]{1,0:T(8,128)S(1)} %get-tuple-element.43), channel_id=1, source_target_pairs={{0,24},{4,28},{8,16},{12,20},{16,8},{20,12},{24,0},{28,4},{1,25},{... | collective-permute-start | bytes 196616 | tf_op jit(solution)/shard_map/ppermute | solution.py:176
  29.3 1.3 %copy-start.1 = (f32[128,128]{1,0:T(8,128)S(1)}, f32[128,128]{1,0:T(8,128)}, u32[]{:S(2)}) copy-start(f32[128,128]{1,0:T(8,128)} %h_ref.3) | copy-start | bytes 196612
  29.3 6.4 %collective-permute-start.18 = (f32[128,128]{1,0:T(8,128)S(1)}, f32[128,128]{1,0:T(8,128)S(1)}, u32[]{:S(2)}, u32[]{:S(2)}) collective-permute-start(f32[128,128]{1,0:T(8,128)S(1)} %get-tuple-element.39), channel_id=1, source_target_pairs={{0,8},{4,12},{8,0},{12,4},{16,24},{20,28},{24,16},{28,20},{1,9},{5... | collective-permute-start | bytes 196616 | tf_op jit(solution)/shard_map/ppermute | solution.py:176
  31.3 6.6 %collective-permute-start.7 = (bf16[128,128]{1,0:T(8,128)(2,1)S(1)}, bf16[128,128]{1,0:T(8,128)(2,1)S(1)}, u32[]{:S(2)}, u32[]{:S(2)}) collective-permute-start(bf16[128,128]{1,0:T(8,128)(2,1)S(1)} %forward_end.2.refs_0_.refs_2_), channel_id=1, source_target_pairs={{0,8},{4,12},{8,0},{12,4},{16,24},{20,28},{24,16},{28,20},{1,9},{5... | collective-permute-start | bytes 98312 | tf_op jit(solution)/shard_map/ppermute | solution.py:176
  32.2 6.1 %collective-permute-start.8 = (bf16[128,128]{1,0:T(8,128)(2,1)S(1)}, bf16[128,128]{1,0:T(8,128)(2,1)S(1)}, u32[]{:S(2)}, u32[]{:S(2)}) collective-permute-start(bf16[128,128]{1,0:T(8,128)(2,1)S(1)} %forward_end.2.refs_0_.refs_2_), channel_id=1, source_target_pairs={{0,16},{4,20},{8,24},{12,28},{16,0},{20,4},{24,8},{28,12},{1,17},{... | collective-permute-start | bytes 98312 | tf_op jit(solution)/shard_map/ppermute | solution.py:176
  34.9 5.7 %collective-permute-start.9 = (bf16[128,128]{1,0:T(8,128)(2,1)S(1)}, bf16[128,128]{1,0:T(8,128)(2,1)S(1)}, u32[]{:S(2)}, u32[]{:S(2)}) collective-permute-start(bf16[128,128]{1,0:T(8,128)(2,1)S(1)} %forward_end.2.refs_0_.refs_2_), channel_id=1, source_target_pairs={{0,24},{4,28},{8,16},{12,20},{16,8},{20,12},{24,0},{28,4},{1,25},{... | collective-permute-start | bytes 98312 | tf_op jit(solution)/shard_map/ppermute | solution.py:176
  36.3 5.1 %collective-permute-start.22 = (bf16[128,128]{1,0:T(8,128)(2,1)S(1)}, bf16[128,128]{1,0:T(8,128)(2,1)S(1)}, u32[]{:S(2)}, u32[]{:S(2)}) collective-permute-start(bf16[128,128]{1,0:T(8,128)(2,1)S(1)} %get-tuple-element.45.refs_1_), channel_id=1, source_target_pairs={{0,1},{1,0},{2,3},{3,2},{4,5},{5,4},{6,7},{7,6},{8,9},{9,8},{10,11... | collective-permute-start | bytes 98312 | tf_op jit(solution)/shard_map/ppermute | solution.py:176
  36.4 5.0 %collective-permute-start.23 = (bf16[128,128]{1,0:T(8,128)(2,1)S(1)}, bf16[128,128]{1,0:T(8,128)(2,1)S(1)}, u32[]{:S(2)}, u32[]{:S(2)}) collective-permute-start(bf16[128,128]{1,0:T(8,128)(2,1)S(1)} %get-tuple-element.45.refs_1_), channel_id=1, source_target_pairs={{0,2},{1,3},{2,0},{3,1},{4,6},{5,7},{6,4},{7,5},{8,10},{9,11},{10,... | collective-permute-start | bytes 98312 | tf_op jit(solution)/shard_map/ppermute | solution.py:176
  37.8 3.5 %collective-permute-start.24 = (bf16[128,128]{1,0:T(8,128)(2,1)S(1)}, bf16[128,128]{1,0:T(8,128)(2,1)S(1)}, u32[]{:S(2)}, u32[]{:S(2)}) collective-permute-start(bf16[128,128]{1,0:T(8,128)(2,1)S(1)} %get-tuple-element.45.refs_1_), channel_id=1, source_target_pairs={{0,3},{1,2},{2,1},{3,0},{4,7},{5,6},{6,5},{7,4},{8,11},{9,10},{10,... | collective-permute-start | bytes 98312 | tf_op jit(solution)/shard_map/ppermute | solution.py:176
  40.6 10.8 %collective-permute-start.10 = (bf16[4,128,128]{2,1,0:T(8,128)(2,1)S(1)}, bf16[4,128,128]{2,1,0:T(8,128)(2,1)S(1)}, u32[]{:S(2)}, u32[]{:S(2)}) collective-permute-start(bf16[4,128,128]{2,1,0:T(8,128)(2,1)S(1)} %pack.3), channel_id=1, source_target_pairs={{0,4},{4,0},{8,12},{12,8},{16,20},{20,16},{24,28},{28,24},{1,5},{5... | collective-permute-start | bytes 393224 | tf_op jit(solution)/shard_map/ppermute | solution.py:176
  41.7 6.1 %collective-permute-start.27 = (bf16[2,128,128]{2,1,0:T(8,128)(2,1)S(1)}, bf16[2,128,128]{2,1,0:T(8,128)(2,1)S(1)}, u32[]{:S(2)}, u32[]{:S(2)}) collective-permute-start(bf16[2,128,128]{2,1,0:T(8,128)(2,1)S(1)} %get-tuple-element.51), channel_id=1, source_target_pairs={{0,4},{4,0},{8,12},{12,8},{16,20},{20,16},{24,28},{28,24},{1,5},{5... | collective-permute-start | bytes 196616 | tf_op jit(solution)/shard_map/ppermute | solution.py:176
  43.1 6.6 %collective-permute-start.25 = (bf16[2,128,128]{2,1,0:T(8,128)(2,1)S(1)}, bf16[2,128,128]{2,1,0:T(8,128)(2,1)S(1)}, u32[]{:S(2)}, u32[]{:S(2)}) collective-permute-start(bf16[2,128,128]{2,1,0:T(8,128)(2,1)S(1)} %get-tuple-element.47), channel_id=1, source_target_pairs={{0,4},{4,0},{8,12},{12,8},{16,20},{20,16},{24,28},{28,24},{1,5},{5... | collective-permute-start | bytes 196616 | tf_op jit(solution)/shard_map/ppermute | solution.py:176
  47.8 5.2 %collective-permute-start.28 = (bf16[128,128]{1,0:T(8,128)(2,1)S(1)}, bf16[128,128]{1,0:T(8,128)(2,1)S(1)}, u32[]{:S(2)}, u32[]{:S(2)}) collective-permute-start(bf16[128,128]{1,0:T(8,128)(2,1)S(1)} %get-tuple-element.52), channel_id=1, source_target_pairs={{0,16},{4,20},{8,24},{12,28},{16,0},{20,4},{24,8},{28,12},{1,17},{... | collective-permute-start | bytes 98312 | tf_op jit(solution)/shard_map/ppermute | solution.py:176
  48.6 5.7 %collective-permute-start.29 = (bf16[128,128]{1,0:T(8,128)(2,1)S(1)}, bf16[128,128]{1,0:T(8,128)(2,1)S(1)}, u32[]{:S(2)}, u32[]{:S(2)}) collective-permute-start(bf16[128,128]{1,0:T(8,128)(2,1)S(1)} %get-tuple-element.53), channel_id=1, source_target_pairs={{0,24},{4,28},{8,16},{12,20},{16,8},{20,12},{24,0},{28,4},{1,25},{... | collective-permute-start | bytes 98312 | tf_op jit(solution)/shard_map/ppermute | solution.py:176
  49.7 4.5 %collective-permute-start.26 = (bf16[128,128]{1,0:T(8,128)(2,1)S(1)}, bf16[128,128]{1,0:T(8,128)(2,1)S(1)}, u32[]{:S(2)}, u32[]{:S(2)}) collective-permute-start(bf16[128,128]{1,0:T(8,128)(2,1)S(1)} %get-tuple-element.49), channel_id=1, source_target_pairs={{0,8},{4,12},{8,0},{12,4},{16,24},{20,28},{24,16},{28,20},{1,9},{5... | collective-permute-start | bytes 98312 | tf_op jit(solution)/shard_map/ppermute | solution.py:176
  51.9 3.7 %collective-permute-start.11 = (bf16[128,128]{1,0:T(8,128)(2,1)S(1)}, bf16[128,128]{1,0:T(8,128)(2,1)S(1)}, u32[]{:S(2)}, u32[]{:S(2)}) collective-permute-start(bf16[128,128]{1,0:T(8,128)(2,1)S(1)} %get-tuple-element.33), channel_id=1, source_target_pairs={{0,1},{1,0},{2,3},{3,2},{4,5},{5,4},{6,7},{7,6},{8,9},{9,8},{10,11... | collective-permute-start | bytes 98312 | tf_op jit(solution)/shard_map/ppermute | solution.py:176
  52.0 4.0 %collective-permute-start.12 = (bf16[128,128]{1,0:T(8,128)(2,1)S(1)}, bf16[128,128]{1,0:T(8,128)(2,1)S(1)}, u32[]{:S(2)}, u32[]{:S(2)}) collective-permute-start(bf16[128,128]{1,0:T(8,128)(2,1)S(1)} %get-tuple-element.34), channel_id=1, source_target_pairs={{0,2},{1,3},{2,0},{3,1},{4,6},{5,7},{6,4},{7,5},{8,10},{9,11},{10,... | collective-permute-start | bytes 98312 | tf_op jit(solution)/shard_map/ppermute | solution.py:176
  53.0 3.3 %collective-permute-start.13 = (bf16[128,128]{1,0:T(8,128)(2,1)S(1)}, bf16[128,128]{1,0:T(8,128)(2,1)S(1)}, u32[]{:S(2)}, u32[]{:S(2)}) collective-permute-start(bf16[128,128]{1,0:T(8,128)(2,1)S(1)} %get-tuple-element.35), channel_id=1, source_target_pairs={{0,3},{1,2},{2,1},{3,0},{4,7},{5,6},{6,5},{7,4},{8,11},{9,10},{10,... | collective-permute-start | bytes 98312 | tf_op jit(solution)/shard_map/ppermute | solution.py:176

commit v4 on v3

--- a/solution.py
+++ b/solution.py
@@ -20,6 +20,10 @@
 
 def hbm():
     return pl.BlockSpec(memory_space=pltpu.HBM)
+
+
+def in_hbm(*arrays):
+    return [pltpu.with_memory_space_constraint(a, pltpu.HBM) for a in arrays]
 
 
 def call(body, outs, in_specs, args, flops, name, scratch=()):
@@ -57,23 +61,54 @@
     return jnp.broadcast_to(row, (width, size)).T
 
 
-def start_body(cot_hbm, types_hbm, teleport_hbm, q_ref, cot_ref, types_ref, teleport_ref, sems):
+def start_body(
+    cot_hbm,
+    h_hbm,
+    types_hbm,
+    teleport_hbm,
+    q_ref,
+    p_ref,
+    row_ref,
+    column_ref,
+    cot_ref,
+    h_ref,
+    types_ref,
+    teleport_ref,
+    sems,
+):
     fetch(
-        [(cot_hbm, cot_ref), (types_hbm, types_ref), (teleport_hbm, teleport_ref)],
+        [
+            (types_hbm, types_ref),
+            (teleport_hbm, teleport_ref),
+            (cot_hbm, cot_ref),
+            (h_hbm, h_ref),
+        ],
         sems,
     )
     rate = rate_row(types_ref, teleport_ref)
+    row_ref[...] = rate
+    column_ref[...] = rate_column(rate, h_ref.shape[1])
     q_ref[...] = ((1.0 - rate) * cot_ref[...].T).astype(BF16)
+    p_ref[...] = h_ref[...].astype(BF16)
 
 
 def dense_body(
-    tiles_hbm, row_hbm, col_hbm, count_hbm, dense_ref, row_ref, col_ref, count_ref, sems, slot_sems
+    q_ref,
+    tiles_hbm,
+    row_hbm,
+    col_hbm,
+    count_ref,
+    dense_ref,
+    row_ref,
+    col_ref,
+    sems,
+    slot_sems,
 ):
     size = tiles_hbm.shape[-1]
     me_row = lax.axis_index("rows")
     me_col = lax.axis_index("cols")
     dense_ref[...] = jnp.zeros_like(dense_ref)
-    fetch([(row_hbm, row_ref), (col_hbm, col_ref), (count_hbm, count_ref)], sems)
+    fetch([(row_hbm, row_ref), (col_hbm, col_ref)], sems)
     count = count_ref[0, 0]
 
     def copy(slot):
@@ -101,8 +136,8 @@
 
 
 def adjoint_body(n_rows, n_cols, dense_ref, *refs):
-    blocks, outs = refs[:n_cols], refs[n_cols:]
-    send_far, send_near, keep_far, keep_near = outs
+    blocks, refs = refs[:n_cols], refs[n_cols:]
+    *pair, send_far, send_near, keep_far, keep_near = refs
     half = n_rows // 2
     near = send_near.shape[0]
     size = blocks[0].shape[1]
@@ -116,6 +151,10 @@
         )
         keep[at] = part[:, :size]
         send[at] = part[:, size:].astype(send.dtype)
+    if pair:
+        own, other, both = pair
+        both[0] = own[...]
+        both[1] = other[...]
 
 
 def add_body(keep_ref, got_ref, *outs):
@@ -129,12 +168,16 @@
         out_ref[at] = part[...]
 
 
-def forward_body(half, n_cols, dense_ref, other_ref, *refs):
-    panels, outs = refs[:half], refs[half:]
-    size = panels[0].shape[0]
+def forward_body(half, n_cols, paired, dense_ref, *refs):
+    count = half if paired else half + 1
+    panels, outs = refs[:count], refs[count:]
+    size = panels[0].shape[-1]
     total = None
     for zz in range(half):
-        panel = jnp.concatenate([panels[zz][...], other_ref[zz]], axis=0)
+        if paired:
+            panel = jnp.concatenate([panels[zz][0], panels[zz][1]], axis=0)
+        else:
+            panel = jnp.concatenate([panels[zz][...], panels[half][zz]], axis=0)
         part = jnp.dot(
             dense_ref[:, 2 * zz * size : (2 * zz + 2) * size], panel, preferred_element_type=F32
         )
@@ -150,26 +193,24 @@
     return terms[0]
 
 
-def forward_end_body(h_ref, types_ref, teleport_ref, *refs):
+def forward_end_body(h_ref, rate_ref, *refs):
     *parts, out_ref = refs
-    rate = rate_column(rate_row(types_ref, teleport_ref), h_ref.shape[1])
+    rate = rate_ref[...]
     value = (1.0 - rate) * sum_refs(parts) + rate * h_ref[...]
     out_ref[...] = value.astype(out_ref.dtype)
 
 
-def adjoint_mid_body(types_ref, teleport_ref, *refs):
+def adjoint_mid_body(rate_ref, *refs):
     *parts, d_ref, q_ref = refs
-    rate = rate_row(types_ref, teleport_ref)
     total = sum_refs(parts)
     d_ref[...] = total
-    q_ref[...] = ((1.0 - rate) * total).astype(BF16)
-
-
-def adjoint_end_body(cot_ref, d_ref, types_ref, teleport_ref, *refs):
+    q_ref[...] = ((1.0 - rate_ref[...]) * total).astype(BF16)
+
+
+def adjoint_end_body(cot_ref, d_ref, row_ref, column_ref, *refs):
     *parts, out_ref = refs
-    rate = rate_row(types_ref, teleport_ref)
-    column = rate_column(rate, cot_ref.shape[1])
-    out_ref[...] = column * cot_ref[...] + (rate * d_ref[...] + sum_refs(parts)).T
+    change = (row_ref[...] * d_ref[...] + sum_refs(parts)).T
+    out_ref[...] = column_ref[...] * cot_ref[...] + change
 
 
 def send(value, axis, count, step):
@@ -190,47 +231,48 @@
     def shape(kind, *lead):
         return jax.ShapeDtypeStruct((*lead, size, features), kind)
 
-    (q0,) = call(
+    q0, p0, rate, column = call(
         start_body,
-        [shape(BF16)],
-        [hbm()] * 3,
-        (cotangent, types, teleport),
+        [shape(BF16), shape(BF16), jax.ShapeDtypeStruct((1, size), F32), shape(F32)],
+        [hbm()] * 4,
+        in_hbm(cotangent, h_start, types, teleport),
         0,
         "start",
         [
             pltpu.VMEM(cotangent.shape, F32),
+            pltpu.VMEM(h_start.shape, F32),
             pltpu.VMEM(types.shape, jnp.int32),
             pltpu.SMEM(teleport.shape, F32),
-            pltpu.SemaphoreType.DMA((3,)),
+            pltpu.SemaphoreType.DMA((4,)),
         ],
     )
     (dense,) = call(
         dense_body,
         [jax.ShapeDtypeStruct((n_cols * size, n_rows * size), BF16)],
-        [hbm()] * 4,
-        (tile_values, tile_row, tile_col, tile_count),
+        [vmem()] + [hbm()] * 3 + [smem()],
+        [q0, *in_hbm(tile_values, tile_row, tile_col), tile_count],
         0,
         "dense",
         [
             pltpu.SMEM(tile_row.shape, jnp.int32),
             pltpu.SMEM(tile_col.shape, jnp.int32),
-            pltpu.SMEM(tile_count.shape, jnp.int32),
-            pltpu.SemaphoreType.DMA((3,)),
+            pltpu.SemaphoreType.DMA((2,)),
             pltpu.SemaphoreType.DMA((slots,)),
         ],
     )
-    p0 = h_start.astype(BF16)
 
     def add(keep, got, kinds, name):
         return call(add_body, [shape(kind) for kind in kinds], [vmem()] * 2, (keep, got), 0, name)
 
-    def adjoint_hop(part, kind):
+    def adjoint_hop(part, kind, pair):
         blocks = [part] + [send(part, "cols", n_cols, s) for s in range(1, n_cols)]
-        send_far, send_near, keep_far, keep_near = call(
+        *both, send_far, send_near, keep_far, keep_near = call(
             lambda *refs: adjoint_body(n_rows, n_cols, *refs),
-            [shape(kind, half - near), shape(kind, near), shape(F32, half - near), shape(F32, near)],
-            [vmem()] * (1 + n_cols),
-            [dense, *blocks],
+            [shape(BF16, 2)] * (len(pair) // 2)
+            + [shape(kind, half - near), shape(kind, near)]
+            + [shape(F32, half - near), shape(F32, near)],
+            [vmem()] * (1 + n_cols + len(pair)),
+            [dense, *blocks, *pair],
             hop_flops,
             "adjoint",
         )
@@ -239,19 +281,20 @@
         kinds = [F32] + [kind] * (near - 1)
         close = add(keep_near, send(send_near, "rows", n_rows, 1), kinds, "add_near")
         close = [close[0]] + [send(close[s], "rows", n_rows, 2 * s) for s in range(1, near)]
-        return close + far
-
-    def forward_hop(part, kind):
+        return close + far, both
+
+    def forward_hop(part, kind, paired):
         panels = [part] + [send(part, "rows", n_rows, 2 * s) for s in range(1, half)]
-        (packed,) = call(
-            pack_body, [shape(BF16, half)], [vmem()] * half, panels, 0, "pack"
-        )
-        other = send(packed, "rows", n_rows, 1)
+        if not paired:
+            (packed,) = call(
+                pack_body, [shape(BF16, half)], [vmem()] * half, panels, 0, "pack"
+            )
+            panels = panels + [send(packed, "rows", n_rows, 1)]
         sums = call(
-            lambda *refs: forward_body(half, n_cols, *refs),
+            lambda *refs: forward_body(half, n_cols, paired, *refs),
             [shape(kind)] * n_cols,
-            [vmem()] * (2 + half),
-            (dense, other, *panels),
+            [vmem()] * (1 + len(panels)),
+            [dense, *panels],
             hop_flops,
             "forward",
         )
@@ -261,31 +304,31 @@
         return call(
             forward_end_body,
             [shape(kind)],
-            [vmem(), vmem(), smem()] + [vmem()] * n_cols,
-            (h_start, types, teleport, *parts),
+            [vmem()] * (2 + n_cols),
+            (h_start, column, *parts),
             0,
             "forward_end",
         )[0]
 
-    back = adjoint_hop(q0, F32)
-    first = forward_hop(p0, F32)
+    back, (both,) = adjoint_hop(q0, F32, [p0, send(p0, "rows", n_rows, 1)])
+    first = forward_hop(both, F32, True)
     d1, q1 = call(
         adjoint_mid_body,
         [shape(F32), shape(BF16)],
-        [vmem(), smem()] + [vmem()] * half,
-        (types, teleport, *back),
+        [vmem()] * (1 + half),
+        (rate, *back),
         0,
         "adjoint_mid",
     )
     p1 = forward_end(first, BF16)
-    back_two = adjoint_hop(q1, BF16)
-    second = forward_hop(p1, BF16)
+    back_two, _ = adjoint_hop(q1, BF16, [])
+    second = forward_hop(p1, BF16, False)
     propagated = forward_end(second, F32)
     (input_grad,) = call(
         adjoint_end_body,
         [shape(F32)],
-        [vmem(), vmem(), vmem(), smem()] + [vmem()] * half,
-        (cotangent, d1, types, teleport, *back_two),
+        [vmem()] * (4 + half),
+        (cotangent, d1, rate, column, *back_two),
         0,
         "adjoint_end",
     )

time: 57.9 us -> 58.8 us (1.016)
  waiting for transfers between devices: 17.4 us -> 19.7 us
  starting transfers between devices: 29.6 us -> 31.4 us
  Pallas kernels: 7.19 us -> 5.75 us
  local copies, waits for them, and re-layouts: 1.16 us -> 0.17 us
  other arithmetic: 0.85 us -> 0 us
    ppermute x30, waiting for transfers between devices: 17.4 us -> 19.7 us  [send(): return lax.ppermute(value, axis, [(i, i ^ step) for i in range(count)])]
    ppermute x30, starting transfers between devices: 29.6 us -> 31.4 us  [send(): return lax.ppermute(value, axis, [(i, i ^ step) for i in range(count)])]
    pallas_call x16 -> x15, Pallas kernels: 7.19 us -> 5.75 us  [call(): pl.pallas_call(body, out_shape=outs, in_specs=in_specs, out_specs=[vmem()...]
    unnamed x14 -> x4, local copies, waits for them, and re-layouts: 1.16 us -> 0.17 us
    convert_element_type x1 -> x0, other arithmetic: 0.85 us -> none  [shards(): p0 = h_start.astype(BF16)]
  transfers between devices with their start and end apart: 30 -> 30, of which waited for: 10 -> 12; matrix products, arithmetic and copies ran while one was open for 0% -> 0% of each run, Pallas kernels for 10% -> 6%
where the time goes in v4:
time: 58.8 us; the launch traced here: 58.5 us
  starting transfers between devices  31.4 us (53%)
  waiting for transfers between devices  19.7 us (34%)
  Pallas kernels  5.75 us (10%)
  between operations  1.45 us (2%)
    ppermute x30, starting transfers between devices, send(): return lax.ppermute(value, axis, [(i, i ^ step) for i in range(count)])  31.4 us
    ppermute x30, waiting for transfers between devices, send(): return lax.ppermute(value, axis, [(i, i ^ step) for i in range(count)])  19.7 us
    pallas_call x15, Pallas kernels, call(): pl.pallas_call(body, out_shape=outs, in_specs=in_specs, out_specs=[vmem()...  5.75 us
  transfers between devices with their start and end apart: 30, of which 12 were waited for; matrix products, arithmetic and copies ran while one was open for 0% of the time, Pallas kernels for 6%

profile of v4, /device:TPU:0, one launch (start us, length us, event | category | flops | bytes accessed | tf_op | source)
XLA Modules:
  0.0 58.5 jit_solution(13263327640116752462)
XLA Ops:
  0.6 1.0 %start.1 = (bf16[128,128]{1,0:T(8,128)(2,1)S(1)}, bf16[128,128]{1,0:T(8,128)(2,1)S(1)}, f32[1,128]{1,0:T(1,128)S(1)}, f32[128,128]{1,0:T(8,128)S(1)}) custom-call(f32[128,128]{1,0:T(8,128)} %cot_ref.1, f32[128,128]{1,0:T(8,128)} %h_ref.3, s32[1,128]{1,0:T(1,128)} %bitcast.1, f32[8]{0:T(128)} %teleport_hbm.1), custom_call_target="tpu_custom_call" | custom-call | bytes 263200 | tf_op jit(solution)/shard_map/start/pallas_call | solution.py:31
  1.7 0.5 collective-permute-start
  2.2 2.6 %collective-permute-start.1 = (bf16[128,128]{1,0:T(8,128)(2,1)S(1)}, bf16[128,128]{1,0:T(8,128)(2,1)S(1)}, u32[]{:S(2)}, u32[]{:S(2)}) collective-permute-start(bf16[128,128]{1,0:T(8,128)(2,1)S(1)} %get-tuple-element.34.q_ref.refs_1_), channel_id=1, source_target_pairs={{0,2},{1,3},{2,0},{3,1},{4,6},{5,7},{6,4},{7,5},{8,10},{9,11},{10,... | collective-permute-start | bytes 98312 | tf_op jit(solution)/shard_map/ppermute | solution.py:217
  4.8 1.8 %collective-permute-start.3 = (bf16[128,128]{1,0:T(8,128)(2,1)S(1)}, bf16[128,128]{1,0:T(8,128)(2,1)S(1)}, u32[]{:S(2)}, u32[]{:S(2)}) collective-permute-start(bf16[128,128]{1,0:T(8,128)(2,1)S(1)} %get-tuple-element.35.refs_5_), channel_id=1, source_target_pairs={{0,4},{4,0},{8,12},{12,8},{16,20},{20,16},{24,28},{28,24},{1,5},{5... | collective-permute-start | bytes 98312 | tf_op jit(solution)/shard_map/ppermute | solution.py:217
  7.2 1.7 %dense.1.refs_0_ = bf16[512,1024]{1,0:T(8,128)(2,1)S(1)} custom-call(bf16[128,128]{1,0:T(8,128)(2,1)S(1)} %get-tuple-element.34.q_ref.refs_1_, bf16[1,1,24,128,128]{4,3,2,1,0:T(8,128)(2,1)} %tiles_hbm.1, s32[1,1,24]{2,1,0:T(1,128)} %row_hbm.1, s32[1,1,24]{2,1,0:T(1,128)} %col_hbm.1, s32[1,1]{1,0:T(1,128)S(6)} %copy.10.count_ref), custom_call_target="tpu_custom_call" | custom-call | bytes 1867972 | tf_op jit(solution)/shard_map/dense/pallas_call | solution.py:31
  9.0 0.3 adjoint.2
  9.3 2.0 %collective-permute-start.4 = (bf16[2,128,128]{2,1,0:T(8,128)(2,1)S(1)}, bf16[2,128,128]{2,1,0:T(8,128)(2,1)S(1)}, u32[]{:S(2)}, u32[]{:S(2)}) collective-permute-start(bf16[2,128,128]{2,1,0:T(8,128)(2,1)S(1)} %get-tuple-element.36.refs_1_), channel_id=1, source_target_pairs={{0,8},{4,12},{8,0},{12,4},{16,24},{20,28},{24,16},{28,20},{1,9},{5... | collective-permute-start | bytes 196616 | tf_op jit(solution)/shard_map/ppermute | solution.py:217
  11.3 2.3 %collective-permute-start.5 = (bf16[2,128,128]{2,1,0:T(8,128)(2,1)S(1)}, bf16[2,128,128]{2,1,0:T(8,128)(2,1)S(1)}, u32[]{:S(2)}, u32[]{:S(2)}) collective-permute-start(bf16[2,128,128]{2,1,0:T(8,128)(2,1)S(1)} %get-tuple-element.36.refs_1_), channel_id=1, source_target_pairs={{0,16},{4,20},{8,24},{12,28},{16,0},{20,4},{24,8},{28,12},{1,17},{... | collective-permute-start | bytes 196616 | tf_op jit(solution)/shard_map/ppermute | solution.py:217
  13.6 0.2 collective-permute-start.6
  13.8 1.5 %collective-permute-start.19 = (f32[2,128,128]{2,1,0:T(8,128)S(1)}, f32[2,128,128]{2,1,0:T(8,128)S(1)}, u32[]{:S(2)}, u32[]{:S(2)}) collective-permute-start(f32[2,128,128]{2,1,0:T(8,128)S(1)} %get-tuple-element.51), channel_id=1, source_target_pairs={{0,4},{4,0},{8,12},{12,8},{16,20},{20,16},{24,28},{28,24},{1,5},{5... | collective-permute-start | bytes 393224 | tf_op jit(solution)/shard_map/ppermute | solution.py:217
  15.3 0.5 collective-permute-start.17
  15.8 3.0 %collective-permute-done.5.refs_3_ = bf16[2,128,128]{2,1,0:T(8,128)(2,1)S(1)} collective-permute-done((bf16[2,128,128]{2,1,0:T(8,128)(2,1)S(1)}, bf16[2,128,128]{2,1,0:T(8,128)(2,1)S(1)}, u32[]{:S(2)}, u32[]{:S(2)}) %collective-permute-start.5) | collective-permute-done | bytes 65568 | tf_op jit(solution)/shard_map/ppermute | solution.py:217
  18.8 1.0 %collective-permute-done.6.refs_4_ = bf16[2,128,128]{2,1,0:T(8,128)(2,1)S(1)} collective-permute-done((bf16[2,128,128]{2,1,0:T(8,128)(2,1)S(1)}, bf16[2,128,128]{2,1,0:T(8,128)(2,1)S(1)}, u32[]{:S(2)}, u32[]{:S(2)}) %collective-permute-start.6) | collective-permute-done | bytes 65568 | tf_op jit(solution)/shard_map/ppermute | solution.py:217
  19.8 0.4 forward.2
  20.2 0.1 collective-permute-start.7
  20.3 1.6 %collective-permute-start.8 = (f32[128,128]{1,0:T(8,128)S(1)}, f32[128,128]{1,0:T(8,128)S(1)}, u32[]{:S(2)}, u32[]{:S(2)}) collective-permute-start(f32[128,128]{1,0:T(8,128)S(1)} %get-tuple-element.39), channel_id=1, source_target_pairs={{0,2},{1,3},{2,0},{3,1},{4,6},{5,7},{6,4},{7,5},{8,10},{9,11},{10,... | collective-permute-start | bytes 196616 | tf_op jit(solution)/shard_map/ppermute | solution.py:217
  21.9 0.3 collective-permute-start.9
  22.2 2.6 %collective-permute-done.8.refs_2_ = f32[128,128]{1,0:T(8,128)S(1)} collective-permute-done((f32[128,128]{1,0:T(8,128)S(1)}, f32[128,128]{1,0:T(8,128)S(1)}, u32[]{:S(2)}, u32[]{:S(2)}) %collective-permute-start.8) | collective-permute-done | bytes 65568 | tf_op jit(solution)/shard_map/ppermute | solution.py:217
  24.8 1.1 %collective-permute-done.9.refs_3_ = f32[128,128]{1,0:T(8,128)S(1)} collective-permute-done((f32[128,128]{1,0:T(8,128)S(1)}, f32[128,128]{1,0:T(8,128)S(1)}, u32[]{:S(2)}, u32[]{:S(2)}) %collective-permute-start.9) | collective-permute-done | bytes 65568 | tf_op jit(solution)/shard_map/ppermute | solution.py:217
  25.9 1.0 %collective-permute-start.10 = (bf16[128,128]{1,0:T(8,128)(2,1)S(1)}, bf16[128,128]{1,0:T(8,128)(2,1)S(1)}, u32[]{:S(2)}, u32[]{:S(2)}) collective-permute-start(bf16[128,128]{1,0:T(8,128)(2,1)S(1)} %forward_end.2.refs_0_.refs_1_), channel_id=1, source_target_pairs={{0,8},{4,12},{8,0},{12,4},{16,24},{20,28},{24,16},{28,20},{1,9},{5... | collective-permute-start | bytes 98312 | tf_op jit(solution)/shard_map/ppermute | solution.py:217
  27.0 1.5 %collective-permute-start.11 = (bf16[128,128]{1,0:T(8,128)(2,1)S(1)}, bf16[128,128]{1,0:T(8,128)(2,1)S(1)}, u32[]{:S(2)}, u32[]{:S(2)}) collective-permute-start(bf16[128,128]{1,0:T(8,128)(2,1)S(1)} %forward_end.2.refs_0_.refs_1_), channel_id=1, source_target_pairs={{0,16},{4,20},{8,24},{12,28},{16,0},{20,4},{24,8},{28,12},{1,17},{... | collective-permute-start | bytes 98312 | tf_op jit(solution)/shard_map/ppermute | solution.py:217
  28.5 1.9 %collective-permute-start.12 = (bf16[128,128]{1,0:T(8,128)(2,1)S(1)}, bf16[128,128]{1,0:T(8,128)(2,1)S(1)}, u32[]{:S(2)}, u32[]{:S(2)}) collective-permute-start(bf16[128,128]{1,0:T(8,128)(2,1)S(1)} %forward_end.2.refs_0_.refs_1_), channel_id=1, source_target_pairs={{0,24},{4,28},{8,16},{12,20},{16,8},{20,12},{24,0},{28,4},{1,25},{... | collective-permute-start | bytes 98312 | tf_op jit(solution)/shard_map/ppermute | solution.py:217
  30.4 0.9 %collective-permute-start.20 = (f32[128,128]{1,0:T(8,128)S(1)}, f32[128,128]{1,0:T(8,128)S(1)}, u32[]{:S(2)}, u32[]{:S(2)}) collective-permute-start(f32[128,128]{1,0:T(8,128)S(1)} %get-tuple-element.52), channel_id=1, source_target_pairs={{0,16},{4,20},{8,24},{12,28},{16,0},{20,4},{24,8},{28,12},{1,17},{... | collective-permute-start | bytes 196616 | tf_op jit(solution)/shard_map/ppermute | solution.py:217
  31.3 1.6 %collective-permute-start.21 = (f32[128,128]{1,0:T(8,128)S(1)}, f32[128,128]{1,0:T(8,128)S(1)}, u32[]{:S(2)}, u32[]{:S(2)}) collective-permute-start(f32[128,128]{1,0:T(8,128)S(1)} %get-tuple-element.53), channel_id=1, source_target_pairs={{0,24},{4,28},{8,16},{12,20},{16,8},{20,12},{24,0},{28,4},{1,25},{... | collective-permute-start | bytes 196616 | tf_op jit(solution)/shard_map/ppermute | solution.py:217
  32.9 1.1 %collective-permute-start.18 = (f32[128,128]{1,0:T(8,128)S(1)}, f32[128,128]{1,0:T(8,128)S(1)}, u32[]{:S(2)}, u32[]{:S(2)}) collective-permute-start(f32[128,128]{1,0:T(8,128)S(1)} %get-tuple-element.49), channel_id=1, source_target_pairs={{0,8},{4,12},{8,0},{12,4},{16,24},{20,28},{24,16},{28,20},{1,9},{5... | collective-permute-start | bytes 196616 | tf_op jit(solution)/shard_map/ppermute | solution.py:217
  34.1 0.1 collective-permute-done.12.refs_3_.refs_4_
  34.2 1.3 %collective-permute-start.13 = (bf16[4,128,128]{2,1,0:T(8,128)(2,1)S(1)}, bf16[4,128,128]{2,1,0:T(8,128)(2,1)S(1)}, u32[]{:S(2)}, u32[]{:S(2)}) collective-permute-start(bf16[4,128,128]{2,1,0:T(8,128)(2,1)S(1)} %pack.1), channel_id=1, source_target_pairs={{0,4},{4,0},{8,12},{12,8},{16,20},{20,16},{24,28},{28,24},{1,5},{5... | collective-permute-start | bytes 393224 | tf_op jit(solution)/shard_map/ppermute | solution.py:217
  35.5 2.6 %collective-permute-done.20.refs_2_ = f32[128,128]{1,0:T(8,128)S(1)} collective-permute-done((f32[128,128]{1,0:T(8,128)S(1)}, f32[128,128]{1,0:T(8,128)S(1)}, u32[]{:S(2)}, u32[]{:S(2)}) %collective-permute-start.20) | collective-permute-done | bytes 65568 | tf_op jit(solution)/shard_map/ppermute | solution.py:217
  38.1 0.4 collective-permute-done.18.refs_1_
  38.5 0.1 collective-permute-start.22
  38.6 1.5 %collective-permute-start.23 = (bf16[128,128]{1,0:T(8,128)(2,1)S(1)}, bf16[128,128]{1,0:T(8,128)(2,1)S(1)}, u32[]{:S(2)}, u32[]{:S(2)}) collective-permute-start(bf16[128,128]{1,0:T(8,128)(2,1)S(1)} %get-tuple-element.55.refs_1_), channel_id=1, source_target_pairs={{0,2},{1,3},{2,0},{3,1},{4,6},{5,7},{6,4},{7,5},{8,10},{9,11},{10,... | collective-permute-start | bytes 98312 | tf_op jit(solution)/shard_map/ppermute | solution.py:217
  40.1 0.3 collective-permute-start.24
  40.4 2.1 %collective-permute-done.23.refs_3_ = bf16[128,128]{1,0:T(8,128)(2,1)S(1)} collective-permute-done((bf16[128,128]{1,0:T(8,128)(2,1)S(1)}, bf16[128,128]{1,0:T(8,128)(2,1)S(1)}, u32[]{:S(2)}, u32[]{:S(2)}) %collective-permute-start.23) | collective-permute-done | bytes 32800 | tf_op jit(solution)/shard_map/ppermute | solution.py:217
  42.5 0.9 %collective-permute-done.24.refs_4_ = bf16[128,128]{1,0:T(8,128)(2,1)S(1)} collective-permute-done((bf16[128,128]{1,0:T(8,128)(2,1)S(1)}, bf16[128,128]{1,0:T(8,128)(2,1)S(1)}, u32[]{:S(2)}, u32[]{:S(2)}) %collective-permute-start.24) | collective-permute-done | bytes 32800 | tf_op jit(solution)/shard_map/ppermute | solution.py:217
  43.4 0.3 adjoint.3
  43.7 1.0 %collective-permute-start.27 = (bf16[2,128,128]{2,1,0:T(8,128)(2,1)S(1)}, bf16[2,128,128]{2,1,0:T(8,128)(2,1)S(1)}, u32[]{:S(2)}, u32[]{:S(2)}) collective-permute-start(bf16[2,128,128]{2,1,0:T(8,128)(2,1)S(1)} %get-tuple-element.61), channel_id=1, source_target_pairs={{0,4},{4,0},{8,12},{12,8},{16,20},{20,16},{24,28},{28,24},{1,5},{5... | collective-permute-start | bytes 196616 | tf_op jit(solution)/shard_map/ppermute | solution.py:217
  44.7 1.1 %collective-permute-start.25 = (bf16[2,128,128]{2,1,0:T(8,128)(2,1)S(1)}, bf16[2,128,128]{2,1,0:T(8,128)(2,1)S(1)}, u32[]{:S(2)}, u32[]{:S(2)}) collective-permute-start(bf16[2,128,128]{2,1,0:T(8,128)(2,1)S(1)} %get-tuple-element.57), channel_id=1, source_target_pairs={{0,4},{4,0},{8,12},{12,8},{16,20},{20,16},{24,28},{28,24},{1,5},{5... | collective-permute-start | bytes 196616 | tf_op jit(solution)/shard_map/ppermute | solution.py:217
  45.8 0.4 forward.3
  46.3 0.1 collective-permute-start.14
  46.4 2.3 %collective-permute-done.27.got_ref = bf16[2,128,128]{2,1,0:T(8,128)(2,1)S(1)} collective-permute-done((bf16[2,128,128]{2,1,0:T(8,128)(2,1)S(1)}, bf16[2,128,128]{2,1,0:T(8,128)(2,1)S(1)}, u32[]{:S(2)}, u32[]{:S(2)}) %collective-permute-start.27) | collective-permute-done | bytes 65568 | tf_op jit(solution)/shard_map/ppermute | solution.py:217
  48.7 1.8 %collective-permute-start.28 = (bf16[128,128]{1,0:T(8,128)(2,1)S(1)}, bf16[128,128]{1,0:T(8,128)(2,1)S(1)}, u32[]{:S(2)}, u32[]{:S(2)}) collective-permute-start(bf16[128,128]{1,0:T(8,128)(2,1)S(1)} %get-tuple-element.62), channel_id=1, source_target_pairs={{0,16},{4,20},{8,24},{12,28},{16,0},{20,4},{24,8},{28,12},{1,17},{... | collective-permute-start | bytes 98312 | tf_op jit(solution)/shard_map/ppermute | solution.py:217
  50.5 1.9 %collective-permute-start.29 = (bf16[128,128]{1,0:T(8,128)(2,1)S(1)}, bf16[128,128]{1,0:T(8,128)(2,1)S(1)}, u32[]{:S(2)}, u32[]{:S(2)}) collective-permute-start(bf16[128,128]{1,0:T(8,128)(2,1)S(1)} %get-tuple-element.63), channel_id=1, source_target_pairs={{0,24},{4,28},{8,16},{12,20},{16,8},{20,12},{24,0},{28,4},{1,25},{... | collective-permute-start | bytes 98312 | tf_op jit(solution)/shard_map/ppermute | solution.py:217
  52.4 0.9 %collective-permute-start.15 = (bf16[128,128]{1,0:T(8,128)(2,1)S(1)}, bf16[128,128]{1,0:T(8,128)(2,1)S(1)}, u32[]{:S(2)}, u32[]{:S(2)}) collective-permute-start(bf16[128,128]{1,0:T(8,128)(2,1)S(1)} %get-tuple-element.43), channel_id=1, source_target_pairs={{0,2},{1,3},{2,0},{3,1},{4,6},{5,7},{6,4},{7,5},{8,10},{9,11},{10,... | collective-permute-start | bytes 98312 | tf_op jit(solution)/shard_map/ppermute | solution.py:217
  53.4 2.9 %collective-permute-done.15.refs_2_ = bf16[128,128]{1,0:T(8,128)(2,1)S(1)} collective-permute-done((bf16[128,128]{1,0:T(8,128)(2,1)S(1)}, bf16[128,128]{1,0:T(8,128)(2,1)S(1)}, u32[]{:S(2)}, u32[]{:S(2)}) %collective-permute-start.15) | collective-permute-done | bytes 32800 | tf_op jit(solution)/shard_map/ppermute | solution.py:217
  56.3 0.6 %collective-permute-done.16.refs_3_ = bf16[128,128]{1,0:T(8,128)(2,1)S(1)} collective-permute-done((bf16[128,128]{1,0:T(8,128)(2,1)S(1)}, bf16[128,128]{1,0:T(8,128)(2,1)S(1)}, u32[]{:S(2)}, u32[]{:S(2)}) %collective-permute-start.16) | collective-permute-done | bytes 32800 | tf_op jit(solution)/shard_map/ppermute | solution.py:217
  56.9 0.7 %forward_end.3 = f32[128,128]{1,0:T(8,128)} custom-call(f32[128,128]{1,0:T(8,128)S(1)} %copy-done, f32[128,128]{1,0:T(8,128)S(1)} %get-tuple-element.33.rate_ref.column_ref, bf16[128,128]{1,0:T(8,128)(2,1)S(1)} %get-tuple-element.41.refs_0_, bf16[128,128]{1,0:T(8,128)(2,1)S(1)} %collective-permute-done.14.refs_1_, ...), custom_call_target="tpu_custom_call" | custom-call | bytes 327680 | tf_op jit(solution)/shard_map/forward_end/pallas_call | solution.py:31
  57.6 0.2 copy-done.1
  57.8 0.7 %adjoint_end.1 = f32[128,128]{1,0:T(8,128)} custom-call(f32[128,128]{1,0:T(8,128)S(1)} %copy-done.1, f32[128,128]{1,0:T(8,128)S(1)} %get-tuple-element.54.d_ref, f32[1,128]{1,0:T(1,128)S(1)} %get-tuple-element.45.rate_ref.row_ref, f32[128,128]{1,0:T(8,128)S(1)} %get-tuple-element.33.rate_ref.column_ref, f32[128,128]{1,0:T(8,128)S(1)} %get-tuple-element.58.refs_0_, ...), custom_call_target="tpu_custom_call" | custom-call | bytes 426496 | tf_op jit(solution)/shard_map/adjoint_end/pallas_call | solution.py:31
  (31 shorter events, 0.3 us)
Async XLA Ops:
  1.7 7.3 %collective-permute-start = (bf16[128,128]{1,0:T(8,128)(2,1)S(1)}, bf16[128,128]{1,0:T(8,128)(2,1)S(1)}, u32[]{:S(2)}, u32[]{:S(2)}) collective-permute-start(bf16[128,128]{1,0:T(8,128)(2,1)S(1)} %get-tuple-element.34.q_ref.refs_1_), channel_id=1, source_target_pairs={{0,1},{1,0},{2,3},{3,2},{4,5},{5,4},{6,7},{7,6},{8,9},{9,8},{10,11... | collective-permute-start | bytes 98312 | tf_op jit(solution)/shard_map/ppermute | solution.py:217
  2.2 6.8 %collective-permute-start.1 = (bf16[128,128]{1,0:T(8,128)(2,1)S(1)}, bf16[128,128]{1,0:T(8,128)(2,1)S(1)}, u32[]{:S(2)}, u32[]{:S(2)}) collective-permute-start(bf16[128,128]{1,0:T(8,128)(2,1)S(1)} %get-tuple-element.34.q_ref.refs_1_), channel_id=1, source_target_pairs={{0,2},{1,3},{2,0},{3,1},{4,6},{5,7},{6,4},{7,5},{8,10},{9,11},{10,... | collective-permute-start | bytes 98312 | tf_op jit(solution)/shard_map/ppermute | solution.py:217
  4.8 4.2 %collective-permute-start.2 = (bf16[128,128]{1,0:T(8,128)(2,1)S(1)}, bf16[128,128]{1,0:T(8,128)(2,1)S(1)}, u32[]{:S(2)}, u32[]{:S(2)}) collective-permute-start(bf16[128,128]{1,0:T(8,128)(2,1)S(1)} %get-tuple-element.34.q_ref.refs_1_), channel_id=1, source_target_pairs={{0,3},{1,2},{2,1},{3,0},{4,7},{5,6},{6,5},{7,4},{8,11},{9,10},{10,... | collective-permute-start | bytes 98312 | tf_op jit(solution)/shard_map/ppermute | solution.py:217
  4.8 4.2 %collective-permute-start.3 = (bf16[128,128]{1,0:T(8,128)(2,1)S(1)}, bf16[128,128]{1,0:T(8,128)(2,1)S(1)}, u32[]{:S(2)}, u32[]{:S(2)}) collective-permute-start(bf16[128,128]{1,0:T(8,128)(2,1)S(1)} %get-tuple-element.35.refs_5_), channel_id=1, source_target_pairs={{0,4},{4,0},{8,12},{12,8},{16,20},{20,16},{24,28},{28,24},{1,5},{5... | collective-permute-start | bytes 98312 | tf_op jit(solution)/shard_map/ppermute | solution.py:217
  9.3 6.5 %collective-permute-start.4 = (bf16[2,128,128]{2,1,0:T(8,128)(2,1)S(1)}, bf16[2,128,128]{2,1,0:T(8,128)(2,1)S(1)}, u32[]{:S(2)}, u32[]{:S(2)}) collective-permute-start(bf16[2,128,128]{2,1,0:T(8,128)(2,1)S(1)} %get-tuple-element.36.refs_1_), channel_id=1, source_target_pairs={{0,8},{4,12},{8,0},{12,4},{16,24},{20,28},{24,16},{28,20},{1,9},{5... | collective-permute-start | bytes 196616 | tf_op jit(solution)/shard_map/ppermute | solution.py:217
  11.3 7.5 %collective-permute-start.5 = (bf16[2,128,128]{2,1,0:T(8,128)(2,1)S(1)}, bf16[2,128,128]{2,1,0:T(8,128)(2,1)S(1)}, u32[]{:S(2)}, u32[]{:S(2)}) collective-permute-start(bf16[2,128,128]{2,1,0:T(8,128)(2,1)S(1)} %get-tuple-element.36.refs_1_), channel_id=1, source_target_pairs={{0,16},{4,20},{8,24},{12,28},{16,0},{20,4},{24,8},{28,12},{1,17},{... | collective-permute-start | bytes 196616 | tf_op jit(solution)/shard_map/ppermute | solution.py:217
  13.6 6.2 %collective-permute-start.6 = (bf16[2,128,128]{2,1,0:T(8,128)(2,1)S(1)}, bf16[2,128,128]{2,1,0:T(8,128)(2,1)S(1)}, u32[]{:S(2)}, u32[]{:S(2)}) collective-permute-start(bf16[2,128,128]{2,1,0:T(8,128)(2,1)S(1)} %get-tuple-element.36.refs_1_), channel_id=1, source_target_pairs={{0,24},{4,28},{8,16},{12,20},{16,8},{20,12},{24,0},{28,4},{1,25},{... | collective-permute-start | bytes 196616 | tf_op jit(solution)/shard_map/ppermute | solution.py:217
  13.8 16.6 %collective-permute-start.19 = (f32[2,128,128]{2,1,0:T(8,128)S(1)}, f32[2,128,128]{2,1,0:T(8,128)S(1)}, u32[]{:S(2)}, u32[]{:S(2)}) collective-permute-start(f32[2,128,128]{2,1,0:T(8,128)S(1)} %get-tuple-element.51), channel_id=1, source_target_pairs={{0,4},{4,0},{8,12},{12,8},{16,20},{20,16},{24,28},{28,24},{1,5},{5... | collective-permute-start | bytes 393224 | tf_op jit(solution)/shard_map/ppermute | solution.py:217
  15.3 10.6 %copy-start = (f32[128,128]{1,0:T(8,128)S(1)}, f32[128,128]{1,0:T(8,128)}, u32[]{:S(2)}) copy-start(f32[128,128]{1,0:T(8,128)} %h_ref.3) | copy-start | bytes 196612
  15.3 16.0 %collective-permute-start.17 = (f32[2,128,128]{2,1,0:T(8,128)S(1)}, f32[2,128,128]{2,1,0:T(8,128)S(1)}, u32[]{:S(2)}, u32[]{:S(2)}) collective-permute-start(f32[2,128,128]{2,1,0:T(8,128)S(1)} %get-tuple-element.47), channel_id=1, source_target_pairs={{0,4},{4,0},{8,12},{12,8},{16,20},{20,16},{24,28},{28,24},{1,5},{5... | collective-permute-start | bytes 393224 | tf_op jit(solution)/shard_map/ppermute | solution.py:217
  20.2 1.9 %collective-permute-start.7 = (f32[128,128]{1,0:T(8,128)S(1)}, f32[128,128]{1,0:T(8,128)S(1)}, u32[]{:S(2)}, u32[]{:S(2)}) collective-permute-start(f32[128,128]{1,0:T(8,128)S(1)} %get-tuple-element.38), channel_id=1, source_target_pairs={{0,1},{1,0},{2,3},{3,2},{4,5},{5,4},{6,7},{7,6},{8,9},{9,8},{10,11... | collective-permute-start | bytes 196616 | tf_op jit(solution)/shard_map/ppermute | solution.py:217
  20.3 4.5 %collective-permute-start.8 = (f32[128,128]{1,0:T(8,128)S(1)}, f32[128,128]{1,0:T(8,128)S(1)}, u32[]{:S(2)}, u32[]{:S(2)}) collective-permute-start(f32[128,128]{1,0:T(8,128)S(1)} %get-tuple-element.39), channel_id=1, source_target_pairs={{0,2},{1,3},{2,0},{3,1},{4,6},{5,7},{6,4},{7,5},{8,10},{9,11},{10,... | collective-permute-start | bytes 196616 | tf_op jit(solution)/shard_map/ppermute | solution.py:217
  21.9 4.0 %collective-permute-start.9 = (f32[128,128]{1,0:T(8,128)S(1)}, f32[128,128]{1,0:T(8,128)S(1)}, u32[]{:S(2)}, u32[]{:S(2)}) collective-permute-start(f32[128,128]{1,0:T(8,128)S(1)} %get-tuple-element.40), channel_id=1, source_target_pairs={{0,3},{1,2},{2,1},{3,0},{4,7},{5,6},{6,5},{7,4},{8,11},{9,10},{10,... | collective-permute-start | bytes 196616 | tf_op jit(solution)/shard_map/ppermute | solution.py:217
  25.9 7.0 %collective-permute-start.10 = (bf16[128,128]{1,0:T(8,128)(2,1)S(1)}, bf16[128,128]{1,0:T(8,128)(2,1)S(1)}, u32[]{:S(2)}, u32[]{:S(2)}) collective-permute-start(bf16[128,128]{1,0:T(8,128)(2,1)S(1)} %forward_end.2.refs_0_.refs_1_), channel_id=1, source_target_pairs={{0,8},{4,12},{8,0},{12,4},{16,24},{20,28},{24,16},{28,20},{1,9},{5... | collective-permute-start | bytes 98312 | tf_op jit(solution)/shard_map/ppermute | solution.py:217
  27.0 7.1 %collective-permute-start.11 = (bf16[128,128]{1,0:T(8,128)(2,1)S(1)}, bf16[128,128]{1,0:T(8,128)(2,1)S(1)}, u32[]{:S(2)}, u32[]{:S(2)}) collective-permute-start(bf16[128,128]{1,0:T(8,128)(2,1)S(1)} %forward_end.2.refs_0_.refs_1_), channel_id=1, source_target_pairs={{0,16},{4,20},{8,24},{12,28},{16,0},{20,4},{24,8},{28,12},{1,17},{... | collective-permute-start | bytes 98312 | tf_op jit(solution)/shard_map/ppermute | solution.py:217
  28.5 5.7 %collective-permute-start.12 = (bf16[128,128]{1,0:T(8,128)(2,1)S(1)}, bf16[128,128]{1,0:T(8,128)(2,1)S(1)}, u32[]{:S(2)}, u32[]{:S(2)}) collective-permute-start(bf16[128,128]{1,0:T(8,128)(2,1)S(1)} %forward_end.2.refs_0_.refs_1_), channel_id=1, source_target_pairs={{0,24},{4,28},{8,16},{12,20},{16,8},{20,12},{24,0},{28,4},{1,25},{... | collective-permute-start | bytes 98312 | tf_op jit(solution)/shard_map/ppermute | solution.py:217
  30.4 7.6 %collective-permute-start.20 = (f32[128,128]{1,0:T(8,128)S(1)}, f32[128,128]{1,0:T(8,128)S(1)}, u32[]{:S(2)}, u32[]{:S(2)}) collective-permute-start(f32[128,128]{1,0:T(8,128)S(1)} %get-tuple-element.52), channel_id=1, source_target_pairs={{0,16},{4,20},{8,24},{12,28},{16,0},{20,4},{24,8},{28,12},{1,17},{... | collective-permute-start | bytes 196616 | tf_op jit(solution)/shard_map/ppermute | solution.py:217
  31.3 6.7 %collective-permute-start.21 = (f32[128,128]{1,0:T(8,128)S(1)}, f32[128,128]{1,0:T(8,128)S(1)}, u32[]{:S(2)}, u32[]{:S(2)}) collective-permute-start(f32[128,128]{1,0:T(8,128)S(1)} %get-tuple-element.53), channel_id=1, source_target_pairs={{0,24},{4,28},{8,16},{12,20},{16,8},{20,12},{24,0},{28,4},{1,25},{... | collective-permute-start | bytes 196616 | tf_op jit(solution)/shard_map/ppermute | solution.py:217
  32.9 5.5 %collective-permute-start.18 = (f32[128,128]{1,0:T(8,128)S(1)}, f32[128,128]{1,0:T(8,128)S(1)}, u32[]{:S(2)}, u32[]{:S(2)}) collective-permute-start(f32[128,128]{1,0:T(8,128)S(1)} %get-tuple-element.49), channel_id=1, source_target_pairs={{0,8},{4,12},{8,0},{12,4},{16,24},{20,28},{24,16},{28,20},{1,9},{5... | collective-permute-start | bytes 196616 | tf_op jit(solution)/shard_map/ppermute | solution.py:217
  34.2 11.6 %collective-permute-start.13 = (bf16[4,128,128]{2,1,0:T(8,128)(2,1)S(1)}, bf16[4,128,128]{2,1,0:T(8,128)(2,1)S(1)}, u32[]{:S(2)}, u32[]{:S(2)}) collective-permute-start(bf16[4,128,128]{2,1,0:T(8,128)(2,1)S(1)} %pack.1), channel_id=1, source_target_pairs={{0,4},{4,0},{8,12},{12,8},{16,20},{20,16},{24,28},{28,24},{1,5},{5... | collective-permute-start | bytes 393224 | tf_op jit(solution)/shard_map/ppermute | solution.py:217
  38.5 1.9 %collective-permute-start.22 = (bf16[128,128]{1,0:T(8,128)(2,1)S(1)}, bf16[128,128]{1,0:T(8,128)(2,1)S(1)}, u32[]{:S(2)}, u32[]{:S(2)}) collective-permute-start(bf16[128,128]{1,0:T(8,128)(2,1)S(1)} %get-tuple-element.55.refs_1_), channel_id=1, source_target_pairs={{0,1},{1,0},{2,3},{3,2},{4,5},{5,4},{6,7},{7,6},{8,9},{9,8},{10,11... | collective-permute-start | bytes 98312 | tf_op jit(solution)/shard_map/ppermute | solution.py:217
  38.6 4.0 %collective-permute-start.23 = (bf16[128,128]{1,0:T(8,128)(2,1)S(1)}, bf16[128,128]{1,0:T(8,128)(2,1)S(1)}, u32[]{:S(2)}, u32[]{:S(2)}) collective-permute-start(bf16[128,128]{1,0:T(8,128)(2,1)S(1)} %get-tuple-element.55.refs_1_), channel_id=1, source_target_pairs={{0,2},{1,3},{2,0},{3,1},{4,6},{5,7},{6,4},{7,5},{8,10},{9,11},{10,... | collective-permute-start | bytes 98312 | tf_op jit(solution)/shard_map/ppermute | solution.py:217
  40.1 3.3 %collective-permute-start.24 = (bf16[128,128]{1,0:T(8,128)(2,1)S(1)}, bf16[128,128]{1,0:T(8,128)(2,1)S(1)}, u32[]{:S(2)}, u32[]{:S(2)}) collective-permute-start(bf16[128,128]{1,0:T(8,128)(2,1)S(1)} %get-tuple-element.55.refs_1_), channel_id=1, source_target_pairs={{0,3},{1,2},{2,1},{3,0},{4,7},{5,6},{6,5},{7,4},{8,11},{9,10},{10,... | collective-permute-start | bytes 98312 | tf_op jit(solution)/shard_map/ppermute | solution.py:217
  43.7 4.9 %collective-permute-start.27 = (bf16[2,128,128]{2,1,0:T(8,128)(2,1)S(1)}, bf16[2,128,128]{2,1,0:T(8,128)(2,1)S(1)}, u32[]{:S(2)}, u32[]{:S(2)}) collective-permute-start(bf16[2,128,128]{2,1,0:T(8,128)(2,1)S(1)} %get-tuple-element.61), channel_id=1, source_target_pairs={{0,4},{4,0},{8,12},{12,8},{16,20},{20,16},{24,28},{28,24},{1,5},{5... | collective-permute-start | bytes 196616 | tf_op jit(solution)/shard_map/ppermute | solution.py:217
  44.7 8.6 %collective-permute-start.25 = (bf16[2,128,128]{2,1,0:T(8,128)(2,1)S(1)}, bf16[2,128,128]{2,1,0:T(8,128)(2,1)S(1)}, u32[]{:S(2)}, u32[]{:S(2)}) collective-permute-start(bf16[2,128,128]{2,1,0:T(8,128)(2,1)S(1)} %get-tuple-element.57), channel_id=1, source_target_pairs={{0,4},{4,0},{8,12},{12,8},{16,20},{20,16},{24,28},{28,24},{1,5},{5... | collective-permute-start | bytes 196616 | tf_op jit(solution)/shard_map/ppermute | solution.py:217
  46.3 7.1 %collective-permute-start.14 = (bf16[128,128]{1,0:T(8,128)(2,1)S(1)}, bf16[128,128]{1,0:T(8,128)(2,1)S(1)}, u32[]{:S(2)}, u32[]{:S(2)}) collective-permute-start(bf16[128,128]{1,0:T(8,128)(2,1)S(1)} %get-tuple-element.42), channel_id=1, source_target_pairs={{0,1},{1,0},{2,3},{3,2},{4,5},{5,4},{6,7},{7,6},{8,9},{9,8},{10,11... | collective-permute-start | bytes 98312 | tf_op jit(solution)/shard_map/ppermute | solution.py:217
  48.7 8.9 %collective-permute-start.28 = (bf16[128,128]{1,0:T(8,128)(2,1)S(1)}, bf16[128,128]{1,0:T(8,128)(2,1)S(1)}, u32[]{:S(2)}, u32[]{:S(2)}) collective-permute-start(bf16[128,128]{1,0:T(8,128)(2,1)S(1)} %get-tuple-element.62), channel_id=1, source_target_pairs={{0,16},{4,20},{8,24},{12,28},{16,0},{20,4},{24,8},{28,12},{1,17},{... | collective-permute-start | bytes 98312 | tf_op jit(solution)/shard_map/ppermute | solution.py:217
  50.5 7.1 %collective-permute-start.29 = (bf16[128,128]{1,0:T(8,128)(2,1)S(1)}, bf16[128,128]{1,0:T(8,128)(2,1)S(1)}, u32[]{:S(2)}, u32[]{:S(2)}) collective-permute-start(bf16[128,128]{1,0:T(8,128)(2,1)S(1)} %get-tuple-element.63), channel_id=1, source_target_pairs={{0,24},{4,28},{8,16},{12,20},{16,8},{20,12},{24,0},{28,4},{1,25},{... | collective-permute-start | bytes 98312 | tf_op jit(solution)/shard_map/ppermute | solution.py:217
  52.4 3.9 %collective-permute-start.15 = (bf16[128,128]{1,0:T(8,128)(2,1)S(1)}, bf16[128,128]{1,0:T(8,128)(2,1)S(1)}, u32[]{:S(2)}, u32[]{:S(2)}) collective-permute-start(bf16[128,128]{1,0:T(8,128)(2,1)S(1)} %get-tuple-element.43), channel_id=1, source_target_pairs={{0,2},{1,3},{2,0},{3,1},{4,6},{5,7},{6,4},{7,5},{8,10},{9,11},{10,... | collective-permute-start | bytes 98312 | tf_op jit(solution)/shard_map/ppermute | solution.py:217
  53.3 3.6 %collective-permute-start.16 = (bf16[128,128]{1,0:T(8,128)(2,1)S(1)}, bf16[128,128]{1,0:T(8,128)(2,1)S(1)}, u32[]{:S(2)}, u32[]{:S(2)}) collective-permute-start(bf16[128,128]{1,0:T(8,128)(2,1)S(1)} %get-tuple-element.44), channel_id=1, source_target_pairs={{0,3},{1,2},{2,1},{3,0},{4,7},{5,6},{6,5},{7,4},{8,11},{9,10},{10,... | collective-permute-start | bytes 98312 | tf_op jit(solution)/shard_map/ppermute | solution.py:217
  53.4 4.2 %collective-permute-start.26 = (bf16[128,128]{1,0:T(8,128)(2,1)S(1)}, bf16[128,128]{1,0:T(8,128)(2,1)S(1)}, u32[]{:S(2)}, u32[]{:S(2)}) collective-permute-start(bf16[128,128]{1,0:T(8,128)(2,1)S(1)} %get-tuple-element.59), channel_id=1, source_target_pairs={{0,8},{4,12},{8,0},{12,4},{16,24},{20,28},{24,16},{28,20},{1,9},{5... | collective-permute-start | bytes 98312 | tf_op jit(solution)/shard_map/ppermute | solution.py:217
  56.9 0.8 %copy-start.1 = (f32[128,128]{1,0:T(8,128)S(1)}, f32[128,128]{1,0:T(8,128)}, u32[]{:S(2)}) copy-start(f32[128,128]{1,0:T(8,128)} %cot_ref.1) | copy-start | bytes 196612

commit v5 on v4

--- a/solution.py
+++ b/solution.py
@@ -26,18 +26,23 @@
     return [pltpu.with_memory_space_constraint(a, pltpu.HBM) for a in arrays]
 
 
-def call(body, outs, in_specs, args, flops, name, scratch=()):
+def call(body, outs, in_specs, args, flops, name, scratch=(), after=()):
     nbytes = sum(a.size * a.dtype.itemsize for a in (*args, *outs))
+    count = len(args)
+
+    def ordered(*refs):
+        body(*refs[:count], *refs[count + len(after) :])
+
     return pl.pallas_call(
-        body,
+        ordered,
         out_shape=outs,
-        in_specs=in_specs,
+        in_specs=[*in_specs, *[pl.BlockSpec(memory_space=pl.ANY)] * len(after)],
         out_specs=[vmem()] * len(outs),
         scratch_shapes=list(scratch),
         compiler_params=pltpu.CompilerParams(vmem_limit_bytes=VMEM_LIMIT),
         cost_estimate=pl.CostEstimate(flops=flops, bytes_accessed=nbytes, transcendentals=0),
         name=name,
-    )(*args)
+    )(*args, *after)
 
 
 def fetch(pairs, sems):
@@ -283,7 +288,7 @@
         close = [close[0]] + [send(close[s], "rows", n_rows, 2 * s) for s in range(1, near)]
         return close + far, both
 
-    def forward_hop(part, kind, paired):
+    def forward_hop(part, kind, paired, after):
         panels = [part] + [send(part, "rows", n_rows, 2 * s) for s in range(1, half)]
         if not paired:
             (packed,) = call(
@@ -297,10 +302,11 @@
             [dense, *panels],
             hop_flops,
             "forward",
+            after=after,
         )
         return [sums[0]] + [send(sums[s], "cols", n_cols, s) for s in range(1, n_cols)]
 
-    def forward_end(parts, kind):
+    def forward_end(parts, kind, after=()):
         return call(
             forward_end_body,
             [shape(kind)],
@@ -308,10 +314,11 @@
             (h_start, column, *parts),
             0,
             "forward_end",
+            after=after,
         )[0]
 
     back, (both,) = adjoint_hop(q0, F32, [p0, send(p0, "rows", n_rows, 1)])
-    first = forward_hop(both, F32, True)
+    first = forward_hop(both, F32, True, back[:1])
     d1, q1 = call(
         adjoint_mid_body,
         [shape(F32), shape(BF16)],
@@ -320,9 +327,9 @@
         0,
         "adjoint_mid",
     )
-    p1 = forward_end(first, BF16)
+    p1 = forward_end(first, BF16, [d1])
     back_two, _ = adjoint_hop(q1, BF16, [])
-    second = forward_hop(p1, BF16, False)
+    second = forward_hop(p1, BF16, False, back_two[:1])
     propagated = forward_end(second, F32)
     (input_grad,) = call(
         adjoint_end_body,

time: 58.8 us -> 56.1 us (0.954)
  waiting for transfers between devices: 19.7 us -> 13.8 us
  starting transfers between devices: 31.4 us -> 34.5 us
    ppermute x30, waiting for transfers between devices: 19.7 us -> 13.8 us  [send(): return lax.ppermute(value, axis, [(i, i ^ step) for i in range(count)])]
    ppermute x30, starting transfers between devices: 31.4 us -> 34.5 us  [send(): return lax.ppermute(value, axis, [(i, i ^ step) for i in range(count)])]
  transfers between devices with their start and end apart: 30 -> 30, of which waited for: 12 -> 9; matrix products, arithmetic and copies ran while one was open for 0% -> 0% of each run, Pallas kernels for 6% -> 7%
where the time goes in v5:
time: 56.1 us; the launch traced here: 55.9 us
  starting transfers between devices  34.5 us (61%)
  waiting for transfers between devices  13.8 us (25%)
  Pallas kernels  6.09 us (11%)
  between operations  1.46 us (3%)
    ppermute x30, starting transfers between devices, send(): return lax.ppermute(value, axis, [(i, i ^ step) for i in range(count)])  34.5 us
    ppermute x30, waiting for transfers between devices, send(): return lax.ppermute(value, axis, [(i, i ^ step) for i in range(count)])  13.8 us
    pallas_call x15, Pallas kernels, call(): pl.pallas_call(ordered, out_shape=outs, in_specs=[*in_specs, *[pl.BlockSp...  6.09 us
  transfers between devices with their start and end apart: 30, of which 9 were waited for; matrix products, arithmetic and copies ran while one was open for 0% of the time, Pallas kernels for 7%

profile of v5, /device:TPU:0, one launch (start us, length us, event | category | flops | bytes accessed | tf_op | source)
XLA Modules:
  0.0 55.9 jit_solution(6942657201745678403)
XLA Ops:
  0.6 1.0 %start.1 = (bf16[128,128]{1,0:T(8,128)(2,1)S(1)}, bf16[128,128]{1,0:T(8,128)(2,1)S(1)}, f32[1,128]{1,0:T(1,128)S(1)}, f32[128,128]{1,0:T(8,128)S(1)}) custom-call(f32[128,128]{1,0:T(8,128)} %refs_0_.7, f32[128,128]{1,0:T(8,128)} %refs_0_.6, s32[1,128]{1,0:T(1,128)} %bitcast.1, f32[8]{0:T(128)} %refs_3_.2), custom_call_target="tpu_custom_call" | custom-call | bytes 263200 | tf_op jit(solution)/shard_map/start/pallas_call | solution.py:36
  1.7 0.5 collective-permute-start
  2.2 2.6 %collective-permute-start.1 = (bf16[128,128]{1,0:T(8,128)(2,1)S(1)}, bf16[128,128]{1,0:T(8,128)(2,1)S(1)}, u32[]{:S(2)}, u32[]{:S(2)}) collective-permute-start(bf16[128,128]{1,0:T(8,128)(2,1)S(1)} %get-tuple-element.34.refs_0_.refs_1_), channel_id=1, source_target_pairs={{0,2},{1,3},{2,0},{3,1},{4,6},{5,7},{6,4},{7,5},{8,10},{9,11},{10,... | collective-permute-start | bytes 98312 | tf_op jit(solution)/shard_map/ppermute | solution.py:222
  4.8 0.1 collective-permute-start.2
  4.8 1.8 %collective-permute-start.3 = (bf16[128,128]{1,0:T(8,128)(2,1)S(1)}, bf16[128,128]{1,0:T(8,128)(2,1)S(1)}, u32[]{:S(2)}, u32[]{:S(2)}) collective-permute-start(bf16[128,128]{1,0:T(8,128)(2,1)S(1)} %get-tuple-element.35.refs_5_), channel_id=1, source_target_pairs={{0,4},{4,0},{8,12},{12,8},{16,20},{20,16},{24,28},{28,24},{1,5},{5... | collective-permute-start | bytes 98312 | tf_op jit(solution)/shard_map/ppermute | solution.py:222
  7.2 2.0 %dense.1.refs_0_ = bf16[512,1024]{1,0:T(8,128)(2,1)S(1)} custom-call(bf16[128,128]{1,0:T(8,128)(2,1)S(1)} %get-tuple-element.34.refs_0_.refs_1_, bf16[1,1,24,128,128]{4,3,2,1,0:T(8,128)(2,1)} %refs_1_.3, s32[1,1,24]{2,1,0:T(1,128)} %refs_2_.1, s32[1,1,24]{2,1,0:T(1,128)} %refs_3_.3, s32[1,1]{1,0:T(1,128)S(6)} %copy.10.refs_4_), custom_call_target="tpu_custom_call" | custom-call | bytes 1867972 | tf_op jit(solution)/shard_map/dense/pallas_call | solution.py:36
  9.3 0.0 collective-permute-done.1.refs_3_
  9.3 0.0 collective-permute-done.2.refs_4_
  9.3 0.3 adjoint.2
  9.6 1.2 %collective-permute-start.12 = (f32[2,128,128]{2,1,0:T(8,128)S(1)}, f32[2,128,128]{2,1,0:T(8,128)S(1)}, u32[]{:S(2)}, u32[]{:S(2)}) collective-permute-start(f32[2,128,128]{2,1,0:T(8,128)S(1)} %get-tuple-element.47), channel_id=1, source_target_pairs={{0,4},{4,0},{8,12},{12,8},{16,20},{20,16},{24,28},{28,24},{1,5},{5... | collective-permute-start | bytes 393224 | tf_op jit(solution)/shard_map/ppermute | solution.py:222
  10.9 0.9 %collective-permute-start.7 = (f32[2,128,128]{2,1,0:T(8,128)S(1)}, f32[2,128,128]{2,1,0:T(8,128)S(1)}, u32[]{:S(2)}, u32[]{:S(2)}) collective-permute-start(f32[2,128,128]{2,1,0:T(8,128)S(1)} %get-tuple-element.38), channel_id=1, source_target_pairs={{0,4},{4,0},{8,12},{12,8},{16,20},{20,16},{24,28},{28,24},{1,5},{5... | collective-permute-start | bytes 393224 | tf_op jit(solution)/shard_map/ppermute | solution.py:222
  11.7 1.4 %collective-permute-start.4 = (bf16[2,128,128]{2,1,0:T(8,128)(2,1)S(1)}, bf16[2,128,128]{2,1,0:T(8,128)(2,1)S(1)}, u32[]{:S(2)}, u32[]{:S(2)}) collective-permute-start(bf16[2,128,128]{2,1,0:T(8,128)(2,1)S(1)} %get-tuple-element.36.refs_1_), channel_id=1, source_target_pairs={{0,8},{4,12},{8,0},{12,4},{16,24},{20,28},{24,16},{28,20},{1,9},{5... | collective-permute-start | bytes 196616 | tf_op jit(solution)/shard_map/ppermute | solution.py:222
  13.1 2.6 %collective-permute-start.5 = (bf16[2,128,128]{2,1,0:T(8,128)(2,1)S(1)}, bf16[2,128,128]{2,1,0:T(8,128)(2,1)S(1)}, u32[]{:S(2)}, u32[]{:S(2)}) collective-permute-start(bf16[2,128,128]{2,1,0:T(8,128)(2,1)S(1)} %get-tuple-element.36.refs_1_), channel_id=1, source_target_pairs={{0,16},{4,20},{8,24},{12,28},{16,0},{20,4},{24,8},{28,12},{1,17},{... | collective-permute-start | bytes 196616 | tf_op jit(solution)/shard_map/ppermute | solution.py:222
  15.7 0.4 collective-permute-start.6
  16.1 2.4 %collective-permute-start.13 = (f32[128,128]{1,0:T(8,128)S(1)}, f32[128,128]{1,0:T(8,128)S(1)}, u32[]{:S(2)}, u32[]{:S(2)}) collective-permute-start(f32[128,128]{1,0:T(8,128)S(1)} %get-tuple-element.48), channel_id=1, source_target_pairs={{0,16},{4,20},{8,24},{12,28},{16,0},{20,4},{24,8},{28,12},{1,17},{... | collective-permute-start | bytes 196616 | tf_op jit(solution)/shard_map/ppermute | solution.py:222
  18.6 2.7 %collective-permute-start.14 = (f32[128,128]{1,0:T(8,128)S(1)}, f32[128,128]{1,0:T(8,128)S(1)}, u32[]{:S(2)}, u32[]{:S(2)}) collective-permute-start(f32[128,128]{1,0:T(8,128)S(1)} %get-tuple-element.49), channel_id=1, source_target_pairs={{0,24},{4,28},{8,16},{12,20},{16,8},{20,12},{24,0},{28,4},{1,25},{... | collective-permute-start | bytes 196616 | tf_op jit(solution)/shard_map/ppermute | solution.py:222
  21.3 0.1 collective-permute-start.11
  21.4 0.7 %collective-permute-done.6.refs_4_ = bf16[2,128,128]{2,1,0:T(8,128)(2,1)S(1)} collective-permute-done((bf16[2,128,128]{2,1,0:T(8,128)(2,1)S(1)}, bf16[2,128,128]{2,1,0:T(8,128)(2,1)S(1)}, u32[]{:S(2)}, u32[]{:S(2)}) %collective-permute-start.6) | collective-permute-done | bytes 65568 | tf_op jit(solution)/shard_map/ppermute | solution.py:222
  22.2 0.4 forward.2
  22.6 0.1 collective-permute-start.10
  22.7 1.3 %collective-permute-start.8 = (f32[128,128]{1,0:T(8,128)S(1)}, f32[128,128]{1,0:T(8,128)S(1)}, u32[]{:S(2)}, u32[]{:S(2)}) collective-permute-start(f32[128,128]{1,0:T(8,128)S(1)} %get-tuple-element.41), channel_id=1, source_target_pairs={{0,1},{1,0},{2,3},{3,2},{4,5},{5,4},{6,7},{7,6},{8,9},{9,8},{10,11... | collective-permute-start | bytes 196616 | tf_op jit(solution)/shard_map/ppermute | solution.py:222
  24.0 2.4 %collective-permute-done.13.refs_3_ = f32[128,128]{1,0:T(8,128)S(1)} collective-permute-done((f32[128,128]{1,0:T(8,128)S(1)}, f32[128,128]{1,0:T(8,128)S(1)}, u32[]{:S(2)}, u32[]{:S(2)}) %collective-permute-start.13) | collective-permute-done | bytes 65568 | tf_op jit(solution)/shard_map/ppermute | solution.py:222
  26.4 1.5 %collective-permute-start.9 = (f32[128,128]{1,0:T(8,128)S(1)}, f32[128,128]{1,0:T(8,128)S(1)}, u32[]{:S(2)}, u32[]{:S(2)}) collective-permute-start(f32[128,128]{1,0:T(8,128)S(1)} %get-tuple-element.42), channel_id=1, source_target_pairs={{0,2},{1,3},{2,0},{3,1},{4,6},{5,7},{6,4},{7,5},{8,10},{9,11},{10,... | collective-permute-start | bytes 196616 | tf_op jit(solution)/shard_map/ppermute | solution.py:222
  27.9 2.7 %collective-permute-done.9.refs_4_ = f32[128,128]{1,0:T(8,128)S(1)} collective-permute-done((f32[128,128]{1,0:T(8,128)S(1)}, f32[128,128]{1,0:T(8,128)S(1)}, u32[]{:S(2)}, u32[]{:S(2)}) %collective-permute-start.9) | collective-permute-done | bytes 65568 | tf_op jit(solution)/shard_map/ppermute | solution.py:222
  30.7 1.6 %collective-permute-start.15 = (bf16[128,128]{1,0:T(8,128)(2,1)S(1)}, bf16[128,128]{1,0:T(8,128)(2,1)S(1)}, u32[]{:S(2)}, u32[]{:S(2)}) collective-permute-start(bf16[128,128]{1,0:T(8,128)(2,1)S(1)} %forward_end.2.refs_0_.refs_1_), channel_id=1, source_target_pairs={{0,8},{4,12},{8,0},{12,4},{16,24},{20,28},{24,16},{28,20},{1,9},{5... | collective-permute-start | bytes 98312 | tf_op jit(solution)/shard_map/ppermute | solution.py:222
  32.3 1.4 %collective-permute-start.16 = (bf16[128,128]{1,0:T(8,128)(2,1)S(1)}, bf16[128,128]{1,0:T(8,128)(2,1)S(1)}, u32[]{:S(2)}, u32[]{:S(2)}) collective-permute-start(bf16[128,128]{1,0:T(8,128)(2,1)S(1)} %forward_end.2.refs_0_.refs_1_), channel_id=1, source_target_pairs={{0,16},{4,20},{8,24},{12,28},{16,0},{20,4},{24,8},{28,12},{1,17},{... | collective-permute-start | bytes 98312 | tf_op jit(solution)/shard_map/ppermute | solution.py:222
  33.7 1.4 %collective-permute-start.17 = (bf16[128,128]{1,0:T(8,128)(2,1)S(1)}, bf16[128,128]{1,0:T(8,128)(2,1)S(1)}, u32[]{:S(2)}, u32[]{:S(2)}) collective-permute-start(bf16[128,128]{1,0:T(8,128)(2,1)S(1)} %forward_end.2.refs_0_.refs_1_), channel_id=1, source_target_pairs={{0,24},{4,28},{8,16},{12,20},{16,8},{20,12},{24,0},{28,4},{1,25},{... | collective-permute-start | bytes 98312 | tf_op jit(solution)/shard_map/ppermute | solution.py:222
  35.1 1.5 %collective-permute-start.20 = (bf16[128,128]{1,0:T(8,128)(2,1)S(1)}, bf16[128,128]{1,0:T(8,128)(2,1)S(1)}, u32[]{:S(2)}, u32[]{:S(2)}) collective-permute-start(bf16[128,128]{1,0:T(8,128)(2,1)S(1)} %get-tuple-element.51.refs_1_), channel_id=1, source_target_pairs={{0,2},{1,3},{2,0},{3,1},{4,6},{5,7},{6,4},{7,5},{8,10},{9,11},{10,... | collective-permute-start | bytes 98312 | tf_op jit(solution)/shard_map/ppermute | solution.py:222
  36.6 0.4 collective-permute-start.21
  37.0 0.8 %collective-permute-done.16.refs_2_.refs_3_ = bf16[128,128]{1,0:T(8,128)(2,1)S(1)} collective-permute-done((bf16[128,128]{1,0:T(8,128)(2,1)S(1)}, bf16[128,128]{1,0:T(8,128)(2,1)S(1)}, u32[]{:S(2)}, u32[]{:S(2)}) %collective-permute-start.16) | collective-permute-done | bytes 32800 | tf_op jit(solution)/shard_map/ppermute | solution.py:222
  37.7 1.6 %collective-permute-done.17.refs_3_.refs_4_ = bf16[128,128]{1,0:T(8,128)(2,1)S(1)} collective-permute-done((bf16[128,128]{1,0:T(8,128)(2,1)S(1)}, bf16[128,128]{1,0:T(8,128)(2,1)S(1)}, u32[]{:S(2)}, u32[]{:S(2)}) %collective-permute-start.17) | collective-permute-done | bytes 32800 | tf_op jit(solution)/shard_map/ppermute | solution.py:222
  39.4 1.0 %collective-permute-start.18 = (bf16[4,128,128]{2,1,0:T(8,128)(2,1)S(1)}, bf16[4,128,128]{2,1,0:T(8,128)(2,1)S(1)}, u32[]{:S(2)}, u32[]{:S(2)}) collective-permute-start(bf16[4,128,128]{2,1,0:T(8,128)(2,1)S(1)} %pack.1), channel_id=1, source_target_pairs={{0,4},{4,0},{8,12},{12,8},{16,20},{20,16},{24,28},{28,24},{1,5},{5... | collective-permute-start | bytes 393224 | tf_op jit(solution)/shard_map/ppermute | solution.py:222
  40.5 0.3 adjoint.3
  40.8 1.1 %collective-permute-start.27 = (bf16[2,128,128]{2,1,0:T(8,128)(2,1)S(1)}, bf16[2,128,128]{2,1,0:T(8,128)(2,1)S(1)}, u32[]{:S(2)}, u32[]{:S(2)}) collective-permute-start(bf16[2,128,128]{2,1,0:T(8,128)(2,1)S(1)} %get-tuple-element.61), channel_id=1, source_target_pairs={{0,4},{4,0},{8,12},{12,8},{16,20},{20,16},{24,28},{28,24},{1,5},{5... | collective-permute-start | bytes 196616 | tf_op jit(solution)/shard_map/ppermute | solution.py:222
  41.9 1.0 %collective-permute-start.22 = (bf16[2,128,128]{2,1,0:T(8,128)(2,1)S(1)}, bf16[2,128,128]{2,1,0:T(8,128)(2,1)S(1)}, u32[]{:S(2)}, u32[]{:S(2)}) collective-permute-start(bf16[2,128,128]{2,1,0:T(8,128)(2,1)S(1)} %get-tuple-element.53), channel_id=1, source_target_pairs={{0,4},{4,0},{8,12},{12,8},{16,20},{20,16},{24,28},{28,24},{1,5},{5... | collective-permute-start | bytes 196616 | tf_op jit(solution)/shard_map/ppermute | solution.py:222
  42.9 3.7 %collective-permute-done.27.refs_1_ = bf16[2,128,128]{2,1,0:T(8,128)(2,1)S(1)} collective-permute-done((bf16[2,128,128]{2,1,0:T(8,128)(2,1)S(1)}, bf16[2,128,128]{2,1,0:T(8,128)(2,1)S(1)}, u32[]{:S(2)}, u32[]{:S(2)}) %collective-permute-start.27) | collective-permute-done | bytes 65568 | tf_op jit(solution)/shard_map/ppermute | solution.py:222
  46.6 0.1 collective-permute-start.28
  46.7 2.2 %collective-permute-start.29 = (bf16[128,128]{1,0:T(8,128)(2,1)S(1)}, bf16[128,128]{1,0:T(8,128)(2,1)S(1)}, u32[]{:S(2)}, u32[]{:S(2)}) collective-permute-start(bf16[128,128]{1,0:T(8,128)(2,1)S(1)} %get-tuple-element.63), channel_id=1, source_target_pairs={{0,24},{4,28},{8,16},{12,20},{16,8},{20,12},{24,0},{28,4},{1,25},{... | collective-permute-start | bytes 98312 | tf_op jit(solution)/shard_map/ppermute | solution.py:222
  48.9 1.3 %collective-permute-start.26 = (bf16[128,128]{1,0:T(8,128)(2,1)S(1)}, bf16[128,128]{1,0:T(8,128)(2,1)S(1)}, u32[]{:S(2)}, u32[]{:S(2)}) collective-permute-start(bf16[128,128]{1,0:T(8,128)(2,1)S(1)} %get-tuple-element.59), channel_id=1, source_target_pairs={{0,8},{4,12},{8,0},{12,4},{16,24},{20,28},{24,16},{28,20},{1,9},{5... | collective-permute-start | bytes 98312 | tf_op jit(solution)/shard_map/ppermute | solution.py:222
  50.2 0.4 forward.3
  50.7 0.1 collective-permute-start.23
  50.7 1.1 %collective-permute-start.24 = (bf16[128,128]{1,0:T(8,128)(2,1)S(1)}, bf16[128,128]{1,0:T(8,128)(2,1)S(1)}, u32[]{:S(2)}, u32[]{:S(2)}) collective-permute-start(bf16[128,128]{1,0:T(8,128)(2,1)S(1)} %get-tuple-element.57), channel_id=1, source_target_pairs={{0,2},{1,3},{2,0},{3,1},{4,6},{5,7},{6,4},{7,5},{8,10},{9,11},{10,... | collective-permute-start | bytes 98312 | tf_op jit(solution)/shard_map/ppermute | solution.py:222
  51.8 0.8 %collective-permute-start.25 = (bf16[128,128]{1,0:T(8,128)(2,1)S(1)}, bf16[128,128]{1,0:T(8,128)(2,1)S(1)}, u32[]{:S(2)}, u32[]{:S(2)}) collective-permute-start(bf16[128,128]{1,0:T(8,128)(2,1)S(1)} %get-tuple-element.58), channel_id=1, source_target_pairs={{0,3},{1,2},{2,1},{3,0},{4,7},{5,6},{6,5},{7,4},{8,11},{9,10},{10,... | collective-permute-start | bytes 98312 | tf_op jit(solution)/shard_map/ppermute | solution.py:222
  52.6 0.3 collective-permute-done.26.refs_5_
  52.9 0.7 %adjoint_end.1 = f32[128,128]{1,0:T(8,128)} custom-call(f32[128,128]{1,0:T(8,128)S(1)} %copy-done.1, f32[128,128]{1,0:T(8,128)S(1)} %get-tuple-element.50.refs_6_.refs_1_, f32[1,128]{1,0:T(1,128)S(1)} %get-tuple-element.44.refs_0_.refs_2_, f32[128,128]{1,0:T(8,128)S(1)} %get-tuple-element.33.refs_1_.refs_3_, ...), custom_call_target="tpu_custom_call" | custom-call | bytes 426496 | tf_op jit(solution)/shard_map/adjoint_end/pallas_call | solution.py:36
  53.7 1.1 %collective-permute-done.24.refs_4_ = bf16[128,128]{1,0:T(8,128)(2,1)S(1)} collective-permute-done((bf16[128,128]{1,0:T(8,128)(2,1)S(1)}, bf16[128,128]{1,0:T(8,128)(2,1)S(1)}, u32[]{:S(2)}, u32[]{:S(2)}) %collective-permute-start.24) | collective-permute-done | bytes 32800 | tf_op jit(solution)/shard_map/ppermute | solution.py:222
  54.7 0.5 collective-permute-done.25.refs_5_
  55.2 0.7 %forward_end.3 = f32[128,128]{1,0:T(8,128)} custom-call(f32[128,128]{1,0:T(8,128)S(1)} %copy-done, f32[128,128]{1,0:T(8,128)S(1)} %get-tuple-element.33.refs_1_.refs_3_, bf16[128,128]{1,0:T(8,128)(2,1)S(1)} %get-tuple-element.55.refs_2_, bf16[128,128]{1,0:T(8,128)(2,1)S(1)} %collective-permute-done.23.refs_3_, ...), custom_call_target="tpu_custom_call" | custom-call | bytes 327680 | tf_op jit(solution)/shard_map/forward_end/pallas_call | solution.py:36
  (31 shorter events, 0.2 us)
Async XLA Ops:
  1.7 7.6 %collective-permute-start = (bf16[128,128]{1,0:T(8,128)(2,1)S(1)}, bf16[128,128]{1,0:T(8,128)(2,1)S(1)}, u32[]{:S(2)}, u32[]{:S(2)}) collective-permute-start(bf16[128,128]{1,0:T(8,128)(2,1)S(1)} %get-tuple-element.34.refs_0_.refs_1_), channel_id=1, source_target_pairs={{0,1},{1,0},{2,3},{3,2},{4,5},{5,4},{6,7},{7,6},{8,9},{9,8},{10,11... | collective-permute-start | bytes 98312 | tf_op jit(solution)/shard_map/ppermute | solution.py:222
  2.2 7.1 %collective-permute-start.1 = (bf16[128,128]{1,0:T(8,128)(2,1)S(1)}, bf16[128,128]{1,0:T(8,128)(2,1)S(1)}, u32[]{:S(2)}, u32[]{:S(2)}) collective-permute-start(bf16[128,128]{1,0:T(8,128)(2,1)S(1)} %get-tuple-element.34.refs_0_.refs_1_), channel_id=1, source_target_pairs={{0,2},{1,3},{2,0},{3,1},{4,6},{5,7},{6,4},{7,5},{8,10},{9,11},{10,... | collective-permute-start | bytes 98312 | tf_op jit(solution)/shard_map/ppermute | solution.py:222
  4.8 4.5 %collective-permute-start.2 = (bf16[128,128]{1,0:T(8,128)(2,1)S(1)}, bf16[128,128]{1,0:T(8,128)(2,1)S(1)}, u32[]{:S(2)}, u32[]{:S(2)}) collective-permute-start(bf16[128,128]{1,0:T(8,128)(2,1)S(1)} %get-tuple-element.34.refs_0_.refs_1_), channel_id=1, source_target_pairs={{0,3},{1,2},{2,1},{3,0},{4,7},{5,6},{6,5},{7,4},{8,11},{9,10},{10,... | collective-permute-start | bytes 98312 | tf_op jit(solution)/shard_map/ppermute | solution.py:222
  4.8 4.5 %collective-permute-start.3 = (bf16[128,128]{1,0:T(8,128)(2,1)S(1)}, bf16[128,128]{1,0:T(8,128)(2,1)S(1)}, u32[]{:S(2)}, u32[]{:S(2)}) collective-permute-start(bf16[128,128]{1,0:T(8,128)(2,1)S(1)} %get-tuple-element.35.refs_5_), channel_id=1, source_target_pairs={{0,4},{4,0},{8,12},{12,8},{16,20},{20,16},{24,28},{28,24},{1,5},{5... | collective-permute-start | bytes 98312 | tf_op jit(solution)/shard_map/ppermute | solution.py:222
  9.6 6.5 %collective-permute-start.12 = (f32[2,128,128]{2,1,0:T(8,128)S(1)}, f32[2,128,128]{2,1,0:T(8,128)S(1)}, u32[]{:S(2)}, u32[]{:S(2)}) collective-permute-start(f32[2,128,128]{2,1,0:T(8,128)S(1)} %get-tuple-element.47), channel_id=1, source_target_pairs={{0,4},{4,0},{8,12},{12,8},{16,20},{20,16},{24,28},{28,24},{1,5},{5... | collective-permute-start | bytes 393224 | tf_op jit(solution)/shard_map/ppermute | solution.py:222
  10.9 7.7 %collective-permute-start.7 = (f32[2,128,128]{2,1,0:T(8,128)S(1)}, f32[2,128,128]{2,1,0:T(8,128)S(1)}, u32[]{:S(2)}, u32[]{:S(2)}) collective-permute-start(f32[2,128,128]{2,1,0:T(8,128)S(1)} %get-tuple-element.38), channel_id=1, source_target_pairs={{0,4},{4,0},{8,12},{12,8},{16,20},{20,16},{24,28},{28,24},{1,5},{5... | collective-permute-start | bytes 393224 | tf_op jit(solution)/shard_map/ppermute | solution.py:222
  11.7 9.6 %collective-permute-start.4 = (bf16[2,128,128]{2,1,0:T(8,128)(2,1)S(1)}, bf16[2,128,128]{2,1,0:T(8,128)(2,1)S(1)}, u32[]{:S(2)}, u32[]{:S(2)}) collective-permute-start(bf16[2,128,128]{2,1,0:T(8,128)(2,1)S(1)} %get-tuple-element.36.refs_1_), channel_id=1, source_target_pairs={{0,8},{4,12},{8,0},{12,4},{16,24},{20,28},{24,16},{28,20},{1,9},{5... | collective-permute-start | bytes 196616 | tf_op jit(solution)/shard_map/ppermute | solution.py:222
  13.1 8.3 %collective-permute-start.5 = (bf16[2,128,128]{2,1,0:T(8,128)(2,1)S(1)}, bf16[2,128,128]{2,1,0:T(8,128)(2,1)S(1)}, u32[]{:S(2)}, u32[]{:S(2)}) collective-permute-start(bf16[2,128,128]{2,1,0:T(8,128)(2,1)S(1)} %get-tuple-element.36.refs_1_), channel_id=1, source_target_pairs={{0,16},{4,20},{8,24},{12,28},{16,0},{20,4},{24,8},{28,12},{1,17},{... | collective-permute-start | bytes 196616 | tf_op jit(solution)/shard_map/ppermute | solution.py:222
  15.7 6.4 %collective-permute-start.6 = (bf16[2,128,128]{2,1,0:T(8,128)(2,1)S(1)}, bf16[2,128,128]{2,1,0:T(8,128)(2,1)S(1)}, u32[]{:S(2)}, u32[]{:S(2)}) collective-permute-start(bf16[2,128,128]{2,1,0:T(8,128)(2,1)S(1)} %get-tuple-element.36.refs_1_), channel_id=1, source_target_pairs={{0,24},{4,28},{8,16},{12,20},{16,8},{20,12},{24,0},{28,4},{1,25},{... | collective-permute-start | bytes 196616 | tf_op jit(solution)/shard_map/ppermute | solution.py:222
  16.1 10.2 %collective-permute-start.13 = (f32[128,128]{1,0:T(8,128)S(1)}, f32[128,128]{1,0:T(8,128)S(1)}, u32[]{:S(2)}, u32[]{:S(2)}) collective-permute-start(f32[128,128]{1,0:T(8,128)S(1)} %get-tuple-element.48), channel_id=1, source_target_pairs={{0,16},{4,20},{8,24},{12,28},{16,0},{20,4},{24,8},{28,12},{1,17},{... | collective-permute-start | bytes 196616 | tf_op jit(solution)/shard_map/ppermute | solution.py:222
  18.6 9.3 %collective-permute-start.14 = (f32[128,128]{1,0:T(8,128)S(1)}, f32[128,128]{1,0:T(8,128)S(1)}, u32[]{:S(2)}, u32[]{:S(2)}) collective-permute-start(f32[128,128]{1,0:T(8,128)S(1)} %get-tuple-element.49), channel_id=1, source_target_pairs={{0,24},{4,28},{8,16},{12,20},{16,8},{20,12},{24,0},{28,4},{1,25},{... | collective-permute-start | bytes 196616 | tf_op jit(solution)/shard_map/ppermute | solution.py:222
  21.3 6.5 %collective-permute-start.11 = (f32[128,128]{1,0:T(8,128)S(1)}, f32[128,128]{1,0:T(8,128)S(1)}, u32[]{:S(2)}, u32[]{:S(2)}) collective-permute-start(f32[128,128]{1,0:T(8,128)S(1)} %get-tuple-element.45), channel_id=1, source_target_pairs={{0,8},{4,12},{8,0},{12,4},{16,24},{20,28},{24,16},{28,20},{1,9},{5... | collective-permute-start | bytes 196616 | tf_op jit(solution)/shard_map/ppermute | solution.py:222
  22.6 5.3 %collective-permute-start.10 = (f32[128,128]{1,0:T(8,128)S(1)}, f32[128,128]{1,0:T(8,128)S(1)}, u32[]{:S(2)}, u32[]{:S(2)}) collective-permute-start(f32[128,128]{1,0:T(8,128)S(1)} %get-tuple-element.43), channel_id=1, source_target_pairs={{0,3},{1,2},{2,1},{3,0},{4,7},{5,6},{6,5},{7,4},{8,11},{9,10},{10,... | collective-permute-start | bytes 196616 | tf_op jit(solution)/shard_map/ppermute | solution.py:222
  22.7 5.2 %collective-permute-start.8 = (f32[128,128]{1,0:T(8,128)S(1)}, f32[128,128]{1,0:T(8,128)S(1)}, u32[]{:S(2)}, u32[]{:S(2)}) collective-permute-start(f32[128,128]{1,0:T(8,128)S(1)} %get-tuple-element.41), channel_id=1, source_target_pairs={{0,1},{1,0},{2,3},{3,2},{4,5},{5,4},{6,7},{7,6},{8,9},{9,8},{10,11... | collective-permute-start | bytes 196616 | tf_op jit(solution)/shard_map/ppermute | solution.py:222
  26.4 4.3 %collective-permute-start.9 = (f32[128,128]{1,0:T(8,128)S(1)}, f32[128,128]{1,0:T(8,128)S(1)}, u32[]{:S(2)}, u32[]{:S(2)}) collective-permute-start(f32[128,128]{1,0:T(8,128)S(1)} %get-tuple-element.42), channel_id=1, source_target_pairs={{0,2},{1,3},{2,0},{3,1},{4,6},{5,7},{6,4},{7,5},{8,10},{9,11},{10,... | collective-permute-start | bytes 196616 | tf_op jit(solution)/shard_map/ppermute | solution.py:222
  27.9 2.8 %copy-start = (f32[128,128]{1,0:T(8,128)S(1)}, f32[128,128]{1,0:T(8,128)}, u32[]{:S(2)}) copy-start(f32[128,128]{1,0:T(8,128)} %refs_0_.6) | copy-start | bytes 196612
  30.7 6.0 %collective-permute-start.15 = (bf16[128,128]{1,0:T(8,128)(2,1)S(1)}, bf16[128,128]{1,0:T(8,128)(2,1)S(1)}, u32[]{:S(2)}, u32[]{:S(2)}) collective-permute-start(bf16[128,128]{1,0:T(8,128)(2,1)S(1)} %forward_end.2.refs_0_.refs_1_), channel_id=1, source_target_pairs={{0,8},{4,12},{8,0},{12,4},{16,24},{20,28},{24,16},{28,20},{1,9},{5... | collective-permute-start | bytes 98312 | tf_op jit(solution)/shard_map/ppermute | solution.py:222
  32.3 5.5 %collective-permute-start.16 = (bf16[128,128]{1,0:T(8,128)(2,1)S(1)}, bf16[128,128]{1,0:T(8,128)(2,1)S(1)}, u32[]{:S(2)}, u32[]{:S(2)}) collective-permute-start(bf16[128,128]{1,0:T(8,128)(2,1)S(1)} %forward_end.2.refs_0_.refs_1_), channel_id=1, source_target_pairs={{0,16},{4,20},{8,24},{12,28},{16,0},{20,4},{24,8},{28,12},{1,17},{... | collective-permute-start | bytes 98312 | tf_op jit(solution)/shard_map/ppermute | solution.py:222
  33.7 5.7 %collective-permute-start.17 = (bf16[128,128]{1,0:T(8,128)(2,1)S(1)}, bf16[128,128]{1,0:T(8,128)(2,1)S(1)}, u32[]{:S(2)}, u32[]{:S(2)}) collective-permute-start(bf16[128,128]{1,0:T(8,128)(2,1)S(1)} %forward_end.2.refs_0_.refs_1_), channel_id=1, source_target_pairs={{0,24},{4,28},{8,16},{12,20},{16,8},{20,12},{24,0},{28,4},{1,25},{... | collective-permute-start | bytes 98312 | tf_op jit(solution)/shard_map/ppermute | solution.py:222
  35.1 5.3 %collective-permute-start.19 = (bf16[128,128]{1,0:T(8,128)(2,1)S(1)}, bf16[128,128]{1,0:T(8,128)(2,1)S(1)}, u32[]{:S(2)}, u32[]{:S(2)}) collective-permute-start(bf16[128,128]{1,0:T(8,128)(2,1)S(1)} %get-tuple-element.51.refs_1_), channel_id=1, source_target_pairs={{0,1},{1,0},{2,3},{3,2},{4,5},{5,4},{6,7},{7,6},{8,9},{9,8},{10,11... | collective-permute-start | bytes 98312 | tf_op jit(solution)/shard_map/ppermute | solution.py:222
  35.1 5.3 %collective-permute-start.20 = (bf16[128,128]{1,0:T(8,128)(2,1)S(1)}, bf16[128,128]{1,0:T(8,128)(2,1)S(1)}, u32[]{:S(2)}, u32[]{:S(2)}) collective-permute-start(bf16[128,128]{1,0:T(8,128)(2,1)S(1)} %get-tuple-element.51.refs_1_), channel_id=1, source_target_pairs={{0,2},{1,3},{2,0},{3,1},{4,6},{5,7},{6,4},{7,5},{8,10},{9,11},{10,... | collective-permute-start | bytes 98312 | tf_op jit(solution)/shard_map/ppermute | solution.py:222
  36.6 3.8 %collective-permute-start.21 = (bf16[128,128]{1,0:T(8,128)(2,1)S(1)}, bf16[128,128]{1,0:T(8,128)(2,1)S(1)}, u32[]{:S(2)}, u32[]{:S(2)}) collective-permute-start(bf16[128,128]{1,0:T(8,128)(2,1)S(1)} %get-tuple-element.51.refs_1_), channel_id=1, source_target_pairs={{0,3},{1,2},{2,1},{3,0},{4,7},{5,6},{6,5},{7,4},{8,11},{9,10},{10,... | collective-permute-start | bytes 98312 | tf_op jit(solution)/shard_map/ppermute | solution.py:222
  39.4 10.8 %collective-permute-start.18 = (bf16[4,128,128]{2,1,0:T(8,128)(2,1)S(1)}, bf16[4,128,128]{2,1,0:T(8,128)(2,1)S(1)}, u32[]{:S(2)}, u32[]{:S(2)}) collective-permute-start(bf16[4,128,128]{2,1,0:T(8,128)(2,1)S(1)} %pack.1), channel_id=1, source_target_pairs={{0,4},{4,0},{8,12},{12,8},{16,20},{20,16},{24,28},{28,24},{1,5},{5... | collective-permute-start | bytes 393224 | tf_op jit(solution)/shard_map/ppermute | solution.py:222
  40.8 5.8 %collective-permute-start.27 = (bf16[2,128,128]{2,1,0:T(8,128)(2,1)S(1)}, bf16[2,128,128]{2,1,0:T(8,128)(2,1)S(1)}, u32[]{:S(2)}, u32[]{:S(2)}) collective-permute-start(bf16[2,128,128]{2,1,0:T(8,128)(2,1)S(1)} %get-tuple-element.61), channel_id=1, source_target_pairs={{0,4},{4,0},{8,12},{12,8},{16,20},{20,16},{24,28},{28,24},{1,5},{5... | collective-permute-start | bytes 196616 | tf_op jit(solution)/shard_map/ppermute | solution.py:222
  41.9 7.0 %collective-permute-start.22 = (bf16[2,128,128]{2,1,0:T(8,128)(2,1)S(1)}, bf16[2,128,128]{2,1,0:T(8,128)(2,1)S(1)}, u32[]{:S(2)}, u32[]{:S(2)}) collective-permute-start(bf16[2,128,128]{2,1,0:T(8,128)(2,1)S(1)} %get-tuple-element.53), channel_id=1, source_target_pairs={{0,4},{4,0},{8,12},{12,8},{16,20},{20,16},{24,28},{28,24},{1,5},{5... | collective-permute-start | bytes 196616 | tf_op jit(solution)/shard_map/ppermute | solution.py:222
  46.6 5.3 %collective-permute-start.28 = (bf16[128,128]{1,0:T(8,128)(2,1)S(1)}, bf16[128,128]{1,0:T(8,128)(2,1)S(1)}, u32[]{:S(2)}, u32[]{:S(2)}) collective-permute-start(bf16[128,128]{1,0:T(8,128)(2,1)S(1)} %get-tuple-element.62), channel_id=1, source_target_pairs={{0,16},{4,20},{8,24},{12,28},{16,0},{20,4},{24,8},{28,12},{1,17},{... | collective-permute-start | bytes 98312 | tf_op jit(solution)/shard_map/ppermute | solution.py:222
  46.7 5.9 %collective-permute-start.29 = (bf16[128,128]{1,0:T(8,128)(2,1)S(1)}, bf16[128,128]{1,0:T(8,128)(2,1)S(1)}, u32[]{:S(2)}, u32[]{:S(2)}) collective-permute-start(bf16[128,128]{1,0:T(8,128)(2,1)S(1)} %get-tuple-element.63), channel_id=1, source_target_pairs={{0,24},{4,28},{8,16},{12,20},{16,8},{20,12},{24,0},{28,4},{1,25},{... | collective-permute-start | bytes 98312 | tf_op jit(solution)/shard_map/ppermute | solution.py:222
  48.9 4.0 %collective-permute-start.26 = (bf16[128,128]{1,0:T(8,128)(2,1)S(1)}, bf16[128,128]{1,0:T(8,128)(2,1)S(1)}, u32[]{:S(2)}, u32[]{:S(2)}) collective-permute-start(bf16[128,128]{1,0:T(8,128)(2,1)S(1)} %get-tuple-element.59), channel_id=1, source_target_pairs={{0,8},{4,12},{8,0},{12,4},{16,24},{20,28},{24,16},{28,20},{1,9},{5... | collective-permute-start | bytes 98312 | tf_op jit(solution)/shard_map/ppermute | solution.py:222
  50.2 2.7 %copy-start.1 = (f32[128,128]{1,0:T(8,128)S(1)}, f32[128,128]{1,0:T(8,128)}, u32[]{:S(2)}) copy-start(f32[128,128]{1,0:T(8,128)} %refs_0_.7) | copy-start | bytes 196612
  50.7 3.0 %collective-permute-start.23 = (bf16[128,128]{1,0:T(8,128)(2,1)S(1)}, bf16[128,128]{1,0:T(8,128)(2,1)S(1)}, u32[]{:S(2)}, u32[]{:S(2)}) collective-permute-start(bf16[128,128]{1,0:T(8,128)(2,1)S(1)} %get-tuple-element.56), channel_id=1, source_target_pairs={{0,1},{1,0},{2,3},{3,2},{4,5},{5,4},{6,7},{7,6},{8,9},{9,8},{10,11... | collective-permute-start | bytes 98312 | tf_op jit(solution)/shard_map/ppermute | solution.py:222
  50.7 4.0 %collective-permute-start.24 = (bf16[128,128]{1,0:T(8,128)(2,1)S(1)}, bf16[128,128]{1,0:T(8,128)(2,1)S(1)}, u32[]{:S(2)}, u32[]{:S(2)}) collective-permute-start(bf16[128,128]{1,0:T(8,128)(2,1)S(1)} %get-tuple-element.57), channel_id=1, source_target_pairs={{0,2},{1,3},{2,0},{3,1},{4,6},{5,7},{6,4},{7,5},{8,10},{9,11},{10,... | collective-permute-start | bytes 98312 | tf_op jit(solution)/shard_map/ppermute | solution.py:222
  51.8 3.3 %collective-permute-start.25 = (bf16[128,128]{1,0:T(8,128)(2,1)S(1)}, bf16[128,128]{1,0:T(8,128)(2,1)S(1)}, u32[]{:S(2)}, u32[]{:S(2)}) collective-permute-start(bf16[128,128]{1,0:T(8,128)(2,1)S(1)} %get-tuple-element.58), channel_id=1, source_target_pairs={{0,3},{1,2},{2,1},{3,0},{4,7},{5,6},{6,5},{7,4},{8,11},{9,10},{10,... | collective-permute-start | bytes 98312 | tf_op jit(solution)/shard_map/ppermute | solution.py:222

commit v6 on v5

--- a/solution.py
+++ b/solution.py
@@ -45,14 +45,6 @@
     )(*args, *after)
 
 
-def fetch(pairs, sems):
-    copies = [pltpu.make_async_copy(a, b, sems.at[i]) for i, (a, b) in enumerate(pairs)]
-    for copy in copies:
-        copy.start()
-    for copy in copies:
-        copy.wait()
-
-
 def rate_row(types_ref, teleport_ref):
     types = types_ref[...]
     rate = jnp.zeros(types.shape, F32)
@@ -67,56 +59,44 @@
 
 
 def start_body(
+    row_hbm,
+    col_hbm,
+    types_hbm,
+    teleport_hbm,
     cot_hbm,
     h_hbm,
-    types_hbm,
-    teleport_hbm,
+    tiles_hbm,
+    count_ref,
     q_ref,
     p_ref,
-    row_ref,
+    rate_ref,
     column_ref,
-    cot_ref,
-    h_ref,
-    types_ref,
-    teleport_ref,
-    sems,
-):
-    fetch(
-        [
-            (types_hbm, types_ref),
-            (teleport_hbm, teleport_ref),
-            (cot_hbm, cot_ref),
-            (h_hbm, h_ref),
-        ],
-        sems,
-    )
-    rate = rate_row(types_ref, teleport_ref)
-    row_ref[...] = rate
-    column_ref[...] = rate_column(rate, h_ref.shape[1])
-    q_ref[...] = ((1.0 - rate) * cot_ref[...].T).astype(BF16)
-    p_ref[...] = h_ref[...].astype(BF16)
-
-
-def dense_body(
-    q_ref,
-    tiles_hbm,
-    row_hbm,
-    col_hbm,
-    count_ref,
     dense_ref,
     row_ref,
     col_ref,
+    types_ref,
+    teleport_ref,
+    cot_ref,
+    h_ref,
     sems,
     slot_sems,
 ):
+    sources = (row_hbm, col_hbm, types_hbm, teleport_hbm, cot_hbm, h_hbm)
+    targets = (row_ref, col_ref, types_ref, teleport_ref, cot_ref, h_ref)
+    copies = [
+        pltpu.make_async_copy(a, b, sems.at[i]) for i, (a, b) in enumerate(zip(sources, targets))
+    ]
+    for copy in copies:
+        copy.start()
     size = tiles_hbm.shape[-1]
     me_row = lax.axis_index("rows")
     me_col = lax.axis_index("cols")
     dense_ref[...] = jnp.zeros_like(dense_ref)
-    fetch([(row_hbm, row_ref), (col_hbm, col_ref)], sems)
+    copies[0].wait()
+    copies[1].wait()
     count = count_ref[0, 0]
 
-    def copy(slot):
+    def tile_copy(slot):
         row = row_ref[0, 0, slot] ^ me_col
         col = col_ref[0, 0, slot] ^ me_row
         return pltpu.make_async_copy(
@@ -129,20 +109,27 @@
         )
 
     def begin(slot, carry):
-        copy(slot).start()
+        tile_copy(slot).start()
         return carry
 
     def end(slot, carry):
-        copy(slot).wait()
+        tile_copy(slot).wait()
         return carry
 
     lax.fori_loop(0, count, begin, 0)
+    for copy in copies[2:]:
+        copy.wait()
+    rate = rate_row(types_ref, teleport_ref)
+    rate_ref[...] = rate
+    column_ref[...] = rate_column(rate, h_ref.shape[1])
+    q_ref[...] = ((1.0 - rate) * cot_ref[...].T).astype(BF16)
+    p_ref[...] = h_ref[...].astype(BF16)
     lax.fori_loop(0, count, end, 0)
 
 
 def adjoint_body(n_rows, n_cols, dense_ref, *refs):
-    blocks, refs = refs[:n_cols], refs[n_cols:]
-    *pair, send_far, send_near, keep_far, keep_near = refs
+    blocks, outs = refs[:n_cols], refs[n_cols:]
+    send_far, send_near, keep_far, keep_near = outs
     half = n_rows // 2
     near = send_near.shape[0]
     size = blocks[0].shape[1]
@@ -156,10 +143,6 @@
         )
         keep[at] = part[:, :size]
         send[at] = part[:, size:].astype(send.dtype)
-    if pair:
-        own, other, both = pair
-        both[0] = own[...]
-        both[1] = other[...]
 
 
 def add_body(keep_ref, got_ref, *outs):
@@ -236,66 +219,74 @@
     def shape(kind, *lead):
         return jax.ShapeDtypeStruct((*lead, size, features), kind)
 
-    q0, p0, rate, column = call(
+    q0, p0, rate, column, dense = call(
         start_body,
-        [shape(BF16), shape(BF16), jax.ShapeDtypeStruct((1, size), F32), shape(F32)],
-        [hbm()] * 4,
-        in_hbm(cotangent, h_start, types, teleport),
+        [
+            shape(BF16),
+            shape(BF16),
+            jax.ShapeDtypeStruct((1, size), F32),
+            shape(F32),
+            jax.ShapeDtypeStruct((n_cols * size, n_rows * size), BF16),
+        ],
+        [hbm()] * 7 + [smem()],
+        [
+            *in_hbm(tile_row, tile_col, types, teleport, cotangent, h_start, tile_values),
+            tile_count,
+        ],
         0,
         "start",
         [
+            pltpu.SMEM(tile_row.shape, jnp.int32),
+            pltpu.SMEM(tile_col.shape, jnp.int32),
+            pltpu.VMEM(types.shape, jnp.int32),
+            pltpu.SMEM(teleport.shape, F32),
             pltpu.VMEM(cotangent.shape, F32),
             pltpu.VMEM(h_start.shape, F32),
-            pltpu.VMEM(types.shape, jnp.int32),
-            pltpu.SMEM(teleport.shape, F32),
-            pltpu.SemaphoreType.DMA((4,)),
-        ],
-    )
-    (dense,) = call(
-        dense_body,
-        [jax.ShapeDtypeStruct((n_cols * size, n_rows * size), BF16)],
-        [vmem()] + [hbm()] * 3 + [smem()],
-        [q0, *in_hbm(tile_values, tile_row, tile_col), tile_count],
-        0,
-        "dense",
-        [
-            pltpu.SMEM(tile_row.shape, jnp.int32),
-            pltpu.SMEM(tile_col.shape, jnp.int32),
-            pltpu.SemaphoreType.DMA((2,)),
+            pltpu.SemaphoreType.DMA((6,)),
             pltpu.SemaphoreType.DMA((slots,)),
         ],
     )
 
-    def add(keep, got, kinds, name):
-        return call(add_body, [shape(kind) for kind in kinds], [vmem()] * 2, (keep, got), 0, name)
-
-    def adjoint_hop(part, kind, pair):
-        blocks = [part] + [send(part, "cols", n_cols, s) for s in range(1, n_cols)]
-        *both, send_far, send_near, keep_far, keep_near = call(
+    def add(keep, got, kinds, name, after=()):
+        outs = [shape(kind) for kind in kinds]
+        return call(add_body, outs, [vmem()] * 2, (keep, got), 0, name, after=after)
+
+    def pack(parts, after=()):
+        (packed,) = call(
+            pack_body, [shape(BF16, len(parts))], [vmem()] * len(parts), parts, 0, "pack", after=after
+        )
+        return packed
+
+    def swap_cols(parts):
+        return [parts[0]] + [send(parts[s], "cols", n_cols, s) for s in range(1, n_cols)]
+
+    def swap_high(part):
+        return [part] + [send(part, "rows", n_rows, 2 * s) for s in range(1, half)]
+
+    def adjoint_products(part, kind, after=()):
+        return call(
             lambda *refs: adjoint_body(n_rows, n_cols, *refs),
-            [shape(BF16, 2)] * (len(pair) // 2)
-            + [shape(kind, half - near), shape(kind, near)]
+            [shape(kind, half - near), shape(kind, near)]
             + [shape(F32, half - near), shape(F32, near)],
-            [vmem()] * (1 + n_cols + len(pair)),
-            [dense, *blocks, *pair],
+            [vmem()] * (1 + n_cols),
+            [dense, *swap_cols([part] * n_cols)],
             hop_flops,
             "adjoint",
-        )
-        far = add(keep_far, send(send_far, "rows", n_rows, 1), [kind] * (half - near), "add_far")
-        far = [send(far[s - near], "rows", n_rows, 2 * s) for s in range(near, half)]
-        kinds = [F32] + [kind] * (near - 1)
-        close = add(keep_near, send(send_near, "rows", n_rows, 1), kinds, "add_near")
-        close = [close[0]] + [send(close[s], "rows", n_rows, 2 * s) for s in range(1, near)]
-        return close + far, both
-
-    def forward_hop(part, kind, paired, after):
-        panels = [part] + [send(part, "rows", n_rows, 2 * s) for s in range(1, half)]
-        if not paired:
-            (packed,) = call(
-                pack_body, [shape(BF16, half)], [vmem()] * half, panels, 0, "pack"
-            )
-            panels = panels + [send(packed, "rows", n_rows, 1)]
-        sums = call(
+            after=after,
+        )
+
+    def far_sums(keep, sent, kind):
+        got = send(sent, "rows", n_rows, 1)
+        sums = add(keep, got, [kind] * (half - near), "add_far")
+        return sums[:1], [send(sums[s - near], "rows", n_rows, 2 * s) for s in range(near, half)]
+
+    def near_sums(keep, sent, kind, after):
+        got = send(sent, "rows", n_rows, 1)
+        sums = add(keep, got, [F32] + [kind] * (near - 1), "add_near", after)
+        return [sums[0]] + [send(sums[s], "rows", n_rows, 2 * s) for s in range(1, near)]
+
+    def forward_products(panels, kind, paired, after):
+        return call(
             lambda *refs: forward_body(half, n_cols, paired, *refs),
             [shape(kind)] * n_cols,
             [vmem()] * (1 + len(panels)),
@@ -304,9 +295,8 @@
             "forward",
             after=after,
         )
-        return [sums[0]] + [send(sums[s], "cols", n_cols, s) for s in range(1, n_cols)]
-
-    def forward_end(parts, kind, after=()):
+
+    def forward_end(parts, kind):
         return call(
             forward_end_body,
             [shape(kind)],
@@ -314,28 +304,36 @@
             (h_start, column, *parts),
             0,
             "forward_end",
-            after=after,
         )[0]
 
-    back, (both,) = adjoint_hop(q0, F32, [p0, send(p0, "rows", n_rows, 1)])
-    first = forward_hop(both, F32, True, back[:1])
+    both = pack([p0, send(p0, "rows", n_rows, 1)])
+    panels = swap_high(both)
+    send_far, send_near, keep_far, keep_near = adjoint_products(q0, F32, [both])
+    last, far = far_sums(keep_far, send_far, F32)
+    close = near_sums(keep_near, send_near, F32, last)
+    first = forward_products(panels, F32, True, close[:1])
+    p1 = forward_end(swap_cols(first), BF16)
+    panels = swap_high(p1)
     d1, q1 = call(
         adjoint_mid_body,
         [shape(F32), shape(BF16)],
         [vmem()] * (1 + half),
-        (rate, *back),
+        (rate, *close, *far),
         0,
         "adjoint_mid",
-    )
-    p1 = forward_end(first, BF16, [d1])
-    back_two, _ = adjoint_hop(q1, BF16, [])
-    second = forward_hop(p1, BF16, False, back_two[:1])
-    propagated = forward_end(second, F32)
+        after=[p1],
+    )
+    panels = panels + [send(pack(panels, [q1]), "rows", n_rows, 1)]
+    send_far, send_near, keep_far, keep_near = adjoint_products(q1, BF16)
+    last, far = far_sums(keep_far, send_far, BF16)
+    close = near_sums(keep_near, send_near, BF16, last)
+    second = forward_products(panels, BF16, False, close[:1])
+    propagated = forward_end(swap_cols(second), F32)
     (input_grad,) = call(
         adjoint_end_body,
         [shape(F32)],
         [vmem()] * (4 + half),
-        (cotangent, d1, rate, column, *back_two),
+        (cotangent, d1, rate, column, *close, *far),
         0,
         "adjoint_end",
     )

time: 56.1 us -> 57.2 us (1.020)
  waiting for transfers between devices: 13.8 us -> 17.2 us
  Pallas kernels: 6.09 us -> 4.78 us
  starting transfers between devices: 34.5 us -> 33.4 us
    ppermute x30, waiting for transfers between devices: 13.8 us -> 17.2 us  [send(): return lax.ppermute(value, axis, [(i, i ^ step) for i in range(count)])]
    pallas_call x15, Pallas kernels: 6.09 us -> 4.78 us  [call(): pl.pallas_call(ordered, out_shape=outs, in_specs=[*in_specs, *[pl.BlockSp...]
    ppermute x30, starting transfers between devices: 34.5 us -> 33.4 us  [send(): return lax.ppermute(value, axis, [(i, i ^ step) for i in range(count)])]
  transfers between devices with their start and end apart: 30 -> 30, of which waited for: 9 -> 13; matrix products, arithmetic and copies ran while one was open for 0% -> 0% of each run, Pallas kernels for 7% -> 3%
where the time goes in v6:
time: 57.2 us; the launch traced here: 56.8 us
  starting transfers between devices  33.4 us (58%)
  waiting for transfers between devices  17.2 us (30%)
  Pallas kernels  4.78 us (8%)
  between operations  1.4 us (2%)
    ppermute x30, starting transfers between devices, send(): return lax.ppermute(value, axis, [(i, i ^ step) for i in range(count)])  33.4 us
    ppermute x30, waiting for transfers between devices, send(): return lax.ppermute(value, axis, [(i, i ^ step) for i in range(count)])  17.2 us
    pallas_call x15, Pallas kernels, call(): pl.pallas_call(ordered, out_shape=outs, in_specs=[*in_specs, *[pl.BlockSp...  4.78 us
  transfers between devices with their start and end apart: 30, of which 13 were waited for; matrix products, arithmetic and copies ran while one was open for 0% of the time, Pallas kernels for 3%

profile of v6, /device:TPU:0, one launch (start us, length us, event | category | flops | bytes accessed | tf_op | source)
XLA Modules:
  0.0 56.8 jit_solution(5430969519802425688)
XLA Ops:
  1.3 1.8 %start.1 = (bf16[128,128]{1,0:T(8,128)(2,1)S(1)}, bf16[128,128]{1,0:T(8,128)(2,1)S(1)}, f32[1,128]{1,0:T(1,128)S(1)}, f32[128,128]{1,0:T(8,128)S(1)}, bf16[512,1024]{1,0:T(8,128)(2,1)S(1)}) custom-call(s32[1,1,24]{2,1,0:T(1,128)} %refs_0_.4, s32[1,1,24]{2,1,0:T(1,128)} %refs_1_.1, s32[1,128]{1,0:T(1,128)} %bitcast.1, f32[8]{0:T(128)} %refs_3_.1, ...), custom_call_target="tpu_custom_call" | custom-call | bytes 2098404 | tf_op jit(solution)/shard_map/start/pallas_call | solution.py:36
  3.0 3.1 %collective-permute-start = (bf16[128,128]{1,0:T(8,128)(2,1)S(1)}, bf16[128,128]{1,0:T(8,128)(2,1)S(1)}, u32[]{:S(2)}, u32[]{:S(2)}) collective-permute-start(bf16[128,128]{1,0:T(8,128)(2,1)S(1)} %get-tuple-element.35.refs_0_), channel_id=1, source_target_pairs={{0,4},{4,0},{8,12},{12,8},{16,20},{20,16},{24,28},{28,24},{1,5},{5... | collective-permute-start | bytes 98312 | tf_op jit(solution)/shard_map/ppermute | solution.py:205
  6.2 1.5 %collective-permute-start.5 = (bf16[128,128]{1,0:T(8,128)(2,1)S(1)}, bf16[128,128]{1,0:T(8,128)(2,1)S(1)}, u32[]{:S(2)}, u32[]{:S(2)}) collective-permute-start(bf16[128,128]{1,0:T(8,128)(2,1)S(1)} %get-tuple-element.36.refs_1_), channel_id=1, source_target_pairs={{0,2},{1,3},{2,0},{3,1},{4,6},{5,7},{6,4},{7,5},{8,10},{9,11},{10,... | collective-permute-start | bytes 98312 | tf_op jit(solution)/shard_map/ppermute | solution.py:205
  7.7 0.4 collective-permute-start.6
  8.0 0.0 collective-permute-done.refs_1_
  8.1 2.0 %collective-permute-done.5.refs_3_ = bf16[128,128]{1,0:T(8,128)(2,1)S(1)} collective-permute-done((bf16[128,128]{1,0:T(8,128)(2,1)S(1)}, bf16[128,128]{1,0:T(8,128)(2,1)S(1)}, u32[]{:S(2)}, u32[]{:S(2)}) %collective-permute-start.5) | collective-permute-done | bytes 32800 | tf_op jit(solution)/shard_map/ppermute | solution.py:205
  10.1 0.9 %collective-permute-done.6.refs_4_ = bf16[128,128]{1,0:T(8,128)(2,1)S(1)} collective-permute-done((bf16[128,128]{1,0:T(8,128)(2,1)S(1)}, bf16[128,128]{1,0:T(8,128)(2,1)S(1)}, u32[]{:S(2)}, u32[]{:S(2)}) %collective-permute-start.6) | collective-permute-done | bytes 32800 | tf_op jit(solution)/shard_map/ppermute | solution.py:205
  11.0 0.3 adjoint.2
  11.3 0.5 collective-permute-start.8
  11.8 1.6 %collective-permute-start.7 = (f32[2,128,128]{2,1,0:T(8,128)S(1)}, f32[2,128,128]{2,1,0:T(8,128)S(1)}, u32[]{:S(2)}, u32[]{:S(2)}) collective-permute-start(f32[2,128,128]{2,1,0:T(8,128)S(1)} %get-tuple-element.38), channel_id=1, source_target_pairs={{0,4},{4,0},{8,12},{12,8},{16,20},{20,16},{24,28},{28,24},{1,5},{5... | collective-permute-start | bytes 393224 | tf_op jit(solution)/shard_map/ppermute | solution.py:205
  13.4 1.6 %collective-permute-start.1 = (bf16[2,128,128]{2,1,0:T(8,128)(2,1)S(1)}, bf16[2,128,128]{2,1,0:T(8,128)(2,1)S(1)}, u32[]{:S(2)}, u32[]{:S(2)}) collective-permute-start(bf16[2,128,128]{2,1,0:T(8,128)(2,1)S(1)} %pack.2.refs_5_.refs_1_), channel_id=1, source_target_pairs={{0,8},{4,12},{8,0},{12,4},{16,24},{20,28},{24,16},{28,20},{1,9},{5... | collective-permute-start | bytes 196616 | tf_op jit(solution)/shard_map/ppermute | solution.py:205
  15.0 2.4 %collective-permute-start.2 = (bf16[2,128,128]{2,1,0:T(8,128)(2,1)S(1)}, bf16[2,128,128]{2,1,0:T(8,128)(2,1)S(1)}, u32[]{:S(2)}, u32[]{:S(2)}) collective-permute-start(bf16[2,128,128]{2,1,0:T(8,128)(2,1)S(1)} %pack.2.refs_5_.refs_1_), channel_id=1, source_target_pairs={{0,16},{4,20},{8,24},{12,28},{16,0},{20,4},{24,8},{28,12},{1,17},{... | collective-permute-start | bytes 196616 | tf_op jit(solution)/shard_map/ppermute | solution.py:205
  17.5 0.3 collective-permute-start.3
  17.8 2.0 %collective-permute-done.7.refs_1_ = f32[2,128,128]{2,1,0:T(8,128)S(1)} collective-permute-done((f32[2,128,128]{2,1,0:T(8,128)S(1)}, f32[2,128,128]{2,1,0:T(8,128)S(1)}, u32[]{:S(2)}, u32[]{:S(2)}) %collective-permute-start.7) | collective-permute-done | bytes 131104 | tf_op jit(solution)/shard_map/ppermute | solution.py:205
  19.8 2.3 %collective-permute-done.2.refs_3_ = bf16[2,128,128]{2,1,0:T(8,128)(2,1)S(1)} collective-permute-done((bf16[2,128,128]{2,1,0:T(8,128)(2,1)S(1)}, bf16[2,128,128]{2,1,0:T(8,128)(2,1)S(1)}, u32[]{:S(2)}, u32[]{:S(2)}) %collective-permute-start.2) | collective-permute-done | bytes 65568 | tf_op jit(solution)/shard_map/ppermute | solution.py:205
  22.1 1.4 %collective-permute-done.3.refs_4_ = bf16[2,128,128]{2,1,0:T(8,128)(2,1)S(1)} collective-permute-done((bf16[2,128,128]{2,1,0:T(8,128)(2,1)S(1)}, bf16[2,128,128]{2,1,0:T(8,128)(2,1)S(1)}, u32[]{:S(2)}, u32[]{:S(2)}) %collective-permute-start.3) | collective-permute-done | bytes 65568 | tf_op jit(solution)/shard_map/ppermute | solution.py:205
  23.5 0.4 forward.2
  24.0 1.1 %collective-permute-start.10 = (f32[128,128]{1,0:T(8,128)S(1)}, f32[128,128]{1,0:T(8,128)S(1)}, u32[]{:S(2)}, u32[]{:S(2)}) collective-permute-start(f32[128,128]{1,0:T(8,128)S(1)} %get-tuple-element.45), channel_id=1, source_target_pairs={{0,2},{1,3},{2,0},{3,1},{4,6},{5,7},{6,4},{7,5},{8,10},{9,11},{10,... | collective-permute-start | bytes 196616 | tf_op jit(solution)/shard_map/ppermute | solution.py:205
  25.1 1.1 %collective-permute-start.9 = (f32[128,128]{1,0:T(8,128)S(1)}, f32[128,128]{1,0:T(8,128)S(1)}, u32[]{:S(2)}, u32[]{:S(2)}) collective-permute-start(f32[128,128]{1,0:T(8,128)S(1)} %get-tuple-element.44), channel_id=1, source_target_pairs={{0,1},{1,0},{2,3},{3,2},{4,5},{5,4},{6,7},{7,6},{8,9},{9,8},{10,11... | collective-permute-start | bytes 196616 | tf_op jit(solution)/shard_map/ppermute | solution.py:205
  26.2 2.2 %collective-permute-start.16 = (f32[128,128]{1,0:T(8,128)S(1)}, f32[128,128]{1,0:T(8,128)S(1)}, u32[]{:S(2)}, u32[]{:S(2)}) collective-permute-start(f32[128,128]{1,0:T(8,128)S(1)} %get-tuple-element.41.refs_2_), channel_id=1, source_target_pairs={{0,16},{4,20},{8,24},{12,28},{16,0},{20,4},{24,8},{28,12},{1,17},{... | collective-permute-start | bytes 196616 | tf_op jit(solution)/shard_map/ppermute | solution.py:205
  28.4 0.3 collective-permute-done.10.refs_4_
  28.7 1.9 %collective-permute-start.17 = (f32[128,128]{1,0:T(8,128)S(1)}, f32[128,128]{1,0:T(8,128)S(1)}, u32[]{:S(2)}, u32[]{:S(2)}) collective-permute-start(f32[128,128]{1,0:T(8,128)S(1)} %get-tuple-element.49), channel_id=1, source_target_pairs={{0,24},{4,28},{8,16},{12,20},{16,8},{20,12},{24,0},{28,4},{1,25},{... | collective-permute-start | bytes 196616 | tf_op jit(solution)/shard_map/ppermute | solution.py:205
  30.6 0.2 collective-permute-start.12
  30.8 2.3 %collective-permute-start.13 = (bf16[128,128]{1,0:T(8,128)(2,1)S(1)}, bf16[128,128]{1,0:T(8,128)(2,1)S(1)}, u32[]{:S(2)}, u32[]{:S(2)}) collective-permute-start(bf16[128,128]{1,0:T(8,128)(2,1)S(1)} %forward_end.2.refs_5_.refs_0_.refs_1_), channel_id=1, source_target_pairs={{0,16},{4,20},{8,24},{12,28},{16,0},{20,4},{24,8},{28,12},{1,17},{... | collective-permute-start | bytes 98312 | tf_op jit(solution)/shard_map/ppermute | solution.py:205
  33.2 1.9 %collective-permute-start.14 = (bf16[128,128]{1,0:T(8,128)(2,1)S(1)}, bf16[128,128]{1,0:T(8,128)(2,1)S(1)}, u32[]{:S(2)}, u32[]{:S(2)}) collective-permute-start(bf16[128,128]{1,0:T(8,128)(2,1)S(1)} %forward_end.2.refs_5_.refs_0_.refs_1_), channel_id=1, source_target_pairs={{0,24},{4,28},{8,16},{12,20},{16,8},{20,12},{24,0},{28,4},{1,25},{... | collective-permute-start | bytes 98312 | tf_op jit(solution)/shard_map/ppermute | solution.py:205
  35.1 0.1 collective-permute-start.19
  35.2 1.1 %collective-permute-start.20 = (bf16[128,128]{1,0:T(8,128)(2,1)S(1)}, bf16[128,128]{1,0:T(8,128)(2,1)S(1)}, u32[]{:S(2)}, u32[]{:S(2)}) collective-permute-start(bf16[128,128]{1,0:T(8,128)(2,1)S(1)} %get-tuple-element.50.refs_4_.refs_1_), channel_id=1, source_target_pairs={{0,2},{1,3},{2,0},{3,1},{4,6},{5,7},{6,4},{7,5},{8,10},{9,11},{10,... | collective-permute-start | bytes 98312 | tf_op jit(solution)/shard_map/ppermute | solution.py:205
  36.3 0.8 %collective-permute-start.21 = (bf16[128,128]{1,0:T(8,128)(2,1)S(1)}, bf16[128,128]{1,0:T(8,128)(2,1)S(1)}, u32[]{:S(2)}, u32[]{:S(2)}) collective-permute-start(bf16[128,128]{1,0:T(8,128)(2,1)S(1)} %get-tuple-element.50.refs_4_.refs_1_), channel_id=1, source_target_pairs={{0,3},{1,2},{2,1},{3,0},{4,7},{5,6},{6,5},{7,4},{8,11},{9,10},{10,... | collective-permute-start | bytes 98312 | tf_op jit(solution)/shard_map/ppermute | solution.py:205
  37.1 0.6 %collective-permute-done.13.refs_2_.refs_3_ = bf16[128,128]{1,0:T(8,128)(2,1)S(1)} collective-permute-done((bf16[128,128]{1,0:T(8,128)(2,1)S(1)}, bf16[128,128]{1,0:T(8,128)(2,1)S(1)}, u32[]{:S(2)}, u32[]{:S(2)}) %collective-permute-start.13) | collective-permute-done | bytes 32800 | tf_op jit(solution)/shard_map/ppermute | solution.py:205
  37.7 1.2 %collective-permute-done.14.refs_3_.refs_4_ = bf16[128,128]{1,0:T(8,128)(2,1)S(1)} collective-permute-done((bf16[128,128]{1,0:T(8,128)(2,1)S(1)}, bf16[128,128]{1,0:T(8,128)(2,1)S(1)}, u32[]{:S(2)}, u32[]{:S(2)}) %collective-permute-start.14) | collective-permute-done | bytes 32800 | tf_op jit(solution)/shard_map/ppermute | solution.py:205
  38.9 0.7 %collective-permute-start.18 = (bf16[4,128,128]{2,1,0:T(8,128)(2,1)S(1)}, bf16[4,128,128]{2,1,0:T(8,128)(2,1)S(1)}, u32[]{:S(2)}, u32[]{:S(2)}) collective-permute-start(bf16[4,128,128]{2,1,0:T(8,128)(2,1)S(1)} %pack.3), channel_id=1, source_target_pairs={{0,4},{4,0},{8,12},{12,8},{16,20},{20,16},{24,28},{28,24},{1,5},{5... | collective-permute-start | bytes 393224 | tf_op jit(solution)/shard_map/ppermute | solution.py:205
  39.7 0.3 adjoint.3
  40.0 1.4 %collective-permute-start.23 = (bf16[2,128,128]{2,1,0:T(8,128)(2,1)S(1)}, bf16[2,128,128]{2,1,0:T(8,128)(2,1)S(1)}, u32[]{:S(2)}, u32[]{:S(2)}) collective-permute-start(bf16[2,128,128]{2,1,0:T(8,128)(2,1)S(1)} %get-tuple-element.54), channel_id=1, source_target_pairs={{0,4},{4,0},{8,12},{12,8},{16,20},{20,16},{24,28},{28,24},{1,5},{5... | collective-permute-start | bytes 196616 | tf_op jit(solution)/shard_map/ppermute | solution.py:205
  41.4 0.7 %collective-permute-start.22 = (bf16[2,128,128]{2,1,0:T(8,128)(2,1)S(1)}, bf16[2,128,128]{2,1,0:T(8,128)(2,1)S(1)}, u32[]{:S(2)}, u32[]{:S(2)}) collective-permute-start(bf16[2,128,128]{2,1,0:T(8,128)(2,1)S(1)} %get-tuple-element.52), channel_id=1, source_target_pairs={{0,4},{4,0},{8,12},{12,8},{16,20},{20,16},{24,28},{28,24},{1,5},{5... | collective-permute-start | bytes 196616 | tf_op jit(solution)/shard_map/ppermute | solution.py:205
  42.1 4.0 %collective-permute-done.23.refs_1_ = bf16[2,128,128]{2,1,0:T(8,128)(2,1)S(1)} collective-permute-done((bf16[2,128,128]{2,1,0:T(8,128)(2,1)S(1)}, bf16[2,128,128]{2,1,0:T(8,128)(2,1)S(1)}, u32[]{:S(2)}, u32[]{:S(2)}) %collective-permute-start.23) | collective-permute-done | bytes 65568 | tf_op jit(solution)/shard_map/ppermute | solution.py:205
  46.1 0.7 %collective-permute-done.22.refs_1_ = bf16[2,128,128]{2,1,0:T(8,128)(2,1)S(1)} collective-permute-done((bf16[2,128,128]{2,1,0:T(8,128)(2,1)S(1)}, bf16[2,128,128]{2,1,0:T(8,128)(2,1)S(1)}, u32[]{:S(2)}, u32[]{:S(2)}) %collective-permute-start.22) | collective-permute-done | bytes 65568 | tf_op jit(solution)/shard_map/ppermute | solution.py:205
  46.8 1.4 %collective-permute-start.27 = (bf16[128,128]{1,0:T(8,128)(2,1)S(1)}, bf16[128,128]{1,0:T(8,128)(2,1)S(1)}, u32[]{:S(2)}, u32[]{:S(2)}) collective-permute-start(bf16[128,128]{1,0:T(8,128)(2,1)S(1)} %get-tuple-element.62), channel_id=1, source_target_pairs={{0,8},{4,12},{8,0},{12,4},{16,24},{20,28},{24,16},{28,20},{1,9},{5... | collective-permute-start | bytes 98312 | tf_op jit(solution)/shard_map/ppermute | solution.py:205
  48.2 1.3 %collective-permute-start.28 = (bf16[128,128]{1,0:T(8,128)(2,1)S(1)}, bf16[128,128]{1,0:T(8,128)(2,1)S(1)}, u32[]{:S(2)}, u32[]{:S(2)}) collective-permute-start(bf16[128,128]{1,0:T(8,128)(2,1)S(1)} %get-tuple-element.55.refs_2_), channel_id=1, source_target_pairs={{0,16},{4,20},{8,24},{12,28},{16,0},{20,4},{24,8},{28,12},{1,17},{... | collective-permute-start | bytes 98312 | tf_op jit(solution)/shard_map/ppermute | solution.py:205
  49.4 1.8 %collective-permute-start.29 = (bf16[128,128]{1,0:T(8,128)(2,1)S(1)}, bf16[128,128]{1,0:T(8,128)(2,1)S(1)}, u32[]{:S(2)}, u32[]{:S(2)}) collective-permute-start(bf16[128,128]{1,0:T(8,128)(2,1)S(1)} %get-tuple-element.63), channel_id=1, source_target_pairs={{0,24},{4,28},{8,16},{12,20},{16,8},{20,12},{24,0},{28,4},{1,25},{... | collective-permute-start | bytes 98312 | tf_op jit(solution)/shard_map/ppermute | solution.py:205
  51.2 0.4 forward.3
  51.7 0.1 collective-permute-start.24
  51.7 1.1 %collective-permute-start.25 = (bf16[128,128]{1,0:T(8,128)(2,1)S(1)}, bf16[128,128]{1,0:T(8,128)(2,1)S(1)}, u32[]{:S(2)}, u32[]{:S(2)}) collective-permute-start(bf16[128,128]{1,0:T(8,128)(2,1)S(1)} %get-tuple-element.59), channel_id=1, source_target_pairs={{0,2},{1,3},{2,0},{3,1},{4,6},{5,7},{6,4},{7,5},{8,10},{9,11},{10,... | collective-permute-start | bytes 98312 | tf_op jit(solution)/shard_map/ppermute | solution.py:205
  52.8 0.8 %collective-permute-start.26 = (bf16[128,128]{1,0:T(8,128)(2,1)S(1)}, bf16[128,128]{1,0:T(8,128)(2,1)S(1)}, u32[]{:S(2)}, u32[]{:S(2)}) collective-permute-start(bf16[128,128]{1,0:T(8,128)(2,1)S(1)} %get-tuple-element.60), channel_id=1, source_target_pairs={{0,3},{1,2},{2,1},{3,0},{4,7},{5,6},{6,5},{7,4},{8,11},{9,10},{10,... | collective-permute-start | bytes 98312 | tf_op jit(solution)/shard_map/ppermute | solution.py:205
  53.6 0.1 collective-permute-done.28.refs_6_
  53.7 1.4 %collective-permute-done.29.refs_7_ = bf16[128,128]{1,0:T(8,128)(2,1)S(1)} collective-permute-done((bf16[128,128]{1,0:T(8,128)(2,1)S(1)}, bf16[128,128]{1,0:T(8,128)(2,1)S(1)}, u32[]{:S(2)}, u32[]{:S(2)}) %collective-permute-start.29) | collective-permute-done | bytes 32800 | tf_op jit(solution)/shard_map/ppermute | solution.py:205
  55.1 0.7 %adjoint_end.1 = f32[128,128]{1,0:T(8,128)} custom-call(f32[128,128]{1,0:T(8,128)S(1)} %copy-done.1, f32[128,128]{1,0:T(8,128)S(1)} %get-tuple-element.61.refs_1_, f32[1,128]{1,0:T(1,128)S(1)} %get-tuple-element.47.refs_0_.refs_2_, f32[128,128]{1,0:T(8,128)S(1)} %get-tuple-element.33.refs_1_.refs_3_, f32[128,128]{1,0:T(8,128)S(1)} %get-tuple-element.56.refs_6_.refs_4_, ...), custom_call_target="tpu_custom_call" | custom-call | bytes 426496 | tf_op jit(solution)/shard_map/adjoint_end/pallas_call | solution.py:36
  55.9 0.3 collective-permute-done.26.refs_5_
  56.2 0.7 %forward_end.3 = f32[128,128]{1,0:T(8,128)} custom-call(f32[128,128]{1,0:T(8,128)S(1)} %copy-done, f32[128,128]{1,0:T(8,128)S(1)} %get-tuple-element.33.refs_1_.refs_3_, bf16[128,128]{1,0:T(8,128)(2,1)S(1)} %get-tuple-element.57.refs_2_, bf16[128,128]{1,0:T(8,128)(2,1)S(1)} %collective-permute-done.24.refs_3_, ...), custom_call_target="tpu_custom_call" | custom-call | bytes 327680 | tf_op jit(solution)/shard_map/forward_end/pallas_call | solution.py:36
  (31 shorter events, 0.2 us)
Async XLA Ops:
  3.0 5.0 %collective-permute-start = (bf16[128,128]{1,0:T(8,128)(2,1)S(1)}, bf16[128,128]{1,0:T(8,128)(2,1)S(1)}, u32[]{:S(2)}, u32[]{:S(2)}) collective-permute-start(bf16[128,128]{1,0:T(8,128)(2,1)S(1)} %get-tuple-element.35.refs_0_), channel_id=1, source_target_pairs={{0,4},{4,0},{8,12},{12,8},{16,20},{20,16},{24,28},{28,24},{1,5},{5... | collective-permute-start | bytes 98312 | tf_op jit(solution)/shard_map/ppermute | solution.py:205
  6.2 1.9 %collective-permute-start.4 = (bf16[128,128]{1,0:T(8,128)(2,1)S(1)}, bf16[128,128]{1,0:T(8,128)(2,1)S(1)}, u32[]{:S(2)}, u32[]{:S(2)}) collective-permute-start(bf16[128,128]{1,0:T(8,128)(2,1)S(1)} %get-tuple-element.36.refs_1_), channel_id=1, source_target_pairs={{0,1},{1,0},{2,3},{3,2},{4,5},{5,4},{6,7},{7,6},{8,9},{9,8},{10,11... | collective-permute-start | bytes 98312 | tf_op jit(solution)/shard_map/ppermute | solution.py:205
  6.2 3.9 %collective-permute-start.5 = (bf16[128,128]{1,0:T(8,128)(2,1)S(1)}, bf16[128,128]{1,0:T(8,128)(2,1)S(1)}, u32[]{:S(2)}, u32[]{:S(2)}) collective-permute-start(bf16[128,128]{1,0:T(8,128)(2,1)S(1)} %get-tuple-element.36.refs_1_), channel_id=1, source_target_pairs={{0,2},{1,3},{2,0},{3,1},{4,6},{5,7},{6,4},{7,5},{8,10},{9,11},{10,... | collective-permute-start | bytes 98312 | tf_op jit(solution)/shard_map/ppermute | solution.py:205
  7.7 3.3 %collective-permute-start.6 = (bf16[128,128]{1,0:T(8,128)(2,1)S(1)}, bf16[128,128]{1,0:T(8,128)(2,1)S(1)}, u32[]{:S(2)}, u32[]{:S(2)}) collective-permute-start(bf16[128,128]{1,0:T(8,128)(2,1)S(1)} %get-tuple-element.36.refs_1_), channel_id=1, source_target_pairs={{0,3},{1,2},{2,1},{3,0},{4,7},{5,6},{6,5},{7,4},{8,11},{9,10},{10,... | collective-permute-start | bytes 98312 | tf_op jit(solution)/shard_map/ppermute | solution.py:205
  11.3 6.5 %collective-permute-start.8 = (f32[2,128,128]{2,1,0:T(8,128)S(1)}, f32[2,128,128]{2,1,0:T(8,128)S(1)}, u32[]{:S(2)}, u32[]{:S(2)}) collective-permute-start(f32[2,128,128]{2,1,0:T(8,128)S(1)} %get-tuple-element.40), channel_id=1, source_target_pairs={{0,4},{4,0},{8,12},{12,8},{16,20},{20,16},{24,28},{28,24},{1,5},{5... | collective-permute-start | bytes 393224 | tf_op jit(solution)/shard_map/ppermute | solution.py:205
  11.8 8.0 %collective-permute-start.7 = (f32[2,128,128]{2,1,0:T(8,128)S(1)}, f32[2,128,128]{2,1,0:T(8,128)S(1)}, u32[]{:S(2)}, u32[]{:S(2)}) collective-permute-start(f32[2,128,128]{2,1,0:T(8,128)S(1)} %get-tuple-element.38), channel_id=1, source_target_pairs={{0,4},{4,0},{8,12},{12,8},{16,20},{20,16},{24,28},{28,24},{1,5},{5... | collective-permute-start | bytes 393224 | tf_op jit(solution)/shard_map/ppermute | solution.py:205
  13.4 6.4 %collective-permute-start.1 = (bf16[2,128,128]{2,1,0:T(8,128)(2,1)S(1)}, bf16[2,128,128]{2,1,0:T(8,128)(2,1)S(1)}, u32[]{:S(2)}, u32[]{:S(2)}) collective-permute-start(bf16[2,128,128]{2,1,0:T(8,128)(2,1)S(1)} %pack.2.refs_5_.refs_1_), channel_id=1, source_target_pairs={{0,8},{4,12},{8,0},{12,4},{16,24},{20,28},{24,16},{28,20},{1,9},{5... | collective-permute-start | bytes 196616 | tf_op jit(solution)/shard_map/ppermute | solution.py:205
  15.0 7.1 %collective-permute-start.2 = (bf16[2,128,128]{2,1,0:T(8,128)(2,1)S(1)}, bf16[2,128,128]{2,1,0:T(8,128)(2,1)S(1)}, u32[]{:S(2)}, u32[]{:S(2)}) collective-permute-start(bf16[2,128,128]{2,1,0:T(8,128)(2,1)S(1)} %pack.2.refs_5_.refs_1_), channel_id=1, source_target_pairs={{0,16},{4,20},{8,24},{12,28},{16,0},{20,4},{24,8},{28,12},{1,17},{... | collective-permute-start | bytes 196616 | tf_op jit(solution)/shard_map/ppermute | solution.py:205
  17.5 6.1 %collective-permute-start.3 = (bf16[2,128,128]{2,1,0:T(8,128)(2,1)S(1)}, bf16[2,128,128]{2,1,0:T(8,128)(2,1)S(1)}, u32[]{:S(2)}, u32[]{:S(2)}) collective-permute-start(bf16[2,128,128]{2,1,0:T(8,128)(2,1)S(1)} %pack.2.refs_5_.refs_1_), channel_id=1, source_target_pairs={{0,24},{4,28},{8,16},{12,20},{16,8},{20,12},{24,0},{28,4},{1,25},{... | collective-permute-start | bytes 196616 | tf_op jit(solution)/shard_map/ppermute | solution.py:205
  23.5 7.1 %copy-start = (f32[128,128]{1,0:T(8,128)S(1)}, f32[128,128]{1,0:T(8,128)}, u32[]{:S(2)}) copy-start(f32[128,128]{1,0:T(8,128)} %refs_0_.6) | copy-start | bytes 196612
  24.0 4.7 %collective-permute-start.10 = (f32[128,128]{1,0:T(8,128)S(1)}, f32[128,128]{1,0:T(8,128)S(1)}, u32[]{:S(2)}, u32[]{:S(2)}) collective-permute-start(f32[128,128]{1,0:T(8,128)S(1)} %get-tuple-element.45), channel_id=1, source_target_pairs={{0,2},{1,3},{2,0},{3,1},{4,6},{5,7},{6,4},{7,5},{8,10},{9,11},{10,... | collective-permute-start | bytes 196616 | tf_op jit(solution)/shard_map/ppermute | solution.py:205
  25.1 5.5 %collective-permute-start.11 = (f32[128,128]{1,0:T(8,128)S(1)}, f32[128,128]{1,0:T(8,128)S(1)}, u32[]{:S(2)}, u32[]{:S(2)}) collective-permute-start(f32[128,128]{1,0:T(8,128)S(1)} %get-tuple-element.46), channel_id=1, source_target_pairs={{0,3},{1,2},{2,1},{3,0},{4,7},{5,6},{6,5},{7,4},{8,11},{9,10},{10,... | collective-permute-start | bytes 196616 | tf_op jit(solution)/shard_map/ppermute | solution.py:205
  25.1 5.5 %collective-permute-start.9 = (f32[128,128]{1,0:T(8,128)S(1)}, f32[128,128]{1,0:T(8,128)S(1)}, u32[]{:S(2)}, u32[]{:S(2)}) collective-permute-start(f32[128,128]{1,0:T(8,128)S(1)} %get-tuple-element.44), channel_id=1, source_target_pairs={{0,1},{1,0},{2,3},{3,2},{4,5},{5,4},{6,7},{7,6},{8,9},{9,8},{10,11... | collective-permute-start | bytes 196616 | tf_op jit(solution)/shard_map/ppermute | solution.py:205
  26.2 7.0 %collective-permute-start.15 = (f32[128,128]{1,0:T(8,128)S(1)}, f32[128,128]{1,0:T(8,128)S(1)}, u32[]{:S(2)}, u32[]{:S(2)}) collective-permute-start(f32[128,128]{1,0:T(8,128)S(1)} %get-tuple-element.48), channel_id=1, source_target_pairs={{0,8},{4,12},{8,0},{12,4},{16,24},{20,28},{24,16},{28,20},{1,9},{5... | collective-permute-start | bytes 196616 | tf_op jit(solution)/shard_map/ppermute | solution.py:205
  26.2 8.9 %collective-permute-start.16 = (f32[128,128]{1,0:T(8,128)S(1)}, f32[128,128]{1,0:T(8,128)S(1)}, u32[]{:S(2)}, u32[]{:S(2)}) collective-permute-start(f32[128,128]{1,0:T(8,128)S(1)} %get-tuple-element.41.refs_2_), channel_id=1, source_target_pairs={{0,16},{4,20},{8,24},{12,28},{16,0},{20,4},{24,8},{28,12},{1,17},{... | collective-permute-start | bytes 196616 | tf_op jit(solution)/shard_map/ppermute | solution.py:205
  28.7 6.4 %collective-permute-start.17 = (f32[128,128]{1,0:T(8,128)S(1)}, f32[128,128]{1,0:T(8,128)S(1)}, u32[]{:S(2)}, u32[]{:S(2)}) collective-permute-start(f32[128,128]{1,0:T(8,128)S(1)} %get-tuple-element.49), channel_id=1, source_target_pairs={{0,24},{4,28},{8,16},{12,20},{16,8},{20,12},{24,0},{28,4},{1,25},{... | collective-permute-start | bytes 196616 | tf_op jit(solution)/shard_map/ppermute | solution.py:205
  30.6 5.6 %collective-permute-start.12 = (bf16[128,128]{1,0:T(8,128)(2,1)S(1)}, bf16[128,128]{1,0:T(8,128)(2,1)S(1)}, u32[]{:S(2)}, u32[]{:S(2)}) collective-permute-start(bf16[128,128]{1,0:T(8,128)(2,1)S(1)} %forward_end.2.refs_5_.refs_0_.refs_1_), channel_id=1, source_target_pairs={{0,8},{4,12},{8,0},{12,4},{16,24},{20,28},{24,16},{28,20},{1,9},{5... | collective-permute-start | bytes 98312 | tf_op jit(solution)/shard_map/ppermute | solution.py:205
  30.8 6.9 %collective-permute-start.13 = (bf16[128,128]{1,0:T(8,128)(2,1)S(1)}, bf16[128,128]{1,0:T(8,128)(2,1)S(1)}, u32[]{:S(2)}, u32[]{:S(2)}) collective-permute-start(bf16[128,128]{1,0:T(8,128)(2,1)S(1)} %forward_end.2.refs_5_.refs_0_.refs_1_), channel_id=1, source_target_pairs={{0,16},{4,20},{8,24},{12,28},{16,0},{20,4},{24,8},{28,12},{1,17},{... | collective-permute-start | bytes 98312 | tf_op jit(solution)/shard_map/ppermute | solution.py:205
  33.2 5.7 %collective-permute-start.14 = (bf16[128,128]{1,0:T(8,128)(2,1)S(1)}, bf16[128,128]{1,0:T(8,128)(2,1)S(1)}, u32[]{:S(2)}, u32[]{:S(2)}) collective-permute-start(bf16[128,128]{1,0:T(8,128)(2,1)S(1)} %forward_end.2.refs_5_.refs_0_.refs_1_), channel_id=1, source_target_pairs={{0,24},{4,28},{8,16},{12,20},{16,8},{20,12},{24,0},{28,4},{1,25},{... | collective-permute-start | bytes 98312 | tf_op jit(solution)/shard_map/ppermute | solution.py:205
  35.1 4.5 %collective-permute-start.19 = (bf16[128,128]{1,0:T(8,128)(2,1)S(1)}, bf16[128,128]{1,0:T(8,128)(2,1)S(1)}, u32[]{:S(2)}, u32[]{:S(2)}) collective-permute-start(bf16[128,128]{1,0:T(8,128)(2,1)S(1)} %get-tuple-element.50.refs_4_.refs_1_), channel_id=1, source_target_pairs={{0,1},{1,0},{2,3},{3,2},{4,5},{5,4},{6,7},{7,6},{8,9},{9,8},{10,11... | collective-permute-start | bytes 98312 | tf_op jit(solution)/shard_map/ppermute | solution.py:205
  35.2 4.4 %collective-permute-start.20 = (bf16[128,128]{1,0:T(8,128)(2,1)S(1)}, bf16[128,128]{1,0:T(8,128)(2,1)S(1)}, u32[]{:S(2)}, u32[]{:S(2)}) collective-permute-start(bf16[128,128]{1,0:T(8,128)(2,1)S(1)} %get-tuple-element.50.refs_4_.refs_1_), channel_id=1, source_target_pairs={{0,2},{1,3},{2,0},{3,1},{4,6},{5,7},{6,4},{7,5},{8,10},{9,11},{10,... | collective-permute-start | bytes 98312 | tf_op jit(solution)/shard_map/ppermute | solution.py:205
  36.3 3.4 %collective-permute-start.21 = (bf16[128,128]{1,0:T(8,128)(2,1)S(1)}, bf16[128,128]{1,0:T(8,128)(2,1)S(1)}, u32[]{:S(2)}, u32[]{:S(2)}) collective-permute-start(bf16[128,128]{1,0:T(8,128)(2,1)S(1)} %get-tuple-element.50.refs_4_.refs_1_), channel_id=1, source_target_pairs={{0,3},{1,2},{2,1},{3,0},{4,7},{5,6},{6,5},{7,4},{8,11},{9,10},{10,... | collective-permute-start | bytes 98312 | tf_op jit(solution)/shard_map/ppermute | solution.py:205
  38.9 12.3 %collective-permute-start.18 = (bf16[4,128,128]{2,1,0:T(8,128)(2,1)S(1)}, bf16[4,128,128]{2,1,0:T(8,128)(2,1)S(1)}, u32[]{:S(2)}, u32[]{:S(2)}) collective-permute-start(bf16[4,128,128]{2,1,0:T(8,128)(2,1)S(1)} %pack.3), channel_id=1, source_target_pairs={{0,4},{4,0},{8,12},{12,8},{16,20},{20,16},{24,28},{28,24},{1,5},{5... | collective-permute-start | bytes 393224 | tf_op jit(solution)/shard_map/ppermute | solution.py:205
  40.0 6.1 %collective-permute-start.23 = (bf16[2,128,128]{2,1,0:T(8,128)(2,1)S(1)}, bf16[2,128,128]{2,1,0:T(8,128)(2,1)S(1)}, u32[]{:S(2)}, u32[]{:S(2)}) collective-permute-start(bf16[2,128,128]{2,1,0:T(8,128)(2,1)S(1)} %get-tuple-element.54), channel_id=1, source_target_pairs={{0,4},{4,0},{8,12},{12,8},{16,20},{20,16},{24,28},{28,24},{1,5},{5... | collective-permute-start | bytes 196616 | tf_op jit(solution)/shard_map/ppermute | solution.py:205
  41.4 5.4 %collective-permute-start.22 = (bf16[2,128,128]{2,1,0:T(8,128)(2,1)S(1)}, bf16[2,128,128]{2,1,0:T(8,128)(2,1)S(1)}, u32[]{:S(2)}, u32[]{:S(2)}) collective-permute-start(bf16[2,128,128]{2,1,0:T(8,128)(2,1)S(1)} %get-tuple-element.52), channel_id=1, source_target_pairs={{0,4},{4,0},{8,12},{12,8},{16,20},{20,16},{24,28},{28,24},{1,5},{5... | collective-permute-start | bytes 196616 | tf_op jit(solution)/shard_map/ppermute | solution.py:205
  46.8 6.0 %collective-permute-start.27 = (bf16[128,128]{1,0:T(8,128)(2,1)S(1)}, bf16[128,128]{1,0:T(8,128)(2,1)S(1)}, u32[]{:S(2)}, u32[]{:S(2)}) collective-permute-start(bf16[128,128]{1,0:T(8,128)(2,1)S(1)} %get-tuple-element.62), channel_id=1, source_target_pairs={{0,8},{4,12},{8,0},{12,4},{16,24},{20,28},{24,16},{28,20},{1,9},{5... | collective-permute-start | bytes 98312 | tf_op jit(solution)/shard_map/ppermute | solution.py:205
  48.2 5.6 %collective-permute-start.28 = (bf16[128,128]{1,0:T(8,128)(2,1)S(1)}, bf16[128,128]{1,0:T(8,128)(2,1)S(1)}, u32[]{:S(2)}, u32[]{:S(2)}) collective-permute-start(bf16[128,128]{1,0:T(8,128)(2,1)S(1)} %get-tuple-element.55.refs_2_), channel_id=1, source_target_pairs={{0,16},{4,20},{8,24},{12,28},{16,0},{20,4},{24,8},{28,12},{1,17},{... | collective-permute-start | bytes 98312 | tf_op jit(solution)/shard_map/ppermute | solution.py:205
  49.4 5.7 %collective-permute-start.29 = (bf16[128,128]{1,0:T(8,128)(2,1)S(1)}, bf16[128,128]{1,0:T(8,128)(2,1)S(1)}, u32[]{:S(2)}, u32[]{:S(2)}) collective-permute-start(bf16[128,128]{1,0:T(8,128)(2,1)S(1)} %get-tuple-element.63), channel_id=1, source_target_pairs={{0,24},{4,28},{8,16},{12,20},{16,8},{20,12},{24,0},{28,4},{1,25},{... | collective-permute-start | bytes 98312 | tf_op jit(solution)/shard_map/ppermute | solution.py:205
  51.2 3.9 %copy-start.1 = (f32[128,128]{1,0:T(8,128)S(1)}, f32[128,128]{1,0:T(8,128)}, u32[]{:S(2)}) copy-start(f32[128,128]{1,0:T(8,128)} %refs_0_.7) | copy-start | bytes 196612
  51.7 4.2 %collective-permute-start.24 = (bf16[128,128]{1,0:T(8,128)(2,1)S(1)}, bf16[128,128]{1,0:T(8,128)(2,1)S(1)}, u32[]{:S(2)}, u32[]{:S(2)}) collective-permute-start(bf16[128,128]{1,0:T(8,128)(2,1)S(1)} %get-tuple-element.58), channel_id=1, source_target_pairs={{0,1},{1,0},{2,3},{3,2},{4,5},{5,4},{6,7},{7,6},{8,9},{9,8},{10,11... | collective-permute-start | bytes 98312 | tf_op jit(solution)/shard_map/ppermute | solution.py:205
  51.7 4.1 %collective-permute-start.25 = (bf16[128,128]{1,0:T(8,128)(2,1)S(1)}, bf16[128,128]{1,0:T(8,128)(2,1)S(1)}, u32[]{:S(2)}, u32[]{:S(2)}) collective-permute-start(bf16[128,128]{1,0:T(8,128)(2,1)S(1)} %get-tuple-element.59), channel_id=1, source_target_pairs={{0,2},{1,3},{2,0},{3,1},{4,6},{5,7},{6,4},{7,5},{8,10},{9,11},{10,... | collective-permute-start | bytes 98312 | tf_op jit(solution)/shard_map/ppermute | solution.py:205
  52.8 3.3 %collective-permute-start.26 = (bf16[128,128]{1,0:T(8,128)(2,1)S(1)}, bf16[128,128]{1,0:T(8,128)(2,1)S(1)}, u32[]{:S(2)}, u32[]{:S(2)}) collective-permute-start(bf16[128,128]{1,0:T(8,128)(2,1)S(1)} %get-tuple-element.60), channel_id=1, source_target_pairs={{0,3},{1,2},{2,1},{3,0},{4,7},{5,6},{6,5},{7,4},{8,11},{9,10},{10,... | collective-permute-start | bytes 98312 | tf_op jit(solution)/shard_map/ppermute | solution.py:205

commit v7 on v5

--- a/solution.py
+++ b/solution.py
@@ -141,8 +141,8 @@
 
 
 def adjoint_body(n_rows, n_cols, dense_ref, *refs):
-    blocks, refs = refs[:n_cols], refs[n_cols:]
-    *pair, send_far, send_near, keep_far, keep_near = refs
+    blocks, outs = refs[:n_cols], refs[n_cols:]
+    send_far, send_near, keep_far, keep_near = outs
     half = n_rows // 2
     near = send_near.shape[0]
     size = blocks[0].shape[1]
@@ -156,10 +156,6 @@
         )
         keep[at] = part[:, :size]
         send[at] = part[:, size:].astype(send.dtype)
-    if pair:
-        own, other, both = pair
-        both[0] = own[...]
-        both[1] = other[...]
 
 
 def add_body(keep_ref, got_ref, *outs):
@@ -173,16 +169,12 @@
         out_ref[at] = part[...]
 
 
-def forward_body(half, n_cols, paired, dense_ref, *refs):
-    count = half if paired else half + 1
-    panels, outs = refs[:count], refs[count:]
-    size = panels[0].shape[-1]
+def forward_body(half, n_cols, dense_ref, *refs):
+    panels, other_ref, outs = refs[:half], refs[half], refs[half + 1 :]
+    size = other_ref.shape[-1]
     total = None
     for zz in range(half):
-        if paired:
-            panel = jnp.concatenate([panels[zz][0], panels[zz][1]], axis=0)
-        else:
-            panel = jnp.concatenate([panels[zz][...], panels[half][zz]], axis=0)
+        panel = jnp.concatenate([panels[zz][...], other_ref[zz]], axis=0)
         part = jnp.dot(
             dense_ref[:, 2 * zz * size : (2 * zz + 2) * size], panel, preferred_element_type=F32
         )
@@ -269,15 +261,14 @@
     def add(keep, got, kinds, name):
         return call(add_body, [shape(kind) for kind in kinds], [vmem()] * 2, (keep, got), 0, name)
 
-    def adjoint_hop(part, kind, pair):
+    def adjoint_hop(part, kind):
         blocks = [part] + [send(part, "cols", n_cols, s) for s in range(1, n_cols)]
-        *both, send_far, send_near, keep_far, keep_near = call(
+        send_far, send_near, keep_far, keep_near = call(
             lambda *refs: adjoint_body(n_rows, n_cols, *refs),
-            [shape(BF16, 2)] * (len(pair) // 2)
-            + [shape(kind, half - near), shape(kind, near)]
+            [shape(kind, half - near), shape(kind, near)]
             + [shape(F32, half - near), shape(F32, near)],
-            [vmem()] * (1 + n_cols + len(pair)),
-            [dense, *blocks, *pair],
+            [vmem()] * (1 + n_cols),
+            [dense, *blocks],
             hop_flops,
             "adjoint",
         )
@@ -286,17 +277,14 @@
         kinds = [F32] + [kind] * (near - 1)
         close = add(keep_near, send(send_near, "rows", n_rows, 1), kinds, "add_near")
         close = [close[0]] + [send(close[s], "rows", n_rows, 2 * s) for s in range(1, near)]
-        return close + far, both
-
-    def forward_hop(part, kind, paired, after):
+        return close + far, blocks
+
+    def forward_hop(part, kind, after):
         panels = [part] + [send(part, "rows", n_rows, 2 * s) for s in range(1, half)]
-        if not paired:
-            (packed,) = call(
-                pack_body, [shape(BF16, half)], [vmem()] * half, panels, 0, "pack"
-            )
-            panels = panels + [send(packed, "rows", n_rows, 1)]
+        (packed,) = call(pack_body, [shape(BF16, half)], [vmem()] * half, panels, 0, "pack")
+        panels = panels + [send(packed, "rows", n_rows, 1)]
         sums = call(
-            lambda *refs: forward_body(half, n_cols, paired, *refs),
+            lambda *refs: forward_body(half, n_cols, *refs),
             [shape(kind)] * n_cols,
             [vmem()] * (1 + len(panels)),
             [dense, *panels],
@@ -317,8 +305,8 @@
             after=after,
         )[0]
 
-    back, (both,) = adjoint_hop(q0, F32, [p0, send(p0, "rows", n_rows, 1)])
-    first = forward_hop(both, F32, True, back[:1])
+    back, _ = adjoint_hop(q0, F32)
+    first = forward_hop(p0, F32, back[:1])
     d1, q1 = call(
         adjoint_mid_body,
         [shape(F32), shape(BF16)],
@@ -327,9 +315,9 @@
         0,
         "adjoint_mid",
     )
-    p1 = forward_end(first, BF16, [d1])
-    back_two, _ = adjoint_hop(q1, BF16, [])
-    second = forward_hop(p1, BF16, False, back_two[:1])
+    back_two, blocks = adjoint_hop(q1, BF16)
+    p1 = forward_end(first, BF16, blocks[1:])
+    second = forward_hop(p1, BF16, back_two[:1])
     propagated = forward_end(second, F32)
     (input_grad,) = call(
         adjoint_end_body,

time: 56.1 us -> 57 us (1.016)
  waiting for transfers between devices: 13.8 us -> 16.5 us
  starting transfers between devices: 34.5 us -> 32.6 us
    ppermute x30, waiting for transfers between devices: 13.8 us -> 16.5 us  [send(): return lax.ppermute(value, axis, [(i, i ^ step) for i in range(count)])]
    ppermute x30, starting transfers between devices: 34.5 us -> 32.6 us  [send(): return lax.ppermute(value, axis, [(i, i ^ step) for i in range(count)])]
    pallas_call x15 -> x16, Pallas kernels: 6.09 us -> 6.09 us  [call(): pl.pallas_call(ordered, out_shape=outs, in_specs=[*in_specs, *[pl.BlockSp...]
  transfers between devices with their start and end apart: 30 -> 30, of which waited for: 9 -> 12; matrix products, arithmetic and copies ran while one was open for 0% -> 0% of each run, Pallas kernels for 7% -> 8%
where the time goes in v7:
time: 57 us; the launch traced here: 56.7 us
  starting transfers between devices  32.6 us (57%)
  waiting for transfers between devices  16.5 us (29%)
  Pallas kernels  6.09 us (11%)
  between operations  1.44 us (3%)
    ppermute x30, starting transfers between devices, send(): return lax.ppermute(value, axis, [(i, i ^ step) for i in range(count)])  32.6 us
    ppermute x30, waiting for transfers between devices, send(): return lax.ppermute(value, axis, [(i, i ^ step) for i in range(count)])  16.5 us
    pallas_call x16, Pallas kernels, call(): pl.pallas_call(ordered, out_shape=outs, in_specs=[*in_specs, *[pl.BlockSp...  6.09 us
  transfers between devices with their start and end apart: 30, of which 12 were waited for; matrix products, arithmetic and copies ran while one was open for 0% of the time, Pallas kernels for 8%

profile of v7, /device:TPU:0, one launch (start us, length us, event | category | flops | bytes accessed | tf_op | source)
XLA Modules:
  0.0 56.7 jit_solution(2275007152462274581)
XLA Ops:
  0.6 1.0 %start.1 = (bf16[128,128]{1,0:T(8,128)(2,1)S(1)}, bf16[128,128]{1,0:T(8,128)(2,1)S(1)}, f32[1,128]{1,0:T(1,128)S(1)}, f32[128,128]{1,0:T(8,128)S(1)}) custom-call(f32[128,128]{1,0:T(8,128)} %refs_0_.7, f32[128,128]{1,0:T(8,128)} %refs_0_.6, s32[1,128]{1,0:T(1,128)} %bitcast.1, f32[8]{0:T(128)} %refs_3_.2), custom_call_target="tpu_custom_call" | custom-call | bytes 263200 | tf_op jit(solution)/shard_map/start/pallas_call | solution.py:36
  1.7 0.5 collective-permute-start.4
  2.2 2.6 %collective-permute-start.5 = (bf16[128,128]{1,0:T(8,128)(2,1)S(1)}, bf16[128,128]{1,0:T(8,128)(2,1)S(1)}, u32[]{:S(2)}, u32[]{:S(2)}) collective-permute-start(bf16[128,128]{1,0:T(8,128)(2,1)S(1)} %get-tuple-element.33.refs_0_.refs_1_), channel_id=1, source_target_pairs={{0,2},{1,3},{2,0},{3,1},{4,6},{5,7},{6,4},{7,5},{8,10},{9,11},{10,... | collective-permute-start | bytes 98312 | tf_op jit(solution)/shard_map/ppermute | solution.py:214
  4.8 1.8 %collective-permute-start = (bf16[128,128]{1,0:T(8,128)(2,1)S(1)}, bf16[128,128]{1,0:T(8,128)(2,1)S(1)}, u32[]{:S(2)}, u32[]{:S(2)}) collective-permute-start(bf16[128,128]{1,0:T(8,128)(2,1)S(1)} %get-tuple-element.34.refs_0_.refs_1_), channel_id=1, source_target_pairs={{0,8},{4,12},{8,0},{12,4},{16,24},{20,28},{24,16},{28,20},{1,9},{5... | collective-permute-start | bytes 98312 | tf_op jit(solution)/shard_map/ppermute | solution.py:214
  6.6 2.6 %collective-permute-start.1 = (bf16[128,128]{1,0:T(8,128)(2,1)S(1)}, bf16[128,128]{1,0:T(8,128)(2,1)S(1)}, u32[]{:S(2)}, u32[]{:S(2)}) collective-permute-start(bf16[128,128]{1,0:T(8,128)(2,1)S(1)} %get-tuple-element.34.refs_0_.refs_1_), channel_id=1, source_target_pairs={{0,16},{4,20},{8,24},{12,28},{16,0},{20,4},{24,8},{28,12},{1,17},{... | collective-permute-start | bytes 98312 | tf_op jit(solution)/shard_map/ppermute | solution.py:214
  9.9 2.0 %dense.1.refs_0_ = bf16[512,1024]{1,0:T(8,128)(2,1)S(1)} custom-call(bf16[128,128]{1,0:T(8,128)(2,1)S(1)} %get-tuple-element.33.refs_0_.refs_1_, bf16[1,1,24,128,128]{4,3,2,1,0:T(8,128)(2,1)} %refs_1_.3, s32[1,1,24]{2,1,0:T(1,128)} %refs_2_.1, s32[1,1,24]{2,1,0:T(1,128)} %refs_3_.3, s32[1,1]{1,0:T(1,128)S(6)} %copy.10.refs_4_), custom_call_target="tpu_custom_call" | custom-call | bytes 1867972 | tf_op jit(solution)/shard_map/dense/pallas_call | solution.py:36
  11.9 0.1 collective-permute-start.2
  12.0 0.3 adjoint.2
  12.3 1.6 %collective-permute-start.12 = (f32[2,128,128]{2,1,0:T(8,128)S(1)}, f32[2,128,128]{2,1,0:T(8,128)S(1)}, u32[]{:S(2)}, u32[]{:S(2)}) collective-permute-start(f32[2,128,128]{2,1,0:T(8,128)S(1)} %get-tuple-element.45), channel_id=1, source_target_pairs={{0,4},{4,0},{8,12},{12,8},{16,20},{20,16},{24,28},{28,24},{1,5},{5... | collective-permute-start | bytes 393224 | tf_op jit(solution)/shard_map/ppermute | solution.py:214
  13.9 0.5 collective-permute-start.7
  14.4 3.3 %collective-permute-done.2.refs_3_.refs_4_ = bf16[128,128]{1,0:T(8,128)(2,1)S(1)} collective-permute-done((bf16[128,128]{1,0:T(8,128)(2,1)S(1)}, bf16[128,128]{1,0:T(8,128)(2,1)S(1)}, u32[]{:S(2)}, u32[]{:S(2)}) %collective-permute-start.2) | collective-permute-done | bytes 32800 | tf_op jit(solution)/shard_map/ppermute | solution.py:214
  17.7 1.3 %collective-permute-start.3 = (bf16[4,128,128]{2,1,0:T(8,128)(2,1)S(1)}, bf16[4,128,128]{2,1,0:T(8,128)(2,1)S(1)}, u32[]{:S(2)}, u32[]{:S(2)}) collective-permute-start(bf16[4,128,128]{2,1,0:T(8,128)(2,1)S(1)} %pack.2), channel_id=1, source_target_pairs={{0,4},{4,0},{8,12},{12,8},{16,20},{20,16},{24,28},{28,24},{1,5},{5... | collective-permute-start | bytes 393224 | tf_op jit(solution)/shard_map/ppermute | solution.py:214
  19.0 1.5 %collective-permute-start.13 = (f32[128,128]{1,0:T(8,128)S(1)}, f32[128,128]{1,0:T(8,128)S(1)}, u32[]{:S(2)}, u32[]{:S(2)}) collective-permute-start(f32[128,128]{1,0:T(8,128)S(1)} %get-tuple-element.46), channel_id=1, source_target_pairs={{0,16},{4,20},{8,24},{12,28},{16,0},{20,4},{24,8},{28,12},{1,17},{... | collective-permute-start | bytes 196616 | tf_op jit(solution)/shard_map/ppermute | solution.py:214
  20.5 2.3 %collective-permute-start.14 = (f32[128,128]{1,0:T(8,128)S(1)}, f32[128,128]{1,0:T(8,128)S(1)}, u32[]{:S(2)}, u32[]{:S(2)}) collective-permute-start(f32[128,128]{1,0:T(8,128)S(1)} %get-tuple-element.47), channel_id=1, source_target_pairs={{0,24},{4,28},{8,16},{12,20},{16,8},{20,12},{24,0},{28,4},{1,25},{... | collective-permute-start | bytes 196616 | tf_op jit(solution)/shard_map/ppermute | solution.py:214
  22.8 0.6 collective-permute-start.11
  23.4 0.4 forward.2
  23.8 0.1 collective-permute-start.10
  23.9 1.6 %collective-permute-start.8 = (f32[128,128]{1,0:T(8,128)S(1)}, f32[128,128]{1,0:T(8,128)S(1)}, u32[]{:S(2)}, u32[]{:S(2)}) collective-permute-start(f32[128,128]{1,0:T(8,128)S(1)} %get-tuple-element.39), channel_id=1, source_target_pairs={{0,1},{1,0},{2,3},{3,2},{4,5},{5,4},{6,7},{7,6},{8,9},{9,8},{10,11... | collective-permute-start | bytes 196616 | tf_op jit(solution)/shard_map/ppermute | solution.py:214
  25.5 0.5 collective-permute-start.9
  26.0 0.6 %collective-permute-done.14.refs_4_ = f32[128,128]{1,0:T(8,128)S(1)} collective-permute-done((f32[128,128]{1,0:T(8,128)S(1)}, f32[128,128]{1,0:T(8,128)S(1)}, u32[]{:S(2)}, u32[]{:S(2)}) %collective-permute-start.14) | collective-permute-done | bytes 65568 | tf_op jit(solution)/shard_map/ppermute | solution.py:214
  26.7 0.6 %collective-permute-done.11.refs_2_ = f32[128,128]{1,0:T(8,128)S(1)} collective-permute-done((f32[128,128]{1,0:T(8,128)S(1)}, f32[128,128]{1,0:T(8,128)S(1)}, u32[]{:S(2)}, u32[]{:S(2)}) %collective-permute-start.11) | collective-permute-done | bytes 65568 | tf_op jit(solution)/shard_map/ppermute | solution.py:214
  27.4 1.6 %collective-permute-start.16 = (bf16[128,128]{1,0:T(8,128)(2,1)S(1)}, bf16[128,128]{1,0:T(8,128)(2,1)S(1)}, u32[]{:S(2)}, u32[]{:S(2)}) collective-permute-start(bf16[128,128]{1,0:T(8,128)(2,1)S(1)} %get-tuple-element.48.refs_1_), channel_id=1, source_target_pairs={{0,2},{1,3},{2,0},{3,1},{4,6},{5,7},{6,4},{7,5},{8,10},{9,11},{10,... | collective-permute-start | bytes 98312 | tf_op jit(solution)/shard_map/ppermute | solution.py:214
  28.9 0.3 collective-permute-start.17
  29.2 0.5 collective-permute-done.9.refs_4_
  29.8 1.6 %collective-permute-done.16.refs_7_.refs_3_ = bf16[128,128]{1,0:T(8,128)(2,1)S(1)} collective-permute-done((bf16[128,128]{1,0:T(8,128)(2,1)S(1)}, bf16[128,128]{1,0:T(8,128)(2,1)S(1)}, u32[]{:S(2)}, u32[]{:S(2)}) %collective-permute-start.16) | collective-permute-done | bytes 32800 | tf_op jit(solution)/shard_map/ppermute | solution.py:214
  31.3 1.0 %collective-permute-done.17.refs_8_.refs_4_ = bf16[128,128]{1,0:T(8,128)(2,1)S(1)} collective-permute-done((bf16[128,128]{1,0:T(8,128)(2,1)S(1)}, bf16[128,128]{1,0:T(8,128)(2,1)S(1)}, u32[]{:S(2)}, u32[]{:S(2)}) %collective-permute-start.17) | collective-permute-done | bytes 32800 | tf_op jit(solution)/shard_map/ppermute | solution.py:214
  32.3 0.9 %collective-permute-start.18 = (bf16[128,128]{1,0:T(8,128)(2,1)S(1)}, bf16[128,128]{1,0:T(8,128)(2,1)S(1)}, u32[]{:S(2)}, u32[]{:S(2)}) collective-permute-start(bf16[128,128]{1,0:T(8,128)(2,1)S(1)} %forward_end.2.refs_0_.refs_1_), channel_id=1, source_target_pairs={{0,8},{4,12},{8,0},{12,4},{16,24},{20,28},{24,16},{28,20},{1,9},{5... | collective-permute-start | bytes 98312 | tf_op jit(solution)/shard_map/ppermute | solution.py:214
  33.3 2.4 %collective-permute-start.19 = (bf16[128,128]{1,0:T(8,128)(2,1)S(1)}, bf16[128,128]{1,0:T(8,128)(2,1)S(1)}, u32[]{:S(2)}, u32[]{:S(2)}) collective-permute-start(bf16[128,128]{1,0:T(8,128)(2,1)S(1)} %forward_end.2.refs_0_.refs_1_), channel_id=1, source_target_pairs={{0,16},{4,20},{8,24},{12,28},{16,0},{20,4},{24,8},{28,12},{1,17},{... | collective-permute-start | bytes 98312 | tf_op jit(solution)/shard_map/ppermute | solution.py:214
  35.6 1.1 %collective-permute-start.20 = (bf16[128,128]{1,0:T(8,128)(2,1)S(1)}, bf16[128,128]{1,0:T(8,128)(2,1)S(1)}, u32[]{:S(2)}, u32[]{:S(2)}) collective-permute-start(bf16[128,128]{1,0:T(8,128)(2,1)S(1)} %forward_end.2.refs_0_.refs_1_), channel_id=1, source_target_pairs={{0,24},{4,28},{8,16},{12,20},{16,8},{20,12},{24,0},{28,4},{1,25},{... | collective-permute-start | bytes 98312 | tf_op jit(solution)/shard_map/ppermute | solution.py:214
  36.8 1.5 %collective-permute-done.19.refs_2_.refs_3_ = bf16[128,128]{1,0:T(8,128)(2,1)S(1)} collective-permute-done((bf16[128,128]{1,0:T(8,128)(2,1)S(1)}, bf16[128,128]{1,0:T(8,128)(2,1)S(1)}, u32[]{:S(2)}, u32[]{:S(2)}) %collective-permute-start.19) | collective-permute-done | bytes 32800 | tf_op jit(solution)/shard_map/ppermute | solution.py:214
  38.3 3.0 %collective-permute-done.20.refs_3_.refs_4_ = bf16[128,128]{1,0:T(8,128)(2,1)S(1)} collective-permute-done((bf16[128,128]{1,0:T(8,128)(2,1)S(1)}, bf16[128,128]{1,0:T(8,128)(2,1)S(1)}, u32[]{:S(2)}, u32[]{:S(2)}) %collective-permute-start.20) | collective-permute-done | bytes 32800 | tf_op jit(solution)/shard_map/ppermute | solution.py:214
  41.4 1.1 %collective-permute-start.21 = (bf16[4,128,128]{2,1,0:T(8,128)(2,1)S(1)}, bf16[4,128,128]{2,1,0:T(8,128)(2,1)S(1)}, u32[]{:S(2)}, u32[]{:S(2)}) collective-permute-start(bf16[4,128,128]{2,1,0:T(8,128)(2,1)S(1)} %pack.3), channel_id=1, source_target_pairs={{0,4},{4,0},{8,12},{12,8},{16,20},{20,16},{24,28},{28,24},{1,5},{5... | collective-permute-start | bytes 393224 | tf_op jit(solution)/shard_map/ppermute | solution.py:214
  42.5 0.3 adjoint.3
  42.8 1.1 %collective-permute-start.27 = (bf16[2,128,128]{2,1,0:T(8,128)(2,1)S(1)}, bf16[2,128,128]{2,1,0:T(8,128)(2,1)S(1)}, u32[]{:S(2)}, u32[]{:S(2)}) collective-permute-start(bf16[2,128,128]{2,1,0:T(8,128)(2,1)S(1)} %get-tuple-element.59), channel_id=1, source_target_pairs={{0,4},{4,0},{8,12},{12,8},{16,20},{20,16},{24,28},{28,24},{1,5},{5... | collective-permute-start | bytes 196616 | tf_op jit(solution)/shard_map/ppermute | solution.py:214
  43.9 1.0 %collective-permute-start.22 = (bf16[2,128,128]{2,1,0:T(8,128)(2,1)S(1)}, bf16[2,128,128]{2,1,0:T(8,128)(2,1)S(1)}, u32[]{:S(2)}, u32[]{:S(2)}) collective-permute-start(bf16[2,128,128]{2,1,0:T(8,128)(2,1)S(1)} %get-tuple-element.50), channel_id=1, source_target_pairs={{0,4},{4,0},{8,12},{12,8},{16,20},{20,16},{24,28},{28,24},{1,5},{5... | collective-permute-start | bytes 196616 | tf_op jit(solution)/shard_map/ppermute | solution.py:214
  44.9 2.6 %collective-permute-done.27.refs_1_ = bf16[2,128,128]{2,1,0:T(8,128)(2,1)S(1)} collective-permute-done((bf16[2,128,128]{2,1,0:T(8,128)(2,1)S(1)}, bf16[2,128,128]{2,1,0:T(8,128)(2,1)S(1)}, u32[]{:S(2)}, u32[]{:S(2)}) %collective-permute-start.27) | collective-permute-done | bytes 65568 | tf_op jit(solution)/shard_map/ppermute | solution.py:214
  47.5 0.1 collective-permute-start.28
  47.6 1.8 %collective-permute-start.29 = (bf16[128,128]{1,0:T(8,128)(2,1)S(1)}, bf16[128,128]{1,0:T(8,128)(2,1)S(1)}, u32[]{:S(2)}, u32[]{:S(2)}) collective-permute-start(bf16[128,128]{1,0:T(8,128)(2,1)S(1)} %get-tuple-element.61), channel_id=1, source_target_pairs={{0,24},{4,28},{8,16},{12,20},{16,8},{20,12},{24,0},{28,4},{1,25},{... | collective-permute-start | bytes 98312 | tf_op jit(solution)/shard_map/ppermute | solution.py:214
  49.4 1.7 %collective-permute-start.26 = (bf16[128,128]{1,0:T(8,128)(2,1)S(1)}, bf16[128,128]{1,0:T(8,128)(2,1)S(1)}, u32[]{:S(2)}, u32[]{:S(2)}) collective-permute-start(bf16[128,128]{1,0:T(8,128)(2,1)S(1)} %get-tuple-element.57), channel_id=1, source_target_pairs={{0,8},{4,12},{8,0},{12,4},{16,24},{20,28},{24,16},{28,20},{1,9},{5... | collective-permute-start | bytes 98312 | tf_op jit(solution)/shard_map/ppermute | solution.py:214
  51.1 0.4 forward.3
  51.6 0.1 collective-permute-start.23
  51.6 1.0 %collective-permute-start.24 = (bf16[128,128]{1,0:T(8,128)(2,1)S(1)}, bf16[128,128]{1,0:T(8,128)(2,1)S(1)}, u32[]{:S(2)}, u32[]{:S(2)}) collective-permute-start(bf16[128,128]{1,0:T(8,128)(2,1)S(1)} %get-tuple-element.54), channel_id=1, source_target_pairs={{0,2},{1,3},{2,0},{3,1},{4,6},{5,7},{6,4},{7,5},{8,10},{9,11},{10,... | collective-permute-start | bytes 98312 | tf_op jit(solution)/shard_map/ppermute | solution.py:214
  52.6 0.9 %collective-permute-start.25 = (bf16[128,128]{1,0:T(8,128)(2,1)S(1)}, bf16[128,128]{1,0:T(8,128)(2,1)S(1)}, u32[]{:S(2)}, u32[]{:S(2)}) collective-permute-start(bf16[128,128]{1,0:T(8,128)(2,1)S(1)} %get-tuple-element.55), channel_id=1, source_target_pairs={{0,3},{1,2},{2,1},{3,0},{4,7},{5,6},{6,5},{7,4},{8,11},{9,10},{10,... | collective-permute-start | bytes 98312 | tf_op jit(solution)/shard_map/ppermute | solution.py:214
  53.5 0.2 collective-permute-done.26.refs_5_
  53.7 0.7 %adjoint_end.1 = f32[128,128]{1,0:T(8,128)} custom-call(f32[128,128]{1,0:T(8,128)S(1)} %copy-done.1, f32[128,128]{1,0:T(8,128)S(1)} %get-tuple-element.56.refs_1_, f32[1,128]{1,0:T(1,128)S(1)} %get-tuple-element.42.refs_0_.refs_2_, f32[128,128]{1,0:T(8,128)S(1)} %get-tuple-element.32.refs_1_.refs_3_, f32[128,128]{1,0:T(8,128)S(1)} %get-tuple-element.51.refs_6_.refs_4_, ...), custom_call_target="tpu_custom_call" | custom-call | bytes 426496 | tf_op jit(solution)/shard_map/adjoint_end/pallas_call | solution.py:36
  54.4 1.2 %collective-permute-done.24.refs_4_ = bf16[128,128]{1,0:T(8,128)(2,1)S(1)} collective-permute-done((bf16[128,128]{1,0:T(8,128)(2,1)S(1)}, bf16[128,128]{1,0:T(8,128)(2,1)S(1)}, u32[]{:S(2)}, u32[]{:S(2)}) %collective-permute-start.24) | collective-permute-done | bytes 32800 | tf_op jit(solution)/shard_map/ppermute | solution.py:214
  55.6 0.4 collective-permute-done.25.refs_5_
  56.0 0.7 %forward_end.3 = f32[128,128]{1,0:T(8,128)} custom-call(f32[128,128]{1,0:T(8,128)S(1)} %copy-done, f32[128,128]{1,0:T(8,128)S(1)} %get-tuple-element.32.refs_1_.refs_3_, bf16[128,128]{1,0:T(8,128)(2,1)S(1)} %get-tuple-element.52.refs_2_, bf16[128,128]{1,0:T(8,128)(2,1)S(1)} %collective-permute-done.23.refs_3_, ...), custom_call_target="tpu_custom_call" | custom-call | bytes 327680 | tf_op jit(solution)/shard_map/forward_end/pallas_call | solution.py:36
  (32 shorter events, 0.3 us)
Async XLA Ops:
  1.7 10.2 %collective-permute-start.4 = (bf16[128,128]{1,0:T(8,128)(2,1)S(1)}, bf16[128,128]{1,0:T(8,128)(2,1)S(1)}, u32[]{:S(2)}, u32[]{:S(2)}) collective-permute-start(bf16[128,128]{1,0:T(8,128)(2,1)S(1)} %get-tuple-element.33.refs_0_.refs_1_), channel_id=1, source_target_pairs={{0,1},{1,0},{2,3},{3,2},{4,5},{5,4},{6,7},{7,6},{8,9},{9,8},{10,11... | collective-permute-start | bytes 98312 | tf_op jit(solution)/shard_map/ppermute | solution.py:214
  2.2 9.8 %collective-permute-start.5 = (bf16[128,128]{1,0:T(8,128)(2,1)S(1)}, bf16[128,128]{1,0:T(8,128)(2,1)S(1)}, u32[]{:S(2)}, u32[]{:S(2)}) collective-permute-start(bf16[128,128]{1,0:T(8,128)(2,1)S(1)} %get-tuple-element.33.refs_0_.refs_1_), channel_id=1, source_target_pairs={{0,2},{1,3},{2,0},{3,1},{4,6},{5,7},{6,4},{7,5},{8,10},{9,11},{10,... | collective-permute-start | bytes 98312 | tf_op jit(solution)/shard_map/ppermute | solution.py:214
  4.8 7.3 %collective-permute-start.6 = (bf16[128,128]{1,0:T(8,128)(2,1)S(1)}, bf16[128,128]{1,0:T(8,128)(2,1)S(1)}, u32[]{:S(2)}, u32[]{:S(2)}) collective-permute-start(bf16[128,128]{1,0:T(8,128)(2,1)S(1)} %get-tuple-element.33.refs_0_.refs_1_), channel_id=1, source_target_pairs={{0,3},{1,2},{2,1},{3,0},{4,7},{5,6},{6,5},{7,4},{8,11},{9,10},{10,... | collective-permute-start | bytes 98312 | tf_op jit(solution)/shard_map/ppermute | solution.py:214
  4.8 9.6 %collective-permute-start = (bf16[128,128]{1,0:T(8,128)(2,1)S(1)}, bf16[128,128]{1,0:T(8,128)(2,1)S(1)}, u32[]{:S(2)}, u32[]{:S(2)}) collective-permute-start(bf16[128,128]{1,0:T(8,128)(2,1)S(1)} %get-tuple-element.34.refs_0_.refs_1_), channel_id=1, source_target_pairs={{0,8},{4,12},{8,0},{12,4},{16,24},{20,28},{24,16},{28,20},{1,9},{5... | collective-permute-start | bytes 98312 | tf_op jit(solution)/shard_map/ppermute | solution.py:214
  6.6 7.8 %collective-permute-start.1 = (bf16[128,128]{1,0:T(8,128)(2,1)S(1)}, bf16[128,128]{1,0:T(8,128)(2,1)S(1)}, u32[]{:S(2)}, u32[]{:S(2)}) collective-permute-start(bf16[128,128]{1,0:T(8,128)(2,1)S(1)} %get-tuple-element.34.refs_0_.refs_1_), channel_id=1, source_target_pairs={{0,16},{4,20},{8,24},{12,28},{16,0},{20,4},{24,8},{28,12},{1,17},{... | collective-permute-start | bytes 98312 | tf_op jit(solution)/shard_map/ppermute | solution.py:214
  11.9 5.8 %collective-permute-start.2 = (bf16[128,128]{1,0:T(8,128)(2,1)S(1)}, bf16[128,128]{1,0:T(8,128)(2,1)S(1)}, u32[]{:S(2)}, u32[]{:S(2)}) collective-permute-start(bf16[128,128]{1,0:T(8,128)(2,1)S(1)} %get-tuple-element.34.refs_0_.refs_1_), channel_id=1, source_target_pairs={{0,24},{4,28},{8,16},{12,20},{16,8},{20,12},{24,0},{28,4},{1,25},{... | collective-permute-start | bytes 98312 | tf_op jit(solution)/shard_map/ppermute | solution.py:214
  12.3 6.7 %collective-permute-start.12 = (f32[2,128,128]{2,1,0:T(8,128)S(1)}, f32[2,128,128]{2,1,0:T(8,128)S(1)}, u32[]{:S(2)}, u32[]{:S(2)}) collective-permute-start(f32[2,128,128]{2,1,0:T(8,128)S(1)} %get-tuple-element.45), channel_id=1, source_target_pairs={{0,4},{4,0},{8,12},{12,8},{16,20},{20,16},{24,28},{28,24},{1,5},{5... | collective-permute-start | bytes 393224 | tf_op jit(solution)/shard_map/ppermute | solution.py:214
  13.9 8.9 %collective-permute-start.7 = (f32[2,128,128]{2,1,0:T(8,128)S(1)}, f32[2,128,128]{2,1,0:T(8,128)S(1)}, u32[]{:S(2)}, u32[]{:S(2)}) collective-permute-start(f32[2,128,128]{2,1,0:T(8,128)S(1)} %get-tuple-element.36), channel_id=1, source_target_pairs={{0,4},{4,0},{8,12},{12,8},{16,20},{20,16},{24,28},{28,24},{1,5},{5... | collective-permute-start | bytes 393224 | tf_op jit(solution)/shard_map/ppermute | solution.py:214
  17.7 5.7 %collective-permute-start.3 = (bf16[4,128,128]{2,1,0:T(8,128)(2,1)S(1)}, bf16[4,128,128]{2,1,0:T(8,128)(2,1)S(1)}, u32[]{:S(2)}, u32[]{:S(2)}) collective-permute-start(bf16[4,128,128]{2,1,0:T(8,128)(2,1)S(1)} %pack.2), channel_id=1, source_target_pairs={{0,4},{4,0},{8,12},{12,8},{16,20},{20,16},{24,28},{28,24},{1,5},{5... | collective-permute-start | bytes 393224 | tf_op jit(solution)/shard_map/ppermute | solution.py:214
  19.0 6.5 %collective-permute-start.13 = (f32[128,128]{1,0:T(8,128)S(1)}, f32[128,128]{1,0:T(8,128)S(1)}, u32[]{:S(2)}, u32[]{:S(2)}) collective-permute-start(f32[128,128]{1,0:T(8,128)S(1)} %get-tuple-element.46), channel_id=1, source_target_pairs={{0,16},{4,20},{8,24},{12,28},{16,0},{20,4},{24,8},{28,12},{1,17},{... | collective-permute-start | bytes 196616 | tf_op jit(solution)/shard_map/ppermute | solution.py:214
  20.5 6.2 %collective-permute-start.14 = (f32[128,128]{1,0:T(8,128)S(1)}, f32[128,128]{1,0:T(8,128)S(1)}, u32[]{:S(2)}, u32[]{:S(2)}) collective-permute-start(f32[128,128]{1,0:T(8,128)S(1)} %get-tuple-element.47), channel_id=1, source_target_pairs={{0,24},{4,28},{8,16},{12,20},{16,8},{20,12},{24,0},{28,4},{1,25},{... | collective-permute-start | bytes 196616 | tf_op jit(solution)/shard_map/ppermute | solution.py:214
  22.8 4.4 %collective-permute-start.11 = (f32[128,128]{1,0:T(8,128)S(1)}, f32[128,128]{1,0:T(8,128)S(1)}, u32[]{:S(2)}, u32[]{:S(2)}) collective-permute-start(f32[128,128]{1,0:T(8,128)S(1)} %get-tuple-element.43), channel_id=1, source_target_pairs={{0,8},{4,12},{8,0},{12,4},{16,24},{20,28},{24,16},{28,20},{1,9},{5... | collective-permute-start | bytes 196616 | tf_op jit(solution)/shard_map/ppermute | solution.py:214
  23.8 5.1 %collective-permute-start.10 = (f32[128,128]{1,0:T(8,128)S(1)}, f32[128,128]{1,0:T(8,128)S(1)}, u32[]{:S(2)}, u32[]{:S(2)}) collective-permute-start(f32[128,128]{1,0:T(8,128)S(1)} %get-tuple-element.41), channel_id=1, source_target_pairs={{0,3},{1,2},{2,1},{3,0},{4,7},{5,6},{6,5},{7,4},{8,11},{9,10},{10,... | collective-permute-start | bytes 196616 | tf_op jit(solution)/shard_map/ppermute | solution.py:214
  23.9 5.3 %collective-permute-start.8 = (f32[128,128]{1,0:T(8,128)S(1)}, f32[128,128]{1,0:T(8,128)S(1)}, u32[]{:S(2)}, u32[]{:S(2)}) collective-permute-start(f32[128,128]{1,0:T(8,128)S(1)} %get-tuple-element.39), channel_id=1, source_target_pairs={{0,1},{1,0},{2,3},{3,2},{4,5},{5,4},{6,7},{7,6},{8,9},{9,8},{10,11... | collective-permute-start | bytes 196616 | tf_op jit(solution)/shard_map/ppermute | solution.py:214
  25.5 4.3 %collective-permute-start.9 = (f32[128,128]{1,0:T(8,128)S(1)}, f32[128,128]{1,0:T(8,128)S(1)}, u32[]{:S(2)}, u32[]{:S(2)}) collective-permute-start(f32[128,128]{1,0:T(8,128)S(1)} %get-tuple-element.40), channel_id=1, source_target_pairs={{0,2},{1,3},{2,0},{3,1},{4,6},{5,7},{6,4},{7,5},{8,10},{9,11},{10,... | collective-permute-start | bytes 196616 | tf_op jit(solution)/shard_map/ppermute | solution.py:214
  27.3 5.0 %copy-start = (f32[128,128]{1,0:T(8,128)S(1)}, f32[128,128]{1,0:T(8,128)}, u32[]{:S(2)}) copy-start(f32[128,128]{1,0:T(8,128)} %refs_0_.6) | copy-start | bytes 196612
  27.3 2.5 %collective-permute-start.15 = (bf16[128,128]{1,0:T(8,128)(2,1)S(1)}, bf16[128,128]{1,0:T(8,128)(2,1)S(1)}, u32[]{:S(2)}, u32[]{:S(2)}) collective-permute-start(bf16[128,128]{1,0:T(8,128)(2,1)S(1)} %get-tuple-element.48.refs_1_), channel_id=1, source_target_pairs={{0,1},{1,0},{2,3},{3,2},{4,5},{5,4},{6,7},{7,6},{8,9},{9,8},{10,11... | collective-permute-start | bytes 98312 | tf_op jit(solution)/shard_map/ppermute | solution.py:214
  27.4 4.0 %collective-permute-start.16 = (bf16[128,128]{1,0:T(8,128)(2,1)S(1)}, bf16[128,128]{1,0:T(8,128)(2,1)S(1)}, u32[]{:S(2)}, u32[]{:S(2)}) collective-permute-start(bf16[128,128]{1,0:T(8,128)(2,1)S(1)} %get-tuple-element.48.refs_1_), channel_id=1, source_target_pairs={{0,2},{1,3},{2,0},{3,1},{4,6},{5,7},{6,4},{7,5},{8,10},{9,11},{10,... | collective-permute-start | bytes 98312 | tf_op jit(solution)/shard_map/ppermute | solution.py:214
  28.9 3.3 %collective-permute-start.17 = (bf16[128,128]{1,0:T(8,128)(2,1)S(1)}, bf16[128,128]{1,0:T(8,128)(2,1)S(1)}, u32[]{:S(2)}, u32[]{:S(2)}) collective-permute-start(bf16[128,128]{1,0:T(8,128)(2,1)S(1)} %get-tuple-element.48.refs_1_), channel_id=1, source_target_pairs={{0,3},{1,2},{2,1},{3,0},{4,7},{5,6},{6,5},{7,4},{8,11},{9,10},{10,... | collective-permute-start | bytes 98312 | tf_op jit(solution)/shard_map/ppermute | solution.py:214
  32.3 4.5 %collective-permute-start.18 = (bf16[128,128]{1,0:T(8,128)(2,1)S(1)}, bf16[128,128]{1,0:T(8,128)(2,1)S(1)}, u32[]{:S(2)}, u32[]{:S(2)}) collective-permute-start(bf16[128,128]{1,0:T(8,128)(2,1)S(1)} %forward_end.2.refs_0_.refs_1_), channel_id=1, source_target_pairs={{0,8},{4,12},{8,0},{12,4},{16,24},{20,28},{24,16},{28,20},{1,9},{5... | collective-permute-start | bytes 98312 | tf_op jit(solution)/shard_map/ppermute | solution.py:214
  33.3 5.1 %collective-permute-start.19 = (bf16[128,128]{1,0:T(8,128)(2,1)S(1)}, bf16[128,128]{1,0:T(8,128)(2,1)S(1)}, u32[]{:S(2)}, u32[]{:S(2)}) collective-permute-start(bf16[128,128]{1,0:T(8,128)(2,1)S(1)} %forward_end.2.refs_0_.refs_1_), channel_id=1, source_target_pairs={{0,16},{4,20},{8,24},{12,28},{16,0},{20,4},{24,8},{28,12},{1,17},{... | collective-permute-start | bytes 98312 | tf_op jit(solution)/shard_map/ppermute | solution.py:214
  35.6 5.7 %collective-permute-start.20 = (bf16[128,128]{1,0:T(8,128)(2,1)S(1)}, bf16[128,128]{1,0:T(8,128)(2,1)S(1)}, u32[]{:S(2)}, u32[]{:S(2)}) collective-permute-start(bf16[128,128]{1,0:T(8,128)(2,1)S(1)} %forward_end.2.refs_0_.refs_1_), channel_id=1, source_target_pairs={{0,24},{4,28},{8,16},{12,20},{16,8},{20,12},{24,0},{28,4},{1,25},{... | collective-permute-start | bytes 98312 | tf_op jit(solution)/shard_map/ppermute | solution.py:214
  41.4 9.8 %collective-permute-start.21 = (bf16[4,128,128]{2,1,0:T(8,128)(2,1)S(1)}, bf16[4,128,128]{2,1,0:T(8,128)(2,1)S(1)}, u32[]{:S(2)}, u32[]{:S(2)}) collective-permute-start(bf16[4,128,128]{2,1,0:T(8,128)(2,1)S(1)} %pack.3), channel_id=1, source_target_pairs={{0,4},{4,0},{8,12},{12,8},{16,20},{20,16},{24,28},{28,24},{1,5},{5... | collective-permute-start | bytes 393224 | tf_op jit(solution)/shard_map/ppermute | solution.py:214
  42.8 4.7 %collective-permute-start.27 = (bf16[2,128,128]{2,1,0:T(8,128)(2,1)S(1)}, bf16[2,128,128]{2,1,0:T(8,128)(2,1)S(1)}, u32[]{:S(2)}, u32[]{:S(2)}) collective-permute-start(bf16[2,128,128]{2,1,0:T(8,128)(2,1)S(1)} %get-tuple-element.59), channel_id=1, source_target_pairs={{0,4},{4,0},{8,12},{12,8},{16,20},{20,16},{24,28},{28,24},{1,5},{5... | collective-permute-start | bytes 196616 | tf_op jit(solution)/shard_map/ppermute | solution.py:214
  43.9 5.5 %collective-permute-start.22 = (bf16[2,128,128]{2,1,0:T(8,128)(2,1)S(1)}, bf16[2,128,128]{2,1,0:T(8,128)(2,1)S(1)}, u32[]{:S(2)}, u32[]{:S(2)}) collective-permute-start(bf16[2,128,128]{2,1,0:T(8,128)(2,1)S(1)} %get-tuple-element.50), channel_id=1, source_target_pairs={{0,4},{4,0},{8,12},{12,8},{16,20},{20,16},{24,28},{28,24},{1,5},{5... | collective-permute-start | bytes 196616 | tf_op jit(solution)/shard_map/ppermute | solution.py:214
  47.5 5.1 %collective-permute-start.28 = (bf16[128,128]{1,0:T(8,128)(2,1)S(1)}, bf16[128,128]{1,0:T(8,128)(2,1)S(1)}, u32[]{:S(2)}, u32[]{:S(2)}) collective-permute-start(bf16[128,128]{1,0:T(8,128)(2,1)S(1)} %get-tuple-element.60), channel_id=1, source_target_pairs={{0,16},{4,20},{8,24},{12,28},{16,0},{20,4},{24,8},{28,12},{1,17},{... | collective-permute-start | bytes 98312 | tf_op jit(solution)/shard_map/ppermute | solution.py:214
  47.6 6.0 %collective-permute-start.29 = (bf16[128,128]{1,0:T(8,128)(2,1)S(1)}, bf16[128,128]{1,0:T(8,128)(2,1)S(1)}, u32[]{:S(2)}, u32[]{:S(2)}) collective-permute-start(bf16[128,128]{1,0:T(8,128)(2,1)S(1)} %get-tuple-element.61), channel_id=1, source_target_pairs={{0,24},{4,28},{8,16},{12,20},{16,8},{20,12},{24,0},{28,4},{1,25},{... | collective-permute-start | bytes 98312 | tf_op jit(solution)/shard_map/ppermute | solution.py:214
  49.4 4.3 %collective-permute-start.26 = (bf16[128,128]{1,0:T(8,128)(2,1)S(1)}, bf16[128,128]{1,0:T(8,128)(2,1)S(1)}, u32[]{:S(2)}, u32[]{:S(2)}) collective-permute-start(bf16[128,128]{1,0:T(8,128)(2,1)S(1)} %get-tuple-element.57), channel_id=1, source_target_pairs={{0,8},{4,12},{8,0},{12,4},{16,24},{20,28},{24,16},{28,20},{1,9},{5... | collective-permute-start | bytes 98312 | tf_op jit(solution)/shard_map/ppermute | solution.py:214
  51.1 2.6 %copy-start.1 = (f32[128,128]{1,0:T(8,128)S(1)}, f32[128,128]{1,0:T(8,128)}, u32[]{:S(2)}) copy-start(f32[128,128]{1,0:T(8,128)} %refs_0_.7) | copy-start | bytes 196612
  51.6 2.9 %collective-permute-start.23 = (bf16[128,128]{1,0:T(8,128)(2,1)S(1)}, bf16[128,128]{1,0:T(8,128)(2,1)S(1)}, u32[]{:S(2)}, u32[]{:S(2)}) collective-permute-start(bf16[128,128]{1,0:T(8,128)(2,1)S(1)} %get-tuple-element.53), channel_id=1, source_target_pairs={{0,1},{1,0},{2,3},{3,2},{4,5},{5,4},{6,7},{7,6},{8,9},{9,8},{10,11... | collective-permute-start | bytes 98312 | tf_op jit(solution)/shard_map/ppermute | solution.py:214
  51.6 4.0 %collective-permute-start.24 = (bf16[128,128]{1,0:T(8,128)(2,1)S(1)}, bf16[128,128]{1,0:T(8,128)(2,1)S(1)}, u32[]{:S(2)}, u32[]{:S(2)}) collective-permute-start(bf16[128,128]{1,0:T(8,128)(2,1)S(1)} %get-tuple-element.54), channel_id=1, source_target_pairs={{0,2},{1,3},{2,0},{3,1},{4,6},{5,7},{6,4},{7,5},{8,10},{9,11},{10,... | collective-permute-start | bytes 98312 | tf_op jit(solution)/shard_map/ppermute | solution.py:214
  52.6 3.4 %collective-permute-start.25 = (bf16[128,128]{1,0:T(8,128)(2,1)S(1)}, bf16[128,128]{1,0:T(8,128)(2,1)S(1)}, u32[]{:S(2)}, u32[]{:S(2)}) collective-permute-start(bf16[128,128]{1,0:T(8,128)(2,1)S(1)} %get-tuple-element.55), channel_id=1, source_target_pairs={{0,3},{1,2},{2,1},{3,0},{4,7},{5,6},{6,5},{7,4},{8,11},{9,10},{10,... | collective-permute-start | bytes 98312 | tf_op jit(solution)/shard_map/ppermute | solution.py:214

commit v8 on v7

--- a/solution.py
+++ b/solution.py
@@ -197,17 +197,23 @@
     out_ref[...] = value.astype(out_ref.dtype)
 
 
-def adjoint_mid_body(rate_ref, *refs):
-    *parts, d_ref, q_ref = refs
-    total = sum_refs(parts)
+def middle_body(half, row_ref, column_ref, h_ref, *refs):
+    back, refs = refs[:half], refs[half:]
+    *first, d_ref, q_ref, p_ref = refs
+    total = sum_refs(back)
     d_ref[...] = total
-    q_ref[...] = ((1.0 - rate_ref[...]) * total).astype(BF16)
+    q_ref[...] = ((1.0 - row_ref[...]) * total).astype(BF16)
+    rate = column_ref[...]
+    p_ref[...] = ((1.0 - rate) * sum_refs(first) + rate * h_ref[...]).astype(BF16)
 
 
 def adjoint_end_body(cot_ref, d_ref, row_ref, column_ref, *refs):
     *parts, out_ref = refs
     change = (row_ref[...] * d_ref[...] + sum_refs(parts)).T
     out_ref[...] = column_ref[...] * cot_ref[...] + change
+
+
+ADD_COST = 400_000_000
 
 
 def send(value, axis, count, step):
@@ -258,8 +264,10 @@
         ],
     )
 
-    def add(keep, got, kinds, name):
-        return call(add_body, [shape(kind) for kind in kinds], [vmem()] * 2, (keep, got), 0, name)
+    def add(keep, got, kinds, name, after=()):
+        outs = [shape(kind) for kind in kinds]
+        hint = ADD_COST if kinds[-1] == BF16 else 0
+        return call(add_body, outs, [vmem()] * 2, (keep, got), hint, name, after=after)
 
     def adjoint_hop(part, kind):
         blocks = [part] + [send(part, "cols", n_cols, s) for s in range(1, n_cols)]
@@ -277,7 +285,7 @@
         kinds = [F32] + [kind] * (near - 1)
         close = add(keep_near, send(send_near, "rows", n_rows, 1), kinds, "add_near")
         close = [close[0]] + [send(close[s], "rows", n_rows, 2 * s) for s in range(1, near)]
-        return close + far, blocks
+        return far + close, close[:1]
 
     def forward_hop(part, kind, after):
         panels = [part] + [send(part, "rows", n_rows, 2 * s) for s in range(1, half)]
@@ -305,19 +313,18 @@
             after=after,
         )[0]
 
-    back, _ = adjoint_hop(q0, F32)
-    first = forward_hop(p0, F32, back[:1])
-    d1, q1 = call(
-        adjoint_mid_body,
-        [shape(F32), shape(BF16)],
-        [vmem()] * (1 + half),
-        (rate, *back),
+    back, last = adjoint_hop(q0, F32)
+    first = forward_hop(p0, F32, last)
+    d1, q1, p1 = call(
+        lambda *refs: middle_body(half, *refs),
+        [shape(F32), shape(BF16), shape(BF16)],
+        [vmem()] * (3 + half + n_cols),
+        (rate, column, h_start, *back, *first),
         0,
-        "adjoint_mid",
-    )
-    back_two, blocks = adjoint_hop(q1, BF16)
-    p1 = forward_end(first, BF16, blocks[1:])
-    second = forward_hop(p1, BF16, back_two[:1])
+        "middle",
+    )
+    back_two, last = adjoint_hop(q1, BF16)
+    second = forward_hop(p1, BF16, last)
     propagated = forward_end(second, F32)
     (input_grad,) = call(
         adjoint_end_body,

time: 57 us -> 52.1 us (0.914)
  starting transfers between devices: 32.6 us -> 29.8 us
  waiting for transfers between devices: 16.5 us -> 14.8 us
    ppermute x30, starting transfers between devices: 32.6 us -> 29.8 us  [send(): return lax.ppermute(value, axis, [(i, i ^ step) for i in range(count)])]
    ppermute x30, waiting for transfers between devices: 16.5 us -> 14.8 us  [send(): return lax.ppermute(value, axis, [(i, i ^ step) for i in range(count)])]
    pallas_call x16 -> x15, Pallas kernels: 6.09 us -> 5.88 us  [call(): pl.pallas_call(ordered, out_shape=outs, in_specs=[*in_specs, *[pl.BlockSp...]
  transfers between devices with their start and end apart: 30 -> 30, of which waited for: 12 -> 11; matrix products, arithmetic and copies ran while one was open for 0% -> 0% of each run, Pallas kernels for 8% -> 7%
where the time goes in v8:
time: 52.1 us; the launch traced here: 51.9 us
  starting transfers between devices  29.8 us (57%)
  waiting for transfers between devices  14.8 us (28%)
  Pallas kernels  5.88 us (11%)
  between operations  1.45 us (3%)
    ppermute x30, starting transfers between devices, send(): return lax.ppermute(value, axis, [(i, i ^ step) for i in range(count)])  29.8 us
    ppermute x30, waiting for transfers between devices, send(): return lax.ppermute(value, axis, [(i, i ^ step) for i in range(count)])  14.8 us
    pallas_call x15, Pallas kernels, call(): pl.pallas_call(ordered, out_shape=outs, in_specs=[*in_specs, *[pl.BlockSp...  5.88 us
  transfers between devices with their start and end apart: 30, of which 11 were waited for; matrix products, arithmetic and copies ran while one was open for 0% of the time, Pallas kernels for 7%

profile of v8, /device:TPU:0, one launch (start us, length us, event | category | flops | bytes accessed | tf_op | source)
XLA Modules:
  0.0 51.9 jit_solution(4590266111160914883)
XLA Ops:
  0.6 1.0 %start.1 = (bf16[128,128]{1,0:T(8,128)(2,1)S(1)}, bf16[128,128]{1,0:T(8,128)(2,1)S(1)}, f32[1,128]{1,0:T(1,128)S(1)}, f32[128,128]{1,0:T(8,128)S(1)}) custom-call(f32[128,128]{1,0:T(8,128)} %refs_0_.5, f32[128,128]{1,0:T(8,128)} %refs_0_.4, s32[1,128]{1,0:T(1,128)} %bitcast.1, f32[8]{0:T(128)} %refs_3_.2), custom_call_target="tpu_custom_call" | custom-call | bytes 263200 | tf_op jit(solution)/shard_map/start/pallas_call | solution.py:36
  1.7 0.5 collective-permute-start
  2.2 2.6 %collective-permute-start.1 = (bf16[128,128]{1,0:T(8,128)(2,1)S(1)}, bf16[128,128]{1,0:T(8,128)(2,1)S(1)}, u32[]{:S(2)}, u32[]{:S(2)}) collective-permute-start(bf16[128,128]{1,0:T(8,128)(2,1)S(1)} %get-tuple-element.34.refs_0_.refs_1_), channel_id=1, source_target_pairs={{0,2},{1,3},{2,0},{3,1},{4,6},{5,7},{6,4},{7,5},{8,10},{9,11},{10,... | collective-permute-start | bytes 98312 | tf_op jit(solution)/shard_map/ppermute | solution.py:220
  4.8 0.1 collective-permute-start.2
  5.5 1.8 %dense.1.refs_0_ = bf16[512,1024]{1,0:T(8,128)(2,1)S(1)} custom-call(bf16[128,128]{1,0:T(8,128)(2,1)S(1)} %get-tuple-element.34.refs_0_.refs_1_, bf16[1,1,24,128,128]{4,3,2,1,0:T(8,128)(2,1)} %refs_1_.3, s32[1,1,24]{2,1,0:T(1,128)} %refs_2_.2, s32[1,1,24]{2,1,0:T(1,128)} %refs_3_.3, s32[1,1]{1,0:T(1,128)S(6)} %copy.10.refs_4_), custom_call_target="tpu_custom_call" | custom-call | bytes 1867972 | tf_op jit(solution)/shard_map/dense/pallas_call | solution.py:36
  7.3 0.8 %collective-permute-done.2.refs_4_ = bf16[128,128]{1,0:T(8,128)(2,1)S(1)} collective-permute-done((bf16[128,128]{1,0:T(8,128)(2,1)S(1)}, bf16[128,128]{1,0:T(8,128)(2,1)S(1)}, u32[]{:S(2)}, u32[]{:S(2)}) %collective-permute-start.2) | collective-permute-done | bytes 32800 | tf_op jit(solution)/shard_map/ppermute | solution.py:220
  8.1 0.3 adjoint.2
  8.4 1.6 %collective-permute-start.3 = (f32[2,128,128]{2,1,0:T(8,128)S(1)}, f32[2,128,128]{2,1,0:T(8,128)S(1)}, u32[]{:S(2)}, u32[]{:S(2)}) collective-permute-start(f32[2,128,128]{2,1,0:T(8,128)S(1)} %get-tuple-element.37), channel_id=1, source_target_pairs={{0,4},{4,0},{8,12},{12,8},{16,20},{20,16},{24,28},{28,24},{1,5},{5... | collective-permute-start | bytes 393224 | tf_op jit(solution)/shard_map/ppermute | solution.py:220
  10.0 1.6 %collective-permute-start.8 = (bf16[128,128]{1,0:T(8,128)(2,1)S(1)}, bf16[128,128]{1,0:T(8,128)(2,1)S(1)}, u32[]{:S(2)}, u32[]{:S(2)}) collective-permute-start(bf16[128,128]{1,0:T(8,128)(2,1)S(1)} %get-tuple-element.44.refs_0_.refs_1_), channel_id=1, source_target_pairs={{0,8},{4,12},{8,0},{12,4},{16,24},{20,28},{24,16},{28,20},{1,9},{5... | collective-permute-start | bytes 98312 | tf_op jit(solution)/shard_map/ppermute | solution.py:220
  11.6 2.6 %collective-permute-start.9 = (bf16[128,128]{1,0:T(8,128)(2,1)S(1)}, bf16[128,128]{1,0:T(8,128)(2,1)S(1)}, u32[]{:S(2)}, u32[]{:S(2)}) collective-permute-start(bf16[128,128]{1,0:T(8,128)(2,1)S(1)} %get-tuple-element.44.refs_0_.refs_1_), channel_id=1, source_target_pairs={{0,16},{4,20},{8,24},{12,28},{16,0},{20,4},{24,8},{28,12},{1,17},{... | collective-permute-start | bytes 98312 | tf_op jit(solution)/shard_map/ppermute | solution.py:220
  14.2 0.2 collective-permute-start.10
  14.4 0.5 collective-permute-start.6
  14.9 2.1 %collective-permute-done.9.refs_2_.refs_3_ = bf16[128,128]{1,0:T(8,128)(2,1)S(1)} collective-permute-done((bf16[128,128]{1,0:T(8,128)(2,1)S(1)}, bf16[128,128]{1,0:T(8,128)(2,1)S(1)}, u32[]{:S(2)}, u32[]{:S(2)}) %collective-permute-start.9) | collective-permute-done | bytes 32800 | tf_op jit(solution)/shard_map/ppermute | solution.py:220
  17.0 2.9 %collective-permute-done.10.refs_3_.refs_4_ = bf16[128,128]{1,0:T(8,128)(2,1)S(1)} collective-permute-done((bf16[128,128]{1,0:T(8,128)(2,1)S(1)}, bf16[128,128]{1,0:T(8,128)(2,1)S(1)}, u32[]{:S(2)}, u32[]{:S(2)}) %collective-permute-start.10) | collective-permute-done | bytes 32800 | tf_op jit(solution)/shard_map/ppermute | solution.py:220
  19.9 0.6 %collective-permute-start.11 = (bf16[4,128,128]{2,1,0:T(8,128)(2,1)S(1)}, bf16[4,128,128]{2,1,0:T(8,128)(2,1)S(1)}, u32[]{:S(2)}, u32[]{:S(2)}) collective-permute-start(bf16[4,128,128]{2,1,0:T(8,128)(2,1)S(1)} %pack.2), channel_id=1, source_target_pairs={{0,4},{4,0},{8,12},{12,8},{16,20},{20,16},{24,28},{28,24},{1,5},{5... | collective-permute-start | bytes 393224 | tf_op jit(solution)/shard_map/ppermute | solution.py:220
  20.5 0.1 collective-permute-start.4
  20.6 1.0 %collective-permute-start.5 = (f32[128,128]{1,0:T(8,128)S(1)}, f32[128,128]{1,0:T(8,128)S(1)}, u32[]{:S(2)}, u32[]{:S(2)}) collective-permute-start(f32[128,128]{1,0:T(8,128)S(1)} %get-tuple-element.39), channel_id=1, source_target_pairs={{0,24},{4,28},{8,16},{12,20},{16,8},{20,12},{24,0},{28,4},{1,25},{... | collective-permute-start | bytes 196616 | tf_op jit(solution)/shard_map/ppermute | solution.py:220
  21.6 2.5 %collective-permute-start.7 = (f32[128,128]{1,0:T(8,128)S(1)}, f32[128,128]{1,0:T(8,128)S(1)}, u32[]{:S(2)}, u32[]{:S(2)}) collective-permute-start(f32[128,128]{1,0:T(8,128)S(1)} %get-tuple-element.43), channel_id=1, source_target_pairs={{0,8},{4,12},{8,0},{12,4},{16,24},{20,28},{24,16},{28,20},{1,9},{5... | collective-permute-start | bytes 196616 | tf_op jit(solution)/shard_map/ppermute | solution.py:220
  24.1 0.8 %collective-permute-done.11.refs_5_ = bf16[4,128,128]{2,1,0:T(8,128)(2,1)S(1)} collective-permute-done((bf16[4,128,128]{2,1,0:T(8,128)(2,1)S(1)}, bf16[4,128,128]{2,1,0:T(8,128)(2,1)S(1)}, u32[]{:S(2)}, u32[]{:S(2)}) %collective-permute-start.11) | collective-permute-done | bytes 131104 | tf_op jit(solution)/shard_map/ppermute | solution.py:220
  24.9 0.4 forward.2
  25.4 0.1 collective-permute-start.12
  25.5 1.1 %collective-permute-start.13 = (f32[128,128]{1,0:T(8,128)S(1)}, f32[128,128]{1,0:T(8,128)S(1)}, u32[]{:S(2)}, u32[]{:S(2)}) collective-permute-start(f32[128,128]{1,0:T(8,128)S(1)} %get-tuple-element.47), channel_id=1, source_target_pairs={{0,2},{1,3},{2,0},{3,1},{4,6},{5,7},{6,4},{7,5},{8,10},{9,11},{10,... | collective-permute-start | bytes 196616 | tf_op jit(solution)/shard_map/ppermute | solution.py:220
  26.5 0.8 %collective-permute-start.14 = (f32[128,128]{1,0:T(8,128)S(1)}, f32[128,128]{1,0:T(8,128)S(1)}, u32[]{:S(2)}, u32[]{:S(2)}) collective-permute-start(f32[128,128]{1,0:T(8,128)S(1)} %get-tuple-element.48), channel_id=1, source_target_pairs={{0,3},{1,2},{2,1},{3,0},{4,7},{5,6},{6,5},{7,4},{8,11},{9,10},{10,... | collective-permute-start | bytes 196616 | tf_op jit(solution)/shard_map/ppermute | solution.py:220
  27.3 3.1 %collective-permute-done.13.refs_9_ = f32[128,128]{1,0:T(8,128)S(1)} collective-permute-done((f32[128,128]{1,0:T(8,128)S(1)}, f32[128,128]{1,0:T(8,128)S(1)}, u32[]{:S(2)}, u32[]{:S(2)}) %collective-permute-start.13) | collective-permute-done | bytes 65568 | tf_op jit(solution)/shard_map/ppermute | solution.py:220
  30.4 0.5 collective-permute-done.14.refs_10_
  31.0 0.3 collective-permute-start.19
  31.3 1.0 %collective-permute-start.20 = (bf16[128,128]{1,0:T(8,128)(2,1)S(1)}, bf16[128,128]{1,0:T(8,128)(2,1)S(1)}, u32[]{:S(2)}, u32[]{:S(2)}) collective-permute-start(bf16[128,128]{1,0:T(8,128)(2,1)S(1)} %get-tuple-element.50.refs_1_), channel_id=1, source_target_pairs={{0,2},{1,3},{2,0},{3,1},{4,6},{5,7},{6,4},{7,5},{8,10},{9,11},{10,... | collective-permute-start | bytes 98312 | tf_op jit(solution)/shard_map/ppermute | solution.py:220
  32.3 0.6 %collective-permute-start.21 = (bf16[128,128]{1,0:T(8,128)(2,1)S(1)}, bf16[128,128]{1,0:T(8,128)(2,1)S(1)}, u32[]{:S(2)}, u32[]{:S(2)}) collective-permute-start(bf16[128,128]{1,0:T(8,128)(2,1)S(1)} %get-tuple-element.50.refs_1_), channel_id=1, source_target_pairs={{0,3},{1,2},{2,1},{3,0},{4,7},{5,6},{6,5},{7,4},{8,11},{9,10},{10,... | collective-permute-start | bytes 98312 | tf_op jit(solution)/shard_map/ppermute | solution.py:220
  32.9 1.3 %collective-permute-start.16 = (bf16[128,128]{1,0:T(8,128)(2,1)S(1)}, bf16[128,128]{1,0:T(8,128)(2,1)S(1)}, u32[]{:S(2)}, u32[]{:S(2)}) collective-permute-start(bf16[128,128]{1,0:T(8,128)(2,1)S(1)} %get-tuple-element.49.refs_0_.refs_1_), channel_id=1, source_target_pairs={{0,16},{4,20},{8,24},{12,28},{16,0},{20,4},{24,8},{28,12},{1,17},{... | collective-permute-start | bytes 98312 | tf_op jit(solution)/shard_map/ppermute | solution.py:220
  34.2 3.1 %collective-permute-start.17 = (bf16[128,128]{1,0:T(8,128)(2,1)S(1)}, bf16[128,128]{1,0:T(8,128)(2,1)S(1)}, u32[]{:S(2)}, u32[]{:S(2)}) collective-permute-start(bf16[128,128]{1,0:T(8,128)(2,1)S(1)} %get-tuple-element.49.refs_0_.refs_1_), channel_id=1, source_target_pairs={{0,24},{4,28},{8,16},{12,20},{16,8},{20,12},{24,0},{28,4},{1,25},{... | collective-permute-start | bytes 98312 | tf_op jit(solution)/shard_map/ppermute | solution.py:220
  37.3 0.3 adjoint.3
  37.6 0.8 %collective-permute-start.26 = (bf16[2,128,128]{2,1,0:T(8,128)(2,1)S(1)}, bf16[2,128,128]{2,1,0:T(8,128)(2,1)S(1)}, u32[]{:S(2)}, u32[]{:S(2)}) collective-permute-start(bf16[2,128,128]{2,1,0:T(8,128)(2,1)S(1)} %get-tuple-element.60), channel_id=1, source_target_pairs={{0,4},{4,0},{8,12},{12,8},{16,20},{20,16},{24,28},{28,24},{1,5},{5... | collective-permute-start | bytes 196616 | tf_op jit(solution)/shard_map/ppermute | solution.py:220
  38.4 1.5 %collective-permute-done.17.refs_3_.refs_4_ = bf16[128,128]{1,0:T(8,128)(2,1)S(1)} collective-permute-done((bf16[128,128]{1,0:T(8,128)(2,1)S(1)}, bf16[128,128]{1,0:T(8,128)(2,1)S(1)}, u32[]{:S(2)}, u32[]{:S(2)}) %collective-permute-start.17) | collective-permute-done | bytes 32800 | tf_op jit(solution)/shard_map/ppermute | solution.py:220
  39.9 1.1 %collective-permute-start.18 = (bf16[4,128,128]{2,1,0:T(8,128)(2,1)S(1)}, bf16[4,128,128]{2,1,0:T(8,128)(2,1)S(1)}, u32[]{:S(2)}, u32[]{:S(2)}) collective-permute-start(bf16[4,128,128]{2,1,0:T(8,128)(2,1)S(1)} %pack.3), channel_id=1, source_target_pairs={{0,4},{4,0},{8,12},{12,8},{16,20},{20,16},{24,28},{28,24},{1,5},{5... | collective-permute-start | bytes 393224 | tf_op jit(solution)/shard_map/ppermute | solution.py:220
  41.0 1.0 %collective-permute-start.22 = (bf16[2,128,128]{2,1,0:T(8,128)(2,1)S(1)}, bf16[2,128,128]{2,1,0:T(8,128)(2,1)S(1)}, u32[]{:S(2)}, u32[]{:S(2)}) collective-permute-start(bf16[2,128,128]{2,1,0:T(8,128)(2,1)S(1)} %get-tuple-element.52), channel_id=1, source_target_pairs={{0,4},{4,0},{8,12},{12,8},{16,20},{20,16},{24,28},{28,24},{1,5},{5... | collective-permute-start | bytes 196616 | tf_op jit(solution)/shard_map/ppermute | solution.py:220
  42.0 0.4 collective-permute-done.26.refs_1_
  42.4 0.1 collective-permute-start.27
  42.5 2.8 %collective-permute-start.28 = (bf16[128,128]{1,0:T(8,128)(2,1)S(1)}, bf16[128,128]{1,0:T(8,128)(2,1)S(1)}, u32[]{:S(2)}, u32[]{:S(2)}) collective-permute-start(bf16[128,128]{1,0:T(8,128)(2,1)S(1)} %get-tuple-element.62), channel_id=1, source_target_pairs={{0,24},{4,28},{8,16},{12,20},{16,8},{20,12},{24,0},{28,4},{1,25},{... | collective-permute-start | bytes 98312 | tf_op jit(solution)/shard_map/ppermute | solution.py:220
  45.3 0.9 %collective-permute-done.22.refs_1_ = bf16[2,128,128]{2,1,0:T(8,128)(2,1)S(1)} collective-permute-done((bf16[2,128,128]{2,1,0:T(8,128)(2,1)S(1)}, bf16[2,128,128]{2,1,0:T(8,128)(2,1)S(1)}, u32[]{:S(2)}, u32[]{:S(2)}) %collective-permute-start.22) | collective-permute-done | bytes 65568 | tf_op jit(solution)/shard_map/ppermute | solution.py:220
  46.2 0.1 collective-permute-start.29
  46.3 0.4 forward.3
  46.7 0.1 collective-permute-start.23
  46.8 1.1 %collective-permute-start.24 = (bf16[128,128]{1,0:T(8,128)(2,1)S(1)}, bf16[128,128]{1,0:T(8,128)(2,1)S(1)}, u32[]{:S(2)}, u32[]{:S(2)}) collective-permute-start(bf16[128,128]{1,0:T(8,128)(2,1)S(1)} %get-tuple-element.56), channel_id=1, source_target_pairs={{0,2},{1,3},{2,0},{3,1},{4,6},{5,7},{6,4},{7,5},{8,10},{9,11},{10,... | collective-permute-start | bytes 98312 | tf_op jit(solution)/shard_map/ppermute | solution.py:220
  47.9 0.8 %collective-permute-start.25 = (bf16[128,128]{1,0:T(8,128)(2,1)S(1)}, bf16[128,128]{1,0:T(8,128)(2,1)S(1)}, u32[]{:S(2)}, u32[]{:S(2)}) collective-permute-start(bf16[128,128]{1,0:T(8,128)(2,1)S(1)} %get-tuple-element.57), channel_id=1, source_target_pairs={{0,3},{1,2},{2,1},{3,0},{4,7},{5,6},{6,5},{7,4},{8,11},{9,10},{10,... | collective-permute-start | bytes 98312 | tf_op jit(solution)/shard_map/ppermute | solution.py:220
  48.7 1.5 %collective-permute-done.29.refs_7_ = bf16[128,128]{1,0:T(8,128)(2,1)S(1)} collective-permute-done((bf16[128,128]{1,0:T(8,128)(2,1)S(1)}, bf16[128,128]{1,0:T(8,128)(2,1)S(1)}, u32[]{:S(2)}, u32[]{:S(2)}) %collective-permute-start.29) | collective-permute-done | bytes 32800 | tf_op jit(solution)/shard_map/ppermute | solution.py:220
  50.2 0.7 %adjoint_end.1 = f32[128,128]{1,0:T(8,128)} custom-call(f32[128,128]{1,0:T(8,128)S(1)} %copy-done.1, f32[128,128]{1,0:T(8,128)S(1)} %get-tuple-element.58.refs_1_, f32[1,128]{1,0:T(1,128)S(1)} %get-tuple-element.35.refs_0_.refs_2_, f32[128,128]{1,0:T(8,128)S(1)} %get-tuple-element.33.refs_1_.refs_3_, bf16[128,128]{1,0:T(8,128)(2,1)S(1)} %collective-permute-done.27.refs_4_, ...), custom_call_target="tpu_custom_call" | custom-call | bytes 426496 | tf_op jit(solution)/shard_map/adjoint_end/pallas_call | solution.py:36
  50.9 0.3 collective-permute-done.25.refs_5_
  51.2 0.7 %forward_end.1 = f32[128,128]{1,0:T(8,128)} custom-call(f32[128,128]{1,0:T(8,128)S(1)} %copy-done, f32[128,128]{1,0:T(8,128)S(1)} %get-tuple-element.33.refs_1_.refs_3_, bf16[128,128]{1,0:T(8,128)(2,1)S(1)} %get-tuple-element.54.refs_2_, bf16[128,128]{1,0:T(8,128)(2,1)S(1)} %collective-permute-done.23.refs_3_, ...), custom_call_target="tpu_custom_call" | custom-call | bytes 327680 | tf_op jit(solution)/shard_map/forward_end/pallas_call | solution.py:36
  (31 shorter events, 0.2 us)
Async XLA Ops:
  1.7 5.6 %collective-permute-start = (bf16[128,128]{1,0:T(8,128)(2,1)S(1)}, bf16[128,128]{1,0:T(8,128)(2,1)S(1)}, u32[]{:S(2)}, u32[]{:S(2)}) collective-permute-start(bf16[128,128]{1,0:T(8,128)(2,1)S(1)} %get-tuple-element.34.refs_0_.refs_1_), channel_id=1, source_target_pairs={{0,1},{1,0},{2,3},{3,2},{4,5},{5,4},{6,7},{7,6},{8,9},{9,8},{10,11... | collective-permute-start | bytes 98312 | tf_op jit(solution)/shard_map/ppermute | solution.py:220
  2.2 5.1 %collective-permute-start.1 = (bf16[128,128]{1,0:T(8,128)(2,1)S(1)}, bf16[128,128]{1,0:T(8,128)(2,1)S(1)}, u32[]{:S(2)}, u32[]{:S(2)}) collective-permute-start(bf16[128,128]{1,0:T(8,128)(2,1)S(1)} %get-tuple-element.34.refs_0_.refs_1_), channel_id=1, source_target_pairs={{0,2},{1,3},{2,0},{3,1},{4,6},{5,7},{6,4},{7,5},{8,10},{9,11},{10,... | collective-permute-start | bytes 98312 | tf_op jit(solution)/shard_map/ppermute | solution.py:220
  4.8 3.3 %collective-permute-start.2 = (bf16[128,128]{1,0:T(8,128)(2,1)S(1)}, bf16[128,128]{1,0:T(8,128)(2,1)S(1)}, u32[]{:S(2)}, u32[]{:S(2)}) collective-permute-start(bf16[128,128]{1,0:T(8,128)(2,1)S(1)} %get-tuple-element.34.refs_0_.refs_1_), channel_id=1, source_target_pairs={{0,3},{1,2},{2,1},{3,0},{4,7},{5,6},{6,5},{7,4},{8,11},{9,10},{10,... | collective-permute-start | bytes 98312 | tf_op jit(solution)/shard_map/ppermute | solution.py:220
  8.4 12.0 %collective-permute-start.3 = (f32[2,128,128]{2,1,0:T(8,128)S(1)}, f32[2,128,128]{2,1,0:T(8,128)S(1)}, u32[]{:S(2)}, u32[]{:S(2)}) collective-permute-start(f32[2,128,128]{2,1,0:T(8,128)S(1)} %get-tuple-element.37), channel_id=1, source_target_pairs={{0,4},{4,0},{8,12},{12,8},{16,20},{20,16},{24,28},{28,24},{1,5},{5... | collective-permute-start | bytes 393224 | tf_op jit(solution)/shard_map/ppermute | solution.py:220
  10.0 4.9 %collective-permute-start.8 = (bf16[128,128]{1,0:T(8,128)(2,1)S(1)}, bf16[128,128]{1,0:T(8,128)(2,1)S(1)}, u32[]{:S(2)}, u32[]{:S(2)}) collective-permute-start(bf16[128,128]{1,0:T(8,128)(2,1)S(1)} %get-tuple-element.44.refs_0_.refs_1_), channel_id=1, source_target_pairs={{0,8},{4,12},{8,0},{12,4},{16,24},{20,28},{24,16},{28,20},{1,9},{5... | collective-permute-start | bytes 98312 | tf_op jit(solution)/shard_map/ppermute | solution.py:220
  11.6 5.4 %collective-permute-start.9 = (bf16[128,128]{1,0:T(8,128)(2,1)S(1)}, bf16[128,128]{1,0:T(8,128)(2,1)S(1)}, u32[]{:S(2)}, u32[]{:S(2)}) collective-permute-start(bf16[128,128]{1,0:T(8,128)(2,1)S(1)} %get-tuple-element.44.refs_0_.refs_1_), channel_id=1, source_target_pairs={{0,16},{4,20},{8,24},{12,28},{16,0},{20,4},{24,8},{28,12},{1,17},{... | collective-permute-start | bytes 98312 | tf_op jit(solution)/shard_map/ppermute | solution.py:220
  14.2 5.7 %collective-permute-start.10 = (bf16[128,128]{1,0:T(8,128)(2,1)S(1)}, bf16[128,128]{1,0:T(8,128)(2,1)S(1)}, u32[]{:S(2)}, u32[]{:S(2)}) collective-permute-start(bf16[128,128]{1,0:T(8,128)(2,1)S(1)} %get-tuple-element.44.refs_0_.refs_1_), channel_id=1, source_target_pairs={{0,24},{4,28},{8,16},{12,20},{16,8},{20,12},{24,0},{28,4},{1,25},{... | collective-permute-start | bytes 98312 | tf_op jit(solution)/shard_map/ppermute | solution.py:220
  14.4 7.2 %collective-permute-start.6 = (f32[2,128,128]{2,1,0:T(8,128)S(1)}, f32[2,128,128]{2,1,0:T(8,128)S(1)}, u32[]{:S(2)}, u32[]{:S(2)}) collective-permute-start(f32[2,128,128]{2,1,0:T(8,128)S(1)} %get-tuple-element.41), channel_id=1, source_target_pairs={{0,4},{4,0},{8,12},{12,8},{16,20},{20,16},{24,28},{28,24},{1,5},{5... | collective-permute-start | bytes 393224 | tf_op jit(solution)/shard_map/ppermute | solution.py:220
  19.9 5.0 %collective-permute-start.11 = (bf16[4,128,128]{2,1,0:T(8,128)(2,1)S(1)}, bf16[4,128,128]{2,1,0:T(8,128)(2,1)S(1)}, u32[]{:S(2)}, u32[]{:S(2)}) collective-permute-start(bf16[4,128,128]{2,1,0:T(8,128)(2,1)S(1)} %pack.2), channel_id=1, source_target_pairs={{0,4},{4,0},{8,12},{12,8},{16,20},{20,16},{24,28},{28,24},{1,5},{5... | collective-permute-start | bytes 393224 | tf_op jit(solution)/shard_map/ppermute | solution.py:220
  20.5 6.0 %collective-permute-start.4 = (f32[128,128]{1,0:T(8,128)S(1)}, f32[128,128]{1,0:T(8,128)S(1)}, u32[]{:S(2)}, u32[]{:S(2)}) collective-permute-start(f32[128,128]{1,0:T(8,128)S(1)} %get-tuple-element.38), channel_id=1, source_target_pairs={{0,16},{4,20},{8,24},{12,28},{16,0},{20,4},{24,8},{28,12},{1,17},{... | collective-permute-start | bytes 196616 | tf_op jit(solution)/shard_map/ppermute | solution.py:220
  20.6 6.8 %collective-permute-start.5 = (f32[128,128]{1,0:T(8,128)S(1)}, f32[128,128]{1,0:T(8,128)S(1)}, u32[]{:S(2)}, u32[]{:S(2)}) collective-permute-start(f32[128,128]{1,0:T(8,128)S(1)} %get-tuple-element.39), channel_id=1, source_target_pairs={{0,24},{4,28},{8,16},{12,20},{16,8},{20,12},{24,0},{28,4},{1,25},{... | collective-permute-start | bytes 196616 | tf_op jit(solution)/shard_map/ppermute | solution.py:220
  21.6 5.7 %collective-permute-start.7 = (f32[128,128]{1,0:T(8,128)S(1)}, f32[128,128]{1,0:T(8,128)S(1)}, u32[]{:S(2)}, u32[]{:S(2)}) collective-permute-start(f32[128,128]{1,0:T(8,128)S(1)} %get-tuple-element.43), channel_id=1, source_target_pairs={{0,8},{4,12},{8,0},{12,4},{16,24},{20,28},{24,16},{28,20},{1,9},{5... | collective-permute-start | bytes 196616 | tf_op jit(solution)/shard_map/ppermute | solution.py:220
  24.9 6.0 %copy-start = (f32[128,128]{1,0:T(8,128)S(1)}, f32[128,128]{1,0:T(8,128)}, u32[]{:S(2)}) copy-start(f32[128,128]{1,0:T(8,128)} %refs_0_.4) | copy-start | bytes 196612
  25.4 2.0 %collective-permute-start.12 = (f32[128,128]{1,0:T(8,128)S(1)}, f32[128,128]{1,0:T(8,128)S(1)}, u32[]{:S(2)}, u32[]{:S(2)}) collective-permute-start(f32[128,128]{1,0:T(8,128)S(1)} %get-tuple-element.46), channel_id=1, source_target_pairs={{0,1},{1,0},{2,3},{3,2},{4,5},{5,4},{6,7},{7,6},{8,9},{9,8},{10,11... | collective-permute-start | bytes 196616 | tf_op jit(solution)/shard_map/ppermute | solution.py:220
  25.5 5.0 %collective-permute-start.13 = (f32[128,128]{1,0:T(8,128)S(1)}, f32[128,128]{1,0:T(8,128)S(1)}, u32[]{:S(2)}, u32[]{:S(2)}) collective-permute-start(f32[128,128]{1,0:T(8,128)S(1)} %get-tuple-element.47), channel_id=1, source_target_pairs={{0,2},{1,3},{2,0},{3,1},{4,6},{5,7},{6,4},{7,5},{8,10},{9,11},{10,... | collective-permute-start | bytes 196616 | tf_op jit(solution)/shard_map/ppermute | solution.py:220
  26.5 4.4 %collective-permute-start.14 = (f32[128,128]{1,0:T(8,128)S(1)}, f32[128,128]{1,0:T(8,128)S(1)}, u32[]{:S(2)}, u32[]{:S(2)}) collective-permute-start(f32[128,128]{1,0:T(8,128)S(1)} %get-tuple-element.48), channel_id=1, source_target_pairs={{0,3},{1,2},{2,1},{3,0},{4,7},{5,6},{6,5},{7,4},{8,11},{9,10},{10,... | collective-permute-start | bytes 196616 | tf_op jit(solution)/shard_map/ppermute | solution.py:220
  31.0 3.2 %collective-permute-start.19 = (bf16[128,128]{1,0:T(8,128)(2,1)S(1)}, bf16[128,128]{1,0:T(8,128)(2,1)S(1)}, u32[]{:S(2)}, u32[]{:S(2)}) collective-permute-start(bf16[128,128]{1,0:T(8,128)(2,1)S(1)} %get-tuple-element.50.refs_1_), channel_id=1, source_target_pairs={{0,1},{1,0},{2,3},{3,2},{4,5},{5,4},{6,7},{7,6},{8,9},{9,8},{10,11... | collective-permute-start | bytes 98312 | tf_op jit(solution)/shard_map/ppermute | solution.py:220
  31.3 6.0 %collective-permute-start.20 = (bf16[128,128]{1,0:T(8,128)(2,1)S(1)}, bf16[128,128]{1,0:T(8,128)(2,1)S(1)}, u32[]{:S(2)}, u32[]{:S(2)}) collective-permute-start(bf16[128,128]{1,0:T(8,128)(2,1)S(1)} %get-tuple-element.50.refs_1_), channel_id=1, source_target_pairs={{0,2},{1,3},{2,0},{3,1},{4,6},{5,7},{6,4},{7,5},{8,10},{9,11},{10,... | collective-permute-start | bytes 98312 | tf_op jit(solution)/shard_map/ppermute | solution.py:220
  32.3 5.0 %collective-permute-start.21 = (bf16[128,128]{1,0:T(8,128)(2,1)S(1)}, bf16[128,128]{1,0:T(8,128)(2,1)S(1)}, u32[]{:S(2)}, u32[]{:S(2)}) collective-permute-start(bf16[128,128]{1,0:T(8,128)(2,1)S(1)} %get-tuple-element.50.refs_1_), channel_id=1, source_target_pairs={{0,3},{1,2},{2,1},{3,0},{4,7},{5,6},{6,5},{7,4},{8,11},{9,10},{10,... | collective-permute-start | bytes 98312 | tf_op jit(solution)/shard_map/ppermute | solution.py:220
  32.9 5.5 %collective-permute-start.15 = (bf16[128,128]{1,0:T(8,128)(2,1)S(1)}, bf16[128,128]{1,0:T(8,128)(2,1)S(1)}, u32[]{:S(2)}, u32[]{:S(2)}) collective-permute-start(bf16[128,128]{1,0:T(8,128)(2,1)S(1)} %get-tuple-element.49.refs_0_.refs_1_), channel_id=1, source_target_pairs={{0,8},{4,12},{8,0},{12,4},{16,24},{20,28},{24,16},{28,20},{1,9},{5... | collective-permute-start | bytes 98312 | tf_op jit(solution)/shard_map/ppermute | solution.py:220
  32.9 5.5 %collective-permute-start.16 = (bf16[128,128]{1,0:T(8,128)(2,1)S(1)}, bf16[128,128]{1,0:T(8,128)(2,1)S(1)}, u32[]{:S(2)}, u32[]{:S(2)}) collective-permute-start(bf16[128,128]{1,0:T(8,128)(2,1)S(1)} %get-tuple-element.49.refs_0_.refs_1_), channel_id=1, source_target_pairs={{0,16},{4,20},{8,24},{12,28},{16,0},{20,4},{24,8},{28,12},{1,17},{... | collective-permute-start | bytes 98312 | tf_op jit(solution)/shard_map/ppermute | solution.py:220
  34.2 5.7 %collective-permute-start.17 = (bf16[128,128]{1,0:T(8,128)(2,1)S(1)}, bf16[128,128]{1,0:T(8,128)(2,1)S(1)}, u32[]{:S(2)}, u32[]{:S(2)}) collective-permute-start(bf16[128,128]{1,0:T(8,128)(2,1)S(1)} %get-tuple-element.49.refs_0_.refs_1_), channel_id=1, source_target_pairs={{0,24},{4,28},{8,16},{12,20},{16,8},{20,12},{24,0},{28,4},{1,25},{... | collective-permute-start | bytes 98312 | tf_op jit(solution)/shard_map/ppermute | solution.py:220
  37.6 4.8 %collective-permute-start.26 = (bf16[2,128,128]{2,1,0:T(8,128)(2,1)S(1)}, bf16[2,128,128]{2,1,0:T(8,128)(2,1)S(1)}, u32[]{:S(2)}, u32[]{:S(2)}) collective-permute-start(bf16[2,128,128]{2,1,0:T(8,128)(2,1)S(1)} %get-tuple-element.60), channel_id=1, source_target_pairs={{0,4},{4,0},{8,12},{12,8},{16,20},{20,16},{24,28},{28,24},{1,5},{5... | collective-permute-start | bytes 196616 | tf_op jit(solution)/shard_map/ppermute | solution.py:220
  39.9 6.3 %collective-permute-start.18 = (bf16[4,128,128]{2,1,0:T(8,128)(2,1)S(1)}, bf16[4,128,128]{2,1,0:T(8,128)(2,1)S(1)}, u32[]{:S(2)}, u32[]{:S(2)}) collective-permute-start(bf16[4,128,128]{2,1,0:T(8,128)(2,1)S(1)} %pack.3), channel_id=1, source_target_pairs={{0,4},{4,0},{8,12},{12,8},{16,20},{20,16},{24,28},{28,24},{1,5},{5... | collective-permute-start | bytes 393224 | tf_op jit(solution)/shard_map/ppermute | solution.py:220
  41.0 5.2 %collective-permute-start.22 = (bf16[2,128,128]{2,1,0:T(8,128)(2,1)S(1)}, bf16[2,128,128]{2,1,0:T(8,128)(2,1)S(1)}, u32[]{:S(2)}, u32[]{:S(2)}) collective-permute-start(bf16[2,128,128]{2,1,0:T(8,128)(2,1)S(1)} %get-tuple-element.52), channel_id=1, source_target_pairs={{0,4},{4,0},{8,12},{12,8},{16,20},{20,16},{24,28},{28,24},{1,5},{5... | collective-permute-start | bytes 196616 | tf_op jit(solution)/shard_map/ppermute | solution.py:220
  42.4 5.5 %collective-permute-start.27 = (bf16[128,128]{1,0:T(8,128)(2,1)S(1)}, bf16[128,128]{1,0:T(8,128)(2,1)S(1)}, u32[]{:S(2)}, u32[]{:S(2)}) collective-permute-start(bf16[128,128]{1,0:T(8,128)(2,1)S(1)} %get-tuple-element.61), channel_id=1, source_target_pairs={{0,16},{4,20},{8,24},{12,28},{16,0},{20,4},{24,8},{28,12},{1,17},{... | collective-permute-start | bytes 98312 | tf_op jit(solution)/shard_map/ppermute | solution.py:220
  42.5 6.2 %collective-permute-start.28 = (bf16[128,128]{1,0:T(8,128)(2,1)S(1)}, bf16[128,128]{1,0:T(8,128)(2,1)S(1)}, u32[]{:S(2)}, u32[]{:S(2)}) collective-permute-start(bf16[128,128]{1,0:T(8,128)(2,1)S(1)} %get-tuple-element.62), channel_id=1, source_target_pairs={{0,24},{4,28},{8,16},{12,20},{16,8},{20,12},{24,0},{28,4},{1,25},{... | collective-permute-start | bytes 98312 | tf_op jit(solution)/shard_map/ppermute | solution.py:220
  46.2 4.0 %collective-permute-start.29 = (bf16[128,128]{1,0:T(8,128)(2,1)S(1)}, bf16[128,128]{1,0:T(8,128)(2,1)S(1)}, u32[]{:S(2)}, u32[]{:S(2)}) collective-permute-start(bf16[128,128]{1,0:T(8,128)(2,1)S(1)} %get-tuple-element.63), channel_id=1, source_target_pairs={{0,8},{4,12},{8,0},{12,4},{16,24},{20,28},{24,16},{28,20},{1,9},{5... | collective-permute-start | bytes 98312 | tf_op jit(solution)/shard_map/ppermute | solution.py:220
  46.3 3.9 %copy-start.1 = (f32[128,128]{1,0:T(8,128)S(1)}, f32[128,128]{1,0:T(8,128)}, u32[]{:S(2)}) copy-start(f32[128,128]{1,0:T(8,128)} %refs_0_.5) | copy-start | bytes 196612
  46.7 4.2 %collective-permute-start.23 = (bf16[128,128]{1,0:T(8,128)(2,1)S(1)}, bf16[128,128]{1,0:T(8,128)(2,1)S(1)}, u32[]{:S(2)}, u32[]{:S(2)}) collective-permute-start(bf16[128,128]{1,0:T(8,128)(2,1)S(1)} %get-tuple-element.55), channel_id=1, source_target_pairs={{0,1},{1,0},{2,3},{3,2},{4,5},{5,4},{6,7},{7,6},{8,9},{9,8},{10,11... | collective-permute-start | bytes 98312 | tf_op jit(solution)/shard_map/ppermute | solution.py:220
  46.8 4.1 %collective-permute-start.24 = (bf16[128,128]{1,0:T(8,128)(2,1)S(1)}, bf16[128,128]{1,0:T(8,128)(2,1)S(1)}, u32[]{:S(2)}, u32[]{:S(2)}) collective-permute-start(bf16[128,128]{1,0:T(8,128)(2,1)S(1)} %get-tuple-element.56), channel_id=1, source_target_pairs={{0,2},{1,3},{2,0},{3,1},{4,6},{5,7},{6,4},{7,5},{8,10},{9,11},{10,... | collective-permute-start | bytes 98312 | tf_op jit(solution)/shard_map/ppermute | solution.py:220
  47.9 3.3 %collective-permute-start.25 = (bf16[128,128]{1,0:T(8,128)(2,1)S(1)}, bf16[128,128]{1,0:T(8,128)(2,1)S(1)}, u32[]{:S(2)}, u32[]{:S(2)}) collective-permute-start(bf16[128,128]{1,0:T(8,128)(2,1)S(1)} %get-tuple-element.57), channel_id=1, source_target_pairs={{0,3},{1,2},{2,1},{3,0},{4,7},{5,6},{6,5},{7,4},{8,11},{9,10},{10,... | collective-permute-start | bytes 98312 | tf_op jit(solution)/shard_map/ppermute | solution.py:220

commit v9 on v8

--- a/solution.py
+++ b/solution.py
@@ -141,26 +141,40 @@
 
 
 def adjoint_body(n_rows, n_cols, dense_ref, *refs):
-    blocks, outs = refs[:n_cols], refs[n_cols:]
+    blocks, through, outs = refs[:2], refs[2:-4], refs[-4:]
     send_far, send_near, keep_far, keep_near = outs
+    for source, target in zip(through[: len(through) // 2], through[len(through) // 2 :]):
+        target[...] = source[...]
     half = n_rows // 2
-    near = send_near.shape[0]
-    size = blocks[0].shape[1]
-    left = jnp.concatenate([b[...] for b in blocks], axis=1)
-    for zz in reversed(range(half)):
+    size = dense_ref.shape[1] // n_rows
+    left = jnp.concatenate([block_at(blocks, n_cols, j) for j in range(n_cols)], axis=1)
+    for zz in [*range(1, half, 2), *range(0, half, 2)]:
         part = jnp.dot(
             left, dense_ref[:, 2 * zz * size : (2 * zz + 2) * size], preferred_element_type=F32
         )
-        keep, send, at = (
-            (keep_near, send_near, zz) if zz < near else (keep_far, send_far, zz - near)
-        )
-        keep[at] = part[:, :size]
-        send[at] = part[:, size:].astype(send.dtype)
-
-
-def add_body(keep_ref, got_ref, *outs):
-    for at, out in enumerate(outs):
-        out[...] = (keep_ref[at] + got_ref[at].astype(F32)).astype(out.dtype)
+        keep, send = (keep_far, send_far) if zz % 2 else (keep_near, send_near)
+        keep[zz // 2] = part[:, :size]
+        send[zz // 2] = part[:, size:].astype(send.dtype)
+
+
+def block_at(blocks, count, index):
+    packed, other = blocks
+    return other[index // 2] if index % 2 else packed[index // 2]
+
+
+def add_body(keep_ref, got_ref, out_ref):
+    for at in range(out_ref.shape[0]):
+        out_ref[at] = (keep_ref[at] + got_ref[at].astype(F32)).astype(out_ref.dtype)
+
+
+def fold_body(*refs):
+    *terms, own_ref, send_ref = refs
+    for at in range(terms[0].shape[0]):
+        total = terms[0][at].astype(F32)
+        for term in terms[1:]:
+            total = total + term[at].astype(F32)
+        out_ref = send_ref if at % 2 else own_ref
+        out_ref[at // 2] = total.astype(out_ref.dtype)
 
 
 def pack_body(*refs):
@@ -170,7 +184,7 @@
 
 
 def forward_body(half, n_cols, dense_ref, *refs):
-    panels, other_ref, outs = refs[:half], refs[half], refs[half + 1 :]
+    panels, other_ref, keep_ref, send_ref = refs[:half], refs[half], refs[half + 1], refs[half + 2]
     size = other_ref.shape[-1]
     total = None
     for zz in range(half):
@@ -180,11 +194,12 @@
         )
         total = part if total is None else total + part
     for j in range(n_cols):
-        outs[j][...] = total[j * size : (j + 1) * size].astype(outs[j].dtype)
+        out_ref = send_ref if j % 2 else keep_ref
+        out_ref[j // 2] = total[j * size : (j + 1) * size]
 
 
 def sum_refs(refs):
-    terms = [ref[...].astype(F32) for ref in refs]
+    terms = [ref[0].astype(F32) for ref in refs]
     while len(terms) > 1:
         terms = [sum(terms[i : i + 2][1:], terms[i]) for i in range(0, len(terms), 2)]
     return terms[0]
@@ -197,14 +212,13 @@
     out_ref[...] = value.astype(out_ref.dtype)
 
 
-def middle_body(half, row_ref, column_ref, h_ref, *refs):
-    back, refs = refs[:half], refs[half:]
-    *first, d_ref, q_ref, p_ref = refs
-    total = sum_refs(back)
+def middle_body(row_ref, column_ref, h_ref, *refs):
+    d_own, d_got, y_own, y_got, d_ref, q_ref, p_ref = refs
+    total = sum_refs((d_own, d_got))
     d_ref[...] = total
     q_ref[...] = ((1.0 - row_ref[...]) * total).astype(BF16)
     rate = column_ref[...]
-    p_ref[...] = ((1.0 - rate) * sum_refs(first) + rate * h_ref[...]).astype(BF16)
+    p_ref[...] = ((1.0 - rate) * sum_refs((y_own, y_got)) + rate * h_ref[...]).astype(BF16)
 
 
 def adjoint_end_body(cot_ref, d_ref, row_ref, column_ref, *refs):
@@ -213,7 +227,8 @@
     out_ref[...] = column_ref[...] * cot_ref[...] + change
 
 
-ADD_COST = 400_000_000
+ADD_COST = 800_000_000
+FIRST_COST = 300_000_000
 
 
 def send(value, axis, count, step):
@@ -224,7 +239,6 @@
     n_rows = lax.axis_size("rows")
     n_cols = lax.axis_size("cols")
     half = n_rows // 2
-    near = half // 2
     size = tile_values.shape[-1]
     slots = tile_values.shape[2]
     features = h_start.shape[-1]
@@ -264,72 +278,81 @@
         ],
     )
 
-    def add(keep, got, kinds, name, after=()):
-        outs = [shape(kind) for kind in kinds]
-        hint = ADD_COST if kinds[-1] == BF16 else 0
-        return call(add_body, outs, [vmem()] * 2, (keep, got), hint, name, after=after)
-
-    def adjoint_hop(part, kind):
-        blocks = [part] + [send(part, "cols", n_cols, s) for s in range(1, n_cols)]
-        send_far, send_near, keep_far, keep_near = call(
+    def pack(parts, after=()):
+        outs = [shape(BF16, len(parts))]
+        return call(pack_body, outs, [vmem()] * len(parts), parts, 0, "pack", after=after)[0]
+
+    def fold(terms, kind, name, cost):
+        count = terms[0].shape[0] // 2
+        outs = [shape(F32, count), shape(kind, count)]
+        return call(fold_body, outs, [vmem()] * len(terms), terms, cost, name)
+
+    def adjoint_hop(part, kind, cost, after=(), through=()):
+        packed = pack([part, send(part, "cols", n_cols, 2)], after)
+        other = send(packed, "cols", n_cols, 1)
+        *through, send_far, send_near, keep_far, keep_near = call(
             lambda *refs: adjoint_body(n_rows, n_cols, *refs),
-            [shape(kind, half - near), shape(kind, near)]
-            + [shape(F32, half - near), shape(F32, near)],
-            [vmem()] * (1 + n_cols),
-            [dense, *blocks],
+            [shape(BF16)] * len(through)
+            + [shape(kind, half // 2)] * 2
+            + [shape(F32, half // 2)] * 2,
+            [vmem()] * (3 + len(through)),
+            [dense, packed, other, *through],
             hop_flops,
             "adjoint",
         )
-        far = add(keep_far, send(send_far, "rows", n_rows, 1), [kind] * (half - near), "add_far")
-        far = [send(far[s - near], "rows", n_rows, 2 * s) for s in range(near, half)]
-        kinds = [F32] + [kind] * (near - 1)
-        close = add(keep_near, send(send_near, "rows", n_rows, 1), kinds, "add_near")
-        close = [close[0]] + [send(close[s], "rows", n_rows, 2 * s) for s in range(1, near)]
-        return far + close, close[:1]
-
-    def forward_hop(part, kind, after):
+        got = send(send_far, "rows", n_rows, 1)
+        (far,) = call(
+            add_body, [shape(kind, half // 2)], [vmem()] * 2, (keep_far, got), cost, "add_far"
+        )
+        order = [far]
+        far = send(far, "rows", n_rows, 2)
+        near = send(send_near, "rows", n_rows, 1)
+        own, sent = fold([keep_near, near, far], kind, "add_near", cost)
+        step = 4
+        while own.shape[0] > 1:
+            own, sent = fold([own, send(sent, "rows", n_rows, step)], kind, "add_rows", 0)
+            step *= 2
+        return (own, send(sent, "rows", n_rows, step)), through, order
+
+    def forward_hop(part, kind, after=()):
         panels = [part] + [send(part, "rows", n_rows, 2 * s) for s in range(1, half)]
-        (packed,) = call(pack_body, [shape(BF16, half)], [vmem()] * half, panels, 0, "pack")
-        panels = panels + [send(packed, "rows", n_rows, 1)]
-        sums = call(
+        other = send(pack(panels), "rows", n_rows, 1)
+        keep, sent = call(
             lambda *refs: forward_body(half, n_cols, *refs),
-            [shape(kind)] * n_cols,
-            [vmem()] * (1 + len(panels)),
-            [dense, *panels],
+            [shape(F32, n_cols // 2)] * 2,
+            [vmem()] * (2 + half),
+            [dense, *panels, other],
             hop_flops,
             "forward",
             after=after,
         )
-        return [sums[0]] + [send(sums[s], "cols", n_cols, s) for s in range(1, n_cols)]
-
-    def forward_end(parts, kind, after=()):
-        return call(
-            forward_end_body,
-            [shape(kind)],
-            [vmem()] * (2 + n_cols),
-            (h_start, column, *parts),
-            0,
-            "forward_end",
-            after=after,
-        )[0]
-
-    back, last = adjoint_hop(q0, F32)
-    first = forward_hop(p0, F32, last)
+        own, sent = fold([keep, send(sent, "cols", n_cols, 1)], kind, "add_cols", 0)
+        return own, send(sent, "cols", n_cols, 2)
+
+    back, (p0,), order = adjoint_hop(q0, F32, FIRST_COST, [dense], [p0])
+    first = forward_hop(p0, F32, order)
     d1, q1, p1 = call(
-        lambda *refs: middle_body(half, *refs),
+        middle_body,
         [shape(F32), shape(BF16), shape(BF16)],
-        [vmem()] * (3 + half + n_cols),
+        [vmem()] * 7,
         (rate, column, h_start, *back, *first),
         0,
         "middle",
     )
-    back_two, last = adjoint_hop(q1, BF16)
-    second = forward_hop(p1, BF16, last)
-    propagated = forward_end(second, F32)
+    back_two, _, order = adjoint_hop(q1, BF16, ADD_COST)
+    second = forward_hop(p1, BF16, order)
+    (propagated,) = call(
+        forward_end_body,
+        [shape(F32)],
+        [vmem()] * 4,
+        (h_start, column, *second),
+        0,
+        "forward_end",
+    )
     (input_grad,) = call(
         adjoint_end_body,
         [shape(F32)],
-        [vmem()] * (4 + half),
+        [vmem()] * 6,
         (cotangent, d1, rate, column, *back_two),
         0,
         "adjoint_end",

time: 52.1 us -> 57.9 us (1.11)
  waiting for transfers between devices: 14.8 us -> 26.2 us
  starting transfers between devices: 29.8 us -> 23.8 us
    ppermute x30 -> x24, waiting for transfers between devices: 14.8 us -> 26.2 us  [send(): return lax.ppermute(value, axis, [(i, i ^ step) for i in range(count)])]
    ppermute x30 -> x24, starting transfers between devices: 29.8 us -> 23.8 us  [send(): return lax.ppermute(value, axis, [(i, i ^ step) for i in range(count)])]
    pallas_call x15 -> x19, Pallas kernels: 5.88 us -> 5.93 us  [call(): pl.pallas_call(ordered, out_shape=outs, in_specs=[*in_specs, *[pl.BlockSp...]
  transfers between devices with their start and end apart: 30 -> 24, of which waited for: 11 -> 13; matrix products, arithmetic and copies ran while one was open for 0% -> 0% of each run, Pallas kernels for 7% -> 7%
where the time goes in v9:
time: 57.9 us; the launch traced here: 57.5 us
  waiting for transfers between devices  26.2 us (45%)
  starting transfers between devices  23.8 us (41%)
  Pallas kernels  5.93 us (10%)
  between operations  1.46 us (3%)
    ppermute x24, waiting for transfers between devices, send(): return lax.ppermute(value, axis, [(i, i ^ step) for i in range(count)])  26.2 us
    ppermute x24, starting transfers between devices, send(): return lax.ppermute(value, axis, [(i, i ^ step) for i in range(count)])  23.8 us
    pallas_call x19, Pallas kernels, call(): pl.pallas_call(ordered, out_shape=outs, in_specs=[*in_specs, *[pl.BlockSp...  5.93 us
  transfers between devices with their start and end apart: 24, of which 13 were waited for; matrix products, arithmetic and copies ran while one was open for 0% of the time, Pallas kernels for 7%

profile of v9, /device:TPU:0, one launch (start us, length us, event | category | flops | bytes accessed | tf_op | source)
XLA Modules:
  0.0 57.5 jit_solution(7897520303848515479)
XLA Ops:
  0.6 1.0 %start.1 = (bf16[128,128]{1,0:T(8,128)(2,1)S(1)}, bf16[128,128]{1,0:T(8,128)(2,1)S(1)}, f32[1,128]{1,0:T(1,128)S(1)}, f32[128,128]{1,0:T(8,128)S(1)}) custom-call(f32[128,128]{1,0:T(8,128)} %refs_0_.5, f32[128,128]{1,0:T(8,128)} %refs_0_.4, s32[1,128]{1,0:T(1,128)} %bitcast.1, f32[8]{0:T(128)} %refs_3_.2), custom_call_target="tpu_custom_call" | custom-call | bytes 263200 | tf_op jit(solution)/shard_map/start/pallas_call | solution.py:36
  1.7 3.0 %collective-permute-start = (bf16[128,128]{1,0:T(8,128)(2,1)S(1)}, bf16[128,128]{1,0:T(8,128)(2,1)S(1)}, u32[]{:S(2)}, u32[]{:S(2)}) collective-permute-start(bf16[128,128]{1,0:T(8,128)(2,1)S(1)} %get-tuple-element.31.refs_0_), channel_id=1, source_target_pairs={{0,2},{1,3},{2,0},{3,1},{4,6},{5,7},{6,4},{7,5},{8,10},{9,11},{10,... | collective-permute-start | bytes 98312 | tf_op jit(solution)/shard_map/ppermute | solution.py:235
  5.3 1.8 %dense.1.refs_2_.refs_0_ = bf16[512,1024]{1,0:T(8,128)(2,1)S(1)} custom-call(bf16[128,128]{1,0:T(8,128)(2,1)S(1)} %get-tuple-element.31.refs_0_, bf16[1,1,24,128,128]{4,3,2,1,0:T(8,128)(2,1)} %refs_1_.3, s32[1,1,24]{2,1,0:T(1,128)} %refs_2_.2, s32[1,1,24]{2,1,0:T(1,128)} %refs_3_.3, s32[1,1]{1,0:T(1,128)S(6)} %copy.10.refs_4_), custom_call_target="tpu_custom_call" | custom-call | bytes 1867972 | tf_op jit(solution)/shard_map/dense/pallas_call | solution.py:36
  7.2 0.0 collective-permute-done.refs_1_
  7.2 0.1 collective-permute-start.1
  7.3 1.2 %collective-permute-done.1.refs_2_ = bf16[2,128,128]{2,1,0:T(8,128)(2,1)S(1)} collective-permute-done((bf16[2,128,128]{2,1,0:T(8,128)(2,1)S(1)}, bf16[2,128,128]{2,1,0:T(8,128)(2,1)S(1)}, u32[]{:S(2)}, u32[]{:S(2)}) %collective-permute-start.1) | collective-permute-done | bytes 65568 | tf_op jit(solution)/shard_map/ppermute | solution.py:235
  8.5 0.3 adjoint.2
  8.8 1.5 %collective-permute-start.3 = (f32[2,128,128]{2,1,0:T(8,128)S(1)}, f32[2,128,128]{2,1,0:T(8,128)S(1)}, u32[]{:S(2)}, u32[]{:S(2)}) collective-permute-start(f32[2,128,128]{2,1,0:T(8,128)S(1)} %get-tuple-element.37), channel_id=1, source_target_pairs={{0,4},{4,0},{8,12},{12,8},{16,20},{20,16},{24,28},{28,24},{1,5},{5... | collective-permute-start | bytes 393224 | tf_op jit(solution)/shard_map/ppermute | solution.py:235
  10.4 1.5 %collective-permute-start.6 = (bf16[128,128]{1,0:T(8,128)(2,1)S(1)}, bf16[128,128]{1,0:T(8,128)(2,1)S(1)}, u32[]{:S(2)}, u32[]{:S(2)}) collective-permute-start(bf16[128,128]{1,0:T(8,128)(2,1)S(1)} %get-tuple-element.40.refs_0_.refs_1_), channel_id=1, source_target_pairs={{0,8},{4,12},{8,0},{12,4},{16,24},{20,28},{24,16},{28,20},{1,9},{5... | collective-permute-start | bytes 98312 | tf_op jit(solution)/shard_map/ppermute | solution.py:235
  11.9 2.7 %collective-permute-start.7 = (bf16[128,128]{1,0:T(8,128)(2,1)S(1)}, bf16[128,128]{1,0:T(8,128)(2,1)S(1)}, u32[]{:S(2)}, u32[]{:S(2)}) collective-permute-start(bf16[128,128]{1,0:T(8,128)(2,1)S(1)} %get-tuple-element.40.refs_0_.refs_1_), channel_id=1, source_target_pairs={{0,16},{4,20},{8,24},{12,28},{16,0},{20,4},{24,8},{28,12},{1,17},{... | collective-permute-start | bytes 98312 | tf_op jit(solution)/shard_map/ppermute | solution.py:235
  14.6 0.2 collective-permute-start.8
  14.8 0.0 collective-permute-done.6.refs_1_.refs_2_
  14.8 2.6 %collective-permute-done.7.refs_2_.refs_3_ = bf16[128,128]{1,0:T(8,128)(2,1)S(1)} collective-permute-done((bf16[128,128]{1,0:T(8,128)(2,1)S(1)}, bf16[128,128]{1,0:T(8,128)(2,1)S(1)}, u32[]{:S(2)}, u32[]{:S(2)}) %collective-permute-start.7) | collective-permute-done | bytes 32800 | tf_op jit(solution)/shard_map/ppermute | solution.py:235
  17.4 2.9 %collective-permute-done.8.refs_3_.refs_4_ = bf16[128,128]{1,0:T(8,128)(2,1)S(1)} collective-permute-done((bf16[128,128]{1,0:T(8,128)(2,1)S(1)}, bf16[128,128]{1,0:T(8,128)(2,1)S(1)}, u32[]{:S(2)}, u32[]{:S(2)}) %collective-permute-start.8) | collective-permute-done | bytes 32800 | tf_op jit(solution)/shard_map/ppermute | solution.py:235
  20.3 0.5 collective-permute-start.9
  20.8 1.6 %collective-permute-start.2 = (f32[2,128,128]{2,1,0:T(8,128)S(1)}, f32[2,128,128]{2,1,0:T(8,128)S(1)}, u32[]{:S(2)}, u32[]{:S(2)}) collective-permute-start(f32[2,128,128]{2,1,0:T(8,128)S(1)} %get-tuple-element.35), channel_id=1, source_target_pairs={{0,4},{4,0},{8,12},{12,8},{16,20},{20,16},{24,28},{28,24},{1,5},{5... | collective-permute-start | bytes 393224 | tf_op jit(solution)/shard_map/ppermute | solution.py:235
  22.4 0.0 collective-permute-done.3.refs_1_
  22.4 0.1 collective-permute-start.4
  22.5 2.9 %collective-permute-done.9.refs_5_ = bf16[4,128,128]{2,1,0:T(8,128)(2,1)S(1)} collective-permute-done((bf16[4,128,128]{2,1,0:T(8,128)(2,1)S(1)}, bf16[4,128,128]{2,1,0:T(8,128)(2,1)S(1)}, u32[]{:S(2)}, u32[]{:S(2)}) %collective-permute-start.9) | collective-permute-done | bytes 131104 | tf_op jit(solution)/shard_map/ppermute | solution.py:235
  25.4 0.4 forward.2
  25.9 0.1 collective-permute-start.10
  25.9 0.9 %collective-permute-done.2.refs_1_ = f32[2,128,128]{2,1,0:T(8,128)S(1)} collective-permute-done((f32[2,128,128]{2,1,0:T(8,128)S(1)}, f32[2,128,128]{2,1,0:T(8,128)S(1)}, u32[]{:S(2)}, u32[]{:S(2)}) %collective-permute-start.2) | collective-permute-done | bytes 131104 | tf_op jit(solution)/shard_map/ppermute | solution.py:235
  26.8 0.6 %collective-permute-done.4.refs_2_ = f32[2,128,128]{2,1,0:T(8,128)S(1)} collective-permute-done((f32[2,128,128]{2,1,0:T(8,128)S(1)}, f32[2,128,128]{2,1,0:T(8,128)S(1)}, u32[]{:S(2)}, u32[]{:S(2)}) %collective-permute-start.4) | collective-permute-done | bytes 131104 | tf_op jit(solution)/shard_map/ppermute | solution.py:235
  27.5 0.1 collective-permute-start.5
  27.6 0.0 copy-start
  27.6 1.4 %collective-permute-start.11 = (f32[1,128,128]{2,1,0:T(8,128)S(1)}, f32[1,128,128]{2,1,0:T(8,128)S(1)}, u32[]{:S(2)}, u32[]{:S(2)}) collective-permute-start(f32[1,128,128]{2,1,0:T(8,128)S(1)} %get-tuple-element.44), channel_id=1, source_target_pairs={{0,2},{1,3},{2,0},{3,1},{4,6},{5,7},{6,4},{7,5},{8,10},{9,11},{10,... | collective-permute-start | bytes 196616 | tf_op jit(solution)/shard_map/ppermute | solution.py:235
  29.0 3.8 %collective-permute-done.5.refs_4_ = f32[1,128,128]{2,1,0:T(8,128)S(1)} collective-permute-done((f32[1,128,128]{2,1,0:T(8,128)S(1)}, f32[1,128,128]{2,1,0:T(8,128)S(1)}, u32[]{:S(2)}, u32[]{:S(2)}) %collective-permute-start.5) | collective-permute-done | bytes 65568 | tf_op jit(solution)/shard_map/ppermute | solution.py:235
  32.9 1.4 %collective-permute-start.16 = (bf16[128,128]{1,0:T(8,128)(2,1)S(1)}, bf16[128,128]{1,0:T(8,128)(2,1)S(1)}, u32[]{:S(2)}, u32[]{:S(2)}) collective-permute-start(bf16[128,128]{1,0:T(8,128)(2,1)S(1)} %get-tuple-element.46.refs_0_), channel_id=1, source_target_pairs={{0,2},{1,3},{2,0},{3,1},{4,6},{5,7},{6,4},{7,5},{8,10},{9,11},{10,... | collective-permute-start | bytes 98312 | tf_op jit(solution)/shard_map/ppermute | solution.py:235
  34.3 2.6 %collective-permute-done.16.refs_1_ = bf16[128,128]{1,0:T(8,128)(2,1)S(1)} collective-permute-done((bf16[128,128]{1,0:T(8,128)(2,1)S(1)}, bf16[128,128]{1,0:T(8,128)(2,1)S(1)}, u32[]{:S(2)}, u32[]{:S(2)}) %collective-permute-start.16) | collective-permute-done | bytes 32800 | tf_op jit(solution)/shard_map/ppermute | solution.py:235
  36.9 0.1 collective-permute-start.12
  37.0 2.0 %collective-permute-start.13 = (bf16[128,128]{1,0:T(8,128)(2,1)S(1)}, bf16[128,128]{1,0:T(8,128)(2,1)S(1)}, u32[]{:S(2)}, u32[]{:S(2)}) collective-permute-start(bf16[128,128]{1,0:T(8,128)(2,1)S(1)} %get-tuple-element.45.refs_0_.refs_1_), channel_id=1, source_target_pairs={{0,16},{4,20},{8,24},{12,28},{16,0},{20,4},{24,8},{28,12},{1,17},{... | collective-permute-start | bytes 98312 | tf_op jit(solution)/shard_map/ppermute | solution.py:235
  39.0 2.3 %collective-permute-start.14 = (bf16[128,128]{1,0:T(8,128)(2,1)S(1)}, bf16[128,128]{1,0:T(8,128)(2,1)S(1)}, u32[]{:S(2)}, u32[]{:S(2)}) collective-permute-start(bf16[128,128]{1,0:T(8,128)(2,1)S(1)} %get-tuple-element.45.refs_0_.refs_1_), channel_id=1, source_target_pairs={{0,24},{4,28},{8,16},{12,20},{16,8},{20,12},{24,0},{28,4},{1,25},{... | collective-permute-start | bytes 98312 | tf_op jit(solution)/shard_map/ppermute | solution.py:235
  41.3 0.3 adjoint.3
  41.7 0.5 collective-permute-start.18
  42.2 2.5 %collective-permute-done.14.refs_3_.refs_4_ = bf16[128,128]{1,0:T(8,128)(2,1)S(1)} collective-permute-done((bf16[128,128]{1,0:T(8,128)(2,1)S(1)}, bf16[128,128]{1,0:T(8,128)(2,1)S(1)}, u32[]{:S(2)}, u32[]{:S(2)}) %collective-permute-start.14) | collective-permute-done | bytes 32800 | tf_op jit(solution)/shard_map/ppermute | solution.py:235
  44.7 0.5 collective-permute-start.15
  45.3 1.6 %collective-permute-start.21 = (bf16[2,128,128]{2,1,0:T(8,128)(2,1)S(1)}, bf16[2,128,128]{2,1,0:T(8,128)(2,1)S(1)}, u32[]{:S(2)}, u32[]{:S(2)}) collective-permute-start(bf16[2,128,128]{2,1,0:T(8,128)(2,1)S(1)} %get-tuple-element.55), channel_id=1, source_target_pairs={{0,4},{4,0},{8,12},{12,8},{16,20},{20,16},{24,28},{28,24},{1,5},{5... | collective-permute-start | bytes 196616 | tf_op jit(solution)/shard_map/ppermute | solution.py:235
  46.8 0.2 collective-permute-start.22
  47.0 2.8 %collective-permute-done.15.refs_5_ = bf16[4,128,128]{2,1,0:T(8,128)(2,1)S(1)} collective-permute-done((bf16[4,128,128]{2,1,0:T(8,128)(2,1)S(1)}, bf16[4,128,128]{2,1,0:T(8,128)(2,1)S(1)}, u32[]{:S(2)}, u32[]{:S(2)}) %collective-permute-start.15) | collective-permute-done | bytes 131104 | tf_op jit(solution)/shard_map/ppermute | solution.py:235
  49.9 0.4 forward.3
  50.3 0.1 collective-permute-start.19
  50.4 0.2 collective-permute-done.21.refs_1_
  50.6 0.6 %collective-permute-done.22.refs_2_ = bf16[2,128,128]{2,1,0:T(8,128)(2,1)S(1)} collective-permute-done((bf16[2,128,128]{2,1,0:T(8,128)(2,1)S(1)}, bf16[2,128,128]{2,1,0:T(8,128)(2,1)S(1)}, u32[]{:S(2)}, u32[]{:S(2)}) %collective-permute-start.22) | collective-permute-done | bytes 65568 | tf_op jit(solution)/shard_map/ppermute | solution.py:235
  51.2 0.9 %collective-permute-start.23 = (bf16[1,128,128]{2,1,0:T(8,128)(2,1)S(1)}, bf16[1,128,128]{2,1,0:T(8,128)(2,1)S(1)}, u32[]{:S(2)}, u32[]{:S(2)}) collective-permute-start(bf16[1,128,128]{2,1,0:T(8,128)(2,1)S(1)} %get-tuple-element.57), channel_id=1, source_target_pairs={{0,16},{4,20},{8,24},{12,28},{16,0},{20,4},{24,8},{28,12},{1,17},{... | collective-permute-start | bytes 98312 | tf_op jit(solution)/shard_map/ppermute | solution.py:235
  52.2 1.4 %collective-permute-start.20 = (bf16[1,128,128]{2,1,0:T(8,128)(2,1)S(1)}, bf16[1,128,128]{2,1,0:T(8,128)(2,1)S(1)}, u32[]{:S(2)}, u32[]{:S(2)}) collective-permute-start(bf16[1,128,128]{2,1,0:T(8,128)(2,1)S(1)} %get-tuple-element.52), channel_id=1, source_target_pairs={{0,2},{1,3},{2,0},{3,1},{4,6},{5,7},{6,4},{7,5},{8,10},{9,11},{10,... | collective-permute-start | bytes 98312 | tf_op jit(solution)/shard_map/ppermute | solution.py:235
  53.6 2.5 %collective-permute-done.23.refs_5_ = bf16[1,128,128]{2,1,0:T(8,128)(2,1)S(1)} collective-permute-done((bf16[1,128,128]{2,1,0:T(8,128)(2,1)S(1)}, bf16[1,128,128]{2,1,0:T(8,128)(2,1)S(1)}, u32[]{:S(2)}, u32[]{:S(2)}) %collective-permute-start.23) | collective-permute-done | bytes 32800 | tf_op jit(solution)/shard_map/ppermute | solution.py:235
  56.1 0.7 %adjoint_end.1 = f32[128,128]{1,0:T(8,128)} custom-call(f32[128,128]{1,0:T(8,128)S(1)} %copy-done.1, f32[128,128]{1,0:T(8,128)S(1)} %get-tuple-element.53.refs_1_, f32[1,128]{1,0:T(1,128)S(1)} %get-tuple-element.32.refs_0_.refs_2_, f32[128,128]{1,0:T(8,128)S(1)} %get-tuple-element.30.refs_1_.refs_3_, f32[1,128,128]{2,1,0:T(8,128)S(1)} %get-tuple-element.56.refs_4_, ...), custom_call_target="tpu_custom_call" | custom-call | bytes 360960 | tf_op jit(solution)/shard_map/adjoint_end/pallas_call | solution.py:36
  56.8 0.6 %forward_end.1 = f32[128,128]{1,0:T(8,128)} custom-call(f32[128,128]{1,0:T(8,128)S(1)} %copy-done, f32[128,128]{1,0:T(8,128)S(1)} %get-tuple-element.30.refs_1_.refs_3_, f32[1,128,128]{2,1,0:T(8,128)S(1)} %get-tuple-element.51.refs_2_, bf16[1,128,128]{2,1,0:T(8,128)(2,1)S(1)} %collective-permute-done.20.refs_3_), custom_call_target="tpu_custom_call" | custom-call | bytes 294912 | tf_op jit(solution)/shard_map/forward_end/pallas_call | solution.py:36
  (23 shorter events, 0.2 us)
Async XLA Ops:
  1.7 5.5 %collective-permute-start = (bf16[128,128]{1,0:T(8,128)(2,1)S(1)}, bf16[128,128]{1,0:T(8,128)(2,1)S(1)}, u32[]{:S(2)}, u32[]{:S(2)}) collective-permute-start(bf16[128,128]{1,0:T(8,128)(2,1)S(1)} %get-tuple-element.31.refs_0_), channel_id=1, source_target_pairs={{0,2},{1,3},{2,0},{3,1},{4,6},{5,7},{6,4},{7,5},{8,10},{9,11},{10,... | collective-permute-start | bytes 98312 | tf_op jit(solution)/shard_map/ppermute | solution.py:235
  7.2 1.3 %collective-permute-start.1 = (bf16[2,128,128]{2,1,0:T(8,128)(2,1)S(1)}, bf16[2,128,128]{2,1,0:T(8,128)(2,1)S(1)}, u32[]{:S(2)}, u32[]{:S(2)}) collective-permute-start(bf16[2,128,128]{2,1,0:T(8,128)(2,1)S(1)} %pack.4.refs_1_), channel_id=1, source_target_pairs={{0,1},{1,0},{2,3},{3,2},{4,5},{5,4},{6,7},{7,6},{8,9},{9,8},{10,11... | collective-permute-start | bytes 196616 | tf_op jit(solution)/shard_map/ppermute | solution.py:235
  8.8 13.6 %collective-permute-start.3 = (f32[2,128,128]{2,1,0:T(8,128)S(1)}, f32[2,128,128]{2,1,0:T(8,128)S(1)}, u32[]{:S(2)}, u32[]{:S(2)}) collective-permute-start(f32[2,128,128]{2,1,0:T(8,128)S(1)} %get-tuple-element.37), channel_id=1, source_target_pairs={{0,4},{4,0},{8,12},{12,8},{16,20},{20,16},{24,28},{28,24},{1,5},{5... | collective-permute-start | bytes 393224 | tf_op jit(solution)/shard_map/ppermute | solution.py:235
  10.4 4.4 %collective-permute-start.6 = (bf16[128,128]{1,0:T(8,128)(2,1)S(1)}, bf16[128,128]{1,0:T(8,128)(2,1)S(1)}, u32[]{:S(2)}, u32[]{:S(2)}) collective-permute-start(bf16[128,128]{1,0:T(8,128)(2,1)S(1)} %get-tuple-element.40.refs_0_.refs_1_), channel_id=1, source_target_pairs={{0,8},{4,12},{8,0},{12,4},{16,24},{20,28},{24,16},{28,20},{1,9},{5... | collective-permute-start | bytes 98312 | tf_op jit(solution)/shard_map/ppermute | solution.py:235
  11.9 5.5 %collective-permute-start.7 = (bf16[128,128]{1,0:T(8,128)(2,1)S(1)}, bf16[128,128]{1,0:T(8,128)(2,1)S(1)}, u32[]{:S(2)}, u32[]{:S(2)}) collective-permute-start(bf16[128,128]{1,0:T(8,128)(2,1)S(1)} %get-tuple-element.40.refs_0_.refs_1_), channel_id=1, source_target_pairs={{0,16},{4,20},{8,24},{12,28},{16,0},{20,4},{24,8},{28,12},{1,17},{... | collective-permute-start | bytes 98312 | tf_op jit(solution)/shard_map/ppermute | solution.py:235
  14.6 5.7 %collective-permute-start.8 = (bf16[128,128]{1,0:T(8,128)(2,1)S(1)}, bf16[128,128]{1,0:T(8,128)(2,1)S(1)}, u32[]{:S(2)}, u32[]{:S(2)}) collective-permute-start(bf16[128,128]{1,0:T(8,128)(2,1)S(1)} %get-tuple-element.40.refs_0_.refs_1_), channel_id=1, source_target_pairs={{0,24},{4,28},{8,16},{12,20},{16,8},{20,12},{24,0},{28,4},{1,25},{... | collective-permute-start | bytes 98312 | tf_op jit(solution)/shard_map/ppermute | solution.py:235
  20.3 5.1 %collective-permute-start.9 = (bf16[4,128,128]{2,1,0:T(8,128)(2,1)S(1)}, bf16[4,128,128]{2,1,0:T(8,128)(2,1)S(1)}, u32[]{:S(2)}, u32[]{:S(2)}) collective-permute-start(bf16[4,128,128]{2,1,0:T(8,128)(2,1)S(1)} %pack.5), channel_id=1, source_target_pairs={{0,4},{4,0},{8,12},{12,8},{16,20},{20,16},{24,28},{28,24},{1,5},{5... | collective-permute-start | bytes 393224 | tf_op jit(solution)/shard_map/ppermute | solution.py:235
  20.8 6.0 %collective-permute-start.2 = (f32[2,128,128]{2,1,0:T(8,128)S(1)}, f32[2,128,128]{2,1,0:T(8,128)S(1)}, u32[]{:S(2)}, u32[]{:S(2)}) collective-permute-start(f32[2,128,128]{2,1,0:T(8,128)S(1)} %get-tuple-element.35), channel_id=1, source_target_pairs={{0,4},{4,0},{8,12},{12,8},{16,20},{20,16},{24,28},{28,24},{1,5},{5... | collective-permute-start | bytes 393224 | tf_op jit(solution)/shard_map/ppermute | solution.py:235
  22.4 5.0 %collective-permute-start.4 = (f32[2,128,128]{2,1,0:T(8,128)S(1)}, f32[2,128,128]{2,1,0:T(8,128)S(1)}, u32[]{:S(2)}, u32[]{:S(2)}) collective-permute-start(f32[2,128,128]{2,1,0:T(8,128)S(1)} %add_far.2.refs_6_), channel_id=1, source_target_pairs={{0,8},{4,12},{8,0},{12,4},{16,24},{20,28},{24,16},{28,20},{1,9},{5... | collective-permute-start | bytes 393224 | tf_op jit(solution)/shard_map/ppermute | solution.py:235
  25.9 1.7 %collective-permute-start.10 = (f32[2,128,128]{2,1,0:T(8,128)S(1)}, f32[2,128,128]{2,1,0:T(8,128)S(1)}, u32[]{:S(2)}, u32[]{:S(2)}) collective-permute-start(f32[2,128,128]{2,1,0:T(8,128)S(1)} %get-tuple-element.42), channel_id=1, source_target_pairs={{0,1},{1,0},{2,3},{3,2},{4,5},{5,4},{6,7},{7,6},{8,9},{9,8},{10,11... | collective-permute-start | bytes 393224 | tf_op jit(solution)/shard_map/ppermute | solution.py:235
  27.5 5.4 %collective-permute-start.5 = (f32[1,128,128]{2,1,0:T(8,128)S(1)}, f32[1,128,128]{2,1,0:T(8,128)S(1)}, u32[]{:S(2)}, u32[]{:S(2)}) collective-permute-start(f32[1,128,128]{2,1,0:T(8,128)S(1)} %get-tuple-element.39), channel_id=1, source_target_pairs={{0,16},{4,20},{8,24},{12,28},{16,0},{20,4},{24,8},{28,12},{1,17},{... | collective-permute-start | bytes 196616 | tf_op jit(solution)/shard_map/ppermute | solution.py:235
  27.6 5.3 %copy-start = (f32[128,128]{1,0:T(8,128)S(1)}, f32[128,128]{1,0:T(8,128)}, u32[]{:S(2)}) copy-start(f32[128,128]{1,0:T(8,128)} %refs_0_.4) | copy-start | bytes 196612
  27.6 5.3 %collective-permute-start.11 = (f32[1,128,128]{2,1,0:T(8,128)S(1)}, f32[1,128,128]{2,1,0:T(8,128)S(1)}, u32[]{:S(2)}, u32[]{:S(2)}) collective-permute-start(f32[1,128,128]{2,1,0:T(8,128)S(1)} %get-tuple-element.44), channel_id=1, source_target_pairs={{0,2},{1,3},{2,0},{3,1},{4,6},{5,7},{6,4},{7,5},{8,10},{9,11},{10,... | collective-permute-start | bytes 196616 | tf_op jit(solution)/shard_map/ppermute | solution.py:235
  32.9 4.0 %collective-permute-start.16 = (bf16[128,128]{1,0:T(8,128)(2,1)S(1)}, bf16[128,128]{1,0:T(8,128)(2,1)S(1)}, u32[]{:S(2)}, u32[]{:S(2)}) collective-permute-start(bf16[128,128]{1,0:T(8,128)(2,1)S(1)} %get-tuple-element.46.refs_0_), channel_id=1, source_target_pairs={{0,2},{1,3},{2,0},{3,1},{4,6},{5,7},{6,4},{7,5},{8,10},{9,11},{10,... | collective-permute-start | bytes 98312 | tf_op jit(solution)/shard_map/ppermute | solution.py:235
  36.9 4.5 %collective-permute-start.17 = (bf16[2,128,128]{2,1,0:T(8,128)(2,1)S(1)}, bf16[2,128,128]{2,1,0:T(8,128)(2,1)S(1)}, u32[]{:S(2)}, u32[]{:S(2)}) collective-permute-start(bf16[2,128,128]{2,1,0:T(8,128)(2,1)S(1)} %pack.7.refs_1_), channel_id=1, source_target_pairs={{0,1},{1,0},{2,3},{3,2},{4,5},{5,4},{6,7},{7,6},{8,9},{9,8},{10,11... | collective-permute-start | bytes 196616 | tf_op jit(solution)/shard_map/ppermute | solution.py:235
  36.9 5.3 %collective-permute-start.12 = (bf16[128,128]{1,0:T(8,128)(2,1)S(1)}, bf16[128,128]{1,0:T(8,128)(2,1)S(1)}, u32[]{:S(2)}, u32[]{:S(2)}) collective-permute-start(bf16[128,128]{1,0:T(8,128)(2,1)S(1)} %get-tuple-element.45.refs_0_.refs_1_), channel_id=1, source_target_pairs={{0,8},{4,12},{8,0},{12,4},{16,24},{20,28},{24,16},{28,20},{1,9},{5... | collective-permute-start | bytes 98312 | tf_op jit(solution)/shard_map/ppermute | solution.py:235
  37.0 5.2 %collective-permute-start.13 = (bf16[128,128]{1,0:T(8,128)(2,1)S(1)}, bf16[128,128]{1,0:T(8,128)(2,1)S(1)}, u32[]{:S(2)}, u32[]{:S(2)}) collective-permute-start(bf16[128,128]{1,0:T(8,128)(2,1)S(1)} %get-tuple-element.45.refs_0_.refs_1_), channel_id=1, source_target_pairs={{0,16},{4,20},{8,24},{12,28},{16,0},{20,4},{24,8},{28,12},{1,17},{... | collective-permute-start | bytes 98312 | tf_op jit(solution)/shard_map/ppermute | solution.py:235
  39.0 5.7 %collective-permute-start.14 = (bf16[128,128]{1,0:T(8,128)(2,1)S(1)}, bf16[128,128]{1,0:T(8,128)(2,1)S(1)}, u32[]{:S(2)}, u32[]{:S(2)}) collective-permute-start(bf16[128,128]{1,0:T(8,128)(2,1)S(1)} %get-tuple-element.45.refs_0_.refs_1_), channel_id=1, source_target_pairs={{0,24},{4,28},{8,16},{12,20},{16,8},{20,12},{24,0},{28,4},{1,25},{... | collective-permute-start | bytes 98312 | tf_op jit(solution)/shard_map/ppermute | solution.py:235
  41.7 5.2 %collective-permute-start.18 = (bf16[2,128,128]{2,1,0:T(8,128)(2,1)S(1)}, bf16[2,128,128]{2,1,0:T(8,128)(2,1)S(1)}, u32[]{:S(2)}, u32[]{:S(2)}) collective-permute-start(bf16[2,128,128]{2,1,0:T(8,128)(2,1)S(1)} %get-tuple-element.48), channel_id=1, source_target_pairs={{0,4},{4,0},{8,12},{12,8},{16,20},{20,16},{24,28},{28,24},{1,5},{5... | collective-permute-start | bytes 196616 | tf_op jit(solution)/shard_map/ppermute | solution.py:235
  44.7 5.1 %collective-permute-start.15 = (bf16[4,128,128]{2,1,0:T(8,128)(2,1)S(1)}, bf16[4,128,128]{2,1,0:T(8,128)(2,1)S(1)}, u32[]{:S(2)}, u32[]{:S(2)}) collective-permute-start(bf16[4,128,128]{2,1,0:T(8,128)(2,1)S(1)} %pack.6), channel_id=1, source_target_pairs={{0,4},{4,0},{8,12},{12,8},{16,20},{20,16},{24,28},{28,24},{1,5},{5... | collective-permute-start | bytes 393224 | tf_op jit(solution)/shard_map/ppermute | solution.py:235
  45.3 5.3 %collective-permute-start.21 = (bf16[2,128,128]{2,1,0:T(8,128)(2,1)S(1)}, bf16[2,128,128]{2,1,0:T(8,128)(2,1)S(1)}, u32[]{:S(2)}, u32[]{:S(2)}) collective-permute-start(bf16[2,128,128]{2,1,0:T(8,128)(2,1)S(1)} %get-tuple-element.55), channel_id=1, source_target_pairs={{0,4},{4,0},{8,12},{12,8},{16,20},{20,16},{24,28},{28,24},{1,5},{5... | collective-permute-start | bytes 196616 | tf_op jit(solution)/shard_map/ppermute | solution.py:235
  46.8 4.3 %collective-permute-start.22 = (bf16[2,128,128]{2,1,0:T(8,128)(2,1)S(1)}, bf16[2,128,128]{2,1,0:T(8,128)(2,1)S(1)}, u32[]{:S(2)}, u32[]{:S(2)}) collective-permute-start(bf16[2,128,128]{2,1,0:T(8,128)(2,1)S(1)} %add_far.3.refs_6_), channel_id=1, source_target_pairs={{0,8},{4,12},{8,0},{12,4},{16,24},{20,28},{24,16},{28,20},{1,9},{5... | collective-permute-start | bytes 196616 | tf_op jit(solution)/shard_map/ppermute | solution.py:235
  50.3 1.8 %collective-permute-start.19 = (f32[2,128,128]{2,1,0:T(8,128)S(1)}, f32[2,128,128]{2,1,0:T(8,128)S(1)}, u32[]{:S(2)}, u32[]{:S(2)}) collective-permute-start(f32[2,128,128]{2,1,0:T(8,128)S(1)} %get-tuple-element.50), channel_id=1, source_target_pairs={{0,1},{1,0},{2,3},{3,2},{4,5},{5,4},{6,7},{7,6},{8,9},{9,8},{10,11... | collective-permute-start | bytes 393224 | tf_op jit(solution)/shard_map/ppermute | solution.py:235
  51.2 4.9 %collective-permute-start.23 = (bf16[1,128,128]{2,1,0:T(8,128)(2,1)S(1)}, bf16[1,128,128]{2,1,0:T(8,128)(2,1)S(1)}, u32[]{:S(2)}, u32[]{:S(2)}) collective-permute-start(bf16[1,128,128]{2,1,0:T(8,128)(2,1)S(1)} %get-tuple-element.57), channel_id=1, source_target_pairs={{0,16},{4,20},{8,24},{12,28},{16,0},{20,4},{24,8},{28,12},{1,17},{... | collective-permute-start | bytes 98312 | tf_op jit(solution)/shard_map/ppermute | solution.py:235
  52.1 3.9 %copy-start.1 = (f32[128,128]{1,0:T(8,128)S(1)}, f32[128,128]{1,0:T(8,128)}, u32[]{:S(2)}) copy-start(f32[128,128]{1,0:T(8,128)} %refs_0_.5) | copy-start | bytes 196612
  52.2 4.7 %collective-permute-start.20 = (bf16[1,128,128]{2,1,0:T(8,128)(2,1)S(1)}, bf16[1,128,128]{2,1,0:T(8,128)(2,1)S(1)}, u32[]{:S(2)}, u32[]{:S(2)}) collective-permute-start(bf16[1,128,128]{2,1,0:T(8,128)(2,1)S(1)} %get-tuple-element.52), channel_id=1, source_target_pairs={{0,2},{1,3},{2,0},{3,1},{4,6},{5,7},{6,4},{7,5},{8,10},{9,11},{10,... | collective-permute-start | bytes 98312 | tf_op jit(solution)/shard_map/ppermute | solution.py:235

commit v10 on v7

--- a/solution.py
+++ b/solution.py
@@ -98,7 +98,6 @@
 
 
 def dense_body(
-    q_ref,
     tiles_hbm,
     row_hbm,
     col_hbm,
@@ -110,13 +109,20 @@
     slot_sems,
 ):
     size = tiles_hbm.shape[-1]
+    ids = [
+        pltpu.make_async_copy(row_hbm, row_ref, sems.at[0]),
+        pltpu.make_async_copy(col_hbm, col_ref, sems.at[1]),
+    ]
+    for copy in ids:
+        copy.start()
     me_row = lax.axis_index("rows")
     me_col = lax.axis_index("cols")
     dense_ref[...] = jnp.zeros_like(dense_ref)
-    fetch([(row_hbm, row_ref), (col_hbm, col_ref)], sems)
+    for copy in ids:
+        copy.wait()
     count = count_ref[0, 0]
 
-    def copy(slot):
+    def tile_copy(slot):
         row = row_ref[0, 0, slot] ^ me_col
         col = col_ref[0, 0, slot] ^ me_row
         return pltpu.make_async_copy(
@@ -129,11 +135,11 @@
         )
 
     def begin(slot, carry):
-        copy(slot).start()
+        tile_copy(slot).start()
         return carry
 
     def end(slot, carry):
-        copy(slot).wait()
+        tile_copy(slot).wait()
         return carry
 
     lax.fori_loop(0, count, begin, 0)
@@ -142,7 +148,7 @@
 
 def adjoint_body(n_rows, n_cols, dense_ref, *refs):
     blocks, outs = refs[:n_cols], refs[n_cols:]
-    send_far, send_near, keep_far, keep_near = outs
+    keep_far, keep_near, send_far, send_near = outs
     half = n_rows // 2
     near = send_near.shape[0]
     size = blocks[0].shape[1]
@@ -170,11 +176,11 @@
 
 
 def forward_body(half, n_cols, dense_ref, *refs):
-    panels, other_ref, outs = refs[:half], refs[half], refs[half + 1 :]
-    size = other_ref.shape[-1]
+    panels, outs = refs[:half], refs[half:]
+    size = panels[0].shape[-1]
     total = None
     for zz in range(half):
-        panel = jnp.concatenate([panels[zz][...], other_ref[zz]], axis=0)
+        panel = jnp.concatenate([panels[zz][0], panels[zz][1]], axis=0)
         part = jnp.dot(
             dense_ref[:, 2 * zz * size : (2 * zz + 2) * size], panel, preferred_element_type=F32
         )
@@ -197,7 +203,13 @@
     out_ref[...] = value.astype(out_ref.dtype)
 
 
-def adjoint_mid_body(rate_ref, *refs):
+def forward_middle_body(h_ref, rate_ref, *refs):
+    *parts, p_ref = refs
+    rate = rate_ref[...]
+    p_ref[...] = ((1.0 - rate) * sum_refs(parts) + rate * h_ref[...]).astype(BF16)
+
+
+def adjoint_middle_body(rate_ref, *refs):
     *parts, d_ref, q_ref = refs
     total = sum_refs(parts)
     d_ref[...] = total
@@ -208,6 +220,17 @@
     *parts, out_ref = refs
     change = (row_ref[...] * d_ref[...] + sum_refs(parts)).T
     out_ref[...] = column_ref[...] * cot_ref[...] + change
+
+
+AFTER = {
+    "dense": ("start",),
+    "pair_one": ("adjoint_one",),
+    "forward_one": ("far_one",),
+    "far_two": ("pair_two",),
+    "forward_two": ("far_two",),
+    "pair_two": ("adjoint_two",),
+}
+COST = {"pair_one": 500, "adjoint_middle": 1000, "near_two": 500}
 
 
 def send(value, axis, count, step):
@@ -228,106 +251,147 @@
     def shape(kind, *lead):
         return jax.ShapeDtypeStruct((*lead, size, features), kind)
 
-    q0, p0, rate, column = call(
-        start_body,
-        [shape(BF16), shape(BF16), jax.ShapeDtypeStruct((1, size), F32), shape(F32)],
-        [hbm()] * 4,
-        in_hbm(cotangent, h_start, types, teleport),
-        0,
-        "start",
-        [
-            pltpu.VMEM(cotangent.shape, F32),
-            pltpu.VMEM(h_start.shape, F32),
-            pltpu.VMEM(types.shape, jnp.int32),
-            pltpu.SMEM(teleport.shape, F32),
-            pltpu.SemaphoreType.DMA((4,)),
-        ],
-    )
-    (dense,) = call(
-        dense_body,
-        [jax.ShapeDtypeStruct((n_cols * size, n_rows * size), BF16)],
-        [vmem()] + [hbm()] * 3 + [smem()],
-        [q0, *in_hbm(tile_values, tile_row, tile_col), tile_count],
-        0,
-        "dense",
-        [
-            pltpu.SMEM(tile_row.shape, jnp.int32),
-            pltpu.SMEM(tile_col.shape, jnp.int32),
-            pltpu.SemaphoreType.DMA((2,)),
-            pltpu.SemaphoreType.DMA((slots,)),
-        ],
-    )
-
-    def add(keep, got, kinds, name):
-        return call(add_body, [shape(kind) for kind in kinds], [vmem()] * 2, (keep, got), 0, name)
-
-    def adjoint_hop(part, kind):
-        blocks = [part] + [send(part, "cols", n_cols, s) for s in range(1, n_cols)]
-        send_far, send_near, keep_far, keep_near = call(
+    made = {}
+    makers = {}
+
+    def get(name):
+        if name not in made:
+            made[name] = makers[name]()
+        return made[name]
+
+    def run(name, body, outs, args, in_specs=None, scratch=(), flops=0):
+        return call(
+            body,
+            outs,
+            in_specs or [vmem()] * len(args),
+            args,
+            COST.get(name, 0) * 1_000_000 or flops,
+            name,
+            scratch,
+            [get(other)[0] for other in AFTER.get(name, ())],
+        )
+
+    def start():
+        return run(
+            "start",
+            start_body,
+            [shape(BF16), shape(BF16), jax.ShapeDtypeStruct((1, size), F32), shape(F32)],
+            in_hbm(cotangent, h_start, types, teleport),
+            [hbm()] * 4,
+            [
+                pltpu.VMEM(cotangent.shape, F32),
+                pltpu.VMEM(h_start.shape, F32),
+                pltpu.VMEM(types.shape, jnp.int32),
+                pltpu.SMEM(teleport.shape, F32),
+                pltpu.SemaphoreType.DMA((4,)),
+            ],
+        )
+
+    def dense():
+        return run(
+            "dense",
+            dense_body,
+            [jax.ShapeDtypeStruct((n_cols * size, n_rows * size), BF16)],
+            [*in_hbm(tile_values, tile_row, tile_col), tile_count],
+            [hbm()] * 3 + [smem()],
+            [
+                pltpu.SMEM(tile_row.shape, jnp.int32),
+                pltpu.SMEM(tile_col.shape, jnp.int32),
+                pltpu.SemaphoreType.DMA((2,)),
+                pltpu.SemaphoreType.DMA((slots,)),
+            ],
+        )
+
+    def spread(part, axis, count, step):
+        return [part] + [send(part, axis, count, step * s) for s in range(1, count // step)]
+
+    def swap_cols(parts):
+        return [parts[0]] + [send(parts[s], "cols", n_cols, s) for s in range(1, n_cols)]
+
+    def adjoint(name, part, kind):
+        return run(
+            name,
             lambda *refs: adjoint_body(n_rows, n_cols, *refs),
-            [shape(kind, half - near), shape(kind, near)]
-            + [shape(F32, half - near), shape(F32, near)],
-            [vmem()] * (1 + n_cols),
-            [dense, *blocks],
-            hop_flops,
-            "adjoint",
-        )
-        far = add(keep_far, send(send_far, "rows", n_rows, 1), [kind] * (half - near), "add_far")
-        far = [send(far[s - near], "rows", n_rows, 2 * s) for s in range(near, half)]
-        kinds = [F32] + [kind] * (near - 1)
-        close = add(keep_near, send(send_near, "rows", n_rows, 1), kinds, "add_near")
-        close = [close[0]] + [send(close[s], "rows", n_rows, 2 * s) for s in range(1, near)]
-        return close + far, blocks
-
-    def forward_hop(part, kind, after):
-        panels = [part] + [send(part, "rows", n_rows, 2 * s) for s in range(1, half)]
-        (packed,) = call(pack_body, [shape(BF16, half)], [vmem()] * half, panels, 0, "pack")
-        panels = panels + [send(packed, "rows", n_rows, 1)]
-        sums = call(
+            [shape(F32, half - near), shape(F32, near), shape(kind, half - near), shape(kind, near)],
+            [get("dense")[0], *spread(part, "cols", n_cols, 1)],
+            flops=hop_flops,
+        )
+
+    def pair(name, part):
+        return run(name, pack_body, [shape(BF16, 2)], [part, send(part, "rows", n_rows, 1)])
+
+    def forward(name, both, kind):
+        return run(
+            name,
             lambda *refs: forward_body(half, n_cols, *refs),
             [shape(kind)] * n_cols,
-            [vmem()] * (1 + len(panels)),
-            [dense, *panels],
-            hop_flops,
-            "forward",
-            after=after,
-        )
-        return [sums[0]] + [send(sums[s], "cols", n_cols, s) for s in range(1, n_cols)]
-
-    def forward_end(parts, kind, after=()):
-        return call(
+            [get("dense")[0], *spread(both, "rows", n_rows, 2)],
+            flops=hop_flops,
+        )
+
+    def sums(name, kept, sent, kinds):
+        got = send(sent, "rows", n_rows, 1)
+        return run(name, add_body, [shape(kind) for kind in kinds], [kept, got])
+
+    def row_parts(far, close):
+        parts = [send(far[s - near], "rows", n_rows, 2 * s) for s in range(near, half)]
+        return parts + [close[0]] + [send(close[s], "rows", n_rows, 2 * s) for s in range(1, near)]
+
+    far_kinds = lambda kind: [kind] * (half - near)
+    near_kinds = lambda kind: [F32] + [kind] * (near - 1)
+    makers.update(
+        start=start,
+        dense=dense,
+        adjoint_one=lambda: adjoint("adjoint_one", get("start")[0], F32),
+        pair_one=lambda: pair("pair_one", get("start")[1]),
+        far_one=lambda: sums(
+            "far_one", get("adjoint_one")[0], get("adjoint_one")[2], far_kinds(F32)
+        ),
+        near_one=lambda: sums(
+            "near_one", get("adjoint_one")[1], get("adjoint_one")[3], near_kinds(F32)
+        ),
+        forward_one=lambda: forward("forward_one", get("pair_one")[0], F32),
+        adjoint_middle=lambda: run(
+            "adjoint_middle",
+            adjoint_middle_body,
+            [shape(F32), shape(BF16)],
+            [get("start")[2], *row_parts(get("far_one"), get("near_one"))],
+        ),
+        forward_middle=lambda: run(
+            "forward_middle",
+            forward_middle_body,
+            [shape(BF16)],
+            [h_start, get("start")[3], *swap_cols(get("forward_one"))],
+        ),
+        adjoint_two=lambda: adjoint("adjoint_two", get("adjoint_middle")[1], BF16),
+        pair_two=lambda: pair("pair_two", get("forward_middle")[0]),
+        far_two=lambda: sums(
+            "far_two", get("adjoint_two")[0], get("adjoint_two")[2], far_kinds(BF16)
+        ),
+        near_two=lambda: sums(
+            "near_two", get("adjoint_two")[1], get("adjoint_two")[3], near_kinds(BF16)
+        ),
+        forward_two=lambda: forward("forward_two", get("pair_two")[0], BF16),
+        forward_end=lambda: run(
+            "forward_end",
             forward_end_body,
-            [shape(kind)],
-            [vmem()] * (2 + n_cols),
-            (h_start, column, *parts),
-            0,
-            "forward_end",
-            after=after,
-        )[0]
-
-    back, _ = adjoint_hop(q0, F32)
-    first = forward_hop(p0, F32, back[:1])
-    d1, q1 = call(
-        adjoint_mid_body,
-        [shape(F32), shape(BF16)],
-        [vmem()] * (1 + half),
-        (rate, *back),
-        0,
-        "adjoint_mid",
+            [shape(F32)],
+            [h_start, get("start")[3], *swap_cols(get("forward_two"))],
+        ),
+        adjoint_end=lambda: run(
+            "adjoint_end",
+            adjoint_end_body,
+            [shape(F32)],
+            [
+                cotangent,
+                get("adjoint_middle")[0],
+                get("start")[2],
+                get("start")[3],
+                *row_parts(get("far_two"), get("near_two")),
+            ],
+        ),
     )
-    back_two, blocks = adjoint_hop(q1, BF16)
-    p1 = forward_end(first, BF16, blocks[1:])
-    second = forward_hop(p1, BF16, back_two[:1])
-    propagated = forward_end(second, F32)
-    (input_grad,) = call(
-        adjoint_end_body,
-        [shape(F32)],
-        [vmem()] * (4 + half),
-        (cotangent, d1, rate, column, *back_two),
-        0,
-        "adjoint_end",
-    )
-    return propagated, input_grad
+    return get("forward_end")[0], get("adjoint_end")[0]
 
 
 def solution(mesh):

time: 57 us -> 50.4 us (0.88)
  waiting for transfers between devices: 16.5 us -> 7.95 us
  starting transfers between devices: 32.6 us -> 34.7 us
    ppermute x30, waiting for transfers between devices: 16.5 us -> 7.95 us  [send(): return lax.ppermute(value, axis, [(i, i ^ step) for i in range(count)])]
    ppermute x30, starting transfers between devices: 32.6 us -> 34.7 us  [send(): return lax.ppermute(value, axis, [(i, i ^ step) for i in range(count)])]
  transfers between devices with their start and end apart: 30 -> 30, of which waited for: 12 -> 9; matrix products, arithmetic and copies ran while one was open for 0% -> 0% of each run, Pallas kernels for 8% -> 8%
where the time goes in v10:
time: 50.4 us; the launch traced here: 49.9 us
  starting transfers between devices  34.7 us (69%)
  waiting for transfers between devices  7.95 us (16%)
  Pallas kernels  5.83 us (12%)
  between operations  1.43 us (3%)
    ppermute x30, starting transfers between devices, send(): return lax.ppermute(value, axis, [(i, i ^ step) for i in range(count)])  34.7 us
    ppermute x30, waiting for transfers between devices, send(): return lax.ppermute(value, axis, [(i, i ^ step) for i in range(count)])  7.95 us
    pallas_call x16, Pallas kernels, call(): pl.pallas_call(ordered, out_shape=outs, in_specs=[*in_specs, *[pl.BlockSp...  5.83 us
  transfers between devices with their start and end apart: 30, of which 9 were waited for; matrix products, arithmetic and copies ran while one was open for 0% of the time, Pallas kernels for 8%

profile of v10, /device:TPU:0, one launch (start us, length us, event | category | flops | bytes accessed | tf_op | source)
XLA Modules:
  0.0 49.9 jit_solution(7849140485308964454)
XLA Ops:
  0.6 1.0 %start.1 = (bf16[128,128]{1,0:T(8,128)(2,1)S(1)}, bf16[128,128]{1,0:T(8,128)(2,1)S(1)}, f32[1,128]{1,0:T(1,128)S(1)}, f32[128,128]{1,0:T(8,128)S(1)}) custom-call(f32[128,128]{1,0:T(8,128)} %refs_0_.9, f32[128,128]{1,0:T(8,128)} %refs_0_.8, s32[1,128]{1,0:T(1,128)} %bitcast.1, f32[8]{0:T(128)} %refs_3_.2), custom_call_target="tpu_custom_call" | custom-call | bytes 263200 | tf_op jit(solution)/shard_map/start/pallas_call | solution.py:36
  1.7 2.4 %collective-permute-start.3 = (bf16[128,128]{1,0:T(8,128)(2,1)S(1)}, bf16[128,128]{1,0:T(8,128)(2,1)S(1)}, u32[]{:S(2)}, u32[]{:S(2)}) collective-permute-start(bf16[128,128]{1,0:T(8,128)(2,1)S(1)} %get-tuple-element.33.refs_4_.refs_1_), channel_id=1, source_target_pairs={{0,3},{1,2},{2,1},{3,0},{4,7},{5,6},{6,5},{7,4},{8,11},{9,10},{10,... | collective-permute-start | bytes 98312 | tf_op jit(solution)/shard_map/ppermute | solution.py:237
  4.1 0.6 %collective-permute-start.2 = (bf16[128,128]{1,0:T(8,128)(2,1)S(1)}, bf16[128,128]{1,0:T(8,128)(2,1)S(1)}, u32[]{:S(2)}, u32[]{:S(2)}) collective-permute-start(bf16[128,128]{1,0:T(8,128)(2,1)S(1)} %get-tuple-element.33.refs_4_.refs_1_), channel_id=1, source_target_pairs={{0,2},{1,3},{2,0},{3,1},{4,6},{5,7},{6,4},{7,5},{8,10},{9,11},{10,... | collective-permute-start | bytes 98312 | tf_op jit(solution)/shard_map/ppermute | solution.py:237
  4.8 0.0 collective-permute-start.1
  4.8 1.8 %collective-permute-start = (bf16[128,128]{1,0:T(8,128)(2,1)S(1)}, bf16[128,128]{1,0:T(8,128)(2,1)S(1)}, u32[]{:S(2)}, u32[]{:S(2)}) collective-permute-start(bf16[128,128]{1,0:T(8,128)(2,1)S(1)} %get-tuple-element.34.refs_0_), channel_id=1, source_target_pairs={{0,4},{4,0},{8,12},{12,8},{16,20},{20,16},{24,28},{28,24},{1,5},{5... | collective-permute-start | bytes 98312 | tf_op jit(solution)/shard_map/ppermute | solution.py:237
  7.2 1.8 %dense.1.refs_0_ = bf16[512,1024]{1,0:T(8,128)(2,1)S(1)} custom-call(bf16[1,1,24,128,128]{4,3,2,1,0:T(8,128)(2,1)} %refs_0_.6, s32[1,1,24]{2,1,0:T(1,128)} %refs_1_.3, s32[1,1,24]{2,1,0:T(1,128)} %refs_2_.1, s32[1,1]{1,0:T(1,128)S(6)} %copy.10.refs_3_, bf16[128,128]{1,0:T(8,128)(2,1)S(1)} %get-tuple-element.33.refs_4_.refs_1_), custom_call_target="tpu_custom_call" | custom-call | bytes 1835204 | tf_op jit(solution)/shard_map/dense/pallas_call | solution.py:36
  9.0 0.0 collective-permute-done.3.refs_4_
  9.0 0.0 collective-permute-done.1.refs_2_
  9.0 0.3 adjoint_one.1
  9.4 0.6 %collective-permute-start.7 = (f32[2,128,128]{2,1,0:T(8,128)S(1)}, f32[2,128,128]{2,1,0:T(8,128)S(1)}, u32[]{:S(2)}, u32[]{:S(2)}) collective-permute-start(f32[2,128,128]{2,1,0:T(8,128)S(1)} %get-tuple-element.36), channel_id=1, source_target_pairs={{0,4},{4,0},{8,12},{12,8},{16,20},{20,16},{24,28},{28,24},{1,5},{5... | collective-permute-start | bytes 393224 | tf_op jit(solution)/shard_map/ppermute | solution.py:237
  10.0 1.5 %collective-permute-start.14 = (f32[2,128,128]{2,1,0:T(8,128)S(1)}, f32[2,128,128]{2,1,0:T(8,128)S(1)}, u32[]{:S(2)}, u32[]{:S(2)}) collective-permute-start(f32[2,128,128]{2,1,0:T(8,128)S(1)} %get-tuple-element.45), channel_id=1, source_target_pairs={{0,4},{4,0},{8,12},{12,8},{16,20},{20,16},{24,28},{28,24},{1,5},{5... | collective-permute-start | bytes 393224 | tf_op jit(solution)/shard_map/ppermute | solution.py:237
  11.5 3.8 %collective-permute-start.6 = (bf16[2,128,128]{2,1,0:T(8,128)(2,1)S(1)}, bf16[2,128,128]{2,1,0:T(8,128)(2,1)S(1)}, u32[]{:S(2)}, u32[]{:S(2)}) collective-permute-start(bf16[2,128,128]{2,1,0:T(8,128)(2,1)S(1)} %pair_one.1.refs_1_), channel_id=1, source_target_pairs={{0,24},{4,28},{8,16},{12,20},{16,8},{20,12},{24,0},{28,4},{1,25},{... | collective-permute-start | bytes 196616 | tf_op jit(solution)/shard_map/ppermute | solution.py:237
  15.2 0.7 %collective-permute-start.4 = (bf16[2,128,128]{2,1,0:T(8,128)(2,1)S(1)}, bf16[2,128,128]{2,1,0:T(8,128)(2,1)S(1)}, u32[]{:S(2)}, u32[]{:S(2)}) collective-permute-start(bf16[2,128,128]{2,1,0:T(8,128)(2,1)S(1)} %pair_one.1.refs_1_), channel_id=1, source_target_pairs={{0,8},{4,12},{8,0},{12,4},{16,24},{20,28},{24,16},{28,20},{1,9},{5... | collective-permute-start | bytes 196616 | tf_op jit(solution)/shard_map/ppermute | solution.py:237
  15.9 0.0 collective-permute-done.7.refs_1_
  15.9 3.8 %collective-permute-start.13 = (f32[128,128]{1,0:T(8,128)S(1)}, f32[128,128]{1,0:T(8,128)S(1)}, u32[]{:S(2)}, u32[]{:S(2)}) collective-permute-start(f32[128,128]{1,0:T(8,128)S(1)} %get-tuple-element.43), channel_id=1, source_target_pairs={{0,24},{4,28},{8,16},{12,20},{16,8},{20,12},{24,0},{28,4},{1,25},{... | collective-permute-start | bytes 196616 | tf_op jit(solution)/shard_map/ppermute | solution.py:237
  19.7 0.5 collective-permute-start.12
  20.2 1.7 %collective-permute-start.15 = (f32[128,128]{1,0:T(8,128)S(1)}, f32[128,128]{1,0:T(8,128)S(1)}, u32[]{:S(2)}, u32[]{:S(2)}) collective-permute-start(f32[128,128]{1,0:T(8,128)S(1)} %get-tuple-element.47), channel_id=1, source_target_pairs={{0,8},{4,12},{8,0},{12,4},{16,24},{20,28},{24,16},{28,20},{1,9},{5... | collective-permute-start | bytes 196616 | tf_op jit(solution)/shard_map/ppermute | solution.py:237
  21.9 1.0 %collective-permute-done.5.refs_3_ = bf16[2,128,128]{2,1,0:T(8,128)(2,1)S(1)} collective-permute-done((bf16[2,128,128]{2,1,0:T(8,128)(2,1)S(1)}, bf16[2,128,128]{2,1,0:T(8,128)(2,1)S(1)}, u32[]{:S(2)}, u32[]{:S(2)}) %collective-permute-start.5) | collective-permute-done | bytes 65568 | tf_op jit(solution)/shard_map/ppermute | solution.py:237
  22.9 0.4 forward_one.1
  23.3 0.1 collective-permute-start.8
  23.4 1.6 %collective-permute-start.9 = (f32[128,128]{1,0:T(8,128)S(1)}, f32[128,128]{1,0:T(8,128)S(1)}, u32[]{:S(2)}, u32[]{:S(2)}) collective-permute-start(f32[128,128]{1,0:T(8,128)S(1)} %get-tuple-element.40), channel_id=1, source_target_pairs={{0,2},{1,3},{2,0},{3,1},{4,6},{5,7},{6,4},{7,5},{8,10},{9,11},{10,... | collective-permute-start | bytes 196616 | tf_op jit(solution)/shard_map/ppermute | solution.py:237
  25.0 0.3 collective-permute-start.10
  25.3 0.7 %collective-permute-done.12.refs_1_ = f32[128,128]{1,0:T(8,128)S(1)} collective-permute-done((f32[128,128]{1,0:T(8,128)S(1)}, f32[128,128]{1,0:T(8,128)S(1)}, u32[]{:S(2)}, u32[]{:S(2)}) %collective-permute-start.12) | collective-permute-done | bytes 65568 | tf_op jit(solution)/shard_map/ppermute | solution.py:237
  26.0 0.9 %collective-permute-start.18 = (bf16[128,128]{1,0:T(8,128)(2,1)S(1)}, bf16[128,128]{1,0:T(8,128)(2,1)S(1)}, u32[]{:S(2)}, u32[]{:S(2)}) collective-permute-start(bf16[128,128]{1,0:T(8,128)(2,1)S(1)} %get-tuple-element.48.refs_1_), channel_id=1, source_target_pairs={{0,3},{1,2},{2,1},{3,0},{4,7},{5,6},{6,5},{7,4},{8,11},{9,10},{10,... | collective-permute-start | bytes 98312 | tf_op jit(solution)/shard_map/ppermute | solution.py:237
  26.9 0.8 %collective-permute-start.17 = (bf16[128,128]{1,0:T(8,128)(2,1)S(1)}, bf16[128,128]{1,0:T(8,128)(2,1)S(1)}, u32[]{:S(2)}, u32[]{:S(2)}) collective-permute-start(bf16[128,128]{1,0:T(8,128)(2,1)S(1)} %get-tuple-element.48.refs_1_), channel_id=1, source_target_pairs={{0,2},{1,3},{2,0},{3,1},{4,6},{5,7},{6,4},{7,5},{8,10},{9,11},{10,... | collective-permute-start | bytes 98312 | tf_op jit(solution)/shard_map/ppermute | solution.py:237
  27.7 0.3 collective-permute-start.16
  27.9 1.1 %collective-permute-done.10.refs_5_ = f32[128,128]{1,0:T(8,128)S(1)} collective-permute-done((f32[128,128]{1,0:T(8,128)S(1)}, f32[128,128]{1,0:T(8,128)S(1)}, u32[]{:S(2)}, u32[]{:S(2)}) %collective-permute-start.10) | collective-permute-done | bytes 65568 | tf_op jit(solution)/shard_map/ppermute | solution.py:237
  29.1 0.7 %collective-permute-start.11 = (bf16[128,128]{1,0:T(8,128)(2,1)S(1)}, bf16[128,128]{1,0:T(8,128)(2,1)S(1)}, u32[]{:S(2)}, u32[]{:S(2)}) collective-permute-start(bf16[128,128]{1,0:T(8,128)(2,1)S(1)} %forward_middle.1.refs_0_), channel_id=1, source_target_pairs={{0,4},{4,0},{8,12},{12,8},{16,20},{20,16},{24,28},{28,24},{1,5},{5... | collective-permute-start | bytes 98312 | tf_op jit(solution)/shard_map/ppermute | solution.py:237
  29.8 1.2 %collective-permute-done.17.refs_3_ = bf16[128,128]{1,0:T(8,128)(2,1)S(1)} collective-permute-done((bf16[128,128]{1,0:T(8,128)(2,1)S(1)}, bf16[128,128]{1,0:T(8,128)(2,1)S(1)}, u32[]{:S(2)}, u32[]{:S(2)}) %collective-permute-start.17) | collective-permute-done | bytes 32800 | tf_op jit(solution)/shard_map/ppermute | solution.py:237
  31.0 0.3 adjoint_two.1
  31.3 0.5 %collective-permute-start.22 = (bf16[2,128,128]{2,1,0:T(8,128)(2,1)S(1)}, bf16[2,128,128]{2,1,0:T(8,128)(2,1)S(1)}, u32[]{:S(2)}, u32[]{:S(2)}) collective-permute-start(bf16[2,128,128]{2,1,0:T(8,128)(2,1)S(1)} %get-tuple-element.50), channel_id=1, source_target_pairs={{0,4},{4,0},{8,12},{12,8},{16,20},{20,16},{24,28},{28,24},{1,5},{5... | collective-permute-start | bytes 196616 | tf_op jit(solution)/shard_map/ppermute | solution.py:237
  31.9 1.4 %collective-permute-done.11.refs_1_ = bf16[128,128]{1,0:T(8,128)(2,1)S(1)} collective-permute-done((bf16[128,128]{1,0:T(8,128)(2,1)S(1)}, bf16[128,128]{1,0:T(8,128)(2,1)S(1)}, u32[]{:S(2)}, u32[]{:S(2)}) %collective-permute-start.11) | collective-permute-done | bytes 32800 | tf_op jit(solution)/shard_map/ppermute | solution.py:237
  33.2 3.3 %collective-permute-start.21 = (bf16[2,128,128]{2,1,0:T(8,128)(2,1)S(1)}, bf16[2,128,128]{2,1,0:T(8,128)(2,1)S(1)}, u32[]{:S(2)}, u32[]{:S(2)}) collective-permute-start(bf16[2,128,128]{2,1,0:T(8,128)(2,1)S(1)} %pair_two.1.refs_2_.refs_1_), channel_id=1, source_target_pairs={{0,24},{4,28},{8,16},{12,20},{16,8},{20,12},{24,0},{28,4},{1,25},{... | collective-permute-start | bytes 196616 | tf_op jit(solution)/shard_map/ppermute | solution.py:237
  36.6 1.0 %collective-permute-start.19 = (bf16[2,128,128]{2,1,0:T(8,128)(2,1)S(1)}, bf16[2,128,128]{2,1,0:T(8,128)(2,1)S(1)}, u32[]{:S(2)}, u32[]{:S(2)}) collective-permute-start(bf16[2,128,128]{2,1,0:T(8,128)(2,1)S(1)} %pair_two.1.refs_2_.refs_1_), channel_id=1, source_target_pairs={{0,8},{4,12},{8,0},{12,4},{16,24},{20,28},{24,16},{28,20},{1,9},{5... | collective-permute-start | bytes 196616 | tf_op jit(solution)/shard_map/ppermute | solution.py:237
  37.6 0.8 %collective-permute-start.28 = (bf16[2,128,128]{2,1,0:T(8,128)(2,1)S(1)}, bf16[2,128,128]{2,1,0:T(8,128)(2,1)S(1)}, u32[]{:S(2)}, u32[]{:S(2)}) collective-permute-start(bf16[2,128,128]{2,1,0:T(8,128)(2,1)S(1)} %get-tuple-element.59), channel_id=1, source_target_pairs={{0,4},{4,0},{8,12},{12,8},{16,20},{20,16},{24,28},{28,24},{1,5},{5... | collective-permute-start | bytes 196616 | tf_op jit(solution)/shard_map/ppermute | solution.py:237
  38.5 3.8 %collective-permute-start.27 = (bf16[128,128]{1,0:T(8,128)(2,1)S(1)}, bf16[128,128]{1,0:T(8,128)(2,1)S(1)}, u32[]{:S(2)}, u32[]{:S(2)}) collective-permute-start(bf16[128,128]{1,0:T(8,128)(2,1)S(1)} %get-tuple-element.57), channel_id=1, source_target_pairs={{0,24},{4,28},{8,16},{12,20},{16,8},{20,12},{24,0},{28,4},{1,25},{... | collective-permute-start | bytes 98312 | tf_op jit(solution)/shard_map/ppermute | solution.py:237
  42.3 0.1 collective-permute-start.26
  42.4 0.4 collective-permute-done.20.refs_3_
  42.8 0.4 forward_two.1
  43.2 0.1 collective-permute-start.23
  43.3 1.1 %collective-permute-start.24 = (bf16[128,128]{1,0:T(8,128)(2,1)S(1)}, bf16[128,128]{1,0:T(8,128)(2,1)S(1)}, u32[]{:S(2)}, u32[]{:S(2)}) collective-permute-start(bf16[128,128]{1,0:T(8,128)(2,1)S(1)} %get-tuple-element.54), channel_id=1, source_target_pairs={{0,2},{1,3},{2,0},{3,1},{4,6},{5,7},{6,4},{7,5},{8,10},{9,11},{10,... | collective-permute-start | bytes 98312 | tf_op jit(solution)/shard_map/ppermute | solution.py:237
  44.4 0.8 %collective-permute-start.25 = (bf16[128,128]{1,0:T(8,128)(2,1)S(1)}, bf16[128,128]{1,0:T(8,128)(2,1)S(1)}, u32[]{:S(2)}, u32[]{:S(2)}) collective-permute-start(bf16[128,128]{1,0:T(8,128)(2,1)S(1)} %get-tuple-element.55), channel_id=1, source_target_pairs={{0,3},{1,2},{2,1},{3,0},{4,7},{5,6},{6,5},{7,4},{8,11},{9,10},{10,... | collective-permute-start | bytes 98312 | tf_op jit(solution)/shard_map/ppermute | solution.py:237
  45.2 1.2 %collective-permute-start.29 = (bf16[128,128]{1,0:T(8,128)(2,1)S(1)}, bf16[128,128]{1,0:T(8,128)(2,1)S(1)}, u32[]{:S(2)}, u32[]{:S(2)}) collective-permute-start(bf16[128,128]{1,0:T(8,128)(2,1)S(1)} %get-tuple-element.61), channel_id=1, source_target_pairs={{0,8},{4,12},{8,0},{12,4},{16,24},{20,28},{24,16},{28,20},{1,9},{5... | collective-permute-start | bytes 98312 | tf_op jit(solution)/shard_map/ppermute | solution.py:237
  46.4 0.9 %collective-permute-done.24.refs_4_ = bf16[128,128]{1,0:T(8,128)(2,1)S(1)} collective-permute-done((bf16[128,128]{1,0:T(8,128)(2,1)S(1)}, bf16[128,128]{1,0:T(8,128)(2,1)S(1)}, u32[]{:S(2)}, u32[]{:S(2)}) %collective-permute-start.24) | collective-permute-done | bytes 32800 | tf_op jit(solution)/shard_map/ppermute | solution.py:237
  47.3 0.5 collective-permute-done.25.refs_5_
  47.8 0.7 %forward_end.1 = f32[128,128]{1,0:T(8,128)} custom-call(f32[128,128]{1,0:T(8,128)S(1)} %copy-done, f32[128,128]{1,0:T(8,128)S(1)} %get-tuple-element.32.refs_1_.refs_3_, bf16[128,128]{1,0:T(8,128)(2,1)S(1)} %get-tuple-element.52.refs_2_, bf16[128,128]{1,0:T(8,128)(2,1)S(1)} %collective-permute-done.23.refs_3_, ...), custom_call_target="tpu_custom_call" | custom-call | bytes 327680 | tf_op jit(solution)/shard_map/forward_end/pallas_call | solution.py:36
  48.4 0.8 %collective-permute-done.29.refs_7_ = bf16[128,128]{1,0:T(8,128)(2,1)S(1)} collective-permute-done((bf16[128,128]{1,0:T(8,128)(2,1)S(1)}, bf16[128,128]{1,0:T(8,128)(2,1)S(1)}, u32[]{:S(2)}, u32[]{:S(2)}) %collective-permute-start.29) | collective-permute-done | bytes 32800 | tf_op jit(solution)/shard_map/ppermute | solution.py:237
  49.2 0.7 %adjoint_end.1 = f32[128,128]{1,0:T(8,128)} custom-call(f32[128,128]{1,0:T(8,128)S(1)} %copy-done.1, f32[128,128]{1,0:T(8,128)S(1)} %get-tuple-element.56.refs_1_, f32[1,128]{1,0:T(1,128)S(1)} %get-tuple-element.42.refs_0_.refs_2_, f32[128,128]{1,0:T(8,128)S(1)} %get-tuple-element.32.refs_1_.refs_3_, bf16[128,128]{1,0:T(8,128)(2,1)S(1)} %collective-permute-done.26.refs_4_, ...), custom_call_target="tpu_custom_call" | custom-call | bytes 426496 | tf_op jit(solution)/shard_map/adjoint_end/pallas_call | solution.py:36
  (32 shorter events, 0.2 us)
Async XLA Ops:
  1.7 7.3 %collective-permute-start.3 = (bf16[128,128]{1,0:T(8,128)(2,1)S(1)}, bf16[128,128]{1,0:T(8,128)(2,1)S(1)}, u32[]{:S(2)}, u32[]{:S(2)}) collective-permute-start(bf16[128,128]{1,0:T(8,128)(2,1)S(1)} %get-tuple-element.33.refs_4_.refs_1_), channel_id=1, source_target_pairs={{0,3},{1,2},{2,1},{3,0},{4,7},{5,6},{6,5},{7,4},{8,11},{9,10},{10,... | collective-permute-start | bytes 98312 | tf_op jit(solution)/shard_map/ppermute | solution.py:237
  4.1 4.9 %collective-permute-start.2 = (bf16[128,128]{1,0:T(8,128)(2,1)S(1)}, bf16[128,128]{1,0:T(8,128)(2,1)S(1)}, u32[]{:S(2)}, u32[]{:S(2)}) collective-permute-start(bf16[128,128]{1,0:T(8,128)(2,1)S(1)} %get-tuple-element.33.refs_4_.refs_1_), channel_id=1, source_target_pairs={{0,2},{1,3},{2,0},{3,1},{4,6},{5,7},{6,4},{7,5},{8,10},{9,11},{10,... | collective-permute-start | bytes 98312 | tf_op jit(solution)/shard_map/ppermute | solution.py:237
  4.8 4.3 %collective-permute-start.1 = (bf16[128,128]{1,0:T(8,128)(2,1)S(1)}, bf16[128,128]{1,0:T(8,128)(2,1)S(1)}, u32[]{:S(2)}, u32[]{:S(2)}) collective-permute-start(bf16[128,128]{1,0:T(8,128)(2,1)S(1)} %get-tuple-element.33.refs_4_.refs_1_), channel_id=1, source_target_pairs={{0,1},{1,0},{2,3},{3,2},{4,5},{5,4},{6,7},{7,6},{8,9},{9,8},{10,11... | collective-permute-start | bytes 98312 | tf_op jit(solution)/shard_map/ppermute | solution.py:237
  4.8 6.7 %collective-permute-start = (bf16[128,128]{1,0:T(8,128)(2,1)S(1)}, bf16[128,128]{1,0:T(8,128)(2,1)S(1)}, u32[]{:S(2)}, u32[]{:S(2)}) collective-permute-start(bf16[128,128]{1,0:T(8,128)(2,1)S(1)} %get-tuple-element.34.refs_0_), channel_id=1, source_target_pairs={{0,4},{4,0},{8,12},{12,8},{16,20},{20,16},{24,28},{28,24},{1,5},{5... | collective-permute-start | bytes 98312 | tf_op jit(solution)/shard_map/ppermute | solution.py:237
  9.4 6.6 %collective-permute-start.7 = (f32[2,128,128]{2,1,0:T(8,128)S(1)}, f32[2,128,128]{2,1,0:T(8,128)S(1)}, u32[]{:S(2)}, u32[]{:S(2)}) collective-permute-start(f32[2,128,128]{2,1,0:T(8,128)S(1)} %get-tuple-element.36), channel_id=1, source_target_pairs={{0,4},{4,0},{8,12},{12,8},{16,20},{20,16},{24,28},{28,24},{1,5},{5... | collective-permute-start | bytes 393224 | tf_op jit(solution)/shard_map/ppermute | solution.py:237
  10.0 9.7 %collective-permute-start.14 = (f32[2,128,128]{2,1,0:T(8,128)S(1)}, f32[2,128,128]{2,1,0:T(8,128)S(1)}, u32[]{:S(2)}, u32[]{:S(2)}) collective-permute-start(f32[2,128,128]{2,1,0:T(8,128)S(1)} %get-tuple-element.45), channel_id=1, source_target_pairs={{0,4},{4,0},{8,12},{12,8},{16,20},{20,16},{24,28},{28,24},{1,5},{5... | collective-permute-start | bytes 393224 | tf_op jit(solution)/shard_map/ppermute | solution.py:237
  11.5 8.7 %collective-permute-start.6 = (bf16[2,128,128]{2,1,0:T(8,128)(2,1)S(1)}, bf16[2,128,128]{2,1,0:T(8,128)(2,1)S(1)}, u32[]{:S(2)}, u32[]{:S(2)}) collective-permute-start(bf16[2,128,128]{2,1,0:T(8,128)(2,1)S(1)} %pair_one.1.refs_1_), channel_id=1, source_target_pairs={{0,24},{4,28},{8,16},{12,20},{16,8},{20,12},{24,0},{28,4},{1,25},{... | collective-permute-start | bytes 196616 | tf_op jit(solution)/shard_map/ppermute | solution.py:237
  15.2 7.7 %collective-permute-start.5 = (bf16[2,128,128]{2,1,0:T(8,128)(2,1)S(1)}, bf16[2,128,128]{2,1,0:T(8,128)(2,1)S(1)}, u32[]{:S(2)}, u32[]{:S(2)}) collective-permute-start(bf16[2,128,128]{2,1,0:T(8,128)(2,1)S(1)} %pair_one.1.refs_1_), channel_id=1, source_target_pairs={{0,16},{4,20},{8,24},{12,28},{16,0},{20,4},{24,8},{28,12},{1,17},{... | collective-permute-start | bytes 196616 | tf_op jit(solution)/shard_map/ppermute | solution.py:237
  15.2 7.7 %collective-permute-start.4 = (bf16[2,128,128]{2,1,0:T(8,128)(2,1)S(1)}, bf16[2,128,128]{2,1,0:T(8,128)(2,1)S(1)}, u32[]{:S(2)}, u32[]{:S(2)}) collective-permute-start(bf16[2,128,128]{2,1,0:T(8,128)(2,1)S(1)} %pair_one.1.refs_1_), channel_id=1, source_target_pairs={{0,8},{4,12},{8,0},{12,4},{16,24},{20,28},{24,16},{28,20},{1,9},{5... | collective-permute-start | bytes 196616 | tf_op jit(solution)/shard_map/ppermute | solution.py:237
  15.9 9.1 %collective-permute-start.13 = (f32[128,128]{1,0:T(8,128)S(1)}, f32[128,128]{1,0:T(8,128)S(1)}, u32[]{:S(2)}, u32[]{:S(2)}) collective-permute-start(f32[128,128]{1,0:T(8,128)S(1)} %get-tuple-element.43), channel_id=1, source_target_pairs={{0,24},{4,28},{8,16},{12,20},{16,8},{20,12},{24,0},{28,4},{1,25},{... | collective-permute-start | bytes 196616 | tf_op jit(solution)/shard_map/ppermute | solution.py:237
  19.7 6.3 %collective-permute-start.12 = (f32[128,128]{1,0:T(8,128)S(1)}, f32[128,128]{1,0:T(8,128)S(1)}, u32[]{:S(2)}, u32[]{:S(2)}) collective-permute-start(f32[128,128]{1,0:T(8,128)S(1)} %get-tuple-element.37.refs_5_), channel_id=1, source_target_pairs={{0,16},{4,20},{8,24},{12,28},{16,0},{20,4},{24,8},{28,12},{1,17},{... | collective-permute-start | bytes 196616 | tf_op jit(solution)/shard_map/ppermute | solution.py:237
  20.2 5.8 %collective-permute-start.15 = (f32[128,128]{1,0:T(8,128)S(1)}, f32[128,128]{1,0:T(8,128)S(1)}, u32[]{:S(2)}, u32[]{:S(2)}) collective-permute-start(f32[128,128]{1,0:T(8,128)S(1)} %get-tuple-element.47), channel_id=1, source_target_pairs={{0,8},{4,12},{8,0},{12,4},{16,24},{20,28},{24,16},{28,20},{1,9},{5... | collective-permute-start | bytes 196616 | tf_op jit(solution)/shard_map/ppermute | solution.py:237
  23.3 4.4 %collective-permute-start.8 = (f32[128,128]{1,0:T(8,128)S(1)}, f32[128,128]{1,0:T(8,128)S(1)}, u32[]{:S(2)}, u32[]{:S(2)}) collective-permute-start(f32[128,128]{1,0:T(8,128)S(1)} %get-tuple-element.39), channel_id=1, source_target_pairs={{0,1},{1,0},{2,3},{3,2},{4,5},{5,4},{6,7},{7,6},{8,9},{9,8},{10,11... | collective-permute-start | bytes 196616 | tf_op jit(solution)/shard_map/ppermute | solution.py:237
  23.4 4.5 %collective-permute-start.9 = (f32[128,128]{1,0:T(8,128)S(1)}, f32[128,128]{1,0:T(8,128)S(1)}, u32[]{:S(2)}, u32[]{:S(2)}) collective-permute-start(f32[128,128]{1,0:T(8,128)S(1)} %get-tuple-element.40), channel_id=1, source_target_pairs={{0,2},{1,3},{2,0},{3,1},{4,6},{5,7},{6,4},{7,5},{8,10},{9,11},{10,... | collective-permute-start | bytes 196616 | tf_op jit(solution)/shard_map/ppermute | solution.py:237
  25.0 4.0 %collective-permute-start.10 = (f32[128,128]{1,0:T(8,128)S(1)}, f32[128,128]{1,0:T(8,128)S(1)}, u32[]{:S(2)}, u32[]{:S(2)}) collective-permute-start(f32[128,128]{1,0:T(8,128)S(1)} %get-tuple-element.41), channel_id=1, source_target_pairs={{0,3},{1,2},{2,1},{3,0},{4,7},{5,6},{6,5},{7,4},{8,11},{9,10},{10,... | collective-permute-start | bytes 196616 | tf_op jit(solution)/shard_map/ppermute | solution.py:237
  26.0 3.1 %copy-start = (f32[128,128]{1,0:T(8,128)S(1)}, f32[128,128]{1,0:T(8,128)}, u32[]{:S(2)}) copy-start(f32[128,128]{1,0:T(8,128)} %refs_0_.8) | copy-start | bytes 196612
  26.0 3.8 %collective-permute-start.18 = (bf16[128,128]{1,0:T(8,128)(2,1)S(1)}, bf16[128,128]{1,0:T(8,128)(2,1)S(1)}, u32[]{:S(2)}, u32[]{:S(2)}) collective-permute-start(bf16[128,128]{1,0:T(8,128)(2,1)S(1)} %get-tuple-element.48.refs_1_), channel_id=1, source_target_pairs={{0,3},{1,2},{2,1},{3,0},{4,7},{5,6},{6,5},{7,4},{8,11},{9,10},{10,... | collective-permute-start | bytes 98312 | tf_op jit(solution)/shard_map/ppermute | solution.py:237
  26.9 4.1 %collective-permute-start.17 = (bf16[128,128]{1,0:T(8,128)(2,1)S(1)}, bf16[128,128]{1,0:T(8,128)(2,1)S(1)}, u32[]{:S(2)}, u32[]{:S(2)}) collective-permute-start(bf16[128,128]{1,0:T(8,128)(2,1)S(1)} %get-tuple-element.48.refs_1_), channel_id=1, source_target_pairs={{0,2},{1,3},{2,0},{3,1},{4,6},{5,7},{6,4},{7,5},{8,10},{9,11},{10,... | collective-permute-start | bytes 98312 | tf_op jit(solution)/shard_map/ppermute | solution.py:237
  27.7 3.3 %collective-permute-start.16 = (bf16[128,128]{1,0:T(8,128)(2,1)S(1)}, bf16[128,128]{1,0:T(8,128)(2,1)S(1)}, u32[]{:S(2)}, u32[]{:S(2)}) collective-permute-start(bf16[128,128]{1,0:T(8,128)(2,1)S(1)} %get-tuple-element.48.refs_1_), channel_id=1, source_target_pairs={{0,1},{1,0},{2,3},{3,2},{4,5},{5,4},{6,7},{7,6},{8,9},{9,8},{10,11... | collective-permute-start | bytes 98312 | tf_op jit(solution)/shard_map/ppermute | solution.py:237
  29.1 4.1 %collective-permute-start.11 = (bf16[128,128]{1,0:T(8,128)(2,1)S(1)}, bf16[128,128]{1,0:T(8,128)(2,1)S(1)}, u32[]{:S(2)}, u32[]{:S(2)}) collective-permute-start(bf16[128,128]{1,0:T(8,128)(2,1)S(1)} %forward_middle.1.refs_0_), channel_id=1, source_target_pairs={{0,4},{4,0},{8,12},{12,8},{16,20},{20,16},{24,28},{28,24},{1,5},{5... | collective-permute-start | bytes 98312 | tf_op jit(solution)/shard_map/ppermute | solution.py:237
  31.3 7.1 %collective-permute-start.22 = (bf16[2,128,128]{2,1,0:T(8,128)(2,1)S(1)}, bf16[2,128,128]{2,1,0:T(8,128)(2,1)S(1)}, u32[]{:S(2)}, u32[]{:S(2)}) collective-permute-start(bf16[2,128,128]{2,1,0:T(8,128)(2,1)S(1)} %get-tuple-element.50), channel_id=1, source_target_pairs={{0,4},{4,0},{8,12},{12,8},{16,20},{20,16},{24,28},{28,24},{1,5},{5... | collective-permute-start | bytes 196616 | tf_op jit(solution)/shard_map/ppermute | solution.py:237
  33.2 9.0 %collective-permute-start.21 = (bf16[2,128,128]{2,1,0:T(8,128)(2,1)S(1)}, bf16[2,128,128]{2,1,0:T(8,128)(2,1)S(1)}, u32[]{:S(2)}, u32[]{:S(2)}) collective-permute-start(bf16[2,128,128]{2,1,0:T(8,128)(2,1)S(1)} %pair_two.1.refs_2_.refs_1_), channel_id=1, source_target_pairs={{0,24},{4,28},{8,16},{12,20},{16,8},{20,12},{24,0},{28,4},{1,25},{... | collective-permute-start | bytes 196616 | tf_op jit(solution)/shard_map/ppermute | solution.py:237
  36.6 6.2 %collective-permute-start.20 = (bf16[2,128,128]{2,1,0:T(8,128)(2,1)S(1)}, bf16[2,128,128]{2,1,0:T(8,128)(2,1)S(1)}, u32[]{:S(2)}, u32[]{:S(2)}) collective-permute-start(bf16[2,128,128]{2,1,0:T(8,128)(2,1)S(1)} %pair_two.1.refs_2_.refs_1_), channel_id=1, source_target_pairs={{0,16},{4,20},{8,24},{12,28},{16,0},{20,4},{24,8},{28,12},{1,17},{... | collective-permute-start | bytes 196616 | tf_op jit(solution)/shard_map/ppermute | solution.py:237
  36.6 6.2 %collective-permute-start.19 = (bf16[2,128,128]{2,1,0:T(8,128)(2,1)S(1)}, bf16[2,128,128]{2,1,0:T(8,128)(2,1)S(1)}, u32[]{:S(2)}, u32[]{:S(2)}) collective-permute-start(bf16[2,128,128]{2,1,0:T(8,128)(2,1)S(1)} %pair_two.1.refs_2_.refs_1_), channel_id=1, source_target_pairs={{0,8},{4,12},{8,0},{12,4},{16,24},{20,28},{24,16},{28,20},{1,9},{5... | collective-permute-start | bytes 196616 | tf_op jit(solution)/shard_map/ppermute | solution.py:237
  37.6 6.8 %collective-permute-start.28 = (bf16[2,128,128]{2,1,0:T(8,128)(2,1)S(1)}, bf16[2,128,128]{2,1,0:T(8,128)(2,1)S(1)}, u32[]{:S(2)}, u32[]{:S(2)}) collective-permute-start(bf16[2,128,128]{2,1,0:T(8,128)(2,1)S(1)} %get-tuple-element.59), channel_id=1, source_target_pairs={{0,4},{4,0},{8,12},{12,8},{16,20},{20,16},{24,28},{28,24},{1,5},{5... | collective-permute-start | bytes 196616 | tf_op jit(solution)/shard_map/ppermute | solution.py:237
  38.5 10.0 %collective-permute-start.27 = (bf16[128,128]{1,0:T(8,128)(2,1)S(1)}, bf16[128,128]{1,0:T(8,128)(2,1)S(1)}, u32[]{:S(2)}, u32[]{:S(2)}) collective-permute-start(bf16[128,128]{1,0:T(8,128)(2,1)S(1)} %get-tuple-element.57), channel_id=1, source_target_pairs={{0,24},{4,28},{8,16},{12,20},{16,8},{20,12},{24,0},{28,4},{1,25},{... | collective-permute-start | bytes 98312 | tf_op jit(solution)/shard_map/ppermute | solution.py:237
  42.3 6.2 %collective-permute-start.26 = (bf16[128,128]{1,0:T(8,128)(2,1)S(1)}, bf16[128,128]{1,0:T(8,128)(2,1)S(1)}, u32[]{:S(2)}, u32[]{:S(2)}) collective-permute-start(bf16[128,128]{1,0:T(8,128)(2,1)S(1)} %get-tuple-element.51.refs_5_), channel_id=1, source_target_pairs={{0,16},{4,20},{8,24},{12,28},{16,0},{20,4},{24,8},{28,12},{1,17},{... | collective-permute-start | bytes 98312 | tf_op jit(solution)/shard_map/ppermute | solution.py:237
  43.2 2.0 %collective-permute-start.23 = (bf16[128,128]{1,0:T(8,128)(2,1)S(1)}, bf16[128,128]{1,0:T(8,128)(2,1)S(1)}, u32[]{:S(2)}, u32[]{:S(2)}) collective-permute-start(bf16[128,128]{1,0:T(8,128)(2,1)S(1)} %get-tuple-element.53), channel_id=1, source_target_pairs={{0,1},{1,0},{2,3},{3,2},{4,5},{5,4},{6,7},{7,6},{8,9},{9,8},{10,11... | collective-permute-start | bytes 98312 | tf_op jit(solution)/shard_map/ppermute | solution.py:237
  43.3 4.0 %collective-permute-start.24 = (bf16[128,128]{1,0:T(8,128)(2,1)S(1)}, bf16[128,128]{1,0:T(8,128)(2,1)S(1)}, u32[]{:S(2)}, u32[]{:S(2)}) collective-permute-start(bf16[128,128]{1,0:T(8,128)(2,1)S(1)} %get-tuple-element.54), channel_id=1, source_target_pairs={{0,2},{1,3},{2,0},{3,1},{4,6},{5,7},{6,4},{7,5},{8,10},{9,11},{10,... | collective-permute-start | bytes 98312 | tf_op jit(solution)/shard_map/ppermute | solution.py:237
  44.4 3.3 %collective-permute-start.25 = (bf16[128,128]{1,0:T(8,128)(2,1)S(1)}, bf16[128,128]{1,0:T(8,128)(2,1)S(1)}, u32[]{:S(2)}, u32[]{:S(2)}) collective-permute-start(bf16[128,128]{1,0:T(8,128)(2,1)S(1)} %get-tuple-element.55), channel_id=1, source_target_pairs={{0,3},{1,2},{2,1},{3,0},{4,7},{5,6},{6,5},{7,4},{8,11},{9,10},{10,... | collective-permute-start | bytes 98312 | tf_op jit(solution)/shard_map/ppermute | solution.py:237
  45.2 4.0 %collective-permute-start.29 = (bf16[128,128]{1,0:T(8,128)(2,1)S(1)}, bf16[128,128]{1,0:T(8,128)(2,1)S(1)}, u32[]{:S(2)}, u32[]{:S(2)}) collective-permute-start(bf16[128,128]{1,0:T(8,128)(2,1)S(1)} %get-tuple-element.61), channel_id=1, source_target_pairs={{0,8},{4,12},{8,0},{12,4},{16,24},{20,28},{24,16},{28,20},{1,9},{5... | collective-permute-start | bytes 98312 | tf_op jit(solution)/shard_map/ppermute | solution.py:237
  47.8 1.4 %copy-start.1 = (f32[128,128]{1,0:T(8,128)S(1)}, f32[128,128]{1,0:T(8,128)}, u32[]{:S(2)}) copy-start(f32[128,128]{1,0:T(8,128)} %refs_0_.9) | copy-start | bytes 196612

commit v11 on v10

--- a/solution.py
+++ b/solution.py
@@ -224,13 +224,26 @@
 
 AFTER = {
     "dense": ("start",),
-    "pair_one": ("adjoint_one",),
-    "forward_one": ("far_one",),
-    "far_two": ("pair_two",),
-    "forward_two": ("far_two",),
-    "pair_two": ("adjoint_two",),
+    "pair_one_late": ("adjoint_one",),
+    "forward_one": ("far_one", "near_one"),
+    "forward_two": ("far_two", "near_two"),
+    "pair_two_late": ("adjoint_two",),
+    "forward_end": ("adjoint_end",),
+    "adjoint_one": ("pair_one_early",),
+    "pair_two_early": ("adjoint_middle",),
+    "forward_middle": ("adjoint_middle",),
 }
-COST = {"pair_one": 500, "adjoint_middle": 1000, "near_two": 500}
+COST = {
+    "pair_one_late": 1000,
+    "adjoint_middle": 1000,
+    "near_two": 500,
+    "pair_two_early": 500,
+    "far_two": 1000,
+    "far_one": 500,
+    "forward_end": 3000,
+    "pair_two_late": 1000,
+    "pair_one_early": 3000,
+}
 
 
 def send(value, axis, count, step):
@@ -317,15 +330,18 @@
             flops=hop_flops,
         )
 
-    def pair(name, part):
-        return run(name, pack_body, [shape(BF16, 2)], [part, send(part, "rows", n_rows, 1)])
-
-    def forward(name, both, kind):
+    def pair(name, part, other):
+        return run(name, pack_body, [shape(BF16, 2)], [part, other])
+
+    def forward(name, early, late, kind):
+        panels = [early] + [
+            send(early if s == half - 1 else late, "rows", n_rows, 2 * s) for s in range(1, half)
+        ]
         return run(
             name,
             lambda *refs: forward_body(half, n_cols, *refs),
             [shape(kind)] * n_cols,
-            [get("dense")[0], *spread(both, "rows", n_rows, 2)],
+            [get("dense")[0], *panels],
             flops=hop_flops,
         )
 
@@ -343,14 +359,19 @@
         start=start,
         dense=dense,
         adjoint_one=lambda: adjoint("adjoint_one", get("start")[0], F32),
-        pair_one=lambda: pair("pair_one", get("start")[1]),
+        other_one=lambda: send(get("start")[1], "rows", n_rows, 1),
+        other_two=lambda: send(get("forward_middle")[0], "rows", n_rows, 1),
+        pair_one_early=lambda: pair("pair_one_early", get("start")[1], get("other_one")),
+        pair_one_late=lambda: pair("pair_one_late", get("start")[1], get("other_one")),
         far_one=lambda: sums(
             "far_one", get("adjoint_one")[0], get("adjoint_one")[2], far_kinds(F32)
         ),
         near_one=lambda: sums(
             "near_one", get("adjoint_one")[1], get("adjoint_one")[3], near_kinds(F32)
         ),
-        forward_one=lambda: forward("forward_one", get("pair_one")[0], F32),
+        forward_one=lambda: forward(
+            "forward_one", get("pair_one_early")[0], get("pair_one_late")[0], F32
+        ),
         adjoint_middle=lambda: run(
             "adjoint_middle",
             adjoint_middle_body,
@@ -364,14 +385,17 @@
             [h_start, get("start")[3], *swap_cols(get("forward_one"))],
         ),
         adjoint_two=lambda: adjoint("adjoint_two", get("adjoint_middle")[1], BF16),
-        pair_two=lambda: pair("pair_two", get("forward_middle")[0]),
+        pair_two_early=lambda: pair("pair_two_early", get("forward_middle")[0], get("other_two")),
+        pair_two_late=lambda: pair("pair_two_late", get("forward_middle")[0], get("other_two")),
         far_two=lambda: sums(
             "far_two", get("adjoint_two")[0], get("adjoint_two")[2], far_kinds(BF16)
         ),
         near_two=lambda: sums(
             "near_two", get("adjoint_two")[1], get("adjoint_two")[3], near_kinds(BF16)
         ),
-        forward_two=lambda: forward("forward_two", get("pair_two")[0], BF16),
+        forward_two=lambda: forward(
+            "forward_two", get("pair_two_early")[0], get("pair_two_late")[0], BF16
+        ),
         forward_end=lambda: run(
             "forward_end",
             forward_end_body,

time: 50.4 us -> 51.2 us (1.016)
  starting transfers between devices: 34.7 us -> 35.6 us
  local copies, waits for them, and re-layouts: 0.01 us -> 0.85 us
  waiting for transfers between devices: 7.95 us -> 7.23 us
    ppermute x30, starting transfers between devices: 34.7 us -> 35.6 us  [send(): return lax.ppermute(value, axis, [(i, i ^ step) for i in range(count)])]
    unnamed x4 -> x6, local copies, waits for them, and re-layouts: 0.01 us -> 0.85 us
    ppermute x30, waiting for transfers between devices: 7.95 us -> 7.23 us  [send(): return lax.ppermute(value, axis, [(i, i ^ step) for i in range(count)])]
    pallas_call x16 -> x18, Pallas kernels: 5.83 us -> 5.86 us  [call(): pl.pallas_call(ordered, out_shape=outs, in_specs=[*in_specs, *[pl.BlockSp...]
  transfers between devices with their start and end apart: 30 -> 30, of which waited for: 9 -> 10; matrix products, arithmetic and copies ran while one was open for 0% -> 0% of each run, Pallas kernels for 8% -> 8%
where the time goes in v11:
time: 51.2 us; the launch traced here: 51 us
  starting transfers between devices  35.6 us (70%)
  waiting for transfers between devices  7.23 us (14%)
  Pallas kernels  5.86 us (11%)
  between operations  1.44 us (3%)
  local copies, waits for them, and re-layouts  0.85 us (2%)
    ppermute x30, starting transfers between devices, send(): return lax.ppermute(value, axis, [(i, i ^ step) for i in range(count)])  35.6 us
    ppermute x30, waiting for transfers between devices, send(): return lax.ppermute(value, axis, [(i, i ^ step) for i in range(count)])  7.23 us
    pallas_call x18, Pallas kernels, call(): pl.pallas_call(ordered, out_shape=outs, in_specs=[*in_specs, *[pl.BlockSp...  5.86 us
  transfers between devices with their start and end apart: 30, of which 10 were waited for; matrix products, arithmetic and copies ran while one was open for 0% of the time, Pallas kernels for 8%

profile of v11, /device:TPU:0, one launch (start us, length us, event | category | flops | bytes accessed | tf_op | source)
XLA Modules:
  0.0 51.0 jit_solution(8448763865477757627)
XLA Ops:
  0.6 1.0 %start.1 = (bf16[128,128]{1,0:T(8,128)(2,1)S(1)}, bf16[128,128]{1,0:T(8,128)(2,1)S(1)}, f32[1,128]{1,0:T(1,128)S(1)}, f32[128,128]{1,0:T(8,128)S(1)}) custom-call(f32[128,128]{1,0:T(8,128)} %refs_0_.8, f32[128,128]{1,0:T(8,128)} %refs_0_.9, s32[1,128]{1,0:T(1,128)} %bitcast.1, f32[8]{0:T(128)} %refs_3_.2), custom_call_target="tpu_custom_call" | custom-call | bytes 263200 | tf_op jit(solution)/shard_map/start/pallas_call | solution.py:36
  1.7 3.0 %collective-permute-start = (bf16[128,128]{1,0:T(8,128)(2,1)S(1)}, bf16[128,128]{1,0:T(8,128)(2,1)S(1)}, u32[]{:S(2)}, u32[]{:S(2)}) collective-permute-start(bf16[128,128]{1,0:T(8,128)(2,1)S(1)} %get-tuple-element.34.refs_0_), channel_id=1, source_target_pairs={{0,4},{4,0},{8,12},{12,8},{16,20},{20,16},{24,28},{28,24},{1,5},{5... | collective-permute-start | bytes 98312 | tf_op jit(solution)/shard_map/ppermute | solution.py:250
  4.7 0.7 %collective-permute-start.3 = (bf16[128,128]{1,0:T(8,128)(2,1)S(1)}, bf16[128,128]{1,0:T(8,128)(2,1)S(1)}, u32[]{:S(2)}, u32[]{:S(2)}) collective-permute-start(bf16[128,128]{1,0:T(8,128)(2,1)S(1)} %get-tuple-element.33.refs_4_.refs_1_), channel_id=1, source_target_pairs={{0,3},{1,2},{2,1},{3,0},{4,7},{5,6},{6,5},{7,4},{8,11},{9,10},{10,... | collective-permute-start | bytes 98312 | tf_op jit(solution)/shard_map/ppermute | solution.py:250
  5.4 0.9 %collective-permute-start.2 = (bf16[128,128]{1,0:T(8,128)(2,1)S(1)}, bf16[128,128]{1,0:T(8,128)(2,1)S(1)}, u32[]{:S(2)}, u32[]{:S(2)}) collective-permute-start(bf16[128,128]{1,0:T(8,128)(2,1)S(1)} %get-tuple-element.33.refs_4_.refs_1_), channel_id=1, source_target_pairs={{0,2},{1,3},{2,0},{3,1},{4,6},{5,7},{6,4},{7,5},{8,10},{9,11},{10,... | collective-permute-start | bytes 98312 | tf_op jit(solution)/shard_map/ppermute | solution.py:250
  6.2 0.3 collective-permute-start.1
  7.2 1.8 %dense.1.refs_0_ = bf16[512,1024]{1,0:T(8,128)(2,1)S(1)} custom-call(bf16[1,1,24,128,128]{4,3,2,1,0:T(8,128)(2,1)} %refs_0_.6, s32[1,1,24]{2,1,0:T(1,128)} %refs_1_.3, s32[1,1,24]{2,1,0:T(1,128)} %refs_2_.1, s32[1,1]{1,0:T(1,128)S(6)} %copy.10.refs_3_, bf16[128,128]{1,0:T(8,128)(2,1)S(1)} %get-tuple-element.33.refs_4_.refs_1_), custom_call_target="tpu_custom_call" | custom-call | bytes 1835204 | tf_op jit(solution)/shard_map/dense/pallas_call | solution.py:36
  9.1 0.6 %collective-permute-done.2.refs_3_ = bf16[128,128]{1,0:T(8,128)(2,1)S(1)} collective-permute-done((bf16[128,128]{1,0:T(8,128)(2,1)S(1)}, bf16[128,128]{1,0:T(8,128)(2,1)S(1)}, u32[]{:S(2)}, u32[]{:S(2)}) %collective-permute-start.2) | collective-permute-done | bytes 32800 | tf_op jit(solution)/shard_map/ppermute | solution.py:250
  9.6 0.3 adjoint_one.1
  9.9 0.6 %collective-permute-start.7 = (f32[2,128,128]{2,1,0:T(8,128)S(1)}, f32[2,128,128]{2,1,0:T(8,128)S(1)}, u32[]{:S(2)}, u32[]{:S(2)}) collective-permute-start(f32[2,128,128]{2,1,0:T(8,128)S(1)} %get-tuple-element.36), channel_id=1, source_target_pairs={{0,4},{4,0},{8,12},{12,8},{16,20},{20,16},{24,28},{28,24},{1,5},{5... | collective-permute-start | bytes 393224 | tf_op jit(solution)/shard_map/ppermute | solution.py:250
  10.5 3.6 %collective-permute-start.6 = (bf16[2,128,128]{2,1,0:T(8,128)(2,1)S(1)}, bf16[2,128,128]{2,1,0:T(8,128)(2,1)S(1)}, u32[]{:S(2)}, u32[]{:S(2)}) collective-permute-start(bf16[2,128,128]{2,1,0:T(8,128)(2,1)S(1)} %pair_one_early.1.refs_5_.refs_1_), channel_id=1, source_target_pairs={{0,24},{4,28},{8,16},{12,20},{16,8},{20,12},{24,0},{28,4},{1,25},{... | collective-permute-start | bytes 196616 | tf_op jit(solution)/shard_map/ppermute | solution.py:250
  14.1 1.5 %collective-permute-start.8 = (f32[2,128,128]{2,1,0:T(8,128)S(1)}, f32[2,128,128]{2,1,0:T(8,128)S(1)}, u32[]{:S(2)}, u32[]{:S(2)}) collective-permute-start(f32[2,128,128]{2,1,0:T(8,128)S(1)} %get-tuple-element.39), channel_id=1, source_target_pairs={{0,4},{4,0},{8,12},{12,8},{16,20},{20,16},{24,28},{28,24},{1,5},{5... | collective-permute-start | bytes 393224 | tf_op jit(solution)/shard_map/ppermute | solution.py:250
  15.6 0.8 %collective-permute-start.4 = (bf16[2,128,128]{2,1,0:T(8,128)(2,1)S(1)}, bf16[2,128,128]{2,1,0:T(8,128)(2,1)S(1)}, u32[]{:S(2)}, u32[]{:S(2)}) collective-permute-start(bf16[2,128,128]{2,1,0:T(8,128)(2,1)S(1)} %pair_one_late.1), channel_id=1, source_target_pairs={{0,8},{4,12},{8,0},{12,4},{16,24},{20,28},{24,16},{28,20},{1,9},{5... | collective-permute-start | bytes 196616 | tf_op jit(solution)/shard_map/ppermute | solution.py:250
  16.4 3.7 %collective-permute-start.13 = (f32[128,128]{1,0:T(8,128)S(1)}, f32[128,128]{1,0:T(8,128)S(1)}, u32[]{:S(2)}, u32[]{:S(2)}) collective-permute-start(f32[128,128]{1,0:T(8,128)S(1)} %get-tuple-element.46), channel_id=1, source_target_pairs={{0,24},{4,28},{8,16},{12,20},{16,8},{20,12},{24,0},{28,4},{1,25},{... | collective-permute-start | bytes 196616 | tf_op jit(solution)/shard_map/ppermute | solution.py:250
  20.1 0.8 %collective-permute-start.12 = (f32[128,128]{1,0:T(8,128)S(1)}, f32[128,128]{1,0:T(8,128)S(1)}, u32[]{:S(2)}, u32[]{:S(2)}) collective-permute-start(f32[128,128]{1,0:T(8,128)S(1)} %get-tuple-element.37.refs_5_), channel_id=1, source_target_pairs={{0,16},{4,20},{8,24},{12,28},{16,0},{20,4},{24,8},{28,12},{1,17},{... | collective-permute-start | bytes 196616 | tf_op jit(solution)/shard_map/ppermute | solution.py:250
  20.9 1.6 %collective-permute-start.14 = (f32[128,128]{1,0:T(8,128)S(1)}, f32[128,128]{1,0:T(8,128)S(1)}, u32[]{:S(2)}, u32[]{:S(2)}) collective-permute-start(f32[128,128]{1,0:T(8,128)S(1)} %get-tuple-element.47), channel_id=1, source_target_pairs={{0,8},{4,12},{8,0},{12,4},{16,24},{20,28},{24,16},{28,20},{1,9},{5... | collective-permute-start | bytes 196616 | tf_op jit(solution)/shard_map/ppermute | solution.py:250
  22.6 0.4 forward_one.1
  23.0 0.1 collective-permute-start.9
  23.1 1.2 %collective-permute-start.10 = (f32[128,128]{1,0:T(8,128)S(1)}, f32[128,128]{1,0:T(8,128)S(1)}, u32[]{:S(2)}, u32[]{:S(2)}) collective-permute-start(f32[128,128]{1,0:T(8,128)S(1)} %get-tuple-element.43), channel_id=1, source_target_pairs={{0,2},{1,3},{2,0},{3,1},{4,6},{5,7},{6,4},{7,5},{8,10},{9,11},{10,... | collective-permute-start | bytes 196616 | tf_op jit(solution)/shard_map/ppermute | solution.py:250
  24.3 0.7 %collective-permute-start.11 = (f32[128,128]{1,0:T(8,128)S(1)}, f32[128,128]{1,0:T(8,128)S(1)}, u32[]{:S(2)}, u32[]{:S(2)}) collective-permute-start(f32[128,128]{1,0:T(8,128)S(1)} %get-tuple-element.44), channel_id=1, source_target_pairs={{0,3},{1,2},{2,1},{3,0},{4,7},{5,6},{6,5},{7,4},{8,11},{9,10},{10,... | collective-permute-start | bytes 196616 | tf_op jit(solution)/shard_map/ppermute | solution.py:250
  25.0 1.2 %collective-permute-done.12.refs_1_ = f32[128,128]{1,0:T(8,128)S(1)} collective-permute-done((f32[128,128]{1,0:T(8,128)S(1)}, f32[128,128]{1,0:T(8,128)S(1)}, u32[]{:S(2)}, u32[]{:S(2)}) %collective-permute-start.12) | collective-permute-done | bytes 65568 | tf_op jit(solution)/shard_map/ppermute | solution.py:250
  26.2 0.1 collective-permute-done.14.refs_4_
  26.3 0.2 collective-permute-start.18
  26.5 1.0 %collective-permute-start.17 = (bf16[128,128]{1,0:T(8,128)(2,1)S(1)}, bf16[128,128]{1,0:T(8,128)(2,1)S(1)}, u32[]{:S(2)}, u32[]{:S(2)}) collective-permute-start(bf16[128,128]{1,0:T(8,128)(2,1)S(1)} %get-tuple-element.49.refs_1_), channel_id=1, source_target_pairs={{0,2},{1,3},{2,0},{3,1},{4,6},{5,7},{6,4},{7,5},{8,10},{9,11},{10,... | collective-permute-start | bytes 98312 | tf_op jit(solution)/shard_map/ppermute | solution.py:250
  27.4 0.8 %collective-permute-start.16 = (bf16[128,128]{1,0:T(8,128)(2,1)S(1)}, bf16[128,128]{1,0:T(8,128)(2,1)S(1)}, u32[]{:S(2)}, u32[]{:S(2)}) collective-permute-start(bf16[128,128]{1,0:T(8,128)(2,1)S(1)} %get-tuple-element.49.refs_1_), channel_id=1, source_target_pairs={{0,1},{1,0},{2,3},{3,2},{4,5},{5,4},{6,7},{7,6},{8,9},{9,8},{10,11... | collective-permute-start | bytes 98312 | tf_op jit(solution)/shard_map/ppermute | solution.py:250
  28.2 0.3 collective-permute-done.11.refs_5_
  28.6 0.6 %collective-permute-start.15 = (bf16[128,128]{1,0:T(8,128)(2,1)S(1)}, bf16[128,128]{1,0:T(8,128)(2,1)S(1)}, u32[]{:S(2)}, u32[]{:S(2)}) collective-permute-start(bf16[128,128]{1,0:T(8,128)(2,1)S(1)} %forward_middle.1.refs_0_), channel_id=1, source_target_pairs={{0,4},{4,0},{8,12},{12,8},{16,20},{20,16},{24,28},{28,24},{1,5},{5... | collective-permute-start | bytes 98312 | tf_op jit(solution)/shard_map/ppermute | solution.py:250
  29.2 0.5 collective-permute-done.18.refs_4_
  29.7 1.0 %collective-permute-done.17.refs_3_ = bf16[128,128]{1,0:T(8,128)(2,1)S(1)} collective-permute-done((bf16[128,128]{1,0:T(8,128)(2,1)S(1)}, bf16[128,128]{1,0:T(8,128)(2,1)S(1)}, u32[]{:S(2)}, u32[]{:S(2)}) %collective-permute-start.17) | collective-permute-done | bytes 32800 | tf_op jit(solution)/shard_map/ppermute | solution.py:250
  30.7 0.3 adjoint_two.1
  31.0 0.5 collective-permute-start.22
  31.5 1.1 %collective-permute-done.15.refs_1_ = bf16[128,128]{1,0:T(8,128)(2,1)S(1)} collective-permute-done((bf16[128,128]{1,0:T(8,128)(2,1)S(1)}, bf16[128,128]{1,0:T(8,128)(2,1)S(1)}, u32[]{:S(2)}, u32[]{:S(2)}) %collective-permute-start.15) | collective-permute-done | bytes 32800 | tf_op jit(solution)/shard_map/ppermute | solution.py:250
  32.6 1.5 %collective-permute-start.20 = (bf16[2,128,128]{2,1,0:T(8,128)(2,1)S(1)}, bf16[2,128,128]{2,1,0:T(8,128)(2,1)S(1)}, u32[]{:S(2)}, u32[]{:S(2)}) collective-permute-start(bf16[2,128,128]{2,1,0:T(8,128)(2,1)S(1)} %pair_two_late.1), channel_id=1, source_target_pairs={{0,16},{4,20},{8,24},{12,28},{16,0},{20,4},{24,8},{28,12},{1,17},{... | collective-permute-start | bytes 196616 | tf_op jit(solution)/shard_map/ppermute | solution.py:250
  34.1 1.3 %collective-permute-start.19 = (bf16[2,128,128]{2,1,0:T(8,128)(2,1)S(1)}, bf16[2,128,128]{2,1,0:T(8,128)(2,1)S(1)}, u32[]{:S(2)}, u32[]{:S(2)}) collective-permute-start(bf16[2,128,128]{2,1,0:T(8,128)(2,1)S(1)} %pair_two_late.1), channel_id=1, source_target_pairs={{0,8},{4,12},{8,0},{12,4},{16,24},{20,28},{24,16},{28,20},{1,9},{5... | collective-permute-start | bytes 196616 | tf_op jit(solution)/shard_map/ppermute | solution.py:250
  35.5 1.5 %collective-permute-start.21 = (bf16[2,128,128]{2,1,0:T(8,128)(2,1)S(1)}, bf16[2,128,128]{2,1,0:T(8,128)(2,1)S(1)}, u32[]{:S(2)}, u32[]{:S(2)}) collective-permute-start(bf16[2,128,128]{2,1,0:T(8,128)(2,1)S(1)} %pair_two_early.1.refs_1_), channel_id=1, source_target_pairs={{0,24},{4,28},{8,16},{12,20},{16,8},{20,12},{24,0},{28,4},{1,25},{... | collective-permute-start | bytes 196616 | tf_op jit(solution)/shard_map/ppermute | solution.py:250
  37.0 0.6 %collective-permute-start.23 = (bf16[2,128,128]{2,1,0:T(8,128)(2,1)S(1)}, bf16[2,128,128]{2,1,0:T(8,128)(2,1)S(1)}, u32[]{:S(2)}, u32[]{:S(2)}) collective-permute-start(bf16[2,128,128]{2,1,0:T(8,128)(2,1)S(1)} %get-tuple-element.54), channel_id=1, source_target_pairs={{0,4},{4,0},{8,12},{12,8},{16,20},{20,16},{24,28},{28,24},{1,5},{5... | collective-permute-start | bytes 196616 | tf_op jit(solution)/shard_map/ppermute | solution.py:250
  37.6 3.4 %collective-permute-start.28 = (bf16[128,128]{1,0:T(8,128)(2,1)S(1)}, bf16[128,128]{1,0:T(8,128)(2,1)S(1)}, u32[]{:S(2)}, u32[]{:S(2)}) collective-permute-start(bf16[128,128]{1,0:T(8,128)(2,1)S(1)} %get-tuple-element.60), channel_id=1, source_target_pairs={{0,24},{4,28},{8,16},{12,20},{16,8},{20,12},{24,0},{28,4},{1,25},{... | collective-permute-start | bytes 98312 | tf_op jit(solution)/shard_map/ppermute | solution.py:250
  41.1 0.2 collective-permute-done.23.refs_1_
  41.3 0.6 %collective-permute-start.27 = (bf16[128,128]{1,0:T(8,128)(2,1)S(1)}, bf16[128,128]{1,0:T(8,128)(2,1)S(1)}, u32[]{:S(2)}, u32[]{:S(2)}) collective-permute-start(bf16[128,128]{1,0:T(8,128)(2,1)S(1)} %get-tuple-element.52.refs_5_), channel_id=1, source_target_pairs={{0,16},{4,20},{8,24},{12,28},{16,0},{20,4},{24,8},{28,12},{1,17},{... | collective-permute-start | bytes 98312 | tf_op jit(solution)/shard_map/ppermute | solution.py:250
  41.9 2.3 %collective-permute-start.29 = (bf16[128,128]{1,0:T(8,128)(2,1)S(1)}, bf16[128,128]{1,0:T(8,128)(2,1)S(1)}, u32[]{:S(2)}, u32[]{:S(2)}) collective-permute-start(bf16[128,128]{1,0:T(8,128)(2,1)S(1)} %get-tuple-element.61), channel_id=1, source_target_pairs={{0,8},{4,12},{8,0},{12,4},{16,24},{20,28},{24,16},{28,20},{1,9},{5... | collective-permute-start | bytes 98312 | tf_op jit(solution)/shard_map/ppermute | solution.py:250
  44.2 0.4 forward_two.1
  44.7 0.1 collective-permute-start.24
  44.7 1.4 %collective-permute-start.25 = (bf16[128,128]{1,0:T(8,128)(2,1)S(1)}, bf16[128,128]{1,0:T(8,128)(2,1)S(1)}, u32[]{:S(2)}, u32[]{:S(2)}) collective-permute-start(bf16[128,128]{1,0:T(8,128)(2,1)S(1)} %get-tuple-element.58), channel_id=1, source_target_pairs={{0,2},{1,3},{2,0},{3,1},{4,6},{5,7},{6,4},{7,5},{8,10},{9,11},{10,... | collective-permute-start | bytes 98312 | tf_op jit(solution)/shard_map/ppermute | solution.py:250
  46.2 0.5 collective-permute-start.26
  46.6 0.7 %adjoint_end.1.refs_6_ = f32[128,128]{1,0:T(8,128)} custom-call(f32[128,128]{1,0:T(8,128)S(1)} %copy-done.1, f32[128,128]{1,0:T(8,128)S(1)} %get-tuple-element.48.refs_6_.refs_2_.refs_1_, f32[1,128]{1,0:T(1,128)S(1)} %get-tuple-element.45.refs_0_.refs_2_, f32[128,128]{1,0:T(8,128)S(1)} %get-tuple-element.32.refs_1_.refs_3_, ...), custom_call_target="tpu_custom_call" | custom-call | bytes 426496 | tf_op jit(solution)/shard_map/adjoint_end/pallas_call | solution.py:36
  47.4 1.4 %collective-permute-done.25.refs_4_ = bf16[128,128]{1,0:T(8,128)(2,1)S(1)} collective-permute-done((bf16[128,128]{1,0:T(8,128)(2,1)S(1)}, bf16[128,128]{1,0:T(8,128)(2,1)S(1)}, u32[]{:S(2)}, u32[]{:S(2)}) %collective-permute-start.25) | collective-permute-done | bytes 32800 | tf_op jit(solution)/shard_map/ppermute | solution.py:250
  48.7 0.8 %collective-permute-done.26.refs_5_ = bf16[128,128]{1,0:T(8,128)(2,1)S(1)} collective-permute-done((bf16[128,128]{1,0:T(8,128)(2,1)S(1)}, bf16[128,128]{1,0:T(8,128)(2,1)S(1)}, u32[]{:S(2)}, u32[]{:S(2)}) %collective-permute-start.26) | collective-permute-done | bytes 32800 | tf_op jit(solution)/shard_map/ppermute | solution.py:250
  49.5 0.8 %copy-done.2 = f32[128,128]{1,0:T(8,128)S(1)} copy-done((f32[128,128]{1,0:T(8,128)S(1)}, f32[128,128]{1,0:T(8,128)}, u32[]{:S(2)}) %copy-start.2) | copy-done | bytes 65560
  50.3 0.7 %forward_end.1 = f32[128,128]{1,0:T(8,128)} custom-call(f32[128,128]{1,0:T(8,128)S(1)} %copy-done, f32[128,128]{1,0:T(8,128)S(1)} %get-tuple-element.32.refs_1_.refs_3_, bf16[128,128]{1,0:T(8,128)(2,1)S(1)} %get-tuple-element.56.refs_2_, bf16[128,128]{1,0:T(8,128)(2,1)S(1)} %collective-permute-done.24.refs_3_, ...), custom_call_target="tpu_custom_call" | custom-call | flops 3000000000 | bytes 327680 | tf_op jit(solution)/shard_map/forward_end/pallas_call | solution.py:36
  (36 shorter events, 0.2 us)
Async XLA Ops:
  1.7 7.4 %collective-permute-start = (bf16[128,128]{1,0:T(8,128)(2,1)S(1)}, bf16[128,128]{1,0:T(8,128)(2,1)S(1)}, u32[]{:S(2)}, u32[]{:S(2)}) collective-permute-start(bf16[128,128]{1,0:T(8,128)(2,1)S(1)} %get-tuple-element.34.refs_0_), channel_id=1, source_target_pairs={{0,4},{4,0},{8,12},{12,8},{16,20},{20,16},{24,28},{28,24},{1,5},{5... | collective-permute-start | bytes 98312 | tf_op jit(solution)/shard_map/ppermute | solution.py:250
  4.7 4.3 %collective-permute-start.3 = (bf16[128,128]{1,0:T(8,128)(2,1)S(1)}, bf16[128,128]{1,0:T(8,128)(2,1)S(1)}, u32[]{:S(2)}, u32[]{:S(2)}) collective-permute-start(bf16[128,128]{1,0:T(8,128)(2,1)S(1)} %get-tuple-element.33.refs_4_.refs_1_), channel_id=1, source_target_pairs={{0,3},{1,2},{2,1},{3,0},{4,7},{5,6},{6,5},{7,4},{8,11},{9,10},{10,... | collective-permute-start | bytes 98312 | tf_op jit(solution)/shard_map/ppermute | solution.py:250
  5.4 4.3 %collective-permute-start.2 = (bf16[128,128]{1,0:T(8,128)(2,1)S(1)}, bf16[128,128]{1,0:T(8,128)(2,1)S(1)}, u32[]{:S(2)}, u32[]{:S(2)}) collective-permute-start(bf16[128,128]{1,0:T(8,128)(2,1)S(1)} %get-tuple-element.33.refs_4_.refs_1_), channel_id=1, source_target_pairs={{0,2},{1,3},{2,0},{3,1},{4,6},{5,7},{6,4},{7,5},{8,10},{9,11},{10,... | collective-permute-start | bytes 98312 | tf_op jit(solution)/shard_map/ppermute | solution.py:250
  6.2 3.4 %collective-permute-start.1 = (bf16[128,128]{1,0:T(8,128)(2,1)S(1)}, bf16[128,128]{1,0:T(8,128)(2,1)S(1)}, u32[]{:S(2)}, u32[]{:S(2)}) collective-permute-start(bf16[128,128]{1,0:T(8,128)(2,1)S(1)} %get-tuple-element.33.refs_4_.refs_1_), channel_id=1, source_target_pairs={{0,1},{1,0},{2,3},{3,2},{4,5},{5,4},{6,7},{7,6},{8,9},{9,8},{10,11... | collective-permute-start | bytes 98312 | tf_op jit(solution)/shard_map/ppermute | solution.py:250
  9.9 6.5 %collective-permute-start.7 = (f32[2,128,128]{2,1,0:T(8,128)S(1)}, f32[2,128,128]{2,1,0:T(8,128)S(1)}, u32[]{:S(2)}, u32[]{:S(2)}) collective-permute-start(f32[2,128,128]{2,1,0:T(8,128)S(1)} %get-tuple-element.36), channel_id=1, source_target_pairs={{0,4},{4,0},{8,12},{12,8},{16,20},{20,16},{24,28},{28,24},{1,5},{5... | collective-permute-start | bytes 393224 | tf_op jit(solution)/shard_map/ppermute | solution.py:250
  10.5 10.4 %collective-permute-start.6 = (bf16[2,128,128]{2,1,0:T(8,128)(2,1)S(1)}, bf16[2,128,128]{2,1,0:T(8,128)(2,1)S(1)}, u32[]{:S(2)}, u32[]{:S(2)}) collective-permute-start(bf16[2,128,128]{2,1,0:T(8,128)(2,1)S(1)} %pair_one_early.1.refs_5_.refs_1_), channel_id=1, source_target_pairs={{0,24},{4,28},{8,16},{12,20},{16,8},{20,12},{24,0},{28,4},{1,25},{... | collective-permute-start | bytes 196616 | tf_op jit(solution)/shard_map/ppermute | solution.py:250
  14.1 6.0 %collective-permute-start.8 = (f32[2,128,128]{2,1,0:T(8,128)S(1)}, f32[2,128,128]{2,1,0:T(8,128)S(1)}, u32[]{:S(2)}, u32[]{:S(2)}) collective-permute-start(f32[2,128,128]{2,1,0:T(8,128)S(1)} %get-tuple-element.39), channel_id=1, source_target_pairs={{0,4},{4,0},{8,12},{12,8},{16,20},{20,16},{24,28},{28,24},{1,5},{5... | collective-permute-start | bytes 393224 | tf_op jit(solution)/shard_map/ppermute | solution.py:250
  15.6 6.9 %collective-permute-start.5 = (bf16[2,128,128]{2,1,0:T(8,128)(2,1)S(1)}, bf16[2,128,128]{2,1,0:T(8,128)(2,1)S(1)}, u32[]{:S(2)}, u32[]{:S(2)}) collective-permute-start(bf16[2,128,128]{2,1,0:T(8,128)(2,1)S(1)} %pair_one_late.1), channel_id=1, source_target_pairs={{0,16},{4,20},{8,24},{12,28},{16,0},{20,4},{24,8},{28,12},{1,17},{... | collective-permute-start | bytes 196616 | tf_op jit(solution)/shard_map/ppermute | solution.py:250
  15.6 6.9 %collective-permute-start.4 = (bf16[2,128,128]{2,1,0:T(8,128)(2,1)S(1)}, bf16[2,128,128]{2,1,0:T(8,128)(2,1)S(1)}, u32[]{:S(2)}, u32[]{:S(2)}) collective-permute-start(bf16[2,128,128]{2,1,0:T(8,128)(2,1)S(1)} %pair_one_late.1), channel_id=1, source_target_pairs={{0,8},{4,12},{8,0},{12,4},{16,24},{20,28},{24,16},{28,20},{1,9},{5... | collective-permute-start | bytes 196616 | tf_op jit(solution)/shard_map/ppermute | solution.py:250
  16.4 7.8 %collective-permute-start.13 = (f32[128,128]{1,0:T(8,128)S(1)}, f32[128,128]{1,0:T(8,128)S(1)}, u32[]{:S(2)}, u32[]{:S(2)}) collective-permute-start(f32[128,128]{1,0:T(8,128)S(1)} %get-tuple-element.46), channel_id=1, source_target_pairs={{0,24},{4,28},{8,16},{12,20},{16,8},{20,12},{24,0},{28,4},{1,25},{... | collective-permute-start | bytes 196616 | tf_op jit(solution)/shard_map/ppermute | solution.py:250
  20.1 6.1 %collective-permute-start.12 = (f32[128,128]{1,0:T(8,128)S(1)}, f32[128,128]{1,0:T(8,128)S(1)}, u32[]{:S(2)}, u32[]{:S(2)}) collective-permute-start(f32[128,128]{1,0:T(8,128)S(1)} %get-tuple-element.37.refs_5_), channel_id=1, source_target_pairs={{0,16},{4,20},{8,24},{12,28},{16,0},{20,4},{24,8},{28,12},{1,17},{... | collective-permute-start | bytes 196616 | tf_op jit(solution)/shard_map/ppermute | solution.py:250
  20.9 5.4 %collective-permute-start.14 = (f32[128,128]{1,0:T(8,128)S(1)}, f32[128,128]{1,0:T(8,128)S(1)}, u32[]{:S(2)}, u32[]{:S(2)}) collective-permute-start(f32[128,128]{1,0:T(8,128)S(1)} %get-tuple-element.47), channel_id=1, source_target_pairs={{0,8},{4,12},{8,0},{12,4},{16,24},{20,28},{24,16},{28,20},{1,9},{5... | collective-permute-start | bytes 196616 | tf_op jit(solution)/shard_map/ppermute | solution.py:250
  23.0 4.4 %collective-permute-start.9 = (f32[128,128]{1,0:T(8,128)S(1)}, f32[128,128]{1,0:T(8,128)S(1)}, u32[]{:S(2)}, u32[]{:S(2)}) collective-permute-start(f32[128,128]{1,0:T(8,128)S(1)} %get-tuple-element.42), channel_id=1, source_target_pairs={{0,1},{1,0},{2,3},{3,2},{4,5},{5,4},{6,7},{7,6},{8,9},{9,8},{10,11... | collective-permute-start | bytes 196616 | tf_op jit(solution)/shard_map/ppermute | solution.py:250
  23.1 5.2 %collective-permute-start.10 = (f32[128,128]{1,0:T(8,128)S(1)}, f32[128,128]{1,0:T(8,128)S(1)}, u32[]{:S(2)}, u32[]{:S(2)}) collective-permute-start(f32[128,128]{1,0:T(8,128)S(1)} %get-tuple-element.43), channel_id=1, source_target_pairs={{0,2},{1,3},{2,0},{3,1},{4,6},{5,7},{6,4},{7,5},{8,10},{9,11},{10,... | collective-permute-start | bytes 196616 | tf_op jit(solution)/shard_map/ppermute | solution.py:250
  24.3 4.3 %collective-permute-start.11 = (f32[128,128]{1,0:T(8,128)S(1)}, f32[128,128]{1,0:T(8,128)S(1)}, u32[]{:S(2)}, u32[]{:S(2)}) collective-permute-start(f32[128,128]{1,0:T(8,128)S(1)} %get-tuple-element.44), channel_id=1, source_target_pairs={{0,3},{1,2},{2,1},{3,0},{4,7},{5,6},{6,5},{7,4},{8,11},{9,10},{10,... | collective-permute-start | bytes 196616 | tf_op jit(solution)/shard_map/ppermute | solution.py:250
  26.3 2.3 %copy-start = (f32[128,128]{1,0:T(8,128)S(1)}, f32[128,128]{1,0:T(8,128)}, u32[]{:S(2)}) copy-start(f32[128,128]{1,0:T(8,128)} %refs_0_.9) | copy-start | bytes 196612
  26.3 3.4 %collective-permute-start.18 = (bf16[128,128]{1,0:T(8,128)(2,1)S(1)}, bf16[128,128]{1,0:T(8,128)(2,1)S(1)}, u32[]{:S(2)}, u32[]{:S(2)}) collective-permute-start(bf16[128,128]{1,0:T(8,128)(2,1)S(1)} %get-tuple-element.49.refs_1_), channel_id=1, source_target_pairs={{0,3},{1,2},{2,1},{3,0},{4,7},{5,6},{6,5},{7,4},{8,11},{9,10},{10,... | collective-permute-start | bytes 98312 | tf_op jit(solution)/shard_map/ppermute | solution.py:250
  26.5 4.3 %collective-permute-start.17 = (bf16[128,128]{1,0:T(8,128)(2,1)S(1)}, bf16[128,128]{1,0:T(8,128)(2,1)S(1)}, u32[]{:S(2)}, u32[]{:S(2)}) collective-permute-start(bf16[128,128]{1,0:T(8,128)(2,1)S(1)} %get-tuple-element.49.refs_1_), channel_id=1, source_target_pairs={{0,2},{1,3},{2,0},{3,1},{4,6},{5,7},{6,4},{7,5},{8,10},{9,11},{10,... | collective-permute-start | bytes 98312 | tf_op jit(solution)/shard_map/ppermute | solution.py:250
  27.4 3.3 %collective-permute-start.16 = (bf16[128,128]{1,0:T(8,128)(2,1)S(1)}, bf16[128,128]{1,0:T(8,128)(2,1)S(1)}, u32[]{:S(2)}, u32[]{:S(2)}) collective-permute-start(bf16[128,128]{1,0:T(8,128)(2,1)S(1)} %get-tuple-element.49.refs_1_), channel_id=1, source_target_pairs={{0,1},{1,0},{2,3},{3,2},{4,5},{5,4},{6,7},{7,6},{8,9},{9,8},{10,11... | collective-permute-start | bytes 98312 | tf_op jit(solution)/shard_map/ppermute | solution.py:250
  28.6 4.0 %collective-permute-start.15 = (bf16[128,128]{1,0:T(8,128)(2,1)S(1)}, bf16[128,128]{1,0:T(8,128)(2,1)S(1)}, u32[]{:S(2)}, u32[]{:S(2)}) collective-permute-start(bf16[128,128]{1,0:T(8,128)(2,1)S(1)} %forward_middle.1.refs_0_), channel_id=1, source_target_pairs={{0,4},{4,0},{8,12},{12,8},{16,20},{20,16},{24,28},{28,24},{1,5},{5... | collective-permute-start | bytes 98312 | tf_op jit(solution)/shard_map/ppermute | solution.py:250
  31.0 6.6 %collective-permute-start.22 = (bf16[2,128,128]{2,1,0:T(8,128)(2,1)S(1)}, bf16[2,128,128]{2,1,0:T(8,128)(2,1)S(1)}, u32[]{:S(2)}, u32[]{:S(2)}) collective-permute-start(bf16[2,128,128]{2,1,0:T(8,128)(2,1)S(1)} %get-tuple-element.51), channel_id=1, source_target_pairs={{0,4},{4,0},{8,12},{12,8},{16,20},{20,16},{24,28},{28,24},{1,5},{5... | collective-permute-start | bytes 196616 | tf_op jit(solution)/shard_map/ppermute | solution.py:250
  32.6 11.6 %collective-permute-start.20 = (bf16[2,128,128]{2,1,0:T(8,128)(2,1)S(1)}, bf16[2,128,128]{2,1,0:T(8,128)(2,1)S(1)}, u32[]{:S(2)}, u32[]{:S(2)}) collective-permute-start(bf16[2,128,128]{2,1,0:T(8,128)(2,1)S(1)} %pair_two_late.1), channel_id=1, source_target_pairs={{0,16},{4,20},{8,24},{12,28},{16,0},{20,4},{24,8},{28,12},{1,17},{... | collective-permute-start | bytes 196616 | tf_op jit(solution)/shard_map/ppermute | solution.py:250
  34.1 10.1 %collective-permute-start.19 = (bf16[2,128,128]{2,1,0:T(8,128)(2,1)S(1)}, bf16[2,128,128]{2,1,0:T(8,128)(2,1)S(1)}, u32[]{:S(2)}, u32[]{:S(2)}) collective-permute-start(bf16[2,128,128]{2,1,0:T(8,128)(2,1)S(1)} %pair_two_late.1), channel_id=1, source_target_pairs={{0,8},{4,12},{8,0},{12,4},{16,24},{20,28},{24,16},{28,20},{1,9},{5... | collective-permute-start | bytes 196616 | tf_op jit(solution)/shard_map/ppermute | solution.py:250
  35.5 6.5 %collective-permute-start.21 = (bf16[2,128,128]{2,1,0:T(8,128)(2,1)S(1)}, bf16[2,128,128]{2,1,0:T(8,128)(2,1)S(1)}, u32[]{:S(2)}, u32[]{:S(2)}) collective-permute-start(bf16[2,128,128]{2,1,0:T(8,128)(2,1)S(1)} %pair_two_early.1.refs_1_), channel_id=1, source_target_pairs={{0,24},{4,28},{8,16},{12,20},{16,8},{20,12},{24,0},{28,4},{1,25},{... | collective-permute-start | bytes 196616 | tf_op jit(solution)/shard_map/ppermute | solution.py:250
  37.0 4.3 %collective-permute-start.23 = (bf16[2,128,128]{2,1,0:T(8,128)(2,1)S(1)}, bf16[2,128,128]{2,1,0:T(8,128)(2,1)S(1)}, u32[]{:S(2)}, u32[]{:S(2)}) collective-permute-start(bf16[2,128,128]{2,1,0:T(8,128)(2,1)S(1)} %get-tuple-element.54), channel_id=1, source_target_pairs={{0,4},{4,0},{8,12},{12,8},{16,20},{20,16},{24,28},{28,24},{1,5},{5... | collective-permute-start | bytes 196616 | tf_op jit(solution)/shard_map/ppermute | solution.py:250
  37.6 8.5 %collective-permute-start.28 = (bf16[128,128]{1,0:T(8,128)(2,1)S(1)}, bf16[128,128]{1,0:T(8,128)(2,1)S(1)}, u32[]{:S(2)}, u32[]{:S(2)}) collective-permute-start(bf16[128,128]{1,0:T(8,128)(2,1)S(1)} %get-tuple-element.60), channel_id=1, source_target_pairs={{0,24},{4,28},{8,16},{12,20},{16,8},{20,12},{24,0},{28,4},{1,25},{... | collective-permute-start | bytes 98312 | tf_op jit(solution)/shard_map/ppermute | solution.py:250
  41.3 5.3 %collective-permute-start.27 = (bf16[128,128]{1,0:T(8,128)(2,1)S(1)}, bf16[128,128]{1,0:T(8,128)(2,1)S(1)}, u32[]{:S(2)}, u32[]{:S(2)}) collective-permute-start(bf16[128,128]{1,0:T(8,128)(2,1)S(1)} %get-tuple-element.52.refs_5_), channel_id=1, source_target_pairs={{0,16},{4,20},{8,24},{12,28},{16,0},{20,4},{24,8},{28,12},{1,17},{... | collective-permute-start | bytes 98312 | tf_op jit(solution)/shard_map/ppermute | solution.py:250
  41.9 4.7 %collective-permute-start.29 = (bf16[128,128]{1,0:T(8,128)(2,1)S(1)}, bf16[128,128]{1,0:T(8,128)(2,1)S(1)}, u32[]{:S(2)}, u32[]{:S(2)}) collective-permute-start(bf16[128,128]{1,0:T(8,128)(2,1)S(1)} %get-tuple-element.61), channel_id=1, source_target_pairs={{0,8},{4,12},{8,0},{12,4},{16,24},{20,28},{24,16},{28,20},{1,9},{5... | collective-permute-start | bytes 98312 | tf_op jit(solution)/shard_map/ppermute | solution.py:250
  44.2 2.4 %copy-start.1 = (f32[128,128]{1,0:T(8,128)S(1)}, f32[128,128]{1,0:T(8,128)}, u32[]{:S(2)}) copy-start(f32[128,128]{1,0:T(8,128)} %refs_0_.8) | copy-start | bytes 196612
  44.7 2.7 %collective-permute-start.24 = (bf16[128,128]{1,0:T(8,128)(2,1)S(1)}, bf16[128,128]{1,0:T(8,128)(2,1)S(1)}, u32[]{:S(2)}, u32[]{:S(2)}) collective-permute-start(bf16[128,128]{1,0:T(8,128)(2,1)S(1)} %get-tuple-element.57), channel_id=1, source_target_pairs={{0,1},{1,0},{2,3},{3,2},{4,5},{5,4},{6,7},{7,6},{8,9},{9,8},{10,11... | collective-permute-start | bytes 98312 | tf_op jit(solution)/shard_map/ppermute | solution.py:250
  44.7 4.0 %collective-permute-start.25 = (bf16[128,128]{1,0:T(8,128)(2,1)S(1)}, bf16[128,128]{1,0:T(8,128)(2,1)S(1)}, u32[]{:S(2)}, u32[]{:S(2)}) collective-permute-start(bf16[128,128]{1,0:T(8,128)(2,1)S(1)} %get-tuple-element.58), channel_id=1, source_target_pairs={{0,2},{1,3},{2,0},{3,1},{4,6},{5,7},{6,4},{7,5},{8,10},{9,11},{10,... | collective-permute-start | bytes 98312 | tf_op jit(solution)/shard_map/ppermute | solution.py:250
  46.2 3.3 %collective-permute-start.26 = (bf16[128,128]{1,0:T(8,128)(2,1)S(1)}, bf16[128,128]{1,0:T(8,128)(2,1)S(1)}, u32[]{:S(2)}, u32[]{:S(2)}) collective-permute-start(bf16[128,128]{1,0:T(8,128)(2,1)S(1)} %get-tuple-element.59), channel_id=1, source_target_pairs={{0,3},{1,2},{2,1},{3,0},{4,7},{5,6},{6,5},{7,4},{8,11},{9,10},{10,... | collective-permute-start | bytes 98312 | tf_op jit(solution)/shard_map/ppermute | solution.py:250
  49.5 0.8 %copy-start.2 = (f32[128,128]{1,0:T(8,128)S(1)}, f32[128,128]{1,0:T(8,128)}, u32[]{:S(2)}) copy-start(f32[128,128]{1,0:T(8,128)} %adjoint_end.1.refs_6_) | copy-start | bytes 196612

commit v12 on v11

--- a/solution.py
+++ b/solution.py
@@ -45,14 +45,6 @@
     )(*args, *after)
 
 
-def fetch(pairs, sems):
-    copies = [pltpu.make_async_copy(a, b, sems.at[i]) for i, (a, b) in enumerate(pairs)]
-    for copy in copies:
-        copy.start()
-    for copy in copies:
-        copy.wait()
-
-
 def rate_row(types_ref, teleport_ref):
     types = types_ref[...]
     rate = jnp.zeros(types.shape, F32)
@@ -67,83 +59,60 @@
 
 
 def start_body(
+    types_hbm,
+    teleport_hbm,
     cot_hbm,
     h_hbm,
-    types_hbm,
-    teleport_hbm,
+    tiles_hbm,
     q_ref,
     p_ref,
     row_ref,
-    column_ref,
+    keep_ref,
+    h_base_ref,
+    cot_base_ref,
+    tiles_ref,
+    types_ref,
+    teleport_ref,
     cot_ref,
     h_ref,
-    types_ref,
-    teleport_ref,
     sems,
 ):
-    fetch(
-        [
-            (types_hbm, types_ref),
-            (teleport_hbm, teleport_ref),
-            (cot_hbm, cot_ref),
-            (h_hbm, h_ref),
-        ],
-        sems,
-    )
+    sources = (types_hbm, teleport_hbm, cot_hbm, h_hbm, tiles_hbm)
+    targets = (types_ref, teleport_ref, cot_ref, h_ref, tiles_ref)
+    copies = [
+        pltpu.make_async_copy(a, b, sems.at[i]) for i, (a, b) in enumerate(zip(sources, targets))
+    ]
+    for copy in copies:
+        copy.start()
+    for copy in copies[:4]:
+        copy.wait()
     rate = rate_row(types_ref, teleport_ref)
+    column = rate_column(rate, h_ref.shape[1])
     row_ref[...] = rate
-    column_ref[...] = rate_column(rate, h_ref.shape[1])
+    keep_ref[...] = 1.0 - column
     q_ref[...] = ((1.0 - rate) * cot_ref[...].T).astype(BF16)
     p_ref[...] = h_ref[...].astype(BF16)
-
-
-def dense_body(
-    tiles_hbm,
-    row_hbm,
-    col_hbm,
-    count_ref,
-    dense_ref,
-    row_ref,
-    col_ref,
-    sems,
-    slot_sems,
-):
-    size = tiles_hbm.shape[-1]
-    ids = [
-        pltpu.make_async_copy(row_hbm, row_ref, sems.at[0]),
-        pltpu.make_async_copy(col_hbm, col_ref, sems.at[1]),
-    ]
-    for copy in ids:
-        copy.start()
+    h_base_ref[...] = column * h_ref[...]
+    cot_base_ref[...] = column * cot_ref[...]
+    copies[4].wait()
+
+
+def dense_body(tiles_ref, row_ref, col_ref, count_ref, dense_ref):
+    size = tiles_ref.shape[-1]
     me_row = lax.axis_index("rows")
     me_col = lax.axis_index("cols")
     dense_ref[...] = jnp.zeros_like(dense_ref)
-    for copy in ids:
-        copy.wait()
-    count = count_ref[0, 0]
-
-    def tile_copy(slot):
+
+    def place(slot, carry):
         row = row_ref[0, 0, slot] ^ me_col
         col = col_ref[0, 0, slot] ^ me_row
-        return pltpu.make_async_copy(
-            tiles_hbm.at[0, 0, slot],
-            dense_ref.at[
-                pl.ds(pl.multiple_of(row * size, size), size),
-                pl.ds(pl.multiple_of(col * size, size), size),
-            ],
-            slot_sems.at[slot],
-        )
-
-    def begin(slot, carry):
-        tile_copy(slot).start()
+        dense_ref[
+            pl.ds(pl.multiple_of(row * size, size), size),
+            pl.ds(pl.multiple_of(col * size, size), size),
+        ] = tiles_ref[0, 0, slot]
         return carry
 
-    def end(slot, carry):
-        tile_copy(slot).wait()
-        return carry
-
-    lax.fori_loop(0, count, begin, 0)
-    lax.fori_loop(0, count, end, 0)
+    lax.fori_loop(0, count_ref[0, 0], place, 0)
 
 
 def adjoint_body(n_rows, n_cols, dense_ref, *refs):
@@ -196,17 +165,9 @@
     return terms[0]
 
 
-def forward_end_body(h_ref, rate_ref, *refs):
+def forward_end_body(base_ref, keep_ref, *refs):
     *parts, out_ref = refs
-    rate = rate_ref[...]
-    value = (1.0 - rate) * sum_refs(parts) + rate * h_ref[...]
-    out_ref[...] = value.astype(out_ref.dtype)
-
-
-def forward_middle_body(h_ref, rate_ref, *refs):
-    *parts, p_ref = refs
-    rate = rate_ref[...]
-    p_ref[...] = ((1.0 - rate) * sum_refs(parts) + rate * h_ref[...]).astype(BF16)
+    out_ref[...] = (keep_ref[...] * sum_refs(parts) + base_ref[...]).astype(out_ref.dtype)
 
 
 def adjoint_middle_body(rate_ref, *refs):
@@ -216,33 +177,32 @@
     q_ref[...] = ((1.0 - rate_ref[...]) * total).astype(BF16)
 
 
-def adjoint_end_body(cot_ref, d_ref, row_ref, column_ref, *refs):
+def adjoint_end_body(base_ref, d_ref, rate_ref, *refs):
     *parts, out_ref = refs
-    change = (row_ref[...] * d_ref[...] + sum_refs(parts)).T
-    out_ref[...] = column_ref[...] * cot_ref[...] + change
+    out_ref[...] = base_ref[...] + (rate_ref[...] * d_ref[...] + sum_refs(parts)).T
 
 
 AFTER = {
-    "dense": ("start",),
     "pair_one_late": ("adjoint_one",),
-    "forward_one": ("far_one", "near_one"),
     "forward_two": ("far_two", "near_two"),
-    "pair_two_late": ("adjoint_two",),
     "forward_end": ("adjoint_end",),
-    "adjoint_one": ("pair_one_early",),
     "pair_two_early": ("adjoint_middle",),
     "forward_middle": ("adjoint_middle",),
+    "pair_one_early": ("dense",),
+    "adjoint_middle": ("forward_one",),
 }
 COST = {
     "pair_one_late": 1000,
     "adjoint_middle": 1000,
-    "near_two": 500,
-    "pair_two_early": 500,
+    "near_two": 200,
+    "pair_two_early": 200,
     "far_two": 1000,
     "far_one": 500,
-    "forward_end": 3000,
+    "forward_end": 1000,
     "pair_two_late": 1000,
     "pair_one_early": 3000,
+    "forward_middle": 3000,
+    "adjoint_end": 3000,
 }
 
 
@@ -256,7 +216,6 @@
     half = n_rows // 2
     near = half // 2
     size = tile_values.shape[-1]
-    slots = tile_values.shape[2]
     features = h_start.shape[-1]
     types = node_type.reshape(1, size)
     hop_flops = 2 * n_rows * n_cols * size * size * features
@@ -288,15 +247,23 @@
         return run(
             "start",
             start_body,
-            [shape(BF16), shape(BF16), jax.ShapeDtypeStruct((1, size), F32), shape(F32)],
-            in_hbm(cotangent, h_start, types, teleport),
-            [hbm()] * 4,
             [
+                shape(BF16),
+                shape(BF16),
+                jax.ShapeDtypeStruct((1, size), F32),
+                shape(F32),
+                shape(F32),
+                shape(F32),
+                jax.ShapeDtypeStruct(tile_values.shape, BF16),
+            ],
+            in_hbm(types, teleport, cotangent, h_start, tile_values),
+            [hbm()] * 5,
+            [
+                pltpu.VMEM(types.shape, jnp.int32),
+                pltpu.SMEM(teleport.shape, F32),
                 pltpu.VMEM(cotangent.shape, F32),
                 pltpu.VMEM(h_start.shape, F32),
-                pltpu.VMEM(types.shape, jnp.int32),
-                pltpu.SMEM(teleport.shape, F32),
-                pltpu.SemaphoreType.DMA((4,)),
+                pltpu.SemaphoreType.DMA((5,)),
             ],
         )
 
@@ -305,14 +272,8 @@
             "dense",
             dense_body,
             [jax.ShapeDtypeStruct((n_cols * size, n_rows * size), BF16)],
-            [*in_hbm(tile_values, tile_row, tile_col), tile_count],
-            [hbm()] * 3 + [smem()],
-            [
-                pltpu.SMEM(tile_row.shape, jnp.int32),
-                pltpu.SMEM(tile_col.shape, jnp.int32),
-                pltpu.SemaphoreType.DMA((2,)),
-                pltpu.SemaphoreType.DMA((slots,)),
-            ],
+            [get("start")[6], *in_hbm(tile_row, tile_col), tile_count],
+            [vmem()] + [smem()] * 3,
         )
 
     def spread(part, axis, count, step):
@@ -380,9 +341,9 @@
         ),
         forward_middle=lambda: run(
             "forward_middle",
-            forward_middle_body,
+            forward_end_body,
             [shape(BF16)],
-            [h_start, get("start")[3], *swap_cols(get("forward_one"))],
+            [get("start")[4], get("start")[3], *swap_cols(get("forward_one"))],
         ),
         adjoint_two=lambda: adjoint("adjoint_two", get("adjoint_middle")[1], BF16),
         pair_two_early=lambda: pair("pair_two_early", get("forward_middle")[0], get("other_two")),
@@ -400,17 +361,16 @@
             "forward_end",
             forward_end_body,
             [shape(F32)],
-            [h_start, get("start")[3], *swap_cols(get("forward_two"))],
+            [get("start")[4], get("start")[3], *swap_cols(get("forward_two"))],
         ),
         adjoint_end=lambda: run(
             "adjoint_end",
             adjoint_end_body,
             [shape(F32)],
             [
-                cotangent,
+                get("start")[5],
                 get("adjoint_middle")[0],
                 get("start")[2],
-                get("start")[3],
                 *row_parts(get("far_two"), get("near_two")),
             ],
         ),

time: 51.2 us -> 51.6 us (level)
  waiting for transfers between devices: 7.23 us -> 8.39 us
  Pallas kernels: 5.86 us -> 5.08 us
    ppermute x30, waiting for transfers between devices: 7.23 us -> 8.39 us  [send(): return lax.ppermute(value, axis, [(i, i ^ step) for i in range(count)])]
    pallas_call x18, Pallas kernels: 5.86 us -> 5.08 us  [call(): pl.pallas_call(ordered, out_shape=outs, in_specs=[*in_specs, *[pl.BlockSp...]
  transfers between devices with their start and end apart: 30 -> 30, of which waited for: 10 -> 13; matrix products, arithmetic and copies ran while one was open for 0% -> 0% of each run, Pallas kernels for 8% -> 6%
where the time goes in v12:
time: 51.6 us; the launch traced here: 51.4 us
  starting transfers between devices  35.6 us (69%)
  waiting for transfers between devices  8.39 us (16%)
  Pallas kernels  5.08 us (10%)
  between operations  1.43 us (3%)
  local copies, waits for them, and re-layouts  0.84 us (2%)
    ppermute x30, starting transfers between devices, send(): return lax.ppermute(value, axis, [(i, i ^ step) for i in range(count)])  35.6 us
    ppermute x30, waiting for transfers between devices, send(): return lax.ppermute(value, axis, [(i, i ^ step) for i in range(count)])  8.39 us
    pallas_call x18, Pallas kernels, call(): pl.pallas_call(ordered, out_shape=outs, in_specs=[*in_specs, *[pl.BlockSp...  5.08 us
  transfers between devices with their start and end apart: 30, of which 13 were waited for; matrix products, arithmetic and copies ran while one was open for 0% of the time, Pallas kernels for 6%

profile of v12, /device:TPU:0, one launch (start us, length us, event | category | flops | bytes accessed | tf_op | source)
XLA Modules:
  0.0 51.4 jit_solution(3971109046764624086)
XLA Ops:
  0.6 1.3 %start.1 = (bf16[128,128]{1,0:T(8,128)(2,1)S(1)}, bf16[128,128]{1,0:T(8,128)(2,1)S(1)}, f32[1,128]{1,0:T(1,128)S(1)}, f32[128,128]{1,0:T(8,128)S(1)}, f32[128,12...) custom-call(s32[1,128]{1,0:T(1,128)} %bitcast.1, f32[8]{0:T(128)} %refs_1_.2, ...), custom_call_target="tpu_custom_call" | custom-call | bytes 1967136 | tf_op jit(solution)/shard_map/start/pallas_call | solution.py:36
  1.9 2.4 %collective-permute-start.3 = (bf16[128,128]{1,0:T(8,128)(2,1)S(1)}, bf16[128,128]{1,0:T(8,128)(2,1)S(1)}, u32[]{:S(2)}, u32[]{:S(2)}) collective-permute-start(bf16[128,128]{1,0:T(8,128)(2,1)S(1)} %get-tuple-element.39.refs_1_), channel_id=1, source_target_pairs={{0,3},{1,2},{2,1},{3,0},{4,7},{5,6},{6,5},{7,4},{8,11},{9,10},{10,... | collective-permute-start | bytes 98312 | tf_op jit(solution)/shard_map/ppermute | solution.py:210
  4.4 0.6 %collective-permute-start.2 = (bf16[128,128]{1,0:T(8,128)(2,1)S(1)}, bf16[128,128]{1,0:T(8,128)(2,1)S(1)}, u32[]{:S(2)}, u32[]{:S(2)}) collective-permute-start(bf16[128,128]{1,0:T(8,128)(2,1)S(1)} %get-tuple-element.39.refs_1_), channel_id=1, source_target_pairs={{0,2},{1,3},{2,0},{3,1},{4,6},{5,7},{6,4},{7,5},{8,10},{9,11},{10,... | collective-permute-start | bytes 98312 | tf_op jit(solution)/shard_map/ppermute | solution.py:210
  5.0 1.8 %collective-permute-start = (bf16[128,128]{1,0:T(8,128)(2,1)S(1)}, bf16[128,128]{1,0:T(8,128)(2,1)S(1)}, u32[]{:S(2)}, u32[]{:S(2)}) collective-permute-start(bf16[128,128]{1,0:T(8,128)(2,1)S(1)} %get-tuple-element.38.refs_0_), channel_id=1, source_target_pairs={{0,4},{4,0},{8,12},{12,8},{16,20},{20,16},{24,28},{28,24},{1,5},{5... | collective-permute-start | bytes 98312 | tf_op jit(solution)/shard_map/ppermute | solution.py:210
  7.5 0.8 %dense.1.refs_2_.refs_0_ = bf16[512,1024]{1,0:T(8,128)(2,1)S(1)} custom-call(bf16[1,1,24,128,128]{4,3,2,1,0:T(8,128)(2,1)S(1)} %get-tuple-element.37.refs_0_, s32[1,1,24]{2,1,0:T(1,128)} %refs_1_.3, s32[1,1,24]{2,1,0:T(1,128)} %refs_2_.3, s32[1,1]{1,0:T(1,128)S(6)} %copy.10.refs_3_), custom_call_target="tpu_custom_call" | custom-call | bytes 1835204 | tf_op jit(solution)/shard_map/dense/pallas_call | solution.py:36
  8.3 0.1 collective-permute-done.2.refs_3_
  8.3 0.3 adjoint_one.1
  8.6 1.6 %collective-permute-start.10 = (f32[2,128,128]{2,1,0:T(8,128)S(1)}, f32[2,128,128]{2,1,0:T(8,128)S(1)}, u32[]{:S(2)}, u32[]{:S(2)}) collective-permute-start(f32[2,128,128]{2,1,0:T(8,128)S(1)} %get-tuple-element.46), channel_id=1, source_target_pairs={{0,4},{4,0},{8,12},{12,8},{16,20},{20,16},{24,28},{28,24},{1,5},{5... | collective-permute-start | bytes 393224 | tf_op jit(solution)/shard_map/ppermute | solution.py:210
  10.2 3.7 %collective-permute-start.6 = (bf16[2,128,128]{2,1,0:T(8,128)(2,1)S(1)}, bf16[2,128,128]{2,1,0:T(8,128)(2,1)S(1)}, u32[]{:S(2)}, u32[]{:S(2)}) collective-permute-start(bf16[2,128,128]{2,1,0:T(8,128)(2,1)S(1)} %pair_one_early.1.refs_1_), channel_id=1, source_target_pairs={{0,24},{4,28},{8,16},{12,20},{16,8},{20,12},{24,0},{28,4},{1,25},{... | collective-permute-start | bytes 196616 | tf_op jit(solution)/shard_map/ppermute | solution.py:210
  13.9 0.5 %collective-permute-start.13 = (f32[2,128,128]{2,1,0:T(8,128)S(1)}, f32[2,128,128]{2,1,0:T(8,128)S(1)}, u32[]{:S(2)}, u32[]{:S(2)}) collective-permute-start(f32[2,128,128]{2,1,0:T(8,128)S(1)} %get-tuple-element.50), channel_id=1, source_target_pairs={{0,4},{4,0},{8,12},{12,8},{16,20},{20,16},{24,28},{28,24},{1,5},{5... | collective-permute-start | bytes 393224 | tf_op jit(solution)/shard_map/ppermute | solution.py:210
  14.5 0.8 %collective-permute-start.4 = (bf16[2,128,128]{2,1,0:T(8,128)(2,1)S(1)}, bf16[2,128,128]{2,1,0:T(8,128)(2,1)S(1)}, u32[]{:S(2)}, u32[]{:S(2)}) collective-permute-start(bf16[2,128,128]{2,1,0:T(8,128)(2,1)S(1)} %pair_one_late.1), channel_id=1, source_target_pairs={{0,8},{4,12},{8,0},{12,4},{16,24},{20,28},{24,16},{28,20},{1,9},{5... | collective-permute-start | bytes 196616 | tf_op jit(solution)/shard_map/ppermute | solution.py:210
  15.2 2.5 %collective-permute-start.11 = (f32[128,128]{1,0:T(8,128)S(1)}, f32[128,128]{1,0:T(8,128)S(1)}, u32[]{:S(2)}, u32[]{:S(2)}) collective-permute-start(f32[128,128]{1,0:T(8,128)S(1)} %get-tuple-element.47), channel_id=1, source_target_pairs={{0,16},{4,20},{8,24},{12,28},{16,0},{20,4},{24,8},{28,12},{1,17},{... | collective-permute-start | bytes 196616 | tf_op jit(solution)/shard_map/ppermute | solution.py:210
  17.8 1.1 %collective-permute-done.13.refs_1_ = f32[2,128,128]{2,1,0:T(8,128)S(1)} collective-permute-done((f32[2,128,128]{2,1,0:T(8,128)S(1)}, f32[2,128,128]{2,1,0:T(8,128)S(1)}, u32[]{:S(2)}, u32[]{:S(2)}) %collective-permute-start.13) | collective-permute-done | bytes 131104 | tf_op jit(solution)/shard_map/ppermute | solution.py:210
  18.9 1.5 %collective-permute-start.12 = (f32[128,128]{1,0:T(8,128)S(1)}, f32[128,128]{1,0:T(8,128)S(1)}, u32[]{:S(2)}, u32[]{:S(2)}) collective-permute-start(f32[128,128]{1,0:T(8,128)S(1)} %get-tuple-element.48), channel_id=1, source_target_pairs={{0,24},{4,28},{8,16},{12,20},{16,8},{20,12},{24,0},{28,4},{1,25},{... | collective-permute-start | bytes 196616 | tf_op jit(solution)/shard_map/ppermute | solution.py:210
  20.4 0.1 collective-permute-start.14
  20.5 0.6 %collective-permute-done.5.refs_3_ = bf16[2,128,128]{2,1,0:T(8,128)(2,1)S(1)} collective-permute-done((bf16[2,128,128]{2,1,0:T(8,128)(2,1)S(1)}, bf16[2,128,128]{2,1,0:T(8,128)(2,1)S(1)}, u32[]{:S(2)}, u32[]{:S(2)}) %collective-permute-start.5) | collective-permute-done | bytes 65568 | tf_op jit(solution)/shard_map/ppermute | solution.py:210
  21.2 0.4 forward_one.1
  21.6 0.1 collective-permute-start.7
  21.7 1.3 %collective-permute-start.8 = (f32[128,128]{1,0:T(8,128)S(1)}, f32[128,128]{1,0:T(8,128)S(1)}, u32[]{:S(2)}, u32[]{:S(2)}) collective-permute-start(f32[128,128]{1,0:T(8,128)S(1)} %get-tuple-element.43), channel_id=1, source_target_pairs={{0,2},{1,3},{2,0},{3,1},{4,6},{5,7},{6,4},{7,5},{8,10},{9,11},{10,... | collective-permute-start | bytes 196616 | tf_op jit(solution)/shard_map/ppermute | solution.py:210
  23.0 0.5 collective-permute-done.11.refs_1_
  23.5 1.5 %collective-permute-done.12.refs_2_ = f32[128,128]{1,0:T(8,128)S(1)} collective-permute-done((f32[128,128]{1,0:T(8,128)S(1)}, f32[128,128]{1,0:T(8,128)S(1)}, u32[]{:S(2)}, u32[]{:S(2)}) %collective-permute-start.12) | collective-permute-done | bytes 65568 | tf_op jit(solution)/shard_map/ppermute | solution.py:210
  25.0 0.4 collective-permute-done.14.refs_4_
  25.5 0.1 collective-permute-start.21
  25.6 1.3 %collective-permute-start.20 = (bf16[128,128]{1,0:T(8,128)(2,1)S(1)}, bf16[128,128]{1,0:T(8,128)(2,1)S(1)}, u32[]{:S(2)}, u32[]{:S(2)}) collective-permute-start(bf16[128,128]{1,0:T(8,128)(2,1)S(1)} %get-tuple-element.54.refs_1_), channel_id=1, source_target_pairs={{0,2},{1,3},{2,0},{3,1},{4,6},{5,7},{6,4},{7,5},{8,10},{9,11},{10,... | collective-permute-start | bytes 98312 | tf_op jit(solution)/shard_map/ppermute | solution.py:210
  26.9 0.5 %collective-permute-start.19 = (bf16[128,128]{1,0:T(8,128)(2,1)S(1)}, bf16[128,128]{1,0:T(8,128)(2,1)S(1)}, u32[]{:S(2)}, u32[]{:S(2)}) collective-permute-start(bf16[128,128]{1,0:T(8,128)(2,1)S(1)} %get-tuple-element.54.refs_1_), channel_id=1, source_target_pairs={{0,1},{1,0},{2,3},{3,2},{4,5},{5,4},{6,7},{7,6},{8,9},{9,8},{10,11... | collective-permute-start | bytes 98312 | tf_op jit(solution)/shard_map/ppermute | solution.py:210
  27.4 0.3 collective-permute-done.9.refs_5_
  27.8 1.4 %collective-permute-start.15 = (bf16[128,128]{1,0:T(8,128)(2,1)S(1)}, bf16[128,128]{1,0:T(8,128)(2,1)S(1)}, u32[]{:S(2)}, u32[]{:S(2)}) collective-permute-start(bf16[128,128]{1,0:T(8,128)(2,1)S(1)} %forward_middle.1.refs_0_), channel_id=1, source_target_pairs={{0,4},{4,0},{8,12},{12,8},{16,20},{20,16},{24,28},{28,24},{1,5},{5... | collective-permute-start | bytes 98312 | tf_op jit(solution)/shard_map/ppermute | solution.py:210
  29.2 0.4 collective-permute-done.20.refs_3_
  29.6 0.3 adjoint_two.1
  29.9 1.0 %collective-permute-start.22 = (bf16[2,128,128]{2,1,0:T(8,128)(2,1)S(1)}, bf16[2,128,128]{2,1,0:T(8,128)(2,1)S(1)}, u32[]{:S(2)}, u32[]{:S(2)}) collective-permute-start(bf16[2,128,128]{2,1,0:T(8,128)(2,1)S(1)} %get-tuple-element.56), channel_id=1, source_target_pairs={{0,4},{4,0},{8,12},{12,8},{16,20},{20,16},{24,28},{28,24},{1,5},{5... | collective-permute-start | bytes 196616 | tf_op jit(solution)/shard_map/ppermute | solution.py:210
  30.9 0.9 %collective-permute-done.15.refs_1_ = bf16[128,128]{1,0:T(8,128)(2,1)S(1)} collective-permute-done((bf16[128,128]{1,0:T(8,128)(2,1)S(1)}, bf16[128,128]{1,0:T(8,128)(2,1)S(1)}, u32[]{:S(2)}, u32[]{:S(2)}) %collective-permute-start.15) | collective-permute-done | bytes 32800 | tf_op jit(solution)/shard_map/ppermute | solution.py:210
  31.8 1.6 %collective-permute-start.17 = (bf16[2,128,128]{2,1,0:T(8,128)(2,1)S(1)}, bf16[2,128,128]{2,1,0:T(8,128)(2,1)S(1)}, u32[]{:S(2)}, u32[]{:S(2)}) collective-permute-start(bf16[2,128,128]{2,1,0:T(8,128)(2,1)S(1)} %pair_two_late.1), channel_id=1, source_target_pairs={{0,16},{4,20},{8,24},{12,28},{16,0},{20,4},{24,8},{28,12},{1,17},{... | collective-permute-start | bytes 196616 | tf_op jit(solution)/shard_map/ppermute | solution.py:210
  33.4 2.9 %collective-permute-start.16 = (bf16[2,128,128]{2,1,0:T(8,128)(2,1)S(1)}, bf16[2,128,128]{2,1,0:T(8,128)(2,1)S(1)}, u32[]{:S(2)}, u32[]{:S(2)}) collective-permute-start(bf16[2,128,128]{2,1,0:T(8,128)(2,1)S(1)} %pair_two_late.1), channel_id=1, source_target_pairs={{0,8},{4,12},{8,0},{12,4},{16,24},{20,28},{24,16},{28,20},{1,9},{5... | collective-permute-start | bytes 196616 | tf_op jit(solution)/shard_map/ppermute | solution.py:210
  36.3 1.3 %collective-permute-start.23 = (bf16[2,128,128]{2,1,0:T(8,128)(2,1)S(1)}, bf16[2,128,128]{2,1,0:T(8,128)(2,1)S(1)}, u32[]{:S(2)}, u32[]{:S(2)}) collective-permute-start(bf16[2,128,128]{2,1,0:T(8,128)(2,1)S(1)} %get-tuple-element.59), channel_id=1, source_target_pairs={{0,4},{4,0},{8,12},{12,8},{16,20},{20,16},{24,28},{28,24},{1,5},{5... | collective-permute-start | bytes 196616 | tf_op jit(solution)/shard_map/ppermute | solution.py:210
  37.5 2.6 %collective-permute-start.28 = (bf16[128,128]{1,0:T(8,128)(2,1)S(1)}, bf16[128,128]{1,0:T(8,128)(2,1)S(1)}, u32[]{:S(2)}, u32[]{:S(2)}) collective-permute-start(bf16[128,128]{1,0:T(8,128)(2,1)S(1)} %get-tuple-element.66), channel_id=1, source_target_pairs={{0,24},{4,28},{8,16},{12,20},{16,8},{20,12},{24,0},{28,4},{1,25},{... | collective-permute-start | bytes 98312 | tf_op jit(solution)/shard_map/ppermute | solution.py:210
  40.2 0.4 collective-permute-done.23.refs_1_
  40.6 1.5 %collective-permute-start.27 = (bf16[128,128]{1,0:T(8,128)(2,1)S(1)}, bf16[128,128]{1,0:T(8,128)(2,1)S(1)}, u32[]{:S(2)}, u32[]{:S(2)}) collective-permute-start(bf16[128,128]{1,0:T(8,128)(2,1)S(1)} %get-tuple-element.57.refs_5_), channel_id=1, source_target_pairs={{0,16},{4,20},{8,24},{12,28},{16,0},{20,4},{24,8},{28,12},{1,17},{... | collective-permute-start | bytes 98312 | tf_op jit(solution)/shard_map/ppermute | solution.py:210
  42.1 0.4 collective-permute-done.18.refs_4_
  42.5 2.5 %collective-permute-start.29 = (bf16[128,128]{1,0:T(8,128)(2,1)S(1)}, bf16[128,128]{1,0:T(8,128)(2,1)S(1)}, u32[]{:S(2)}, u32[]{:S(2)}) collective-permute-start(bf16[128,128]{1,0:T(8,128)(2,1)S(1)} %get-tuple-element.67), channel_id=1, source_target_pairs={{0,8},{4,12},{8,0},{12,4},{16,24},{20,28},{24,16},{28,20},{1,9},{5... | collective-permute-start | bytes 98312 | tf_op jit(solution)/shard_map/ppermute | solution.py:210
  45.0 0.4 forward_two.1
  45.4 0.1 collective-permute-start.24
  45.5 1.0 %collective-permute-start.25 = (bf16[128,128]{1,0:T(8,128)(2,1)S(1)}, bf16[128,128]{1,0:T(8,128)(2,1)S(1)}, u32[]{:S(2)}, u32[]{:S(2)}) collective-permute-start(bf16[128,128]{1,0:T(8,128)(2,1)S(1)} %get-tuple-element.63), channel_id=1, source_target_pairs={{0,2},{1,3},{2,0},{3,1},{4,6},{5,7},{6,4},{7,5},{8,10},{9,11},{10,... | collective-permute-start | bytes 98312 | tf_op jit(solution)/shard_map/ppermute | solution.py:210
  46.5 0.9 %collective-permute-start.26 = (bf16[128,128]{1,0:T(8,128)(2,1)S(1)}, bf16[128,128]{1,0:T(8,128)(2,1)S(1)}, u32[]{:S(2)}, u32[]{:S(2)}) collective-permute-start(bf16[128,128]{1,0:T(8,128)(2,1)S(1)} %get-tuple-element.64), channel_id=1, source_target_pairs={{0,3},{1,2},{2,1},{3,0},{4,7},{5,6},{6,5},{7,4},{8,11},{9,10},{10,... | collective-permute-start | bytes 98312 | tf_op jit(solution)/shard_map/ppermute | solution.py:210
  47.4 0.7 %adjoint_end.1.refs_6_ = f32[128,128]{1,0:T(8,128)} custom-call(f32[128,128]{1,0:T(8,128)S(1)} %get-tuple-element.65.refs_0_, f32[128,128]{1,0:T(8,128)S(1)} %get-tuple-element.53.refs_6_.refs_2_.refs_1_, f32[1,128]{1,0:T(1,128)S(1)} %get-tuple-element.45.refs_0_.refs_2_, bf16[128,128]{1,0:T(8,128)(2,1)S(1)} %collective-permute-done.27.refs_3_, ...), custom_call_target="tpu_custom_call" | custom-call | flops 3000000000 | bytes 360960 | tf_op jit(solution)/shard_map/adjoint_end/pallas_call | solution.py:36
  48.1 1.4 %collective-permute-done.25.refs_4_ = bf16[128,128]{1,0:T(8,128)(2,1)S(1)} collective-permute-done((bf16[128,128]{1,0:T(8,128)(2,1)S(1)}, bf16[128,128]{1,0:T(8,128)(2,1)S(1)}, u32[]{:S(2)}, u32[]{:S(2)}) %collective-permute-start.25) | collective-permute-done | bytes 32800 | tf_op jit(solution)/shard_map/ppermute | solution.py:210
  49.5 0.4 collective-permute-done.26.refs_5_
  49.9 0.8 %copy-done = f32[128,128]{1,0:T(8,128)S(1)} copy-done((f32[128,128]{1,0:T(8,128)S(1)}, f32[128,128]{1,0:T(8,128)}, u32[]{:S(2)}) %copy-start) | copy-done | bytes 65560
  50.7 0.7 %forward_end.1 = f32[128,128]{1,0:T(8,128)} custom-call(f32[128,128]{1,0:T(8,128)S(1)} %get-tuple-element.35.refs_0_, f32[128,128]{1,0:T(8,128)S(1)} %get-tuple-element.36.refs_1_, bf16[128,128]{1,0:T(8,128)(2,1)S(1)} %get-tuple-element.61.refs_2_, bf16[128,128]{1,0:T(8,128)(2,1)S(1)} %collective-permute-done.24.refs_3_, ...), custom_call_target="tpu_custom_call" | custom-call | flops 1000000000 | bytes 327680 | tf_op jit(solution)/shard_map/forward_end/pallas_call | solution.py:36
  (32 shorter events, 0.3 us)
Async XLA Ops:
  1.9 6.3 %collective-permute-start.3 = (bf16[128,128]{1,0:T(8,128)(2,1)S(1)}, bf16[128,128]{1,0:T(8,128)(2,1)S(1)}, u32[]{:S(2)}, u32[]{:S(2)}) collective-permute-start(bf16[128,128]{1,0:T(8,128)(2,1)S(1)} %get-tuple-element.39.refs_1_), channel_id=1, source_target_pairs={{0,3},{1,2},{2,1},{3,0},{4,7},{5,6},{6,5},{7,4},{8,11},{9,10},{10,... | collective-permute-start | bytes 98312 | tf_op jit(solution)/shard_map/ppermute | solution.py:210
  4.4 4.0 %collective-permute-start.2 = (bf16[128,128]{1,0:T(8,128)(2,1)S(1)}, bf16[128,128]{1,0:T(8,128)(2,1)S(1)}, u32[]{:S(2)}, u32[]{:S(2)}) collective-permute-start(bf16[128,128]{1,0:T(8,128)(2,1)S(1)} %get-tuple-element.39.refs_1_), channel_id=1, source_target_pairs={{0,2},{1,3},{2,0},{3,1},{4,6},{5,7},{6,4},{7,5},{8,10},{9,11},{10,... | collective-permute-start | bytes 98312 | tf_op jit(solution)/shard_map/ppermute | solution.py:210
  5.0 3.3 %collective-permute-start.1 = (bf16[128,128]{1,0:T(8,128)(2,1)S(1)}, bf16[128,128]{1,0:T(8,128)(2,1)S(1)}, u32[]{:S(2)}, u32[]{:S(2)}) collective-permute-start(bf16[128,128]{1,0:T(8,128)(2,1)S(1)} %get-tuple-element.39.refs_1_), channel_id=1, source_target_pairs={{0,1},{1,0},{2,3},{3,2},{4,5},{5,4},{6,7},{7,6},{8,9},{9,8},{10,11... | collective-permute-start | bytes 98312 | tf_op jit(solution)/shard_map/ppermute | solution.py:210
  5.0 5.2 %collective-permute-start = (bf16[128,128]{1,0:T(8,128)(2,1)S(1)}, bf16[128,128]{1,0:T(8,128)(2,1)S(1)}, u32[]{:S(2)}, u32[]{:S(2)}) collective-permute-start(bf16[128,128]{1,0:T(8,128)(2,1)S(1)} %get-tuple-element.38.refs_0_), channel_id=1, source_target_pairs={{0,4},{4,0},{8,12},{12,8},{16,20},{20,16},{24,28},{28,24},{1,5},{5... | collective-permute-start | bytes 98312 | tf_op jit(solution)/shard_map/ppermute | solution.py:210
  8.6 6.6 %collective-permute-start.10 = (f32[2,128,128]{2,1,0:T(8,128)S(1)}, f32[2,128,128]{2,1,0:T(8,128)S(1)}, u32[]{:S(2)}, u32[]{:S(2)}) collective-permute-start(f32[2,128,128]{2,1,0:T(8,128)S(1)} %get-tuple-element.46), channel_id=1, source_target_pairs={{0,4},{4,0},{8,12},{12,8},{16,20},{20,16},{24,28},{28,24},{1,5},{5... | collective-permute-start | bytes 393224 | tf_op jit(solution)/shard_map/ppermute | solution.py:210
  10.2 10.2 %collective-permute-start.6 = (bf16[2,128,128]{2,1,0:T(8,128)(2,1)S(1)}, bf16[2,128,128]{2,1,0:T(8,128)(2,1)S(1)}, u32[]{:S(2)}, u32[]{:S(2)}) collective-permute-start(bf16[2,128,128]{2,1,0:T(8,128)(2,1)S(1)} %pair_one_early.1.refs_1_), channel_id=1, source_target_pairs={{0,24},{4,28},{8,16},{12,20},{16,8},{20,12},{24,0},{28,4},{1,25},{... | collective-permute-start | bytes 196616 | tf_op jit(solution)/shard_map/ppermute | solution.py:210
  13.9 5.0 %collective-permute-start.13 = (f32[2,128,128]{2,1,0:T(8,128)S(1)}, f32[2,128,128]{2,1,0:T(8,128)S(1)}, u32[]{:S(2)}, u32[]{:S(2)}) collective-permute-start(f32[2,128,128]{2,1,0:T(8,128)S(1)} %get-tuple-element.50), channel_id=1, source_target_pairs={{0,4},{4,0},{8,12},{12,8},{16,20},{20,16},{24,28},{28,24},{1,5},{5... | collective-permute-start | bytes 393224 | tf_op jit(solution)/shard_map/ppermute | solution.py:210
  14.4 6.7 %collective-permute-start.5 = (bf16[2,128,128]{2,1,0:T(8,128)(2,1)S(1)}, bf16[2,128,128]{2,1,0:T(8,128)(2,1)S(1)}, u32[]{:S(2)}, u32[]{:S(2)}) collective-permute-start(bf16[2,128,128]{2,1,0:T(8,128)(2,1)S(1)} %pair_one_late.1), channel_id=1, source_target_pairs={{0,16},{4,20},{8,24},{12,28},{16,0},{20,4},{24,8},{28,12},{1,17},{... | collective-permute-start | bytes 196616 | tf_op jit(solution)/shard_map/ppermute | solution.py:210
  14.5 6.7 %collective-permute-start.4 = (bf16[2,128,128]{2,1,0:T(8,128)(2,1)S(1)}, bf16[2,128,128]{2,1,0:T(8,128)(2,1)S(1)}, u32[]{:S(2)}, u32[]{:S(2)}) collective-permute-start(bf16[2,128,128]{2,1,0:T(8,128)(2,1)S(1)} %pair_one_late.1), channel_id=1, source_target_pairs={{0,8},{4,12},{8,0},{12,4},{16,24},{20,28},{24,16},{28,20},{1,9},{5... | collective-permute-start | bytes 196616 | tf_op jit(solution)/shard_map/ppermute | solution.py:210
  15.2 8.3 %collective-permute-start.11 = (f32[128,128]{1,0:T(8,128)S(1)}, f32[128,128]{1,0:T(8,128)S(1)}, u32[]{:S(2)}, u32[]{:S(2)}) collective-permute-start(f32[128,128]{1,0:T(8,128)S(1)} %get-tuple-element.47), channel_id=1, source_target_pairs={{0,16},{4,20},{8,24},{12,28},{16,0},{20,4},{24,8},{28,12},{1,17},{... | collective-permute-start | bytes 196616 | tf_op jit(solution)/shard_map/ppermute | solution.py:210
  18.9 6.2 %collective-permute-start.12 = (f32[128,128]{1,0:T(8,128)S(1)}, f32[128,128]{1,0:T(8,128)S(1)}, u32[]{:S(2)}, u32[]{:S(2)}) collective-permute-start(f32[128,128]{1,0:T(8,128)S(1)} %get-tuple-element.48), channel_id=1, source_target_pairs={{0,24},{4,28},{8,16},{12,20},{16,8},{20,12},{24,0},{28,4},{1,25},{... | collective-permute-start | bytes 196616 | tf_op jit(solution)/shard_map/ppermute | solution.py:210
  20.4 5.0 %collective-permute-start.14 = (f32[128,128]{1,0:T(8,128)S(1)}, f32[128,128]{1,0:T(8,128)S(1)}, u32[]{:S(2)}, u32[]{:S(2)}) collective-permute-start(f32[128,128]{1,0:T(8,128)S(1)} %get-tuple-element.52), channel_id=1, source_target_pairs={{0,8},{4,12},{8,0},{12,4},{16,24},{20,28},{24,16},{28,20},{1,9},{5... | collective-permute-start | bytes 196616 | tf_op jit(solution)/shard_map/ppermute | solution.py:210
  21.6 5.3 %collective-permute-start.7 = (f32[128,128]{1,0:T(8,128)S(1)}, f32[128,128]{1,0:T(8,128)S(1)}, u32[]{:S(2)}, u32[]{:S(2)}) collective-permute-start(f32[128,128]{1,0:T(8,128)S(1)} %get-tuple-element.42), channel_id=1, source_target_pairs={{0,1},{1,0},{2,3},{3,2},{4,5},{5,4},{6,7},{7,6},{8,9},{9,8},{10,11... | collective-permute-start | bytes 196616 | tf_op jit(solution)/shard_map/ppermute | solution.py:210
  21.7 5.7 %collective-permute-start.8 = (f32[128,128]{1,0:T(8,128)S(1)}, f32[128,128]{1,0:T(8,128)S(1)}, u32[]{:S(2)}, u32[]{:S(2)}) collective-permute-start(f32[128,128]{1,0:T(8,128)S(1)} %get-tuple-element.43), channel_id=1, source_target_pairs={{0,2},{1,3},{2,0},{3,1},{4,6},{5,7},{6,4},{7,5},{8,10},{9,11},{10,... | collective-permute-start | bytes 196616 | tf_op jit(solution)/shard_map/ppermute | solution.py:210
  23.5 4.3 %collective-permute-start.9 = (f32[128,128]{1,0:T(8,128)S(1)}, f32[128,128]{1,0:T(8,128)S(1)}, u32[]{:S(2)}, u32[]{:S(2)}) collective-permute-start(f32[128,128]{1,0:T(8,128)S(1)} %get-tuple-element.44), channel_id=1, source_target_pairs={{0,3},{1,2},{2,1},{3,0},{4,7},{5,6},{6,5},{7,4},{8,11},{9,10},{10,... | collective-permute-start | bytes 196616 | tf_op jit(solution)/shard_map/ppermute | solution.py:210
  25.5 3.7 %collective-permute-start.21 = (bf16[128,128]{1,0:T(8,128)(2,1)S(1)}, bf16[128,128]{1,0:T(8,128)(2,1)S(1)}, u32[]{:S(2)}, u32[]{:S(2)}) collective-permute-start(bf16[128,128]{1,0:T(8,128)(2,1)S(1)} %get-tuple-element.54.refs_1_), channel_id=1, source_target_pairs={{0,3},{1,2},{2,1},{3,0},{4,7},{5,6},{6,5},{7,4},{8,11},{9,10},{10,... | collective-permute-start | bytes 98312 | tf_op jit(solution)/shard_map/ppermute | solution.py:210
  25.6 4.0 %collective-permute-start.20 = (bf16[128,128]{1,0:T(8,128)(2,1)S(1)}, bf16[128,128]{1,0:T(8,128)(2,1)S(1)}, u32[]{:S(2)}, u32[]{:S(2)}) collective-permute-start(bf16[128,128]{1,0:T(8,128)(2,1)S(1)} %get-tuple-element.54.refs_1_), channel_id=1, source_target_pairs={{0,2},{1,3},{2,0},{3,1},{4,6},{5,7},{6,4},{7,5},{8,10},{9,11},{10,... | collective-permute-start | bytes 98312 | tf_op jit(solution)/shard_map/ppermute | solution.py:210
  26.9 2.7 %collective-permute-start.19 = (bf16[128,128]{1,0:T(8,128)(2,1)S(1)}, bf16[128,128]{1,0:T(8,128)(2,1)S(1)}, u32[]{:S(2)}, u32[]{:S(2)}) collective-permute-start(bf16[128,128]{1,0:T(8,128)(2,1)S(1)} %get-tuple-element.54.refs_1_), channel_id=1, source_target_pairs={{0,1},{1,0},{2,3},{3,2},{4,5},{5,4},{6,7},{7,6},{8,9},{9,8},{10,11... | collective-permute-start | bytes 98312 | tf_op jit(solution)/shard_map/ppermute | solution.py:210
  27.8 4.0 %collective-permute-start.15 = (bf16[128,128]{1,0:T(8,128)(2,1)S(1)}, bf16[128,128]{1,0:T(8,128)(2,1)S(1)}, u32[]{:S(2)}, u32[]{:S(2)}) collective-permute-start(bf16[128,128]{1,0:T(8,128)(2,1)S(1)} %forward_middle.1.refs_0_), channel_id=1, source_target_pairs={{0,4},{4,0},{8,12},{12,8},{16,20},{20,16},{24,28},{28,24},{1,5},{5... | collective-permute-start | bytes 98312 | tf_op jit(solution)/shard_map/ppermute | solution.py:210
  29.9 7.6 %collective-permute-start.22 = (bf16[2,128,128]{2,1,0:T(8,128)(2,1)S(1)}, bf16[2,128,128]{2,1,0:T(8,128)(2,1)S(1)}, u32[]{:S(2)}, u32[]{:S(2)}) collective-permute-start(bf16[2,128,128]{2,1,0:T(8,128)(2,1)S(1)} %get-tuple-element.56), channel_id=1, source_target_pairs={{0,4},{4,0},{8,12},{12,8},{16,20},{20,16},{24,28},{28,24},{1,5},{5... | collective-permute-start | bytes 196616 | tf_op jit(solution)/shard_map/ppermute | solution.py:210
  31.8 13.2 %collective-permute-start.17 = (bf16[2,128,128]{2,1,0:T(8,128)(2,1)S(1)}, bf16[2,128,128]{2,1,0:T(8,128)(2,1)S(1)}, u32[]{:S(2)}, u32[]{:S(2)}) collective-permute-start(bf16[2,128,128]{2,1,0:T(8,128)(2,1)S(1)} %pair_two_late.1), channel_id=1, source_target_pairs={{0,16},{4,20},{8,24},{12,28},{16,0},{20,4},{24,8},{28,12},{1,17},{... | collective-permute-start | bytes 196616 | tf_op jit(solution)/shard_map/ppermute | solution.py:210
  33.4 11.6 %collective-permute-start.16 = (bf16[2,128,128]{2,1,0:T(8,128)(2,1)S(1)}, bf16[2,128,128]{2,1,0:T(8,128)(2,1)S(1)}, u32[]{:S(2)}, u32[]{:S(2)}) collective-permute-start(bf16[2,128,128]{2,1,0:T(8,128)(2,1)S(1)} %pair_two_late.1), channel_id=1, source_target_pairs={{0,8},{4,12},{8,0},{12,4},{16,24},{20,28},{24,16},{28,20},{1,9},{5... | collective-permute-start | bytes 196616 | tf_op jit(solution)/shard_map/ppermute | solution.py:210
  36.2 6.2 %collective-permute-start.18 = (bf16[2,128,128]{2,1,0:T(8,128)(2,1)S(1)}, bf16[2,128,128]{2,1,0:T(8,128)(2,1)S(1)}, u32[]{:S(2)}, u32[]{:S(2)}) collective-permute-start(bf16[2,128,128]{2,1,0:T(8,128)(2,1)S(1)} %pair_two_early.1.refs_1_), channel_id=1, source_target_pairs={{0,24},{4,28},{8,16},{12,20},{16,8},{20,12},{24,0},{28,4},{1,25},{... | collective-permute-start | bytes 196616 | tf_op jit(solution)/shard_map/ppermute | solution.py:210
  36.3 4.3 %collective-permute-start.23 = (bf16[2,128,128]{2,1,0:T(8,128)(2,1)S(1)}, bf16[2,128,128]{2,1,0:T(8,128)(2,1)S(1)}, u32[]{:S(2)}, u32[]{:S(2)}) collective-permute-start(bf16[2,128,128]{2,1,0:T(8,128)(2,1)S(1)} %get-tuple-element.59), channel_id=1, source_target_pairs={{0,4},{4,0},{8,12},{12,8},{16,20},{20,16},{24,28},{28,24},{1,5},{5... | collective-permute-start | bytes 196616 | tf_op jit(solution)/shard_map/ppermute | solution.py:210
  37.5 9.0 %collective-permute-start.28 = (bf16[128,128]{1,0:T(8,128)(2,1)S(1)}, bf16[128,128]{1,0:T(8,128)(2,1)S(1)}, u32[]{:S(2)}, u32[]{:S(2)}) collective-permute-start(bf16[128,128]{1,0:T(8,128)(2,1)S(1)} %get-tuple-element.66), channel_id=1, source_target_pairs={{0,24},{4,28},{8,16},{12,20},{16,8},{20,12},{24,0},{28,4},{1,25},{... | collective-permute-start | bytes 98312 | tf_op jit(solution)/shard_map/ppermute | solution.py:210
  40.6 6.8 %collective-permute-start.27 = (bf16[128,128]{1,0:T(8,128)(2,1)S(1)}, bf16[128,128]{1,0:T(8,128)(2,1)S(1)}, u32[]{:S(2)}, u32[]{:S(2)}) collective-permute-start(bf16[128,128]{1,0:T(8,128)(2,1)S(1)} %get-tuple-element.57.refs_5_), channel_id=1, source_target_pairs={{0,16},{4,20},{8,24},{12,28},{16,0},{20,4},{24,8},{28,12},{1,17},{... | collective-permute-start | bytes 98312 | tf_op jit(solution)/shard_map/ppermute | solution.py:210
  42.5 4.9 %collective-permute-start.29 = (bf16[128,128]{1,0:T(8,128)(2,1)S(1)}, bf16[128,128]{1,0:T(8,128)(2,1)S(1)}, u32[]{:S(2)}, u32[]{:S(2)}) collective-permute-start(bf16[128,128]{1,0:T(8,128)(2,1)S(1)} %get-tuple-element.67), channel_id=1, source_target_pairs={{0,8},{4,12},{8,0},{12,4},{16,24},{20,28},{24,16},{28,20},{1,9},{5... | collective-permute-start | bytes 98312 | tf_op jit(solution)/shard_map/ppermute | solution.py:210
  45.4 2.7 %collective-permute-start.24 = (bf16[128,128]{1,0:T(8,128)(2,1)S(1)}, bf16[128,128]{1,0:T(8,128)(2,1)S(1)}, u32[]{:S(2)}, u32[]{:S(2)}) collective-permute-start(bf16[128,128]{1,0:T(8,128)(2,1)S(1)} %get-tuple-element.62), channel_id=1, source_target_pairs={{0,1},{1,0},{2,3},{3,2},{4,5},{5,4},{6,7},{7,6},{8,9},{9,8},{10,11... | collective-permute-start | bytes 98312 | tf_op jit(solution)/shard_map/ppermute | solution.py:210
  45.5 4.0 %collective-permute-start.25 = (bf16[128,128]{1,0:T(8,128)(2,1)S(1)}, bf16[128,128]{1,0:T(8,128)(2,1)S(1)}, u32[]{:S(2)}, u32[]{:S(2)}) collective-permute-start(bf16[128,128]{1,0:T(8,128)(2,1)S(1)} %get-tuple-element.63), channel_id=1, source_target_pairs={{0,2},{1,3},{2,0},{3,1},{4,6},{5,7},{6,4},{7,5},{8,10},{9,11},{10,... | collective-permute-start | bytes 98312 | tf_op jit(solution)/shard_map/ppermute | solution.py:210
  46.5 3.3 %collective-permute-start.26 = (bf16[128,128]{1,0:T(8,128)(2,1)S(1)}, bf16[128,128]{1,0:T(8,128)(2,1)S(1)}, u32[]{:S(2)}, u32[]{:S(2)}) collective-permute-start(bf16[128,128]{1,0:T(8,128)(2,1)S(1)} %get-tuple-element.64), channel_id=1, source_target_pairs={{0,3},{1,2},{2,1},{3,0},{4,7},{5,6},{6,5},{7,4},{8,11},{9,10},{10,... | collective-permute-start | bytes 98312 | tf_op jit(solution)/shard_map/ppermute | solution.py:210
  49.9 0.8 %copy-start = (f32[128,128]{1,0:T(8,128)S(1)}, f32[128,128]{1,0:T(8,128)}, u32[]{:S(2)}) copy-start(f32[128,128]{1,0:T(8,128)} %adjoint_end.1.refs_6_) | copy-start | bytes 196612

commit v13 on v12

--- a/solution.py
+++ b/solution.py
@@ -178,8 +178,9 @@
 
 
 def adjoint_end_body(base_ref, d_ref, rate_ref, *refs):
-    *parts, out_ref = refs
+    *parts, out_ref, token_ref = refs
     out_ref[...] = base_ref[...] + (rate_ref[...] * d_ref[...] + sum_refs(parts)).T
+    token_ref[...] = jnp.zeros_like(token_ref)
 
 
 AFTER = {
@@ -240,7 +241,7 @@
             COST.get(name, 0) * 1_000_000 or flops,
             name,
             scratch,
-            [get(other)[0] for other in AFTER.get(name, ())],
+            [get(other)[-1] for other in AFTER.get(name, ())],
         )
 
     def start():
@@ -366,7 +367,7 @@
         adjoint_end=lambda: run(
             "adjoint_end",
             adjoint_end_body,
-            [shape(F32)],
+            [shape(F32), jax.ShapeDtypeStruct((8, features), F32)],
             [
                 get("start")[5],
                 get("adjoint_middle")[0],

time: 51.6 us -> 50.1 us (0.971)
  starting transfers between devices: 35.6 us -> 33 us
  waiting for transfers between devices: 8.39 us -> 10.3 us
  local copies, waits for them, and re-layouts: 0.84 us -> 0 us
    ppermute x30, starting transfers between devices: 35.6 us -> 33 us  [send(): return lax.ppermute(value, axis, [(i, i ^ step) for i in range(count)])]
    ppermute x30, waiting for transfers between devices: 8.39 us -> 10.3 us  [send(): return lax.ppermute(value, axis, [(i, i ^ step) for i in range(count)])]
    unnamed x2 -> x0, local copies, waits for them, and re-layouts: 0.84 us -> none
  transfers between devices with their start and end apart: 30 -> 30, of which waited for: 13 -> 11; matrix products, arithmetic and copies ran while one was open for 0% -> 0% of each run, Pallas kernels for 6% -> 6%
where the time goes in v13:
time: 50.1 us; the launch traced here: 49.9 us
  starting transfers between devices  33 us (66%)
  waiting for transfers between devices  10.3 us (21%)
  Pallas kernels  5.15 us (10%)
  between operations  1.47 us (3%)
    ppermute x30, starting transfers between devices, send(): return lax.ppermute(value, axis, [(i, i ^ step) for i in range(count)])  33 us
    ppermute x30, waiting for transfers between devices, send(): return lax.ppermute(value, axis, [(i, i ^ step) for i in range(count)])  10.3 us
    pallas_call x18, Pallas kernels, call(): pl.pallas_call(ordered, out_shape=outs, in_specs=[*in_specs, *[pl.BlockSp...  5.15 us
  transfers between devices with their start and end apart: 30, of which 11 were waited for; matrix products, arithmetic and copies ran while one was open for 0% of the time, Pallas kernels for 6%

profile of v13, /device:TPU:0, one launch (start us, length us, event | category | flops | bytes accessed | tf_op | source)
XLA Modules:
  0.0 49.9 jit_solution(17494130936009819715)
XLA Ops:
  0.6 1.3 %start.1 = (bf16[128,128]{1,0:T(8,128)(2,1)S(1)}, bf16[128,128]{1,0:T(8,128)(2,1)S(1)}, f32[1,128]{1,0:T(1,128)S(1)}, f32[128,128]{1,0:T(8,128)S(1)}, f32[128,12...) custom-call(s32[1,128]{1,0:T(1,128)} %bitcast.1, f32[8]{0:T(128)} %refs_1_.2, ...), custom_call_target="tpu_custom_call" | custom-call | bytes 1967136 | tf_op jit(solution)/shard_map/start/pallas_call | solution.py:36
  1.9 2.4 %collective-permute-start.3 = (bf16[128,128]{1,0:T(8,128)(2,1)S(1)}, bf16[128,128]{1,0:T(8,128)(2,1)S(1)}, u32[]{:S(2)}, u32[]{:S(2)}) collective-permute-start(bf16[128,128]{1,0:T(8,128)(2,1)S(1)} %get-tuple-element.41.refs_1_), channel_id=1, source_target_pairs={{0,3},{1,2},{2,1},{3,0},{4,7},{5,6},{6,5},{7,4},{8,11},{9,10},{10,... | collective-permute-start | bytes 98312 | tf_op jit(solution)/shard_map/ppermute | solution.py:211
  4.4 0.6 %collective-permute-start.2 = (bf16[128,128]{1,0:T(8,128)(2,1)S(1)}, bf16[128,128]{1,0:T(8,128)(2,1)S(1)}, u32[]{:S(2)}, u32[]{:S(2)}) collective-permute-start(bf16[128,128]{1,0:T(8,128)(2,1)S(1)} %get-tuple-element.41.refs_1_), channel_id=1, source_target_pairs={{0,2},{1,3},{2,0},{3,1},{4,6},{5,7},{6,4},{7,5},{8,10},{9,11},{10,... | collective-permute-start | bytes 98312 | tf_op jit(solution)/shard_map/ppermute | solution.py:211
  5.0 0.0 collective-permute-start.1
  5.0 1.8 %collective-permute-start = (bf16[128,128]{1,0:T(8,128)(2,1)S(1)}, bf16[128,128]{1,0:T(8,128)(2,1)S(1)}, u32[]{:S(2)}, u32[]{:S(2)}) collective-permute-start(bf16[128,128]{1,0:T(8,128)(2,1)S(1)} %get-tuple-element.40.refs_0_), channel_id=1, source_target_pairs={{0,4},{4,0},{8,12},{12,8},{16,20},{20,16},{24,28},{28,24},{1,5},{5... | collective-permute-start | bytes 98312 | tf_op jit(solution)/shard_map/ppermute | solution.py:211
  7.5 0.9 %dense.1.refs_2_.refs_0_ = bf16[512,1024]{1,0:T(8,128)(2,1)S(1)} custom-call(bf16[1,1,24,128,128]{4,3,2,1,0:T(8,128)(2,1)S(1)} %get-tuple-element.39.refs_0_, s32[1,1,24]{2,1,0:T(1,128)} %refs_1_.3, s32[1,1,24]{2,1,0:T(1,128)} %refs_2_.3, s32[1,1]{1,0:T(1,128)S(6)} %copy.10.refs_3_), custom_call_target="tpu_custom_call" | custom-call | bytes 1835204 | tf_op jit(solution)/shard_map/dense/pallas_call | solution.py:36
  8.3 0.0 collective-permute-done.3.refs_4_
  8.4 0.3 adjoint_one.1
  8.7 1.6 %collective-permute-start.10 = (f32[2,128,128]{2,1,0:T(8,128)S(1)}, f32[2,128,128]{2,1,0:T(8,128)S(1)}, u32[]{:S(2)}, u32[]{:S(2)}) collective-permute-start(f32[2,128,128]{2,1,0:T(8,128)S(1)} %get-tuple-element.49), channel_id=1, source_target_pairs={{0,4},{4,0},{8,12},{12,8},{16,20},{20,16},{24,28},{28,24},{1,5},{5... | collective-permute-start | bytes 393224 | tf_op jit(solution)/shard_map/ppermute | solution.py:211
  10.2 3.7 %collective-permute-start.6 = (bf16[2,128,128]{2,1,0:T(8,128)(2,1)S(1)}, bf16[2,128,128]{2,1,0:T(8,128)(2,1)S(1)}, u32[]{:S(2)}, u32[]{:S(2)}) collective-permute-start(bf16[2,128,128]{2,1,0:T(8,128)(2,1)S(1)} %pair_one_early.1.refs_1_), channel_id=1, source_target_pairs={{0,24},{4,28},{8,16},{12,20},{16,8},{20,12},{24,0},{28,4},{1,25},{... | collective-permute-start | bytes 196616 | tf_op jit(solution)/shard_map/ppermute | solution.py:211
  13.9 0.5 collective-permute-start.13
  14.4 0.8 %collective-permute-start.4 = (bf16[2,128,128]{2,1,0:T(8,128)(2,1)S(1)}, bf16[2,128,128]{2,1,0:T(8,128)(2,1)S(1)}, u32[]{:S(2)}, u32[]{:S(2)}) collective-permute-start(bf16[2,128,128]{2,1,0:T(8,128)(2,1)S(1)} %pair_one_late.1), channel_id=1, source_target_pairs={{0,8},{4,12},{8,0},{12,4},{16,24},{20,28},{24,16},{28,20},{1,9},{5... | collective-permute-start | bytes 196616 | tf_op jit(solution)/shard_map/ppermute | solution.py:211
  15.3 2.5 %collective-permute-start.11 = (f32[128,128]{1,0:T(8,128)S(1)}, f32[128,128]{1,0:T(8,128)S(1)}, u32[]{:S(2)}, u32[]{:S(2)}) collective-permute-start(f32[128,128]{1,0:T(8,128)S(1)} %get-tuple-element.50), channel_id=1, source_target_pairs={{0,16},{4,20},{8,24},{12,28},{16,0},{20,4},{24,8},{28,12},{1,17},{... | collective-permute-start | bytes 196616 | tf_op jit(solution)/shard_map/ppermute | solution.py:211
  17.8 1.1 %collective-permute-done.13.refs_1_ = f32[2,128,128]{2,1,0:T(8,128)S(1)} collective-permute-done((f32[2,128,128]{2,1,0:T(8,128)S(1)}, f32[2,128,128]{2,1,0:T(8,128)S(1)}, u32[]{:S(2)}, u32[]{:S(2)}) %collective-permute-start.13) | collective-permute-done | bytes 131104 | tf_op jit(solution)/shard_map/ppermute | solution.py:211
  18.9 1.6 %collective-permute-start.12 = (f32[128,128]{1,0:T(8,128)S(1)}, f32[128,128]{1,0:T(8,128)S(1)}, u32[]{:S(2)}, u32[]{:S(2)}) collective-permute-start(f32[128,128]{1,0:T(8,128)S(1)} %get-tuple-element.51), channel_id=1, source_target_pairs={{0,24},{4,28},{8,16},{12,20},{16,8},{20,12},{24,0},{28,4},{1,25},{... | collective-permute-start | bytes 196616 | tf_op jit(solution)/shard_map/ppermute | solution.py:211
  20.5 0.1 collective-permute-start.14
  20.6 0.5 collective-permute-done.5.refs_3_
  21.1 0.4 forward_one.1
  21.5 0.1 collective-permute-start.7
  21.6 1.3 %collective-permute-start.8 = (f32[128,128]{1,0:T(8,128)S(1)}, f32[128,128]{1,0:T(8,128)S(1)}, u32[]{:S(2)}, u32[]{:S(2)}) collective-permute-start(f32[128,128]{1,0:T(8,128)S(1)} %get-tuple-element.45), channel_id=1, source_target_pairs={{0,2},{1,3},{2,0},{3,1},{4,6},{5,7},{6,4},{7,5},{8,10},{9,11},{10,... | collective-permute-start | bytes 196616 | tf_op jit(solution)/shard_map/ppermute | solution.py:211
  22.9 0.5 %collective-permute-done.11.refs_1_ = f32[128,128]{1,0:T(8,128)S(1)} collective-permute-done((f32[128,128]{1,0:T(8,128)S(1)}, f32[128,128]{1,0:T(8,128)S(1)}, u32[]{:S(2)}, u32[]{:S(2)}) %collective-permute-start.11) | collective-permute-done | bytes 65568 | tf_op jit(solution)/shard_map/ppermute | solution.py:211
  23.5 0.0 collective-permute-start.9
  23.5 1.6 %collective-permute-done.12.refs_2_ = f32[128,128]{1,0:T(8,128)S(1)} collective-permute-done((f32[128,128]{1,0:T(8,128)S(1)}, f32[128,128]{1,0:T(8,128)S(1)}, u32[]{:S(2)}, u32[]{:S(2)}) %collective-permute-start.12) | collective-permute-done | bytes 65568 | tf_op jit(solution)/shard_map/ppermute | solution.py:211
  25.1 0.5 %collective-permute-done.14.refs_4_ = f32[128,128]{1,0:T(8,128)S(1)} collective-permute-done((f32[128,128]{1,0:T(8,128)S(1)}, f32[128,128]{1,0:T(8,128)S(1)}, u32[]{:S(2)}, u32[]{:S(2)}) %collective-permute-start.14) | collective-permute-done | bytes 65568 | tf_op jit(solution)/shard_map/ppermute | solution.py:211
  25.6 0.1 collective-permute-start.21
  25.7 1.2 %collective-permute-start.20 = (bf16[128,128]{1,0:T(8,128)(2,1)S(1)}, bf16[128,128]{1,0:T(8,128)(2,1)S(1)}, u32[]{:S(2)}, u32[]{:S(2)}) collective-permute-start(bf16[128,128]{1,0:T(8,128)(2,1)S(1)} %get-tuple-element.55.refs_6_.refs_2_.refs_1_), channel_id=1, source_target_pairs={{0,2},{1,3},{2,0},{3,1},{4,6},{5,7},{6,4},{7,5},{8,10},{9,11},{10,... | collective-permute-start | bytes 98312 | tf_op jit(solution)/shard_map/ppermute | solution.py:211
  26.9 0.6 %collective-permute-start.19 = (bf16[128,128]{1,0:T(8,128)(2,1)S(1)}, bf16[128,128]{1,0:T(8,128)(2,1)S(1)}, u32[]{:S(2)}, u32[]{:S(2)}) collective-permute-start(bf16[128,128]{1,0:T(8,128)(2,1)S(1)} %get-tuple-element.55.refs_6_.refs_2_.refs_1_), channel_id=1, source_target_pairs={{0,1},{1,0},{2,3},{3,2},{4,5},{5,4},{6,7},{7,6},{8,9},{9,8},{10,11... | collective-permute-start | bytes 98312 | tf_op jit(solution)/shard_map/ppermute | solution.py:211
  27.5 0.2 collective-permute-done.9.refs_5_
  27.7 1.5 %collective-permute-start.15 = (bf16[128,128]{1,0:T(8,128)(2,1)S(1)}, bf16[128,128]{1,0:T(8,128)(2,1)S(1)}, u32[]{:S(2)}, u32[]{:S(2)}) collective-permute-start(bf16[128,128]{1,0:T(8,128)(2,1)S(1)} %forward_middle.1.refs_0_), channel_id=1, source_target_pairs={{0,4},{4,0},{8,12},{12,8},{16,20},{20,16},{24,28},{28,24},{1,5},{5... | collective-permute-start | bytes 98312 | tf_op jit(solution)/shard_map/ppermute | solution.py:211
  29.2 0.6 %collective-permute-done.20.refs_3_ = bf16[128,128]{1,0:T(8,128)(2,1)S(1)} collective-permute-done((bf16[128,128]{1,0:T(8,128)(2,1)S(1)}, bf16[128,128]{1,0:T(8,128)(2,1)S(1)}, u32[]{:S(2)}, u32[]{:S(2)}) %collective-permute-start.20) | collective-permute-done | bytes 32800 | tf_op jit(solution)/shard_map/ppermute | solution.py:211
  29.8 0.3 adjoint_two.1
  30.1 0.8 %collective-permute-start.22 = (bf16[2,128,128]{2,1,0:T(8,128)(2,1)S(1)}, bf16[2,128,128]{2,1,0:T(8,128)(2,1)S(1)}, u32[]{:S(2)}, u32[]{:S(2)}) collective-permute-start(bf16[2,128,128]{2,1,0:T(8,128)(2,1)S(1)} %get-tuple-element.57), channel_id=1, source_target_pairs={{0,4},{4,0},{8,12},{12,8},{16,20},{20,16},{24,28},{28,24},{1,5},{5... | collective-permute-start | bytes 196616 | tf_op jit(solution)/shard_map/ppermute | solution.py:211
  30.9 0.8 %collective-permute-done.15.refs_1_ = bf16[128,128]{1,0:T(8,128)(2,1)S(1)} collective-permute-done((bf16[128,128]{1,0:T(8,128)(2,1)S(1)}, bf16[128,128]{1,0:T(8,128)(2,1)S(1)}, u32[]{:S(2)}, u32[]{:S(2)}) %collective-permute-start.15) | collective-permute-done | bytes 32800 | tf_op jit(solution)/shard_map/ppermute | solution.py:211
  31.7 1.7 %collective-permute-start.17 = (bf16[2,128,128]{2,1,0:T(8,128)(2,1)S(1)}, bf16[2,128,128]{2,1,0:T(8,128)(2,1)S(1)}, u32[]{:S(2)}, u32[]{:S(2)}) collective-permute-start(bf16[2,128,128]{2,1,0:T(8,128)(2,1)S(1)} %pair_two_late.1), channel_id=1, source_target_pairs={{0,16},{4,20},{8,24},{12,28},{16,0},{20,4},{24,8},{28,12},{1,17},{... | collective-permute-start | bytes 196616 | tf_op jit(solution)/shard_map/ppermute | solution.py:211
  33.4 2.8 %collective-permute-start.16 = (bf16[2,128,128]{2,1,0:T(8,128)(2,1)S(1)}, bf16[2,128,128]{2,1,0:T(8,128)(2,1)S(1)}, u32[]{:S(2)}, u32[]{:S(2)}) collective-permute-start(bf16[2,128,128]{2,1,0:T(8,128)(2,1)S(1)} %pair_two_late.1), channel_id=1, source_target_pairs={{0,8},{4,12},{8,0},{12,4},{16,24},{20,28},{24,16},{28,20},{1,9},{5... | collective-permute-start | bytes 196616 | tf_op jit(solution)/shard_map/ppermute | solution.py:211
  36.2 1.3 %collective-permute-start.23 = (bf16[2,128,128]{2,1,0:T(8,128)(2,1)S(1)}, bf16[2,128,128]{2,1,0:T(8,128)(2,1)S(1)}, u32[]{:S(2)}, u32[]{:S(2)}) collective-permute-start(bf16[2,128,128]{2,1,0:T(8,128)(2,1)S(1)} %get-tuple-element.60), channel_id=1, source_target_pairs={{0,4},{4,0},{8,12},{12,8},{16,20},{20,16},{24,28},{28,24},{1,5},{5... | collective-permute-start | bytes 196616 | tf_op jit(solution)/shard_map/ppermute | solution.py:211
  37.5 0.3 collective-permute-start.27
  37.8 2.7 %collective-permute-done.23.refs_1_ = bf16[2,128,128]{2,1,0:T(8,128)(2,1)S(1)} collective-permute-done((bf16[2,128,128]{2,1,0:T(8,128)(2,1)S(1)}, bf16[2,128,128]{2,1,0:T(8,128)(2,1)S(1)}, u32[]{:S(2)}, u32[]{:S(2)}) %collective-permute-start.23) | collective-permute-done | bytes 65568 | tf_op jit(solution)/shard_map/ppermute | solution.py:211
  40.5 3.8 %collective-permute-start.28 = (bf16[128,128]{1,0:T(8,128)(2,1)S(1)}, bf16[128,128]{1,0:T(8,128)(2,1)S(1)}, u32[]{:S(2)}, u32[]{:S(2)}) collective-permute-start(bf16[128,128]{1,0:T(8,128)(2,1)S(1)} %get-tuple-element.58.refs_5_), channel_id=1, source_target_pairs={{0,24},{4,28},{8,16},{12,20},{16,8},{20,12},{24,0},{28,4},{1,25},{... | collective-permute-start | bytes 98312 | tf_op jit(solution)/shard_map/ppermute | solution.py:211
  44.3 0.1 collective-permute-start.29
  44.4 0.4 forward_two.1
  44.9 0.1 collective-permute-start.24
  44.9 1.0 %collective-permute-start.25 = (bf16[128,128]{1,0:T(8,128)(2,1)S(1)}, bf16[128,128]{1,0:T(8,128)(2,1)S(1)}, u32[]{:S(2)}, u32[]{:S(2)}) collective-permute-start(bf16[128,128]{1,0:T(8,128)(2,1)S(1)} %get-tuple-element.64), channel_id=1, source_target_pairs={{0,2},{1,3},{2,0},{3,1},{4,6},{5,7},{6,4},{7,5},{8,10},{9,11},{10,... | collective-permute-start | bytes 98312 | tf_op jit(solution)/shard_map/ppermute | solution.py:211
  45.9 0.9 %collective-permute-start.26 = (bf16[128,128]{1,0:T(8,128)(2,1)S(1)}, bf16[128,128]{1,0:T(8,128)(2,1)S(1)}, u32[]{:S(2)}, u32[]{:S(2)}) collective-permute-start(bf16[128,128]{1,0:T(8,128)(2,1)S(1)} %get-tuple-element.65), channel_id=1, source_target_pairs={{0,3},{1,2},{2,1},{3,0},{4,7},{5,6},{6,5},{7,4},{8,11},{9,10},{10,... | collective-permute-start | bytes 98312 | tf_op jit(solution)/shard_map/ppermute | solution.py:211
  46.8 1.5 %collective-permute-done.29.refs_6_ = bf16[128,128]{1,0:T(8,128)(2,1)S(1)} collective-permute-done((bf16[128,128]{1,0:T(8,128)(2,1)S(1)}, bf16[128,128]{1,0:T(8,128)(2,1)S(1)}, u32[]{:S(2)}, u32[]{:S(2)}) %collective-permute-start.29) | collective-permute-done | bytes 32800 | tf_op jit(solution)/shard_map/ppermute | solution.py:211
  48.3 0.7 %adjoint_end.1 = (f32[128,128]{1,0:T(8,128)}, f32[8,128]{1,0:T(8,128)S(1)}) custom-call(f32[128,128]{1,0:T(8,128)S(1)} %get-tuple-element.66.refs_0_, f32[128,128]{1,0:T(8,128)S(1)} %get-tuple-element.67.refs_1_, f32[1,128]{1,0:T(1,128)S(1)} %get-tuple-element.47.refs_0_.refs_2_, bf16[128,128]{1,0:T(8,128)(2,1)S(1)} %collective-permute-done.27.refs_3_, ...), custom_call_target="tpu_custom_call" | custom-call | flops 3000000000 | bytes 365056 | tf_op jit(solution)/shard_map/adjoint_end/pallas_call | solution.py:36
  49.1 0.2 collective-permute-done.26.refs_5_
  49.3 0.7 %forward_end.1 = f32[128,128]{1,0:T(8,128)} custom-call(f32[128,128]{1,0:T(8,128)S(1)} %get-tuple-element.37.refs_0_, f32[128,128]{1,0:T(8,128)S(1)} %get-tuple-element.38.refs_1_, bf16[128,128]{1,0:T(8,128)(2,1)S(1)} %get-tuple-element.62.refs_2_, bf16[128,128]{1,0:T(8,128)(2,1)S(1)} %collective-permute-done.24.refs_3_, ...), custom_call_target="tpu_custom_call" | custom-call | flops 1000000000 | bytes 327680 | tf_op jit(solution)/shard_map/forward_end/pallas_call | solution.py:36
  (30 shorter events, 0.2 us)
Async XLA Ops:
  1.9 6.4 %collective-permute-start.3 = (bf16[128,128]{1,0:T(8,128)(2,1)S(1)}, bf16[128,128]{1,0:T(8,128)(2,1)S(1)}, u32[]{:S(2)}, u32[]{:S(2)}) collective-permute-start(bf16[128,128]{1,0:T(8,128)(2,1)S(1)} %get-tuple-element.41.refs_1_), channel_id=1, source_target_pairs={{0,3},{1,2},{2,1},{3,0},{4,7},{5,6},{6,5},{7,4},{8,11},{9,10},{10,... | collective-permute-start | bytes 98312 | tf_op jit(solution)/shard_map/ppermute | solution.py:211
  4.4 4.0 %collective-permute-start.2 = (bf16[128,128]{1,0:T(8,128)(2,1)S(1)}, bf16[128,128]{1,0:T(8,128)(2,1)S(1)}, u32[]{:S(2)}, u32[]{:S(2)}) collective-permute-start(bf16[128,128]{1,0:T(8,128)(2,1)S(1)} %get-tuple-element.41.refs_1_), channel_id=1, source_target_pairs={{0,2},{1,3},{2,0},{3,1},{4,6},{5,7},{6,4},{7,5},{8,10},{9,11},{10,... | collective-permute-start | bytes 98312 | tf_op jit(solution)/shard_map/ppermute | solution.py:211
  5.0 3.3 %collective-permute-start.1 = (bf16[128,128]{1,0:T(8,128)(2,1)S(1)}, bf16[128,128]{1,0:T(8,128)(2,1)S(1)}, u32[]{:S(2)}, u32[]{:S(2)}) collective-permute-start(bf16[128,128]{1,0:T(8,128)(2,1)S(1)} %get-tuple-element.41.refs_1_), channel_id=1, source_target_pairs={{0,1},{1,0},{2,3},{3,2},{4,5},{5,4},{6,7},{7,6},{8,9},{9,8},{10,11... | collective-permute-start | bytes 98312 | tf_op jit(solution)/shard_map/ppermute | solution.py:211
  5.0 5.2 %collective-permute-start = (bf16[128,128]{1,0:T(8,128)(2,1)S(1)}, bf16[128,128]{1,0:T(8,128)(2,1)S(1)}, u32[]{:S(2)}, u32[]{:S(2)}) collective-permute-start(bf16[128,128]{1,0:T(8,128)(2,1)S(1)} %get-tuple-element.40.refs_0_), channel_id=1, source_target_pairs={{0,4},{4,0},{8,12},{12,8},{16,20},{20,16},{24,28},{28,24},{1,5},{5... | collective-permute-start | bytes 98312 | tf_op jit(solution)/shard_map/ppermute | solution.py:211
  8.7 6.6 %collective-permute-start.10 = (f32[2,128,128]{2,1,0:T(8,128)S(1)}, f32[2,128,128]{2,1,0:T(8,128)S(1)}, u32[]{:S(2)}, u32[]{:S(2)}) collective-permute-start(f32[2,128,128]{2,1,0:T(8,128)S(1)} %get-tuple-element.49), channel_id=1, source_target_pairs={{0,4},{4,0},{8,12},{12,8},{16,20},{20,16},{24,28},{28,24},{1,5},{5... | collective-permute-start | bytes 393224 | tf_op jit(solution)/shard_map/ppermute | solution.py:211
  10.2 10.3 %collective-permute-start.6 = (bf16[2,128,128]{2,1,0:T(8,128)(2,1)S(1)}, bf16[2,128,128]{2,1,0:T(8,128)(2,1)S(1)}, u32[]{:S(2)}, u32[]{:S(2)}) collective-permute-start(bf16[2,128,128]{2,1,0:T(8,128)(2,1)S(1)} %pair_one_early.1.refs_1_), channel_id=1, source_target_pairs={{0,24},{4,28},{8,16},{12,20},{16,8},{20,12},{24,0},{28,4},{1,25},{... | collective-permute-start | bytes 196616 | tf_op jit(solution)/shard_map/ppermute | solution.py:211
  13.9 5.0 %collective-permute-start.13 = (f32[2,128,128]{2,1,0:T(8,128)S(1)}, f32[2,128,128]{2,1,0:T(8,128)S(1)}, u32[]{:S(2)}, u32[]{:S(2)}) collective-permute-start(f32[2,128,128]{2,1,0:T(8,128)S(1)} %get-tuple-element.42.refs_2_), channel_id=1, source_target_pairs={{0,4},{4,0},{8,12},{12,8},{16,20},{20,16},{24,28},{28,24},{1,5},{5... | collective-permute-start | bytes 393224 | tf_op jit(solution)/shard_map/ppermute | solution.py:211
  14.4 6.7 %collective-permute-start.5 = (bf16[2,128,128]{2,1,0:T(8,128)(2,1)S(1)}, bf16[2,128,128]{2,1,0:T(8,128)(2,1)S(1)}, u32[]{:S(2)}, u32[]{:S(2)}) collective-permute-start(bf16[2,128,128]{2,1,0:T(8,128)(2,1)S(1)} %pair_one_late.1), channel_id=1, source_target_pairs={{0,16},{4,20},{8,24},{12,28},{16,0},{20,4},{24,8},{28,12},{1,17},{... | collective-permute-start | bytes 196616 | tf_op jit(solution)/shard_map/ppermute | solution.py:211
  14.4 6.7 %collective-permute-start.4 = (bf16[2,128,128]{2,1,0:T(8,128)(2,1)S(1)}, bf16[2,128,128]{2,1,0:T(8,128)(2,1)S(1)}, u32[]{:S(2)}, u32[]{:S(2)}) collective-permute-start(bf16[2,128,128]{2,1,0:T(8,128)(2,1)S(1)} %pair_one_late.1), channel_id=1, source_target_pairs={{0,8},{4,12},{8,0},{12,4},{16,24},{20,28},{24,16},{28,20},{1,9},{5... | collective-permute-start | bytes 196616 | tf_op jit(solution)/shard_map/ppermute | solution.py:211
  15.3 8.2 %collective-permute-start.11 = (f32[128,128]{1,0:T(8,128)S(1)}, f32[128,128]{1,0:T(8,128)S(1)}, u32[]{:S(2)}, u32[]{:S(2)}) collective-permute-start(f32[128,128]{1,0:T(8,128)S(1)} %get-tuple-element.50), channel_id=1, source_target_pairs={{0,16},{4,20},{8,24},{12,28},{16,0},{20,4},{24,8},{28,12},{1,17},{... | collective-permute-start | bytes 196616 | tf_op jit(solution)/shard_map/ppermute | solution.py:211
  18.9 6.2 %collective-permute-start.12 = (f32[128,128]{1,0:T(8,128)S(1)}, f32[128,128]{1,0:T(8,128)S(1)}, u32[]{:S(2)}, u32[]{:S(2)}) collective-permute-start(f32[128,128]{1,0:T(8,128)S(1)} %get-tuple-element.51), channel_id=1, source_target_pairs={{0,24},{4,28},{8,16},{12,20},{16,8},{20,12},{24,0},{28,4},{1,25},{... | collective-permute-start | bytes 196616 | tf_op jit(solution)/shard_map/ppermute | solution.py:211
  20.5 5.0 %collective-permute-start.14 = (f32[128,128]{1,0:T(8,128)S(1)}, f32[128,128]{1,0:T(8,128)S(1)}, u32[]{:S(2)}, u32[]{:S(2)}) collective-permute-start(f32[128,128]{1,0:T(8,128)S(1)} %get-tuple-element.54), channel_id=1, source_target_pairs={{0,8},{4,12},{8,0},{12,4},{16,24},{20,28},{24,16},{28,20},{1,9},{5... | collective-permute-start | bytes 196616 | tf_op jit(solution)/shard_map/ppermute | solution.py:211
  21.5 5.4 %collective-permute-start.7 = (f32[128,128]{1,0:T(8,128)S(1)}, f32[128,128]{1,0:T(8,128)S(1)}, u32[]{:S(2)}, u32[]{:S(2)}) collective-permute-start(f32[128,128]{1,0:T(8,128)S(1)} %get-tuple-element.44), channel_id=1, source_target_pairs={{0,1},{1,0},{2,3},{3,2},{4,5},{5,4},{6,7},{7,6},{8,9},{9,8},{10,11... | collective-permute-start | bytes 196616 | tf_op jit(solution)/shard_map/ppermute | solution.py:211
  21.6 5.9 %collective-permute-start.8 = (f32[128,128]{1,0:T(8,128)S(1)}, f32[128,128]{1,0:T(8,128)S(1)}, u32[]{:S(2)}, u32[]{:S(2)}) collective-permute-start(f32[128,128]{1,0:T(8,128)S(1)} %get-tuple-element.45), channel_id=1, source_target_pairs={{0,2},{1,3},{2,0},{3,1},{4,6},{5,7},{6,4},{7,5},{8,10},{9,11},{10,... | collective-permute-start | bytes 196616 | tf_op jit(solution)/shard_map/ppermute | solution.py:211
  23.5 4.2 %collective-permute-start.9 = (f32[128,128]{1,0:T(8,128)S(1)}, f32[128,128]{1,0:T(8,128)S(1)}, u32[]{:S(2)}, u32[]{:S(2)}) collective-permute-start(f32[128,128]{1,0:T(8,128)S(1)} %get-tuple-element.46.refs_5_), channel_id=1, source_target_pairs={{0,3},{1,2},{2,1},{3,0},{4,7},{5,6},{6,5},{7,4},{8,11},{9,10},{10,... | collective-permute-start | bytes 196616 | tf_op jit(solution)/shard_map/ppermute | solution.py:211
  25.6 3.6 %collective-permute-start.21 = (bf16[128,128]{1,0:T(8,128)(2,1)S(1)}, bf16[128,128]{1,0:T(8,128)(2,1)S(1)}, u32[]{:S(2)}, u32[]{:S(2)}) collective-permute-start(bf16[128,128]{1,0:T(8,128)(2,1)S(1)} %get-tuple-element.55.refs_6_.refs_2_.refs_1_), channel_id=1, source_target_pairs={{0,3},{1,2},{2,1},{3,0},{4,7},{5,6},{6,5},{7,4},{8,11},{9,10},{10,... | collective-permute-start | bytes 98312 | tf_op jit(solution)/shard_map/ppermute | solution.py:211
  25.7 4.1 %collective-permute-start.20 = (bf16[128,128]{1,0:T(8,128)(2,1)S(1)}, bf16[128,128]{1,0:T(8,128)(2,1)S(1)}, u32[]{:S(2)}, u32[]{:S(2)}) collective-permute-start(bf16[128,128]{1,0:T(8,128)(2,1)S(1)} %get-tuple-element.55.refs_6_.refs_2_.refs_1_), channel_id=1, source_target_pairs={{0,2},{1,3},{2,0},{3,1},{4,6},{5,7},{6,4},{7,5},{8,10},{9,11},{10,... | collective-permute-start | bytes 98312 | tf_op jit(solution)/shard_map/ppermute | solution.py:211
  26.9 2.9 %collective-permute-start.19 = (bf16[128,128]{1,0:T(8,128)(2,1)S(1)}, bf16[128,128]{1,0:T(8,128)(2,1)S(1)}, u32[]{:S(2)}, u32[]{:S(2)}) collective-permute-start(bf16[128,128]{1,0:T(8,128)(2,1)S(1)} %get-tuple-element.55.refs_6_.refs_2_.refs_1_), channel_id=1, source_target_pairs={{0,1},{1,0},{2,3},{3,2},{4,5},{5,4},{6,7},{7,6},{8,9},{9,8},{10,11... | collective-permute-start | bytes 98312 | tf_op jit(solution)/shard_map/ppermute | solution.py:211
  27.7 4.0 %collective-permute-start.15 = (bf16[128,128]{1,0:T(8,128)(2,1)S(1)}, bf16[128,128]{1,0:T(8,128)(2,1)S(1)}, u32[]{:S(2)}, u32[]{:S(2)}) collective-permute-start(bf16[128,128]{1,0:T(8,128)(2,1)S(1)} %forward_middle.1.refs_0_), channel_id=1, source_target_pairs={{0,4},{4,0},{8,12},{12,8},{16,20},{20,16},{24,28},{28,24},{1,5},{5... | collective-permute-start | bytes 98312 | tf_op jit(solution)/shard_map/ppermute | solution.py:211
  30.1 7.4 %collective-permute-start.22 = (bf16[2,128,128]{2,1,0:T(8,128)(2,1)S(1)}, bf16[2,128,128]{2,1,0:T(8,128)(2,1)S(1)}, u32[]{:S(2)}, u32[]{:S(2)}) collective-permute-start(bf16[2,128,128]{2,1,0:T(8,128)(2,1)S(1)} %get-tuple-element.57), channel_id=1, source_target_pairs={{0,4},{4,0},{8,12},{12,8},{16,20},{20,16},{24,28},{28,24},{1,5},{5... | collective-permute-start | bytes 196616 | tf_op jit(solution)/shard_map/ppermute | solution.py:211
  31.7 12.7 %collective-permute-start.17 = (bf16[2,128,128]{2,1,0:T(8,128)(2,1)S(1)}, bf16[2,128,128]{2,1,0:T(8,128)(2,1)S(1)}, u32[]{:S(2)}, u32[]{:S(2)}) collective-permute-start(bf16[2,128,128]{2,1,0:T(8,128)(2,1)S(1)} %pair_two_late.1), channel_id=1, source_target_pairs={{0,16},{4,20},{8,24},{12,28},{16,0},{20,4},{24,8},{28,12},{1,17},{... | collective-permute-start | bytes 196616 | tf_op jit(solution)/shard_map/ppermute | solution.py:211
  33.4 11.0 %collective-permute-start.16 = (bf16[2,128,128]{2,1,0:T(8,128)(2,1)S(1)}, bf16[2,128,128]{2,1,0:T(8,128)(2,1)S(1)}, u32[]{:S(2)}, u32[]{:S(2)}) collective-permute-start(bf16[2,128,128]{2,1,0:T(8,128)(2,1)S(1)} %pair_two_late.1), channel_id=1, source_target_pairs={{0,8},{4,12},{8,0},{12,4},{16,24},{20,28},{24,16},{28,20},{1,9},{5... | collective-permute-start | bytes 196616 | tf_op jit(solution)/shard_map/ppermute | solution.py:211
  36.2 8.1 %collective-permute-start.18 = (bf16[2,128,128]{2,1,0:T(8,128)(2,1)S(1)}, bf16[2,128,128]{2,1,0:T(8,128)(2,1)S(1)}, u32[]{:S(2)}, u32[]{:S(2)}) collective-permute-start(bf16[2,128,128]{2,1,0:T(8,128)(2,1)S(1)} %pair_two_early.1.refs_1_), channel_id=1, source_target_pairs={{0,24},{4,28},{8,16},{12,20},{16,8},{20,12},{24,0},{28,4},{1,25},{... | collective-permute-start | bytes 196616 | tf_op jit(solution)/shard_map/ppermute | solution.py:211
  36.2 4.3 %collective-permute-start.23 = (bf16[2,128,128]{2,1,0:T(8,128)(2,1)S(1)}, bf16[2,128,128]{2,1,0:T(8,128)(2,1)S(1)}, u32[]{:S(2)}, u32[]{:S(2)}) collective-permute-start(bf16[2,128,128]{2,1,0:T(8,128)(2,1)S(1)} %get-tuple-element.60), channel_id=1, source_target_pairs={{0,4},{4,0},{8,12},{12,8},{16,20},{20,16},{24,28},{28,24},{1,5},{5... | collective-permute-start | bytes 196616 | tf_op jit(solution)/shard_map/ppermute | solution.py:211
  37.5 8.4 %collective-permute-start.27 = (bf16[128,128]{1,0:T(8,128)(2,1)S(1)}, bf16[128,128]{1,0:T(8,128)(2,1)S(1)}, u32[]{:S(2)}, u32[]{:S(2)}) collective-permute-start(bf16[128,128]{1,0:T(8,128)(2,1)S(1)} %get-tuple-element.68), channel_id=1, source_target_pairs={{0,16},{4,20},{8,24},{12,28},{16,0},{20,4},{24,8},{28,12},{1,17},{... | collective-permute-start | bytes 98312 | tf_op jit(solution)/shard_map/ppermute | solution.py:211
  40.5 6.3 %collective-permute-start.28 = (bf16[128,128]{1,0:T(8,128)(2,1)S(1)}, bf16[128,128]{1,0:T(8,128)(2,1)S(1)}, u32[]{:S(2)}, u32[]{:S(2)}) collective-permute-start(bf16[128,128]{1,0:T(8,128)(2,1)S(1)} %get-tuple-element.58.refs_5_), channel_id=1, source_target_pairs={{0,24},{4,28},{8,16},{12,20},{16,8},{20,12},{24,0},{28,4},{1,25},{... | collective-permute-start | bytes 98312 | tf_op jit(solution)/shard_map/ppermute | solution.py:211
  44.3 4.0 %collective-permute-start.29 = (bf16[128,128]{1,0:T(8,128)(2,1)S(1)}, bf16[128,128]{1,0:T(8,128)(2,1)S(1)}, u32[]{:S(2)}, u32[]{:S(2)}) collective-permute-start(bf16[128,128]{1,0:T(8,128)(2,1)S(1)} %get-tuple-element.61.refs_6_), channel_id=1, source_target_pairs={{0,8},{4,12},{8,0},{12,4},{16,24},{20,28},{24,16},{28,20},{1,9},{5... | collective-permute-start | bytes 98312 | tf_op jit(solution)/shard_map/ppermute | solution.py:211
  44.9 4.2 %collective-permute-start.24 = (bf16[128,128]{1,0:T(8,128)(2,1)S(1)}, bf16[128,128]{1,0:T(8,128)(2,1)S(1)}, u32[]{:S(2)}, u32[]{:S(2)}) collective-permute-start(bf16[128,128]{1,0:T(8,128)(2,1)S(1)} %get-tuple-element.63), channel_id=1, source_target_pairs={{0,1},{1,0},{2,3},{3,2},{4,5},{5,4},{6,7},{7,6},{8,9},{9,8},{10,11... | collective-permute-start | bytes 98312 | tf_op jit(solution)/shard_map/ppermute | solution.py:211
  44.9 4.1 %collective-permute-start.25 = (bf16[128,128]{1,0:T(8,128)(2,1)S(1)}, bf16[128,128]{1,0:T(8,128)(2,1)S(1)}, u32[]{:S(2)}, u32[]{:S(2)}) collective-permute-start(bf16[128,128]{1,0:T(8,128)(2,1)S(1)} %get-tuple-element.64), channel_id=1, source_target_pairs={{0,2},{1,3},{2,0},{3,1},{4,6},{5,7},{6,4},{7,5},{8,10},{9,11},{10,... | collective-permute-start | bytes 98312 | tf_op jit(solution)/shard_map/ppermute | solution.py:211
  45.9 3.3 %collective-permute-start.26 = (bf16[128,128]{1,0:T(8,128)(2,1)S(1)}, bf16[128,128]{1,0:T(8,128)(2,1)S(1)}, u32[]{:S(2)}, u32[]{:S(2)}) collective-permute-start(bf16[128,128]{1,0:T(8,128)(2,1)S(1)} %get-tuple-element.65), channel_id=1, source_target_pairs={{0,3},{1,2},{2,1},{3,0},{4,7},{5,6},{6,5},{7,4},{8,11},{9,10},{10,... | collective-permute-start | bytes 98312 | tf_op jit(solution)/shard_map/ppermute | solution.py:211

commit v14 on v13

--- a/solution.py
+++ b/solution.py
@@ -187,8 +187,7 @@
     "pair_one_late": ("adjoint_one",),
     "forward_two": ("far_two", "near_two"),
     "forward_end": ("adjoint_end",),
-    "pair_two_early": ("adjoint_middle",),
-    "forward_middle": ("adjoint_middle",),
+    "pair_two_early": ("adjoint_middle", "adjoint_two"),
     "pair_one_early": ("dense",),
     "adjoint_middle": ("forward_one",),
 }

time: 50.1 us -> 48.3 us (0.964)
  starting transfers between devices: 33 us -> 29.8 us
  waiting for transfers between devices: 10.3 us -> 11.5 us
    ppermute x30, starting transfers between devices: 33 us -> 29.8 us  [send(): return lax.ppermute(value, axis, [(i, i ^ step) for i in range(count)])]
    ppermute x30, waiting for transfers between devices: 10.3 us -> 11.5 us  [send(): return lax.ppermute(value, axis, [(i, i ^ step) for i in range(count)])]
  transfers between devices with their start and end apart: 30 -> 30, of which waited for: 11 -> 12; matrix products, arithmetic and copies ran while one was open for 0% -> 0% of each run, Pallas kernels for 6% -> 7%
where the time goes in v14:
time: 48.3 us; the launch traced here: 47.9 us
  starting transfers between devices  29.8 us (62%)
  waiting for transfers between devices  11.5 us (24%)
  Pallas kernels  5.16 us (11%)
  between operations  1.45 us (3%)
    ppermute x30, starting transfers between devices, send(): return lax.ppermute(value, axis, [(i, i ^ step) for i in range(count)])  29.8 us
    ppermute x30, waiting for transfers between devices, send(): return lax.ppermute(value, axis, [(i, i ^ step) for i in range(count)])  11.5 us
    pallas_call x18, Pallas kernels, call(): pl.pallas_call(ordered, out_shape=outs, in_specs=[*in_specs, *[pl.BlockSp...  5.16 us
  transfers between devices with their start and end apart: 30, of which 12 were waited for; matrix products, arithmetic and copies ran while one was open for 0% of the time, Pallas kernels for 7%

profile of v14, /device:TPU:0, one launch (start us, length us, event | category | flops | bytes accessed | tf_op | source)
XLA Modules:
  0.0 47.9 jit_solution(12988191888202625165)
XLA Ops:
  0.6 1.3 %start.1 = (bf16[128,128]{1,0:T(8,128)(2,1)S(1)}, bf16[128,128]{1,0:T(8,128)(2,1)S(1)}, f32[1,128]{1,0:T(1,128)S(1)}, f32[128,128]{1,0:T(8,128)S(1)}, f32[128,12...) custom-call(s32[1,128]{1,0:T(1,128)} %bitcast.1, f32[8]{0:T(128)} %refs_1_.2, ...), custom_call_target="tpu_custom_call" | custom-call | bytes 1967136 | tf_op jit(solution)/shard_map/start/pallas_call | solution.py:36
  1.9 2.4 %collective-permute-start.3 = (bf16[128,128]{1,0:T(8,128)(2,1)S(1)}, bf16[128,128]{1,0:T(8,128)(2,1)S(1)}, u32[]{:S(2)}, u32[]{:S(2)}) collective-permute-start(bf16[128,128]{1,0:T(8,128)(2,1)S(1)} %get-tuple-element.41.refs_1_), channel_id=1, source_target_pairs={{0,3},{1,2},{2,1},{3,0},{4,7},{5,6},{6,5},{7,4},{8,11},{9,10},{10,... | collective-permute-start | bytes 98312 | tf_op jit(solution)/shard_map/ppermute | solution.py:210
  4.4 0.6 %collective-permute-start.2 = (bf16[128,128]{1,0:T(8,128)(2,1)S(1)}, bf16[128,128]{1,0:T(8,128)(2,1)S(1)}, u32[]{:S(2)}, u32[]{:S(2)}) collective-permute-start(bf16[128,128]{1,0:T(8,128)(2,1)S(1)} %get-tuple-element.41.refs_1_), channel_id=1, source_target_pairs={{0,2},{1,3},{2,0},{3,1},{4,6},{5,7},{6,4},{7,5},{8,10},{9,11},{10,... | collective-permute-start | bytes 98312 | tf_op jit(solution)/shard_map/ppermute | solution.py:210
  5.0 0.0 collective-permute-start.1
  5.0 1.8 %collective-permute-start = (bf16[128,128]{1,0:T(8,128)(2,1)S(1)}, bf16[128,128]{1,0:T(8,128)(2,1)S(1)}, u32[]{:S(2)}, u32[]{:S(2)}) collective-permute-start(bf16[128,128]{1,0:T(8,128)(2,1)S(1)} %get-tuple-element.40.refs_0_), channel_id=1, source_target_pairs={{0,4},{4,0},{8,12},{12,8},{16,20},{20,16},{24,28},{28,24},{1,5},{5... | collective-permute-start | bytes 98312 | tf_op jit(solution)/shard_map/ppermute | solution.py:210
  7.5 0.9 %dense.1.refs_2_.refs_0_ = bf16[512,1024]{1,0:T(8,128)(2,1)S(1)} custom-call(bf16[1,1,24,128,128]{4,3,2,1,0:T(8,128)(2,1)S(1)} %get-tuple-element.39.refs_0_, s32[1,1,24]{2,1,0:T(1,128)} %refs_1_.3, s32[1,1,24]{2,1,0:T(1,128)} %refs_2_.3, s32[1,1]{1,0:T(1,128)S(6)} %copy.10.refs_3_), custom_call_target="tpu_custom_call" | custom-call | bytes 1835204 | tf_op jit(solution)/shard_map/dense/pallas_call | solution.py:36
  8.4 0.3 adjoint_one.1
  8.7 1.6 %collective-permute-start.11 = (f32[2,128,128]{2,1,0:T(8,128)S(1)}, f32[2,128,128]{2,1,0:T(8,128)S(1)}, u32[]{:S(2)}, u32[]{:S(2)}) collective-permute-start(f32[2,128,128]{2,1,0:T(8,128)S(1)} %get-tuple-element.49), channel_id=1, source_target_pairs={{0,4},{4,0},{8,12},{12,8},{16,20},{20,16},{24,28},{28,24},{1,5},{5... | collective-permute-start | bytes 393224 | tf_op jit(solution)/shard_map/ppermute | solution.py:210
  10.2 3.7 %collective-permute-start.6 = (bf16[2,128,128]{2,1,0:T(8,128)(2,1)S(1)}, bf16[2,128,128]{2,1,0:T(8,128)(2,1)S(1)}, u32[]{:S(2)}, u32[]{:S(2)}) collective-permute-start(bf16[2,128,128]{2,1,0:T(8,128)(2,1)S(1)} %pair_one_early.1.refs_1_), channel_id=1, source_target_pairs={{0,24},{4,28},{8,16},{12,20},{16,8},{20,12},{24,0},{28,4},{1,25},{... | collective-permute-start | bytes 196616 | tf_op jit(solution)/shard_map/ppermute | solution.py:210
  13.9 0.7 %collective-permute-start.14 = (f32[2,128,128]{2,1,0:T(8,128)S(1)}, f32[2,128,128]{2,1,0:T(8,128)S(1)}, u32[]{:S(2)}, u32[]{:S(2)}) collective-permute-start(f32[2,128,128]{2,1,0:T(8,128)S(1)} %get-tuple-element.42.refs_2_), channel_id=1, source_target_pairs={{0,4},{4,0},{8,12},{12,8},{16,20},{20,16},{24,28},{28,24},{1,5},{5... | collective-permute-start | bytes 393224 | tf_op jit(solution)/shard_map/ppermute | solution.py:210
  14.6 0.6 %collective-permute-start.4 = (bf16[2,128,128]{2,1,0:T(8,128)(2,1)S(1)}, bf16[2,128,128]{2,1,0:T(8,128)(2,1)S(1)}, u32[]{:S(2)}, u32[]{:S(2)}) collective-permute-start(bf16[2,128,128]{2,1,0:T(8,128)(2,1)S(1)} %pair_one_late.1), channel_id=1, source_target_pairs={{0,8},{4,12},{8,0},{12,4},{16,24},{20,28},{24,16},{28,20},{1,9},{5... | collective-permute-start | bytes 196616 | tf_op jit(solution)/shard_map/ppermute | solution.py:210
  15.3 2.5 %collective-permute-start.12 = (f32[128,128]{1,0:T(8,128)S(1)}, f32[128,128]{1,0:T(8,128)S(1)}, u32[]{:S(2)}, u32[]{:S(2)}) collective-permute-start(f32[128,128]{1,0:T(8,128)S(1)} %get-tuple-element.50), channel_id=1, source_target_pairs={{0,16},{4,20},{8,24},{12,28},{16,0},{20,4},{24,8},{28,12},{1,17},{... | collective-permute-start | bytes 196616 | tf_op jit(solution)/shard_map/ppermute | solution.py:210
  17.8 1.1 %collective-permute-done.14.refs_1_ = f32[2,128,128]{2,1,0:T(8,128)S(1)} collective-permute-done((f32[2,128,128]{2,1,0:T(8,128)S(1)}, f32[2,128,128]{2,1,0:T(8,128)S(1)}, u32[]{:S(2)}, u32[]{:S(2)}) %collective-permute-start.14) | collective-permute-done | bytes 131104 | tf_op jit(solution)/shard_map/ppermute | solution.py:210
  18.9 1.8 %collective-permute-start.13 = (f32[128,128]{1,0:T(8,128)S(1)}, f32[128,128]{1,0:T(8,128)S(1)}, u32[]{:S(2)}, u32[]{:S(2)}) collective-permute-start(f32[128,128]{1,0:T(8,128)S(1)} %get-tuple-element.51), channel_id=1, source_target_pairs={{0,24},{4,28},{8,16},{12,20},{16,8},{20,12},{24,0},{28,4},{1,25},{... | collective-permute-start | bytes 196616 | tf_op jit(solution)/shard_map/ppermute | solution.py:210
  20.7 0.1 collective-permute-start.15
  20.7 0.5 %collective-permute-done.5.refs_3_ = bf16[2,128,128]{2,1,0:T(8,128)(2,1)S(1)} collective-permute-done((bf16[2,128,128]{2,1,0:T(8,128)(2,1)S(1)}, bf16[2,128,128]{2,1,0:T(8,128)(2,1)S(1)}, u32[]{:S(2)}, u32[]{:S(2)}) %collective-permute-start.5) | collective-permute-done | bytes 65568 | tf_op jit(solution)/shard_map/ppermute | solution.py:210
  21.2 0.4 forward_one.1
  21.7 0.1 collective-permute-start.7
  21.8 1.6 %collective-permute-start.8 = (f32[128,128]{1,0:T(8,128)S(1)}, f32[128,128]{1,0:T(8,128)S(1)}, u32[]{:S(2)}, u32[]{:S(2)}) collective-permute-start(f32[128,128]{1,0:T(8,128)S(1)} %get-tuple-element.45), channel_id=1, source_target_pairs={{0,2},{1,3},{2,0},{3,1},{4,6},{5,7},{6,4},{7,5},{8,10},{9,11},{10,... | collective-permute-start | bytes 196616 | tf_op jit(solution)/shard_map/ppermute | solution.py:210
  23.3 0.2 collective-permute-done.12.refs_1_
  23.6 0.1 collective-permute-start.9
  23.6 1.4 %collective-permute-done.13.refs_2_ = f32[128,128]{1,0:T(8,128)S(1)} collective-permute-done((f32[128,128]{1,0:T(8,128)S(1)}, f32[128,128]{1,0:T(8,128)S(1)}, u32[]{:S(2)}, u32[]{:S(2)}) %collective-permute-start.13) | collective-permute-done | bytes 65568 | tf_op jit(solution)/shard_map/ppermute | solution.py:210
  25.0 0.6 %collective-permute-done.15.refs_4_ = f32[128,128]{1,0:T(8,128)S(1)} collective-permute-done((f32[128,128]{1,0:T(8,128)S(1)}, f32[128,128]{1,0:T(8,128)S(1)}, u32[]{:S(2)}, u32[]{:S(2)}) %collective-permute-start.15) | collective-permute-done | bytes 65568 | tf_op jit(solution)/shard_map/ppermute | solution.py:210
  25.7 0.1 collective-permute-start.18
  25.7 1.2 %collective-permute-start.17 = (bf16[128,128]{1,0:T(8,128)(2,1)S(1)}, bf16[128,128]{1,0:T(8,128)(2,1)S(1)}, u32[]{:S(2)}, u32[]{:S(2)}) collective-permute-start(bf16[128,128]{1,0:T(8,128)(2,1)S(1)} %get-tuple-element.55.refs_1_.refs_2_), channel_id=1, source_target_pairs={{0,2},{1,3},{2,0},{3,1},{4,6},{5,7},{6,4},{7,5},{8,10},{9,11},{10,... | collective-permute-start | bytes 98312 | tf_op jit(solution)/shard_map/ppermute | solution.py:210
  26.9 0.7 %collective-permute-start.16 = (bf16[128,128]{1,0:T(8,128)(2,1)S(1)}, bf16[128,128]{1,0:T(8,128)(2,1)S(1)}, u32[]{:S(2)}, u32[]{:S(2)}) collective-permute-start(bf16[128,128]{1,0:T(8,128)(2,1)S(1)} %get-tuple-element.55.refs_1_.refs_2_), channel_id=1, source_target_pairs={{0,1},{1,0},{2,3},{3,2},{4,5},{5,4},{6,7},{7,6},{8,9},{9,8},{10,11... | collective-permute-start | bytes 98312 | tf_op jit(solution)/shard_map/ppermute | solution.py:210
  27.6 0.2 collective-permute-done.9.refs_5_
  27.9 1.3 %collective-permute-start.10 = (bf16[128,128]{1,0:T(8,128)(2,1)S(1)}, bf16[128,128]{1,0:T(8,128)(2,1)S(1)}, u32[]{:S(2)}, u32[]{:S(2)}) collective-permute-start(bf16[128,128]{1,0:T(8,128)(2,1)S(1)} %forward_middle.1.refs_0_), channel_id=1, source_target_pairs={{0,4},{4,0},{8,12},{12,8},{16,20},{20,16},{24,28},{28,24},{1,5},{5... | collective-permute-start | bytes 98312 | tf_op jit(solution)/shard_map/ppermute | solution.py:210
  29.1 0.8 %collective-permute-done.17.refs_3_ = bf16[128,128]{1,0:T(8,128)(2,1)S(1)} collective-permute-done((bf16[128,128]{1,0:T(8,128)(2,1)S(1)}, bf16[128,128]{1,0:T(8,128)(2,1)S(1)}, u32[]{:S(2)}, u32[]{:S(2)}) %collective-permute-start.17) | collective-permute-done | bytes 32800 | tf_op jit(solution)/shard_map/ppermute | solution.py:210
  29.9 0.3 adjoint_two.1
  30.2 0.7 %collective-permute-start.22 = (bf16[2,128,128]{2,1,0:T(8,128)(2,1)S(1)}, bf16[2,128,128]{2,1,0:T(8,128)(2,1)S(1)}, u32[]{:S(2)}, u32[]{:S(2)}) collective-permute-start(bf16[2,128,128]{2,1,0:T(8,128)(2,1)S(1)} %get-tuple-element.58), channel_id=1, source_target_pairs={{0,4},{4,0},{8,12},{12,8},{16,20},{20,16},{24,28},{28,24},{1,5},{5... | collective-permute-start | bytes 196616 | tf_op jit(solution)/shard_map/ppermute | solution.py:210
  30.9 0.9 %collective-permute-done.10.refs_1_ = bf16[128,128]{1,0:T(8,128)(2,1)S(1)} collective-permute-done((bf16[128,128]{1,0:T(8,128)(2,1)S(1)}, bf16[128,128]{1,0:T(8,128)(2,1)S(1)}, u32[]{:S(2)}, u32[]{:S(2)}) %collective-permute-start.10) | collective-permute-done | bytes 32800 | tf_op jit(solution)/shard_map/ppermute | solution.py:210
  31.9 1.5 %collective-permute-start.20 = (bf16[2,128,128]{2,1,0:T(8,128)(2,1)S(1)}, bf16[2,128,128]{2,1,0:T(8,128)(2,1)S(1)}, u32[]{:S(2)}, u32[]{:S(2)}) collective-permute-start(bf16[2,128,128]{2,1,0:T(8,128)(2,1)S(1)} %pair_two_late.1), channel_id=1, source_target_pairs={{0,16},{4,20},{8,24},{12,28},{16,0},{20,4},{24,8},{28,12},{1,17},{... | collective-permute-start | bytes 196616 | tf_op jit(solution)/shard_map/ppermute | solution.py:210
  33.4 2.8 %collective-permute-start.19 = (bf16[2,128,128]{2,1,0:T(8,128)(2,1)S(1)}, bf16[2,128,128]{2,1,0:T(8,128)(2,1)S(1)}, u32[]{:S(2)}, u32[]{:S(2)}) collective-permute-start(bf16[2,128,128]{2,1,0:T(8,128)(2,1)S(1)} %pair_two_late.1), channel_id=1, source_target_pairs={{0,8},{4,12},{8,0},{12,4},{16,24},{20,28},{24,16},{28,20},{1,9},{5... | collective-permute-start | bytes 196616 | tf_op jit(solution)/shard_map/ppermute | solution.py:210
  36.1 1.3 %collective-permute-start.21 = (bf16[2,128,128]{2,1,0:T(8,128)(2,1)S(1)}, bf16[2,128,128]{2,1,0:T(8,128)(2,1)S(1)}, u32[]{:S(2)}, u32[]{:S(2)}) collective-permute-start(bf16[2,128,128]{2,1,0:T(8,128)(2,1)S(1)} %pair_two_early.1.refs_1_), channel_id=1, source_target_pairs={{0,24},{4,28},{8,16},{12,20},{16,8},{20,12},{24,0},{28,4},{1,25},{... | collective-permute-start | bytes 196616 | tf_op jit(solution)/shard_map/ppermute | solution.py:210
  37.5 0.3 collective-permute-start.27
  37.8 2.6 %collective-permute-done.23.refs_1_ = bf16[2,128,128]{2,1,0:T(8,128)(2,1)S(1)} collective-permute-done((bf16[2,128,128]{2,1,0:T(8,128)(2,1)S(1)}, bf16[2,128,128]{2,1,0:T(8,128)(2,1)S(1)}, u32[]{:S(2)}, u32[]{:S(2)}) %collective-permute-start.23) | collective-permute-done | bytes 65568 | tf_op jit(solution)/shard_map/ppermute | solution.py:210
  40.4 0.1 collective-permute-start.28
  40.5 0.6 %collective-permute-start.29 = (bf16[128,128]{1,0:T(8,128)(2,1)S(1)}, bf16[128,128]{1,0:T(8,128)(2,1)S(1)}, u32[]{:S(2)}, u32[]{:S(2)}) collective-permute-start(bf16[128,128]{1,0:T(8,128)(2,1)S(1)} %get-tuple-element.61.refs_6_), channel_id=1, source_target_pairs={{0,8},{4,12},{8,0},{12,4},{16,24},{20,28},{24,16},{28,20},{1,9},{5... | collective-permute-start | bytes 98312 | tf_op jit(solution)/shard_map/ppermute | solution.py:210
  41.1 1.5 %collective-permute-done.21.refs_4_ = bf16[2,128,128]{2,1,0:T(8,128)(2,1)S(1)} collective-permute-done((bf16[2,128,128]{2,1,0:T(8,128)(2,1)S(1)}, bf16[2,128,128]{2,1,0:T(8,128)(2,1)S(1)}, u32[]{:S(2)}, u32[]{:S(2)}) %collective-permute-start.21) | collective-permute-done | bytes 65568 | tf_op jit(solution)/shard_map/ppermute | solution.py:210
  42.6 0.4 forward_two.1
  43.0 0.1 collective-permute-start.24
  43.1 0.4 collective-permute-start.25
  43.5 1.4 %collective-permute-start.26 = (bf16[128,128]{1,0:T(8,128)(2,1)S(1)}, bf16[128,128]{1,0:T(8,128)(2,1)S(1)}, u32[]{:S(2)}, u32[]{:S(2)}) collective-permute-start(bf16[128,128]{1,0:T(8,128)(2,1)S(1)} %get-tuple-element.65), channel_id=1, source_target_pairs={{0,3},{1,2},{2,1},{3,0},{4,7},{5,6},{6,5},{7,4},{8,11},{9,10},{10,... | collective-permute-start | bytes 98312 | tf_op jit(solution)/shard_map/ppermute | solution.py:210
  45.0 1.1 %collective-permute-done.28.refs_4_ = bf16[128,128]{1,0:T(8,128)(2,1)S(1)} collective-permute-done((bf16[128,128]{1,0:T(8,128)(2,1)S(1)}, bf16[128,128]{1,0:T(8,128)(2,1)S(1)}, u32[]{:S(2)}, u32[]{:S(2)}) %collective-permute-start.28) | collective-permute-done | bytes 32800 | tf_op jit(solution)/shard_map/ppermute | solution.py:210
  46.1 0.7 %adjoint_end.1 = (f32[128,128]{1,0:T(8,128)}, f32[8,128]{1,0:T(8,128)S(1)}) custom-call(f32[128,128]{1,0:T(8,128)S(1)} %get-tuple-element.66.refs_0_, f32[128,128]{1,0:T(8,128)S(1)} %get-tuple-element.67.refs_1_, f32[1,128]{1,0:T(1,128)S(1)} %get-tuple-element.47.refs_0_.refs_2_, bf16[128,128]{1,0:T(8,128)(2,1)S(1)} %collective-permute-done.27.refs_3_, ...), custom_call_target="tpu_custom_call" | custom-call | flops 3000000000 | bytes 365056 | tf_op jit(solution)/shard_map/adjoint_end/pallas_call | solution.py:36
  46.9 0.4 collective-permute-done.25.refs_4_
  47.3 0.7 %forward_end.1 = f32[128,128]{1,0:T(8,128)} custom-call(f32[128,128]{1,0:T(8,128)S(1)} %get-tuple-element.37.refs_0_, f32[128,128]{1,0:T(8,128)S(1)} %get-tuple-element.38.refs_1_, bf16[128,128]{1,0:T(8,128)(2,1)S(1)} %get-tuple-element.62.refs_2_, bf16[128,128]{1,0:T(8,128)(2,1)S(1)} %collective-permute-done.24.refs_3_, ...), custom_call_target="tpu_custom_call" | custom-call | flops 1000000000 | bytes 327680 | tf_op jit(solution)/shard_map/forward_end/pallas_call | solution.py:36
  (30 shorter events, 0.2 us)
Async XLA Ops:
  1.9 6.4 %collective-permute-start.3 = (bf16[128,128]{1,0:T(8,128)(2,1)S(1)}, bf16[128,128]{1,0:T(8,128)(2,1)S(1)}, u32[]{:S(2)}, u32[]{:S(2)}) collective-permute-start(bf16[128,128]{1,0:T(8,128)(2,1)S(1)} %get-tuple-element.41.refs_1_), channel_id=1, source_target_pairs={{0,3},{1,2},{2,1},{3,0},{4,7},{5,6},{6,5},{7,4},{8,11},{9,10},{10,... | collective-permute-start | bytes 98312 | tf_op jit(solution)/shard_map/ppermute | solution.py:210
  4.4 4.0 %collective-permute-start.2 = (bf16[128,128]{1,0:T(8,128)(2,1)S(1)}, bf16[128,128]{1,0:T(8,128)(2,1)S(1)}, u32[]{:S(2)}, u32[]{:S(2)}) collective-permute-start(bf16[128,128]{1,0:T(8,128)(2,1)S(1)} %get-tuple-element.41.refs_1_), channel_id=1, source_target_pairs={{0,2},{1,3},{2,0},{3,1},{4,6},{5,7},{6,4},{7,5},{8,10},{9,11},{10,... | collective-permute-start | bytes 98312 | tf_op jit(solution)/shard_map/ppermute | solution.py:210
  5.0 3.4 %collective-permute-start.1 = (bf16[128,128]{1,0:T(8,128)(2,1)S(1)}, bf16[128,128]{1,0:T(8,128)(2,1)S(1)}, u32[]{:S(2)}, u32[]{:S(2)}) collective-permute-start(bf16[128,128]{1,0:T(8,128)(2,1)S(1)} %get-tuple-element.41.refs_1_), channel_id=1, source_target_pairs={{0,1},{1,0},{2,3},{3,2},{4,5},{5,4},{6,7},{7,6},{8,9},{9,8},{10,11... | collective-permute-start | bytes 98312 | tf_op jit(solution)/shard_map/ppermute | solution.py:210
  5.0 5.2 %collective-permute-start = (bf16[128,128]{1,0:T(8,128)(2,1)S(1)}, bf16[128,128]{1,0:T(8,128)(2,1)S(1)}, u32[]{:S(2)}, u32[]{:S(2)}) collective-permute-start(bf16[128,128]{1,0:T(8,128)(2,1)S(1)} %get-tuple-element.40.refs_0_), channel_id=1, source_target_pairs={{0,4},{4,0},{8,12},{12,8},{16,20},{20,16},{24,28},{28,24},{1,5},{5... | collective-permute-start | bytes 98312 | tf_op jit(solution)/shard_map/ppermute | solution.py:210
  8.7 6.6 %collective-permute-start.11 = (f32[2,128,128]{2,1,0:T(8,128)S(1)}, f32[2,128,128]{2,1,0:T(8,128)S(1)}, u32[]{:S(2)}, u32[]{:S(2)}) collective-permute-start(f32[2,128,128]{2,1,0:T(8,128)S(1)} %get-tuple-element.49), channel_id=1, source_target_pairs={{0,4},{4,0},{8,12},{12,8},{16,20},{20,16},{24,28},{28,24},{1,5},{5... | collective-permute-start | bytes 393224 | tf_op jit(solution)/shard_map/ppermute | solution.py:210
  10.2 10.4 %collective-permute-start.6 = (bf16[2,128,128]{2,1,0:T(8,128)(2,1)S(1)}, bf16[2,128,128]{2,1,0:T(8,128)(2,1)S(1)}, u32[]{:S(2)}, u32[]{:S(2)}) collective-permute-start(bf16[2,128,128]{2,1,0:T(8,128)(2,1)S(1)} %pair_one_early.1.refs_1_), channel_id=1, source_target_pairs={{0,24},{4,28},{8,16},{12,20},{16,8},{20,12},{24,0},{28,4},{1,25},{... | collective-permute-start | bytes 196616 | tf_op jit(solution)/shard_map/ppermute | solution.py:210
  13.9 5.0 %collective-permute-start.14 = (f32[2,128,128]{2,1,0:T(8,128)S(1)}, f32[2,128,128]{2,1,0:T(8,128)S(1)}, u32[]{:S(2)}, u32[]{:S(2)}) collective-permute-start(f32[2,128,128]{2,1,0:T(8,128)S(1)} %get-tuple-element.42.refs_2_), channel_id=1, source_target_pairs={{0,4},{4,0},{8,12},{12,8},{16,20},{20,16},{24,28},{28,24},{1,5},{5... | collective-permute-start | bytes 393224 | tf_op jit(solution)/shard_map/ppermute | solution.py:210
  14.6 6.6 %collective-permute-start.5 = (bf16[2,128,128]{2,1,0:T(8,128)(2,1)S(1)}, bf16[2,128,128]{2,1,0:T(8,128)(2,1)S(1)}, u32[]{:S(2)}, u32[]{:S(2)}) collective-permute-start(bf16[2,128,128]{2,1,0:T(8,128)(2,1)S(1)} %pair_one_late.1), channel_id=1, source_target_pairs={{0,16},{4,20},{8,24},{12,28},{16,0},{20,4},{24,8},{28,12},{1,17},{... | collective-permute-start | bytes 196616 | tf_op jit(solution)/shard_map/ppermute | solution.py:210
  14.6 6.6 %collective-permute-start.4 = (bf16[2,128,128]{2,1,0:T(8,128)(2,1)S(1)}, bf16[2,128,128]{2,1,0:T(8,128)(2,1)S(1)}, u32[]{:S(2)}, u32[]{:S(2)}) collective-permute-start(bf16[2,128,128]{2,1,0:T(8,128)(2,1)S(1)} %pair_one_late.1), channel_id=1, source_target_pairs={{0,8},{4,12},{8,0},{12,4},{16,24},{20,28},{24,16},{28,20},{1,9},{5... | collective-permute-start | bytes 196616 | tf_op jit(solution)/shard_map/ppermute | solution.py:210
  15.3 8.3 %collective-permute-start.12 = (f32[128,128]{1,0:T(8,128)S(1)}, f32[128,128]{1,0:T(8,128)S(1)}, u32[]{:S(2)}, u32[]{:S(2)}) collective-permute-start(f32[128,128]{1,0:T(8,128)S(1)} %get-tuple-element.50), channel_id=1, source_target_pairs={{0,16},{4,20},{8,24},{12,28},{16,0},{20,4},{24,8},{28,12},{1,17},{... | collective-permute-start | bytes 196616 | tf_op jit(solution)/shard_map/ppermute | solution.py:210
  18.9 6.1 %collective-permute-start.13 = (f32[128,128]{1,0:T(8,128)S(1)}, f32[128,128]{1,0:T(8,128)S(1)}, u32[]{:S(2)}, u32[]{:S(2)}) collective-permute-start(f32[128,128]{1,0:T(8,128)S(1)} %get-tuple-element.51), channel_id=1, source_target_pairs={{0,24},{4,28},{8,16},{12,20},{16,8},{20,12},{24,0},{28,4},{1,25},{... | collective-permute-start | bytes 196616 | tf_op jit(solution)/shard_map/ppermute | solution.py:210
  20.7 5.0 %collective-permute-start.15 = (f32[128,128]{1,0:T(8,128)S(1)}, f32[128,128]{1,0:T(8,128)S(1)}, u32[]{:S(2)}, u32[]{:S(2)}) collective-permute-start(f32[128,128]{1,0:T(8,128)S(1)} %get-tuple-element.54), channel_id=1, source_target_pairs={{0,8},{4,12},{8,0},{12,4},{16,24},{20,28},{24,16},{28,20},{1,9},{5... | collective-permute-start | bytes 196616 | tf_op jit(solution)/shard_map/ppermute | solution.py:210
  21.7 5.2 %collective-permute-start.7 = (f32[128,128]{1,0:T(8,128)S(1)}, f32[128,128]{1,0:T(8,128)S(1)}, u32[]{:S(2)}, u32[]{:S(2)}) collective-permute-start(f32[128,128]{1,0:T(8,128)S(1)} %get-tuple-element.44), channel_id=1, source_target_pairs={{0,1},{1,0},{2,3},{3,2},{4,5},{5,4},{6,7},{7,6},{8,9},{9,8},{10,11... | collective-permute-start | bytes 196616 | tf_op jit(solution)/shard_map/ppermute | solution.py:210
  21.8 5.8 %collective-permute-start.8 = (f32[128,128]{1,0:T(8,128)S(1)}, f32[128,128]{1,0:T(8,128)S(1)}, u32[]{:S(2)}, u32[]{:S(2)}) collective-permute-start(f32[128,128]{1,0:T(8,128)S(1)} %get-tuple-element.45), channel_id=1, source_target_pairs={{0,2},{1,3},{2,0},{3,1},{4,6},{5,7},{6,4},{7,5},{8,10},{9,11},{10,... | collective-permute-start | bytes 196616 | tf_op jit(solution)/shard_map/ppermute | solution.py:210
  23.6 4.3 %collective-permute-start.9 = (f32[128,128]{1,0:T(8,128)S(1)}, f32[128,128]{1,0:T(8,128)S(1)}, u32[]{:S(2)}, u32[]{:S(2)}) collective-permute-start(f32[128,128]{1,0:T(8,128)S(1)} %get-tuple-element.46.refs_5_), channel_id=1, source_target_pairs={{0,3},{1,2},{2,1},{3,0},{4,7},{5,6},{6,5},{7,4},{8,11},{9,10},{10,... | collective-permute-start | bytes 196616 | tf_op jit(solution)/shard_map/ppermute | solution.py:210
  25.7 3.5 %collective-permute-start.18 = (bf16[128,128]{1,0:T(8,128)(2,1)S(1)}, bf16[128,128]{1,0:T(8,128)(2,1)S(1)}, u32[]{:S(2)}, u32[]{:S(2)}) collective-permute-start(bf16[128,128]{1,0:T(8,128)(2,1)S(1)} %get-tuple-element.55.refs_1_.refs_2_), channel_id=1, source_target_pairs={{0,3},{1,2},{2,1},{3,0},{4,7},{5,6},{6,5},{7,4},{8,11},{9,10},{10,... | collective-permute-start | bytes 98312 | tf_op jit(solution)/shard_map/ppermute | solution.py:210
  25.7 4.2 %collective-permute-start.17 = (bf16[128,128]{1,0:T(8,128)(2,1)S(1)}, bf16[128,128]{1,0:T(8,128)(2,1)S(1)}, u32[]{:S(2)}, u32[]{:S(2)}) collective-permute-start(bf16[128,128]{1,0:T(8,128)(2,1)S(1)} %get-tuple-element.55.refs_1_.refs_2_), channel_id=1, source_target_pairs={{0,2},{1,3},{2,0},{3,1},{4,6},{5,7},{6,4},{7,5},{8,10},{9,11},{10,... | collective-permute-start | bytes 98312 | tf_op jit(solution)/shard_map/ppermute | solution.py:210
  26.9 3.0 %collective-permute-start.16 = (bf16[128,128]{1,0:T(8,128)(2,1)S(1)}, bf16[128,128]{1,0:T(8,128)(2,1)S(1)}, u32[]{:S(2)}, u32[]{:S(2)}) collective-permute-start(bf16[128,128]{1,0:T(8,128)(2,1)S(1)} %get-tuple-element.55.refs_1_.refs_2_), channel_id=1, source_target_pairs={{0,1},{1,0},{2,3},{3,2},{4,5},{5,4},{6,7},{7,6},{8,9},{9,8},{10,11... | collective-permute-start | bytes 98312 | tf_op jit(solution)/shard_map/ppermute | solution.py:210
  27.9 4.0 %collective-permute-start.10 = (bf16[128,128]{1,0:T(8,128)(2,1)S(1)}, bf16[128,128]{1,0:T(8,128)(2,1)S(1)}, u32[]{:S(2)}, u32[]{:S(2)}) collective-permute-start(bf16[128,128]{1,0:T(8,128)(2,1)S(1)} %forward_middle.1.refs_0_), channel_id=1, source_target_pairs={{0,4},{4,0},{8,12},{12,8},{16,20},{20,16},{24,28},{28,24},{1,5},{5... | collective-permute-start | bytes 98312 | tf_op jit(solution)/shard_map/ppermute | solution.py:210
  30.2 7.2 %collective-permute-start.22 = (bf16[2,128,128]{2,1,0:T(8,128)(2,1)S(1)}, bf16[2,128,128]{2,1,0:T(8,128)(2,1)S(1)}, u32[]{:S(2)}, u32[]{:S(2)}) collective-permute-start(bf16[2,128,128]{2,1,0:T(8,128)(2,1)S(1)} %get-tuple-element.58), channel_id=1, source_target_pairs={{0,4},{4,0},{8,12},{12,8},{16,20},{20,16},{24,28},{28,24},{1,5},{5... | collective-permute-start | bytes 196616 | tf_op jit(solution)/shard_map/ppermute | solution.py:210
  31.9 8.7 %collective-permute-start.20 = (bf16[2,128,128]{2,1,0:T(8,128)(2,1)S(1)}, bf16[2,128,128]{2,1,0:T(8,128)(2,1)S(1)}, u32[]{:S(2)}, u32[]{:S(2)}) collective-permute-start(bf16[2,128,128]{2,1,0:T(8,128)(2,1)S(1)} %pair_two_late.1), channel_id=1, source_target_pairs={{0,16},{4,20},{8,24},{12,28},{16,0},{20,4},{24,8},{28,12},{1,17},{... | collective-permute-start | bytes 196616 | tf_op jit(solution)/shard_map/ppermute | solution.py:210
  33.4 7.8 %collective-permute-start.19 = (bf16[2,128,128]{2,1,0:T(8,128)(2,1)S(1)}, bf16[2,128,128]{2,1,0:T(8,128)(2,1)S(1)}, u32[]{:S(2)}, u32[]{:S(2)}) collective-permute-start(bf16[2,128,128]{2,1,0:T(8,128)(2,1)S(1)} %pair_two_late.1), channel_id=1, source_target_pairs={{0,8},{4,12},{8,0},{12,4},{16,24},{20,28},{24,16},{28,20},{1,9},{5... | collective-permute-start | bytes 196616 | tf_op jit(solution)/shard_map/ppermute | solution.py:210
  36.1 4.3 %collective-permute-start.23 = (bf16[2,128,128]{2,1,0:T(8,128)(2,1)S(1)}, bf16[2,128,128]{2,1,0:T(8,128)(2,1)S(1)}, u32[]{:S(2)}, u32[]{:S(2)}) collective-permute-start(bf16[2,128,128]{2,1,0:T(8,128)(2,1)S(1)} %get-tuple-element.56.refs_3_), channel_id=1, source_target_pairs={{0,4},{4,0},{8,12},{12,8},{16,20},{20,16},{24,28},{28,24},{1,5},{5... | collective-permute-start | bytes 196616 | tf_op jit(solution)/shard_map/ppermute | solution.py:210
  36.1 6.4 %collective-permute-start.21 = (bf16[2,128,128]{2,1,0:T(8,128)(2,1)S(1)}, bf16[2,128,128]{2,1,0:T(8,128)(2,1)S(1)}, u32[]{:S(2)}, u32[]{:S(2)}) collective-permute-start(bf16[2,128,128]{2,1,0:T(8,128)(2,1)S(1)} %pair_two_early.1.refs_1_), channel_id=1, source_target_pairs={{0,24},{4,28},{8,16},{12,20},{16,8},{20,12},{24,0},{28,4},{1,25},{... | collective-permute-start | bytes 196616 | tf_op jit(solution)/shard_map/ppermute | solution.py:210
  37.5 6.1 %collective-permute-start.27 = (bf16[128,128]{1,0:T(8,128)(2,1)S(1)}, bf16[128,128]{1,0:T(8,128)(2,1)S(1)}, u32[]{:S(2)}, u32[]{:S(2)}) collective-permute-start(bf16[128,128]{1,0:T(8,128)(2,1)S(1)} %get-tuple-element.68), channel_id=1, source_target_pairs={{0,16},{4,20},{8,24},{12,28},{16,0},{20,4},{24,8},{28,12},{1,17},{... | collective-permute-start | bytes 98312 | tf_op jit(solution)/shard_map/ppermute | solution.py:210
  40.4 5.7 %collective-permute-start.28 = (bf16[128,128]{1,0:T(8,128)(2,1)S(1)}, bf16[128,128]{1,0:T(8,128)(2,1)S(1)}, u32[]{:S(2)}, u32[]{:S(2)}) collective-permute-start(bf16[128,128]{1,0:T(8,128)(2,1)S(1)} %get-tuple-element.59.refs_5_), channel_id=1, source_target_pairs={{0,24},{4,28},{8,16},{12,20},{16,8},{20,12},{24,0},{28,4},{1,25},{... | collective-permute-start | bytes 98312 | tf_op jit(solution)/shard_map/ppermute | solution.py:210
  40.5 5.6 %collective-permute-start.29 = (bf16[128,128]{1,0:T(8,128)(2,1)S(1)}, bf16[128,128]{1,0:T(8,128)(2,1)S(1)}, u32[]{:S(2)}, u32[]{:S(2)}) collective-permute-start(bf16[128,128]{1,0:T(8,128)(2,1)S(1)} %get-tuple-element.61.refs_6_), channel_id=1, source_target_pairs={{0,8},{4,12},{8,0},{12,4},{16,24},{20,28},{24,16},{28,20},{1,9},{5... | collective-permute-start | bytes 98312 | tf_op jit(solution)/shard_map/ppermute | solution.py:210
  43.0 3.8 %collective-permute-start.24 = (bf16[128,128]{1,0:T(8,128)(2,1)S(1)}, bf16[128,128]{1,0:T(8,128)(2,1)S(1)}, u32[]{:S(2)}, u32[]{:S(2)}) collective-permute-start(bf16[128,128]{1,0:T(8,128)(2,1)S(1)} %get-tuple-element.63), channel_id=1, source_target_pairs={{0,1},{1,0},{2,3},{3,2},{4,5},{5,4},{6,7},{7,6},{8,9},{9,8},{10,11... | collective-permute-start | bytes 98312 | tf_op jit(solution)/shard_map/ppermute | solution.py:210
  43.1 4.2 %collective-permute-start.25 = (bf16[128,128]{1,0:T(8,128)(2,1)S(1)}, bf16[128,128]{1,0:T(8,128)(2,1)S(1)}, u32[]{:S(2)}, u32[]{:S(2)}) collective-permute-start(bf16[128,128]{1,0:T(8,128)(2,1)S(1)} %get-tuple-element.64), channel_id=1, source_target_pairs={{0,2},{1,3},{2,0},{3,1},{4,6},{5,7},{6,4},{7,5},{8,10},{9,11},{10,... | collective-permute-start | bytes 98312 | tf_op jit(solution)/shard_map/ppermute | solution.py:210
  43.5 3.7 %collective-permute-start.26 = (bf16[128,128]{1,0:T(8,128)(2,1)S(1)}, bf16[128,128]{1,0:T(8,128)(2,1)S(1)}, u32[]{:S(2)}, u32[]{:S(2)}) collective-permute-start(bf16[128,128]{1,0:T(8,128)(2,1)S(1)} %get-tuple-element.65), channel_id=1, source_target_pairs={{0,3},{1,2},{2,1},{3,0},{4,7},{5,6},{6,5},{7,4},{8,11},{9,10},{10,... | collective-permute-start | bytes 98312 | tf_op jit(solution)/shard_map/ppermute | solution.py:210

commit v15 on v14

--- a/solution.py
+++ b/solution.py
@@ -117,18 +117,16 @@
 
 def adjoint_body(n_rows, n_cols, dense_ref, *refs):
     blocks, outs = refs[:n_cols], refs[n_cols:]
-    keep_far, keep_near, send_far, send_near = outs
+    chunks = list(zip(outs[: len(outs) // 2], outs[len(outs) // 2 :]))
+    places = [(keep, send, at) for keep, send in reversed(chunks) for at in range(keep.shape[0])]
     half = n_rows // 2
-    near = send_near.shape[0]
     size = blocks[0].shape[1]
     left = jnp.concatenate([b[...] for b in blocks], axis=1)
     for zz in reversed(range(half)):
         part = jnp.dot(
             left, dense_ref[:, 2 * zz * size : (2 * zz + 2) * size], preferred_element_type=F32
         )
-        keep, send, at = (
-            (keep_near, send_near, zz) if zz < near else (keep_far, send_far, zz - near)
-        )
+        keep, send, at = places[zz]
         keep[at] = part[:, :size]
         send[at] = part[:, size:].astype(send.dtype)
 
@@ -185,7 +183,7 @@
 
 AFTER = {
     "pair_one_late": ("adjoint_one",),
-    "forward_two": ("far_two", "near_two"),
+    "forward_two": ("sums_two",),
     "forward_end": ("adjoint_end",),
     "pair_two_early": ("adjoint_middle", "adjoint_two"),
     "pair_one_early": ("dense",),
@@ -194,9 +192,8 @@
 COST = {
     "pair_one_late": 1000,
     "adjoint_middle": 1000,
-    "near_two": 200,
     "pair_two_early": 200,
-    "far_two": 1000,
+    "sums_two": 1000,
     "far_one": 500,
     "forward_end": 1000,
     "pair_two_late": 1000,
@@ -282,11 +279,11 @@
     def swap_cols(parts):
         return [parts[0]] + [send(parts[s], "cols", n_cols, s) for s in range(1, n_cols)]
 
-    def adjoint(name, part, kind):
+    def adjoint(name, part, kind, counts):
         return run(
             name,
             lambda *refs: adjoint_body(n_rows, n_cols, *refs),
-            [shape(F32, half - near), shape(F32, near), shape(kind, half - near), shape(kind, near)],
+            [shape(F32, count) for count in counts] + [shape(kind, count) for count in counts],
             [get("dense")[0], *spread(part, "cols", n_cols, 1)],
             flops=hop_flops,
         )
@@ -310,25 +307,25 @@
         got = send(sent, "rows", n_rows, 1)
         return run(name, add_body, [shape(kind) for kind in kinds], [kept, got])
 
-    def row_parts(far, close):
-        parts = [send(far[s - near], "rows", n_rows, 2 * s) for s in range(near, half)]
-        return parts + [close[0]] + [send(close[s], "rows", n_rows, 2 * s) for s in range(1, near)]
-
-    far_kinds = lambda kind: [kind] * (half - near)
-    near_kinds = lambda kind: [F32] + [kind] * (near - 1)
+    def row_parts(parts):
+        order = [*range(near, half), *range(1, near)]
+        return [send(parts[s], "rows", n_rows, 2 * s) for s in order] + [parts[0]]
+
     makers.update(
         start=start,
         dense=dense,
-        adjoint_one=lambda: adjoint("adjoint_one", get("start")[0], F32),
+        adjoint_one=lambda: adjoint(
+            "adjoint_one", get("start")[0], F32, [half - near, near]
+        ),
         other_one=lambda: send(get("start")[1], "rows", n_rows, 1),
         other_two=lambda: send(get("forward_middle")[0], "rows", n_rows, 1),
         pair_one_early=lambda: pair("pair_one_early", get("start")[1], get("other_one")),
         pair_one_late=lambda: pair("pair_one_late", get("start")[1], get("other_one")),
         far_one=lambda: sums(
-            "far_one", get("adjoint_one")[0], get("adjoint_one")[2], far_kinds(F32)
+            "far_one", get("adjoint_one")[0], get("adjoint_one")[2], [F32] * (half - near)
         ),
         near_one=lambda: sums(
-            "near_one", get("adjoint_one")[1], get("adjoint_one")[3], near_kinds(F32)
+            "near_one", get("adjoint_one")[1], get("adjoint_one")[3], [F32] * near
         ),
         forward_one=lambda: forward(
             "forward_one", get("pair_one_early")[0], get("pair_one_late")[0], F32
@@ -337,7 +334,7 @@
             "adjoint_middle",
             adjoint_middle_body,
             [shape(F32), shape(BF16)],
-            [get("start")[2], *row_parts(get("far_one"), get("near_one"))],
+            [get("start")[2], *row_parts([*get("near_one"), *get("far_one")])],
         ),
         forward_middle=lambda: run(
             "forward_middle",
@@ -345,14 +342,13 @@
             [shape(BF16)],
             [get("start")[4], get("start")[3], *swap_cols(get("forward_one"))],
         ),
-        adjoint_two=lambda: adjoint("adjoint_two", get("adjoint_middle")[1], BF16),
+        adjoint_two=lambda: adjoint(
+            "adjoint_two", get("adjoint_middle")[1], BF16, [half]
+        ),
         pair_two_early=lambda: pair("pair_two_early", get("forward_middle")[0], get("other_two")),
         pair_two_late=lambda: pair("pair_two_late", get("forward_middle")[0], get("other_two")),
-        far_two=lambda: sums(
-            "far_two", get("adjoint_two")[0], get("adjoint_two")[2], far_kinds(BF16)
-        ),
-        near_two=lambda: sums(
-            "near_two", get("adjoint_two")[1], get("adjoint_two")[3], near_kinds(BF16)
+        sums_two=lambda: sums(
+            "sums_two", get("adjoint_two")[0], get("adjoint_two")[1], [F32] + [BF16] * (half - 1)
         ),
         forward_two=lambda: forward(
             "forward_two", get("pair_two_early")[0], get("pair_two_late")[0], BF16
@@ -371,7 +367,7 @@
                 get("start")[5],
                 get("adjoint_middle")[0],
                 get("start")[2],
-                *row_parts(get("far_two"), get("near_two")),
+                *row_parts(get("sums_two")),
             ],
         ),
     )

time: 48.3 us -> 48.8 us (1.010)
  starting transfers between devices: 29.8 us -> 33.3 us
  waiting for transfers between devices: 11.5 us -> 8.68 us
    ppermute x30 -> x29, starting transfers between devices: 29.8 us -> 33.3 us  [send(): return lax.ppermute(value, axis, [(i, i ^ step) for i in range(count)])]
    ppermute x30 -> x29, waiting for transfers between devices: 11.5 us -> 8.68 us  [send(): return lax.ppermute(value, axis, [(i, i ^ step) for i in range(count)])]
    pallas_call x18 -> x17, Pallas kernels: 5.16 us -> 5.3 us  [call(): pl.pallas_call(ordered, out_shape=outs, in_specs=[*in_specs, *[pl.BlockSp...]
  transfers between devices with their start and end apart: 30 -> 29, of which waited for: 12 -> 11; matrix products, arithmetic and copies ran while one was open for 0% -> 0% of each run, Pallas kernels for 7% -> 7%
where the time goes in v15:
time: 48.8 us; the launch traced here: 48.7 us
  starting transfers between devices  33.3 us (68%)
  waiting for transfers between devices  8.68 us (18%)
  Pallas kernels  5.3 us (11%)
  between operations  1.44 us (3%)
    ppermute x29, starting transfers between devices, send(): return lax.ppermute(value, axis, [(i, i ^ step) for i in range(count)])  33.3 us
    ppermute x29, waiting for transfers between devices, send(): return lax.ppermute(value, axis, [(i, i ^ step) for i in range(count)])  8.68 us
    pallas_call x17, Pallas kernels, call(): pl.pallas_call(ordered, out_shape=outs, in_specs=[*in_specs, *[pl.BlockSp...  5.3 us
  transfers between devices with their start and end apart: 29, of which 11 were waited for; matrix products, arithmetic and copies ran while one was open for 0% of the time, Pallas kernels for 7%

profile of v15, /device:TPU:0, one launch (start us, length us, event | category | flops | bytes accessed | tf_op | source)
XLA Modules:
  0.0 48.7 jit_solution(3762262971541565497)
XLA Ops:
  0.6 1.3 %start.1 = (bf16[128,128]{1,0:T(8,128)(2,1)S(1)}, bf16[128,128]{1,0:T(8,128)(2,1)S(1)}, f32[1,128]{1,0:T(1,128)S(1)}, f32[128,128]{1,0:T(8,128)S(1)}, f32[128,12...) custom-call(s32[1,128]{1,0:T(1,128)} %bitcast.1, f32[8]{0:T(128)} %refs_1_.2, ...), custom_call_target="tpu_custom_call" | custom-call | bytes 1967136 | tf_op jit(solution)/shard_map/start/pallas_call | solution.py:36
  1.9 2.4 %collective-permute-start.3 = (bf16[128,128]{1,0:T(8,128)(2,1)S(1)}, bf16[128,128]{1,0:T(8,128)(2,1)S(1)}, u32[]{:S(2)}, u32[]{:S(2)}) collective-permute-start(bf16[128,128]{1,0:T(8,128)(2,1)S(1)} %get-tuple-element.39.refs_1_), channel_id=1, source_target_pairs={{0,3},{1,2},{2,1},{3,0},{4,7},{5,6},{6,5},{7,4},{8,11},{9,10},{10,... | collective-permute-start | bytes 98312 | tf_op jit(solution)/shard_map/ppermute | solution.py:207
  4.4 0.6 %collective-permute-start.2 = (bf16[128,128]{1,0:T(8,128)(2,1)S(1)}, bf16[128,128]{1,0:T(8,128)(2,1)S(1)}, u32[]{:S(2)}, u32[]{:S(2)}) collective-permute-start(bf16[128,128]{1,0:T(8,128)(2,1)S(1)} %get-tuple-element.39.refs_1_), channel_id=1, source_target_pairs={{0,2},{1,3},{2,0},{3,1},{4,6},{5,7},{6,4},{7,5},{8,10},{9,11},{10,... | collective-permute-start | bytes 98312 | tf_op jit(solution)/shard_map/ppermute | solution.py:207
  5.0 0.0 collective-permute-start.1
  5.0 1.8 %collective-permute-start = (bf16[128,128]{1,0:T(8,128)(2,1)S(1)}, bf16[128,128]{1,0:T(8,128)(2,1)S(1)}, u32[]{:S(2)}, u32[]{:S(2)}) collective-permute-start(bf16[128,128]{1,0:T(8,128)(2,1)S(1)} %get-tuple-element.38.refs_0_), channel_id=1, source_target_pairs={{0,4},{4,0},{8,12},{12,8},{16,20},{20,16},{24,28},{28,24},{1,5},{5... | collective-permute-start | bytes 98312 | tf_op jit(solution)/shard_map/ppermute | solution.py:207
  7.5 1.0 %dense.1.refs_2_.refs_0_ = bf16[512,1024]{1,0:T(8,128)(2,1)S(1)} custom-call(bf16[1,1,24,128,128]{4,3,2,1,0:T(8,128)(2,1)S(1)} %get-tuple-element.37.refs_0_, s32[1,1,24]{2,1,0:T(1,128)} %refs_1_.3, s32[1,1,24]{2,1,0:T(1,128)} %refs_2_.3, s32[1,1]{1,0:T(1,128)S(6)} %copy.10.refs_3_), custom_call_target="tpu_custom_call" | custom-call | bytes 1835204 | tf_op jit(solution)/shard_map/dense/pallas_call | solution.py:36
  8.5 0.0 collective-permute-done.3.refs_4_
  8.5 0.3 adjoint_one.1
  8.8 1.4 %collective-permute-start.11 = (f32[2,128,128]{2,1,0:T(8,128)S(1)}, f32[2,128,128]{2,1,0:T(8,128)S(1)}, u32[]{:S(2)}, u32[]{:S(2)}) collective-permute-start(f32[2,128,128]{2,1,0:T(8,128)S(1)} %get-tuple-element.47), channel_id=1, source_target_pairs={{0,4},{4,0},{8,12},{12,8},{16,20},{20,16},{24,28},{28,24},{1,5},{5... | collective-permute-start | bytes 393224 | tf_op jit(solution)/shard_map/ppermute | solution.py:207
  10.2 3.7 %collective-permute-start.6 = (bf16[2,128,128]{2,1,0:T(8,128)(2,1)S(1)}, bf16[2,128,128]{2,1,0:T(8,128)(2,1)S(1)}, u32[]{:S(2)}, u32[]{:S(2)}) collective-permute-start(bf16[2,128,128]{2,1,0:T(8,128)(2,1)S(1)} %pair_one_early.1.refs_1_), channel_id=1, source_target_pairs={{0,24},{4,28},{8,16},{12,20},{16,8},{20,12},{24,0},{28,4},{1,25},{... | collective-permute-start | bytes 196616 | tf_op jit(solution)/shard_map/ppermute | solution.py:207
  13.9 0.5 %collective-permute-start.14 = (f32[2,128,128]{2,1,0:T(8,128)S(1)}, f32[2,128,128]{2,1,0:T(8,128)S(1)}, u32[]{:S(2)}, u32[]{:S(2)}) collective-permute-start(f32[2,128,128]{2,1,0:T(8,128)S(1)} %get-tuple-element.40.refs_2_), channel_id=1, source_target_pairs={{0,4},{4,0},{8,12},{12,8},{16,20},{20,16},{24,28},{28,24},{1,5},{5... | collective-permute-start | bytes 393224 | tf_op jit(solution)/shard_map/ppermute | solution.py:207
  14.4 1.0 %collective-permute-start.4 = (bf16[2,128,128]{2,1,0:T(8,128)(2,1)S(1)}, bf16[2,128,128]{2,1,0:T(8,128)(2,1)S(1)}, u32[]{:S(2)}, u32[]{:S(2)}) collective-permute-start(bf16[2,128,128]{2,1,0:T(8,128)(2,1)S(1)} %pair_one_late.1), channel_id=1, source_target_pairs={{0,8},{4,12},{8,0},{12,4},{16,24},{20,28},{24,16},{28,20},{1,9},{5... | collective-permute-start | bytes 196616 | tf_op jit(solution)/shard_map/ppermute | solution.py:207
  15.4 2.3 %collective-permute-start.12 = (f32[128,128]{1,0:T(8,128)S(1)}, f32[128,128]{1,0:T(8,128)S(1)}, u32[]{:S(2)}, u32[]{:S(2)}) collective-permute-start(f32[128,128]{1,0:T(8,128)S(1)} %get-tuple-element.48), channel_id=1, source_target_pairs={{0,16},{4,20},{8,24},{12,28},{16,0},{20,4},{24,8},{28,12},{1,17},{... | collective-permute-start | bytes 196616 | tf_op jit(solution)/shard_map/ppermute | solution.py:207
  17.8 1.1 %collective-permute-done.14.refs_1_ = f32[2,128,128]{2,1,0:T(8,128)S(1)} collective-permute-done((f32[2,128,128]{2,1,0:T(8,128)S(1)}, f32[2,128,128]{2,1,0:T(8,128)S(1)}, u32[]{:S(2)}, u32[]{:S(2)}) %collective-permute-start.14) | collective-permute-done | bytes 131104 | tf_op jit(solution)/shard_map/ppermute | solution.py:207
  18.9 1.6 %collective-permute-start.13 = (f32[128,128]{1,0:T(8,128)S(1)}, f32[128,128]{1,0:T(8,128)S(1)}, u32[]{:S(2)}, u32[]{:S(2)}) collective-permute-start(f32[128,128]{1,0:T(8,128)S(1)} %get-tuple-element.49), channel_id=1, source_target_pairs={{0,24},{4,28},{8,16},{12,20},{16,8},{20,12},{24,0},{28,4},{1,25},{... | collective-permute-start | bytes 196616 | tf_op jit(solution)/shard_map/ppermute | solution.py:207
  20.5 0.1 collective-permute-start.15
  20.6 0.5 %collective-permute-done.5.refs_3_ = bf16[2,128,128]{2,1,0:T(8,128)(2,1)S(1)} collective-permute-done((bf16[2,128,128]{2,1,0:T(8,128)(2,1)S(1)}, bf16[2,128,128]{2,1,0:T(8,128)(2,1)S(1)}, u32[]{:S(2)}, u32[]{:S(2)}) %collective-permute-start.5) | collective-permute-done | bytes 65568 | tf_op jit(solution)/shard_map/ppermute | solution.py:207
  21.1 0.4 forward_one.1
  21.6 0.1 collective-permute-start.7
  21.6 1.4 %collective-permute-start.8 = (f32[128,128]{1,0:T(8,128)S(1)}, f32[128,128]{1,0:T(8,128)S(1)}, u32[]{:S(2)}, u32[]{:S(2)}) collective-permute-start(f32[128,128]{1,0:T(8,128)S(1)} %get-tuple-element.43), channel_id=1, source_target_pairs={{0,2},{1,3},{2,0},{3,1},{4,6},{5,7},{6,4},{7,5},{8,10},{9,11},{10,... | collective-permute-start | bytes 196616 | tf_op jit(solution)/shard_map/ppermute | solution.py:207
  23.1 0.4 collective-permute-done.12.refs_1_
  23.5 0.0 collective-permute-start.9
  23.5 1.5 %collective-permute-done.13.refs_2_ = f32[128,128]{1,0:T(8,128)S(1)} collective-permute-done((f32[128,128]{1,0:T(8,128)S(1)}, f32[128,128]{1,0:T(8,128)S(1)}, u32[]{:S(2)}, u32[]{:S(2)}) %collective-permute-start.13) | collective-permute-done | bytes 65568 | tf_op jit(solution)/shard_map/ppermute | solution.py:207
  25.1 0.5 %collective-permute-done.15.refs_3_ = f32[128,128]{1,0:T(8,128)S(1)} collective-permute-done((f32[128,128]{1,0:T(8,128)S(1)}, f32[128,128]{1,0:T(8,128)S(1)}, u32[]{:S(2)}, u32[]{:S(2)}) %collective-permute-start.15) | collective-permute-done | bytes 65568 | tf_op jit(solution)/shard_map/ppermute | solution.py:207
  25.6 0.1 collective-permute-start.18
  25.7 1.2 %collective-permute-start.17 = (bf16[128,128]{1,0:T(8,128)(2,1)S(1)}, bf16[128,128]{1,0:T(8,128)(2,1)S(1)}, u32[]{:S(2)}, u32[]{:S(2)}) collective-permute-start(bf16[128,128]{1,0:T(8,128)(2,1)S(1)} %get-tuple-element.53.refs_1_.refs_2_), channel_id=1, source_target_pairs={{0,2},{1,3},{2,0},{3,1},{4,6},{5,7},{6,4},{7,5},{8,10},{9,11},{10,... | collective-permute-start | bytes 98312 | tf_op jit(solution)/shard_map/ppermute | solution.py:207
  26.9 0.6 %collective-permute-start.16 = (bf16[128,128]{1,0:T(8,128)(2,1)S(1)}, bf16[128,128]{1,0:T(8,128)(2,1)S(1)}, u32[]{:S(2)}, u32[]{:S(2)}) collective-permute-start(bf16[128,128]{1,0:T(8,128)(2,1)S(1)} %get-tuple-element.53.refs_1_.refs_2_), channel_id=1, source_target_pairs={{0,1},{1,0},{2,3},{3,2},{4,5},{5,4},{6,7},{7,6},{8,9},{9,8},{10,11... | collective-permute-start | bytes 98312 | tf_op jit(solution)/shard_map/ppermute | solution.py:207
  27.5 0.3 collective-permute-done.9.refs_5_
  27.8 1.3 %collective-permute-start.10 = (bf16[128,128]{1,0:T(8,128)(2,1)S(1)}, bf16[128,128]{1,0:T(8,128)(2,1)S(1)}, u32[]{:S(2)}, u32[]{:S(2)}) collective-permute-start(bf16[128,128]{1,0:T(8,128)(2,1)S(1)} %forward_middle.1.refs_0_), channel_id=1, source_target_pairs={{0,4},{4,0},{8,12},{12,8},{16,20},{20,16},{24,28},{28,24},{1,5},{5... | collective-permute-start | bytes 98312 | tf_op jit(solution)/shard_map/ppermute | solution.py:207
  29.2 0.6 %collective-permute-done.17.refs_3_ = bf16[128,128]{1,0:T(8,128)(2,1)S(1)} collective-permute-done((bf16[128,128]{1,0:T(8,128)(2,1)S(1)}, bf16[128,128]{1,0:T(8,128)(2,1)S(1)}, u32[]{:S(2)}, u32[]{:S(2)}) %collective-permute-start.17) | collective-permute-done | bytes 32800 | tf_op jit(solution)/shard_map/ppermute | solution.py:207
  29.8 0.3 adjoint_two.1
  30.1 0.8 %collective-permute-start.22 = (bf16[4,128,128]{2,1,0:T(8,128)(2,1)S(1)}, bf16[4,128,128]{2,1,0:T(8,128)(2,1)S(1)}, u32[]{:S(2)}, u32[]{:S(2)}) collective-permute-start(bf16[4,128,128]{2,1,0:T(8,128)(2,1)S(1)} %get-tuple-element.54.refs_3_), channel_id=1, source_target_pairs={{0,4},{4,0},{8,12},{12,8},{16,20},{20,16},{24,28},{28,24},{1,5},{5... | collective-permute-start | bytes 393224 | tf_op jit(solution)/shard_map/ppermute | solution.py:207
  30.9 0.9 %collective-permute-done.10.refs_1_ = bf16[128,128]{1,0:T(8,128)(2,1)S(1)} collective-permute-done((bf16[128,128]{1,0:T(8,128)(2,1)S(1)}, bf16[128,128]{1,0:T(8,128)(2,1)S(1)}, u32[]{:S(2)}, u32[]{:S(2)}) %collective-permute-start.10) | collective-permute-done | bytes 32800 | tf_op jit(solution)/shard_map/ppermute | solution.py:207
  31.8 1.6 %collective-permute-start.20 = (bf16[2,128,128]{2,1,0:T(8,128)(2,1)S(1)}, bf16[2,128,128]{2,1,0:T(8,128)(2,1)S(1)}, u32[]{:S(2)}, u32[]{:S(2)}) collective-permute-start(bf16[2,128,128]{2,1,0:T(8,128)(2,1)S(1)} %pair_two_late.1), channel_id=1, source_target_pairs={{0,16},{4,20},{8,24},{12,28},{16,0},{20,4},{24,8},{28,12},{1,17},{... | collective-permute-start | bytes 196616 | tf_op jit(solution)/shard_map/ppermute | solution.py:207
  33.4 2.8 %collective-permute-start.19 = (bf16[2,128,128]{2,1,0:T(8,128)(2,1)S(1)}, bf16[2,128,128]{2,1,0:T(8,128)(2,1)S(1)}, u32[]{:S(2)}, u32[]{:S(2)}) collective-permute-start(bf16[2,128,128]{2,1,0:T(8,128)(2,1)S(1)} %pair_two_late.1), channel_id=1, source_target_pairs={{0,8},{4,12},{8,0},{12,4},{16,24},{20,28},{24,16},{28,20},{1,9},{5... | collective-permute-start | bytes 196616 | tf_op jit(solution)/shard_map/ppermute | solution.py:207
  36.2 0.0 collective-permute-start.21
  36.2 1.6 %collective-permute-start.26 = (bf16[128,128]{1,0:T(8,128)(2,1)S(1)}, bf16[128,128]{1,0:T(8,128)(2,1)S(1)}, u32[]{:S(2)}, u32[]{:S(2)}) collective-permute-start(bf16[128,128]{1,0:T(8,128)(2,1)S(1)} %get-tuple-element.63), channel_id=1, source_target_pairs={{0,16},{4,20},{8,24},{12,28},{16,0},{20,4},{24,8},{28,12},{1,17},{... | collective-permute-start | bytes 98312 | tf_op jit(solution)/shard_map/ppermute | solution.py:207
  37.8 2.9 %collective-permute-start.28 = (bf16[128,128]{1,0:T(8,128)(2,1)S(1)}, bf16[128,128]{1,0:T(8,128)(2,1)S(1)}, u32[]{:S(2)}, u32[]{:S(2)}) collective-permute-start(bf16[128,128]{1,0:T(8,128)(2,1)S(1)} %get-tuple-element.64), channel_id=1, source_target_pairs={{0,8},{4,12},{8,0},{12,4},{16,24},{20,28},{24,16},{28,20},{1,9},{5... | collective-permute-start | bytes 98312 | tf_op jit(solution)/shard_map/ppermute | solution.py:207
  40.7 1.4 %collective-permute-start.27 = (bf16[128,128]{1,0:T(8,128)(2,1)S(1)}, bf16[128,128]{1,0:T(8,128)(2,1)S(1)}, u32[]{:S(2)}, u32[]{:S(2)}) collective-permute-start(bf16[128,128]{1,0:T(8,128)(2,1)S(1)} %get-tuple-element.56.refs_5_), channel_id=1, source_target_pairs={{0,24},{4,28},{8,16},{12,20},{16,8},{20,12},{24,0},{28,4},{1,25},{... | collective-permute-start | bytes 98312 | tf_op jit(solution)/shard_map/ppermute | solution.py:207
  42.1 0.2 collective-permute-done.21.refs_4_
  42.3 0.4 forward_two.1
  42.7 0.1 collective-permute-start.23
  42.8 1.9 %collective-permute-start.24 = (bf16[128,128]{1,0:T(8,128)(2,1)S(1)}, bf16[128,128]{1,0:T(8,128)(2,1)S(1)}, u32[]{:S(2)}, u32[]{:S(2)}) collective-permute-start(bf16[128,128]{1,0:T(8,128)(2,1)S(1)} %get-tuple-element.59), channel_id=1, source_target_pairs={{0,2},{1,3},{2,0},{3,1},{4,6},{5,7},{6,4},{7,5},{8,10},{9,11},{10,... | collective-permute-start | bytes 98312 | tf_op jit(solution)/shard_map/ppermute | solution.py:207
  44.7 0.1 collective-permute-start.25
  44.8 1.6 %collective-permute-done.27.refs_4_ = bf16[128,128]{1,0:T(8,128)(2,1)S(1)} collective-permute-done((bf16[128,128]{1,0:T(8,128)(2,1)S(1)}, bf16[128,128]{1,0:T(8,128)(2,1)S(1)}, u32[]{:S(2)}, u32[]{:S(2)}) %collective-permute-start.27) | collective-permute-done | bytes 32800 | tf_op jit(solution)/shard_map/ppermute | solution.py:207
  46.4 0.7 %adjoint_end.1 = (f32[128,128]{1,0:T(8,128)}, f32[8,128]{1,0:T(8,128)S(1)}) custom-call(f32[128,128]{1,0:T(8,128)S(1)} %get-tuple-element.61.refs_0_, f32[128,128]{1,0:T(8,128)S(1)} %get-tuple-element.62.refs_1_, f32[1,128]{1,0:T(1,128)S(1)} %get-tuple-element.45.refs_0_.refs_2_, bf16[128,128]{1,0:T(8,128)(2,1)S(1)} %collective-permute-done.26.refs_3_, ...), custom_call_target="tpu_custom_call" | custom-call | flops 3000000000 | bytes 365056 | tf_op jit(solution)/shard_map/adjoint_end/pallas_call | solution.py:36
  47.1 0.9 %collective-permute-done.25.refs_5_ = bf16[128,128]{1,0:T(8,128)(2,1)S(1)} collective-permute-done((bf16[128,128]{1,0:T(8,128)(2,1)S(1)}, bf16[128,128]{1,0:T(8,128)(2,1)S(1)}, u32[]{:S(2)}, u32[]{:S(2)}) %collective-permute-start.25) | collective-permute-done | bytes 32800 | tf_op jit(solution)/shard_map/ppermute | solution.py:207
  48.1 0.7 %forward_end.1 = f32[128,128]{1,0:T(8,128)} custom-call(f32[128,128]{1,0:T(8,128)S(1)} %get-tuple-element.35.refs_0_, f32[128,128]{1,0:T(8,128)S(1)} %get-tuple-element.36.refs_1_, bf16[128,128]{1,0:T(8,128)(2,1)S(1)} %get-tuple-element.57.refs_2_, bf16[128,128]{1,0:T(8,128)(2,1)S(1)} %collective-permute-done.23.refs_3_, ...), custom_call_target="tpu_custom_call" | custom-call | flops 1000000000 | bytes 327680 | tf_op jit(solution)/shard_map/forward_end/pallas_call | solution.py:36
  (27 shorter events, 0.2 us)
Async XLA Ops:
  1.9 6.6 %collective-permute-start.3 = (bf16[128,128]{1,0:T(8,128)(2,1)S(1)}, bf16[128,128]{1,0:T(8,128)(2,1)S(1)}, u32[]{:S(2)}, u32[]{:S(2)}) collective-permute-start(bf16[128,128]{1,0:T(8,128)(2,1)S(1)} %get-tuple-element.39.refs_1_), channel_id=1, source_target_pairs={{0,3},{1,2},{2,1},{3,0},{4,7},{5,6},{6,5},{7,4},{8,11},{9,10},{10,... | collective-permute-start | bytes 98312 | tf_op jit(solution)/shard_map/ppermute | solution.py:207
  4.4 4.1 %collective-permute-start.2 = (bf16[128,128]{1,0:T(8,128)(2,1)S(1)}, bf16[128,128]{1,0:T(8,128)(2,1)S(1)}, u32[]{:S(2)}, u32[]{:S(2)}) collective-permute-start(bf16[128,128]{1,0:T(8,128)(2,1)S(1)} %get-tuple-element.39.refs_1_), channel_id=1, source_target_pairs={{0,2},{1,3},{2,0},{3,1},{4,6},{5,7},{6,4},{7,5},{8,10},{9,11},{10,... | collective-permute-start | bytes 98312 | tf_op jit(solution)/shard_map/ppermute | solution.py:207
  5.0 3.5 %collective-permute-start.1 = (bf16[128,128]{1,0:T(8,128)(2,1)S(1)}, bf16[128,128]{1,0:T(8,128)(2,1)S(1)}, u32[]{:S(2)}, u32[]{:S(2)}) collective-permute-start(bf16[128,128]{1,0:T(8,128)(2,1)S(1)} %get-tuple-element.39.refs_1_), channel_id=1, source_target_pairs={{0,1},{1,0},{2,3},{3,2},{4,5},{5,4},{6,7},{7,6},{8,9},{9,8},{10,11... | collective-permute-start | bytes 98312 | tf_op jit(solution)/shard_map/ppermute | solution.py:207
  5.0 5.2 %collective-permute-start = (bf16[128,128]{1,0:T(8,128)(2,1)S(1)}, bf16[128,128]{1,0:T(8,128)(2,1)S(1)}, u32[]{:S(2)}, u32[]{:S(2)}) collective-permute-start(bf16[128,128]{1,0:T(8,128)(2,1)S(1)} %get-tuple-element.38.refs_0_), channel_id=1, source_target_pairs={{0,4},{4,0},{8,12},{12,8},{16,20},{20,16},{24,28},{28,24},{1,5},{5... | collective-permute-start | bytes 98312 | tf_op jit(solution)/shard_map/ppermute | solution.py:207
  8.8 6.6 %collective-permute-start.11 = (f32[2,128,128]{2,1,0:T(8,128)S(1)}, f32[2,128,128]{2,1,0:T(8,128)S(1)}, u32[]{:S(2)}, u32[]{:S(2)}) collective-permute-start(f32[2,128,128]{2,1,0:T(8,128)S(1)} %get-tuple-element.47), channel_id=1, source_target_pairs={{0,4},{4,0},{8,12},{12,8},{16,20},{20,16},{24,28},{28,24},{1,5},{5... | collective-permute-start | bytes 393224 | tf_op jit(solution)/shard_map/ppermute | solution.py:207
  10.2 10.3 %collective-permute-start.6 = (bf16[2,128,128]{2,1,0:T(8,128)(2,1)S(1)}, bf16[2,128,128]{2,1,0:T(8,128)(2,1)S(1)}, u32[]{:S(2)}, u32[]{:S(2)}) collective-permute-start(bf16[2,128,128]{2,1,0:T(8,128)(2,1)S(1)} %pair_one_early.1.refs_1_), channel_id=1, source_target_pairs={{0,24},{4,28},{8,16},{12,20},{16,8},{20,12},{24,0},{28,4},{1,25},{... | collective-permute-start | bytes 196616 | tf_op jit(solution)/shard_map/ppermute | solution.py:207
  13.9 5.0 %collective-permute-start.14 = (f32[2,128,128]{2,1,0:T(8,128)S(1)}, f32[2,128,128]{2,1,0:T(8,128)S(1)}, u32[]{:S(2)}, u32[]{:S(2)}) collective-permute-start(f32[2,128,128]{2,1,0:T(8,128)S(1)} %get-tuple-element.40.refs_2_), channel_id=1, source_target_pairs={{0,4},{4,0},{8,12},{12,8},{16,20},{20,16},{24,28},{28,24},{1,5},{5... | collective-permute-start | bytes 393224 | tf_op jit(solution)/shard_map/ppermute | solution.py:207
  14.4 6.7 %collective-permute-start.5 = (bf16[2,128,128]{2,1,0:T(8,128)(2,1)S(1)}, bf16[2,128,128]{2,1,0:T(8,128)(2,1)S(1)}, u32[]{:S(2)}, u32[]{:S(2)}) collective-permute-start(bf16[2,128,128]{2,1,0:T(8,128)(2,1)S(1)} %pair_one_late.1), channel_id=1, source_target_pairs={{0,16},{4,20},{8,24},{12,28},{16,0},{20,4},{24,8},{28,12},{1,17},{... | collective-permute-start | bytes 196616 | tf_op jit(solution)/shard_map/ppermute | solution.py:207
  14.4 6.7 %collective-permute-start.4 = (bf16[2,128,128]{2,1,0:T(8,128)(2,1)S(1)}, bf16[2,128,128]{2,1,0:T(8,128)(2,1)S(1)}, u32[]{:S(2)}, u32[]{:S(2)}) collective-permute-start(bf16[2,128,128]{2,1,0:T(8,128)(2,1)S(1)} %pair_one_late.1), channel_id=1, source_target_pairs={{0,8},{4,12},{8,0},{12,4},{16,24},{20,28},{24,16},{28,20},{1,9},{5... | collective-permute-start | bytes 196616 | tf_op jit(solution)/shard_map/ppermute | solution.py:207
  15.4 8.1 %collective-permute-start.12 = (f32[128,128]{1,0:T(8,128)S(1)}, f32[128,128]{1,0:T(8,128)S(1)}, u32[]{:S(2)}, u32[]{:S(2)}) collective-permute-start(f32[128,128]{1,0:T(8,128)S(1)} %get-tuple-element.48), channel_id=1, source_target_pairs={{0,16},{4,20},{8,24},{12,28},{16,0},{20,4},{24,8},{28,12},{1,17},{... | collective-permute-start | bytes 196616 | tf_op jit(solution)/shard_map/ppermute | solution.py:207
  18.9 6.2 %collective-permute-start.13 = (f32[128,128]{1,0:T(8,128)S(1)}, f32[128,128]{1,0:T(8,128)S(1)}, u32[]{:S(2)}, u32[]{:S(2)}) collective-permute-start(f32[128,128]{1,0:T(8,128)S(1)} %get-tuple-element.49), channel_id=1, source_target_pairs={{0,24},{4,28},{8,16},{12,20},{16,8},{20,12},{24,0},{28,4},{1,25},{... | collective-permute-start | bytes 196616 | tf_op jit(solution)/shard_map/ppermute | solution.py:207
  20.5 5.0 %collective-permute-start.15 = (f32[128,128]{1,0:T(8,128)S(1)}, f32[128,128]{1,0:T(8,128)S(1)}, u32[]{:S(2)}, u32[]{:S(2)}) collective-permute-start(f32[128,128]{1,0:T(8,128)S(1)} %get-tuple-element.51), channel_id=1, source_target_pairs={{0,8},{4,12},{8,0},{12,4},{16,24},{20,28},{24,16},{28,20},{1,9},{5... | collective-permute-start | bytes 196616 | tf_op jit(solution)/shard_map/ppermute | solution.py:207
  21.6 5.3 %collective-permute-start.7 = (f32[128,128]{1,0:T(8,128)S(1)}, f32[128,128]{1,0:T(8,128)S(1)}, u32[]{:S(2)}, u32[]{:S(2)}) collective-permute-start(f32[128,128]{1,0:T(8,128)S(1)} %get-tuple-element.42), channel_id=1, source_target_pairs={{0,1},{1,0},{2,3},{3,2},{4,5},{5,4},{6,7},{7,6},{8,9},{9,8},{10,11... | collective-permute-start | bytes 196616 | tf_op jit(solution)/shard_map/ppermute | solution.py:207
  21.6 5.9 %collective-permute-start.8 = (f32[128,128]{1,0:T(8,128)S(1)}, f32[128,128]{1,0:T(8,128)S(1)}, u32[]{:S(2)}, u32[]{:S(2)}) collective-permute-start(f32[128,128]{1,0:T(8,128)S(1)} %get-tuple-element.43), channel_id=1, source_target_pairs={{0,2},{1,3},{2,0},{3,1},{4,6},{5,7},{6,4},{7,5},{8,10},{9,11},{10,... | collective-permute-start | bytes 196616 | tf_op jit(solution)/shard_map/ppermute | solution.py:207
  23.5 4.3 %collective-permute-start.9 = (f32[128,128]{1,0:T(8,128)S(1)}, f32[128,128]{1,0:T(8,128)S(1)}, u32[]{:S(2)}, u32[]{:S(2)}) collective-permute-start(f32[128,128]{1,0:T(8,128)S(1)} %get-tuple-element.44.refs_5_), channel_id=1, source_target_pairs={{0,3},{1,2},{2,1},{3,0},{4,7},{5,6},{6,5},{7,4},{8,11},{9,10},{10,... | collective-permute-start | bytes 196616 | tf_op jit(solution)/shard_map/ppermute | solution.py:207
  25.6 3.6 %collective-permute-start.18 = (bf16[128,128]{1,0:T(8,128)(2,1)S(1)}, bf16[128,128]{1,0:T(8,128)(2,1)S(1)}, u32[]{:S(2)}, u32[]{:S(2)}) collective-permute-start(bf16[128,128]{1,0:T(8,128)(2,1)S(1)} %get-tuple-element.53.refs_1_.refs_2_), channel_id=1, source_target_pairs={{0,3},{1,2},{2,1},{3,0},{4,7},{5,6},{6,5},{7,4},{8,11},{9,10},{10,... | collective-permute-start | bytes 98312 | tf_op jit(solution)/shard_map/ppermute | solution.py:207
  25.7 4.1 %collective-permute-start.17 = (bf16[128,128]{1,0:T(8,128)(2,1)S(1)}, bf16[128,128]{1,0:T(8,128)(2,1)S(1)}, u32[]{:S(2)}, u32[]{:S(2)}) collective-permute-start(bf16[128,128]{1,0:T(8,128)(2,1)S(1)} %get-tuple-element.53.refs_1_.refs_2_), channel_id=1, source_target_pairs={{0,2},{1,3},{2,0},{3,1},{4,6},{5,7},{6,4},{7,5},{8,10},{9,11},{10,... | collective-permute-start | bytes 98312 | tf_op jit(solution)/shard_map/ppermute | solution.py:207
  26.9 2.9 %collective-permute-start.16 = (bf16[128,128]{1,0:T(8,128)(2,1)S(1)}, bf16[128,128]{1,0:T(8,128)(2,1)S(1)}, u32[]{:S(2)}, u32[]{:S(2)}) collective-permute-start(bf16[128,128]{1,0:T(8,128)(2,1)S(1)} %get-tuple-element.53.refs_1_.refs_2_), channel_id=1, source_target_pairs={{0,1},{1,0},{2,3},{3,2},{4,5},{5,4},{6,7},{7,6},{8,9},{9,8},{10,11... | collective-permute-start | bytes 98312 | tf_op jit(solution)/shard_map/ppermute | solution.py:207
  27.8 4.0 %collective-permute-start.10 = (bf16[128,128]{1,0:T(8,128)(2,1)S(1)}, bf16[128,128]{1,0:T(8,128)(2,1)S(1)}, u32[]{:S(2)}, u32[]{:S(2)}) collective-permute-start(bf16[128,128]{1,0:T(8,128)(2,1)S(1)} %forward_middle.1.refs_0_), channel_id=1, source_target_pairs={{0,4},{4,0},{8,12},{12,8},{16,20},{20,16},{24,28},{28,24},{1,5},{5... | collective-permute-start | bytes 98312 | tf_op jit(solution)/shard_map/ppermute | solution.py:207
  30.1 6.1 %collective-permute-start.22 = (bf16[4,128,128]{2,1,0:T(8,128)(2,1)S(1)}, bf16[4,128,128]{2,1,0:T(8,128)(2,1)S(1)}, u32[]{:S(2)}, u32[]{:S(2)}) collective-permute-start(bf16[4,128,128]{2,1,0:T(8,128)(2,1)S(1)} %get-tuple-element.54.refs_3_), channel_id=1, source_target_pairs={{0,4},{4,0},{8,12},{12,8},{16,20},{20,16},{24,28},{28,24},{1,5},{5... | collective-permute-start | bytes 393224 | tf_op jit(solution)/shard_map/ppermute | solution.py:207
  31.8 8.9 %collective-permute-start.20 = (bf16[2,128,128]{2,1,0:T(8,128)(2,1)S(1)}, bf16[2,128,128]{2,1,0:T(8,128)(2,1)S(1)}, u32[]{:S(2)}, u32[]{:S(2)}) collective-permute-start(bf16[2,128,128]{2,1,0:T(8,128)(2,1)S(1)} %pair_two_late.1), channel_id=1, source_target_pairs={{0,16},{4,20},{8,24},{12,28},{16,0},{20,4},{24,8},{28,12},{1,17},{... | collective-permute-start | bytes 196616 | tf_op jit(solution)/shard_map/ppermute | solution.py:207
  33.4 8.7 %collective-permute-start.19 = (bf16[2,128,128]{2,1,0:T(8,128)(2,1)S(1)}, bf16[2,128,128]{2,1,0:T(8,128)(2,1)S(1)}, u32[]{:S(2)}, u32[]{:S(2)}) collective-permute-start(bf16[2,128,128]{2,1,0:T(8,128)(2,1)S(1)} %pair_two_late.1), channel_id=1, source_target_pairs={{0,8},{4,12},{8,0},{12,4},{16,24},{20,28},{24,16},{28,20},{1,9},{5... | collective-permute-start | bytes 196616 | tf_op jit(solution)/shard_map/ppermute | solution.py:207
  36.2 6.1 %collective-permute-start.21 = (bf16[2,128,128]{2,1,0:T(8,128)(2,1)S(1)}, bf16[2,128,128]{2,1,0:T(8,128)(2,1)S(1)}, u32[]{:S(2)}, u32[]{:S(2)}) collective-permute-start(bf16[2,128,128]{2,1,0:T(8,128)(2,1)S(1)} %pair_two_early.1.refs_1_), channel_id=1, source_target_pairs={{0,24},{4,28},{8,16},{12,20},{16,8},{20,12},{24,0},{28,4},{1,25},{... | collective-permute-start | bytes 196616 | tf_op jit(solution)/shard_map/ppermute | solution.py:207
  36.2 8.5 %collective-permute-start.26 = (bf16[128,128]{1,0:T(8,128)(2,1)S(1)}, bf16[128,128]{1,0:T(8,128)(2,1)S(1)}, u32[]{:S(2)}, u32[]{:S(2)}) collective-permute-start(bf16[128,128]{1,0:T(8,128)(2,1)S(1)} %get-tuple-element.63), channel_id=1, source_target_pairs={{0,16},{4,20},{8,24},{12,28},{16,0},{20,4},{24,8},{28,12},{1,17},{... | collective-permute-start | bytes 98312 | tf_op jit(solution)/shard_map/ppermute | solution.py:207
  37.8 7.0 %collective-permute-start.28 = (bf16[128,128]{1,0:T(8,128)(2,1)S(1)}, bf16[128,128]{1,0:T(8,128)(2,1)S(1)}, u32[]{:S(2)}, u32[]{:S(2)}) collective-permute-start(bf16[128,128]{1,0:T(8,128)(2,1)S(1)} %get-tuple-element.64), channel_id=1, source_target_pairs={{0,8},{4,12},{8,0},{12,4},{16,24},{20,28},{24,16},{28,20},{1,9},{5... | collective-permute-start | bytes 98312 | tf_op jit(solution)/shard_map/ppermute | solution.py:207
  40.7 5.7 %collective-permute-start.27 = (bf16[128,128]{1,0:T(8,128)(2,1)S(1)}, bf16[128,128]{1,0:T(8,128)(2,1)S(1)}, u32[]{:S(2)}, u32[]{:S(2)}) collective-permute-start(bf16[128,128]{1,0:T(8,128)(2,1)S(1)} %get-tuple-element.56.refs_5_), channel_id=1, source_target_pairs={{0,24},{4,28},{8,16},{12,20},{16,8},{20,12},{24,0},{28,4},{1,25},{... | collective-permute-start | bytes 98312 | tf_op jit(solution)/shard_map/ppermute | solution.py:207
  42.7 4.4 %collective-permute-start.23 = (bf16[128,128]{1,0:T(8,128)(2,1)S(1)}, bf16[128,128]{1,0:T(8,128)(2,1)S(1)}, u32[]{:S(2)}, u32[]{:S(2)}) collective-permute-start(bf16[128,128]{1,0:T(8,128)(2,1)S(1)} %get-tuple-element.58), channel_id=1, source_target_pairs={{0,1},{1,0},{2,3},{3,2},{4,5},{5,4},{6,7},{7,6},{8,9},{9,8},{10,11... | collective-permute-start | bytes 98312 | tf_op jit(solution)/shard_map/ppermute | solution.py:207
  42.8 4.4 %collective-permute-start.24 = (bf16[128,128]{1,0:T(8,128)(2,1)S(1)}, bf16[128,128]{1,0:T(8,128)(2,1)S(1)}, u32[]{:S(2)}, u32[]{:S(2)}) collective-permute-start(bf16[128,128]{1,0:T(8,128)(2,1)S(1)} %get-tuple-element.59), channel_id=1, source_target_pairs={{0,2},{1,3},{2,0},{3,1},{4,6},{5,7},{6,4},{7,5},{8,10},{9,11},{10,... | collective-permute-start | bytes 98312 | tf_op jit(solution)/shard_map/ppermute | solution.py:207
  44.7 3.3 %collective-permute-start.25 = (bf16[128,128]{1,0:T(8,128)(2,1)S(1)}, bf16[128,128]{1,0:T(8,128)(2,1)S(1)}, u32[]{:S(2)}, u32[]{:S(2)}) collective-permute-start(bf16[128,128]{1,0:T(8,128)(2,1)S(1)} %get-tuple-element.60), channel_id=1, source_target_pairs={{0,3},{1,2},{2,1},{3,0},{4,7},{5,6},{6,5},{7,4},{8,11},{9,10},{10,... | collective-permute-start | bytes 98312 | tf_op jit(solution)/shard_map/ppermute | solution.py:207

commit v16 on v14

--- a/solution.py
+++ b/solution.py
@@ -147,13 +147,8 @@
 def forward_body(half, n_cols, dense_ref, *refs):
     panels, outs = refs[:half], refs[half:]
     size = panels[0].shape[-1]
-    total = None
-    for zz in range(half):
-        panel = jnp.concatenate([panels[zz][0], panels[zz][1]], axis=0)
-        part = jnp.dot(
-            dense_ref[:, 2 * zz * size : (2 * zz + 2) * size], panel, preferred_element_type=F32
-        )
-        total = part if total is None else total + part
+    panel = jnp.concatenate([ref[at] for ref in panels for at in range(2)], axis=0)
+    total = jnp.dot(dense_ref[...], panel, preferred_element_type=F32)
     for j in range(n_cols):
         outs[j][...] = total[j * size : (j + 1) * size].astype(outs[j].dtype)
 

time: 48.3 us -> 48.3 us (level)
  transfers between devices with their start and end apart: 30 -> 30, of which waited for: 12 -> 13; matrix products, arithmetic and copies ran while one was open for 0% -> 0% of each run, Pallas kernels for 7% -> 7%
where the time goes in v16:
time: 48.3 us; the launch traced here: 48.4 us
  starting transfers between devices  30 us (62%)
  waiting for transfers between devices  11.8 us (24%)
  Pallas kernels  5.13 us (11%)
  between operations  1.44 us (3%)
    ppermute x30, starting transfers between devices, send(): return lax.ppermute(value, axis, [(i, i ^ step) for i in range(count)])  30 us
    ppermute x30, waiting for transfers between devices, send(): return lax.ppermute(value, axis, [(i, i ^ step) for i in range(count)])  11.8 us
    pallas_call x18, Pallas kernels, call(): pl.pallas_call(ordered, out_shape=outs, in_specs=[*in_specs, *[pl.BlockSp...  5.13 us
  transfers between devices with their start and end apart: 30, of which 13 were waited for; matrix products, arithmetic and copies ran while one was open for 0% of the time, Pallas kernels for 7%

profile of v16, /device:TPU:0, one launch (start us, length us, event | category | flops | bytes accessed | tf_op | source)
XLA Modules:
  0.0 48.4 jit_solution(15356878819169112743)
XLA Ops:
  0.6 1.3 %start.1 = (bf16[128,128]{1,0:T(8,128)(2,1)S(1)}, bf16[128,128]{1,0:T(8,128)(2,1)S(1)}, f32[1,128]{1,0:T(1,128)S(1)}, f32[128,128]{1,0:T(8,128)S(1)}, f32[128,12...) custom-call(s32[1,128]{1,0:T(1,128)} %bitcast.1, f32[8]{0:T(128)} %refs_1_.2, ...), custom_call_target="tpu_custom_call" | custom-call | bytes 1967136 | tf_op jit(solution)/shard_map/start/pallas_call | solution.py:36
  1.9 2.4 %collective-permute-start.3 = (bf16[128,128]{1,0:T(8,128)(2,1)S(1)}, bf16[128,128]{1,0:T(8,128)(2,1)S(1)}, u32[]{:S(2)}, u32[]{:S(2)}) collective-permute-start(bf16[128,128]{1,0:T(8,128)(2,1)S(1)} %get-tuple-element.41.refs_1_), channel_id=1, source_target_pairs={{0,3},{1,2},{2,1},{3,0},{4,7},{5,6},{6,5},{7,4},{8,11},{9,10},{10,... | collective-permute-start | bytes 98312 | tf_op jit(solution)/shard_map/ppermute | solution.py:205
  4.4 0.6 %collective-permute-start.2 = (bf16[128,128]{1,0:T(8,128)(2,1)S(1)}, bf16[128,128]{1,0:T(8,128)(2,1)S(1)}, u32[]{:S(2)}, u32[]{:S(2)}) collective-permute-start(bf16[128,128]{1,0:T(8,128)(2,1)S(1)} %get-tuple-element.41.refs_1_), channel_id=1, source_target_pairs={{0,2},{1,3},{2,0},{3,1},{4,6},{5,7},{6,4},{7,5},{8,10},{9,11},{10,... | collective-permute-start | bytes 98312 | tf_op jit(solution)/shard_map/ppermute | solution.py:205
  5.0 0.0 collective-permute-start.1
  5.0 1.8 %collective-permute-start = (bf16[128,128]{1,0:T(8,128)(2,1)S(1)}, bf16[128,128]{1,0:T(8,128)(2,1)S(1)}, u32[]{:S(2)}, u32[]{:S(2)}) collective-permute-start(bf16[128,128]{1,0:T(8,128)(2,1)S(1)} %get-tuple-element.40.refs_0_), channel_id=1, source_target_pairs={{0,4},{4,0},{8,12},{12,8},{16,20},{20,16},{24,28},{28,24},{1,5},{5... | collective-permute-start | bytes 98312 | tf_op jit(solution)/shard_map/ppermute | solution.py:205
  7.5 0.8 %dense.1.refs_2_.refs_0_ = bf16[512,1024]{1,0:T(8,128)(2,1)S(1)} custom-call(bf16[1,1,24,128,128]{4,3,2,1,0:T(8,128)(2,1)S(1)} %get-tuple-element.39.refs_0_, s32[1,1,24]{2,1,0:T(1,128)} %refs_1_.3, s32[1,1,24]{2,1,0:T(1,128)} %refs_2_.3, s32[1,1]{1,0:T(1,128)S(6)} %copy.10.refs_3_), custom_call_target="tpu_custom_call" | custom-call | bytes 1835204 | tf_op jit(solution)/shard_map/dense/pallas_call | solution.py:36
  8.3 0.3 adjoint_one.1
  8.6 1.6 %collective-permute-start.11 = (f32[2,128,128]{2,1,0:T(8,128)S(1)}, f32[2,128,128]{2,1,0:T(8,128)S(1)}, u32[]{:S(2)}, u32[]{:S(2)}) collective-permute-start(f32[2,128,128]{2,1,0:T(8,128)S(1)} %get-tuple-element.49), channel_id=1, source_target_pairs={{0,4},{4,0},{8,12},{12,8},{16,20},{20,16},{24,28},{28,24},{1,5},{5... | collective-permute-start | bytes 393224 | tf_op jit(solution)/shard_map/ppermute | solution.py:205
  10.2 3.7 %collective-permute-start.6 = (bf16[2,128,128]{2,1,0:T(8,128)(2,1)S(1)}, bf16[2,128,128]{2,1,0:T(8,128)(2,1)S(1)}, u32[]{:S(2)}, u32[]{:S(2)}) collective-permute-start(bf16[2,128,128]{2,1,0:T(8,128)(2,1)S(1)} %pair_one_early.1.refs_1_), channel_id=1, source_target_pairs={{0,24},{4,28},{8,16},{12,20},{16,8},{20,12},{24,0},{28,4},{1,25},{... | collective-permute-start | bytes 196616 | tf_op jit(solution)/shard_map/ppermute | solution.py:205
  13.9 0.5 %collective-permute-start.14 = (f32[2,128,128]{2,1,0:T(8,128)S(1)}, f32[2,128,128]{2,1,0:T(8,128)S(1)}, u32[]{:S(2)}, u32[]{:S(2)}) collective-permute-start(f32[2,128,128]{2,1,0:T(8,128)S(1)} %get-tuple-element.42.refs_2_), channel_id=1, source_target_pairs={{0,4},{4,0},{8,12},{12,8},{16,20},{20,16},{24,28},{28,24},{1,5},{5... | collective-permute-start | bytes 393224 | tf_op jit(solution)/shard_map/ppermute | solution.py:205
  14.4 0.8 %collective-permute-start.4 = (bf16[2,128,128]{2,1,0:T(8,128)(2,1)S(1)}, bf16[2,128,128]{2,1,0:T(8,128)(2,1)S(1)}, u32[]{:S(2)}, u32[]{:S(2)}) collective-permute-start(bf16[2,128,128]{2,1,0:T(8,128)(2,1)S(1)} %pair_one_late.1), channel_id=1, source_target_pairs={{0,8},{4,12},{8,0},{12,4},{16,24},{20,28},{24,16},{28,20},{1,9},{5... | collective-permute-start | bytes 196616 | tf_op jit(solution)/shard_map/ppermute | solution.py:205
  15.2 2.5 %collective-permute-start.12 = (f32[128,128]{1,0:T(8,128)S(1)}, f32[128,128]{1,0:T(8,128)S(1)}, u32[]{:S(2)}, u32[]{:S(2)}) collective-permute-start(f32[128,128]{1,0:T(8,128)S(1)} %get-tuple-element.50), channel_id=1, source_target_pairs={{0,16},{4,20},{8,24},{12,28},{16,0},{20,4},{24,8},{28,12},{1,17},{... | collective-permute-start | bytes 196616 | tf_op jit(solution)/shard_map/ppermute | solution.py:205
  17.8 1.1 %collective-permute-done.14.refs_1_ = f32[2,128,128]{2,1,0:T(8,128)S(1)} collective-permute-done((f32[2,128,128]{2,1,0:T(8,128)S(1)}, f32[2,128,128]{2,1,0:T(8,128)S(1)}, u32[]{:S(2)}, u32[]{:S(2)}) %collective-permute-start.14) | collective-permute-done | bytes 131104 | tf_op jit(solution)/shard_map/ppermute | solution.py:205
  18.9 1.5 %collective-permute-start.13 = (f32[128,128]{1,0:T(8,128)S(1)}, f32[128,128]{1,0:T(8,128)S(1)}, u32[]{:S(2)}, u32[]{:S(2)}) collective-permute-start(f32[128,128]{1,0:T(8,128)S(1)} %get-tuple-element.51), channel_id=1, source_target_pairs={{0,24},{4,28},{8,16},{12,20},{16,8},{20,12},{24,0},{28,4},{1,25},{... | collective-permute-start | bytes 196616 | tf_op jit(solution)/shard_map/ppermute | solution.py:205
  20.4 0.1 collective-permute-start.15
  20.5 0.6 %collective-permute-done.5.refs_3_ = bf16[2,128,128]{2,1,0:T(8,128)(2,1)S(1)} collective-permute-done((bf16[2,128,128]{2,1,0:T(8,128)(2,1)S(1)}, bf16[2,128,128]{2,1,0:T(8,128)(2,1)S(1)}, u32[]{:S(2)}, u32[]{:S(2)}) %collective-permute-start.5) | collective-permute-done | bytes 65568 | tf_op jit(solution)/shard_map/ppermute | solution.py:205
  21.1 0.4 forward_one.1
  21.6 0.1 collective-permute-start.7
  21.6 1.2 %collective-permute-start.8 = (f32[128,128]{1,0:T(8,128)S(1)}, f32[128,128]{1,0:T(8,128)S(1)}, u32[]{:S(2)}, u32[]{:S(2)}) collective-permute-start(f32[128,128]{1,0:T(8,128)S(1)} %get-tuple-element.45), channel_id=1, source_target_pairs={{0,2},{1,3},{2,0},{3,1},{4,6},{5,7},{6,4},{7,5},{8,10},{9,11},{10,... | collective-permute-start | bytes 196616 | tf_op jit(solution)/shard_map/ppermute | solution.py:205
  22.9 0.6 %collective-permute-done.12.refs_1_ = f32[128,128]{1,0:T(8,128)S(1)} collective-permute-done((f32[128,128]{1,0:T(8,128)S(1)}, f32[128,128]{1,0:T(8,128)S(1)}, u32[]{:S(2)}, u32[]{:S(2)}) %collective-permute-start.12) | collective-permute-done | bytes 65568 | tf_op jit(solution)/shard_map/ppermute | solution.py:205
  23.5 0.0 collective-permute-start.9
  23.5 1.5 %collective-permute-done.13.refs_2_ = f32[128,128]{1,0:T(8,128)S(1)} collective-permute-done((f32[128,128]{1,0:T(8,128)S(1)}, f32[128,128]{1,0:T(8,128)S(1)}, u32[]{:S(2)}, u32[]{:S(2)}) %collective-permute-start.13) | collective-permute-done | bytes 65568 | tf_op jit(solution)/shard_map/ppermute | solution.py:205
  25.0 0.4 collective-permute-done.15.refs_4_
  25.5 0.1 collective-permute-start.18
  25.6 1.3 %collective-permute-start.17 = (bf16[128,128]{1,0:T(8,128)(2,1)S(1)}, bf16[128,128]{1,0:T(8,128)(2,1)S(1)}, u32[]{:S(2)}, u32[]{:S(2)}) collective-permute-start(bf16[128,128]{1,0:T(8,128)(2,1)S(1)} %get-tuple-element.55.refs_1_.refs_2_), channel_id=1, source_target_pairs={{0,2},{1,3},{2,0},{3,1},{4,6},{5,7},{6,4},{7,5},{8,10},{9,11},{10,... | collective-permute-start | bytes 98312 | tf_op jit(solution)/shard_map/ppermute | solution.py:205
  26.9 0.5 %collective-permute-start.16 = (bf16[128,128]{1,0:T(8,128)(2,1)S(1)}, bf16[128,128]{1,0:T(8,128)(2,1)S(1)}, u32[]{:S(2)}, u32[]{:S(2)}) collective-permute-start(bf16[128,128]{1,0:T(8,128)(2,1)S(1)} %get-tuple-element.55.refs_1_.refs_2_), channel_id=1, source_target_pairs={{0,1},{1,0},{2,3},{3,2},{4,5},{5,4},{6,7},{7,6},{8,9},{9,8},{10,11... | collective-permute-start | bytes 98312 | tf_op jit(solution)/shard_map/ppermute | solution.py:205
  27.4 0.2 collective-permute-done.9.refs_5_
  27.7 1.5 %collective-permute-start.10 = (bf16[128,128]{1,0:T(8,128)(2,1)S(1)}, bf16[128,128]{1,0:T(8,128)(2,1)S(1)}, u32[]{:S(2)}, u32[]{:S(2)}) collective-permute-start(bf16[128,128]{1,0:T(8,128)(2,1)S(1)} %forward_middle.1.refs_0_), channel_id=1, source_target_pairs={{0,4},{4,0},{8,12},{12,8},{16,20},{20,16},{24,28},{28,24},{1,5},{5... | collective-permute-start | bytes 98312 | tf_op jit(solution)/shard_map/ppermute | solution.py:205
  29.2 0.4 collective-permute-done.17.refs_3_
  29.6 0.3 adjoint_two.1
  29.9 1.0 %collective-permute-start.22 = (bf16[2,128,128]{2,1,0:T(8,128)(2,1)S(1)}, bf16[2,128,128]{2,1,0:T(8,128)(2,1)S(1)}, u32[]{:S(2)}, u32[]{:S(2)}) collective-permute-start(bf16[2,128,128]{2,1,0:T(8,128)(2,1)S(1)} %get-tuple-element.58), channel_id=1, source_target_pairs={{0,4},{4,0},{8,12},{12,8},{16,20},{20,16},{24,28},{28,24},{1,5},{5... | collective-permute-start | bytes 196616 | tf_op jit(solution)/shard_map/ppermute | solution.py:205
  30.9 0.8 %collective-permute-done.10.refs_1_ = bf16[128,128]{1,0:T(8,128)(2,1)S(1)} collective-permute-done((bf16[128,128]{1,0:T(8,128)(2,1)S(1)}, bf16[128,128]{1,0:T(8,128)(2,1)S(1)}, u32[]{:S(2)}, u32[]{:S(2)}) %collective-permute-start.10) | collective-permute-done | bytes 32800 | tf_op jit(solution)/shard_map/ppermute | solution.py:205
  31.7 1.7 %collective-permute-start.20 = (bf16[2,128,128]{2,1,0:T(8,128)(2,1)S(1)}, bf16[2,128,128]{2,1,0:T(8,128)(2,1)S(1)}, u32[]{:S(2)}, u32[]{:S(2)}) collective-permute-start(bf16[2,128,128]{2,1,0:T(8,128)(2,1)S(1)} %pair_two_late.1), channel_id=1, source_target_pairs={{0,16},{4,20},{8,24},{12,28},{16,0},{20,4},{24,8},{28,12},{1,17},{... | collective-permute-start | bytes 196616 | tf_op jit(solution)/shard_map/ppermute | solution.py:205
  33.4 2.9 %collective-permute-start.19 = (bf16[2,128,128]{2,1,0:T(8,128)(2,1)S(1)}, bf16[2,128,128]{2,1,0:T(8,128)(2,1)S(1)}, u32[]{:S(2)}, u32[]{:S(2)}) collective-permute-start(bf16[2,128,128]{2,1,0:T(8,128)(2,1)S(1)} %pair_two_late.1), channel_id=1, source_target_pairs={{0,8},{4,12},{8,0},{12,4},{16,24},{20,28},{24,16},{28,20},{1,9},{5... | collective-permute-start | bytes 196616 | tf_op jit(solution)/shard_map/ppermute | solution.py:205
  36.3 1.2 %collective-permute-start.21 = (bf16[2,128,128]{2,1,0:T(8,128)(2,1)S(1)}, bf16[2,128,128]{2,1,0:T(8,128)(2,1)S(1)}, u32[]{:S(2)}, u32[]{:S(2)}) collective-permute-start(bf16[2,128,128]{2,1,0:T(8,128)(2,1)S(1)} %pair_two_early.1.refs_1_), channel_id=1, source_target_pairs={{0,24},{4,28},{8,16},{12,20},{16,8},{20,12},{24,0},{28,4},{1,25},{... | collective-permute-start | bytes 196616 | tf_op jit(solution)/shard_map/ppermute | solution.py:205
  37.5 0.4 collective-permute-start.27
  37.9 2.6 %collective-permute-done.23.refs_1_ = bf16[2,128,128]{2,1,0:T(8,128)(2,1)S(1)} collective-permute-done((bf16[2,128,128]{2,1,0:T(8,128)(2,1)S(1)}, bf16[2,128,128]{2,1,0:T(8,128)(2,1)S(1)}, u32[]{:S(2)}, u32[]{:S(2)}) %collective-permute-start.23) | collective-permute-done | bytes 65568 | tf_op jit(solution)/shard_map/ppermute | solution.py:205
  40.6 0.7 %collective-permute-start.29 = (bf16[128,128]{1,0:T(8,128)(2,1)S(1)}, bf16[128,128]{1,0:T(8,128)(2,1)S(1)}, u32[]{:S(2)}, u32[]{:S(2)}) collective-permute-start(bf16[128,128]{1,0:T(8,128)(2,1)S(1)} %get-tuple-element.61.refs_6_), channel_id=1, source_target_pairs={{0,8},{4,12},{8,0},{12,4},{16,24},{20,28},{24,16},{28,20},{1,9},{5... | collective-permute-start | bytes 98312 | tf_op jit(solution)/shard_map/ppermute | solution.py:205
  41.3 1.3 %collective-permute-done.21.refs_4_ = bf16[2,128,128]{2,1,0:T(8,128)(2,1)S(1)} collective-permute-done((bf16[2,128,128]{2,1,0:T(8,128)(2,1)S(1)}, bf16[2,128,128]{2,1,0:T(8,128)(2,1)S(1)}, u32[]{:S(2)}, u32[]{:S(2)}) %collective-permute-start.21) | collective-permute-done | bytes 65568 | tf_op jit(solution)/shard_map/ppermute | solution.py:205
  42.6 0.4 forward_two.1
  43.0 0.1 collective-permute-start.24
  43.1 1.3 %collective-permute-start.25 = (bf16[128,128]{1,0:T(8,128)(2,1)S(1)}, bf16[128,128]{1,0:T(8,128)(2,1)S(1)}, u32[]{:S(2)}, u32[]{:S(2)}) collective-permute-start(bf16[128,128]{1,0:T(8,128)(2,1)S(1)} %get-tuple-element.64), channel_id=1, source_target_pairs={{0,2},{1,3},{2,0},{3,1},{4,6},{5,7},{6,4},{7,5},{8,10},{9,11},{10,... | collective-permute-start | bytes 98312 | tf_op jit(solution)/shard_map/ppermute | solution.py:205
  44.4 0.6 %collective-permute-start.26 = (bf16[128,128]{1,0:T(8,128)(2,1)S(1)}, bf16[128,128]{1,0:T(8,128)(2,1)S(1)}, u32[]{:S(2)}, u32[]{:S(2)}) collective-permute-start(bf16[128,128]{1,0:T(8,128)(2,1)S(1)} %get-tuple-element.65), channel_id=1, source_target_pairs={{0,3},{1,2},{2,1},{3,0},{4,7},{5,6},{6,5},{7,4},{8,11},{9,10},{10,... | collective-permute-start | bytes 98312 | tf_op jit(solution)/shard_map/ppermute | solution.py:205
  45.0 1.3 %collective-permute-done.28.refs_4_ = bf16[128,128]{1,0:T(8,128)(2,1)S(1)} collective-permute-done((bf16[128,128]{1,0:T(8,128)(2,1)S(1)}, bf16[128,128]{1,0:T(8,128)(2,1)S(1)}, u32[]{:S(2)}, u32[]{:S(2)}) %collective-permute-start.28) | collective-permute-done | bytes 32800 | tf_op jit(solution)/shard_map/ppermute | solution.py:205
  46.2 0.7 %adjoint_end.1 = (f32[128,128]{1,0:T(8,128)}, f32[8,128]{1,0:T(8,128)S(1)}) custom-call(f32[128,128]{1,0:T(8,128)S(1)} %get-tuple-element.66.refs_0_, f32[128,128]{1,0:T(8,128)S(1)} %get-tuple-element.67.refs_1_, f32[1,128]{1,0:T(1,128)S(1)} %get-tuple-element.47.refs_0_.refs_2_, bf16[128,128]{1,0:T(8,128)(2,1)S(1)} %collective-permute-done.27.refs_3_, ...), custom_call_target="tpu_custom_call" | custom-call | flops 3000000000 | bytes 365056 | tf_op jit(solution)/shard_map/adjoint_end/pallas_call | solution.py:36
  47.0 0.1 collective-permute-done.25.refs_4_
  47.1 0.6 %collective-permute-done.26.refs_5_ = bf16[128,128]{1,0:T(8,128)(2,1)S(1)} collective-permute-done((bf16[128,128]{1,0:T(8,128)(2,1)S(1)}, bf16[128,128]{1,0:T(8,128)(2,1)S(1)}, u32[]{:S(2)}, u32[]{:S(2)}) %collective-permute-start.26) | collective-permute-done | bytes 32800 | tf_op jit(solution)/shard_map/ppermute | solution.py:205
  47.7 0.7 %forward_end.1 = f32[128,128]{1,0:T(8,128)} custom-call(f32[128,128]{1,0:T(8,128)S(1)} %get-tuple-element.37.refs_0_, f32[128,128]{1,0:T(8,128)S(1)} %get-tuple-element.38.refs_1_, bf16[128,128]{1,0:T(8,128)(2,1)S(1)} %get-tuple-element.62.refs_2_, bf16[128,128]{1,0:T(8,128)(2,1)S(1)} %collective-permute-done.24.refs_3_, ...), custom_call_target="tpu_custom_call" | custom-call | flops 1000000000 | bytes 327680 | tf_op jit(solution)/shard_map/forward_end/pallas_call | solution.py:36
  (30 shorter events, 0.2 us)
Async XLA Ops:
  1.9 6.4 %collective-permute-start.3 = (bf16[128,128]{1,0:T(8,128)(2,1)S(1)}, bf16[128,128]{1,0:T(8,128)(2,1)S(1)}, u32[]{:S(2)}, u32[]{:S(2)}) collective-permute-start(bf16[128,128]{1,0:T(8,128)(2,1)S(1)} %get-tuple-element.41.refs_1_), channel_id=1, source_target_pairs={{0,3},{1,2},{2,1},{3,0},{4,7},{5,6},{6,5},{7,4},{8,11},{9,10},{10,... | collective-permute-start | bytes 98312 | tf_op jit(solution)/shard_map/ppermute | solution.py:205
  4.4 4.0 %collective-permute-start.2 = (bf16[128,128]{1,0:T(8,128)(2,1)S(1)}, bf16[128,128]{1,0:T(8,128)(2,1)S(1)}, u32[]{:S(2)}, u32[]{:S(2)}) collective-permute-start(bf16[128,128]{1,0:T(8,128)(2,1)S(1)} %get-tuple-element.41.refs_1_), channel_id=1, source_target_pairs={{0,2},{1,3},{2,0},{3,1},{4,6},{5,7},{6,4},{7,5},{8,10},{9,11},{10,... | collective-permute-start | bytes 98312 | tf_op jit(solution)/shard_map/ppermute | solution.py:205
  5.0 3.3 %collective-permute-start.1 = (bf16[128,128]{1,0:T(8,128)(2,1)S(1)}, bf16[128,128]{1,0:T(8,128)(2,1)S(1)}, u32[]{:S(2)}, u32[]{:S(2)}) collective-permute-start(bf16[128,128]{1,0:T(8,128)(2,1)S(1)} %get-tuple-element.41.refs_1_), channel_id=1, source_target_pairs={{0,1},{1,0},{2,3},{3,2},{4,5},{5,4},{6,7},{7,6},{8,9},{9,8},{10,11... | collective-permute-start | bytes 98312 | tf_op jit(solution)/shard_map/ppermute | solution.py:205
  5.0 5.2 %collective-permute-start = (bf16[128,128]{1,0:T(8,128)(2,1)S(1)}, bf16[128,128]{1,0:T(8,128)(2,1)S(1)}, u32[]{:S(2)}, u32[]{:S(2)}) collective-permute-start(bf16[128,128]{1,0:T(8,128)(2,1)S(1)} %get-tuple-element.40.refs_0_), channel_id=1, source_target_pairs={{0,4},{4,0},{8,12},{12,8},{16,20},{20,16},{24,28},{28,24},{1,5},{5... | collective-permute-start | bytes 98312 | tf_op jit(solution)/shard_map/ppermute | solution.py:205
  8.6 6.6 %collective-permute-start.11 = (f32[2,128,128]{2,1,0:T(8,128)S(1)}, f32[2,128,128]{2,1,0:T(8,128)S(1)}, u32[]{:S(2)}, u32[]{:S(2)}) collective-permute-start(f32[2,128,128]{2,1,0:T(8,128)S(1)} %get-tuple-element.49), channel_id=1, source_target_pairs={{0,4},{4,0},{8,12},{12,8},{16,20},{20,16},{24,28},{28,24},{1,5},{5... | collective-permute-start | bytes 393224 | tf_op jit(solution)/shard_map/ppermute | solution.py:205
  10.2 10.2 %collective-permute-start.6 = (bf16[2,128,128]{2,1,0:T(8,128)(2,1)S(1)}, bf16[2,128,128]{2,1,0:T(8,128)(2,1)S(1)}, u32[]{:S(2)}, u32[]{:S(2)}) collective-permute-start(bf16[2,128,128]{2,1,0:T(8,128)(2,1)S(1)} %pair_one_early.1.refs_1_), channel_id=1, source_target_pairs={{0,24},{4,28},{8,16},{12,20},{16,8},{20,12},{24,0},{28,4},{1,25},{... | collective-permute-start | bytes 196616 | tf_op jit(solution)/shard_map/ppermute | solution.py:205
  13.9 5.0 %collective-permute-start.14 = (f32[2,128,128]{2,1,0:T(8,128)S(1)}, f32[2,128,128]{2,1,0:T(8,128)S(1)}, u32[]{:S(2)}, u32[]{:S(2)}) collective-permute-start(f32[2,128,128]{2,1,0:T(8,128)S(1)} %get-tuple-element.42.refs_2_), channel_id=1, source_target_pairs={{0,4},{4,0},{8,12},{12,8},{16,20},{20,16},{24,28},{28,24},{1,5},{5... | collective-permute-start | bytes 393224 | tf_op jit(solution)/shard_map/ppermute | solution.py:205
  14.4 6.7 %collective-permute-start.5 = (bf16[2,128,128]{2,1,0:T(8,128)(2,1)S(1)}, bf16[2,128,128]{2,1,0:T(8,128)(2,1)S(1)}, u32[]{:S(2)}, u32[]{:S(2)}) collective-permute-start(bf16[2,128,128]{2,1,0:T(8,128)(2,1)S(1)} %pair_one_late.1), channel_id=1, source_target_pairs={{0,16},{4,20},{8,24},{12,28},{16,0},{20,4},{24,8},{28,12},{1,17},{... | collective-permute-start | bytes 196616 | tf_op jit(solution)/shard_map/ppermute | solution.py:205
  14.4 6.7 %collective-permute-start.4 = (bf16[2,128,128]{2,1,0:T(8,128)(2,1)S(1)}, bf16[2,128,128]{2,1,0:T(8,128)(2,1)S(1)}, u32[]{:S(2)}, u32[]{:S(2)}) collective-permute-start(bf16[2,128,128]{2,1,0:T(8,128)(2,1)S(1)} %pair_one_late.1), channel_id=1, source_target_pairs={{0,8},{4,12},{8,0},{12,4},{16,24},{20,28},{24,16},{28,20},{1,9},{5... | collective-permute-start | bytes 196616 | tf_op jit(solution)/shard_map/ppermute | solution.py:205
  15.2 8.2 %collective-permute-start.12 = (f32[128,128]{1,0:T(8,128)S(1)}, f32[128,128]{1,0:T(8,128)S(1)}, u32[]{:S(2)}, u32[]{:S(2)}) collective-permute-start(f32[128,128]{1,0:T(8,128)S(1)} %get-tuple-element.50), channel_id=1, source_target_pairs={{0,16},{4,20},{8,24},{12,28},{16,0},{20,4},{24,8},{28,12},{1,17},{... | collective-permute-start | bytes 196616 | tf_op jit(solution)/shard_map/ppermute | solution.py:205
  18.9 6.2 %collective-permute-start.13 = (f32[128,128]{1,0:T(8,128)S(1)}, f32[128,128]{1,0:T(8,128)S(1)}, u32[]{:S(2)}, u32[]{:S(2)}) collective-permute-start(f32[128,128]{1,0:T(8,128)S(1)} %get-tuple-element.51), channel_id=1, source_target_pairs={{0,24},{4,28},{8,16},{12,20},{16,8},{20,12},{24,0},{28,4},{1,25},{... | collective-permute-start | bytes 196616 | tf_op jit(solution)/shard_map/ppermute | solution.py:205
  20.4 5.0 %collective-permute-start.15 = (f32[128,128]{1,0:T(8,128)S(1)}, f32[128,128]{1,0:T(8,128)S(1)}, u32[]{:S(2)}, u32[]{:S(2)}) collective-permute-start(f32[128,128]{1,0:T(8,128)S(1)} %get-tuple-element.54), channel_id=1, source_target_pairs={{0,8},{4,12},{8,0},{12,4},{16,24},{20,28},{24,16},{28,20},{1,9},{5... | collective-permute-start | bytes 196616 | tf_op jit(solution)/shard_map/ppermute | solution.py:205
  21.6 5.3 %collective-permute-start.7 = (f32[128,128]{1,0:T(8,128)S(1)}, f32[128,128]{1,0:T(8,128)S(1)}, u32[]{:S(2)}, u32[]{:S(2)}) collective-permute-start(f32[128,128]{1,0:T(8,128)S(1)} %get-tuple-element.44), channel_id=1, source_target_pairs={{0,1},{1,0},{2,3},{3,2},{4,5},{5,4},{6,7},{7,6},{8,9},{9,8},{10,11... | collective-permute-start | bytes 196616 | tf_op jit(solution)/shard_map/ppermute | solution.py:205
  21.6 5.8 %collective-permute-start.8 = (f32[128,128]{1,0:T(8,128)S(1)}, f32[128,128]{1,0:T(8,128)S(1)}, u32[]{:S(2)}, u32[]{:S(2)}) collective-permute-start(f32[128,128]{1,0:T(8,128)S(1)} %get-tuple-element.45), channel_id=1, source_target_pairs={{0,2},{1,3},{2,0},{3,1},{4,6},{5,7},{6,4},{7,5},{8,10},{9,11},{10,... | collective-permute-start | bytes 196616 | tf_op jit(solution)/shard_map/ppermute | solution.py:205
  23.5 4.2 %collective-permute-start.9 = (f32[128,128]{1,0:T(8,128)S(1)}, f32[128,128]{1,0:T(8,128)S(1)}, u32[]{:S(2)}, u32[]{:S(2)}) collective-permute-start(f32[128,128]{1,0:T(8,128)S(1)} %get-tuple-element.46.refs_5_), channel_id=1, source_target_pairs={{0,3},{1,2},{2,1},{3,0},{4,7},{5,6},{6,5},{7,4},{8,11},{9,10},{10,... | collective-permute-start | bytes 196616 | tf_op jit(solution)/shard_map/ppermute | solution.py:205
  25.5 3.7 %collective-permute-start.18 = (bf16[128,128]{1,0:T(8,128)(2,1)S(1)}, bf16[128,128]{1,0:T(8,128)(2,1)S(1)}, u32[]{:S(2)}, u32[]{:S(2)}) collective-permute-start(bf16[128,128]{1,0:T(8,128)(2,1)S(1)} %get-tuple-element.55.refs_1_.refs_2_), channel_id=1, source_target_pairs={{0,3},{1,2},{2,1},{3,0},{4,7},{5,6},{6,5},{7,4},{8,11},{9,10},{10,... | collective-permute-start | bytes 98312 | tf_op jit(solution)/shard_map/ppermute | solution.py:205
  25.6 4.0 %collective-permute-start.17 = (bf16[128,128]{1,0:T(8,128)(2,1)S(1)}, bf16[128,128]{1,0:T(8,128)(2,1)S(1)}, u32[]{:S(2)}, u32[]{:S(2)}) collective-permute-start(bf16[128,128]{1,0:T(8,128)(2,1)S(1)} %get-tuple-element.55.refs_1_.refs_2_), channel_id=1, source_target_pairs={{0,2},{1,3},{2,0},{3,1},{4,6},{5,7},{6,4},{7,5},{8,10},{9,11},{10,... | collective-permute-start | bytes 98312 | tf_op jit(solution)/shard_map/ppermute | solution.py:205
  26.9 2.7 %collective-permute-start.16 = (bf16[128,128]{1,0:T(8,128)(2,1)S(1)}, bf16[128,128]{1,0:T(8,128)(2,1)S(1)}, u32[]{:S(2)}, u32[]{:S(2)}) collective-permute-start(bf16[128,128]{1,0:T(8,128)(2,1)S(1)} %get-tuple-element.55.refs_1_.refs_2_), channel_id=1, source_target_pairs={{0,1},{1,0},{2,3},{3,2},{4,5},{5,4},{6,7},{7,6},{8,9},{9,8},{10,11... | collective-permute-start | bytes 98312 | tf_op jit(solution)/shard_map/ppermute | solution.py:205
  27.7 4.0 %collective-permute-start.10 = (bf16[128,128]{1,0:T(8,128)(2,1)S(1)}, bf16[128,128]{1,0:T(8,128)(2,1)S(1)}, u32[]{:S(2)}, u32[]{:S(2)}) collective-permute-start(bf16[128,128]{1,0:T(8,128)(2,1)S(1)} %forward_middle.1.refs_0_), channel_id=1, source_target_pairs={{0,4},{4,0},{8,12},{12,8},{16,20},{20,16},{24,28},{28,24},{1,5},{5... | collective-permute-start | bytes 98312 | tf_op jit(solution)/shard_map/ppermute | solution.py:205
  29.9 7.6 %collective-permute-start.22 = (bf16[2,128,128]{2,1,0:T(8,128)(2,1)S(1)}, bf16[2,128,128]{2,1,0:T(8,128)(2,1)S(1)}, u32[]{:S(2)}, u32[]{:S(2)}) collective-permute-start(bf16[2,128,128]{2,1,0:T(8,128)(2,1)S(1)} %get-tuple-element.58), channel_id=1, source_target_pairs={{0,4},{4,0},{8,12},{12,8},{16,20},{20,16},{24,28},{28,24},{1,5},{5... | collective-permute-start | bytes 196616 | tf_op jit(solution)/shard_map/ppermute | solution.py:205
  31.7 8.8 %collective-permute-start.20 = (bf16[2,128,128]{2,1,0:T(8,128)(2,1)S(1)}, bf16[2,128,128]{2,1,0:T(8,128)(2,1)S(1)}, u32[]{:S(2)}, u32[]{:S(2)}) collective-permute-start(bf16[2,128,128]{2,1,0:T(8,128)(2,1)S(1)} %pair_two_late.1), channel_id=1, source_target_pairs={{0,16},{4,20},{8,24},{12,28},{16,0},{20,4},{24,8},{28,12},{1,17},{... | collective-permute-start | bytes 196616 | tf_op jit(solution)/shard_map/ppermute | solution.py:205
  33.4 7.9 %collective-permute-start.19 = (bf16[2,128,128]{2,1,0:T(8,128)(2,1)S(1)}, bf16[2,128,128]{2,1,0:T(8,128)(2,1)S(1)}, u32[]{:S(2)}, u32[]{:S(2)}) collective-permute-start(bf16[2,128,128]{2,1,0:T(8,128)(2,1)S(1)} %pair_two_late.1), channel_id=1, source_target_pairs={{0,8},{4,12},{8,0},{12,4},{16,24},{20,28},{24,16},{28,20},{1,9},{5... | collective-permute-start | bytes 196616 | tf_op jit(solution)/shard_map/ppermute | solution.py:205
  36.3 4.3 %collective-permute-start.23 = (bf16[2,128,128]{2,1,0:T(8,128)(2,1)S(1)}, bf16[2,128,128]{2,1,0:T(8,128)(2,1)S(1)}, u32[]{:S(2)}, u32[]{:S(2)}) collective-permute-start(bf16[2,128,128]{2,1,0:T(8,128)(2,1)S(1)} %get-tuple-element.56.refs_3_), channel_id=1, source_target_pairs={{0,4},{4,0},{8,12},{12,8},{16,20},{20,16},{24,28},{28,24},{1,5},{5... | collective-permute-start | bytes 196616 | tf_op jit(solution)/shard_map/ppermute | solution.py:205
  36.3 6.3 %collective-permute-start.21 = (bf16[2,128,128]{2,1,0:T(8,128)(2,1)S(1)}, bf16[2,128,128]{2,1,0:T(8,128)(2,1)S(1)}, u32[]{:S(2)}, u32[]{:S(2)}) collective-permute-start(bf16[2,128,128]{2,1,0:T(8,128)(2,1)S(1)} %pair_two_early.1.refs_1_), channel_id=1, source_target_pairs={{0,24},{4,28},{8,16},{12,20},{16,8},{20,12},{24,0},{28,4},{1,25},{... | collective-permute-start | bytes 196616 | tf_op jit(solution)/shard_map/ppermute | solution.py:205
  37.5 6.8 %collective-permute-start.27 = (bf16[128,128]{1,0:T(8,128)(2,1)S(1)}, bf16[128,128]{1,0:T(8,128)(2,1)S(1)}, u32[]{:S(2)}, u32[]{:S(2)}) collective-permute-start(bf16[128,128]{1,0:T(8,128)(2,1)S(1)} %get-tuple-element.68), channel_id=1, source_target_pairs={{0,16},{4,20},{8,24},{12,28},{16,0},{20,4},{24,8},{28,12},{1,17},{... | collective-permute-start | bytes 98312 | tf_op jit(solution)/shard_map/ppermute | solution.py:205
  40.5 5.7 %collective-permute-start.28 = (bf16[128,128]{1,0:T(8,128)(2,1)S(1)}, bf16[128,128]{1,0:T(8,128)(2,1)S(1)}, u32[]{:S(2)}, u32[]{:S(2)}) collective-permute-start(bf16[128,128]{1,0:T(8,128)(2,1)S(1)} %get-tuple-element.59.refs_5_), channel_id=1, source_target_pairs={{0,24},{4,28},{8,16},{12,20},{16,8},{20,12},{24,0},{28,4},{1,25},{... | collective-permute-start | bytes 98312 | tf_op jit(solution)/shard_map/ppermute | solution.py:205
  40.6 5.7 %collective-permute-start.29 = (bf16[128,128]{1,0:T(8,128)(2,1)S(1)}, bf16[128,128]{1,0:T(8,128)(2,1)S(1)}, u32[]{:S(2)}, u32[]{:S(2)}) collective-permute-start(bf16[128,128]{1,0:T(8,128)(2,1)S(1)} %get-tuple-element.61.refs_6_), channel_id=1, source_target_pairs={{0,8},{4,12},{8,0},{12,4},{16,24},{20,28},{24,16},{28,20},{1,9},{5... | collective-permute-start | bytes 98312 | tf_op jit(solution)/shard_map/ppermute | solution.py:205
  43.0 4.0 %collective-permute-start.24 = (bf16[128,128]{1,0:T(8,128)(2,1)S(1)}, bf16[128,128]{1,0:T(8,128)(2,1)S(1)}, u32[]{:S(2)}, u32[]{:S(2)}) collective-permute-start(bf16[128,128]{1,0:T(8,128)(2,1)S(1)} %get-tuple-element.63), channel_id=1, source_target_pairs={{0,1},{1,0},{2,3},{3,2},{4,5},{5,4},{6,7},{7,6},{8,9},{9,8},{10,11... | collective-permute-start | bytes 98312 | tf_op jit(solution)/shard_map/ppermute | solution.py:205
  43.1 4.0 %collective-permute-start.25 = (bf16[128,128]{1,0:T(8,128)(2,1)S(1)}, bf16[128,128]{1,0:T(8,128)(2,1)S(1)}, u32[]{:S(2)}, u32[]{:S(2)}) collective-permute-start(bf16[128,128]{1,0:T(8,128)(2,1)S(1)} %get-tuple-element.64), channel_id=1, source_target_pairs={{0,2},{1,3},{2,0},{3,1},{4,6},{5,7},{6,4},{7,5},{8,10},{9,11},{10,... | collective-permute-start | bytes 98312 | tf_op jit(solution)/shard_map/ppermute | solution.py:205
  44.4 3.3 %collective-permute-start.26 = (bf16[128,128]{1,0:T(8,128)(2,1)S(1)}, bf16[128,128]{1,0:T(8,128)(2,1)S(1)}, u32[]{:S(2)}, u32[]{:S(2)}) collective-permute-start(bf16[128,128]{1,0:T(8,128)(2,1)S(1)} %get-tuple-element.65), channel_id=1, source_target_pairs={{0,3},{1,2},{2,1},{3,0},{4,7},{5,6},{6,5},{7,4},{8,11},{9,10},{10,... | collective-permute-start | bytes 98312 | tf_op jit(solution)/shard_map/ppermute | solution.py:205

commit v17 on v15

--- a/solution.py
+++ b/solution.py
@@ -293,7 +293,7 @@
 
     def forward(name, early, late, kind):
         panels = [early] + [
-            send(early if s == half - 1 else late, "rows", n_rows, 2 * s) for s in range(1, half)
+            send(early if s == near else late, "rows", n_rows, 2 * s) for s in range(1, half)
         ]
         return run(
             name,

time: 48.8 us -> 48.1 us (0.986)
  waiting for transfers between devices: 8.68 us -> 7.46 us
    ppermute x29, waiting for transfers between devices: 8.68 us -> 7.46 us  [send(): return lax.ppermute(value, axis, [(i, i ^ step) for i in range(count)])]
  transfers between devices with their start and end apart: 29 -> 29, of which waited for: 11 -> 6; matrix products, arithmetic and copies ran while one was open for 0% -> 0% of each run, Pallas kernels for 7% -> 7%
where the time goes in v17:
time: 48.1 us; the launch traced here: 47.7 us
  starting transfers between devices  33.7 us (70%)
  waiting for transfers between devices  7.46 us (16%)
  Pallas kernels  5.16 us (11%)
  between operations  1.45 us (3%)
    ppermute x29, starting transfers between devices, send(): return lax.ppermute(value, axis, [(i, i ^ step) for i in range(count)])  33.7 us
    ppermute x29, waiting for transfers between devices, send(): return lax.ppermute(value, axis, [(i, i ^ step) for i in range(count)])  7.46 us
    pallas_call x17, Pallas kernels, call(): pl.pallas_call(ordered, out_shape=outs, in_specs=[*in_specs, *[pl.BlockSp...  5.16 us
  transfers between devices with their start and end apart: 29, of which 6 were waited for; matrix products, arithmetic and copies ran while one was open for 0% of the time, Pallas kernels for 7%

profile of v17, /device:TPU:0, one launch (start us, length us, event | category | flops | bytes accessed | tf_op | source)
XLA Modules:
  0.0 47.7 jit_solution(16018732246971532134)
XLA Ops:
  0.6 1.3 %start.1 = (bf16[128,128]{1,0:T(8,128)(2,1)S(1)}, bf16[128,128]{1,0:T(8,128)(2,1)S(1)}, f32[1,128]{1,0:T(1,128)S(1)}, f32[128,128]{1,0:T(8,128)S(1)}, f32[128,12...) custom-call(s32[1,128]{1,0:T(1,128)} %bitcast.1, f32[8]{0:T(128)} %refs_1_.2, ...), custom_call_target="tpu_custom_call" | custom-call | bytes 1967136 | tf_op jit(solution)/shard_map/start/pallas_call | solution.py:36
  1.9 2.4 %collective-permute-start.3 = (bf16[128,128]{1,0:T(8,128)(2,1)S(1)}, bf16[128,128]{1,0:T(8,128)(2,1)S(1)}, u32[]{:S(2)}, u32[]{:S(2)}) collective-permute-start(bf16[128,128]{1,0:T(8,128)(2,1)S(1)} %get-tuple-element.39.refs_1_), channel_id=1, source_target_pairs={{0,3},{1,2},{2,1},{3,0},{4,7},{5,6},{6,5},{7,4},{8,11},{9,10},{10,... | collective-permute-start | bytes 98312 | tf_op jit(solution)/shard_map/ppermute | solution.py:207
  4.4 0.6 %collective-permute-start.2 = (bf16[128,128]{1,0:T(8,128)(2,1)S(1)}, bf16[128,128]{1,0:T(8,128)(2,1)S(1)}, u32[]{:S(2)}, u32[]{:S(2)}) collective-permute-start(bf16[128,128]{1,0:T(8,128)(2,1)S(1)} %get-tuple-element.39.refs_1_), channel_id=1, source_target_pairs={{0,2},{1,3},{2,0},{3,1},{4,6},{5,7},{6,4},{7,5},{8,10},{9,11},{10,... | collective-permute-start | bytes 98312 | tf_op jit(solution)/shard_map/ppermute | solution.py:207
  5.0 0.0 collective-permute-start.1
  5.0 1.8 %collective-permute-start = (bf16[128,128]{1,0:T(8,128)(2,1)S(1)}, bf16[128,128]{1,0:T(8,128)(2,1)S(1)}, u32[]{:S(2)}, u32[]{:S(2)}) collective-permute-start(bf16[128,128]{1,0:T(8,128)(2,1)S(1)} %get-tuple-element.38.refs_0_), channel_id=1, source_target_pairs={{0,4},{4,0},{8,12},{12,8},{16,20},{20,16},{24,28},{28,24},{1,5},{5... | collective-permute-start | bytes 98312 | tf_op jit(solution)/shard_map/ppermute | solution.py:207
  7.5 0.9 %dense.1.refs_2_.refs_0_ = bf16[512,1024]{1,0:T(8,128)(2,1)S(1)} custom-call(bf16[1,1,24,128,128]{4,3,2,1,0:T(8,128)(2,1)S(1)} %get-tuple-element.37.refs_0_, s32[1,1,24]{2,1,0:T(1,128)} %refs_1_.3, s32[1,1,24]{2,1,0:T(1,128)} %refs_2_.3, s32[1,1]{1,0:T(1,128)S(6)} %copy.10.refs_3_), custom_call_target="tpu_custom_call" | custom-call | bytes 1835204 | tf_op jit(solution)/shard_map/dense/pallas_call | solution.py:36
  8.4 0.0 collective-permute-done.1.refs_2_
  8.4 0.3 adjoint_one.1
  8.7 1.6 %collective-permute-start.11 = (f32[2,128,128]{2,1,0:T(8,128)S(1)}, f32[2,128,128]{2,1,0:T(8,128)S(1)}, u32[]{:S(2)}, u32[]{:S(2)}) collective-permute-start(f32[2,128,128]{2,1,0:T(8,128)S(1)} %get-tuple-element.47), channel_id=1, source_target_pairs={{0,4},{4,0},{8,12},{12,8},{16,20},{20,16},{24,28},{28,24},{1,5},{5... | collective-permute-start | bytes 393224 | tf_op jit(solution)/shard_map/ppermute | solution.py:207
  10.2 0.0 collective-permute-done.refs_1_
  10.2 2.7 %collective-permute-start.5 = (bf16[2,128,128]{2,1,0:T(8,128)(2,1)S(1)}, bf16[2,128,128]{2,1,0:T(8,128)(2,1)S(1)}, u32[]{:S(2)}, u32[]{:S(2)}) collective-permute-start(bf16[2,128,128]{2,1,0:T(8,128)(2,1)S(1)} %pair_one_early.1.refs_1_), channel_id=1, source_target_pairs={{0,16},{4,20},{8,24},{12,28},{16,0},{20,4},{24,8},{28,12},{1,17},{... | collective-permute-start | bytes 196616 | tf_op jit(solution)/shard_map/ppermute | solution.py:207
  12.9 0.5 %collective-permute-start.14 = (f32[2,128,128]{2,1,0:T(8,128)S(1)}, f32[2,128,128]{2,1,0:T(8,128)S(1)}, u32[]{:S(2)}, u32[]{:S(2)}) collective-permute-start(f32[2,128,128]{2,1,0:T(8,128)S(1)} %get-tuple-element.40.refs_2_), channel_id=1, source_target_pairs={{0,4},{4,0},{8,12},{12,8},{16,20},{20,16},{24,28},{28,24},{1,5},{5... | collective-permute-start | bytes 393224 | tf_op jit(solution)/shard_map/ppermute | solution.py:207
  13.4 1.5 %collective-permute-start.6 = (bf16[2,128,128]{2,1,0:T(8,128)(2,1)S(1)}, bf16[2,128,128]{2,1,0:T(8,128)(2,1)S(1)}, u32[]{:S(2)}, u32[]{:S(2)}) collective-permute-start(bf16[2,128,128]{2,1,0:T(8,128)(2,1)S(1)} %pair_one_late.1), channel_id=1, source_target_pairs={{0,24},{4,28},{8,16},{12,20},{16,8},{20,12},{24,0},{28,4},{1,25},{... | collective-permute-start | bytes 196616 | tf_op jit(solution)/shard_map/ppermute | solution.py:207
  14.9 0.1 collective-permute-start.4
  15.1 2.8 %collective-permute-start.12 = (f32[128,128]{1,0:T(8,128)S(1)}, f32[128,128]{1,0:T(8,128)S(1)}, u32[]{:S(2)}, u32[]{:S(2)}) collective-permute-start(f32[128,128]{1,0:T(8,128)S(1)} %get-tuple-element.48), channel_id=1, source_target_pairs={{0,16},{4,20},{8,24},{12,28},{16,0},{20,4},{24,8},{28,12},{1,17},{... | collective-permute-start | bytes 196616 | tf_op jit(solution)/shard_map/ppermute | solution.py:207
  17.9 2.5 %collective-permute-start.13 = (f32[128,128]{1,0:T(8,128)S(1)}, f32[128,128]{1,0:T(8,128)S(1)}, u32[]{:S(2)}, u32[]{:S(2)}) collective-permute-start(f32[128,128]{1,0:T(8,128)S(1)} %get-tuple-element.49), channel_id=1, source_target_pairs={{0,24},{4,28},{8,16},{12,20},{16,8},{20,12},{24,0},{28,4},{1,25},{... | collective-permute-start | bytes 196616 | tf_op jit(solution)/shard_map/ppermute | solution.py:207
  20.4 0.0 collective-permute-done.5.refs_3_
  20.4 0.1 collective-permute-start.15
  20.5 0.0 collective-permute-done.4.refs_2_
  20.5 0.4 forward_one.1
  21.0 0.1 collective-permute-start.7
  21.1 1.5 %collective-permute-start.8 = (f32[128,128]{1,0:T(8,128)S(1)}, f32[128,128]{1,0:T(8,128)S(1)}, u32[]{:S(2)}, u32[]{:S(2)}) collective-permute-start(f32[128,128]{1,0:T(8,128)S(1)} %get-tuple-element.43), channel_id=1, source_target_pairs={{0,2},{1,3},{2,0},{3,1},{4,6},{5,7},{6,4},{7,5},{8,10},{9,11},{10,... | collective-permute-start | bytes 196616 | tf_op jit(solution)/shard_map/ppermute | solution.py:207
  22.5 1.7 %collective-permute-done.12.refs_1_ = f32[128,128]{1,0:T(8,128)S(1)} collective-permute-done((f32[128,128]{1,0:T(8,128)S(1)}, f32[128,128]{1,0:T(8,128)S(1)}, u32[]{:S(2)}, u32[]{:S(2)}) %collective-permute-start.12) | collective-permute-done | bytes 65568 | tf_op jit(solution)/shard_map/ppermute | solution.py:207
  24.2 0.0 collective-permute-start.9
  24.2 0.0 collective-permute-done.13.refs_2_
  24.2 0.7 %collective-permute-done.15.refs_3_ = f32[128,128]{1,0:T(8,128)S(1)} collective-permute-done((f32[128,128]{1,0:T(8,128)S(1)}, f32[128,128]{1,0:T(8,128)S(1)}, u32[]{:S(2)}, u32[]{:S(2)}) %collective-permute-start.15) | collective-permute-done | bytes 65568 | tf_op jit(solution)/shard_map/ppermute | solution.py:207
  24.9 1.1 %collective-permute-start.18 = (bf16[128,128]{1,0:T(8,128)(2,1)S(1)}, bf16[128,128]{1,0:T(8,128)(2,1)S(1)}, u32[]{:S(2)}, u32[]{:S(2)}) collective-permute-start(bf16[128,128]{1,0:T(8,128)(2,1)S(1)} %get-tuple-element.53.refs_1_.refs_2_), channel_id=1, source_target_pairs={{0,3},{1,2},{2,1},{3,0},{4,7},{5,6},{6,5},{7,4},{8,11},{9,10},{10,... | collective-permute-start | bytes 98312 | tf_op jit(solution)/shard_map/ppermute | solution.py:207
  26.1 0.5 %collective-permute-start.17 = (bf16[128,128]{1,0:T(8,128)(2,1)S(1)}, bf16[128,128]{1,0:T(8,128)(2,1)S(1)}, u32[]{:S(2)}, u32[]{:S(2)}) collective-permute-start(bf16[128,128]{1,0:T(8,128)(2,1)S(1)} %get-tuple-element.53.refs_1_.refs_2_), channel_id=1, source_target_pairs={{0,2},{1,3},{2,0},{3,1},{4,6},{5,7},{6,4},{7,5},{8,10},{9,11},{10,... | collective-permute-start | bytes 98312 | tf_op jit(solution)/shard_map/ppermute | solution.py:207
  26.6 0.3 collective-permute-start.16
  26.9 1.0 %collective-permute-done.9.refs_5_ = f32[128,128]{1,0:T(8,128)S(1)} collective-permute-done((f32[128,128]{1,0:T(8,128)S(1)}, f32[128,128]{1,0:T(8,128)S(1)}, u32[]{:S(2)}, u32[]{:S(2)}) %collective-permute-start.9) | collective-permute-done | bytes 65568 | tf_op jit(solution)/shard_map/ppermute | solution.py:207
  27.9 0.7 %collective-permute-start.10 = (bf16[128,128]{1,0:T(8,128)(2,1)S(1)}, bf16[128,128]{1,0:T(8,128)(2,1)S(1)}, u32[]{:S(2)}, u32[]{:S(2)}) collective-permute-start(bf16[128,128]{1,0:T(8,128)(2,1)S(1)} %forward_middle.1.refs_0_), channel_id=1, source_target_pairs={{0,4},{4,0},{8,12},{12,8},{16,20},{20,16},{24,28},{28,24},{1,5},{5... | collective-permute-start | bytes 98312 | tf_op jit(solution)/shard_map/ppermute | solution.py:207
  28.7 1.3 %collective-permute-done.17.refs_3_ = bf16[128,128]{1,0:T(8,128)(2,1)S(1)} collective-permute-done((bf16[128,128]{1,0:T(8,128)(2,1)S(1)}, bf16[128,128]{1,0:T(8,128)(2,1)S(1)}, u32[]{:S(2)}, u32[]{:S(2)}) %collective-permute-start.17) | collective-permute-done | bytes 32800 | tf_op jit(solution)/shard_map/ppermute | solution.py:207
  30.0 0.3 adjoint_two.1
  30.3 1.2 %collective-permute-start.22 = (bf16[4,128,128]{2,1,0:T(8,128)(2,1)S(1)}, bf16[4,128,128]{2,1,0:T(8,128)(2,1)S(1)}, u32[]{:S(2)}, u32[]{:S(2)}) collective-permute-start(bf16[4,128,128]{2,1,0:T(8,128)(2,1)S(1)} %get-tuple-element.54.refs_3_), channel_id=1, source_target_pairs={{0,4},{4,0},{8,12},{12,8},{16,20},{20,16},{24,28},{28,24},{1,5},{5... | collective-permute-start | bytes 393224 | tf_op jit(solution)/shard_map/ppermute | solution.py:207
  31.5 0.4 collective-permute-done.10.refs_1_
  31.9 3.6 %collective-permute-start.21 = (bf16[2,128,128]{2,1,0:T(8,128)(2,1)S(1)}, bf16[2,128,128]{2,1,0:T(8,128)(2,1)S(1)}, u32[]{:S(2)}, u32[]{:S(2)}) collective-permute-start(bf16[2,128,128]{2,1,0:T(8,128)(2,1)S(1)} %pair_two_late.1), channel_id=1, source_target_pairs={{0,24},{4,28},{8,16},{12,20},{16,8},{20,12},{24,0},{28,4},{1,25},{... | collective-permute-start | bytes 196616 | tf_op jit(solution)/shard_map/ppermute | solution.py:207
  35.5 0.8 %collective-permute-start.20 = (bf16[2,128,128]{2,1,0:T(8,128)(2,1)S(1)}, bf16[2,128,128]{2,1,0:T(8,128)(2,1)S(1)}, u32[]{:S(2)}, u32[]{:S(2)}) collective-permute-start(bf16[2,128,128]{2,1,0:T(8,128)(2,1)S(1)} %pair_two_early.1.refs_1_), channel_id=1, source_target_pairs={{0,16},{4,20},{8,24},{12,28},{16,0},{20,4},{24,8},{28,12},{1,17},{... | collective-permute-start | bytes 196616 | tf_op jit(solution)/shard_map/ppermute | solution.py:207
  36.4 2.3 %collective-permute-start.26 = (bf16[128,128]{1,0:T(8,128)(2,1)S(1)}, bf16[128,128]{1,0:T(8,128)(2,1)S(1)}, u32[]{:S(2)}, u32[]{:S(2)}) collective-permute-start(bf16[128,128]{1,0:T(8,128)(2,1)S(1)} %get-tuple-element.63), channel_id=1, source_target_pairs={{0,16},{4,20},{8,24},{12,28},{16,0},{20,4},{24,8},{28,12},{1,17},{... | collective-permute-start | bytes 98312 | tf_op jit(solution)/shard_map/ppermute | solution.py:207
  38.6 2.0 %collective-permute-start.28 = (bf16[128,128]{1,0:T(8,128)(2,1)S(1)}, bf16[128,128]{1,0:T(8,128)(2,1)S(1)}, u32[]{:S(2)}, u32[]{:S(2)}) collective-permute-start(bf16[128,128]{1,0:T(8,128)(2,1)S(1)} %get-tuple-element.64), channel_id=1, source_target_pairs={{0,8},{4,12},{8,0},{12,4},{16,24},{20,28},{24,16},{28,20},{1,9},{5... | collective-permute-start | bytes 98312 | tf_op jit(solution)/shard_map/ppermute | solution.py:207
  40.6 1.1 %collective-permute-start.27 = (bf16[128,128]{1,0:T(8,128)(2,1)S(1)}, bf16[128,128]{1,0:T(8,128)(2,1)S(1)}, u32[]{:S(2)}, u32[]{:S(2)}) collective-permute-start(bf16[128,128]{1,0:T(8,128)(2,1)S(1)} %get-tuple-element.56.refs_5_), channel_id=1, source_target_pairs={{0,24},{4,28},{8,16},{12,20},{16,8},{20,12},{24,0},{28,4},{1,25},{... | collective-permute-start | bytes 98312 | tf_op jit(solution)/shard_map/ppermute | solution.py:207
  41.7 0.4 forward_two.1
  42.1 0.1 collective-permute-start.23
  42.2 1.1 %collective-permute-start.24 = (bf16[128,128]{1,0:T(8,128)(2,1)S(1)}, bf16[128,128]{1,0:T(8,128)(2,1)S(1)}, u32[]{:S(2)}, u32[]{:S(2)}) collective-permute-start(bf16[128,128]{1,0:T(8,128)(2,1)S(1)} %get-tuple-element.59), channel_id=1, source_target_pairs={{0,2},{1,3},{2,0},{3,1},{4,6},{5,7},{6,4},{7,5},{8,10},{9,11},{10,... | collective-permute-start | bytes 98312 | tf_op jit(solution)/shard_map/ppermute | solution.py:207
  43.3 0.0 collective-permute-done.26.refs_3_
  43.3 0.8 %collective-permute-start.25 = (bf16[128,128]{1,0:T(8,128)(2,1)S(1)}, bf16[128,128]{1,0:T(8,128)(2,1)S(1)}, u32[]{:S(2)}, u32[]{:S(2)}) collective-permute-start(bf16[128,128]{1,0:T(8,128)(2,1)S(1)} %get-tuple-element.60), channel_id=1, source_target_pairs={{0,3},{1,2},{2,1},{3,0},{4,7},{5,6},{6,5},{7,4},{8,11},{9,10},{10,... | collective-permute-start | bytes 98312 | tf_op jit(solution)/shard_map/ppermute | solution.py:207
  44.1 2.2 %collective-permute-done.27.refs_4_ = bf16[128,128]{1,0:T(8,128)(2,1)S(1)} collective-permute-done((bf16[128,128]{1,0:T(8,128)(2,1)S(1)}, bf16[128,128]{1,0:T(8,128)(2,1)S(1)}, u32[]{:S(2)}, u32[]{:S(2)}) %collective-permute-start.27) | collective-permute-done | bytes 32800 | tf_op jit(solution)/shard_map/ppermute | solution.py:207
  46.3 0.7 %adjoint_end.1 = (f32[128,128]{1,0:T(8,128)}, f32[8,128]{1,0:T(8,128)S(1)}) custom-call(f32[128,128]{1,0:T(8,128)S(1)} %get-tuple-element.61.refs_0_, f32[128,128]{1,0:T(8,128)S(1)} %get-tuple-element.62.refs_1_, f32[1,128]{1,0:T(1,128)S(1)} %get-tuple-element.45.refs_0_.refs_2_, bf16[128,128]{1,0:T(8,128)(2,1)S(1)} %collective-permute-done.26.refs_3_, ...), custom_call_target="tpu_custom_call" | custom-call | flops 3000000000 | bytes 365056 | tf_op jit(solution)/shard_map/adjoint_end/pallas_call | solution.py:36
  47.1 0.7 %forward_end.1 = f32[128,128]{1,0:T(8,128)} custom-call(f32[128,128]{1,0:T(8,128)S(1)} %get-tuple-element.35.refs_0_, f32[128,128]{1,0:T(8,128)S(1)} %get-tuple-element.36.refs_1_, bf16[128,128]{1,0:T(8,128)(2,1)S(1)} %get-tuple-element.57.refs_2_, bf16[128,128]{1,0:T(8,128)(2,1)S(1)} %collective-permute-done.23.refs_3_, ...), custom_call_target="tpu_custom_call" | custom-call | flops 1000000000 | bytes 327680 | tf_op jit(solution)/shard_map/forward_end/pallas_call | solution.py:36
  (27 shorter events, 0.2 us)
Async XLA Ops:
  1.9 6.4 %collective-permute-start.3 = (bf16[128,128]{1,0:T(8,128)(2,1)S(1)}, bf16[128,128]{1,0:T(8,128)(2,1)S(1)}, u32[]{:S(2)}, u32[]{:S(2)}) collective-permute-start(bf16[128,128]{1,0:T(8,128)(2,1)S(1)} %get-tuple-element.39.refs_1_), channel_id=1, source_target_pairs={{0,3},{1,2},{2,1},{3,0},{4,7},{5,6},{6,5},{7,4},{8,11},{9,10},{10,... | collective-permute-start | bytes 98312 | tf_op jit(solution)/shard_map/ppermute | solution.py:207
  4.4 4.0 %collective-permute-start.2 = (bf16[128,128]{1,0:T(8,128)(2,1)S(1)}, bf16[128,128]{1,0:T(8,128)(2,1)S(1)}, u32[]{:S(2)}, u32[]{:S(2)}) collective-permute-start(bf16[128,128]{1,0:T(8,128)(2,1)S(1)} %get-tuple-element.39.refs_1_), channel_id=1, source_target_pairs={{0,2},{1,3},{2,0},{3,1},{4,6},{5,7},{6,4},{7,5},{8,10},{9,11},{10,... | collective-permute-start | bytes 98312 | tf_op jit(solution)/shard_map/ppermute | solution.py:207
  5.0 3.4 %collective-permute-start.1 = (bf16[128,128]{1,0:T(8,128)(2,1)S(1)}, bf16[128,128]{1,0:T(8,128)(2,1)S(1)}, u32[]{:S(2)}, u32[]{:S(2)}) collective-permute-start(bf16[128,128]{1,0:T(8,128)(2,1)S(1)} %get-tuple-element.39.refs_1_), channel_id=1, source_target_pairs={{0,1},{1,0},{2,3},{3,2},{4,5},{5,4},{6,7},{7,6},{8,9},{9,8},{10,11... | collective-permute-start | bytes 98312 | tf_op jit(solution)/shard_map/ppermute | solution.py:207
  5.0 5.2 %collective-permute-start = (bf16[128,128]{1,0:T(8,128)(2,1)S(1)}, bf16[128,128]{1,0:T(8,128)(2,1)S(1)}, u32[]{:S(2)}, u32[]{:S(2)}) collective-permute-start(bf16[128,128]{1,0:T(8,128)(2,1)S(1)} %get-tuple-element.38.refs_0_), channel_id=1, source_target_pairs={{0,4},{4,0},{8,12},{12,8},{16,20},{20,16},{24,28},{28,24},{1,5},{5... | collective-permute-start | bytes 98312 | tf_op jit(solution)/shard_map/ppermute | solution.py:207
  8.7 6.4 %collective-permute-start.11 = (f32[2,128,128]{2,1,0:T(8,128)S(1)}, f32[2,128,128]{2,1,0:T(8,128)S(1)}, u32[]{:S(2)}, u32[]{:S(2)}) collective-permute-start(f32[2,128,128]{2,1,0:T(8,128)S(1)} %get-tuple-element.47), channel_id=1, source_target_pairs={{0,4},{4,0},{8,12},{12,8},{16,20},{20,16},{24,28},{28,24},{1,5},{5... | collective-permute-start | bytes 393224 | tf_op jit(solution)/shard_map/ppermute | solution.py:207
  10.2 10.2 %collective-permute-start.5 = (bf16[2,128,128]{2,1,0:T(8,128)(2,1)S(1)}, bf16[2,128,128]{2,1,0:T(8,128)(2,1)S(1)}, u32[]{:S(2)}, u32[]{:S(2)}) collective-permute-start(bf16[2,128,128]{2,1,0:T(8,128)(2,1)S(1)} %pair_one_early.1.refs_1_), channel_id=1, source_target_pairs={{0,16},{4,20},{8,24},{12,28},{16,0},{20,4},{24,8},{28,12},{1,17},{... | collective-permute-start | bytes 196616 | tf_op jit(solution)/shard_map/ppermute | solution.py:207
  12.9 5.0 %collective-permute-start.14 = (f32[2,128,128]{2,1,0:T(8,128)S(1)}, f32[2,128,128]{2,1,0:T(8,128)S(1)}, u32[]{:S(2)}, u32[]{:S(2)}) collective-permute-start(f32[2,128,128]{2,1,0:T(8,128)S(1)} %get-tuple-element.40.refs_2_), channel_id=1, source_target_pairs={{0,4},{4,0},{8,12},{12,8},{16,20},{20,16},{24,28},{28,24},{1,5},{5... | collective-permute-start | bytes 393224 | tf_op jit(solution)/shard_map/ppermute | solution.py:207
  13.4 7.1 %collective-permute-start.6 = (bf16[2,128,128]{2,1,0:T(8,128)(2,1)S(1)}, bf16[2,128,128]{2,1,0:T(8,128)(2,1)S(1)}, u32[]{:S(2)}, u32[]{:S(2)}) collective-permute-start(bf16[2,128,128]{2,1,0:T(8,128)(2,1)S(1)} %pair_one_late.1), channel_id=1, source_target_pairs={{0,24},{4,28},{8,16},{12,20},{16,8},{20,12},{24,0},{28,4},{1,25},{... | collective-permute-start | bytes 196616 | tf_op jit(solution)/shard_map/ppermute | solution.py:207
  14.9 5.6 %collective-permute-start.4 = (bf16[2,128,128]{2,1,0:T(8,128)(2,1)S(1)}, bf16[2,128,128]{2,1,0:T(8,128)(2,1)S(1)}, u32[]{:S(2)}, u32[]{:S(2)}) collective-permute-start(bf16[2,128,128]{2,1,0:T(8,128)(2,1)S(1)} %pair_one_late.1), channel_id=1, source_target_pairs={{0,8},{4,12},{8,0},{12,4},{16,24},{20,28},{24,16},{28,20},{1,9},{5... | collective-permute-start | bytes 196616 | tf_op jit(solution)/shard_map/ppermute | solution.py:207
  15.1 9.1 %collective-permute-start.12 = (f32[128,128]{1,0:T(8,128)S(1)}, f32[128,128]{1,0:T(8,128)S(1)}, u32[]{:S(2)}, u32[]{:S(2)}) collective-permute-start(f32[128,128]{1,0:T(8,128)S(1)} %get-tuple-element.48), channel_id=1, source_target_pairs={{0,16},{4,20},{8,24},{12,28},{16,0},{20,4},{24,8},{28,12},{1,17},{... | collective-permute-start | bytes 196616 | tf_op jit(solution)/shard_map/ppermute | solution.py:207
  17.9 6.3 %collective-permute-start.13 = (f32[128,128]{1,0:T(8,128)S(1)}, f32[128,128]{1,0:T(8,128)S(1)}, u32[]{:S(2)}, u32[]{:S(2)}) collective-permute-start(f32[128,128]{1,0:T(8,128)S(1)} %get-tuple-element.49), channel_id=1, source_target_pairs={{0,24},{4,28},{8,16},{12,20},{16,8},{20,12},{24,0},{28,4},{1,25},{... | collective-permute-start | bytes 196616 | tf_op jit(solution)/shard_map/ppermute | solution.py:207
  20.4 4.5 %collective-permute-start.15 = (f32[128,128]{1,0:T(8,128)S(1)}, f32[128,128]{1,0:T(8,128)S(1)}, u32[]{:S(2)}, u32[]{:S(2)}) collective-permute-start(f32[128,128]{1,0:T(8,128)S(1)} %get-tuple-element.51), channel_id=1, source_target_pairs={{0,8},{4,12},{8,0},{12,4},{16,24},{20,28},{24,16},{28,20},{1,9},{5... | collective-permute-start | bytes 196616 | tf_op jit(solution)/shard_map/ppermute | solution.py:207
  21.0 5.6 %collective-permute-start.7 = (f32[128,128]{1,0:T(8,128)S(1)}, f32[128,128]{1,0:T(8,128)S(1)}, u32[]{:S(2)}, u32[]{:S(2)}) collective-permute-start(f32[128,128]{1,0:T(8,128)S(1)} %get-tuple-element.42), channel_id=1, source_target_pairs={{0,1},{1,0},{2,3},{3,2},{4,5},{5,4},{6,7},{7,6},{8,9},{9,8},{10,11... | collective-permute-start | bytes 196616 | tf_op jit(solution)/shard_map/ppermute | solution.py:207
  21.1 5.8 %collective-permute-start.8 = (f32[128,128]{1,0:T(8,128)S(1)}, f32[128,128]{1,0:T(8,128)S(1)}, u32[]{:S(2)}, u32[]{:S(2)}) collective-permute-start(f32[128,128]{1,0:T(8,128)S(1)} %get-tuple-element.43), channel_id=1, source_target_pairs={{0,2},{1,3},{2,0},{3,1},{4,6},{5,7},{6,4},{7,5},{8,10},{9,11},{10,... | collective-permute-start | bytes 196616 | tf_op jit(solution)/shard_map/ppermute | solution.py:207
  24.2 3.7 %collective-permute-start.9 = (f32[128,128]{1,0:T(8,128)S(1)}, f32[128,128]{1,0:T(8,128)S(1)}, u32[]{:S(2)}, u32[]{:S(2)}) collective-permute-start(f32[128,128]{1,0:T(8,128)S(1)} %get-tuple-element.44.refs_5_), channel_id=1, source_target_pairs={{0,3},{1,2},{2,1},{3,0},{4,7},{5,6},{6,5},{7,4},{8,11},{9,10},{10,... | collective-permute-start | bytes 196616 | tf_op jit(solution)/shard_map/ppermute | solution.py:207
  24.9 3.7 %collective-permute-start.18 = (bf16[128,128]{1,0:T(8,128)(2,1)S(1)}, bf16[128,128]{1,0:T(8,128)(2,1)S(1)}, u32[]{:S(2)}, u32[]{:S(2)}) collective-permute-start(bf16[128,128]{1,0:T(8,128)(2,1)S(1)} %get-tuple-element.53.refs_1_.refs_2_), channel_id=1, source_target_pairs={{0,3},{1,2},{2,1},{3,0},{4,7},{5,6},{6,5},{7,4},{8,11},{9,10},{10,... | collective-permute-start | bytes 98312 | tf_op jit(solution)/shard_map/ppermute | solution.py:207
  26.1 3.9 %collective-permute-start.17 = (bf16[128,128]{1,0:T(8,128)(2,1)S(1)}, bf16[128,128]{1,0:T(8,128)(2,1)S(1)}, u32[]{:S(2)}, u32[]{:S(2)}) collective-permute-start(bf16[128,128]{1,0:T(8,128)(2,1)S(1)} %get-tuple-element.53.refs_1_.refs_2_), channel_id=1, source_target_pairs={{0,2},{1,3},{2,0},{3,1},{4,6},{5,7},{6,4},{7,5},{8,10},{9,11},{10,... | collective-permute-start | bytes 98312 | tf_op jit(solution)/shard_map/ppermute | solution.py:207
  26.6 3.4 %collective-permute-start.16 = (bf16[128,128]{1,0:T(8,128)(2,1)S(1)}, bf16[128,128]{1,0:T(8,128)(2,1)S(1)}, u32[]{:S(2)}, u32[]{:S(2)}) collective-permute-start(bf16[128,128]{1,0:T(8,128)(2,1)S(1)} %get-tuple-element.53.refs_1_.refs_2_), channel_id=1, source_target_pairs={{0,1},{1,0},{2,3},{3,2},{4,5},{5,4},{6,7},{7,6},{8,9},{9,8},{10,11... | collective-permute-start | bytes 98312 | tf_op jit(solution)/shard_map/ppermute | solution.py:207
  27.9 4.0 %collective-permute-start.10 = (bf16[128,128]{1,0:T(8,128)(2,1)S(1)}, bf16[128,128]{1,0:T(8,128)(2,1)S(1)}, u32[]{:S(2)}, u32[]{:S(2)}) collective-permute-start(bf16[128,128]{1,0:T(8,128)(2,1)S(1)} %forward_middle.1.refs_0_), channel_id=1, source_target_pairs={{0,4},{4,0},{8,12},{12,8},{16,20},{20,16},{24,28},{28,24},{1,5},{5... | collective-permute-start | bytes 98312 | tf_op jit(solution)/shard_map/ppermute | solution.py:207
  30.3 6.0 %collective-permute-start.22 = (bf16[4,128,128]{2,1,0:T(8,128)(2,1)S(1)}, bf16[4,128,128]{2,1,0:T(8,128)(2,1)S(1)}, u32[]{:S(2)}, u32[]{:S(2)}) collective-permute-start(bf16[4,128,128]{2,1,0:T(8,128)(2,1)S(1)} %get-tuple-element.54.refs_3_), channel_id=1, source_target_pairs={{0,4},{4,0},{8,12},{12,8},{16,20},{20,16},{24,28},{28,24},{1,5},{5... | collective-permute-start | bytes 393224 | tf_op jit(solution)/shard_map/ppermute | solution.py:207
  31.9 8.7 %collective-permute-start.21 = (bf16[2,128,128]{2,1,0:T(8,128)(2,1)S(1)}, bf16[2,128,128]{2,1,0:T(8,128)(2,1)S(1)}, u32[]{:S(2)}, u32[]{:S(2)}) collective-permute-start(bf16[2,128,128]{2,1,0:T(8,128)(2,1)S(1)} %pair_two_late.1), channel_id=1, source_target_pairs={{0,24},{4,28},{8,16},{12,20},{16,8},{20,12},{24,0},{28,4},{1,25},{... | collective-permute-start | bytes 196616 | tf_op jit(solution)/shard_map/ppermute | solution.py:207
  35.5 6.1 %collective-permute-start.19 = (bf16[2,128,128]{2,1,0:T(8,128)(2,1)S(1)}, bf16[2,128,128]{2,1,0:T(8,128)(2,1)S(1)}, u32[]{:S(2)}, u32[]{:S(2)}) collective-permute-start(bf16[2,128,128]{2,1,0:T(8,128)(2,1)S(1)} %pair_two_late.1), channel_id=1, source_target_pairs={{0,8},{4,12},{8,0},{12,4},{16,24},{20,28},{24,16},{28,20},{1,9},{5... | collective-permute-start | bytes 196616 | tf_op jit(solution)/shard_map/ppermute | solution.py:207
  35.5 6.1 %collective-permute-start.20 = (bf16[2,128,128]{2,1,0:T(8,128)(2,1)S(1)}, bf16[2,128,128]{2,1,0:T(8,128)(2,1)S(1)}, u32[]{:S(2)}, u32[]{:S(2)}) collective-permute-start(bf16[2,128,128]{2,1,0:T(8,128)(2,1)S(1)} %pair_two_early.1.refs_1_), channel_id=1, source_target_pairs={{0,16},{4,20},{8,24},{12,28},{16,0},{20,4},{24,8},{28,12},{1,17},{... | collective-permute-start | bytes 196616 | tf_op jit(solution)/shard_map/ppermute | solution.py:207
  36.4 6.9 %collective-permute-start.26 = (bf16[128,128]{1,0:T(8,128)(2,1)S(1)}, bf16[128,128]{1,0:T(8,128)(2,1)S(1)}, u32[]{:S(2)}, u32[]{:S(2)}) collective-permute-start(bf16[128,128]{1,0:T(8,128)(2,1)S(1)} %get-tuple-element.63), channel_id=1, source_target_pairs={{0,16},{4,20},{8,24},{12,28},{16,0},{20,4},{24,8},{28,12},{1,17},{... | collective-permute-start | bytes 98312 | tf_op jit(solution)/shard_map/ppermute | solution.py:207
  38.6 5.4 %collective-permute-start.28 = (bf16[128,128]{1,0:T(8,128)(2,1)S(1)}, bf16[128,128]{1,0:T(8,128)(2,1)S(1)}, u32[]{:S(2)}, u32[]{:S(2)}) collective-permute-start(bf16[128,128]{1,0:T(8,128)(2,1)S(1)} %get-tuple-element.64), channel_id=1, source_target_pairs={{0,8},{4,12},{8,0},{12,4},{16,24},{20,28},{24,16},{28,20},{1,9},{5... | collective-permute-start | bytes 98312 | tf_op jit(solution)/shard_map/ppermute | solution.py:207
  40.6 5.7 %collective-permute-start.27 = (bf16[128,128]{1,0:T(8,128)(2,1)S(1)}, bf16[128,128]{1,0:T(8,128)(2,1)S(1)}, u32[]{:S(2)}, u32[]{:S(2)}) collective-permute-start(bf16[128,128]{1,0:T(8,128)(2,1)S(1)} %get-tuple-element.56.refs_5_), channel_id=1, source_target_pairs={{0,24},{4,28},{8,16},{12,20},{16,8},{20,12},{24,0},{28,4},{1,25},{... | collective-permute-start | bytes 98312 | tf_op jit(solution)/shard_map/ppermute | solution.py:207
  42.1 4.9 %collective-permute-start.23 = (bf16[128,128]{1,0:T(8,128)(2,1)S(1)}, bf16[128,128]{1,0:T(8,128)(2,1)S(1)}, u32[]{:S(2)}, u32[]{:S(2)}) collective-permute-start(bf16[128,128]{1,0:T(8,128)(2,1)S(1)} %get-tuple-element.58), channel_id=1, source_target_pairs={{0,1},{1,0},{2,3},{3,2},{4,5},{5,4},{6,7},{7,6},{8,9},{9,8},{10,11... | collective-permute-start | bytes 98312 | tf_op jit(solution)/shard_map/ppermute | solution.py:207
  42.2 4.9 %collective-permute-start.24 = (bf16[128,128]{1,0:T(8,128)(2,1)S(1)}, bf16[128,128]{1,0:T(8,128)(2,1)S(1)}, u32[]{:S(2)}, u32[]{:S(2)}) collective-permute-start(bf16[128,128]{1,0:T(8,128)(2,1)S(1)} %get-tuple-element.59), channel_id=1, source_target_pairs={{0,2},{1,3},{2,0},{3,1},{4,6},{5,7},{6,4},{7,5},{8,10},{9,11},{10,... | collective-permute-start | bytes 98312 | tf_op jit(solution)/shard_map/ppermute | solution.py:207
  43.3 3.8 %collective-permute-start.25 = (bf16[128,128]{1,0:T(8,128)(2,1)S(1)}, bf16[128,128]{1,0:T(8,128)(2,1)S(1)}, u32[]{:S(2)}, u32[]{:S(2)}) collective-permute-start(bf16[128,128]{1,0:T(8,128)(2,1)S(1)} %get-tuple-element.60), channel_id=1, source_target_pairs={{0,3},{1,2},{2,1},{3,0},{4,7},{5,6},{6,5},{7,4},{8,11},{9,10},{10,... | collective-permute-start | bytes 98312 | tf_op jit(solution)/shard_map/ppermute | solution.py:207

commit v18 on v17

--- a/solution.py
+++ b/solution.py
@@ -293,7 +293,7 @@
 
     def forward(name, early, late, kind):
         panels = [early] + [
-            send(early if s == near else late, "rows", n_rows, 2 * s) for s in range(1, half)
+            send(early if s == 1 else late, "rows", n_rows, 2 * s) for s in range(1, half)
         ]
         return run(
             name,

time: 48.1 us -> 50.1 us (1.042)
  waiting for transfers between devices: 7.46 us -> 10.2 us
  starting transfers between devices: 33.7 us -> 33 us
    ppermute x29, waiting for transfers between devices: 7.46 us -> 10.2 us  [send(): return lax.ppermute(value, axis, [(i, i ^ step) for i in range(count)])]
    ppermute x29, starting transfers between devices: 33.7 us -> 33 us  [send(): return lax.ppermute(value, axis, [(i, i ^ step) for i in range(count)])]
  transfers between devices with their start and end apart: 29 -> 29, of which waited for: 6 -> 8; matrix products, arithmetic and copies ran while one was open for 0% -> 0% of each run, Pallas kernels for 7% -> 7%
where the time goes in v18:
time: 50.1 us; the launch traced here: 50 us
  starting transfers between devices  33 us (66%)
  waiting for transfers between devices  10.2 us (20%)
  Pallas kernels  5.3 us (11%)
  between operations  1.44 us (3%)
    ppermute x29, starting transfers between devices, send(): return lax.ppermute(value, axis, [(i, i ^ step) for i in range(count)])  33 us
    ppermute x29, waiting for transfers between devices, send(): return lax.ppermute(value, axis, [(i, i ^ step) for i in range(count)])  10.2 us
    pallas_call x17, Pallas kernels, call(): pl.pallas_call(ordered, out_shape=outs, in_specs=[*in_specs, *[pl.BlockSp...  5.3 us
  transfers between devices with their start and end apart: 29, of which 8 were waited for; matrix products, arithmetic and copies ran while one was open for 0% of the time, Pallas kernels for 7%

profile of v18, /device:TPU:0, one launch (start us, length us, event | category | flops | bytes accessed | tf_op | source)
XLA Modules:
  0.0 50.0 jit_solution(5077606670989599078)
XLA Ops:
  0.6 1.3 %start.1 = (bf16[128,128]{1,0:T(8,128)(2,1)S(1)}, bf16[128,128]{1,0:T(8,128)(2,1)S(1)}, f32[1,128]{1,0:T(1,128)S(1)}, f32[128,128]{1,0:T(8,128)S(1)}, f32[128,12...) custom-call(s32[1,128]{1,0:T(1,128)} %bitcast.1, f32[8]{0:T(128)} %refs_1_.2, ...), custom_call_target="tpu_custom_call" | custom-call | bytes 1967136 | tf_op jit(solution)/shard_map/start/pallas_call | solution.py:36
  1.9 2.4 %collective-permute-start.4 = (bf16[128,128]{1,0:T(8,128)(2,1)S(1)}, bf16[128,128]{1,0:T(8,128)(2,1)S(1)}, u32[]{:S(2)}, u32[]{:S(2)}) collective-permute-start(bf16[128,128]{1,0:T(8,128)(2,1)S(1)} %get-tuple-element.39.refs_1_), channel_id=1, source_target_pairs={{0,3},{1,2},{2,1},{3,0},{4,7},{5,6},{6,5},{7,4},{8,11},{9,10},{10,... | collective-permute-start | bytes 98312 | tf_op jit(solution)/shard_map/ppermute | solution.py:207
  4.4 0.6 %collective-permute-start.3 = (bf16[128,128]{1,0:T(8,128)(2,1)S(1)}, bf16[128,128]{1,0:T(8,128)(2,1)S(1)}, u32[]{:S(2)}, u32[]{:S(2)}) collective-permute-start(bf16[128,128]{1,0:T(8,128)(2,1)S(1)} %get-tuple-element.39.refs_1_), channel_id=1, source_target_pairs={{0,2},{1,3},{2,0},{3,1},{4,6},{5,7},{6,4},{7,5},{8,10},{9,11},{10,... | collective-permute-start | bytes 98312 | tf_op jit(solution)/shard_map/ppermute | solution.py:207
  5.0 0.0 collective-permute-start.2
  5.0 1.8 %collective-permute-start = (bf16[128,128]{1,0:T(8,128)(2,1)S(1)}, bf16[128,128]{1,0:T(8,128)(2,1)S(1)}, u32[]{:S(2)}, u32[]{:S(2)}) collective-permute-start(bf16[128,128]{1,0:T(8,128)(2,1)S(1)} %get-tuple-element.38.refs_0_), channel_id=1, source_target_pairs={{0,4},{4,0},{8,12},{12,8},{16,20},{20,16},{24,28},{28,24},{1,5},{5... | collective-permute-start | bytes 98312 | tf_op jit(solution)/shard_map/ppermute | solution.py:207
  7.5 1.0 %dense.1.refs_2_.refs_0_ = bf16[512,1024]{1,0:T(8,128)(2,1)S(1)} custom-call(bf16[1,1,24,128,128]{4,3,2,1,0:T(8,128)(2,1)S(1)} %get-tuple-element.37.refs_0_, s32[1,1,24]{2,1,0:T(1,128)} %refs_1_.3, s32[1,1,24]{2,1,0:T(1,128)} %refs_2_.3, s32[1,1]{1,0:T(1,128)S(6)} %copy.10.refs_3_), custom_call_target="tpu_custom_call" | custom-call | bytes 1835204 | tf_op jit(solution)/shard_map/dense/pallas_call | solution.py:36
  8.5 0.0 collective-permute-done.2.refs_2_
  8.5 0.3 adjoint_one.1
  8.8 1.4 %collective-permute-start.11 = (f32[2,128,128]{2,1,0:T(8,128)S(1)}, f32[2,128,128]{2,1,0:T(8,128)S(1)}, u32[]{:S(2)}, u32[]{:S(2)}) collective-permute-start(f32[2,128,128]{2,1,0:T(8,128)S(1)} %get-tuple-element.47), channel_id=1, source_target_pairs={{0,4},{4,0},{8,12},{12,8},{16,20},{20,16},{24,28},{28,24},{1,5},{5... | collective-permute-start | bytes 393224 | tf_op jit(solution)/shard_map/ppermute | solution.py:207
  10.2 1.6 %collective-permute-start.1 = (bf16[2,128,128]{2,1,0:T(8,128)(2,1)S(1)}, bf16[2,128,128]{2,1,0:T(8,128)(2,1)S(1)}, u32[]{:S(2)}, u32[]{:S(2)}) collective-permute-start(bf16[2,128,128]{2,1,0:T(8,128)(2,1)S(1)} %pair_one_early.1.refs_1_), channel_id=1, source_target_pairs={{0,8},{4,12},{8,0},{12,4},{16,24},{20,28},{24,16},{28,20},{1,9},{5... | collective-permute-start | bytes 196616 | tf_op jit(solution)/shard_map/ppermute | solution.py:207
  11.9 0.5 %collective-permute-start.14 = (f32[2,128,128]{2,1,0:T(8,128)S(1)}, f32[2,128,128]{2,1,0:T(8,128)S(1)}, u32[]{:S(2)}, u32[]{:S(2)}) collective-permute-start(f32[2,128,128]{2,1,0:T(8,128)S(1)} %get-tuple-element.40.refs_2_), channel_id=1, source_target_pairs={{0,4},{4,0},{8,12},{12,8},{16,20},{20,16},{24,28},{28,24},{1,5},{5... | collective-permute-start | bytes 393224 | tf_op jit(solution)/shard_map/ppermute | solution.py:207
  12.4 2.5 %collective-permute-start.6 = (bf16[2,128,128]{2,1,0:T(8,128)(2,1)S(1)}, bf16[2,128,128]{2,1,0:T(8,128)(2,1)S(1)}, u32[]{:S(2)}, u32[]{:S(2)}) collective-permute-start(bf16[2,128,128]{2,1,0:T(8,128)(2,1)S(1)} %pair_one_late.1), channel_id=1, source_target_pairs={{0,24},{4,28},{8,16},{12,20},{16,8},{20,12},{24,0},{28,4},{1,25},{... | collective-permute-start | bytes 196616 | tf_op jit(solution)/shard_map/ppermute | solution.py:207
  14.9 0.2 collective-permute-start.5
  15.1 0.0 collective-permute-done.11.refs_1_
  15.1 2.8 %collective-permute-start.12 = (f32[128,128]{1,0:T(8,128)S(1)}, f32[128,128]{1,0:T(8,128)S(1)}, u32[]{:S(2)}, u32[]{:S(2)}) collective-permute-start(f32[128,128]{1,0:T(8,128)S(1)} %get-tuple-element.48), channel_id=1, source_target_pairs={{0,16},{4,20},{8,24},{12,28},{16,0},{20,4},{24,8},{28,12},{1,17},{... | collective-permute-start | bytes 196616 | tf_op jit(solution)/shard_map/ppermute | solution.py:207
  17.9 0.0 collective-permute-done.14.refs_1_
  17.9 2.6 %collective-permute-start.13 = (f32[128,128]{1,0:T(8,128)S(1)}, f32[128,128]{1,0:T(8,128)S(1)}, u32[]{:S(2)}, u32[]{:S(2)}) collective-permute-start(f32[128,128]{1,0:T(8,128)S(1)} %get-tuple-element.49), channel_id=1, source_target_pairs={{0,24},{4,28},{8,16},{12,20},{16,8},{20,12},{24,0},{28,4},{1,25},{... | collective-permute-start | bytes 196616 | tf_op jit(solution)/shard_map/ppermute | solution.py:207
  20.5 0.1 collective-permute-start.15
  20.6 0.0 collective-permute-done.6.refs_4_
  20.6 3.8 %collective-permute-done.5.refs_3_ = bf16[2,128,128]{2,1,0:T(8,128)(2,1)S(1)} collective-permute-done((bf16[2,128,128]{2,1,0:T(8,128)(2,1)S(1)}, bf16[2,128,128]{2,1,0:T(8,128)(2,1)S(1)}, u32[]{:S(2)}, u32[]{:S(2)}) %collective-permute-start.5) | collective-permute-done | bytes 65568 | tf_op jit(solution)/shard_map/ppermute | solution.py:207
  24.4 0.4 forward_one.1
  24.9 0.1 collective-permute-start.7
  24.9 1.4 %collective-permute-start.8 = (f32[128,128]{1,0:T(8,128)S(1)}, f32[128,128]{1,0:T(8,128)S(1)}, u32[]{:S(2)}, u32[]{:S(2)}) collective-permute-start(f32[128,128]{1,0:T(8,128)S(1)} %get-tuple-element.43), channel_id=1, source_target_pairs={{0,2},{1,3},{2,0},{3,1},{4,6},{5,7},{6,4},{7,5},{8,10},{9,11},{10,... | collective-permute-start | bytes 196616 | tf_op jit(solution)/shard_map/ppermute | solution.py:207
  26.4 0.0 collective-permute-done.12.refs_1_
  26.4 0.4 collective-permute-start.9
  26.8 1.4 %collective-permute-start.18 = (bf16[128,128]{1,0:T(8,128)(2,1)S(1)}, bf16[128,128]{1,0:T(8,128)(2,1)S(1)}, u32[]{:S(2)}, u32[]{:S(2)}) collective-permute-start(bf16[128,128]{1,0:T(8,128)(2,1)S(1)} %get-tuple-element.53.refs_1_.refs_2_), channel_id=1, source_target_pairs={{0,3},{1,2},{2,1},{3,0},{4,7},{5,6},{6,5},{7,4},{8,11},{9,10},{10,... | collective-permute-start | bytes 98312 | tf_op jit(solution)/shard_map/ppermute | solution.py:207
  28.2 0.8 %collective-permute-start.17 = (bf16[128,128]{1,0:T(8,128)(2,1)S(1)}, bf16[128,128]{1,0:T(8,128)(2,1)S(1)}, u32[]{:S(2)}, u32[]{:S(2)}) collective-permute-start(bf16[128,128]{1,0:T(8,128)(2,1)S(1)} %get-tuple-element.53.refs_1_.refs_2_), channel_id=1, source_target_pairs={{0,2},{1,3},{2,0},{3,1},{4,6},{5,7},{6,4},{7,5},{8,10},{9,11},{10,... | collective-permute-start | bytes 98312 | tf_op jit(solution)/shard_map/ppermute | solution.py:207
  29.0 0.6 %collective-permute-done.8.refs_4_ = f32[128,128]{1,0:T(8,128)S(1)} collective-permute-done((f32[128,128]{1,0:T(8,128)S(1)}, f32[128,128]{1,0:T(8,128)S(1)}, u32[]{:S(2)}, u32[]{:S(2)}) %collective-permute-start.8) | collective-permute-done | bytes 65568 | tf_op jit(solution)/shard_map/ppermute | solution.py:207
  29.6 1.0 %collective-permute-done.9.refs_5_ = f32[128,128]{1,0:T(8,128)S(1)} collective-permute-done((f32[128,128]{1,0:T(8,128)S(1)}, f32[128,128]{1,0:T(8,128)S(1)}, u32[]{:S(2)}, u32[]{:S(2)}) %collective-permute-start.9) | collective-permute-done | bytes 65568 | tf_op jit(solution)/shard_map/ppermute | solution.py:207
  30.6 0.6 %collective-permute-start.10 = (bf16[128,128]{1,0:T(8,128)(2,1)S(1)}, bf16[128,128]{1,0:T(8,128)(2,1)S(1)}, u32[]{:S(2)}, u32[]{:S(2)}) collective-permute-start(bf16[128,128]{1,0:T(8,128)(2,1)S(1)} %forward_middle.1.refs_0_), channel_id=1, source_target_pairs={{0,4},{4,0},{8,12},{12,8},{16,20},{20,16},{24,28},{28,24},{1,5},{5... | collective-permute-start | bytes 98312 | tf_op jit(solution)/shard_map/ppermute | solution.py:207
  31.2 0.1 collective-permute-done.18.refs_4_
  31.3 1.0 %collective-permute-done.17.refs_3_ = bf16[128,128]{1,0:T(8,128)(2,1)S(1)} collective-permute-done((bf16[128,128]{1,0:T(8,128)(2,1)S(1)}, bf16[128,128]{1,0:T(8,128)(2,1)S(1)}, u32[]{:S(2)}, u32[]{:S(2)}) %collective-permute-start.17) | collective-permute-done | bytes 32800 | tf_op jit(solution)/shard_map/ppermute | solution.py:207
  32.3 0.3 adjoint_two.1
  32.6 0.6 %collective-permute-start.22 = (bf16[4,128,128]{2,1,0:T(8,128)(2,1)S(1)}, bf16[4,128,128]{2,1,0:T(8,128)(2,1)S(1)}, u32[]{:S(2)}, u32[]{:S(2)}) collective-permute-start(bf16[4,128,128]{2,1,0:T(8,128)(2,1)S(1)} %get-tuple-element.54.refs_3_), channel_id=1, source_target_pairs={{0,4},{4,0},{8,12},{12,8},{16,20},{20,16},{24,28},{28,24},{1,5},{5... | collective-permute-start | bytes 393224 | tf_op jit(solution)/shard_map/ppermute | solution.py:207
  33.1 1.5 %collective-permute-done.10.refs_1_ = bf16[128,128]{1,0:T(8,128)(2,1)S(1)} collective-permute-done((bf16[128,128]{1,0:T(8,128)(2,1)S(1)}, bf16[128,128]{1,0:T(8,128)(2,1)S(1)}, u32[]{:S(2)}, u32[]{:S(2)}) %collective-permute-start.10) | collective-permute-done | bytes 32800 | tf_op jit(solution)/shard_map/ppermute | solution.py:207
  34.6 2.6 %collective-permute-start.21 = (bf16[2,128,128]{2,1,0:T(8,128)(2,1)S(1)}, bf16[2,128,128]{2,1,0:T(8,128)(2,1)S(1)}, u32[]{:S(2)}, u32[]{:S(2)}) collective-permute-start(bf16[2,128,128]{2,1,0:T(8,128)(2,1)S(1)} %pair_two_late.1), channel_id=1, source_target_pairs={{0,24},{4,28},{8,16},{12,20},{16,8},{20,12},{24,0},{28,4},{1,25},{... | collective-permute-start | bytes 196616 | tf_op jit(solution)/shard_map/ppermute | solution.py:207
  37.2 1.8 %collective-permute-start.19 = (bf16[2,128,128]{2,1,0:T(8,128)(2,1)S(1)}, bf16[2,128,128]{2,1,0:T(8,128)(2,1)S(1)}, u32[]{:S(2)}, u32[]{:S(2)}) collective-permute-start(bf16[2,128,128]{2,1,0:T(8,128)(2,1)S(1)} %pair_two_early.1.refs_1_), channel_id=1, source_target_pairs={{0,8},{4,12},{8,0},{12,4},{16,24},{20,28},{24,16},{28,20},{1,9},{5... | collective-permute-start | bytes 196616 | tf_op jit(solution)/shard_map/ppermute | solution.py:207
  39.0 1.2 %collective-permute-start.26 = (bf16[128,128]{1,0:T(8,128)(2,1)S(1)}, bf16[128,128]{1,0:T(8,128)(2,1)S(1)}, u32[]{:S(2)}, u32[]{:S(2)}) collective-permute-start(bf16[128,128]{1,0:T(8,128)(2,1)S(1)} %get-tuple-element.63), channel_id=1, source_target_pairs={{0,16},{4,20},{8,24},{12,28},{16,0},{20,4},{24,8},{28,12},{1,17},{... | collective-permute-start | bytes 98312 | tf_op jit(solution)/shard_map/ppermute | solution.py:207
  40.2 2.0 %collective-permute-start.28 = (bf16[128,128]{1,0:T(8,128)(2,1)S(1)}, bf16[128,128]{1,0:T(8,128)(2,1)S(1)}, u32[]{:S(2)}, u32[]{:S(2)}) collective-permute-start(bf16[128,128]{1,0:T(8,128)(2,1)S(1)} %get-tuple-element.64), channel_id=1, source_target_pairs={{0,8},{4,12},{8,0},{12,4},{16,24},{20,28},{24,16},{28,20},{1,9},{5... | collective-permute-start | bytes 98312 | tf_op jit(solution)/shard_map/ppermute | solution.py:207
  42.2 1.8 %collective-permute-start.27 = (bf16[128,128]{1,0:T(8,128)(2,1)S(1)}, bf16[128,128]{1,0:T(8,128)(2,1)S(1)}, u32[]{:S(2)}, u32[]{:S(2)}) collective-permute-start(bf16[128,128]{1,0:T(8,128)(2,1)S(1)} %get-tuple-element.56.refs_5_), channel_id=1, source_target_pairs={{0,24},{4,28},{8,16},{12,20},{16,8},{20,12},{24,0},{28,4},{1,25},{... | collective-permute-start | bytes 98312 | tf_op jit(solution)/shard_map/ppermute | solution.py:207
  44.0 0.4 forward_two.1
  44.4 0.1 collective-permute-start.23
  44.5 1.4 %collective-permute-start.24 = (bf16[128,128]{1,0:T(8,128)(2,1)S(1)}, bf16[128,128]{1,0:T(8,128)(2,1)S(1)}, u32[]{:S(2)}, u32[]{:S(2)}) collective-permute-start(bf16[128,128]{1,0:T(8,128)(2,1)S(1)} %get-tuple-element.59), channel_id=1, source_target_pairs={{0,2},{1,3},{2,0},{3,1},{4,6},{5,7},{6,4},{7,5},{8,10},{9,11},{10,... | collective-permute-start | bytes 98312 | tf_op jit(solution)/shard_map/ppermute | solution.py:207
  46.0 0.4 collective-permute-start.25
  46.4 1.5 %collective-permute-done.27.refs_4_ = bf16[128,128]{1,0:T(8,128)(2,1)S(1)} collective-permute-done((bf16[128,128]{1,0:T(8,128)(2,1)S(1)}, bf16[128,128]{1,0:T(8,128)(2,1)S(1)}, u32[]{:S(2)}, u32[]{:S(2)}) %collective-permute-start.27) | collective-permute-done | bytes 32800 | tf_op jit(solution)/shard_map/ppermute | solution.py:207
  47.9 0.7 %adjoint_end.1 = (f32[128,128]{1,0:T(8,128)}, f32[8,128]{1,0:T(8,128)S(1)}) custom-call(f32[128,128]{1,0:T(8,128)S(1)} %get-tuple-element.61.refs_0_, f32[128,128]{1,0:T(8,128)S(1)} %get-tuple-element.62.refs_1_, f32[1,128]{1,0:T(1,128)S(1)} %get-tuple-element.45.refs_0_.refs_2_, bf16[128,128]{1,0:T(8,128)(2,1)S(1)} %collective-permute-done.26.refs_3_, ...), custom_call_target="tpu_custom_call" | custom-call | flops 3000000000 | bytes 365056 | tf_op jit(solution)/shard_map/adjoint_end/pallas_call | solution.py:36
  48.7 0.6 %collective-permute-done.25.refs_5_ = bf16[128,128]{1,0:T(8,128)(2,1)S(1)} collective-permute-done((bf16[128,128]{1,0:T(8,128)(2,1)S(1)}, bf16[128,128]{1,0:T(8,128)(2,1)S(1)}, u32[]{:S(2)}, u32[]{:S(2)}) %collective-permute-start.25) | collective-permute-done | bytes 32800 | tf_op jit(solution)/shard_map/ppermute | solution.py:207
  49.3 0.7 %forward_end.1 = f32[128,128]{1,0:T(8,128)} custom-call(f32[128,128]{1,0:T(8,128)S(1)} %get-tuple-element.35.refs_0_, f32[128,128]{1,0:T(8,128)S(1)} %get-tuple-element.36.refs_1_, bf16[128,128]{1,0:T(8,128)(2,1)S(1)} %get-tuple-element.57.refs_2_, bf16[128,128]{1,0:T(8,128)(2,1)S(1)} %collective-permute-done.23.refs_3_, ...), custom_call_target="tpu_custom_call" | custom-call | flops 1000000000 | bytes 327680 | tf_op jit(solution)/shard_map/forward_end/pallas_call | solution.py:36
  (27 shorter events, 0.2 us)
Async XLA Ops:
  1.9 6.6 %collective-permute-start.4 = (bf16[128,128]{1,0:T(8,128)(2,1)S(1)}, bf16[128,128]{1,0:T(8,128)(2,1)S(1)}, u32[]{:S(2)}, u32[]{:S(2)}) collective-permute-start(bf16[128,128]{1,0:T(8,128)(2,1)S(1)} %get-tuple-element.39.refs_1_), channel_id=1, source_target_pairs={{0,3},{1,2},{2,1},{3,0},{4,7},{5,6},{6,5},{7,4},{8,11},{9,10},{10,... | collective-permute-start | bytes 98312 | tf_op jit(solution)/shard_map/ppermute | solution.py:207
  4.4 4.1 %collective-permute-start.3 = (bf16[128,128]{1,0:T(8,128)(2,1)S(1)}, bf16[128,128]{1,0:T(8,128)(2,1)S(1)}, u32[]{:S(2)}, u32[]{:S(2)}) collective-permute-start(bf16[128,128]{1,0:T(8,128)(2,1)S(1)} %get-tuple-element.39.refs_1_), channel_id=1, source_target_pairs={{0,2},{1,3},{2,0},{3,1},{4,6},{5,7},{6,4},{7,5},{8,10},{9,11},{10,... | collective-permute-start | bytes 98312 | tf_op jit(solution)/shard_map/ppermute | solution.py:207
  5.0 3.5 %collective-permute-start.2 = (bf16[128,128]{1,0:T(8,128)(2,1)S(1)}, bf16[128,128]{1,0:T(8,128)(2,1)S(1)}, u32[]{:S(2)}, u32[]{:S(2)}) collective-permute-start(bf16[128,128]{1,0:T(8,128)(2,1)S(1)} %get-tuple-element.39.refs_1_), channel_id=1, source_target_pairs={{0,1},{1,0},{2,3},{3,2},{4,5},{5,4},{6,7},{7,6},{8,9},{9,8},{10,11... | collective-permute-start | bytes 98312 | tf_op jit(solution)/shard_map/ppermute | solution.py:207
  5.0 5.2 %collective-permute-start = (bf16[128,128]{1,0:T(8,128)(2,1)S(1)}, bf16[128,128]{1,0:T(8,128)(2,1)S(1)}, u32[]{:S(2)}, u32[]{:S(2)}) collective-permute-start(bf16[128,128]{1,0:T(8,128)(2,1)S(1)} %get-tuple-element.38.refs_0_), channel_id=1, source_target_pairs={{0,4},{4,0},{8,12},{12,8},{16,20},{20,16},{24,28},{28,24},{1,5},{5... | collective-permute-start | bytes 98312 | tf_op jit(solution)/shard_map/ppermute | solution.py:207
  8.8 6.2 %collective-permute-start.11 = (f32[2,128,128]{2,1,0:T(8,128)S(1)}, f32[2,128,128]{2,1,0:T(8,128)S(1)}, u32[]{:S(2)}, u32[]{:S(2)}) collective-permute-start(f32[2,128,128]{2,1,0:T(8,128)S(1)} %get-tuple-element.47), channel_id=1, source_target_pairs={{0,4},{4,0},{8,12},{12,8},{16,20},{20,16},{24,28},{28,24},{1,5},{5... | collective-permute-start | bytes 393224 | tf_op jit(solution)/shard_map/ppermute | solution.py:207
  10.2 10.2 %collective-permute-start.1 = (bf16[2,128,128]{2,1,0:T(8,128)(2,1)S(1)}, bf16[2,128,128]{2,1,0:T(8,128)(2,1)S(1)}, u32[]{:S(2)}, u32[]{:S(2)}) collective-permute-start(bf16[2,128,128]{2,1,0:T(8,128)(2,1)S(1)} %pair_one_early.1.refs_1_), channel_id=1, source_target_pairs={{0,8},{4,12},{8,0},{12,4},{16,24},{20,28},{24,16},{28,20},{1,9},{5... | collective-permute-start | bytes 196616 | tf_op jit(solution)/shard_map/ppermute | solution.py:207
  11.9 6.0 %collective-permute-start.14 = (f32[2,128,128]{2,1,0:T(8,128)S(1)}, f32[2,128,128]{2,1,0:T(8,128)S(1)}, u32[]{:S(2)}, u32[]{:S(2)}) collective-permute-start(f32[2,128,128]{2,1,0:T(8,128)S(1)} %get-tuple-element.40.refs_2_), channel_id=1, source_target_pairs={{0,4},{4,0},{8,12},{12,8},{16,20},{20,16},{24,28},{28,24},{1,5},{5... | collective-permute-start | bytes 393224 | tf_op jit(solution)/shard_map/ppermute | solution.py:207
  12.4 8.2 %collective-permute-start.6 = (bf16[2,128,128]{2,1,0:T(8,128)(2,1)S(1)}, bf16[2,128,128]{2,1,0:T(8,128)(2,1)S(1)}, u32[]{:S(2)}, u32[]{:S(2)}) collective-permute-start(bf16[2,128,128]{2,1,0:T(8,128)(2,1)S(1)} %pair_one_late.1), channel_id=1, source_target_pairs={{0,24},{4,28},{8,16},{12,20},{16,8},{20,12},{24,0},{28,4},{1,25},{... | collective-permute-start | bytes 196616 | tf_op jit(solution)/shard_map/ppermute | solution.py:207
  14.9 9.5 %collective-permute-start.5 = (bf16[2,128,128]{2,1,0:T(8,128)(2,1)S(1)}, bf16[2,128,128]{2,1,0:T(8,128)(2,1)S(1)}, u32[]{:S(2)}, u32[]{:S(2)}) collective-permute-start(bf16[2,128,128]{2,1,0:T(8,128)(2,1)S(1)} %pair_one_late.1), channel_id=1, source_target_pairs={{0,16},{4,20},{8,24},{12,28},{16,0},{20,4},{24,8},{28,12},{1,17},{... | collective-permute-start | bytes 196616 | tf_op jit(solution)/shard_map/ppermute | solution.py:207
  15.1 11.3 %collective-permute-start.12 = (f32[128,128]{1,0:T(8,128)S(1)}, f32[128,128]{1,0:T(8,128)S(1)}, u32[]{:S(2)}, u32[]{:S(2)}) collective-permute-start(f32[128,128]{1,0:T(8,128)S(1)} %get-tuple-element.48), channel_id=1, source_target_pairs={{0,16},{4,20},{8,24},{12,28},{16,0},{20,4},{24,8},{28,12},{1,17},{... | collective-permute-start | bytes 196616 | tf_op jit(solution)/shard_map/ppermute | solution.py:207
  17.9 8.9 %collective-permute-start.13 = (f32[128,128]{1,0:T(8,128)S(1)}, f32[128,128]{1,0:T(8,128)S(1)}, u32[]{:S(2)}, u32[]{:S(2)}) collective-permute-start(f32[128,128]{1,0:T(8,128)S(1)} %get-tuple-element.49), channel_id=1, source_target_pairs={{0,24},{4,28},{8,16},{12,20},{16,8},{20,12},{24,0},{28,4},{1,25},{... | collective-permute-start | bytes 196616 | tf_op jit(solution)/shard_map/ppermute | solution.py:207
  20.5 6.3 %collective-permute-start.15 = (f32[128,128]{1,0:T(8,128)S(1)}, f32[128,128]{1,0:T(8,128)S(1)}, u32[]{:S(2)}, u32[]{:S(2)}) collective-permute-start(f32[128,128]{1,0:T(8,128)S(1)} %get-tuple-element.51), channel_id=1, source_target_pairs={{0,8},{4,12},{8,0},{12,4},{16,24},{20,28},{24,16},{28,20},{1,9},{5... | collective-permute-start | bytes 196616 | tf_op jit(solution)/shard_map/ppermute | solution.py:207
  24.9 4.1 %collective-permute-start.7 = (f32[128,128]{1,0:T(8,128)S(1)}, f32[128,128]{1,0:T(8,128)S(1)}, u32[]{:S(2)}, u32[]{:S(2)}) collective-permute-start(f32[128,128]{1,0:T(8,128)S(1)} %get-tuple-element.42), channel_id=1, source_target_pairs={{0,1},{1,0},{2,3},{3,2},{4,5},{5,4},{6,7},{7,6},{8,9},{9,8},{10,11... | collective-permute-start | bytes 196616 | tf_op jit(solution)/shard_map/ppermute | solution.py:207
  24.9 4.6 %collective-permute-start.8 = (f32[128,128]{1,0:T(8,128)S(1)}, f32[128,128]{1,0:T(8,128)S(1)}, u32[]{:S(2)}, u32[]{:S(2)}) collective-permute-start(f32[128,128]{1,0:T(8,128)S(1)} %get-tuple-element.43), channel_id=1, source_target_pairs={{0,2},{1,3},{2,0},{3,1},{4,6},{5,7},{6,4},{7,5},{8,10},{9,11},{10,... | collective-permute-start | bytes 196616 | tf_op jit(solution)/shard_map/ppermute | solution.py:207
  26.4 4.2 %collective-permute-start.9 = (f32[128,128]{1,0:T(8,128)S(1)}, f32[128,128]{1,0:T(8,128)S(1)}, u32[]{:S(2)}, u32[]{:S(2)}) collective-permute-start(f32[128,128]{1,0:T(8,128)S(1)} %get-tuple-element.44.refs_5_), channel_id=1, source_target_pairs={{0,3},{1,2},{2,1},{3,0},{4,7},{5,6},{6,5},{7,4},{8,11},{9,10},{10,... | collective-permute-start | bytes 196616 | tf_op jit(solution)/shard_map/ppermute | solution.py:207
  26.8 4.5 %collective-permute-start.18 = (bf16[128,128]{1,0:T(8,128)(2,1)S(1)}, bf16[128,128]{1,0:T(8,128)(2,1)S(1)}, u32[]{:S(2)}, u32[]{:S(2)}) collective-permute-start(bf16[128,128]{1,0:T(8,128)(2,1)S(1)} %get-tuple-element.53.refs_1_.refs_2_), channel_id=1, source_target_pairs={{0,3},{1,2},{2,1},{3,0},{4,7},{5,6},{6,5},{7,4},{8,11},{9,10},{10,... | collective-permute-start | bytes 98312 | tf_op jit(solution)/shard_map/ppermute | solution.py:207
  28.2 4.0 %collective-permute-start.17 = (bf16[128,128]{1,0:T(8,128)(2,1)S(1)}, bf16[128,128]{1,0:T(8,128)(2,1)S(1)}, u32[]{:S(2)}, u32[]{:S(2)}) collective-permute-start(bf16[128,128]{1,0:T(8,128)(2,1)S(1)} %get-tuple-element.53.refs_1_.refs_2_), channel_id=1, source_target_pairs={{0,2},{1,3},{2,0},{3,1},{4,6},{5,7},{6,4},{7,5},{8,10},{9,11},{10,... | collective-permute-start | bytes 98312 | tf_op jit(solution)/shard_map/ppermute | solution.py:207
  29.0 3.3 %collective-permute-start.16 = (bf16[128,128]{1,0:T(8,128)(2,1)S(1)}, bf16[128,128]{1,0:T(8,128)(2,1)S(1)}, u32[]{:S(2)}, u32[]{:S(2)}) collective-permute-start(bf16[128,128]{1,0:T(8,128)(2,1)S(1)} %get-tuple-element.53.refs_1_.refs_2_), channel_id=1, source_target_pairs={{0,1},{1,0},{2,3},{3,2},{4,5},{5,4},{6,7},{7,6},{8,9},{9,8},{10,11... | collective-permute-start | bytes 98312 | tf_op jit(solution)/shard_map/ppermute | solution.py:207
  30.6 4.0 %collective-permute-start.10 = (bf16[128,128]{1,0:T(8,128)(2,1)S(1)}, bf16[128,128]{1,0:T(8,128)(2,1)S(1)}, u32[]{:S(2)}, u32[]{:S(2)}) collective-permute-start(bf16[128,128]{1,0:T(8,128)(2,1)S(1)} %forward_middle.1.refs_0_), channel_id=1, source_target_pairs={{0,4},{4,0},{8,12},{12,8},{16,20},{20,16},{24,28},{28,24},{1,5},{5... | collective-permute-start | bytes 98312 | tf_op jit(solution)/shard_map/ppermute | solution.py:207
  32.6 6.4 %collective-permute-start.22 = (bf16[4,128,128]{2,1,0:T(8,128)(2,1)S(1)}, bf16[4,128,128]{2,1,0:T(8,128)(2,1)S(1)}, u32[]{:S(2)}, u32[]{:S(2)}) collective-permute-start(bf16[4,128,128]{2,1,0:T(8,128)(2,1)S(1)} %get-tuple-element.54.refs_3_), channel_id=1, source_target_pairs={{0,4},{4,0},{8,12},{12,8},{16,20},{20,16},{24,28},{28,24},{1,5},{5... | collective-permute-start | bytes 393224 | tf_op jit(solution)/shard_map/ppermute | solution.py:207
  34.6 7.6 %collective-permute-start.21 = (bf16[2,128,128]{2,1,0:T(8,128)(2,1)S(1)}, bf16[2,128,128]{2,1,0:T(8,128)(2,1)S(1)}, u32[]{:S(2)}, u32[]{:S(2)}) collective-permute-start(bf16[2,128,128]{2,1,0:T(8,128)(2,1)S(1)} %pair_two_late.1), channel_id=1, source_target_pairs={{0,24},{4,28},{8,16},{12,20},{16,8},{20,12},{24,0},{28,4},{1,25},{... | collective-permute-start | bytes 196616 | tf_op jit(solution)/shard_map/ppermute | solution.py:207
  37.2 6.8 %collective-permute-start.20 = (bf16[2,128,128]{2,1,0:T(8,128)(2,1)S(1)}, bf16[2,128,128]{2,1,0:T(8,128)(2,1)S(1)}, u32[]{:S(2)}, u32[]{:S(2)}) collective-permute-start(bf16[2,128,128]{2,1,0:T(8,128)(2,1)S(1)} %pair_two_late.1), channel_id=1, source_target_pairs={{0,16},{4,20},{8,24},{12,28},{16,0},{20,4},{24,8},{28,12},{1,17},{... | collective-permute-start | bytes 196616 | tf_op jit(solution)/shard_map/ppermute | solution.py:207
  37.2 6.8 %collective-permute-start.19 = (bf16[2,128,128]{2,1,0:T(8,128)(2,1)S(1)}, bf16[2,128,128]{2,1,0:T(8,128)(2,1)S(1)}, u32[]{:S(2)}, u32[]{:S(2)}) collective-permute-start(bf16[2,128,128]{2,1,0:T(8,128)(2,1)S(1)} %pair_two_early.1.refs_1_), channel_id=1, source_target_pairs={{0,8},{4,12},{8,0},{12,4},{16,24},{20,28},{24,16},{28,20},{1,9},{5... | collective-permute-start | bytes 196616 | tf_op jit(solution)/shard_map/ppermute | solution.py:207
  39.0 6.9 %collective-permute-start.26 = (bf16[128,128]{1,0:T(8,128)(2,1)S(1)}, bf16[128,128]{1,0:T(8,128)(2,1)S(1)}, u32[]{:S(2)}, u32[]{:S(2)}) collective-permute-start(bf16[128,128]{1,0:T(8,128)(2,1)S(1)} %get-tuple-element.63), channel_id=1, source_target_pairs={{0,16},{4,20},{8,24},{12,28},{16,0},{20,4},{24,8},{28,12},{1,17},{... | collective-permute-start | bytes 98312 | tf_op jit(solution)/shard_map/ppermute | solution.py:207
  40.2 6.2 %collective-permute-start.28 = (bf16[128,128]{1,0:T(8,128)(2,1)S(1)}, bf16[128,128]{1,0:T(8,128)(2,1)S(1)}, u32[]{:S(2)}, u32[]{:S(2)}) collective-permute-start(bf16[128,128]{1,0:T(8,128)(2,1)S(1)} %get-tuple-element.64), channel_id=1, source_target_pairs={{0,8},{4,12},{8,0},{12,4},{16,24},{20,28},{24,16},{28,20},{1,9},{5... | collective-permute-start | bytes 98312 | tf_op jit(solution)/shard_map/ppermute | solution.py:207
  42.2 5.7 %collective-permute-start.27 = (bf16[128,128]{1,0:T(8,128)(2,1)S(1)}, bf16[128,128]{1,0:T(8,128)(2,1)S(1)}, u32[]{:S(2)}, u32[]{:S(2)}) collective-permute-start(bf16[128,128]{1,0:T(8,128)(2,1)S(1)} %get-tuple-element.56.refs_5_), channel_id=1, source_target_pairs={{0,24},{4,28},{8,16},{12,20},{16,8},{20,12},{24,0},{28,4},{1,25},{... | collective-permute-start | bytes 98312 | tf_op jit(solution)/shard_map/ppermute | solution.py:207
  44.4 4.2 %collective-permute-start.23 = (bf16[128,128]{1,0:T(8,128)(2,1)S(1)}, bf16[128,128]{1,0:T(8,128)(2,1)S(1)}, u32[]{:S(2)}, u32[]{:S(2)}) collective-permute-start(bf16[128,128]{1,0:T(8,128)(2,1)S(1)} %get-tuple-element.58), channel_id=1, source_target_pairs={{0,1},{1,0},{2,3},{3,2},{4,5},{5,4},{6,7},{7,6},{8,9},{9,8},{10,11... | collective-permute-start | bytes 98312 | tf_op jit(solution)/shard_map/ppermute | solution.py:207
  44.5 4.2 %collective-permute-start.24 = (bf16[128,128]{1,0:T(8,128)(2,1)S(1)}, bf16[128,128]{1,0:T(8,128)(2,1)S(1)}, u32[]{:S(2)}, u32[]{:S(2)}) collective-permute-start(bf16[128,128]{1,0:T(8,128)(2,1)S(1)} %get-tuple-element.59), channel_id=1, source_target_pairs={{0,2},{1,3},{2,0},{3,1},{4,6},{5,7},{6,4},{7,5},{8,10},{9,11},{10,... | collective-permute-start | bytes 98312 | tf_op jit(solution)/shard_map/ppermute | solution.py:207
  46.0 3.3 %collective-permute-start.25 = (bf16[128,128]{1,0:T(8,128)(2,1)S(1)}, bf16[128,128]{1,0:T(8,128)(2,1)S(1)}, u32[]{:S(2)}, u32[]{:S(2)}) collective-permute-start(bf16[128,128]{1,0:T(8,128)(2,1)S(1)} %get-tuple-element.60), channel_id=1, source_target_pairs={{0,3},{1,2},{2,1},{3,0},{4,7},{5,6},{6,5},{7,4},{8,11},{9,10},{10,... | collective-permute-start | bytes 98312 | tf_op jit(solution)/shard_map/ppermute | solution.py:207
